TPU v7x, 32 devices: a whole 2x2x4 slice. The times are simulated.
32 devices in a mesh: gx: 4 (over z), gy: 2 (over y), gz: 4 (over x, core).
Axes of the slice: x: 2, y: 2, z: 4, core: 2. Of those that a mesh axis runs over, the one named last changes fastest.
Arguments:
- enthalpy: float32 [32, 64, 512], P('gx', 'gy', 'gz'), may hold values from -6 to 6
- conductivity: float32 [32, 64, 512], P('gx', 'gy', 'gz'), may hold values from 0.25 to 1
- phase: float32 [4, 2, 4, 16, 16, 256], P('gx', 'gy', 'gz'), may hold values from -1 to 1
- solute: float32 [4, 2, 4, 16, 16, 256], P('gx', 'gy', 'gz'), may hold values from -3 to 3
- tile_source: int32 [4, 2, 4, 16, 1], P('gx', 'gy', 'gz'), may hold values from 0 to 3; in each aligned block of 16 rows (0 to 15, 16 to 31, ..., all dimensions but the last counted through in order) at most 8 rows name the same one
- tile_block: int32 [4, 2, 4, 16], P('gx', 'gy', 'gz'), may hold values from 0 to 63
- tile_neighbour: int32 [4, 2, 4, 16, 6], P('gx', 'gy', 'gz'), may hold values from -1 to 63, as said below
Outputs:
- enthalpy_out: float32 [32, 64, 512], P('gx', 'gy', 'gz')
- phase_out: float32 [4, 2, 4, 16, 16, 256], P('gx', 'gy', 'gz')
- solute_out: float32 [4, 2, 4, 16, 16, 256], P('gx', 'gy', 'gz')
Inputs may be any that keep to these rules, and one draw needn't show every extreme that they name: `tile_source`: on one device at most 8 slots name the same brick, and some device reaches 8 in every draw. `tile_neighbour`: entries are tile numbers 16 * owner + slot among the tiles with the same gy and gz indices, or -1. A tile is never its own neighbour. If face f of tile a names tile b, face f xor 1 of tile b names tile a. For each face, at most 6 tiles of one owner name tiles of one same other owner, and some owner reaches 6 in every draw.
All inputs are finite; a program needn't handle non-finite values.
Results may differ from a plain program's by a relative error of at most 0.000084.
Values sent between devices are 32-bit elements; how exact they have to be, the bound alone decides.
No kernel may reach another device: no remote copies, remote signals or barrier semaphores. Data moves between devices by JAX's collectives and lax.ppermute only.
A program may use at most 64 MiB of HBM per device.

v0:
```python
import functools

import jax
import jax.numpy as jnp
import numpy as np
from jax import lax
from jax.experimental import pallas as pl
from jax.experimental.pallas import tpu as pltpu
from jax.sharding import PartitionSpec as P

CB = 8
TE = 16
PLANE = TE * TE
SLOTS = 16
FACES = 6
PHASE_STEPS = 4
REC = 24

RATE = 0.16
ORDER_SPEED = 0.1
SOLUTE_RATE = 0.15
COUPLING = 0.5
REJECTION = 0.5

F32 = jnp.float32
BF16 = jnp.bfloat16
VMEM = pl.BlockSpec(memory_space=pltpu.VMEM)
SMEM = pl.BlockSpec(memory_space=pltpu.SMEM)
PARAMS = pltpu.CompilerParams(vmem_limit_bytes=16 * 1024 * 1024)


def plane_lane(face):
    j = np.arange(TE)
    return [j, PLANE - TE + j, j * TE, j * TE + TE - 1][face - 2]


def constant_tables():
    pick = np.zeros((2, PLANE, 256), np.float32)
    place = np.zeros((2, 128, PLANE), np.float32)
    for field in range(2):
        for face in range(2, 6):
            at = field * 64 + (face - 2) * TE + np.arange(TE)
            pick[field, plane_lane(face ^ 1), at] = 1.0
            pick[field, plane_lane(face), 128 + at] = 1.0
            place[field, at, plane_lane(face)] = 1.0
    y, z = np.divmod(np.arange(PLANE), TE)
    dy, dz = np.abs(y[:, None] - y[None, :]), np.abs(z[:, None] - z[None, :])
    stencil = ((dy + dz) == 1).astype(np.float32)
    lane = np.arange(128)
    spread = (lane[:, None] % CB == z[None, :] // 2).astype(np.float32)
    return pick, place, stencil, spread


def tables():
    pick, place, stencil, spread = constant_tables()
    picks = np.concatenate([pick[0], pick[0], pick[1], pick[1]], axis=0)
    laps = [np.concatenate([stencil, stencil, place[f], place[f]], axis=0) for f in range(2)]
    spreads = np.concatenate([spread, spread], axis=0)
    return (
        jnp.asarray(picks, BF16),
        jnp.asarray(laps[0], BF16),
        jnp.asarray(laps[1], BF16),
        jnp.asarray(spreads, BF16),
    )


def halves(value):
    high = value.astype(BF16)
    return high, (value - high.astype(F32)).astype(BF16)


def dot(a, b):
    return jnp.dot(a, b, preferred_element_type=F32)


def temperature(h):
    return jnp.minimum(h, 0.0) + jnp.maximum(h - 1.0, 0.0)


def iota(shape, dim):
    return lax.broadcasted_iota(jnp.int32, shape, dim)


def write_faces(t, xlo, xhi, ylo, yhi, zlo, zhi):
    bx, by, bz = t.shape
    xlo[...] = t[0]
    xhi[...] = t[bx - 1]
    for x in range(bx):
        ylo[x : x + 1, :] = t[x, 0:1, :]
        yhi[x : x + 1, :] = t[x, by - 1 : by, :]
    diagonal = iota((bx, by, bz), 1) == iota((bx, by, bz), 2)
    zlo[...] = jnp.sum(jnp.where(diagonal, t[:, :, 0:1], 0.0), axis=1)
    zhi[...] = jnp.sum(jnp.where(diagonal, t[:, :, bz - 1 : bz], 0.0), axis=1)


def conduct(h, k, xlo, xhi, ylo, yhi, zlo, zhi):
    bx, by, bz = h.shape
    t = temperature(h)
    row, lane = iota((bx, by, bz), 1), iota((bx, by, bz), 2)
    diagonal = row == lane
    total = jnp.concatenate([xlo[None], t[:-1]], axis=0) + jnp.concatenate([t[1:], xhi[None]], axis=0)
    total += jnp.where(row == 0, ylo[:, None, :], pltpu.roll(t, 1, 1))
    total += jnp.where(row == by - 1, yhi[:, None, :], pltpu.roll(t, by - 1, 1))
    zl = jnp.sum(jnp.where(diagonal, zlo[:, None, :], 0.0), axis=2, keepdims=True)
    zh = jnp.sum(jnp.where(diagonal, zhi[:, None, :], 0.0), axis=2, keepdims=True)
    total += jnp.where(lane == 0, zl, pltpu.roll(t, 1, 2))
    total += jnp.where(lane == bz - 1, zh, pltpu.roll(t, bz - 1, 2))
    return h + RATE * k * (total - 6.0 * t)


def faces_kernel(h, *faces):
    write_faces(temperature(h[...]), *faces)


def first_heat_kernel(h, k, xlo, xhi, ylo, yhi, zlo, zhi, out, *faces):
    halo = [r[...] for r in (xlo, xhi, ylo, yhi, zlo, zhi)]
    h1 = conduct(h[...], k[...], *halo)
    out[...] = h1
    write_faces(temperature(h1), *faces)


def block_layout(cap):
    parts = 128 // CB // cap
    return parts, CB // parts


def second_heat_kernel(cap, request, h, k, xlo, xhi, ylo, yhi, zlo, zhi, out, send, held):
    halo = [r[...] for r in (xlo, xhi, ylo, yhi, zlo, zhi)]
    h2 = conduct(h[...], k[...], *halo)
    out[...] = h2
    bx, by, bz = h2.shape
    held[...] = temperature(h2).reshape(bx, by // CB, CB, bz)
    parts, deep = block_layout(cap)
    nby, nbz = by // CB, bz // CB
    group = iota((deep, CB, bz), 2) // CB
    for owner in range(send.shape[0]):
        total = jnp.zeros((deep, CB, bz), F32)
        for rank in range(cap):
            block = request[owner * cap + rank]
            a, b, c = block // (nby * nbz), (block // nbz) % nby, block % nbz
            for part in range(parts):
                at = rank * parts + part
                patch = held[pl.ds(a * CB + part * deep, deep), b]
                moved = pltpu.roll(patch, (CB * at - CB * c + bz) % bz, 2)
                total = jnp.where(group == at, moved, total)
        send[owner] = total.reshape(deep * CB, bz)


def axis_shift(lo_face, hi_face, axis):
    count = lax.axis_size(axis)
    if count == 2:
        first = lax.axis_index(axis) == 0
        got = lax.ppermute(jnp.where(first, hi_face, lo_face), axis, [(0, 1), (1, 0)])
        zero = jnp.zeros_like(got)
        return jnp.where(first, zero, got), jnp.where(first, got, zero)
    forward = [(i, i + 1) for i in range(count - 1)]
    backward = [(b, a) for a, b in forward]
    return lax.ppermute(hi_face, axis, forward), lax.ppermute(lo_face, axis, backward)


def exchange(faces):
    xlo, xhi, ylo, yhi, zlo, zhi = faces
    return (
        *axis_shift(xlo, xhi, "gx"),
        *axis_shift(ylo, yhi, "gy"),
        *axis_shift(zlo, zhi, "gz"),
    )


def write_records(phase, solute, picks, own):
    flat = [f.reshape(SLOTS * TE, PLANE) for f in (phase, solute)]
    parts = jnp.concatenate([*halves(flat[0]), *halves(flat[1])], axis=1)
    planes = dot(parts, picks)
    own[0:SLOTS, 0:TE, :] = planes[:, 0:128].reshape(SLOTS, TE, 128)
    own[SLOTS : 2 * SLOTS, 0:TE, :] = planes[:, 128:256].reshape(SLOTS, TE, 128)
    for face in range(2):
        for number, field in enumerate((phase, solute)):
            for half in range(2):
                row = TE + face * 4 + number * 2 + half
                lanes = slice(half * 128, half * 128 + 128)
                near, far = (0, TE - 1) if face == 0 else (TE - 1, 0)
                own[0:SLOTS, row : row + 1, :] = field[:, far : far + 1, lanes]
                own[SLOTS : 2 * SLOTS, row : row + 1, :] = field[:, near : near + 1, lanes]


def merge_record(source, number):
    side = (iota((TE, 128), 1) % 64) // TE
    out = source[number(2), 0:TE, :]
    for face in range(3, 6):
        out = jnp.where(side == face - 2, source[number(face), 0:TE, :], out)
    edge = jnp.where(
        iota((8, 128), 0) < 4, source[number(0), TE:REC, :], source[number(1), TE:REC, :]
    )
    return out, edge


def pack(own, send_index, send):
    records = send_index.shape[0] // FACES
    for record in range(records):
        out, edge = merge_record(own, lambda face: send_index[record * FACES + face])
        send[record, 0:TE, :] = out
        send[record, TE:REC, :] = edge


def first_pack_kernel(send_index, phase, solute, picks, own, send):
    write_records(phase[...], solute[...], picks[...], own)
    pack(own, send_index, send)


def take_heat(cap, place, blocks, spreads, held, heat):
    parts, deep = block_layout(cap)
    group = iota((CB, 128), 1) // CB
    for slot in range(SLOTS):
        source, rank = place[slot], place[SLOTS + slot]
        for x in range(CB):
            row = (x % deep) * CB
            patch = blocks[source, row : row + CB, :]
            held[slot * CB + x] = jnp.where(group == rank * parts + x // deep, patch, 0.0)
    rows = held[...].reshape(SLOTS * CB * CB, 128)
    wide = dot(jnp.concatenate(halves(rows), axis=1), spreads)
    wide = wide.reshape(SLOTS * CB, CB, PLANE)
    keep = iota(wide.shape, 1) == iota(wide.shape, 2) // TE // 2
    coarse = jnp.sum(jnp.where(keep, wide, 0.0), axis=1)
    for half in range(2):
        for odd in range(2):
            heat[half, pl.ds(odd, SLOTS * CB, 2), :] = coarse[:, half * 128 : half * 128 + 128]


def step(receive_index, phase, solute, heat, got, own, laps, all_records, ghosts):
    records = got.shape[0]
    all_records[0:records] = got[...]
    all_records[records : records + 2 * SLOTS] = own[...]
    for slot in range(SLOTS):
        out, edge = merge_record(all_records, lambda face: receive_index[slot * FACES + face])
        ghosts[slot, 0:TE, :] = out
        ghosts[slot, TE:REC, :] = edge
    beside = jnp.concatenate(halves(ghosts[:, 0:TE, :].reshape(SLOTS * TE, 128)), axis=1)
    row = iota((SLOTS, TE, PLANE), 1)
    lap = []
    for number, (field, table) in enumerate(((phase, laps[0]), (solute, laps[1]))):
        flat = field.reshape(SLOTS * TE, PLANE)
        total = dot(jnp.concatenate([*halves(flat), beside], axis=1), table)
        total = total.reshape(SLOTS, TE, PLANE) - 6.0 * field
        sides = []
        for face in range(2):
            at = TE + face * 4 + number * 2
            sides.append(
                jnp.concatenate([ghosts[:, at : at + 1, :], ghosts[:, at + 1 : at + 2, :]], axis=2)
            )
        total += jnp.where(row == 0, sides[0], pltpu.roll(field, 1, 1))
        total += jnp.where(row == TE - 1, sides[1], pltpu.roll(field, TE - 1, 1))
        lap.append(total)
    warm = jnp.concatenate([heat[0], heat[1]], axis=1).reshape(SLOTS, TE, PLANE)
    squared = 1.0 - phase * phase
    new_phase = phase + ORDER_SPEED * (
        lap[0] + phase - phase * phase * phase - COUPLING * (warm + solute) * squared * squared
    )
    new_solute = solute + SOLUTE_RATE * lap[1] + REJECTION * (new_phase - phase)
    return new_phase, new_solute


def first_step_kernel(
    cap, receive_index, send_index, place, phase, solute, blocks, got, own, picks, lap0, lap1, spreads,
    phase_out, solute_out, heat_out, own_out, send, all_records, ghosts, held,
):
    take_heat(cap, place, blocks, spreads[...], held, heat_out)
    new_phase, new_solute = step(
        receive_index, phase[...], solute[...], heat_out[...], got, own, (lap0[...], lap1[...]),
        all_records, ghosts,
    )
    phase_out[...] = new_phase
    solute_out[...] = new_solute
    write_records(new_phase, new_solute, picks[...], own_out)
    pack(own_out, send_index, send)


def middle_step_kernel(
    receive_index, send_index, phase, solute, heat, got, own, picks, lap0, lap1,
    phase_out, solute_out, own_out, send, all_records, ghosts,
):
    new_phase, new_solute = step(
        receive_index, phase[...], solute[...], heat[...], got, own, (lap0[...], lap1[...]),
        all_records, ghosts,
    )
    phase_out[...] = new_phase
    solute_out[...] = new_solute
    write_records(new_phase, new_solute, picks[...], own_out)
    pack(own_out, send_index, send)


def last_step_kernel(
    receive_index, phase, solute, heat, got, own, lap0, lap1, phase_out, solute_out, all_records, ghosts
):
    new_phase, new_solute = step(
        receive_index, phase[...], solute[...], heat[...], got, own, (lap0[...], lap1[...]),
        all_records, ghosts,
    )
    phase_out[...] = new_phase
    solute_out[...] = new_solute


def call(kernel, in_specs, out_shapes, scratch=()):
    return pl.pallas_call(
        kernel,
        out_shape=out_shapes,
        in_specs=in_specs,
        out_specs=jax.tree.map(lambda _: VMEM, out_shapes),
        scratch_shapes=list(scratch),
        compiler_params=PARAMS,
    )


def shape(*dims):
    return jax.ShapeDtypeStruct(dims, F32)


def tile_indices(neighbour, cap, me):
    count = lax.axis_size("gx")
    owner = neighbour >> 4
    other = (neighbour >= 0) & (owner != me)
    slot = jnp.arange(SLOTS, dtype=jnp.int32)
    alike = (owner[None] == owner[:, None]) & other[None]
    receive_rank = jnp.sum((alike & (neighbour[None] < neighbour[:, None])).astype(jnp.int32), axis=1)
    send_rank = jnp.sum(
        (alike & (slot[None, :, None] < slot[:, None, None])).astype(jnp.int32), axis=1
    )
    records = count * cap
    receive = jnp.where(
        neighbour < 0,
        records + SLOTS + slot[:, None],
        jnp.where(owner == me, records + (neighbour & (SLOTS - 1)), owner * cap + receive_rank),
    )
    key = jnp.where(other, owner * cap + send_rank, -1)
    hit = key[None] == jnp.arange(records, dtype=jnp.int32)[:, None, None]
    sender = jnp.sum(jnp.where(hit, slot[None, :, None], 0), axis=1)
    sender = sender.reshape(records, 3, 2)[:, :, ::-1]
    return receive.reshape(-1), sender.reshape(-1)


def local(enthalpy, conductivity, phase, solute, tile_source, tile_block, tile_neighbour):
    count = lax.axis_size("gx")
    me = lax.axis_index("gx")
    plane_cap = -(-SLOTS // (count - 1))
    block_cap = 2 * SLOTS // count
    bx, by, bz = enthalpy.shape
    picks, lap0, lap1, spreads = tables()

    face_shapes = [shape(by, bz)] * 2 + [shape(bx, bz)] * 4
    faces = call(faces_kernel, [VMEM], face_shapes)(enthalpy)
    halo = exchange(faces)

    neighbour = tile_neighbour.reshape(SLOTS, FACES)
    receive_index, send_index = tile_indices(neighbour, plane_cap, me)
    phase_field = phase.reshape(SLOTS, TE, PLANE)
    solute_field = solute.reshape(SLOTS, TE, PLANE)
    records = count * plane_cap
    own_shape, send_shape = shape(2 * SLOTS, REC, 128), shape(records, REC, 128)
    own, send = call(first_pack_kernel, [SMEM, VMEM, VMEM, VMEM], [own_shape, send_shape])(
        send_index, phase_field, solute_field, picks
    )
    sources = tile_source.reshape(SLOTS)
    wanted = tile_block.reshape(SLOTS)
    slot = jnp.arange(SLOTS, dtype=jnp.int32)
    ranks = jnp.sum(
        ((sources[None] == sources[:, None]) & (slot[None] < slot[:, None])).astype(jnp.int32), axis=1
    )
    key = sources * block_cap + ranks
    all_keys = jnp.arange(count * block_cap, dtype=jnp.int32)
    request = jnp.sum(jnp.where(key[None] == all_keys[:, None], wanted[None], 0), axis=1)
    request = lax.all_to_all(
        request.reshape(count, block_cap), "gx", split_axis=0, concat_axis=0, tiled=True
    ).reshape(-1)
    got = lax.all_to_all(send, "gx", split_axis=0, concat_axis=0, tiled=True)

    brick = shape(bx, by, bz)
    h1, *faces = call(first_heat_kernel, [VMEM] * 8, [brick] + face_shapes)(
        enthalpy, conductivity, *halo
    )
    halo = exchange(faces)
    _, deep = block_layout(block_cap)
    block_rows = deep * CB
    h2, found = call(
        functools.partial(second_heat_kernel, block_cap),
        [SMEM] + [VMEM] * 8,
        [brick, shape(count, block_rows, bz)],
        [pltpu.VMEM((bx, by // CB, CB, bz), F32)],
    )(request, h1, conductivity, *halo)
    blocks = lax.all_to_all(found, "gx", split_axis=0, concat_axis=0, tiled=True)

    place = jnp.concatenate([sources, ranks])
    field = shape(SLOTS, TE, PLANE)
    step_scratch = [
        pltpu.VMEM((records + 2 * SLOTS, REC, 128), F32),
        pltpu.VMEM((SLOTS, REC, 128), F32),
    ]
    phase_field, solute_field, heat, own, send = call(
        functools.partial(first_step_kernel, block_cap),
        [SMEM] * 3 + [VMEM] * 9,
        [field, field, shape(2, SLOTS * TE, 128), own_shape, send_shape],
        step_scratch + [pltpu.VMEM((SLOTS * CB, CB, 128), F32)],
    )(
        receive_index, send_index, place, phase_field, solute_field, blocks, got, own, picks, lap0, lap1,
        spreads,
    )
    for _ in range(PHASE_STEPS - 2):
        got = lax.all_to_all(send, "gx", split_axis=0, concat_axis=0, tiled=True)
        phase_field, solute_field, own, send = call(
            middle_step_kernel, [SMEM] * 2 + [VMEM] * 8, [field, field, own_shape, send_shape], step_scratch
        )(receive_index, send_index, phase_field, solute_field, heat, got, own, picks, lap0, lap1)
    got = lax.all_to_all(send, "gx", split_axis=0, concat_axis=0, tiled=True)
    phase_field, solute_field = call(
        last_step_kernel, [SMEM] + [VMEM] * 7, [field, field], step_scratch
    )(receive_index, phase_field, solute_field, heat, got, own, lap0, lap1)
    return h2, phase_field.reshape(phase.shape), solute_field.reshape(solute.shape)


def solution(mesh):
    grid = P("gx", "gy", "gz")
    tiles = P("gx", "gy", "gz", None, None, None)
    return jax.shard_map(
        local,
        mesh=mesh,
        in_specs=(
            grid,
            grid,
            tiles,
            tiles,
            P("gx", "gy", "gz", None, None),
            P("gx", "gy", "gz", None),
            P("gx", "gy", "gz", None, None),
        ),
        out_specs=(grid, tiles, tiles),
        check_vma=False,
    )
```

profile of v0, /device:TPU:0, one launch (start us, length us, event | category | flops | bytes accessed | tf_op | source)
XLA Modules:
  0.0 108.7 jit_solution(14582919848873965702)
XLA Ops:
  0.6 0.6 copy-done.11
  1.3 0.2 convert_reduce_fusion.2
  1.5 0.6 copy-done.10
  2.1 0.1 select_reduce_fusion.1
  2.2 0.7 all_to_all.21
  2.9 6.3 %all-to-all-start = ((s32[4,1,8]{2,1,0:T(1,128)}), s32[4,1,8]{2,1,0:T(1,128)S(1)}, u32[]{:S(2)}, u32[]{:S(2)}) async-start(s32[4,1,8]{2,1,0:T(1,128)} %bitcast.2), calls=%async_computation | async-start | bytes 4096 | tf_op jit(solution)/shard_map/all_to_all | solution.py:370
  9.2 0.9 copy-done.6
  10.1 0.1 shard_map.130
  10.3 1.6 %collective-permute-start.2 = (f32[8,128]{1,0:T(8,128)S(1)}, f32[8,128]{1,0:T(8,128)S(1)}, u32[]{:S(2)}, u32[]{:S(2)}) collective-permute-start(f32[8,128]{1,0:T(8,128)S(1)} %broadcast_select_fusion.5), channel_id=1, source_target_pairs={{0,4},{4,0},{1,5},{5,1},{2,6},{6,2},{3,7},{7,3},{8,12},{12,8},{9,1... | collective-permute-start | bytes 12296 | tf_op jit(solution)/shard_map/ppermute | solution.py:153
  11.9 1.3 %collective-permute-start.3 = (f32[8,128]{1,0:T(8,128)S(1)}, f32[8,128]{1,0:T(8,128)S(1)}, u32[]{:S(2)}, u32[]{:S(2)}) collective-permute-start(f32[8,128]{1,0:T(8,128)S(1)} %get-tuple-element.39), channel_id=1, source_target_pairs={{0,1},{1,2},{2,3},{4,5},{5,6},{6,7},{8,9},{9,10},{10,11},{12,13},{... | collective-permute-start | bytes 12296 | tf_op jit(solution)/shard_map/ppermute | solution.py:158
  13.2 0.0 copy-start.9
  13.2 1.3 %collective-permute-start.4 = (f32[8,128]{1,0:T(8,128)S(1)}, f32[8,128]{1,0:T(8,128)S(1)}, u32[]{:S(2)}, u32[]{:S(2)}) collective-permute-start(f32[8,128]{1,0:T(8,128)S(1)} %get-tuple-element.40), channel_id=1, source_target_pairs={{1,0},{2,1},{3,2},{5,4},{6,5},{7,6},{9,8},{10,9},{11,10},{13,12},{... | collective-permute-start | bytes 12296 | tf_op jit(solution)/shard_map/ppermute | solution.py:158
  14.5 3.9 %collective-permute-start = (f32[32,128]{1,0:T(8,128)S(1)}, f32[32,128]{1,0:T(8,128)S(1)}, u32[]{:S(2)}, u32[]{:S(2)}) collective-permute-start(f32[32,128]{1,0:T(8,128)S(1)} %get-tuple-element.35), channel_id=1, source_target_pairs={{0,8},{8,16},{16,24},{1,9},{9,17},{17,25},{2,10},{10,18},{18,26},{... | collective-permute-start | bytes 49160 | tf_op jit(solution)/shard_map/ppermute | solution.py:158
  18.4 1.3 %collective-permute-start.1 = (f32[32,128]{1,0:T(8,128)S(1)}, f32[32,128]{1,0:T(8,128)S(1)}, u32[]{:S(2)}, u32[]{:S(2)}) collective-permute-start(f32[32,128]{1,0:T(8,128)S(1)} %get-tuple-element.36), channel_id=1, source_target_pairs={{8,0},{16,8},{24,16},{9,1},{17,9},{25,17},{10,2},{18,10},{26,18},{... | collective-permute-start | bytes 49160 | tf_op jit(solution)/shard_map/ppermute | solution.py:158
  19.8 0.0 copy-start
  19.8 0.4 convert_reduce_fusion
  20.2 0.0 collective-permute-done.2
  20.2 0.0 collective-permute-done.3.zlo
  20.2 0.0 collective-permute-done.4.zhi
  20.2 0.0 collective-permute-done.xlo
  20.3 3.8 %collective-permute-done.1.xhi = f32[32,128]{1,0:T(8,128)S(1)} collective-permute-done((f32[32,128]{1,0:T(8,128)S(1)}, f32[32,128]{1,0:T(8,128)S(1)}, u32[]{:S(2)}, u32[]{:S(2)}) %collective-permute-start.1) | collective-permute-done | bytes 16416 | tf_op jit(solution)/shard_map/ppermute | solution.py:158
  24.1 0.9 copy-done.7
  25.0 0.3 shard_map.131
  25.3 0.6 collective-permute-start.7
  25.9 0.0 all-to-all-done
  25.9 0.5 broadcast.114
  26.4 0.7 reduce.3
  27.1 0.1 reshape.117.request
  27.2 3.0 %collective-permute-start.8 = (f32[8,128]{1,0:T(8,128)S(1)}, f32[8,128]{1,0:T(8,128)S(1)}, u32[]{:S(2)}, u32[]{:S(2)}) collective-permute-start(f32[8,128]{1,0:T(8,128)S(1)} %get-tuple-element.46), channel_id=1, source_target_pairs={{0,1},{1,2},{2,3},{4,5},{5,6},{6,7},{8,9},{9,10},{10,11},{12,13},{... | collective-permute-start | bytes 12296 | tf_op jit(solution)/shard_map/ppermute | solution.py:158
  30.2 1.3 %collective-permute-start.9 = (f32[8,128]{1,0:T(8,128)S(1)}, f32[8,128]{1,0:T(8,128)S(1)}, u32[]{:S(2)}, u32[]{:S(2)}) collective-permute-start(f32[8,128]{1,0:T(8,128)S(1)} %get-tuple-element.47), channel_id=1, source_target_pairs={{1,0},{2,1},{3,2},{5,4},{6,5},{7,6},{9,8},{10,9},{11,10},{13,12},{... | collective-permute-start | bytes 12296 | tf_op jit(solution)/shard_map/ppermute | solution.py:158
  31.5 3.4 %collective-permute-start.5 = (f32[32,128]{1,0:T(8,128)S(1)}, f32[32,128]{1,0:T(8,128)S(1)}, u32[]{:S(2)}, u32[]{:S(2)}) collective-permute-start(f32[32,128]{1,0:T(8,128)S(1)} %get-tuple-element.42), channel_id=1, source_target_pairs={{0,8},{8,16},{16,24},{1,9},{9,17},{17,25},{2,10},{10,18},{18,26},{... | collective-permute-start | bytes 49160 | tf_op jit(solution)/shard_map/ppermute | solution.py:158
  34.9 1.3 %collective-permute-start.6 = (f32[32,128]{1,0:T(8,128)S(1)}, f32[32,128]{1,0:T(8,128)S(1)}, u32[]{:S(2)}, u32[]{:S(2)}) collective-permute-start(f32[32,128]{1,0:T(8,128)S(1)} %get-tuple-element.43), channel_id=1, source_target_pairs={{8,0},{16,8},{24,16},{9,1},{17,9},{25,17},{10,2},{18,10},{26,18},{... | collective-permute-start | bytes 49160 | tf_op jit(solution)/shard_map/ppermute | solution.py:158
  36.3 0.1 collective-permute-done.5.xlo
  36.3 4.2 %collective-permute-done.6.xhi = f32[32,128]{1,0:T(8,128)S(1)} collective-permute-done((f32[32,128]{1,0:T(8,128)S(1)}, f32[32,128]{1,0:T(8,128)S(1)}, u32[]{:S(2)}, u32[]{:S(2)}) %collective-permute-start.6) | collective-permute-done | bytes 16416 | tf_op jit(solution)/shard_map/ppermute | solution.py:158
  40.5 2.0 %shard_map.132 = (f32[8,32,128]{2,1,0:T(8,128)}, f32[4,32,128]{2,1,0:T(8,128)}) custom-call(s32[32]{0:T(128)S(1)} %reshape.117.request, f32[8,32,128]{2,1,0:T(8,128)S(1)} %get-tuple-element.41.h, f32[8,32,128]{2,1,0:T(8,128)S(1)} %copy-done.5, f32[32,128]{1,0:T(8,128)S(1)} %collective-permute-done.5.xlo, f32[32,128]{1,0:T(8,128)S(1)} %collective-permute-done.6.xhi, ...), custom_call_target="tpu_custom_call" | custom-call | tf_op jit(solution)/shard_map/pallas_call | solution.py:382
  42.5 3.3 %all-to-all-start.1 = ((f32[4,32,128]{2,1,0:T(8,128)}), f32[4,32,128]{2,1,0:T(8,128)S(1)}, u32[]{:S(2)}, u32[]{:S(2)}) async-start(f32[4,32,128]{2,1,0:T(8,128)} %get-tuple-element.49), calls=%async_computation.1 | async-start | bytes 131072 | tf_op jit(solution)/shard_map/all_to_all | solution.py:388
  45.8 0.1 select_reduce_fusion
  46.0 0.1 copy.49
  46.1 0.1 eq.77
  46.1 0.1 copy.48
  46.2 0.1 lt.55
  46.3 0.1 copy.51
  46.4 0.1 mul.23
  46.5 0.1 copy.53
  46.6 0.2 reshape.120.send_index
  46.8 0.0 copy-start.2
  46.8 1.7 %shard_map.133 = (f32[32,24,128]{2,1,0:T(8,128)S(1)}, f32[24,24,128]{2,1,0:T(8,128)}) custom-call(s32[144]{0:T(256)S(1)} %reshape.120.send_index, f32[16,16,256]{2,1,0:T(8,128)S(1)} %bitcast.29, f32[16,16,256]{2,1,0:T(8,128)S(1)} %bitcast.31, bf16[1024,256]{1,0:T(8,128)(2,1)S(1)} %copy-done), custom_call_target="tpu_custom_call" | custom-call | tf_op jit(solution)/shard_map/pallas_call | solution.py:358
  48.5 3.1 %all-to-all-done.1.blocks = f32[4,32,128]{2,1,0:T(8,128)S(1)} async-done(((f32[4,32,128]{2,1,0:T(8,128)}), f32[4,32,128]{2,1,0:T(8,128)S(1)}, u32[]{:S(2)}, u32[]{:S(2)}) %all-to-all-start.1) | async-done | bytes 65568 | tf_op jit(solution)/shard_map/all_to_all | solution.py:388
  51.6 3.6 %all-to-all-start.2 = ((f32[24,24,128]{2,1,0:T(8,128)}), f32[24,24,128]{2,1,0:T(8,128)S(1)}, u32[]{:S(2)}, u32[]{:S(2)}) async-start(f32[24,24,128]{2,1,0:T(8,128)} %get-tuple-element.50), calls=%async_computation.2 | async-start | bytes 589824 | tf_op jit(solution)/shard_map/all_to_all | solution.py:373
  55.2 0.1 broadcast_in_dim.56
  55.2 0.1 broadcast_in_dim.57
  55.3 0.1 copy.50
  55.4 0.1 add.40
  55.5 0.1 copy.52
  55.6 0.1 reduce_sum.50
  55.7 0.1 pad_add_fusion.place
  55.8 9.9 %all-to-all-done.2.got = f32[24,24,128]{2,1,0:T(8,128)S(1)} async-done(((f32[24,24,128]{2,1,0:T(8,128)}), f32[24,24,128]{2,1,0:T(8,128)S(1)}, u32[]{:S(2)}, u32[]{:S(2)}) %all-to-all-start.2) | async-done | bytes 294944 | tf_op jit(solution)/shard_map/all_to_all | solution.py:373
  65.7 1.9 %shard_map.134 = (f32[16,16,256]{2,1,0:T(8,128)S(1)}, f32[16,16,256]{2,1,0:T(8,128)S(1)}, f32[2,256,128]{2,1,0:T(8,128)S(1)}, f32[32,24,128]{2,1,0:T(8,128)S(1)}, f32[24,24,128]{2,1,0:T(8,128)S(1)}) custom-call(s32[96]{0:T(128)S(1)} %select_select_fusion.receive_index, s32[144]{0:T(256)S(1)} %reshape.120.send_index, s32[32]{0:T(128)S(1)} %pad_add_fusion.place, ...), custom_call_target="tpu_custom_call" | custom-call | tf_op jit(solution)/shard_map/pallas_call | solution.py:396
  67.6 12.6 %all_to_all.34.got = f32[24,24,128]{2,1,0:T(8,128)S(1)} all-to-all(f32[24,24,128]{2,1,0:T(8,128)S(1)} %get-tuple-element.55), channel_id=1, replica_groups=mesh['gx'=4,'gy'=2,'gz'=4] {'gx'}, dimensions={0} | all-to-all | bytes 589824 | tf_op jit(solution)/shard_map/all_to_all | solution.py:406
  80.2 1.6 %shard_map.135 = (f32[16,16,256]{2,1,0:T(8,128)S(1)}, f32[16,16,256]{2,1,0:T(8,128)S(1)}, f32[32,24,128]{2,1,0:T(8,128)S(1)}, f32[24,24,128]{2,1,0:T(8,128)S(1)}) custom-call(s32[96]{0:T(128)S(1)} %select_select_fusion.receive_index, s32[144]{0:T(256)S(1)} %reshape.120.send_index, f32[16,16,256]{2,1,0:T(8,128)S(1)} %get-tuple-element.52.phase, ...), custom_call_target="tpu_custom_call" | custom-call | tf_op jit(solution)/shard_map/pallas_call | solution.py:407
  81.8 12.0 %all_to_all.35.got = f32[24,24,128]{2,1,0:T(8,128)S(1)} all-to-all(f32[24,24,128]{2,1,0:T(8,128)S(1)} %get-tuple-element.59), channel_id=1, replica_groups=mesh['gx'=4,'gy'=2,'gz'=4] {'gx'}, dimensions={0} | all-to-all | bytes 589824 | tf_op jit(solution)/shard_map/all_to_all | solution.py:406
  93.8 1.6 %shard_map.136 = (f32[16,16,256]{2,1,0:T(8,128)S(1)}, f32[16,16,256]{2,1,0:T(8,128)S(1)}, f32[32,24,128]{2,1,0:T(8,128)S(1)}, f32[24,24,128]{2,1,0:T(8,128)S(1)}) custom-call(s32[96]{0:T(128)S(1)} %select_select_fusion.receive_index, s32[144]{0:T(256)S(1)} %reshape.120.send_index, f32[16,16,256]{2,1,0:T(8,128)S(1)} %get-tuple-element.57.phase, ...), custom_call_target="tpu_custom_call" | custom-call | tf_op jit(solution)/shard_map/pallas_call | solution.py:407
  95.3 11.4 %all_to_all.36.got = f32[24,24,128]{2,1,0:T(8,128)S(1)} all-to-all(f32[24,24,128]{2,1,0:T(8,128)S(1)} %get-tuple-element.63), channel_id=1, replica_groups=mesh['gx'=4,'gy'=2,'gz'=4] {'gx'}, dimensions={0} | all-to-all | bytes 589824 | tf_op jit(solution)/shard_map/all_to_all | solution.py:410
  106.7 2.0 %shard_map.137 = (f32[16,16,256]{2,1,0:T(8,128)}, f32[16,16,256]{2,1,0:T(8,128)}) custom-call(s32[96]{0:T(128)S(1)} %select_select_fusion.receive_index, f32[16,16,256]{2,1,0:T(8,128)S(1)} %get-tuple-element.61.phase, f32[16,16,256]{2,1,0:T(8,128)S(1)} %get-tuple-element.62.solute, f32[2,256,128]{2,1,0:T(8,128)S(1)} %get-tuple-element.54.heat, ...), custom_call_target="tpu_custom_call" | custom-call | tf_op jit(solution)/shard_map/pallas_call | solution.py:411
  (36 shorter events, 0.2 us)
Async XLA Ops:
  0.6 0.7 copy-start.11
  1.5 0.7 copy-start.10
  2.9 23.0 %all-to-all-start = ((s32[4,1,8]{2,1,0:T(1,128)}), s32[4,1,8]{2,1,0:T(1,128)S(1)}, u32[]{:S(2)}, u32[]{:S(2)}) async-start(s32[4,1,8]{2,1,0:T(1,128)} %bitcast.2), calls=%async_computation | async-start | bytes 4096 | tf_op jit(solution)/shard_map/all_to_all | solution.py:370
  9.2 14.9 %copy-start.5 = (f32[8,32,128]{2,1,0:T(8,128)S(1)}, f32[8,32,128]{2,1,0:T(8,128)}, u32[]{:S(2)}) copy-start(f32[8,32,128]{2,1,0:T(8,128)} %k.3) | copy-start | bytes 393220
  9.2 0.9 copy-start.6
  10.3 9.9 %collective-permute-start.2 = (f32[8,128]{1,0:T(8,128)S(1)}, f32[8,128]{1,0:T(8,128)S(1)}, u32[]{:S(2)}, u32[]{:S(2)}) collective-permute-start(f32[8,128]{1,0:T(8,128)S(1)} %broadcast_select_fusion.5), channel_id=1, source_target_pairs={{0,4},{4,0},{1,5},{5,1},{2,6},{6,2},{3,7},{7,3},{8,12},{12,8},{9,1... | collective-permute-start | bytes 12296 | tf_op jit(solution)/shard_map/ppermute | solution.py:153
  11.9 8.3 %collective-permute-start.3 = (f32[8,128]{1,0:T(8,128)S(1)}, f32[8,128]{1,0:T(8,128)S(1)}, u32[]{:S(2)}, u32[]{:S(2)}) collective-permute-start(f32[8,128]{1,0:T(8,128)S(1)} %get-tuple-element.39), channel_id=1, source_target_pairs={{0,1},{1,2},{2,3},{4,5},{5,6},{6,7},{8,9},{9,10},{10,11},{12,13},{... | collective-permute-start | bytes 12296 | tf_op jit(solution)/shard_map/ppermute | solution.py:158
  13.2 6.6 %copy-start.9 = (s32[1,1,1,16,6]{3,2,4,1,0:T(1,128)S(1)}, s32[1,1,1,16,6]{3,2,4,1,0:T(1,128)}, u32[]{:S(2)}) copy-start(s32[1,1,1,16,6]{3,2,4,1,0:T(1,128)} %param.17) | copy-start | bytes 1156
  13.2 7.0 %collective-permute-start.4 = (f32[8,128]{1,0:T(8,128)S(1)}, f32[8,128]{1,0:T(8,128)S(1)}, u32[]{:S(2)}, u32[]{:S(2)}) collective-permute-start(f32[8,128]{1,0:T(8,128)S(1)} %get-tuple-element.40), channel_id=1, source_target_pairs={{1,0},{2,1},{3,2},{5,4},{6,5},{7,6},{9,8},{10,9},{11,10},{13,12},{... | collective-permute-start | bytes 12296 | tf_op jit(solution)/shard_map/ppermute | solution.py:158
  14.5 5.8 %collective-permute-start = (f32[32,128]{1,0:T(8,128)S(1)}, f32[32,128]{1,0:T(8,128)S(1)}, u32[]{:S(2)}, u32[]{:S(2)}) collective-permute-start(f32[32,128]{1,0:T(8,128)S(1)} %get-tuple-element.35), channel_id=1, source_target_pairs={{0,8},{8,16},{16,24},{1,9},{9,17},{17,25},{2,10},{10,18},{18,26},{... | collective-permute-start | bytes 49160 | tf_op jit(solution)/shard_map/ppermute | solution.py:158
  18.4 5.6 %collective-permute-start.1 = (f32[32,128]{1,0:T(8,128)S(1)}, f32[32,128]{1,0:T(8,128)S(1)}, u32[]{:S(2)}, u32[]{:S(2)}) collective-permute-start(f32[32,128]{1,0:T(8,128)S(1)} %get-tuple-element.36), channel_id=1, source_target_pairs={{8,0},{16,8},{24,16},{9,1},{17,9},{25,17},{10,2},{18,10},{26,18},{... | collective-permute-start | bytes 49160 | tf_op jit(solution)/shard_map/ppermute | solution.py:158
  19.8 27.0 %copy-start = (bf16[1024,256]{1,0:T(8,128)(2,1)S(1)}, bf16[1024,256]{1,0:T(8,128)(2,1)}, u32[]{:S(2)}) copy-start(bf16[1024,256]{1,0:T(8,128)(2,1)} %constant.37.clone.picks) | copy-start | bytes 1572868
  24.1 0.9 copy-start.7
  25.3 10.9 %collective-permute-start.7 = (f32[8,128]{1,0:T(8,128)S(1)}, f32[8,128]{1,0:T(8,128)S(1)}, u32[]{:S(2)}, u32[]{:S(2)}) collective-permute-start(f32[8,128]{1,0:T(8,128)S(1)} %broadcast_select_fusion.4), channel_id=1, source_target_pairs={{0,4},{4,0},{1,5},{5,1},{2,6},{6,2},{3,7},{7,3},{8,12},{12,8},{9,1... | collective-permute-start | bytes 12296 | tf_op jit(solution)/shard_map/ppermute | solution.py:153
  27.2 9.1 %collective-permute-start.8 = (f32[8,128]{1,0:T(8,128)S(1)}, f32[8,128]{1,0:T(8,128)S(1)}, u32[]{:S(2)}, u32[]{:S(2)}) collective-permute-start(f32[8,128]{1,0:T(8,128)S(1)} %get-tuple-element.46), channel_id=1, source_target_pairs={{0,1},{1,2},{2,3},{4,5},{5,6},{6,7},{8,9},{9,10},{10,11},{12,13},{... | collective-permute-start | bytes 12296 | tf_op jit(solution)/shard_map/ppermute | solution.py:158
  30.2 6.0 %collective-permute-start.9 = (f32[8,128]{1,0:T(8,128)S(1)}, f32[8,128]{1,0:T(8,128)S(1)}, u32[]{:S(2)}, u32[]{:S(2)}) collective-permute-start(f32[8,128]{1,0:T(8,128)S(1)} %get-tuple-element.47), channel_id=1, source_target_pairs={{1,0},{2,1},{3,2},{5,4},{6,5},{7,6},{9,8},{10,9},{11,10},{13,12},{... | collective-permute-start | bytes 12296 | tf_op jit(solution)/shard_map/ppermute | solution.py:158
  31.5 4.8 %collective-permute-start.5 = (f32[32,128]{1,0:T(8,128)S(1)}, f32[32,128]{1,0:T(8,128)S(1)}, u32[]{:S(2)}, u32[]{:S(2)}) collective-permute-start(f32[32,128]{1,0:T(8,128)S(1)} %get-tuple-element.42), channel_id=1, source_target_pairs={{0,8},{8,16},{16,24},{1,9},{9,17},{17,25},{2,10},{10,18},{18,26},{... | collective-permute-start | bytes 49160 | tf_op jit(solution)/shard_map/ppermute | solution.py:158
  34.9 5.6 %collective-permute-start.6 = (f32[32,128]{1,0:T(8,128)S(1)}, f32[32,128]{1,0:T(8,128)S(1)}, u32[]{:S(2)}, u32[]{:S(2)}) collective-permute-start(f32[32,128]{1,0:T(8,128)S(1)} %get-tuple-element.43), channel_id=1, source_target_pairs={{8,0},{16,8},{24,16},{9,1},{17,9},{25,17},{10,2},{18,10},{26,18},{... | collective-permute-start | bytes 49160 | tf_op jit(solution)/shard_map/ppermute | solution.py:158
  40.5 6.3 %copy-start.3 = (f32[1,1,1,16,16,256]{5,4,3,2,1,0:T(8,128)S(1)}, f32[1,1,1,16,16,256]{5,4,3,2,1,0:T(8,128)}, u32[]{:S(2)}) copy-start(f32[1,1,1,16,16,256]{5,4,3,2,1,0:T(8,128)} %param.13) | copy-start | bytes 786436
  40.5 6.3 %copy-start.4 = (f32[1,1,1,16,16,256]{5,4,3,2,1,0:T(8,128)S(1)}, f32[1,1,1,16,16,256]{5,4,3,2,1,0:T(8,128)}, u32[]{:S(2)}) copy-start(f32[1,1,1,16,16,256]{5,4,3,2,1,0:T(8,128)} %param.14) | copy-start | bytes 786436
  42.5 9.1 %all-to-all-start.1 = ((f32[4,32,128]{2,1,0:T(8,128)}), f32[4,32,128]{2,1,0:T(8,128)S(1)}, u32[]{:S(2)}, u32[]{:S(2)}) async-start(f32[4,32,128]{2,1,0:T(8,128)} %get-tuple-element.49), calls=%async_computation.1 | async-start | bytes 131072 | tf_op jit(solution)/shard_map/all_to_all | solution.py:388
  46.8 18.9 %copy-start.2 = (bf16[768,256]{1,0:T(8,128)(2,1)S(1)}, bf16[768,256]{1,0:T(8,128)(2,1)}, u32[]{:S(2)}) copy-start(bf16[768,256]{1,0:T(8,128)(2,1)} %constant.38.clone.lap0) | copy-start | bytes 1179652
  48.5 17.2 %copy-start.1 = (bf16[768,256]{1,0:T(8,128)(2,1)S(1)}, bf16[768,256]{1,0:T(8,128)(2,1)}, u32[]{:S(2)}) copy-start(bf16[768,256]{1,0:T(8,128)(2,1)} %constant.39.clone.lap1) | copy-start | bytes 1179652
  51.6 14.1 %copy-start.8 = (bf16[256,256]{1,0:T(8,128)(2,1)S(1)}, bf16[256,256]{1,0:T(8,128)(2,1)}, u32[]{:S(2)}) copy-start(bf16[256,256]{1,0:T(8,128)(2,1)} %constant.40.clone.spreads) | copy-start | bytes 393220
  51.6 14.1 %all-to-all-start.2 = ((f32[24,24,128]{2,1,0:T(8,128)}), f32[24,24,128]{2,1,0:T(8,128)S(1)}, u32[]{:S(2)}, u32[]{:S(2)}) async-start(f32[24,24,128]{2,1,0:T(8,128)} %get-tuple-element.50), calls=%async_computation.2 | async-start | bytes 589824 | tf_op jit(solution)/shard_map/all_to_all | solution.py:373
where the time goes:
time: 109 us
  blocking collectives  36 us (33%)
  starting transfers between devices  32.1 us (29%)
  waiting for transfers between devices  21.1 us (19%)
  Pallas kernels  11.2 us (10%)
  local copies, waits for them, and re-layouts  5.81 us (5%)
  other arithmetic  1.54 us (1%)
    all_to_all x3, blocking collectives, local(): got = lax.all_to_all(send, 'gx', split_axis=0, concat_axis=0, tiled=True)  36 us
    ppermute x4, starting transfers between devices, axis_shift(): lax.ppermute(hi_face, axis, forward)  11.6 us
    all_to_all x1, waiting for transfers between devices, local(): got = lax.all_to_all(send, 'gx', split_axis=0, concat_axis=0, tiled=True)  9.94 us
    ppermute x4, waiting for transfers between devices, axis_shift(): lax.ppermute(lo_face, axis, backward)  8.02 us
    all_to_all x1, starting transfers between devices, local(): lax.all_to_all(request.reshape(count, block_cap), 'gx', split_axis=0, con...  6.32 us
    ppermute x4, starting transfers between devices, axis_shift(): lax.ppermute(lo_face, axis, backward)  5.17 us
    all_to_all x1, starting transfers between devices, local(): got = lax.all_to_all(send, 'gx', split_axis=0, concat_axis=0, tiled=True)  3.58 us
    all_to_all x1, starting transfers between devices, local(): lax.all_to_all(found, 'gx', split_axis=0, concat_axis=0, tiled=True)  3.28 us
  transfers between devices with their start and end apart: 13, of which 5 were waited for; matrix products, arithmetic and copies ran while one was open for 3% of the time, Pallas kernels for 2%

commit v1 on v0

--- a/solution.py
+++ b/solution.py
@@ -81,42 +81,85 @@
     return lax.broadcasted_iota(jnp.int32, shape, dim)
 
 
-def write_faces(t, xlo, xhi, ylo, yhi, zlo, zhi):
-    bx, by, bz = t.shape
-    xlo[...] = t[0]
-    xhi[...] = t[bx - 1]
-    for x in range(bx):
-        ylo[x : x + 1, :] = t[x, 0:1, :]
-        yhi[x : x + 1, :] = t[x, by - 1 : by, :]
-    diagonal = iota((bx, by, bz), 1) == iota((bx, by, bz), 2)
-    zlo[...] = jnp.sum(jnp.where(diagonal, t[:, :, 0:1], 0.0), axis=1)
-    zhi[...] = jnp.sum(jnp.where(diagonal, t[:, :, bz - 1 : bz], 0.0), axis=1)
+def to_lanes(column):
+    bx, by, _ = column.shape
+    diagonal = iota((bx, by, 128), 1) == iota((bx, by, 128), 2)
+    return jnp.sum(jnp.where(diagonal, column, 0.0), axis=1)
+
+
+def to_column(line, by):
+    bx = line.shape[0]
+    diagonal = iota((bx, by, 128), 1) == iota((bx, by, 128), 2)
+    return jnp.sum(jnp.where(diagonal, line[:, None, :], 0.0), axis=2, keepdims=True)
 
 
 def conduct(h, k, xlo, xhi, ylo, yhi, zlo, zhi):
     bx, by, bz = h.shape
     t = temperature(h)
     row, lane = iota((bx, by, bz), 1), iota((bx, by, bz), 2)
-    diagonal = row == lane
-    total = jnp.concatenate([xlo[None], t[:-1]], axis=0) + jnp.concatenate([t[1:], xhi[None]], axis=0)
+    if bx > 1:
+        total = jnp.concatenate([xlo, t[:-1]], axis=0) + jnp.concatenate([t[1:], xhi], axis=0)
+    else:
+        total = xlo + xhi
     total += jnp.where(row == 0, ylo[:, None, :], pltpu.roll(t, 1, 1))
     total += jnp.where(row == by - 1, yhi[:, None, :], pltpu.roll(t, by - 1, 1))
-    zl = jnp.sum(jnp.where(diagonal, zlo[:, None, :], 0.0), axis=2, keepdims=True)
-    zh = jnp.sum(jnp.where(diagonal, zhi[:, None, :], 0.0), axis=2, keepdims=True)
-    total += jnp.where(lane == 0, zl, pltpu.roll(t, 1, 2))
-    total += jnp.where(lane == bz - 1, zh, pltpu.roll(t, bz - 1, 2))
+    total += jnp.where(lane == 0, to_column(zlo, by), pltpu.roll(t, 1, 2))
+    total += jnp.where(lane == bz - 1, to_column(zhi, by), pltpu.roll(t, bz - 1, 2))
     return h + RATE * k * (total - 6.0 * t)
 
 
-def faces_kernel(h, *faces):
-    write_faces(temperature(h[...]), *faces)
-
-
-def first_heat_kernel(h, k, xlo, xhi, ylo, yhi, zlo, zhi, out, *faces):
-    halo = [r[...] for r in (xlo, xhi, ylo, yhi, zlo, zhi)]
-    h1 = conduct(h[...], k[...], *halo)
-    out[...] = h1
-    write_faces(temperature(h1), *faces)
+def sublanes(value, y):
+    return jnp.concatenate([value[x, y : y + 1, :] for x in range(value.shape[0])], axis=0)
+
+
+def side_blocks(h, k):
+    by, bz = h.shape[1:]
+    return [
+        (sublanes(h, 0), sublanes(h, 1), sublanes(k, 0)),
+        (sublanes(h, by - 1), sublanes(h, by - 2), sublanes(k, by - 1)),
+        (to_lanes(h[:, :, 0:1]), to_lanes(h[:, :, 1:2]), to_lanes(k[:, :, 0:1])),
+        (to_lanes(h[:, :, bz - 1 : bz]), to_lanes(h[:, :, bz - 2 : bz - 1]), to_lanes(k[:, :, bz - 1 : bz])),
+    ]
+
+
+def sides_kernel(sizes, h, k, send):
+    ny, nz = sizes
+    my_y, my_z = lax.axis_index("gy"), lax.axis_index("gz")
+    bx = h.shape[0]
+    blocks = side_blocks(h[...], k[...])
+    for y in range(ny):
+        for z in range(nz):
+            for part in range(3):
+                ylo, yhi, zlo, zhi = [block[part] for block in blocks]
+                chosen = jnp.where(
+                    my_y == y, jnp.where(z < my_z, zlo, zhi), jnp.where(y < my_y, ylo, yhi)
+                )
+                send[y * nz + z, part * bx : part * bx + bx, :] = chosen
+
+
+def side_reader(sizes, got, bx):
+    ny, nz = sizes
+    my_y, my_z = lax.axis_index("gy"), lax.axis_index("gz")
+
+    def read(dy, dz, part=0):
+        y, z = my_y + dy, my_z + dz
+        inside = (y >= 0) & (y < ny) & (z >= 0) & (z < nz)
+        at = jnp.where(inside, y * nz + z, 0)
+        return jnp.where(inside, got[at, part * bx : part * bx + bx, :], 0.0)
+
+    return read
+
+
+def layers_kernel(sizes, h, k, got, _, low, high):
+    bx, by, bz = h.shape
+    read = side_reader(sizes, got, bx)
+    around = [read(-1, 0), read(1, 0), read(0, -1), read(0, 1)]
+    for out, near, far in ((low, 0, 1), (high, bx - 1, bx - 2)):
+        out[0:by, :] = h[near]
+        out[by : 2 * by, :] = h[far]
+        out[2 * by : 3 * by, :] = k[near]
+        for number, side in enumerate(around):
+            out[3 * by + number : 3 * by + number + 1, :] = side[near : near + 1, :]
 
 
 def block_layout(cap):
@@ -124,11 +167,58 @@
     return parts, CB // parts
 
 
-def second_heat_kernel(cap, request, h, k, xlo, xhi, ylo, yhi, zlo, zhi, out, send, held):
-    halo = [r[...] for r in (xlo, xhi, ylo, yhi, zlo, zhi)]
-    h2 = conduct(h[...], k[...], *halo)
+def flat_step(h, k, inner, outer, first, last, before, after, length):
+    bx, lanes = h.shape
+    t = temperature(h)
+    row, lane = iota(h.shape, 0), iota(h.shape, 1)
+    total = temperature(inner) + temperature(outer)
+    total += jnp.where(row == 0, temperature(first), pltpu.roll(t, 1, 0))
+    total += jnp.where(row == bx - 1, temperature(last), pltpu.roll(t, bx - 1, 0))
+    total += jnp.where(lane == 0, temperature(before), pltpu.roll(t, 1, 1))
+    total += jnp.where(lane == length - 1, temperature(after), pltpu.roll(t, lanes - 1, 1))
+    return h + RATE * k * (total - 6.0 * t)
+
+
+def heat_kernel(cap, sizes, request, h, k, got, low, high, out, send, held):
+    bx, by, bz = h.shape
+    h0, k0 = h[...], k[...]
+    read = side_reader(sizes, got, bx)
+    layers = []
+    for r in (low, high):
+        layers.append([r[part * by : part * by + by, :][None] for part in range(3)])
+    lines = [[r[3 * by + n : 3 * by + n + 1, :] for n in range(4)] for r in (low, high)]
+    y_sides = [[read(d, 0, part) for part in range(3)] for d in (-1, 1)]
+    z_sides = [[read(0, d, part) for part in range(3)] for d in (-1, 1)]
+    corner = [[read(dy, dz) for dz in (-1, 1)] for dy in (-1, 1)]
+    to_first = [[pltpu.roll(c[0], 1, 1), c[1]] for c in corner]
+    y_inner = [sublanes(h0, 0), sublanes(h0, by - 1)]
+    z_inner = [to_lanes(h0[:, :, 0:1]), to_lanes(h0[:, :, bz - 1 : bz])]
+
+    sides = [temperature(layers[0][0]), temperature(layers[1][0])]
+    sides += [temperature(side[0]) for side in y_sides + z_sides]
+    h1 = conduct(h0, k0, *sides)
+    next_sides = []
+    for side in range(2):
+        near, far, near_k = layers[side]
+        across = [temperature(far), temperature(h0[0:1])]
+        if side:
+            across = [temperature(h0[bx - 1 : bx]), temperature(far)]
+        next_sides.append(conduct(near, near_k, *across, *[temperature(line) for line in lines[side]]))
+    for side in range(2):
+        near, far, near_k = y_sides[side]
+        ends = [to_first[side][0], pltpu.roll(to_first[side][1], bz - 1, 1)]
+        next_sides.append(
+            flat_step(near, near_k, y_inner[side], far, lines[0][side], lines[1][side], *ends, bz)
+        )
+    for side in range(2):
+        near, far, near_k = z_sides[side]
+        ends = [to_first[0][side], pltpu.roll(to_first[1][side], by - 1, 1)]
+        next_sides.append(
+            flat_step(near, near_k, z_inner[side], far, lines[0][2 + side], lines[1][2 + side], *ends, by)
+        )
+    h2 = conduct(h1, k0, *[temperature(side) for side in next_sides])
     out[...] = h2
-    bx, by, bz = h2.shape
+
     held[...] = temperature(h2).reshape(bx, by // CB, CB, bz)
     parts, deep = block_layout(cap)
     nby, nbz = by // CB, bz // CB
@@ -146,27 +236,6 @@
         send[owner] = total.reshape(deep * CB, bz)
 
 
-def axis_shift(lo_face, hi_face, axis):
-    count = lax.axis_size(axis)
-    if count == 2:
-        first = lax.axis_index(axis) == 0
-        got = lax.ppermute(jnp.where(first, hi_face, lo_face), axis, [(0, 1), (1, 0)])
-        zero = jnp.zeros_like(got)
-        return jnp.where(first, zero, got), jnp.where(first, got, zero)
-    forward = [(i, i + 1) for i in range(count - 1)]
-    backward = [(b, a) for a, b in forward]
-    return lax.ppermute(hi_face, axis, forward), lax.ppermute(lo_face, axis, backward)
-
-
-def exchange(faces):
-    xlo, xhi, ylo, yhi, zlo, zhi = faces
-    return (
-        *axis_shift(xlo, xhi, "gx"),
-        *axis_shift(ylo, yhi, "gy"),
-        *axis_shift(zlo, zhi, "gz"),
-    )
-
-
 def write_records(phase, solute, picks, own):
     flat = [f.reshape(SLOTS * TE, PLANE) for f in (phase, solute)]
     parts = jnp.concatenate([*halves(flat[0]), *halves(flat[1])], axis=1)
@@ -196,15 +265,25 @@
 
 def pack(own, send_index, send):
     records = send_index.shape[0] // FACES
+    cap = records // send.shape[0]
     for record in range(records):
         out, edge = merge_record(own, lambda face: send_index[record * FACES + face])
-        send[record, 0:TE, :] = out
-        send[record, TE:REC, :] = edge
-
-
-def first_pack_kernel(send_index, phase, solute, picks, own, send):
+        owner, row = record // cap, record % cap * REC
+        send[owner, row : row + TE, :] = out
+        send[owner, row + TE : row + REC, :] = edge
+
+
+def first_pack_kernel(send_index, place, wanted, phase, solute, picks, own, send):
     write_records(phase[...], solute[...], picks[...], own)
     pack(own, send_index, send)
+    count, rows, _ = send.shape
+    lane = iota((8, 128), 1)
+    for owner in range(count):
+        asked = jnp.zeros((8, 128), F32)
+        for slot in range(SLOTS):
+            here = jnp.where(place[slot] == owner, place[SLOTS + slot], -1)
+            asked = jnp.where(lane == here, wanted[slot].astype(F32), asked)
+        send[owner, rows - 8 : rows, :] = asked
 
 
 def take_heat(cap, place, blocks, spreads, held, heat):
@@ -227,8 +306,12 @@
 
 
 def step(receive_index, phase, solute, heat, got, own, laps, all_records, ghosts):
-    records = got.shape[0]
-    all_records[0:records] = got[...]
+    records = all_records.shape[0] - 2 * SLOTS
+    count = got.shape[0]
+    cap = records // count
+    for owner in range(count):
+        mine = got[owner, 0 : cap * REC, :]
+        all_records[owner * cap : owner * cap + cap] = mine.reshape(cap, REC, 128)
     all_records[records : records + 2 * SLOTS] = own[...]
     for slot in range(SLOTS):
         out, edge = merge_record(all_records, lambda face: receive_index[slot * FACES + face])
@@ -339,55 +422,58 @@
 
 def local(enthalpy, conductivity, phase, solute, tile_source, tile_block, tile_neighbour):
     count = lax.axis_size("gx")
+    sizes = (lax.axis_size("gy"), lax.axis_size("gz"))
     me = lax.axis_index("gx")
     plane_cap = -(-SLOTS // (count - 1))
     block_cap = 2 * SLOTS // count
     bx, by, bz = enthalpy.shape
     picks, lap0, lap1, spreads = tables()
 
-    face_shapes = [shape(by, bz)] * 2 + [shape(bx, bz)] * 4
-    faces = call(faces_kernel, [VMEM], face_shapes)(enthalpy)
-    halo = exchange(faces)
-
+    sides = call(
+        functools.partial(sides_kernel, sizes), [VMEM] * 2, shape(sizes[0] * sizes[1], 3 * bx, 128)
+    )(enthalpy, conductivity)
+    sides = lax.all_to_all(sides, ("gy", "gz"), split_axis=0, concat_axis=0, tiled=True)
+
+    sources = tile_source.reshape(SLOTS)
+    wanted = tile_block.reshape(SLOTS)
+    slot = jnp.arange(SLOTS, dtype=jnp.int32)
+    ranks = jnp.sum(
+        ((sources[None] == sources[:, None]) & (slot[None] < slot[:, None])).astype(jnp.int32), axis=1
+    )
+    place = jnp.concatenate([sources, ranks])
     neighbour = tile_neighbour.reshape(SLOTS, FACES)
     receive_index, send_index = tile_indices(neighbour, plane_cap, me)
     phase_field = phase.reshape(SLOTS, TE, PLANE)
     solute_field = solute.reshape(SLOTS, TE, PLANE)
     records = count * plane_cap
-    own_shape, send_shape = shape(2 * SLOTS, REC, 128), shape(records, REC, 128)
-    own, send = call(first_pack_kernel, [SMEM, VMEM, VMEM, VMEM], [own_shape, send_shape])(
-        send_index, phase_field, solute_field, picks
-    )
-    sources = tile_source.reshape(SLOTS)
-    wanted = tile_block.reshape(SLOTS)
-    slot = jnp.arange(SLOTS, dtype=jnp.int32)
-    ranks = jnp.sum(
-        ((sources[None] == sources[:, None]) & (slot[None] < slot[:, None])).astype(jnp.int32), axis=1
-    )
-    key = sources * block_cap + ranks
-    all_keys = jnp.arange(count * block_cap, dtype=jnp.int32)
-    request = jnp.sum(jnp.where(key[None] == all_keys[:, None], wanted[None], 0), axis=1)
-    request = lax.all_to_all(
-        request.reshape(count, block_cap), "gx", split_axis=0, concat_axis=0, tiled=True
-    ).reshape(-1)
+    own_shape, send_shape = shape(2 * SLOTS, REC, 128), shape(count, plane_cap * REC, 128)
+    own, send = call(
+        first_pack_kernel,
+        [SMEM] * 3 + [VMEM] * 3,
+        [own_shape, shape(count, plane_cap * REC + 8, 128)],
+    )(send_index, place, wanted, phase_field, solute_field, picks)
     got = lax.all_to_all(send, "gx", split_axis=0, concat_axis=0, tiled=True)
-
-    brick = shape(bx, by, bz)
-    h1, *faces = call(first_heat_kernel, [VMEM] * 8, [brick] + face_shapes)(
-        enthalpy, conductivity, *halo
-    )
-    halo = exchange(faces)
+    request = got[:, plane_cap * REC, :block_cap].astype(jnp.int32).reshape(-1)
+
+    layer = shape(3 * by + 8, bz)
+    low, high = call(
+        functools.partial(layers_kernel, sizes),
+        [VMEM] * 3 + [pl.BlockSpec(memory_space=pl.ANY)],
+        [layer, layer],
+    )(enthalpy, conductivity, sides, send)
+    forward = [(i, i + 1) for i in range(count - 1)]
+    backward = [(b, a) for a, b in forward]
+    from_low = lax.ppermute(high, "gx", forward)
+    from_high = lax.ppermute(low, "gx", backward)
     _, deep = block_layout(block_cap)
-    block_rows = deep * CB
-    h2, found = call(
-        functools.partial(second_heat_kernel, block_cap),
-        [SMEM] + [VMEM] * 8,
-        [brick, shape(count, block_rows, bz)],
+    heat_out, found = call(
+        functools.partial(heat_kernel, block_cap, sizes),
+        [SMEM] + [VMEM] * 5,
+        [shape(bx, by, bz), shape(count, deep * CB, bz)],
         [pltpu.VMEM((bx, by // CB, CB, bz), F32)],
-    )(request, h1, conductivity, *halo)
+    )(request, enthalpy, conductivity, sides, from_low, from_high)
     blocks = lax.all_to_all(found, "gx", split_axis=0, concat_axis=0, tiled=True)
 
-    place = jnp.concatenate([sources, ranks])
     field = shape(SLOTS, TE, PLANE)
     step_scratch = [
         pltpu.VMEM((records + 2 * SLOTS, REC, 128), F32),
@@ -411,7 +497,7 @@
     phase_field, solute_field = call(
         last_step_kernel, [SMEM] + [VMEM] * 7, [field, field], step_scratch
     )(receive_index, phase_field, solute_field, heat, got, own, lap0, lap1)
-    return h2, phase_field.reshape(phase.shape), solute_field.reshape(solute.shape)
+    return heat_out, phase_field.reshape(phase.shape), solute_field.reshape(solute.shape)
 
 
 def solution(mesh):

time: 109 us -> 80.2 us (0.74)
  starting transfers between devices: 32.1 us -> 19.4 us
  waiting for transfers between devices: 21.1 us -> 10.9 us
  blocking collectives: 36 us -> 30.4 us
    ppermute x10 -> x2, starting transfers between devices: 18.9 us -> 5.35 us  [the longest x1 4.06 us: local(): from_low = lax.ppermute(high, 'gx', forward)]
    ppermute x10 -> x2, waiting for transfers between devices: 8.11 us -> 0.5 us  [the longest x1 0.5 us: local(): from_high = lax.ppermute(low, 'gx', backward)]
    all_to_all x1, waiting for transfers between devices: 9.94 us -> 4.12 us  [local(): got = lax.all_to_all(send, 'gx', split_axis=0, concat_axis=0, tiled=True)]
    all_to_all x3, blocking collectives: 36 us -> 30.4 us  [local(): got = lax.all_to_all(send, 'gx', split_axis=0, concat_axis=0, tiled=True)]
    all_to_all x1, waiting for transfers between devices: 3.05 us -> 5.74 us  [local(): lax.all_to_all(found, 'gx', split_axis=0, concat_axis=0, tiled=True)]
    all_to_all x1, starting transfers between devices: 3.58 us -> 5 us  [local(): got = lax.all_to_all(send, 'gx', split_axis=0, concat_axis=0, tiled=True)]
    all_to_all x2 -> x0, local copies, waits for them, and re-layouts: 1.18 us -> none  [local(): lax.all_to_all(request.reshape(count, block_cap), 'gx', split_axis=0, con...]
    unnamed x25 -> x29, local copies, waits for them, and re-layouts: 3.18 us -> 3.51 us
  transfers between devices with their start and end apart: 13 -> 5, of which waited for: 5 -> 4; matrix products, arithmetic and copies ran while one was open for 3% -> 3% of each run, Pallas kernels for 2% -> 2%
where the time goes in v1:
time: 80.2 us; the launch traced here: 79.5 us
  blocking collectives  30.4 us (38%)
  starting transfers between devices  19.4 us (24%)
  Pallas kernels  12.2 us (15%)
  waiting for transfers between devices  10.9 us (14%)
  local copies, waits for them, and re-layouts  4.97 us (6%)
  between operations  0.86 us (1%)
    all_to_all x3, blocking collectives, local(): got = lax.all_to_all(send, 'gx', split_axis=0, concat_axis=0, tiled=True)  30.4 us
    all_to_all x1, waiting for transfers between devices, local(): lax.all_to_all(found, 'gx', split_axis=0, concat_axis=0, tiled=True)  5.74 us
    all_to_all x1, starting transfers between devices, local(): lax.all_to_all(sides, ('gy', 'gz'), split_axis=0, concat_axis=0, tiled=True)  5.3 us
    all_to_all x1, starting transfers between devices, local(): got = lax.all_to_all(send, 'gx', split_axis=0, concat_axis=0, tiled=True)  5 us
    all_to_all x1, waiting for transfers between devices, local(): got = lax.all_to_all(send, 'gx', split_axis=0, concat_axis=0, tiled=True)  4.12 us
    ppermute x1, starting transfers between devices, local(): from_low = lax.ppermute(high, 'gx', forward)  4.06 us
    all_to_all x1, starting transfers between devices, local(): lax.all_to_all(found, 'gx', split_axis=0, concat_axis=0, tiled=True)  3.76 us
    unnamed x29, local copies, waits for them, and re-layouts  3.51 us
  transfers between devices with their start and end apart: 5, of which 4 were waited for; matrix products, arithmetic and copies ran while one was open for 3% of the time, Pallas kernels for 2%

profile of v1, /device:TPU:0, one launch (start us, length us, event | category | flops | bytes accessed | tf_op | source)
XLA Modules:
  0.0 79.5 jit_solution(6724526239020977398)
XLA Ops:
  0.6 0.0 copy-start
  0.6 0.0 copy-start.3
  0.7 1.0 %copy-done.3 = f32[8,32,128]{2,1,0:T(8,128)S(1)} copy-done((f32[8,32,128]{2,1,0:T(8,128)S(1)}, f32[8,32,128]{2,1,0:T(8,128)}, u32[]{:S(2)}) %copy-start.3) | copy-done | bytes 131096
  1.6 0.0 copy-start.5
  1.6 0.9 %copy-done.5 = f32[8,32,128]{2,1,0:T(8,128)S(1)} copy-done((f32[8,32,128]{2,1,0:T(8,128)S(1)}, f32[8,32,128]{2,1,0:T(8,128)}, u32[]{:S(2)}) %copy-start.5) | copy-done | bytes 131096
  2.5 0.0 copy-start.12
  2.5 0.0 copy-start.13
  2.5 0.9 %shard_map.131 = f32[8,24,128]{2,1,0:T(8,128)} custom-call(f32[8,32,128]{2,1,0:T(8,128)S(1)} %copy-done.3, f32[8,32,128]{2,1,0:T(8,128)S(1)} %copy-done.5), custom_call_target="tpu_custom_call" | custom-call | tf_op jit(solution)/shard_map/pallas_call | solution.py:432
  3.4 0.0 copy-start.7
  3.4 5.3 %all-to-all-start.1 = ((f32[8,24,128]{2,1,0:T(8,128)}), f32[8,24,128]{2,1,0:T(8,128)S(1)}, u32[]{:S(2)}, u32[]{:S(2)}) async-start(f32[8,24,128]{2,1,0:T(8,128)} %shard_map.131), calls=%async_computation.1 | async-start | bytes 196608 | tf_op jit(solution)/shard_map/all_to_all | solution.py:435
  8.8 0.0 copy-done.12
  8.8 0.0 copy-done.13
  8.8 0.2 convert_reduce_fusion.2
  9.0 0.4 convert_reduce_fusion
  9.4 0.1 copy.40
  9.4 0.1 reduce_sum.42
  9.6 0.1 select_reduce_fusion
  9.7 0.1 copy.35
  9.8 0.1 reshape.107.send_index
  9.9 0.1 pad_add_fusion.place
  10.0 0.0 copy-start.11
  10.0 0.0 copy-done
  10.0 0.0 copy-done.7
  10.0 0.7 copy-done.11
  10.7 0.0 copy-start.8
  10.7 0.9 %copy-done.8 = f32[1,1,1,16,16,256]{5,4,3,2,1,0:T(8,128)S(1)} copy-done((f32[1,1,1,16,16,256]{5,4,3,2,1,0:T(8,128)S(1)}, f32[1,1,1,16,16,256]{5,4,3,2,1,0:T(8,128)}, u32[]{:S(2)}) %copy-start.8) | copy-done | bytes 262168
  11.6 1.8 %shard_map.130 = (f32[32,24,128]{2,1,0:T(8,128)S(1)}, f32[4,152,128]{2,1,0:T(8,128)}) custom-call(s32[144]{0:T(256)S(1)} %reshape.107.send_index, s32[32]{0:T(128)S(1)} %pad_add_fusion.place, s32[16]{0:T(128)S(1)} %bitcast.31, f32[16,16,256]{2,1,0:T(8,128)S(1)} %bitcast.27, f32[16,16,256]{2,1,0:T(8,128)S(1)} %bitcast.29, bf16[1024,256]{1,0:T(8,128)(2,1)S(1)} %copy-done), custom_call_target="tpu_custom_call" | custom-call | tf_op jit(solution)/shard_map/pallas_call | solution.py:450
  13.4 0.5 all-to-all-done.1.got
  13.9 5.0 %all-to-all-start = ((f32[4,152,128]{2,1,0:T(8,128)}), f32[4,152,128]{2,1,0:T(8,128)S(1)}, u32[]{:S(2)}, u32[]{:S(2)}) async-start(f32[4,152,128]{2,1,0:T(8,128)} %get-tuple-element.24._), calls=%async_computation | async-start | bytes 622592 | tf_op jit(solution)/shard_map/all_to_all | solution.py:455
  19.0 0.1 copy.37
  19.1 0.1 eq.57
  19.2 0.1 copy.36
  19.3 0.1 lt.55
  19.4 0.1 copy.39
  19.5 0.1 mul.16
  19.6 0.1 broadcast_in_dim.40
  19.6 0.1 broadcast_in_dim.41
  19.7 0.1 copy.38
  19.8 0.1 add.33
  19.9 0.0 copy-done.4
  19.9 0.0 copy-done.6
  19.9 0.0 copy-start.2
  19.9 0.0 copy-start.9
  20.0 0.0 copy-start.1
  20.0 4.1 %collective-permute-start = (f32[104,128]{1,0:T(8,128)S(1)}, f32[104,128]{1,0:T(8,128)S(1)}, u32[]{:S(2)}, u32[]{:S(2)}) collective-permute-start(f32[104,128]{1,0:T(8,128)S(1)} %get-tuple-element.25), channel_id=1, source_target_pairs={{0,8},{8,16},{16,24},{1,9},{9,17},{17,25},{2,10},{10,18},{18,26},{... | collective-permute-start | bytes 159752 | tf_op jit(solution)/shard_map/ppermute | solution.py:466
  24.1 1.3 %collective-permute-start.1 = (f32[104,128]{1,0:T(8,128)S(1)}, f32[104,128]{1,0:T(8,128)S(1)}, u32[]{:S(2)}, u32[]{:S(2)}) collective-permute-start(f32[104,128]{1,0:T(8,128)S(1)} %get-tuple-element.26), channel_id=1, source_target_pairs={{8,0},{16,8},{24,16},{9,1},{17,9},{25,17},{10,2},{18,10},{26,18},{... | collective-permute-start | bytes 159752 | tf_op jit(solution)/shard_map/ppermute | solution.py:467
  25.4 4.1 %all-to-all-done.got = f32[4,152,128]{2,1,0:T(8,128)S(1)} async-done(((f32[4,152,128]{2,1,0:T(8,128)}), f32[4,152,128]{2,1,0:T(8,128)S(1)}, u32[]{:S(2)}, u32[]{:S(2)}) %all-to-all-start) | async-done | bytes 311328 | tf_op jit(solution)/shard_map/all_to_all | solution.py:455
  29.5 0.1 convert_element_type.19.request
  29.6 0.0 collective-permute-done.low
  29.6 0.5 collective-permute-done.1.high
  30.1 2.5 %shard_map.133 = (f32[8,32,128]{2,1,0:T(8,128)}, f32[4,32,128]{2,1,0:T(8,128)}) custom-call(s32[32]{0:T(128)S(1)} %convert_element_type.19.request, f32[8,32,128]{2,1,0:T(8,128)S(1)} %copy-done.4, f32[8,32,128]{2,1,0:T(8,128)S(1)} %copy-done.6, f32[8,24,128]{2,1,0:T(8,128)S(1)} %all-to-all-done.1.got, f32[104,128]{1,0:T(8,128)S(1)} %collective-permute-done.low, ...), custom_call_target="tpu_custom_call" | custom-call | tf_op jit(solution)/shard_map/pallas_call | solution.py:469
  32.6 3.8 %all-to-all-start.2 = ((f32[4,32,128]{2,1,0:T(8,128)}), f32[4,32,128]{2,1,0:T(8,128)S(1)}, u32[]{:S(2)}, u32[]{:S(2)}) async-start(f32[4,32,128]{2,1,0:T(8,128)} %get-tuple-element.28), calls=%async_computation.2 | async-start | bytes 131072 | tf_op jit(solution)/shard_map/all_to_all | solution.py:475
  36.4 5.7 %all-to-all-done.2.blocks = f32[4,32,128]{2,1,0:T(8,128)S(1)} async-done(((f32[4,32,128]{2,1,0:T(8,128)}), f32[4,32,128]{2,1,0:T(8,128)S(1)}, u32[]{:S(2)}, u32[]{:S(2)}) %all-to-all-start.2) | async-done | bytes 65568 | tf_op jit(solution)/shard_map/all_to_all | solution.py:475
  42.1 0.0 copy-done.2
  42.1 0.0 copy-done.9
  42.1 0.0 copy-done.1
  42.1 0.0 copy-done.10
  42.1 1.8 %shard_map.134 = (f32[16,16,256]{2,1,0:T(8,128)S(1)}, f32[16,16,256]{2,1,0:T(8,128)S(1)}, f32[2,256,128]{2,1,0:T(8,128)S(1)}, f32[32,24,128]{2,1,0:T(8,128)S(1)}, f32[4,144,128]{2,1,0:T(8,128)S(1)}) custom-call(s32[96]{0:T(128)S(1)} %select_select_fusion.receive_index, s32[144]{0:T(256)S(1)} %reshape.107.send_index, s32[32]{0:T(128)S(1)} %pad_add_fusion.place, ...), custom_call_target="tpu_custom_call" | custom-call | tf_op jit(solution)/shard_map/pallas_call | solution.py:482
  44.0 10.1 %all_to_all.30.got = f32[4,144,128]{2,1,0:T(8,128)S(1)} all-to-all(f32[4,144,128]{2,1,0:T(8,128)S(1)} %get-tuple-element.33), channel_id=1, replica_groups=mesh['gx'=4,'gy'=2,'gz'=4] {'gx'}, dimensions={0} | all-to-all | bytes 589824 | tf_op jit(solution)/shard_map/all_to_all | solution.py:492
  54.1 1.5 %shard_map.135 = (f32[16,16,256]{2,1,0:T(8,128)S(1)}, f32[16,16,256]{2,1,0:T(8,128)S(1)}, f32[32,24,128]{2,1,0:T(8,128)S(1)}, f32[4,144,128]{2,1,0:T(8,128)S(1)}) custom-call(s32[96]{0:T(128)S(1)} %select_select_fusion.receive_index, s32[144]{0:T(256)S(1)} %reshape.107.send_index, f32[16,16,256]{2,1,0:T(8,128)S(1)} %get-tuple-element.30.phase, ...), custom_call_target="tpu_custom_call" | custom-call | tf_op jit(solution)/shard_map/pallas_call | solution.py:493
  55.7 10.2 %all_to_all.31.got = f32[4,144,128]{2,1,0:T(8,128)S(1)} all-to-all(f32[4,144,128]{2,1,0:T(8,128)S(1)} %get-tuple-element.37), channel_id=1, replica_groups=mesh['gx'=4,'gy'=2,'gz'=4] {'gx'}, dimensions={0} | all-to-all | bytes 589824 | tf_op jit(solution)/shard_map/all_to_all | solution.py:492
  65.8 1.6 %shard_map.136 = (f32[16,16,256]{2,1,0:T(8,128)S(1)}, f32[16,16,256]{2,1,0:T(8,128)S(1)}, f32[32,24,128]{2,1,0:T(8,128)S(1)}, f32[4,144,128]{2,1,0:T(8,128)S(1)}) custom-call(s32[96]{0:T(128)S(1)} %select_select_fusion.receive_index, s32[144]{0:T(256)S(1)} %reshape.107.send_index, f32[16,16,256]{2,1,0:T(8,128)S(1)} %get-tuple-element.35.phase, ...), custom_call_target="tpu_custom_call" | custom-call | tf_op jit(solution)/shard_map/pallas_call | solution.py:493
  67.4 10.1 %all_to_all.32.got = f32[4,144,128]{2,1,0:T(8,128)S(1)} all-to-all(f32[4,144,128]{2,1,0:T(8,128)S(1)} %get-tuple-element.41), channel_id=1, replica_groups=mesh['gx'=4,'gy'=2,'gz'=4] {'gx'}, dimensions={0} | all-to-all | bytes 589824 | tf_op jit(solution)/shard_map/all_to_all | solution.py:496
  77.5 2.0 %shard_map.137 = (f32[16,16,256]{2,1,0:T(8,128)}, f32[16,16,256]{2,1,0:T(8,128)}) custom-call(s32[96]{0:T(128)S(1)} %select_select_fusion.receive_index, f32[16,16,256]{2,1,0:T(8,128)S(1)} %get-tuple-element.39.phase, f32[16,16,256]{2,1,0:T(8,128)S(1)} %get-tuple-element.40.solute, f32[2,256,128]{2,1,0:T(8,128)S(1)} %get-tuple-element.32.heat, ...), custom_call_target="tpu_custom_call" | custom-call | tf_op jit(solution)/shard_map/pallas_call | solution.py:497
  (16 shorter events, 0.1 us)
Async XLA Ops:
  0.6 9.4 %copy-start = (bf16[1024,256]{1,0:T(8,128)(2,1)S(1)}, bf16[1024,256]{1,0:T(8,128)(2,1)}, u32[]{:S(2)}) copy-start(bf16[1024,256]{1,0:T(8,128)(2,1)} %constant.28.clone.picks) | copy-start | bytes 1572868
  0.6 1.0 %copy-start.3 = (f32[8,32,128]{2,1,0:T(8,128)S(1)}, f32[8,32,128]{2,1,0:T(8,128)}, u32[]{:S(2)}) copy-start(f32[8,32,128]{2,1,0:T(8,128)} %h.5) | copy-start | bytes 393220
  1.6 0.9 %copy-start.5 = (f32[8,32,128]{2,1,0:T(8,128)S(1)}, f32[8,32,128]{2,1,0:T(8,128)}, u32[]{:S(2)}) copy-start(f32[8,32,128]{2,1,0:T(8,128)} %k.5) | copy-start | bytes 393220
  2.5 6.2 %copy-start.12 = (s32[1,1,1,16,6]{3,2,4,1,0:T(1,128)S(1)}, s32[1,1,1,16,6]{3,2,4,1,0:T(1,128)}, u32[]{:S(2)}) copy-start(s32[1,1,1,16,6]{3,2,4,1,0:T(1,128)} %param.17) | copy-start | bytes 1156
  2.5 6.3 %copy-start.13 = (s32[1,1,1,16,1]{3,4,2,1,0:T(1,128)S(1)}, s32[1,1,1,16,1]{3,4,2,1,0:T(1,128)}, u32[]{:S(2)}) copy-start(s32[1,1,1,16,1]{3,4,2,1,0:T(1,128)} %param.15) | copy-start | bytes 196
  3.4 6.6 %copy-start.7 = (f32[1,1,1,16,16,256]{5,4,3,2,1,0:T(8,128)S(1)}, f32[1,1,1,16,16,256]{5,4,3,2,1,0:T(8,128)}, u32[]{:S(2)}) copy-start(f32[1,1,1,16,16,256]{5,4,3,2,1,0:T(8,128)} %param.13) | copy-start | bytes 786436
  3.4 10.5 %all-to-all-start.1 = ((f32[8,24,128]{2,1,0:T(8,128)}), f32[8,24,128]{2,1,0:T(8,128)S(1)}, u32[]{:S(2)}, u32[]{:S(2)}) async-start(f32[8,24,128]{2,1,0:T(8,128)} %shard_map.131), calls=%async_computation.1 | async-start | bytes 196608 | tf_op jit(solution)/shard_map/all_to_all | solution.py:435
  10.0 0.7 copy-start.11
  10.7 0.9 %copy-start.8 = (f32[1,1,1,16,16,256]{5,4,3,2,1,0:T(8,128)S(1)}, f32[1,1,1,16,16,256]{5,4,3,2,1,0:T(8,128)}, u32[]{:S(2)}) copy-start(f32[1,1,1,16,16,256]{5,4,3,2,1,0:T(8,128)} %param.14) | copy-start | bytes 786436
  13.9 6.0 %copy-start.4 = (f32[8,32,128]{2,1,0:T(8,128)S(1)}, f32[8,32,128]{2,1,0:T(8,128)}, u32[]{:S(2)}) copy-start(f32[8,32,128]{2,1,0:T(8,128)} %h.5) | copy-start | bytes 393220
  13.9 6.0 %copy-start.6 = (f32[8,32,128]{2,1,0:T(8,128)S(1)}, f32[8,32,128]{2,1,0:T(8,128)}, u32[]{:S(2)}) copy-start(f32[8,32,128]{2,1,0:T(8,128)} %k.5) | copy-start | bytes 393220
  13.9 15.5 %all-to-all-start = ((f32[4,152,128]{2,1,0:T(8,128)}), f32[4,152,128]{2,1,0:T(8,128)S(1)}, u32[]{:S(2)}, u32[]{:S(2)}) async-start(f32[4,152,128]{2,1,0:T(8,128)} %get-tuple-element.24._), calls=%async_computation | async-start | bytes 622592 | tf_op jit(solution)/shard_map/all_to_all | solution.py:455
  19.9 22.2 %copy-start.2 = (bf16[768,256]{1,0:T(8,128)(2,1)S(1)}, bf16[768,256]{1,0:T(8,128)(2,1)}, u32[]{:S(2)}) copy-start(bf16[768,256]{1,0:T(8,128)(2,1)} %constant.29.clone.lap0) | copy-start | bytes 1179652
  19.9 22.2 %copy-start.9 = (f32[1,1,1,16,16,256]{5,4,3,2,1,0:T(8,128)S(1)}, f32[1,1,1,16,16,256]{5,4,3,2,1,0:T(8,128)}, u32[]{:S(2)}) copy-start(f32[1,1,1,16,16,256]{5,4,3,2,1,0:T(8,128)} %param.14) | copy-start | bytes 786436
  20.0 22.1 %copy-start.1 = (bf16[768,256]{1,0:T(8,128)(2,1)S(1)}, bf16[768,256]{1,0:T(8,128)(2,1)}, u32[]{:S(2)}) copy-start(bf16[768,256]{1,0:T(8,128)(2,1)} %constant.30.clone.lap1) | copy-start | bytes 1179652
  20.0 9.6 %collective-permute-start = (f32[104,128]{1,0:T(8,128)S(1)}, f32[104,128]{1,0:T(8,128)S(1)}, u32[]{:S(2)}, u32[]{:S(2)}) collective-permute-start(f32[104,128]{1,0:T(8,128)S(1)} %get-tuple-element.25), channel_id=1, source_target_pairs={{0,8},{8,16},{16,24},{1,9},{9,17},{17,25},{2,10},{10,18},{18,26},{... | collective-permute-start | bytes 159752 | tf_op jit(solution)/shard_map/ppermute | solution.py:466
  24.1 6.0 %collective-permute-start.1 = (f32[104,128]{1,0:T(8,128)S(1)}, f32[104,128]{1,0:T(8,128)S(1)}, u32[]{:S(2)}, u32[]{:S(2)}) collective-permute-start(f32[104,128]{1,0:T(8,128)S(1)} %get-tuple-element.26), channel_id=1, source_target_pairs={{8,0},{16,8},{24,16},{9,1},{17,9},{25,17},{10,2},{18,10},{26,18},{... | collective-permute-start | bytes 159752 | tf_op jit(solution)/shard_map/ppermute | solution.py:467
  32.6 9.5 %copy-start.10 = (bf16[256,256]{1,0:T(8,128)(2,1)S(1)}, bf16[256,256]{1,0:T(8,128)(2,1)}, u32[]{:S(2)}) copy-start(bf16[256,256]{1,0:T(8,128)(2,1)} %constant.31.clone.spreads) | copy-start | bytes 393220
  32.6 9.5 %all-to-all-start.2 = ((f32[4,32,128]{2,1,0:T(8,128)}), f32[4,32,128]{2,1,0:T(8,128)S(1)}, u32[]{:S(2)}, u32[]{:S(2)}) async-start(f32[4,32,128]{2,1,0:T(8,128)} %get-tuple-element.28), calls=%async_computation.2 | async-start | bytes 131072 | tf_op jit(solution)/shard_map/all_to_all | solution.py:475

commit v2 on v1

--- a/solution.py
+++ b/solution.py
@@ -26,6 +26,7 @@
 BF16 = jnp.bfloat16
 VMEM = pl.BlockSpec(memory_space=pltpu.VMEM)
 SMEM = pl.BlockSpec(memory_space=pltpu.SMEM)
+HBM = pl.BlockSpec(memory_space=pltpu.HBM)
 PARAMS = pltpu.CompilerParams(vmem_limit_bytes=16 * 1024 * 1024)
 
 
@@ -122,10 +123,34 @@
     ]
 
 
-def sides_kernel(sizes, h, k, send):
+def ask(sources, wanted, asked, place):
+    lane = iota(asked.shape[1:], 1)
+    ranks = []
+    for slot in range(SLOTS):
+        alike = [jnp.where(sources[other] == sources[slot], 1, 0) for other in range(slot)]
+        ranks.append(sum(alike, jnp.int32(0)))
+        place[slot] = sources[slot]
+        place[SLOTS + slot] = ranks[slot]
+    for owner in range(asked.shape[0]):
+        row = jnp.zeros(lane.shape, jnp.int32)
+        for slot in range(SLOTS):
+            row = jnp.where(lane == jnp.where(sources[slot] == owner, ranks[slot], -1), wanted[slot], row)
+        asked[owner] = row
+
+
+def sides_kernel(sizes, sources, wanted, h_far, k_far, send, asked, place, h, k, sems):
     ny, nz = sizes
     my_y, my_z = lax.axis_index("gy"), lax.axis_index("gz")
     bx = h.shape[0]
+    copies = []
+    for x in range(bx):
+        copies.append(pltpu.make_async_copy(h_far.at[x], h.at[x], sems.at[x]))
+        copies.append(pltpu.make_async_copy(k_far.at[x], k.at[x], sems.at[bx + x]))
+    for copy in copies:
+        copy.start()
+    ask(sources, wanted, asked, place)
+    for copy in copies:
+        copy.wait()
     blocks = side_blocks(h[...], k[...])
     for y in range(ny):
         for z in range(nz):
@@ -150,7 +175,7 @@
     return read
 
 
-def layers_kernel(sizes, h, k, got, _, low, high):
+def layers_kernel(sizes, h, k, got, low, high):
     bx, by, bz = h.shape
     read = side_reader(sizes, got, bx)
     around = [read(-1, 0), read(1, 0), read(0, -1), read(0, 1)]
@@ -179,7 +204,7 @@
     return h + RATE * k * (total - 6.0 * t)
 
 
-def heat_kernel(cap, sizes, request, h, k, got, low, high, out, send, held):
+def heat_kernel(cap, sizes, request, h, k, got, low, high, packed, out, send, held):
     bx, by, bz = h.shape
     h0, k0 = h[...], k[...]
     read = side_reader(sizes, got, bx)
@@ -233,7 +258,9 @@
                 patch = held[pl.ds(a * CB + part * deep, deep), b]
                 moved = pltpu.roll(patch, (CB * at - CB * c + bz) % bz, 2)
                 total = jnp.where(group == at, moved, total)
-        send[owner] = total.reshape(deep * CB, bz)
+        behind = packed.shape[1]
+        send[owner, 0:behind, :] = packed[owner]
+        send[owner, behind:, :] = total.reshape(deep * CB, bz)
 
 
 def write_records(phase, solute, picks, own):
@@ -273,27 +300,20 @@
         send[owner, row + TE : row + REC, :] = edge
 
 
-def first_pack_kernel(send_index, place, wanted, phase, solute, picks, own, send):
+def first_pack_kernel(send_index, phase, solute, picks, own, send):
     write_records(phase[...], solute[...], picks[...], own)
     pack(own, send_index, send)
-    count, rows, _ = send.shape
-    lane = iota((8, 128), 1)
-    for owner in range(count):
-        asked = jnp.zeros((8, 128), F32)
-        for slot in range(SLOTS):
-            here = jnp.where(place[slot] == owner, place[SLOTS + slot], -1)
-            asked = jnp.where(lane == here, wanted[slot].astype(F32), asked)
-        send[owner, rows - 8 : rows, :] = asked
-
-
-def take_heat(cap, place, blocks, spreads, held, heat):
+
+
+def take_heat(cap, place, got, spreads, held, heat):
     parts, deep = block_layout(cap)
+    first = got.shape[1] - deep * CB
     group = iota((CB, 128), 1) // CB
     for slot in range(SLOTS):
         source, rank = place[slot], place[SLOTS + slot]
         for x in range(CB):
-            row = (x % deep) * CB
-            patch = blocks[source, row : row + CB, :]
+            row = first + (x % deep) * CB
+            patch = got[source, row : row + CB, :]
             held[slot * CB + x] = jnp.where(group == rank * parts + x // deep, patch, 0.0)
     rows = held[...].reshape(SLOTS * CB * CB, 128)
     wide = dot(jnp.concatenate(halves(rows), axis=1), spreads)
@@ -343,10 +363,12 @@
 
 
 def first_step_kernel(
-    cap, receive_index, send_index, place, phase, solute, blocks, got, own, picks, lap0, lap1, spreads,
-    phase_out, solute_out, heat_out, own_out, send, all_records, ghosts, held,
+    cap, receive_index, send_index, place, phase, solute, got, own, picks, lap0, lap1, spreads, brick,
+    phase_out, solute_out, heat_out, own_out, send, brick_out, all_records, ghosts, held, sem,
 ):
-    take_heat(cap, place, blocks, spreads[...], held, heat_out)
+    copy = pltpu.make_async_copy(brick, brick_out, sem)
+    copy.start()
+    take_heat(cap, place, got, spreads[...], held, heat_out)
     new_phase, new_solute = step(
         receive_index, phase[...], solute[...], heat_out[...], got, own, (lap0[...], lap1[...]),
         all_records, ghosts,
@@ -355,6 +377,7 @@
     solute_out[...] = new_solute
     write_records(new_phase, new_solute, picks[...], own_out)
     pack(own_out, send_index, send)
+    copy.wait()
 
 
 def middle_step_kernel(
@@ -382,12 +405,12 @@
     solute_out[...] = new_solute
 
 
-def call(kernel, in_specs, out_shapes, scratch=()):
+def call(kernel, in_specs, out_shapes, scratch=(), out_specs=None):
     return pl.pallas_call(
         kernel,
         out_shape=out_shapes,
         in_specs=in_specs,
-        out_specs=jax.tree.map(lambda _: VMEM, out_shapes),
+        out_specs=out_specs or jax.tree.map(lambda _: VMEM, out_shapes),
         scratch_shapes=list(scratch),
         compiler_params=PARAMS,
     )
@@ -429,64 +452,66 @@
     bx, by, bz = enthalpy.shape
     picks, lap0, lap1, spreads = tables()
 
-    sides = call(
-        functools.partial(sides_kernel, sizes), [VMEM] * 2, shape(sizes[0] * sizes[1], 3 * bx, 128)
-    )(enthalpy, conductivity)
-    sides = lax.all_to_all(sides, ("gy", "gz"), split_axis=0, concat_axis=0, tiled=True)
-
     sources = tile_source.reshape(SLOTS)
     wanted = tile_block.reshape(SLOTS)
-    slot = jnp.arange(SLOTS, dtype=jnp.int32)
-    ranks = jnp.sum(
-        ((sources[None] == sources[:, None]) & (slot[None] < slot[:, None])).astype(jnp.int32), axis=1
-    )
-    place = jnp.concatenate([sources, ranks])
+    integers = jax.ShapeDtypeStruct((count, 8, 128), jnp.int32)
+    sides, asked, place = call(
+        functools.partial(sides_kernel, sizes),
+        [SMEM] * 2 + [HBM] * 2,
+        [
+            shape(sizes[0] * sizes[1], 3 * bx, 128),
+            integers,
+            jax.ShapeDtypeStruct((2 * SLOTS,), jnp.int32),
+        ],
+        [pltpu.VMEM((bx, by, bz), F32)] * 2 + [pltpu.SemaphoreType.DMA((2 * bx,))],
+        [VMEM, VMEM, SMEM],
+    )(sources, wanted, enthalpy, conductivity)
+    sides = lax.all_to_all(sides, ("gy", "gz"), split_axis=0, concat_axis=0, tiled=True)
+    asked = lax.all_to_all(asked, "gx", split_axis=0, concat_axis=0, tiled=True)
+    request = asked[:, 0, :block_cap].reshape(-1)
+
     neighbour = tile_neighbour.reshape(SLOTS, FACES)
     receive_index, send_index = tile_indices(neighbour, plane_cap, me)
     phase_field = phase.reshape(SLOTS, TE, PLANE)
     solute_field = solute.reshape(SLOTS, TE, PLANE)
     records = count * plane_cap
     own_shape, send_shape = shape(2 * SLOTS, REC, 128), shape(count, plane_cap * REC, 128)
-    own, send = call(
-        first_pack_kernel,
-        [SMEM] * 3 + [VMEM] * 3,
-        [own_shape, shape(count, plane_cap * REC + 8, 128)],
-    )(send_index, place, wanted, phase_field, solute_field, picks)
-    got = lax.all_to_all(send, "gx", split_axis=0, concat_axis=0, tiled=True)
-    request = got[:, plane_cap * REC, :block_cap].astype(jnp.int32).reshape(-1)
+    own, packed = call(first_pack_kernel, [SMEM] + [VMEM] * 3, [own_shape, send_shape])(
+        send_index, phase_field, solute_field, picks
+    )
 
     layer = shape(3 * by + 8, bz)
-    low, high = call(
-        functools.partial(layers_kernel, sizes),
-        [VMEM] * 3 + [pl.BlockSpec(memory_space=pl.ANY)],
-        [layer, layer],
-    )(enthalpy, conductivity, sides, send)
+    low, high = call(functools.partial(layers_kernel, sizes), [VMEM] * 3, [layer, layer])(
+        enthalpy, conductivity, sides
+    )
     forward = [(i, i + 1) for i in range(count - 1)]
     backward = [(b, a) for a, b in forward]
     from_low = lax.ppermute(high, "gx", forward)
     from_high = lax.ppermute(low, "gx", backward)
     _, deep = block_layout(block_cap)
-    heat_out, found = call(
+    brick = shape(bx, by, bz)
+    heated, send = call(
         functools.partial(heat_kernel, block_cap, sizes),
-        [SMEM] + [VMEM] * 5,
-        [shape(bx, by, bz), shape(count, deep * CB, bz)],
+        [SMEM] + [VMEM] * 6,
+        [brick, shape(count, plane_cap * REC + deep * CB, 128)],
         [pltpu.VMEM((bx, by // CB, CB, bz), F32)],
-    )(request, enthalpy, conductivity, sides, from_low, from_high)
-    blocks = lax.all_to_all(found, "gx", split_axis=0, concat_axis=0, tiled=True)
+    )(request, enthalpy, conductivity, sides, from_low, from_high, packed)
+    got = lax.all_to_all(send, "gx", split_axis=0, concat_axis=0, tiled=True)
 
     field = shape(SLOTS, TE, PLANE)
     step_scratch = [
         pltpu.VMEM((records + 2 * SLOTS, REC, 128), F32),
         pltpu.VMEM((SLOTS, REC, 128), F32),
     ]
-    phase_field, solute_field, heat, own, send = call(
+    phase_field, solute_field, heat, own, send, heat_out = call(
         functools.partial(first_step_kernel, block_cap),
         [SMEM] * 3 + [VMEM] * 9,
-        [field, field, shape(2, SLOTS * TE, 128), own_shape, send_shape],
-        step_scratch + [pltpu.VMEM((SLOTS * CB, CB, 128), F32)],
+        [field, field, shape(2, SLOTS * TE, 128), own_shape, send_shape, brick],
+        step_scratch + [pltpu.VMEM((SLOTS * CB, CB, 128), F32), pltpu.SemaphoreType.DMA],
+        [VMEM] * 5 + [HBM],
     )(
-        receive_index, send_index, place, phase_field, solute_field, blocks, got, own, picks, lap0, lap1,
-        spreads,
+        receive_index, send_index, place, phase_field, solute_field, got, own, picks, lap0, lap1, spreads,
+        heated,
     )
     for _ in range(PHASE_STEPS - 2):
         got = lax.all_to_all(send, "gx", split_axis=0, concat_axis=0, tiled=True)

time: 80.2 us -> 89.6 us (1.12)
  waiting for transfers between devices: 10.9 us -> 15.1 us
  local copies, waits for them, and re-layouts: 4.97 us -> 7.58 us
  Pallas kernels: 12.2 us -> 13.5 us
  other arithmetic: 0.78 us -> 1.86 us
    all_to_all x1, waiting for transfers between devices: 5.74 us -> 0.01 us  [local(): asked = lax.all_to_all(asked, 'gx', split_axis=0, concat_axis=0, tiled=True)]
    all_to_all x1, waiting for transfers between devices: 4.12 us -> 8.08 us  [local(): got = lax.all_to_all(send, 'gx', split_axis=0, concat_axis=0, tiled=True)]
    ppermute x1, waiting for transfers between devices: 0.5 us -> 4.26 us  [local(): from_high = lax.ppermute(low, 'gx', backward)]
    unnamed x29 -> x31, local copies, waits for them, and re-layouts: 3.51 us -> 6.11 us
    all_to_all x1, waiting for transfers between devices: 0.54 us -> 2.42 us  [local(): lax.all_to_all(sides, ('gy', 'gz'), split_axis=0, concat_axis=0, tiled=True)]
    all_to_all x1, starting transfers between devices: 5 us -> 3.76 us  [local(): got = lax.all_to_all(send, 'gx', split_axis=0, concat_axis=0, tiled=True)]
    all_to_all x1, starting transfers between devices: 3.76 us -> 4.87 us  [local(): asked = lax.all_to_all(asked, 'gx', split_axis=0, concat_axis=0, tiled=True)]
  transfers between devices with their start and end apart: 5 -> 5, of which waited for: 4 -> 4; matrix products, arithmetic and copies ran while one was open for 3% -> 5% of each run, Pallas kernels for 2% -> 1%
where the time goes in v2:
time: 89.6 us; the launch traced here: 88.5 us
  blocking collectives  30.6 us (34%)
  starting transfers between devices  19 us (21%)
  waiting for transfers between devices  15.1 us (17%)
  Pallas kernels  13.5 us (15%)
  local copies, waits for them, and re-layouts  7.58 us (8%)
  other arithmetic  1.86 us (2%)
    all_to_all x3, blocking collectives, local(): got = lax.all_to_all(send, 'gx', split_axis=0, concat_axis=0, tiled=True)  30.6 us
    all_to_all x1, waiting for transfers between devices, local(): got = lax.all_to_all(send, 'gx', split_axis=0, concat_axis=0, tiled=True)  8.08 us
    unnamed x31, local copies, waits for them, and re-layouts  6.11 us
    all_to_all x1, starting transfers between devices, local(): lax.all_to_all(sides, ('gy', 'gz'), split_axis=0, concat_axis=0, tiled=True)  5.18 us
    all_to_all x1, starting transfers between devices, local(): asked = lax.all_to_all(asked, 'gx', split_axis=0, concat_axis=0, tiled=True)  4.87 us
    ppermute x1, waiting for transfers between devices, local(): from_high = lax.ppermute(low, 'gx', backward)  4.26 us
    ppermute x1, starting transfers between devices, local(): from_low = lax.ppermute(high, 'gx', forward)  3.93 us
    all_to_all x1, starting transfers between devices, local(): got = lax.all_to_all(send, 'gx', split_axis=0, concat_axis=0, tiled=True)  3.76 us
  transfers between devices with their start and end apart: 5, of which 4 were waited for; matrix products, arithmetic and copies ran while one was open for 5% of the time, Pallas kernels for 1%

profile of v2, /device:TPU:0, one launch (start us, length us, event | category | flops | bytes accessed | tf_op | source)
XLA Modules:
  0.0 88.5 jit_solution(17255670574095420300)
XLA Ops:
  0.6 0.0 copy-start
  0.6 0.0 copy-start.3
  0.7 1.0 %copy-done.3 = f32[8,32,128]{2,1,0:T(8,128)S(1)} copy-done((f32[8,32,128]{2,1,0:T(8,128)S(1)}, f32[8,32,128]{2,1,0:T(8,128)}, u32[]{:S(2)}) %copy-start.3) | copy-done | bytes 131096
  1.6 0.0 copy-start.5
  1.6 0.9 %copy-done.5 = f32[8,32,128]{2,1,0:T(8,128)S(1)} copy-done((f32[8,32,128]{2,1,0:T(8,128)S(1)}, f32[8,32,128]{2,1,0:T(8,128)}, u32[]{:S(2)}) %copy-start.5) | copy-done | bytes 131096
  2.5 0.0 copy-start.12
  2.5 0.7 copy-done.12
  3.2 0.0 copy-start.13
  3.2 0.7 copy-done.13
  3.8 2.2 %shard_map.130 = (f32[8,24,128]{2,1,0:T(8,128)}, s32[4,8,128]{2,1,0:T(8,128)}, s32[32]{0:T(128)S(1)}) custom-call(s32[16]{0:T(128)S(1)} %bitcast.31, s32[16]{0:T(128)S(1)} %bitcast.32, f32[8,32,128]{2,1,0:T(8,128)S(1)} %copy-done.3, f32[8,32,128]{2,1,0:T(8,128)S(1)} %copy-done.5), custom_call_target="tpu_custom_call" | custom-call | tf_op jit(solution)/shard_map/pallas_call | solution.py:458
  6.0 5.2 %all-to-all-start.1 = ((f32[8,24,128]{2,1,0:T(8,128)}), f32[8,24,128]{2,1,0:T(8,128)S(1)}, u32[]{:S(2)}, u32[]{:S(2)}) async-start(f32[8,24,128]{2,1,0:T(8,128)} %get-tuple-element.30), calls=%async_computation.1 | async-start | bytes 196608 | tf_op jit(solution)/shard_map/all_to_all | solution.py:469
  11.2 0.7 copy.51
  11.9 0.7 broadcast_shift-right-arithmetic_fusion
  12.6 0.7 compare_and_fusion.1
  13.3 0.4 convert_reduce_fusion
  13.7 0.3 copy-done.14
  14.0 2.4 %all-to-all-done.1.got = f32[8,24,128]{2,1,0:T(8,128)S(1)} async-done(((f32[8,24,128]{2,1,0:T(8,128)}), f32[8,24,128]{2,1,0:T(8,128)S(1)}, u32[]{:S(2)}, u32[]{:S(2)}) %all-to-all-start.1) | async-done | bytes 98336 | tf_op jit(solution)/shard_map/all_to_all | solution.py:469
  16.4 4.9 %all-to-all-start = ((s32[4,8,128]{2,1,0:T(8,128)}), s32[4,8,128]{2,1,0:T(8,128)S(1)}, u32[]{:S(2)}, u32[]{:S(2)}) async-start(s32[4,8,128]{2,1,0:T(8,128)} %get-tuple-element.29), calls=%async_computation | async-start | bytes 32768 | tf_op jit(solution)/shard_map/all_to_all | solution.py:470
  21.3 0.1 select_reduce_fusion
  21.4 0.1 copy.36
  21.5 0.1 eq.40
  21.6 0.1 copy.35
  21.7 0.1 lt.39
  21.8 0.1 copy.40
  21.9 0.2 reshape.102.send_index
  22.1 0.0 copy-done
  22.1 0.0 copy-start.7
  22.1 0.9 %copy-done.7 = f32[1,1,1,16,16,256]{5,4,3,2,1,0:T(8,128)S(1)} copy-done((f32[1,1,1,16,16,256]{5,4,3,2,1,0:T(8,128)S(1)}, f32[1,1,1,16,16,256]{5,4,3,2,1,0:T(8,128)}, u32[]{:S(2)}) %copy-start.7) | copy-done | bytes 262168
  23.1 0.0 copy-start.9
  23.1 0.9 %copy-done.9 = f32[1,1,1,16,16,256]{5,4,3,2,1,0:T(8,128)S(1)} copy-done((f32[1,1,1,16,16,256]{5,4,3,2,1,0:T(8,128)S(1)}, f32[1,1,1,16,16,256]{5,4,3,2,1,0:T(8,128)}, u32[]{:S(2)}) %copy-start.9) | copy-done | bytes 262168
  24.0 0.0 copy-start.4
  24.0 0.0 copy-start.6
  24.0 1.0 %shard_map.132 = (f32[32,24,128]{2,1,0:T(8,128)S(1)}, f32[4,144,128]{2,1,0:T(8,128)S(1)}) custom-call(s32[144]{0:T(256)S(1)} %reshape.102.send_index, f32[16,16,256]{2,1,0:T(8,128)S(1)} %bitcast.27, f32[16,16,256]{2,1,0:T(8,128)S(1)} %bitcast.29, bf16[1024,256]{1,0:T(8,128)(2,1)S(1)} %copy-done), custom_call_target="tpu_custom_call" | custom-call | tf_op jit(solution)/shard_map/pallas_call | solution.py:479
  25.0 0.0 copy-done.4
  25.0 0.0 copy-done.6
  25.0 3.9 %collective-permute-start = (f32[104,128]{1,0:T(8,128)S(1)}, f32[104,128]{1,0:T(8,128)S(1)}, u32[]{:S(2)}, u32[]{:S(2)}) collective-permute-start(f32[104,128]{1,0:T(8,128)S(1)} %get-tuple-element.31), channel_id=1, source_target_pairs={{0,8},{8,16},{16,24},{1,9},{9,17},{17,25},{2,10},{10,18},{18,26},{... | collective-permute-start | bytes 159752 | tf_op jit(solution)/shard_map/ppermute | solution.py:489
  29.0 1.3 %collective-permute-start.1 = (f32[104,128]{1,0:T(8,128)S(1)}, f32[104,128]{1,0:T(8,128)S(1)}, u32[]{:S(2)}, u32[]{:S(2)}) collective-permute-start(f32[104,128]{1,0:T(8,128)S(1)} %get-tuple-element.32), channel_id=1, source_target_pairs={{8,0},{16,8},{24,16},{9,1},{17,9},{25,17},{10,2},{18,10},{26,18},{... | collective-permute-start | bytes 159752 | tf_op jit(solution)/shard_map/ppermute | solution.py:490
  30.3 0.0 all-to-all-done
  30.3 0.1 reshape_squeeze.3.request
  30.4 0.4 collective-permute-done.low
  30.8 4.3 %collective-permute-done.1.high = f32[104,128]{1,0:T(8,128)S(1)} collective-permute-done((f32[104,128]{1,0:T(8,128)S(1)}, f32[104,128]{1,0:T(8,128)S(1)}, u32[]{:S(2)}, u32[]{:S(2)}) %collective-permute-start.1) | collective-permute-done | bytes 53280 | tf_op jit(solution)/shard_map/ppermute | solution.py:490
  35.0 2.6 %shard_map.133 = (f32[8,32,128]{2,1,0:T(8,128)S(1)}, f32[4,176,128]{2,1,0:T(8,128)}) custom-call(s32[32]{0:T(128)S(1)} %reshape_squeeze.3.request, f32[8,32,128]{2,1,0:T(8,128)S(1)} %copy-done.4, f32[8,32,128]{2,1,0:T(8,128)S(1)} %copy-done.6, f32[8,24,128]{2,1,0:T(8,128)S(1)} %all-to-all-done.1.got, f32[104,128]{1,0:T(8,128)S(1)} %collective-permute-done.low, ...), custom_call_target="tpu_custom_call" | custom-call | tf_op jit(solution)/shard_map/pallas_call | solution.py:493
  37.6 3.8 %all-to-all-start.2 = ((f32[4,176,128]{2,1,0:T(8,128)}), f32[4,176,128]{2,1,0:T(8,128)S(1)}, u32[]{:S(2)}, u32[]{:S(2)}) async-start(f32[4,176,128]{2,1,0:T(8,128)} %get-tuple-element.34), calls=%async_computation.2 | async-start | bytes 720896 | tf_op jit(solution)/shard_map/all_to_all | solution.py:499
  41.4 0.1 copy.38
  41.5 0.1 mul.15
  41.6 0.1 broadcast_in_dim.35
  41.7 0.1 broadcast_in_dim.36
  41.7 0.1 copy.37
  41.8 0.1 add.32
  41.9 0.1 copy.39
  42.0 0.1 reduce_sum.30
  42.1 8.1 %all-to-all-done.2.got = f32[4,176,128]{2,1,0:T(8,128)S(1)} async-done(((f32[4,176,128]{2,1,0:T(8,128)}), f32[4,176,128]{2,1,0:T(8,128)S(1)}, u32[]{:S(2)}, u32[]{:S(2)}) %all-to-all-start.2) | async-done | bytes 360480 | tf_op jit(solution)/shard_map/all_to_all | solution.py:499
  50.2 0.0 copy-done.8
  50.2 0.0 copy-done.10
  50.2 0.0 copy-done.11
  50.2 0.0 copy-done.1
  50.2 0.0 copy-done.2
  50.2 2.5 %shard_map.134 = (f32[16,16,256]{2,1,0:T(8,128)S(1)}, f32[16,16,256]{2,1,0:T(8,128)S(1)}, f32[2,256,128]{2,1,0:T(8,128)S(1)}, f32[32,24,128]{2,1,0:T(8,128)S(1)}...) custom-call(s32[96]{0:T(128)S(1)} %select_select_fusion.receive_index, s32[144]{0:T(256)S(1)} %reshape.102.send_index, ...), custom_call_target="tpu_custom_call" | custom-call | tf_op jit(solution)/shard_map/pallas_call | solution.py:506
  52.8 10.3 %all_to_all.30.got = f32[4,144,128]{2,1,0:T(8,128)S(1)} all-to-all(f32[4,144,128]{2,1,0:T(8,128)S(1)} %get-tuple-element.41), channel_id=1, replica_groups=mesh['gx'=4,'gy'=2,'gz'=4] {'gx'}, dimensions={0} | all-to-all | bytes 589824 | tf_op jit(solution)/shard_map/all_to_all | solution.py:517
  63.0 1.6 %shard_map.135 = (f32[16,16,256]{2,1,0:T(8,128)S(1)}, f32[16,16,256]{2,1,0:T(8,128)S(1)}, f32[32,24,128]{2,1,0:T(8,128)S(1)}, f32[4,144,128]{2,1,0:T(8,128)S(1)}) custom-call(s32[96]{0:T(128)S(1)} %select_select_fusion.receive_index, s32[144]{0:T(256)S(1)} %reshape.102.send_index, f32[16,16,256]{2,1,0:T(8,128)S(1)} %get-tuple-element.38.phase, ...), custom_call_target="tpu_custom_call" | custom-call | tf_op jit(solution)/shard_map/pallas_call | solution.py:518
  64.6 10.2 %all_to_all.31.got = f32[4,144,128]{2,1,0:T(8,128)S(1)} all-to-all(f32[4,144,128]{2,1,0:T(8,128)S(1)} %get-tuple-element.45), channel_id=1, replica_groups=mesh['gx'=4,'gy'=2,'gz'=4] {'gx'}, dimensions={0} | all-to-all | bytes 589824 | tf_op jit(solution)/shard_map/all_to_all | solution.py:517
  74.8 1.6 %shard_map.136 = (f32[16,16,256]{2,1,0:T(8,128)S(1)}, f32[16,16,256]{2,1,0:T(8,128)S(1)}, f32[32,24,128]{2,1,0:T(8,128)S(1)}, f32[4,144,128]{2,1,0:T(8,128)S(1)}) custom-call(s32[96]{0:T(128)S(1)} %select_select_fusion.receive_index, s32[144]{0:T(256)S(1)} %reshape.102.send_index, f32[16,16,256]{2,1,0:T(8,128)S(1)} %get-tuple-element.43.phase, ...), custom_call_target="tpu_custom_call" | custom-call | tf_op jit(solution)/shard_map/pallas_call | solution.py:518
  76.4 10.2 %all_to_all.32.got = f32[4,144,128]{2,1,0:T(8,128)S(1)} all-to-all(f32[4,144,128]{2,1,0:T(8,128)S(1)} %get-tuple-element.49), channel_id=1, replica_groups=mesh['gx'=4,'gy'=2,'gz'=4] {'gx'}, dimensions={0} | all-to-all | bytes 589824 | tf_op jit(solution)/shard_map/all_to_all | solution.py:521
  86.5 2.0 %shard_map.137 = (f32[16,16,256]{2,1,0:T(8,128)}, f32[16,16,256]{2,1,0:T(8,128)}) custom-call(s32[96]{0:T(128)S(1)} %select_select_fusion.receive_index, f32[16,16,256]{2,1,0:T(8,128)S(1)} %get-tuple-element.47.phase, f32[16,16,256]{2,1,0:T(8,128)S(1)} %get-tuple-element.48.solute, f32[2,256,128]{2,1,0:T(8,128)S(1)} %get-tuple-element.40.heat, ...), custom_call_target="tpu_custom_call" | custom-call | tf_op jit(solution)/shard_map/pallas_call | solution.py:522
  (16 shorter events, 0.1 us)
Async XLA Ops:
  0.6 21.5 %copy-start = (bf16[1024,256]{1,0:T(8,128)(2,1)S(1)}, bf16[1024,256]{1,0:T(8,128)(2,1)}, u32[]{:S(2)}) copy-start(bf16[1024,256]{1,0:T(8,128)(2,1)} %constant.28.clone.picks) | copy-start | bytes 1572868
  0.6 1.0 %copy-start.3 = (f32[8,32,128]{2,1,0:T(8,128)S(1)}, f32[8,32,128]{2,1,0:T(8,128)}, u32[]{:S(2)}) copy-start(f32[8,32,128]{2,1,0:T(8,128)} %h.3) | copy-start | bytes 393220
  1.6 0.9 %copy-start.5 = (f32[8,32,128]{2,1,0:T(8,128)S(1)}, f32[8,32,128]{2,1,0:T(8,128)}, u32[]{:S(2)}) copy-start(f32[8,32,128]{2,1,0:T(8,128)} %k.3) | copy-start | bytes 393220
  2.5 0.7 copy-start.12
  3.2 0.7 copy-start.13
  6.0 10.4 %all-to-all-start.1 = ((f32[8,24,128]{2,1,0:T(8,128)}), f32[8,24,128]{2,1,0:T(8,128)S(1)}, u32[]{:S(2)}, u32[]{:S(2)}) async-start(f32[8,24,128]{2,1,0:T(8,128)} %get-tuple-element.30), calls=%async_computation.1 | async-start | bytes 196608 | tf_op jit(solution)/shard_map/all_to_all | solution.py:469
  13.3 0.7 copy-start.14
  16.4 13.9 %all-to-all-start = ((s32[4,8,128]{2,1,0:T(8,128)}), s32[4,8,128]{2,1,0:T(8,128)S(1)}, u32[]{:S(2)}, u32[]{:S(2)}) async-start(s32[4,8,128]{2,1,0:T(8,128)} %get-tuple-element.29), calls=%async_computation | async-start | bytes 32768 | tf_op jit(solution)/shard_map/all_to_all | solution.py:470
  22.1 1.0 %copy-start.7 = (f32[1,1,1,16,16,256]{5,4,3,2,1,0:T(8,128)S(1)}, f32[1,1,1,16,16,256]{5,4,3,2,1,0:T(8,128)}, u32[]{:S(2)}) copy-start(f32[1,1,1,16,16,256]{5,4,3,2,1,0:T(8,128)} %param.13) | copy-start | bytes 786436
  23.1 0.9 %copy-start.9 = (f32[1,1,1,16,16,256]{5,4,3,2,1,0:T(8,128)S(1)}, f32[1,1,1,16,16,256]{5,4,3,2,1,0:T(8,128)}, u32[]{:S(2)}) copy-start(f32[1,1,1,16,16,256]{5,4,3,2,1,0:T(8,128)} %param.14) | copy-start | bytes 786436
  24.0 1.0 %copy-start.4 = (f32[8,32,128]{2,1,0:T(8,128)S(1)}, f32[8,32,128]{2,1,0:T(8,128)}, u32[]{:S(2)}) copy-start(f32[8,32,128]{2,1,0:T(8,128)} %h.3) | copy-start | bytes 393220
  24.0 1.0 %copy-start.6 = (f32[8,32,128]{2,1,0:T(8,128)S(1)}, f32[8,32,128]{2,1,0:T(8,128)}, u32[]{:S(2)}) copy-start(f32[8,32,128]{2,1,0:T(8,128)} %k.3) | copy-start | bytes 393220
  25.0 5.7 %collective-permute-start = (f32[104,128]{1,0:T(8,128)S(1)}, f32[104,128]{1,0:T(8,128)S(1)}, u32[]{:S(2)}, u32[]{:S(2)}) collective-permute-start(f32[104,128]{1,0:T(8,128)S(1)} %get-tuple-element.31), channel_id=1, source_target_pairs={{0,8},{8,16},{16,24},{1,9},{9,17},{17,25},{2,10},{10,18},{18,26},{... | collective-permute-start | bytes 159752 | tf_op jit(solution)/shard_map/ppermute | solution.py:489
  29.0 6.0 %collective-permute-start.1 = (f32[104,128]{1,0:T(8,128)S(1)}, f32[104,128]{1,0:T(8,128)S(1)}, u32[]{:S(2)}, u32[]{:S(2)}) collective-permute-start(f32[104,128]{1,0:T(8,128)S(1)} %get-tuple-element.32), channel_id=1, source_target_pairs={{8,0},{16,8},{24,16},{9,1},{17,9},{25,17},{10,2},{18,10},{26,18},{... | collective-permute-start | bytes 159752 | tf_op jit(solution)/shard_map/ppermute | solution.py:490
  35.0 15.2 %copy-start.8 = (f32[1,1,1,16,16,256]{5,4,3,2,1,0:T(8,128)S(1)}, f32[1,1,1,16,16,256]{5,4,3,2,1,0:T(8,128)}, u32[]{:S(2)}) copy-start(f32[1,1,1,16,16,256]{5,4,3,2,1,0:T(8,128)} %param.13) | copy-start | bytes 786436
  35.0 15.2 %copy-start.10 = (f32[1,1,1,16,16,256]{5,4,3,2,1,0:T(8,128)S(1)}, f32[1,1,1,16,16,256]{5,4,3,2,1,0:T(8,128)}, u32[]{:S(2)}) copy-start(f32[1,1,1,16,16,256]{5,4,3,2,1,0:T(8,128)} %param.14) | copy-start | bytes 786436
  35.0 15.2 %copy-start.11 = (bf16[256,256]{1,0:T(8,128)(2,1)S(1)}, bf16[256,256]{1,0:T(8,128)(2,1)}, u32[]{:S(2)}) copy-start(bf16[256,256]{1,0:T(8,128)(2,1)} %constant.31.clone.spreads) | copy-start | bytes 393220
  37.6 12.6 %copy-start.1 = (bf16[768,256]{1,0:T(8,128)(2,1)S(1)}, bf16[768,256]{1,0:T(8,128)(2,1)}, u32[]{:S(2)}) copy-start(bf16[768,256]{1,0:T(8,128)(2,1)} %constant.30.clone.lap1) | copy-start | bytes 1179652
  37.6 12.6 %copy-start.2 = (bf16[768,256]{1,0:T(8,128)(2,1)S(1)}, bf16[768,256]{1,0:T(8,128)(2,1)}, u32[]{:S(2)}) copy-start(bf16[768,256]{1,0:T(8,128)(2,1)} %constant.29.clone.lap0) | copy-start | bytes 1179652
  37.6 12.6 %all-to-all-start.2 = ((f32[4,176,128]{2,1,0:T(8,128)}), f32[4,176,128]{2,1,0:T(8,128)S(1)}, u32[]{:S(2)}, u32[]{:S(2)}) async-start(f32[4,176,128]{2,1,0:T(8,128)} %get-tuple-element.34), calls=%async_computation.2 | async-start | bytes 720896 | tf_op jit(solution)/shard_map/all_to_all | solution.py:499

commit v3 on v2

--- a/solution.py
+++ b/solution.py
@@ -26,8 +26,7 @@
 BF16 = jnp.bfloat16
 VMEM = pl.BlockSpec(memory_space=pltpu.VMEM)
 SMEM = pl.BlockSpec(memory_space=pltpu.SMEM)
-HBM = pl.BlockSpec(memory_space=pltpu.HBM)
-PARAMS = pltpu.CompilerParams(vmem_limit_bytes=16 * 1024 * 1024)
+ANY = pl.BlockSpec(memory_space=pl.ANY)
 
 
 def plane_lane(face):
@@ -123,22 +122,55 @@
     ]
 
 
-def ask(sources, wanted, asked, place):
-    lane = iota(asked.shape[1:], 1)
-    ranks = []
-    for slot in range(SLOTS):
-        alike = [jnp.where(sources[other] == sources[slot], 1, 0) for other in range(slot)]
-        ranks.append(sum(alike, jnp.int32(0)))
-        place[slot] = sources[slot]
-        place[SLOTS + slot] = ranks[slot]
-    for owner in range(asked.shape[0]):
-        row = jnp.zeros(lane.shape, jnp.int32)
-        for slot in range(SLOTS):
-            row = jnp.where(lane == jnp.where(sources[slot] == owner, ranks[slot], -1), wanted[slot], row)
-        asked[owner] = row
-
-
-def sides_kernel(sizes, sources, wanted, h_far, k_far, send, asked, place, h, k, sems):
+def column_of(row):
+    square = (row.shape[1], row.shape[1])
+    return jnp.sum(jnp.where(iota(square, 0) == iota(square, 1), row, 0.0), axis=1, keepdims=True)
+
+
+def write_tables(block_cap, source, block, neighbour, asked, table, senders):
+    me = lax.axis_index("gx").astype(F32)
+    count, records = asked.shape[0], senders.shape[0]
+    cap = float(records // count)
+    square = (SLOTS, SLOTS)
+    before = iota(square, 0) < iota(square, 1)
+    slot = iota((1, SLOTS), 1).astype(F32)
+    source_row, block_column = source[...].astype(F32), column_of(block[...].astype(F32))
+    source_column = column_of(source_row)
+    rank = jnp.sum(
+        jnp.where((source_column == source_row) & before, 1.0, 0.0), axis=0, keepdims=True
+    )
+    rank_column = column_of(rank)
+    lane = iota((SLOTS, 128), 1).astype(F32)
+    for owner in range(count):
+        hit = (source_column == float(owner)) & (rank_column == lane)
+        asked[owner : owner + 1, :] = jnp.sum(jnp.where(hit, block_column, 0.0), axis=0, keepdims=True)
+    table[6:7, 0:SLOTS] = source[...]
+    table[7:8, 0:SLOTS] = rank.astype(jnp.int32)
+    sent = jnp.zeros((records, 128), F32)
+    for face in range(FACES):
+        number = neighbour[face]
+        owner_row, number_row = (number >> 4).astype(F32), number.astype(F32)
+        owner_column, number_column = column_of(owner_row), column_of(number_row)
+        other_row = (number_row >= 0.0) & (owner_row != me)
+        alike = (owner_column == owner_row) & (owner_column >= 0.0) & (owner_column != me)
+        receive_rank = jnp.sum(
+            jnp.where(alike & (number_column < number_row), 1.0, 0.0), axis=0, keepdims=True
+        )
+        send_rank = jnp.sum(jnp.where(alike & before, 1.0, 0.0), axis=0, keepdims=True)
+        here = records + (number_row - owner_row * SLOTS)
+        receive = jnp.where(owner_row == me, here, owner_row * cap + receive_rank)
+        receive = jnp.where(number_row < 0.0, records + SLOTS + slot, receive)
+        table[face : face + 1, 0:SLOTS] = receive.astype(jnp.int32)
+        key = jnp.where(other_row, owner_row * cap + send_rank, -1.0)
+        hit = iota((records, SLOTS), 0).astype(F32) == key
+        tile = jnp.sum(jnp.where(hit, slot, 0.0), axis=1, keepdims=True)
+        sent = jnp.where(iota(sent.shape, 1) == (face ^ 1), tile, sent)
+    senders[...] = sent.astype(jnp.int32)
+
+
+def sides_kernel(
+    sizes, block_cap, source, block, neighbour, h_far, k_far, send, asked, table, senders, h, k, sems
+):
     ny, nz = sizes
     my_y, my_z = lax.axis_index("gy"), lax.axis_index("gz")
     bx = h.shape[0]
@@ -148,7 +180,7 @@
         copies.append(pltpu.make_async_copy(k_far.at[x], k.at[x], sems.at[bx + x]))
     for copy in copies:
         copy.start()
-    ask(sources, wanted, asked, place)
+    write_tables(block_cap, source, block, neighbour, asked, table, senders)
     for copy in copies:
         copy.wait()
     blocks = side_blocks(h[...], k[...])
@@ -175,16 +207,21 @@
     return read
 
 
-def layers_kernel(sizes, h, k, got, low, high):
+def layers_kernel(sizes, h, k, got, asked, _, send):
     bx, by, bz = h.shape
+    me = lax.axis_index("gx")
     read = side_reader(sizes, got, bx)
     around = [read(-1, 0), read(1, 0), read(0, -1), read(0, 1)]
-    for out, near, far in ((low, 0, 1), (high, bx - 1, bx - 2)):
-        out[0:by, :] = h[near]
-        out[by : 2 * by, :] = h[far]
-        out[2 * by : 3 * by, :] = k[near]
+    for owner in range(send.shape[0]):
+        low = owner < me
+        layers = [(h[0], h[bx - 1]), (h[1], h[bx - 2]), (k[0], k[bx - 1])]
+        for part, (lower, upper) in enumerate(layers):
+            send[owner, part * by : part * by + by, :] = jnp.where(low, lower, upper)
         for number, side in enumerate(around):
-            out[3 * by + number : 3 * by + number + 1, :] = side[near : near + 1, :]
+            line = jnp.where(low, side[0:1, :], side[bx - 1 : bx, :])
+            send[owner, 3 * by + number : 3 * by + number + 1, :] = line
+        send[owner, 3 * by + 4 : 3 * by + 5, :] = asked[owner : owner + 1, :]
+        send[owner, 3 * by + 5 : 3 * by + 8, :] = jnp.zeros((3, bz), F32)
 
 
 def block_layout(cap):
@@ -204,14 +241,17 @@
     return h + RATE * k * (total - 6.0 * t)
 
 
-def heat_kernel(cap, sizes, request, h, k, got, low, high, packed, out, send, held):
+def heat_kernel(cap, sizes, request, h, k, got, got_x, packed, out, send, held):
     bx, by, bz = h.shape
     h0, k0 = h[...], k[...]
     read = side_reader(sizes, got, bx)
-    layers = []
-    for r in (low, high):
-        layers.append([r[part * by : part * by + by, :][None] for part in range(3)])
-    lines = [[r[3 * by + n : 3 * by + n + 1, :] for n in range(4)] for r in (low, high)]
+    count, me = got_x.shape[0], lax.axis_index("gx")
+    layers, lines = [], []
+    for owner in (me - 1, me + 1):
+        inside = (owner >= 0) & (owner < count)
+        beside = jnp.where(inside, got_x[jnp.where(inside, owner, 0)], 0.0)
+        layers.append([beside[part * by : part * by + by, :][None] for part in range(3)])
+        lines.append([beside[3 * by + n : 3 * by + n + 1, :] for n in range(4)])
     y_sides = [[read(d, 0, part) for part in range(3)] for d in (-1, 1)]
     z_sides = [[read(0, d, part) for part in range(3)] for d in (-1, 1)]
     corner = [[read(dy, dz) for dz in (-1, 1)] for dy in (-1, 1)]
@@ -251,7 +291,7 @@
     for owner in range(send.shape[0]):
         total = jnp.zeros((deep, CB, bz), F32)
         for rank in range(cap):
-            block = request[owner * cap + rank]
+            block = request[owner, rank]
             a, b, c = block // (nby * nbz), (block // nbz) % nby, block % nbz
             for part in range(parts):
                 at = rank * parts + part
@@ -290,27 +330,27 @@
     return out, edge
 
 
-def pack(own, send_index, send):
-    records = send_index.shape[0] // FACES
+def pack(own, senders, send):
+    records = senders.shape[0]
     cap = records // send.shape[0]
     for record in range(records):
-        out, edge = merge_record(own, lambda face: send_index[record * FACES + face])
+        out, edge = merge_record(own, lambda face: senders[record, face])
         owner, row = record // cap, record % cap * REC
         send[owner, row : row + TE, :] = out
         send[owner, row + TE : row + REC, :] = edge
 
 
-def first_pack_kernel(send_index, phase, solute, picks, own, send):
+def first_pack_kernel(senders, phase, solute, picks, own, send):
     write_records(phase[...], solute[...], picks[...], own)
-    pack(own, send_index, send)
-
-
-def take_heat(cap, place, got, spreads, held, heat):
+    pack(own, senders, send)
+
+
+def take_heat(cap, table, got, spreads, held, heat):
     parts, deep = block_layout(cap)
     first = got.shape[1] - deep * CB
     group = iota((CB, 128), 1) // CB
     for slot in range(SLOTS):
-        source, rank = place[slot], place[SLOTS + slot]
+        source, rank = table[6, slot], table[7, slot]
         for x in range(CB):
             row = first + (x % deep) * CB
             patch = got[source, row : row + CB, :]
@@ -325,7 +365,7 @@
             heat[half, pl.ds(odd, SLOTS * CB, 2), :] = coarse[:, half * 128 : half * 128 + 128]
 
 
-def step(receive_index, phase, solute, heat, got, own, laps, all_records, ghosts):
+def step(table, phase, solute, heat, got, own, laps, all_records, ghosts):
     records = all_records.shape[0] - 2 * SLOTS
     count = got.shape[0]
     cap = records // count
@@ -334,7 +374,7 @@
         all_records[owner * cap : owner * cap + cap] = mine.reshape(cap, REC, 128)
     all_records[records : records + 2 * SLOTS] = own[...]
     for slot in range(SLOTS):
-        out, edge = merge_record(all_records, lambda face: receive_index[slot * FACES + face])
+        out, edge = merge_record(all_records, lambda face: table[face, slot])
         ghosts[slot, 0:TE, :] = out
         ghosts[slot, TE:REC, :] = edge
     beside = jnp.concatenate(halves(ghosts[:, 0:TE, :].reshape(SLOTS * TE, 128)), axis=1)
@@ -363,139 +403,115 @@
 
 
 def first_step_kernel(
-    cap, receive_index, send_index, place, phase, solute, got, own, picks, lap0, lap1, spreads, brick,
+    cap, table, senders, phase, solute, got, own, picks, lap0, lap1, spreads, brick,
     phase_out, solute_out, heat_out, own_out, send, brick_out, all_records, ghosts, held, sem,
 ):
     copy = pltpu.make_async_copy(brick, brick_out, sem)
     copy.start()
-    take_heat(cap, place, got, spreads[...], held, heat_out)
+    take_heat(cap, table, got, spreads[...], held, heat_out)
     new_phase, new_solute = step(
-        receive_index, phase[...], solute[...], heat_out[...], got, own, (lap0[...], lap1[...]),
+        table, phase[...], solute[...], heat_out[...], got, own, (lap0[...], lap1[...]),
         all_records, ghosts,
     )
     phase_out[...] = new_phase
     solute_out[...] = new_solute
     write_records(new_phase, new_solute, picks[...], own_out)
-    pack(own_out, send_index, send)
+    pack(own_out, senders, send)
     copy.wait()
 
 
 def middle_step_kernel(
-    receive_index, send_index, phase, solute, heat, got, own, picks, lap0, lap1,
+    table, senders, phase, solute, heat, got, own, picks, lap0, lap1,
     phase_out, solute_out, own_out, send, all_records, ghosts,
 ):
     new_phase, new_solute = step(
-        receive_index, phase[...], solute[...], heat[...], got, own, (lap0[...], lap1[...]),
+        table, phase[...], solute[...], heat[...], got, own, (lap0[...], lap1[...]),
         all_records, ghosts,
     )
     phase_out[...] = new_phase
     solute_out[...] = new_solute
     write_records(new_phase, new_solute, picks[...], own_out)
-    pack(own_out, send_index, send)
+    pack(own_out, senders, send)
 
 
 def last_step_kernel(
-    receive_index, phase, solute, heat, got, own, lap0, lap1, phase_out, solute_out, all_records, ghosts
+    table, phase, solute, heat, got, own, lap0, lap1, phase_out, solute_out, all_records, ghosts
 ):
     new_phase, new_solute = step(
-        receive_index, phase[...], solute[...], heat[...], got, own, (lap0[...], lap1[...]),
+        table, phase[...], solute[...], heat[...], got, own, (lap0[...], lap1[...]),
         all_records, ghosts,
     )
     phase_out[...] = new_phase
     solute_out[...] = new_solute
 
 
-def call(kernel, in_specs, out_shapes, scratch=(), out_specs=None):
+def call(kernel, in_specs, out_shapes, scratch=(), out_specs=None, mib=16):
     return pl.pallas_call(
         kernel,
         out_shape=out_shapes,
         in_specs=in_specs,
         out_specs=out_specs or jax.tree.map(lambda _: VMEM, out_shapes),
         scratch_shapes=list(scratch),
-        compiler_params=PARAMS,
+        compiler_params=pltpu.CompilerParams(vmem_limit_bytes=mib * 1024 * 1024),
     )
 
 
 def shape(*dims):
     return jax.ShapeDtypeStruct(dims, F32)
-
-
-def tile_indices(neighbour, cap, me):
-    count = lax.axis_size("gx")
-    owner = neighbour >> 4
-    other = (neighbour >= 0) & (owner != me)
-    slot = jnp.arange(SLOTS, dtype=jnp.int32)
-    alike = (owner[None] == owner[:, None]) & other[None]
-    receive_rank = jnp.sum((alike & (neighbour[None] < neighbour[:, None])).astype(jnp.int32), axis=1)
-    send_rank = jnp.sum(
-        (alike & (slot[None, :, None] < slot[:, None, None])).astype(jnp.int32), axis=1
-    )
-    records = count * cap
-    receive = jnp.where(
-        neighbour < 0,
-        records + SLOTS + slot[:, None],
-        jnp.where(owner == me, records + (neighbour & (SLOTS - 1)), owner * cap + receive_rank),
-    )
-    key = jnp.where(other, owner * cap + send_rank, -1)
-    hit = key[None] == jnp.arange(records, dtype=jnp.int32)[:, None, None]
-    sender = jnp.sum(jnp.where(hit, slot[None, :, None], 0), axis=1)
-    sender = sender.reshape(records, 3, 2)[:, :, ::-1]
-    return receive.reshape(-1), sender.reshape(-1)
 
 
 def local(enthalpy, conductivity, phase, solute, tile_source, tile_block, tile_neighbour):
     count = lax.axis_size("gx")
     sizes = (lax.axis_size("gy"), lax.axis_size("gz"))
-    me = lax.axis_index("gx")
     plane_cap = -(-SLOTS // (count - 1))
     block_cap = 2 * SLOTS // count
+    records = count * plane_cap
     bx, by, bz = enthalpy.shape
     picks, lap0, lap1, spreads = tables()
 
-    sources = tile_source.reshape(SLOTS)
-    wanted = tile_block.reshape(SLOTS)
-    integers = jax.ShapeDtypeStruct((count, 8, 128), jnp.int32)
-    sides, asked, place = call(
-        functools.partial(sides_kernel, sizes),
-        [SMEM] * 2 + [HBM] * 2,
+    integers = functools.partial(jax.ShapeDtypeStruct, dtype=jnp.int32)
+    sides, asked, table, senders = call(
+        functools.partial(sides_kernel, sizes, block_cap),
+        [VMEM] * 3 + [ANY] * 2,
         [
             shape(sizes[0] * sizes[1], 3 * bx, 128),
-            integers,
-            jax.ShapeDtypeStruct((2 * SLOTS,), jnp.int32),
+            shape(count, 128),
+            integers((8, 128)),
+            integers((records, 128)),
         ],
         [pltpu.VMEM((bx, by, bz), F32)] * 2 + [pltpu.SemaphoreType.DMA((2 * bx,))],
-        [VMEM, VMEM, SMEM],
-    )(sources, wanted, enthalpy, conductivity)
+        mib=56,
+    )(
+        tile_source.reshape(1, SLOTS),
+        tile_block.reshape(1, SLOTS),
+        jnp.transpose(tile_neighbour, (0, 1, 4, 2, 3)).reshape(FACES, 1, SLOTS),
+        enthalpy,
+        conductivity,
+    )
     sides = lax.all_to_all(sides, ("gy", "gz"), split_axis=0, concat_axis=0, tiled=True)
-    asked = lax.all_to_all(asked, "gx", split_axis=0, concat_axis=0, tiled=True)
-    request = asked[:, 0, :block_cap].reshape(-1)
-
-    neighbour = tile_neighbour.reshape(SLOTS, FACES)
-    receive_index, send_index = tile_indices(neighbour, plane_cap, me)
+
     phase_field = phase.reshape(SLOTS, TE, PLANE)
     solute_field = solute.reshape(SLOTS, TE, PLANE)
-    records = count * plane_cap
     own_shape, send_shape = shape(2 * SLOTS, REC, 128), shape(count, plane_cap * REC, 128)
     own, packed = call(first_pack_kernel, [SMEM] + [VMEM] * 3, [own_shape, send_shape])(
-        send_index, phase_field, solute_field, picks
-    )
-
-    layer = shape(3 * by + 8, bz)
-    low, high = call(functools.partial(layers_kernel, sizes), [VMEM] * 3, [layer, layer])(
-        enthalpy, conductivity, sides
-    )
-    forward = [(i, i + 1) for i in range(count - 1)]
-    backward = [(b, a) for a, b in forward]
-    from_low = lax.ppermute(high, "gx", forward)
-    from_high = lax.ppermute(low, "gx", backward)
+        senders, phase_field, solute_field, picks
+    )
+
+    layers = call(
+        functools.partial(layers_kernel, sizes),
+        [VMEM] * 4 + [ANY],
+        shape(count, 3 * by + 8, bz),
+    )(enthalpy, conductivity, sides, asked, packed)
+    layers = lax.all_to_all(layers, "gx", split_axis=0, concat_axis=0, tiled=True)
+    request = layers[:, 3 * by + 4, :block_cap].astype(jnp.int32)
     _, deep = block_layout(block_cap)
     brick = shape(bx, by, bz)
     heated, send = call(
         functools.partial(heat_kernel, block_cap, sizes),
-        [SMEM] + [VMEM] * 6,
+        [SMEM] + [VMEM] * 5,
         [brick, shape(count, plane_cap * REC + deep * CB, 128)],
         [pltpu.VMEM((bx, by // CB, CB, bz), F32)],
-    )(request, enthalpy, conductivity, sides, from_low, from_high, packed)
+    )(request, enthalpy, conductivity, sides, layers, packed)
     got = lax.all_to_all(send, "gx", split_axis=0, concat_axis=0, tiled=True)
 
     field = shape(SLOTS, TE, PLANE)
@@ -505,23 +521,23 @@
     ]
     phase_field, solute_field, heat, own, send, heat_out = call(
         functools.partial(first_step_kernel, block_cap),
-        [SMEM] * 3 + [VMEM] * 9,
+        [SMEM] * 2 + [VMEM] * 9,
         [field, field, shape(2, SLOTS * TE, 128), own_shape, send_shape, brick],
         step_scratch + [pltpu.VMEM((SLOTS * CB, CB, 128), F32), pltpu.SemaphoreType.DMA],
-        [VMEM] * 5 + [HBM],
+        [VMEM] * 5 + [ANY],
     )(
-        receive_index, send_index, place, phase_field, solute_field, got, own, picks, lap0, lap1, spreads,
+        table, senders, phase_field, solute_field, got, own, picks, lap0, lap1, spreads,
         heated,
     )
     for _ in range(PHASE_STEPS - 2):
         got = lax.all_to_all(send, "gx", split_axis=0, concat_axis=0, tiled=True)
         phase_field, solute_field, own, send = call(
             middle_step_kernel, [SMEM] * 2 + [VMEM] * 8, [field, field, own_shape, send_shape], step_scratch
-        )(receive_index, send_index, phase_field, solute_field, heat, got, own, picks, lap0, lap1)
+        )(table, senders, phase_field, solute_field, heat, got, own, picks, lap0, lap1)
     got = lax.all_to_all(send, "gx", split_axis=0, concat_axis=0, tiled=True)
     phase_field, solute_field = call(
         last_step_kernel, [SMEM] + [VMEM] * 7, [field, field], step_scratch
-    )(receive_index, phase_field, solute_field, heat, got, own, lap0, lap1)
+    )(table, phase_field, solute_field, heat, got, own, lap0, lap1)
     return heat_out, phase_field.reshape(phase.shape), solute_field.reshape(solute.shape)
 
 

time: 89.6 us -> 85.7 us (0.956)
  blocking collectives: 30.6 us -> 60.1 us
  starting transfers between devices: 19 us -> 5.18 us
  waiting for transfers between devices: 15.1 us -> 2.01 us
  local copies, waits for them, and re-layouts: 7.58 us -> 2.69 us
  other arithmetic: 1.86 us -> 0.01 us
    all_to_all x3 -> x4, blocking collectives: 30.6 us -> 47.7 us  [local(): got = lax.all_to_all(send, 'gx', split_axis=0, concat_axis=0, tiled=True)]
    all_to_all x0 -> x1, blocking collectives: none -> 12.5 us  [local(): lax.all_to_all(layers, 'gx', split_axis=0, concat_axis=0, tiled=True)]
    all_to_all x2 -> x0, starting transfers between devices: 8.63 us -> none  [the longest x1 4.87 us: local(): asked = lax.all_to_all(asked, 'gx', split_axis=0, concat_axis=0, tiled=True)]
    all_to_all x2 -> x0, waiting for transfers between devices: 8.08 us -> none  [the longest x1 8.08 us: local(): got = lax.all_to_all(send, 'gx', split_axis=0, concat_axis=0, tiled=True)]
    ppermute x2 -> x0, starting transfers between devices: 5.23 us -> none  [the longest x1 3.93 us: local(): from_low = lax.ppermute(high, 'gx', forward)]
    ppermute x2 -> x0, waiting for transfers between devices: 4.61 us -> none  [the longest x1 4.26 us: local(): from_high = lax.ppermute(low, 'gx', backward)]
    unnamed x31 -> x26, local copies, waits for them, and re-layouts: 6.11 us -> 2.69 us
  transfers between devices with their start and end apart: 5 -> 1, of which waited for: 4 -> 1; matrix products, arithmetic and copies ran while one was open for 5% -> 0% of each run, Pallas kernels for 1% -> 1%
where the time goes in v3:
time: 85.7 us; the launch traced here: 85 us
  blocking collectives  60.1 us (70%)
  Pallas kernels  14.2 us (17%)
  starting transfers between devices  5.18 us (6%)
  local copies, waits for them, and re-layouts  2.69 us (3%)
  waiting for transfers between devices  2.01 us (2%)
    all_to_all x4, blocking collectives, local(): got = lax.all_to_all(send, 'gx', split_axis=0, concat_axis=0, tiled=True)  47.7 us
    all_to_all x1, blocking collectives, local(): lax.all_to_all(layers, 'gx', split_axis=0, concat_axis=0, tiled=True)  12.5 us
    all_to_all x1, starting transfers between devices, local(): lax.all_to_all(sides, ('gy', 'gz'), split_axis=0, concat_axis=0, tiled=True)  5.18 us
    pallas_call x2, Pallas kernels, local(): call(middle_step_kernel, [SMEM] * 2 + [VMEM] * 8, [field, field, own_shap...  3.53 us
    pallas_call x1, Pallas kernels, local(): call(functools.partial(first_step_kernel, block_cap), [SMEM] * 2 + [VMEM]...  2.77 us
    pallas_call x1, Pallas kernels, local(): call(functools.partial(sides_kernel, sizes, block_cap), [VMEM] * 3 + [ANY...  2.74 us
    unnamed x26, local copies, waits for them, and re-layouts  2.69 us
    pallas_call x1, Pallas kernels, local(): call(last_step_kernel, [SMEM] + [VMEM] * 7, [field, field], step_scratch)  2.05 us
  transfers between devices with their start and end apart: 1, of which 1 were waited for; matrix products, arithmetic and copies ran while one was open for 0% of the time, Pallas kernels for 1%

profile of v3, /device:TPU:0, one launch (start us, length us, event | category | flops | bytes accessed | tf_op | source)
XLA Modules:
  0.0 85.0 jit_solution(10669859343832571553)
XLA Ops:
  0.6 0.0 copy-start.6
  0.6 2.7 %shard_map.130 = (f32[8,24,128]{2,1,0:T(8,128)}, f32[4,128]{1,0:T(4,128)}, s32[8,128]{1,0:T(8,128)}, s32[24,128]{1,0:T(8,128)}) custom-call(s32[1,16]{1,0:T(1,128)} %bitcast.16, s32[1,16]{1,0:T(1,128)} %bitcast.17, s32[6,1,16]{2,1,0:T(1,128)} %bitcast.15, f32[8,32,128]{2,1,0:T(8,128)} %h.3, f32[8,32,128]{2,1,0:T(8,128)} %k.3), custom_call_target="tpu_custom_call" | custom-call | tf_op jit(solution)/shard_map/pallas_call | solution.py:473
  3.4 0.0 copy-start.9
  3.4 5.2 %all-to-all-start = ((f32[8,24,128]{2,1,0:T(8,128)}), f32[8,24,128]{2,1,0:T(8,128)S(1)}, u32[]{:S(2)}, u32[]{:S(2)}) async-start(f32[8,24,128]{2,1,0:T(8,128)} %get-tuple-element.29), calls=%async_computation | async-start | bytes 196608 | tf_op jit(solution)/shard_map/all_to_all | solution.py:491
  8.6 0.0 copy-done.6
  8.6 0.0 copy-done.9
  8.6 0.0 copy-start
  8.6 1.0 %copy-done = bf16[1024,256]{1,0:T(8,128)(2,1)S(1)} copy-done((bf16[1024,256]{1,0:T(8,128)(2,1)S(1)}, bf16[1024,256]{1,0:T(8,128)(2,1)}, u32[]{:S(2)}) %copy-start) | copy-done | bytes 524312
  9.6 0.0 copy-start.7
  9.6 0.9 %copy-done.7 = f32[1,1,1,16,16,256]{5,4,3,2,1,0:T(8,128)S(1)} copy-done((f32[1,1,1,16,16,256]{5,4,3,2,1,0:T(8,128)S(1)}, f32[1,1,1,16,16,256]{5,4,3,2,1,0:T(8,128)}, u32[]{:S(2)}) %copy-start.7) | copy-done | bytes 262168
  10.6 0.0 copy-start.4
  10.6 0.0 copy-start.5
  10.6 1.2 %shard_map.131 = (f32[32,24,128]{2,1,0:T(8,128)S(1)}, f32[4,144,128]{2,1,0:T(8,128)S(1)}) custom-call(s32[24,128]{1,0:T(8,128)S(1)} %copy-done.9, f32[16,16,256]{2,1,0:T(8,128)S(1)} %bitcast.10, f32[16,16,256]{2,1,0:T(8,128)S(1)} %bitcast.12, bf16[1024,256]{1,0:T(8,128)(2,1)S(1)} %copy-done), custom_call_target="tpu_custom_call" | custom-call | tf_op jit(solution)/shard_map/pallas_call | solution.py:496
  11.8 0.0 copy-start.12
  11.8 2.0 %all-to-all-done.got = f32[8,24,128]{2,1,0:T(8,128)S(1)} async-done(((f32[8,24,128]{2,1,0:T(8,128)}), f32[8,24,128]{2,1,0:T(8,128)S(1)}, u32[]{:S(2)}, u32[]{:S(2)}) %all-to-all-start) | async-done | bytes 98336 | tf_op jit(solution)/shard_map/all_to_all | solution.py:491
  13.8 0.0 copy-done.4
  13.8 0.0 copy-done.5
  13.8 0.0 copy-done.12
  13.8 0.0 copy-start.10
  13.9 12.5 %all_to_all.30.got_x = f32[4,104,128]{2,1,0:T(8,128)S(1)} all-to-all(f32[4,104,128]{2,1,0:T(8,128)S(1)} %shard_map.132), channel_id=1, replica_groups=mesh['gx'=4,'gy'=2,'gz'=4] {'gx'}, dimensions={0} | all-to-all | bytes 425984 | tf_op jit(solution)/shard_map/all_to_all | solution.py:505
  26.3 0.0 copy-start.2
  26.3 0.0 copy-start.3
  26.4 0.0 copy-start.8
  26.4 1.9 %shard_map.133 = (f32[8,32,128]{2,1,0:T(8,128)S(1)}, f32[4,176,128]{2,1,0:T(8,128)S(1)}) custom-call(s32[4,8]{1,0:T(4,128)S(1)} %bitcast.14, f32[8,32,128]{2,1,0:T(8,128)S(1)} %copy-done.4, f32[8,32,128]{2,1,0:T(8,128)S(1)} %copy-done.5, f32[8,24,128]{2,1,0:T(8,128)S(1)} %all-to-all-done.got, f32[4,104,128]{2,1,0:T(8,128)S(1)} %all_to_all.30.got_x, ...), custom_call_target="tpu_custom_call" | custom-call | tf_op jit(solution)/shard_map/pallas_call | solution.py:509
  28.3 0.0 copy-start.1
  28.3 13.2 %all_to_all.31.got = f32[4,176,128]{2,1,0:T(8,128)S(1)} all-to-all(f32[4,176,128]{2,1,0:T(8,128)S(1)} %get-tuple-element.32), channel_id=1, replica_groups=mesh['gx'=4,'gy'=2,'gz'=4] {'gx'}, dimensions={0} | all-to-all | bytes 720896 | tf_op jit(solution)/shard_map/all_to_all | solution.py:515
  41.5 0.0 copy-start.11
  41.5 0.0 copy-done.10
  41.5 0.0 copy-done.2
  41.5 0.0 copy-done.3
  41.5 0.0 copy-done.8
  41.5 0.0 copy-done.1
  41.5 0.7 copy-done.11
  42.2 2.8 %shard_map.134 = (f32[16,16,256]{2,1,0:T(8,128)S(1)}, f32[16,16,256]{2,1,0:T(8,128)S(1)}, f32[2,256,128]{2,1,0:T(8,128)S(1)}, f32[32,24,128]{2,1,0:T(8,128)S(1)}...) custom-call(s32[8,128]{1,0:T(8,128)S(1)} %copy-done.11, s32[24,128]{1,0:T(8,128)S(1)} %copy-done.9, ...), custom_call_target="tpu_custom_call" | custom-call | tf_op jit(solution)/shard_map/pallas_call | solution.py:522
  45.0 11.6 %all_to_all.32.got = f32[4,144,128]{2,1,0:T(8,128)S(1)} all-to-all(f32[4,144,128]{2,1,0:T(8,128)S(1)} %get-tuple-element.39), channel_id=1, replica_groups=mesh['gx'=4,'gy'=2,'gz'=4] {'gx'}, dimensions={0} | all-to-all | bytes 589824 | tf_op jit(solution)/shard_map/all_to_all | solution.py:533
  56.6 1.8 %shard_map.135 = (f32[16,16,256]{2,1,0:T(8,128)S(1)}, f32[16,16,256]{2,1,0:T(8,128)S(1)}, f32[32,24,128]{2,1,0:T(8,128)S(1)}, f32[4,144,128]{2,1,0:T(8,128)S(1)}) custom-call(s32[8,128]{1,0:T(8,128)S(1)} %copy-done.11, s32[24,128]{1,0:T(8,128)S(1)} %copy-done.9, f32[16,16,256]{2,1,0:T(8,128)S(1)} %get-tuple-element.36.phase, ...), custom_call_target="tpu_custom_call" | custom-call | tf_op jit(solution)/shard_map/pallas_call | solution.py:534
  58.4 11.4 %all_to_all.33.got = f32[4,144,128]{2,1,0:T(8,128)S(1)} all-to-all(f32[4,144,128]{2,1,0:T(8,128)S(1)} %get-tuple-element.43), channel_id=1, replica_groups=mesh['gx'=4,'gy'=2,'gz'=4] {'gx'}, dimensions={0} | all-to-all | bytes 589824 | tf_op jit(solution)/shard_map/all_to_all | solution.py:533
  69.7 1.8 %shard_map.136 = (f32[16,16,256]{2,1,0:T(8,128)S(1)}, f32[16,16,256]{2,1,0:T(8,128)S(1)}, f32[32,24,128]{2,1,0:T(8,128)S(1)}, f32[4,144,128]{2,1,0:T(8,128)S(1)}) custom-call(s32[8,128]{1,0:T(8,128)S(1)} %copy-done.11, s32[24,128]{1,0:T(8,128)S(1)} %copy-done.9, f32[16,16,256]{2,1,0:T(8,128)S(1)} %get-tuple-element.41.phase, ...), custom_call_target="tpu_custom_call" | custom-call | tf_op jit(solution)/shard_map/pallas_call | solution.py:534
  71.5 11.5 %all_to_all.34.got = f32[4,144,128]{2,1,0:T(8,128)S(1)} all-to-all(f32[4,144,128]{2,1,0:T(8,128)S(1)} %get-tuple-element.47), channel_id=1, replica_groups=mesh['gx'=4,'gy'=2,'gz'=4] {'gx'}, dimensions={0} | all-to-all | bytes 589824 | tf_op jit(solution)/shard_map/all_to_all | solution.py:537
  83.0 2.1 %shard_map.137 = (f32[16,16,256]{2,1,0:T(8,128)}, f32[16,16,256]{2,1,0:T(8,128)}) custom-call(s32[8,128]{1,0:T(8,128)S(1)} %copy-done.11, f32[16,16,256]{2,1,0:T(8,128)S(1)} %get-tuple-element.45.phase, f32[16,16,256]{2,1,0:T(8,128)S(1)} %get-tuple-element.46.solute, f32[2,256,128]{2,1,0:T(8,128)S(1)} %get-tuple-element.38.heat, ...), custom_call_target="tpu_custom_call" | custom-call | tf_op jit(solution)/shard_map/pallas_call | solution.py:538
  (2 shorter events, 0.0 us)
Async XLA Ops:
  0.6 8.0 %copy-start.6 = (f32[1,1,1,16,16,256]{5,4,3,2,1,0:T(8,128)S(1)}, f32[1,1,1,16,16,256]{5,4,3,2,1,0:T(8,128)}, u32[]{:S(2)}) copy-start(f32[1,1,1,16,16,256]{5,4,3,2,1,0:T(8,128)} %param.13) | copy-start | bytes 786436
  3.4 5.2 %copy-start.9 = (s32[24,128]{1,0:T(8,128)S(1)}, s32[24,128]{1,0:T(8,128)}, u32[]{:S(2)}) copy-start(s32[24,128]{1,0:T(8,128)} %get-tuple-element.28.senders) | copy-start | bytes 36868
  3.4 10.4 %all-to-all-start = ((f32[8,24,128]{2,1,0:T(8,128)}), f32[8,24,128]{2,1,0:T(8,128)S(1)}, u32[]{:S(2)}, u32[]{:S(2)}) async-start(f32[8,24,128]{2,1,0:T(8,128)} %get-tuple-element.29), calls=%async_computation | async-start | bytes 196608 | tf_op jit(solution)/shard_map/all_to_all | solution.py:491
  8.6 1.0 %copy-start = (bf16[1024,256]{1,0:T(8,128)(2,1)S(1)}, bf16[1024,256]{1,0:T(8,128)(2,1)}, u32[]{:S(2)}) copy-start(bf16[1024,256]{1,0:T(8,128)(2,1)} %constant.8.clone.picks) | copy-start | bytes 1572868
  9.6 0.9 %copy-start.7 = (f32[1,1,1,16,16,256]{5,4,3,2,1,0:T(8,128)S(1)}, f32[1,1,1,16,16,256]{5,4,3,2,1,0:T(8,128)}, u32[]{:S(2)}) copy-start(f32[1,1,1,16,16,256]{5,4,3,2,1,0:T(8,128)} %param.14) | copy-start | bytes 786436
  10.6 3.2 %copy-start.4 = (f32[8,32,128]{2,1,0:T(8,128)S(1)}, f32[8,32,128]{2,1,0:T(8,128)}, u32[]{:S(2)}) copy-start(f32[8,32,128]{2,1,0:T(8,128)} %h.3) | copy-start | bytes 393220
  10.6 3.2 %copy-start.5 = (f32[8,32,128]{2,1,0:T(8,128)S(1)}, f32[8,32,128]{2,1,0:T(8,128)}, u32[]{:S(2)}) copy-start(f32[8,32,128]{2,1,0:T(8,128)} %k.3) | copy-start | bytes 393220
  11.8 2.0 %copy-start.12 = (f32[4,128]{1,0:T(4,128)S(1)}, f32[4,128]{1,0:T(4,128)}, u32[]{:S(2)}) copy-start(f32[4,128]{1,0:T(4,128)} %get-tuple-element.30.asked) | copy-start | bytes 6148
  13.8 27.7 %copy-start.10 = (bf16[256,256]{1,0:T(8,128)(2,1)S(1)}, bf16[256,256]{1,0:T(8,128)(2,1)}, u32[]{:S(2)}) copy-start(bf16[256,256]{1,0:T(8,128)(2,1)} %constant.11.clone.spreads) | copy-start | bytes 393220
  26.3 15.2 %copy-start.2 = (bf16[768,256]{1,0:T(8,128)(2,1)S(1)}, bf16[768,256]{1,0:T(8,128)(2,1)}, u32[]{:S(2)}) copy-start(bf16[768,256]{1,0:T(8,128)(2,1)} %constant.10.clone.lap1) | copy-start | bytes 1179652
  26.3 15.2 %copy-start.3 = (bf16[768,256]{1,0:T(8,128)(2,1)S(1)}, bf16[768,256]{1,0:T(8,128)(2,1)}, u32[]{:S(2)}) copy-start(bf16[768,256]{1,0:T(8,128)(2,1)} %constant.9.clone.lap0) | copy-start | bytes 1179652
  26.4 15.2 %copy-start.8 = (f32[1,1,1,16,16,256]{5,4,3,2,1,0:T(8,128)S(1)}, f32[1,1,1,16,16,256]{5,4,3,2,1,0:T(8,128)}, u32[]{:S(2)}) copy-start(f32[1,1,1,16,16,256]{5,4,3,2,1,0:T(8,128)} %param.14) | copy-start | bytes 786436
  28.3 13.2 %copy-start.1 = (bf16[1024,256]{1,0:T(8,128)(2,1)S(1)}, bf16[1024,256]{1,0:T(8,128)(2,1)}, u32[]{:S(2)}) copy-start(bf16[1024,256]{1,0:T(8,128)(2,1)} %constant.8.clone.picks) | copy-start | bytes 1572868
  41.5 0.7 copy-start.11

commit v4 on v3

--- a/solution.py
+++ b/solution.py
@@ -53,14 +53,12 @@
 
 def tables():
     pick, place, stencil, spread = constant_tables()
-    picks = np.concatenate([pick[0], pick[0], pick[1], pick[1]], axis=0)
-    laps = [np.concatenate([stencil, stencil, place[f], place[f]], axis=0) for f in range(2)]
-    spreads = np.concatenate([spread, spread], axis=0)
+    place = np.concatenate([place[0], place[1]], axis=1)
     return (
-        jnp.asarray(picks, BF16),
-        jnp.asarray(laps[0], BF16),
-        jnp.asarray(laps[1], BF16),
-        jnp.asarray(spreads, BF16),
+        jnp.asarray(np.concatenate([pick[0], pick[1]], axis=0), BF16),
+        jnp.asarray(stencil, BF16),
+        jnp.asarray(np.concatenate([place, place], axis=0), BF16),
+        jnp.asarray(np.concatenate([spread, spread], axis=0), BF16),
     )
 
 
@@ -127,10 +125,11 @@
     return jnp.sum(jnp.where(iota(square, 0) == iota(square, 1), row, 0.0), axis=1, keepdims=True)
 
 
-def write_tables(block_cap, source, block, neighbour, asked, table, senders):
+def write_tables(plane_cap, source, block, neighbour, asked, table):
     me = lax.axis_index("gx").astype(F32)
-    count, records = asked.shape[0], senders.shape[0]
-    cap = float(records // count)
+    count = asked.shape[0]
+    records = count * plane_cap
+    cap = float(plane_cap)
     square = (SLOTS, SLOTS)
     before = iota(square, 0) < iota(square, 1)
     slot = iota((1, SLOTS), 1).astype(F32)
@@ -141,12 +140,14 @@
     )
     rank_column = column_of(rank)
     lane = iota((SLOTS, 128), 1).astype(F32)
-    for owner in range(count):
-        hit = (source_column == float(owner)) & (rank_column == lane)
-        asked[owner : owner + 1, :] = jnp.sum(jnp.where(hit, block_column, 0.0), axis=0, keepdims=True)
+    for shift in range(count):
+        owner = me + float(shift)
+        owner = jnp.where(owner >= float(count), owner - float(count), owner)
+        hit = (source_column == owner) & (rank_column == lane)
+        asked[shift : shift + 1, :] = jnp.sum(jnp.where(hit, block_column, 0.0), axis=0, keepdims=True)
     table[6:7, 0:SLOTS] = source[...]
     table[7:8, 0:SLOTS] = rank.astype(jnp.int32)
-    sent = jnp.zeros((records, 128), F32)
+    slot_column = iota((SLOTS, records), 0).astype(F32)
     for face in range(FACES):
         number = neighbour[face]
         owner_row, number_row = (number >> 4).astype(F32), number.astype(F32)
@@ -162,14 +163,13 @@
         receive = jnp.where(number_row < 0.0, records + SLOTS + slot, receive)
         table[face : face + 1, 0:SLOTS] = receive.astype(jnp.int32)
         key = jnp.where(other_row, owner_row * cap + send_rank, -1.0)
-        hit = iota((records, SLOTS), 0).astype(F32) == key
-        tile = jnp.sum(jnp.where(hit, slot, 0.0), axis=1, keepdims=True)
-        sent = jnp.where(iota(sent.shape, 1) == (face ^ 1), tile, sent)
-    senders[...] = sent.astype(jnp.int32)
+        hit = iota((SLOTS, records), 1).astype(F32) == column_of(key)
+        tile = jnp.sum(jnp.where(hit, slot_column, 0.0), axis=0, keepdims=True)
+        table[face ^ 1 : (face ^ 1) + 1, SLOTS : SLOTS + records] = tile.astype(jnp.int32)
 
 
 def sides_kernel(
-    sizes, block_cap, source, block, neighbour, h_far, k_far, send, asked, table, senders, h, k, sems
+    sizes, plane_cap, source, block, neighbour, h_far, k_far, send, asked, table, h, k, sems
 ):
     ny, nz = sizes
     my_y, my_z = lax.axis_index("gy"), lax.axis_index("gz")
@@ -180,7 +180,7 @@
         copies.append(pltpu.make_async_copy(k_far.at[x], k.at[x], sems.at[bx + x]))
     for copy in copies:
         copy.start()
-    write_tables(block_cap, source, block, neighbour, asked, table, senders)
+    write_tables(plane_cap, source, block, neighbour, asked, table)
     for copy in copies:
         copy.wait()
     blocks = side_blocks(h[...], k[...])
@@ -207,21 +207,21 @@
     return read
 
 
-def layers_kernel(sizes, h, k, got, asked, _, send):
+def layers_kernel(sizes, h, k, got, asked, _, down, up, *farther):
     bx, by, bz = h.shape
-    me = lax.axis_index("gx")
+    count = asked.shape[0]
     read = side_reader(sizes, got, bx)
     around = [read(-1, 0), read(1, 0), read(0, -1), read(0, 1)]
-    for owner in range(send.shape[0]):
-        low = owner < me
-        layers = [(h[0], h[bx - 1]), (h[1], h[bx - 2]), (k[0], k[bx - 1])]
-        for part, (lower, upper) in enumerate(layers):
-            send[owner, part * by : part * by + by, :] = jnp.where(low, lower, upper)
+    for out, near, far, shift in ((down, 0, 1, count - 1), (up, bx - 1, bx - 2, 1)):
+        out[0:by, :] = h[near]
+        out[by : 2 * by, :] = h[far]
+        out[2 * by : 3 * by, :] = k[near]
         for number, side in enumerate(around):
-            line = jnp.where(low, side[0:1, :], side[bx - 1 : bx, :])
-            send[owner, 3 * by + number : 3 * by + number + 1, :] = line
-        send[owner, 3 * by + 4 : 3 * by + 5, :] = asked[owner : owner + 1, :]
-        send[owner, 3 * by + 5 : 3 * by + 8, :] = jnp.zeros((3, bz), F32)
+            out[3 * by + number : 3 * by + number + 1, :] = side[near : near + 1, :]
+        out[3 * by + 4 : 3 * by + 5, :] = asked[shift : shift + 1, :]
+        out[3 * by + 5 : 3 * by + 8, :] = jnp.zeros((3, bz), F32)
+    for number, out in enumerate(farther):
+        out[...] = jnp.broadcast_to(asked[2 + number : 3 + number, :], out.shape)
 
 
 def block_layout(cap):
@@ -241,15 +241,14 @@
     return h + RATE * k * (total - 6.0 * t)
 
 
-def heat_kernel(cap, sizes, request, h, k, got, got_x, packed, out, send, held):
+def heat_kernel(cap, sizes, request, h, k, got, low, high, packed, out, send, held):
     bx, by, bz = h.shape
     h0, k0 = h[...], k[...]
     read = side_reader(sizes, got, bx)
-    count, me = got_x.shape[0], lax.axis_index("gx")
+    count, me = send.shape[0], lax.axis_index("gx")
     layers, lines = [], []
-    for owner in (me - 1, me + 1):
-        inside = (owner >= 0) & (owner < count)
-        beside = jnp.where(inside, got_x[jnp.where(inside, owner, 0)], 0.0)
+    for beside, inside in ((low, me > 0), (high, me < count - 1)):
+        beside = jnp.where(inside, beside[...], 0.0)
         layers.append([beside[part * by : part * by + by, :][None] for part in range(3)])
         lines.append([beside[3 * by + n : 3 * by + n + 1, :] for n in range(4)])
     y_sides = [[read(d, 0, part) for part in range(3)] for d in (-1, 1)]
@@ -288,10 +287,11 @@
     parts, deep = block_layout(cap)
     nby, nbz = by // CB, bz // CB
     group = iota((deep, CB, bz), 2) // CB
-    for owner in range(send.shape[0]):
+    for owner in range(count):
+        shift = lax.rem(me - owner + count, count)
         total = jnp.zeros((deep, CB, bz), F32)
         for rank in range(cap):
-            block = request[owner, rank]
+            block = request[shift, rank]
             a, b, c = block // (nby * nbz), (block // nbz) % nby, block % nbz
             for part in range(parts):
                 at = rank * parts + part
@@ -305,8 +305,8 @@
 
 def write_records(phase, solute, picks, own):
     flat = [f.reshape(SLOTS * TE, PLANE) for f in (phase, solute)]
-    parts = jnp.concatenate([*halves(flat[0]), *halves(flat[1])], axis=1)
-    planes = dot(parts, picks)
+    high, low = halves(jnp.concatenate(flat, axis=1))
+    planes = dot(high, picks) + dot(low, picks)
     own[0:SLOTS, 0:TE, :] = planes[:, 0:128].reshape(SLOTS, TE, 128)
     own[SLOTS : 2 * SLOTS, 0:TE, :] = planes[:, 128:256].reshape(SLOTS, TE, 128)
     for face in range(2):
@@ -330,19 +330,19 @@
     return out, edge
 
 
-def pack(own, senders, send):
-    records = senders.shape[0]
+def pack(own, table, send):
+    records = send.shape[0] * (send.shape[1] // REC)
     cap = records // send.shape[0]
     for record in range(records):
-        out, edge = merge_record(own, lambda face: senders[record, face])
+        out, edge = merge_record(own, lambda face: table[face, SLOTS + record])
         owner, row = record // cap, record % cap * REC
         send[owner, row : row + TE, :] = out
         send[owner, row + TE : row + REC, :] = edge
 
 
-def first_pack_kernel(senders, phase, solute, picks, own, send):
+def first_pack_kernel(table, phase, solute, picks, own, send):
     write_records(phase[...], solute[...], picks[...], own)
-    pack(own, senders, send)
+    pack(own, table, send)
 
 
 def take_heat(cap, table, got, spreads, held, heat):
@@ -365,7 +365,7 @@
             heat[half, pl.ds(odd, SLOTS * CB, 2), :] = coarse[:, half * 128 : half * 128 + 128]
 
 
-def step(table, phase, solute, heat, got, own, laps, all_records, ghosts):
+def step(table, phase, solute, heat, got, own, stencil, places, all_records, ghosts):
     records = all_records.shape[0] - 2 * SLOTS
     count = got.shape[0]
     cap = records // count
@@ -378,11 +378,13 @@
         ghosts[slot, 0:TE, :] = out
         ghosts[slot, TE:REC, :] = edge
     beside = jnp.concatenate(halves(ghosts[:, 0:TE, :].reshape(SLOTS * TE, 128)), axis=1)
+    beside = dot(beside, places)
     row = iota((SLOTS, TE, PLANE), 1)
     lap = []
-    for number, (field, table) in enumerate(((phase, laps[0]), (solute, laps[1]))):
-        flat = field.reshape(SLOTS * TE, PLANE)
-        total = dot(jnp.concatenate([*halves(flat), beside], axis=1), table)
+    for number, field in enumerate((phase, solute)):
+        high, low = halves(field.reshape(SLOTS * TE, PLANE))
+        total = dot(high, stencil) + dot(low, stencil)
+        total += beside[:, number * PLANE : number * PLANE + PLANE]
         total = total.reshape(SLOTS, TE, PLANE) - 6.0 * field
         sides = []
         for face in range(2):
@@ -403,42 +405,42 @@
 
 
 def first_step_kernel(
-    cap, table, senders, phase, solute, got, own, picks, lap0, lap1, spreads, brick,
+    cap, table, phase, solute, got, own, picks, stencil, places, spreads, brick,
     phase_out, solute_out, heat_out, own_out, send, brick_out, all_records, ghosts, held, sem,
 ):
     copy = pltpu.make_async_copy(brick, brick_out, sem)
     copy.start()
     take_heat(cap, table, got, spreads[...], held, heat_out)
     new_phase, new_solute = step(
-        table, phase[...], solute[...], heat_out[...], got, own, (lap0[...], lap1[...]),
+        table, phase[...], solute[...], heat_out[...], got, own, stencil[...], places[...],
         all_records, ghosts,
     )
     phase_out[...] = new_phase
     solute_out[...] = new_solute
     write_records(new_phase, new_solute, picks[...], own_out)
-    pack(own_out, senders, send)
+    pack(own_out, table, send)
     copy.wait()
 
 
 def middle_step_kernel(
-    table, senders, phase, solute, heat, got, own, picks, lap0, lap1,
+    table, phase, solute, heat, got, own, picks, stencil, places,
     phase_out, solute_out, own_out, send, all_records, ghosts,
 ):
     new_phase, new_solute = step(
-        table, phase[...], solute[...], heat[...], got, own, (lap0[...], lap1[...]),
+        table, phase[...], solute[...], heat[...], got, own, stencil[...], places[...],
         all_records, ghosts,
     )
     phase_out[...] = new_phase
     solute_out[...] = new_solute
     write_records(new_phase, new_solute, picks[...], own_out)
-    pack(own_out, senders, send)
+    pack(own_out, table, send)
 
 
 def last_step_kernel(
-    table, phase, solute, heat, got, own, lap0, lap1, phase_out, solute_out, all_records, ghosts
+    table, phase, solute, heat, got, own, stencil, places, phase_out, solute_out, all_records, ghosts
 ):
     new_phase, new_solute = step(
-        table, phase[...], solute[...], heat[...], got, own, (lap0[...], lap1[...]),
+        table, phase[...], solute[...], heat[...], got, own, stencil[...], places[...],
         all_records, ghosts,
     )
     phase_out[...] = new_phase
@@ -467,17 +469,16 @@
     block_cap = 2 * SLOTS // count
     records = count * plane_cap
     bx, by, bz = enthalpy.shape
-    picks, lap0, lap1, spreads = tables()
+    picks, stencil, places, spreads = tables()
 
     integers = functools.partial(jax.ShapeDtypeStruct, dtype=jnp.int32)
-    sides, asked, table, senders = call(
-        functools.partial(sides_kernel, sizes, block_cap),
+    sides, asked, table = call(
+        functools.partial(sides_kernel, sizes, plane_cap),
         [VMEM] * 3 + [ANY] * 2,
         [
             shape(sizes[0] * sizes[1], 3 * bx, 128),
             shape(count, 128),
             integers((8, 128)),
-            integers((records, 128)),
         ],
         [pltpu.VMEM((bx, by, bz), F32)] * 2 + [pltpu.SemaphoreType.DMA((2 * bx,))],
         mib=56,
@@ -494,24 +495,33 @@
     solute_field = solute.reshape(SLOTS, TE, PLANE)
     own_shape, send_shape = shape(2 * SLOTS, REC, 128), shape(count, plane_cap * REC, 128)
     own, packed = call(first_pack_kernel, [SMEM] + [VMEM] * 3, [own_shape, send_shape])(
-        senders, phase_field, solute_field, picks
-    )
-
-    layers = call(
+        table, phase_field, solute_field, picks
+    )
+
+    layer = shape(3 * by + 8, bz)
+    down, up, *farther = call(
         functools.partial(layers_kernel, sizes),
         [VMEM] * 4 + [ANY],
-        shape(count, 3 * by + 8, bz),
+        [layer, layer] + [shape(8, 128)] * (count - 3),
     )(enthalpy, conductivity, sides, asked, packed)
-    layers = lax.all_to_all(layers, "gx", split_axis=0, concat_axis=0, tiled=True)
-    request = layers[:, 3 * by + 4, :block_cap].astype(jnp.int32)
+
+    def pass_on(value, shift):
+        return lax.ppermute(value, "gx", [(i, (i + shift) % count) for i in range(count)])
+
+    from_low, from_high = pass_on(up, 1), pass_on(down, count - 1)
+    farther = [pass_on(value, 2 + number) for number, value in enumerate(farther)]
+    row = 3 * by + 4
+    request = [asked[0:1], from_low[row : row + 1]]
+    request += [value[0:1] for value in farther] + [from_high[row : row + 1]]
+    request = jnp.concatenate(request, axis=0)[:, :block_cap].astype(jnp.int32)
     _, deep = block_layout(block_cap)
     brick = shape(bx, by, bz)
     heated, send = call(
         functools.partial(heat_kernel, block_cap, sizes),
-        [SMEM] + [VMEM] * 5,
+        [SMEM] + [VMEM] * 6,
         [brick, shape(count, plane_cap * REC + deep * CB, 128)],
         [pltpu.VMEM((bx, by // CB, CB, bz), F32)],
-    )(request, enthalpy, conductivity, sides, layers, packed)
+    )(request, enthalpy, conductivity, sides, from_low, from_high, packed)
     got = lax.all_to_all(send, "gx", split_axis=0, concat_axis=0, tiled=True)
 
     field = shape(SLOTS, TE, PLANE)
@@ -521,23 +531,23 @@
     ]
     phase_field, solute_field, heat, own, send, heat_out = call(
         functools.partial(first_step_kernel, block_cap),
-        [SMEM] * 2 + [VMEM] * 9,
+        [SMEM] + [VMEM] * 9,
         [field, field, shape(2, SLOTS * TE, 128), own_shape, send_shape, brick],
         step_scratch + [pltpu.VMEM((SLOTS * CB, CB, 128), F32), pltpu.SemaphoreType.DMA],
         [VMEM] * 5 + [ANY],
     )(
-        table, senders, phase_field, solute_field, got, own, picks, lap0, lap1, spreads,
+        table, phase_field, solute_field, got, own, picks, stencil, places, spreads,
         heated,
     )
     for _ in range(PHASE_STEPS - 2):
         got = lax.all_to_all(send, "gx", split_axis=0, concat_axis=0, tiled=True)
         phase_field, solute_field, own, send = call(
-            middle_step_kernel, [SMEM] * 2 + [VMEM] * 8, [field, field, own_shape, send_shape], step_scratch
-        )(table, senders, phase_field, solute_field, heat, got, own, picks, lap0, lap1)
+            middle_step_kernel, [SMEM] + [VMEM] * 8, [field, field, own_shape, send_shape], step_scratch
+        )(table, phase_field, solute_field, heat, got, own, picks, stencil, places)
     got = lax.all_to_all(send, "gx", split_axis=0, concat_axis=0, tiled=True)
     phase_field, solute_field = call(
         last_step_kernel, [SMEM] + [VMEM] * 7, [field, field], step_scratch
-    )(table, phase_field, solute_field, heat, got, own, lap0, lap1)
+    )(table, phase_field, solute_field, heat, got, own, stencil, places)
     return heat_out, phase_field.reshape(phase.shape), solute_field.reshape(solute.shape)
 
 

time: 85.7 us -> 79 us (0.922)
  blocking collectives: 60.1 us -> 46.1 us
  starting transfers between devices: 5.18 us -> 9.85 us
  waiting for transfers between devices: 2.01 us -> 5.31 us
    all_to_all x1 -> x0, blocking collectives: 12.5 us -> none  [local(): lax.all_to_all(layers, 'gx', split_axis=0, concat_axis=0, tiled=True)]
    ppermute x0 -> x3, starting transfers between devices: none -> 4.67 us  [pass_on(): lax.ppermute(value, 'gx', [(i, (i + shift) % count) for i in range(count)])]
    ppermute x0 -> x3, waiting for transfers between devices: none -> 3.72 us  [pass_on(): lax.ppermute(value, 'gx', [(i, (i + shift) % count) for i in range(count)])]
    all_to_all x4, blocking collectives: 47.7 us -> 46.1 us  [local(): got = lax.all_to_all(send, 'gx', split_axis=0, concat_axis=0, tiled=True)]
    unnamed x26 -> x24, local copies, waits for them, and re-layouts: 2.69 us -> 2.62 us
  transfers between devices with their start and end apart: 1 -> 4, of which waited for: 1 -> 2; matrix products, arithmetic and copies ran while one was open for 0% -> 0% of each run, Pallas kernels for 1% -> 1%
where the time goes in v4:
time: 79 us; the launch traced here: 78.4 us
  blocking collectives  46.1 us (58%)
  Pallas kernels  13.7 us (17%)
  starting transfers between devices  9.85 us (12%)
  waiting for transfers between devices  5.31 us (7%)
  local copies, waits for them, and re-layouts  2.63 us (3%)
  between operations  0.81 us (1%)
    all_to_all x4, blocking collectives, local(): got = lax.all_to_all(send, 'gx', split_axis=0, concat_axis=0, tiled=True)  46.1 us
    all_to_all x1, starting transfers between devices, local(): lax.all_to_all(sides, ('gy', 'gz'), split_axis=0, concat_axis=0, tiled=True)  5.18 us
    ppermute x3, starting transfers between devices, pass_on(): lax.ppermute(value, 'gx', [(i, (i + shift) % count) for i in range(count)])  4.67 us
    ppermute x3, waiting for transfers between devices, pass_on(): lax.ppermute(value, 'gx', [(i, (i + shift) % count) for i in range(count)])  3.72 us
    pallas_call x2, Pallas kernels, local(): call(middle_step_kernel, [SMEM] + [VMEM] * 8, [field, field, own_shape, s...  3.25 us
    pallas_call x1, Pallas kernels, local(): call(functools.partial(sides_kernel, sizes, plane_cap), [VMEM] * 3 + [ANY...  2.91 us
    unnamed x24, local copies, waits for them, and re-layouts  2.62 us
    pallas_call x1, Pallas kernels, local(): call(functools.partial(first_step_kernel, block_cap), [SMEM] + [VMEM] * 9...  2.55 us
  transfers between devices with their start and end apart: 4, of which 2 were waited for; matrix products, arithmetic and copies ran while one was open for 0% of the time, Pallas kernels for 1%

profile of v4, /device:TPU:0, one launch (start us, length us, event | category | flops | bytes accessed | tf_op | source)
XLA Modules:
  0.0 78.4 jit_solution(11307989929824128331)
XLA Ops:
  0.6 0.0 copy-start.1
  0.6 2.9 %shard_map.130 = (f32[8,24,128]{2,1,0:T(8,128)}, f32[4,128]{1,0:T(4,128)}, s32[8,128]{1,0:T(8,128)}) custom-call(s32[1,16]{1,0:T(1,128)} %bitcast.14, s32[1,16]{1,0:T(1,128)} %bitcast.15, s32[6,1,16]{2,1,0:T(1,128)} %bitcast.13, f32[8,32,128]{2,1,0:T(8,128)} %h.3, f32[8,32,128]{2,1,0:T(8,128)} %k.3), custom_call_target="tpu_custom_call" | custom-call | tf_op jit(solution)/shard_map/pallas_call | solution.py:475
  3.6 5.2 %all-to-all-start = ((f32[8,24,128]{2,1,0:T(8,128)}), f32[8,24,128]{2,1,0:T(8,128)S(1)}, u32[]{:S(2)}, u32[]{:S(2)}) async-start(f32[8,24,128]{2,1,0:T(8,128)} %get-tuple-element.31), calls=%async_computation | async-start | bytes 196608 | tf_op jit(solution)/shard_map/all_to_all | solution.py:492
  8.7 0.0 copy-start.10
  8.7 0.0 copy-done.1
  8.8 0.7 copy-done.10
  9.4 0.0 copy-start.5
  9.4 0.9 %copy-done.5 = f32[1,1,1,16,16,256]{5,4,3,2,1,0:T(8,128)S(1)} copy-done((f32[1,1,1,16,16,256]{5,4,3,2,1,0:T(8,128)S(1)}, f32[1,1,1,16,16,256]{5,4,3,2,1,0:T(8,128)}, u32[]{:S(2)}) %copy-start.5) | copy-done | bytes 262168
  10.4 0.0 copy-start.7
  10.4 0.9 %copy-done.7 = f32[1,1,1,16,16,256]{5,4,3,2,1,0:T(8,128)S(1)} copy-done((f32[1,1,1,16,16,256]{5,4,3,2,1,0:T(8,128)S(1)}, f32[1,1,1,16,16,256]{5,4,3,2,1,0:T(8,128)}, u32[]{:S(2)}) %copy-start.7) | copy-done | bytes 262168
  11.3 0.0 copy-start.3
  11.3 0.0 copy-start.4
  11.3 1.0 %shard_map.131 = (f32[32,24,128]{2,1,0:T(8,128)S(1)}, f32[4,144,128]{2,1,0:T(8,128)S(1)}) custom-call(s32[8,128]{1,0:T(8,128)S(1)} %copy-done.10, f32[16,16,256]{2,1,0:T(8,128)S(1)} %bitcast.9, f32[16,16,256]{2,1,0:T(8,128)S(1)} %bitcast.11, bf16[512,256]{1,0:T(8,128)(2,1)S(1)} %copy-done.1), custom_call_target="tpu_custom_call" | custom-call | tf_op jit(solution)/shard_map/pallas_call | solution.py:497
  12.3 0.0 copy-start.11
  12.3 1.6 %all-to-all-done.got = f32[8,24,128]{2,1,0:T(8,128)S(1)} async-done(((f32[8,24,128]{2,1,0:T(8,128)}), f32[8,24,128]{2,1,0:T(8,128)S(1)}, u32[]{:S(2)}, u32[]{:S(2)}) %all-to-all-start) | async-done | bytes 98336 | tf_op jit(solution)/shard_map/all_to_all | solution.py:492
  13.9 0.0 copy-done.3
  13.9 0.0 copy-done.4
  13.9 0.0 copy-done.11
  14.0 1.6 %collective-permute-start = (f32[104,128]{1,0:T(8,128)S(1)}, f32[104,128]{1,0:T(8,128)S(1)}, u32[]{:S(2)}, u32[]{:S(2)}) collective-permute-start(f32[104,128]{1,0:T(8,128)S(1)} %get-tuple-element.33), channel_id=1, source_target_pairs={{0,8},{8,16},{16,24},{24,0},{1,9},{9,17},{17,25},{25,1},{2,10},{10... | collective-permute-start | bytes 159752 | tf_op jit(solution)/shard_map/ppermute | solution.py:509
  15.6 2.2 %collective-permute-start.2 = (f32[104,128]{1,0:T(8,128)S(1)}, f32[104,128]{1,0:T(8,128)S(1)}, u32[]{:S(2)}, u32[]{:S(2)}) collective-permute-start(f32[104,128]{1,0:T(8,128)S(1)} %get-tuple-element.35), channel_id=1, source_target_pairs={{0,24},{8,0},{16,8},{24,16},{1,25},{9,1},{17,9},{25,17},{2,26},{10... | collective-permute-start | bytes 159752 | tf_op jit(solution)/shard_map/ppermute | solution.py:509
  17.9 0.8 %collective-permute-start.1 = (f32[8,128]{1,0:T(8,128)S(1)}, f32[8,128]{1,0:T(8,128)S(1)}, u32[]{:S(2)}, u32[]{:S(2)}) collective-permute-start(f32[8,128]{1,0:T(8,128)S(1)} %get-tuple-element.34), channel_id=1, source_target_pairs={{0,16},{8,24},{16,0},{24,8},{1,17},{9,25},{17,1},{25,9},{2,18},{10... | collective-permute-start | bytes 12296 | tf_op jit(solution)/shard_map/ppermute | solution.py:509
  18.7 3.7 %collective-permute-done.1 = f32[8,128]{1,0:T(8,128)S(1)} collective-permute-done((f32[8,128]{1,0:T(8,128)S(1)}, f32[8,128]{1,0:T(8,128)S(1)}, u32[]{:S(2)}, u32[]{:S(2)}) %collective-permute-start.1) | collective-permute-done | bytes 4128 | tf_op jit(solution)/shard_map/ppermute | solution.py:509
  22.4 0.0 collective-permute-done.low
  22.4 0.0 collective-permute-done.2.high
  22.4 0.0 copy-start.8
  22.4 0.0 copy-start.9
  22.5 1.9 %shard_map.133 = (f32[8,32,128]{2,1,0:T(8,128)S(1)}, f32[4,176,128]{2,1,0:T(8,128)S(1)}) custom-call(s32[4,8]{1,0:T(4,128)S(1)} %slice_convert_fusion.request, f32[8,32,128]{2,1,0:T(8,128)S(1)} %copy-done.3, f32[8,32,128]{2,1,0:T(8,128)S(1)} %copy-done.4, f32[8,24,128]{2,1,0:T(8,128)S(1)} %all-to-all-done.got, f32[104,128]{1,0:T(8,128)S(1)} %collective-permute-done.low, ...), custom_call_target="tpu_custom_call" | custom-call | tf_op jit(solution)/shard_map/pallas_call | solution.py:519
  24.4 0.0 copy-start
  24.4 0.0 copy-start.2
  24.4 0.0 copy-start.6
  24.4 12.2 %all_to_all.25.got = f32[4,176,128]{2,1,0:T(8,128)S(1)} all-to-all(f32[4,176,128]{2,1,0:T(8,128)S(1)} %get-tuple-element.36), channel_id=1, replica_groups=mesh['gx'=4,'gy'=2,'gz'=4] {'gx'}, dimensions={0} | all-to-all | bytes 720896 | tf_op jit(solution)/shard_map/all_to_all | solution.py:525
  36.6 0.0 copy-done.8
  36.6 0.0 copy-done.9
  36.6 0.0 copy-done
  36.6 0.0 copy-done.2
  36.6 0.0 copy-done.6
  36.6 2.5 %shard_map.134 = (f32[16,16,256]{2,1,0:T(8,128)S(1)}, f32[16,16,256]{2,1,0:T(8,128)S(1)}, f32[2,256,128]{2,1,0:T(8,128)S(1)}, f32[32,24,128]{2,1,0:T(8,128)S(1)}...) custom-call(s32[8,128]{1,0:T(8,128)S(1)} %copy-done.10, f32[16,16,256]{2,1,0:T(8,128)S(1)} %bitcast.10, ...), custom_call_target="tpu_custom_call" | custom-call | tf_op jit(solution)/shard_map/pallas_call | solution.py:532
  39.2 11.1 %all_to_all.26.got = f32[4,144,128]{2,1,0:T(8,128)S(1)} all-to-all(f32[4,144,128]{2,1,0:T(8,128)S(1)} %get-tuple-element.43), channel_id=1, replica_groups=mesh['gx'=4,'gy'=2,'gz'=4] {'gx'}, dimensions={0} | all-to-all | bytes 589824 | tf_op jit(solution)/shard_map/all_to_all | solution.py:543
  50.2 1.6 %shard_map.135 = (f32[16,16,256]{2,1,0:T(8,128)S(1)}, f32[16,16,256]{2,1,0:T(8,128)S(1)}, f32[32,24,128]{2,1,0:T(8,128)S(1)}, f32[4,144,128]{2,1,0:T(8,128)S(1)}) custom-call(s32[8,128]{1,0:T(8,128)S(1)} %copy-done.10, f32[16,16,256]{2,1,0:T(8,128)S(1)} %get-tuple-element.40.phase, f32[16,16,256]{2,1,0:T(8,128)S(1)} %get-tuple-element.41.solute, ...), custom_call_target="tpu_custom_call" | custom-call | tf_op jit(solution)/shard_map/pallas_call | solution.py:544
  51.9 11.5 %all_to_all.27.got = f32[4,144,128]{2,1,0:T(8,128)S(1)} all-to-all(f32[4,144,128]{2,1,0:T(8,128)S(1)} %get-tuple-element.47), channel_id=1, replica_groups=mesh['gx'=4,'gy'=2,'gz'=4] {'gx'}, dimensions={0} | all-to-all | bytes 589824 | tf_op jit(solution)/shard_map/all_to_all | solution.py:543
  63.3 1.6 %shard_map.136 = (f32[16,16,256]{2,1,0:T(8,128)S(1)}, f32[16,16,256]{2,1,0:T(8,128)S(1)}, f32[32,24,128]{2,1,0:T(8,128)S(1)}, f32[4,144,128]{2,1,0:T(8,128)S(1)}) custom-call(s32[8,128]{1,0:T(8,128)S(1)} %copy-done.10, f32[16,16,256]{2,1,0:T(8,128)S(1)} %get-tuple-element.45.phase, f32[16,16,256]{2,1,0:T(8,128)S(1)} %get-tuple-element.46.solute, ...), custom_call_target="tpu_custom_call" | custom-call | tf_op jit(solution)/shard_map/pallas_call | solution.py:544
  65.0 11.4 %all_to_all.28.got = f32[4,144,128]{2,1,0:T(8,128)S(1)} all-to-all(f32[4,144,128]{2,1,0:T(8,128)S(1)} %get-tuple-element.51), channel_id=1, replica_groups=mesh['gx'=4,'gy'=2,'gz'=4] {'gx'}, dimensions={0} | all-to-all | bytes 589824 | tf_op jit(solution)/shard_map/all_to_all | solution.py:547
  76.3 2.0 %shard_map.137 = (f32[16,16,256]{2,1,0:T(8,128)}, f32[16,16,256]{2,1,0:T(8,128)}) custom-call(s32[8,128]{1,0:T(8,128)S(1)} %copy-done.10, f32[16,16,256]{2,1,0:T(8,128)S(1)} %get-tuple-element.49.phase, f32[16,16,256]{2,1,0:T(8,128)S(1)} %get-tuple-element.50.solute, f32[2,256,128]{2,1,0:T(8,128)S(1)} %get-tuple-element.42.heat, ...), custom_call_target="tpu_custom_call" | custom-call | tf_op jit(solution)/shard_map/pallas_call | solution.py:548
  (7 shorter events, 0.1 us)
Async XLA Ops:
  0.6 8.1 %copy-start.1 = (bf16[512,256]{1,0:T(8,128)(2,1)S(1)}, bf16[512,256]{1,0:T(8,128)(2,1)}, u32[]{:S(2)}) copy-start(bf16[512,256]{1,0:T(8,128)(2,1)} %constant.8.clone.picks) | copy-start | bytes 786436
  3.6 10.4 %all-to-all-start = ((f32[8,24,128]{2,1,0:T(8,128)}), f32[8,24,128]{2,1,0:T(8,128)S(1)}, u32[]{:S(2)}, u32[]{:S(2)}) async-start(f32[8,24,128]{2,1,0:T(8,128)} %get-tuple-element.31), calls=%async_computation | async-start | bytes 196608 | tf_op jit(solution)/shard_map/all_to_all | solution.py:492
  8.7 0.7 copy-start.10
  9.4 0.9 %copy-start.5 = (f32[1,1,1,16,16,256]{5,4,3,2,1,0:T(8,128)S(1)}, f32[1,1,1,16,16,256]{5,4,3,2,1,0:T(8,128)}, u32[]{:S(2)}) copy-start(f32[1,1,1,16,16,256]{5,4,3,2,1,0:T(8,128)} %param.13) | copy-start | bytes 786436
  10.4 0.9 %copy-start.7 = (f32[1,1,1,16,16,256]{5,4,3,2,1,0:T(8,128)S(1)}, f32[1,1,1,16,16,256]{5,4,3,2,1,0:T(8,128)}, u32[]{:S(2)}) copy-start(f32[1,1,1,16,16,256]{5,4,3,2,1,0:T(8,128)} %param.14) | copy-start | bytes 786436
  11.3 2.6 %copy-start.3 = (f32[8,32,128]{2,1,0:T(8,128)S(1)}, f32[8,32,128]{2,1,0:T(8,128)}, u32[]{:S(2)}) copy-start(f32[8,32,128]{2,1,0:T(8,128)} %h.3) | copy-start | bytes 393220
  11.3 2.6 %copy-start.4 = (f32[8,32,128]{2,1,0:T(8,128)S(1)}, f32[8,32,128]{2,1,0:T(8,128)}, u32[]{:S(2)}) copy-start(f32[8,32,128]{2,1,0:T(8,128)} %k.3) | copy-start | bytes 393220
  12.3 1.6 %copy-start.11 = (f32[4,128]{1,0:T(4,128)S(1)}, f32[4,128]{1,0:T(4,128)}, u32[]{:S(2)}) copy-start(f32[4,128]{1,0:T(4,128)} %get-tuple-element.30.asked) | copy-start | bytes 6148
  14.0 8.4 %collective-permute-start = (f32[104,128]{1,0:T(8,128)S(1)}, f32[104,128]{1,0:T(8,128)S(1)}, u32[]{:S(2)}, u32[]{:S(2)}) collective-permute-start(f32[104,128]{1,0:T(8,128)S(1)} %get-tuple-element.33), channel_id=1, source_target_pairs={{0,8},{8,16},{16,24},{24,0},{1,9},{9,17},{17,25},{25,1},{2,10},{10... | collective-permute-start | bytes 159752 | tf_op jit(solution)/shard_map/ppermute | solution.py:509
  15.6 6.8 %collective-permute-start.2 = (f32[104,128]{1,0:T(8,128)S(1)}, f32[104,128]{1,0:T(8,128)S(1)}, u32[]{:S(2)}, u32[]{:S(2)}) collective-permute-start(f32[104,128]{1,0:T(8,128)S(1)} %get-tuple-element.35), channel_id=1, source_target_pairs={{0,24},{8,0},{16,8},{24,16},{1,25},{9,1},{17,9},{25,17},{2,26},{10... | collective-permute-start | bytes 159752 | tf_op jit(solution)/shard_map/ppermute | solution.py:509
  17.9 4.5 %collective-permute-start.1 = (f32[8,128]{1,0:T(8,128)S(1)}, f32[8,128]{1,0:T(8,128)S(1)}, u32[]{:S(2)}, u32[]{:S(2)}) collective-permute-start(f32[8,128]{1,0:T(8,128)S(1)} %get-tuple-element.34), channel_id=1, source_target_pairs={{0,16},{8,24},{16,0},{24,8},{1,17},{9,25},{17,1},{25,9},{2,18},{10... | collective-permute-start | bytes 12296 | tf_op jit(solution)/shard_map/ppermute | solution.py:509
  22.4 14.2 %copy-start.8 = (f32[1,1,1,16,16,256]{5,4,3,2,1,0:T(8,128)S(1)}, f32[1,1,1,16,16,256]{5,4,3,2,1,0:T(8,128)}, u32[]{:S(2)}) copy-start(f32[1,1,1,16,16,256]{5,4,3,2,1,0:T(8,128)} %param.14) | copy-start | bytes 786436
  22.4 14.2 %copy-start.9 = (bf16[256,256]{1,0:T(8,128)(2,1)S(1)}, bf16[256,256]{1,0:T(8,128)(2,1)}, u32[]{:S(2)}) copy-start(bf16[256,256]{1,0:T(8,128)(2,1)} %constant.11.clone.spreads) | copy-start | bytes 393220
  24.4 12.2 %copy-start = (bf16[256,512]{1,0:T(8,128)(2,1)S(1)}, bf16[256,512]{1,0:T(8,128)(2,1)}, u32[]{:S(2)}) copy-start(bf16[256,512]{1,0:T(8,128)(2,1)} %constant.10.clone.places) | copy-start | bytes 786436
  24.4 12.2 %copy-start.2 = (bf16[256,256]{1,0:T(8,128)(2,1)S(1)}, bf16[256,256]{1,0:T(8,128)(2,1)}, u32[]{:S(2)}) copy-start(bf16[256,256]{1,0:T(8,128)(2,1)} %constant.9.clone.stencil) | copy-start | bytes 393220
  24.4 12.2 %copy-start.6 = (f32[1,1,1,16,16,256]{5,4,3,2,1,0:T(8,128)S(1)}, f32[1,1,1,16,16,256]{5,4,3,2,1,0:T(8,128)}, u32[]{:S(2)}) copy-start(f32[1,1,1,16,16,256]{5,4,3,2,1,0:T(8,128)} %param.13) | copy-start | bytes 786436

commit v5 on v4

--- a/solution.py
+++ b/solution.py
@@ -128,8 +128,12 @@
 def write_tables(plane_cap, source, block, neighbour, asked, table):
     me = lax.axis_index("gx").astype(F32)
     count = asked.shape[0]
-    records = count * plane_cap
+    records = (count - 1) * plane_cap
     cap = float(plane_cap)
+
+    def wrapped(shift):
+        return jnp.where(shift < 0.0, shift + float(count), shift)
+
     square = (SLOTS, SLOTS)
     before = iota(square, 0) < iota(square, 1)
     slot = iota((1, SLOTS), 1).astype(F32)
@@ -141,11 +145,9 @@
     rank_column = column_of(rank)
     lane = iota((SLOTS, 128), 1).astype(F32)
     for shift in range(count):
-        owner = me + float(shift)
-        owner = jnp.where(owner >= float(count), owner - float(count), owner)
-        hit = (source_column == owner) & (rank_column == lane)
+        hit = (wrapped(source_column - me) == float(shift)) & (rank_column == lane)
         asked[shift : shift + 1, :] = jnp.sum(jnp.where(hit, block_column, 0.0), axis=0, keepdims=True)
-    table[6:7, 0:SLOTS] = source[...]
+    table[6:7, 0:SLOTS] = wrapped(me - source_row).astype(jnp.int32)
     table[7:8, 0:SLOTS] = rank.astype(jnp.int32)
     slot_column = iota((SLOTS, records), 0).astype(F32)
     for face in range(FACES):
@@ -159,10 +161,11 @@
         )
         send_rank = jnp.sum(jnp.where(alike & before, 1.0, 0.0), axis=0, keepdims=True)
         here = records + (number_row - owner_row * SLOTS)
-        receive = jnp.where(owner_row == me, here, owner_row * cap + receive_rank)
+        there = (wrapped(me - owner_row) - 1.0) * cap + receive_rank
+        receive = jnp.where(owner_row == me, here, there)
         receive = jnp.where(number_row < 0.0, records + SLOTS + slot, receive)
         table[face : face + 1, 0:SLOTS] = receive.astype(jnp.int32)
-        key = jnp.where(other_row, owner_row * cap + send_rank, -1.0)
+        key = jnp.where(other_row, (wrapped(owner_row - me) - 1.0) * cap + send_rank, -1.0)
         hit = iota((SLOTS, records), 1).astype(F32) == column_of(key)
         tile = jnp.sum(jnp.where(hit, slot_column, 0.0), axis=0, keepdims=True)
         table[face ^ 1 : (face ^ 1) + 1, SLOTS : SLOTS + records] = tile.astype(jnp.int32)
@@ -241,11 +244,14 @@
     return h + RATE * k * (total - 6.0 * t)
 
 
-def heat_kernel(cap, sizes, request, h, k, got, low, high, packed, out, send, held):
+def heat_kernel(cap, sizes, request, h, k, got, low, high, *rest):
+    count = lax.axis_size("gx")
+    packed, (out, found, *send, held) = rest[: count - 1], rest[count - 1 :]
+
     bx, by, bz = h.shape
     h0, k0 = h[...], k[...]
     read = side_reader(sizes, got, bx)
-    count, me = send.shape[0], lax.axis_index("gx")
+    me = lax.axis_index("gx")
     layers, lines = [], []
     for beside, inside in ((low, me > 0), (high, me < count - 1)):
         beside = jnp.where(inside, beside[...], 0.0)
@@ -287,20 +293,23 @@
     parts, deep = block_layout(cap)
     nby, nbz = by // CB, bz // CB
     group = iota((deep, CB, bz), 2) // CB
-    for owner in range(count):
-        shift = lax.rem(me - owner + count, count)
+    for shift in range(count):
         total = jnp.zeros((deep, CB, bz), F32)
         for rank in range(cap):
-            block = request[shift, rank]
+            block = request[(count - shift) % count, rank]
             a, b, c = block // (nby * nbz), (block // nbz) % nby, block % nbz
             for part in range(parts):
                 at = rank * parts + part
                 patch = held[pl.ds(a * CB + part * deep, deep), b]
                 moved = pltpu.roll(patch, (CB * at - CB * c + bz) % bz, 2)
                 total = jnp.where(group == at, moved, total)
-        behind = packed.shape[1]
-        send[owner, 0:behind, :] = packed[owner]
-        send[owner, behind:, :] = total.reshape(deep * CB, bz)
+        total = total.reshape(deep * CB, bz)
+        if shift == 0:
+            found[...] = total
+        else:
+            behind = packed[shift - 1].shape[0]
+            send[shift - 1][0:behind, :] = packed[shift - 1][...]
+            send[shift - 1][behind:, :] = total
 
 
 def write_records(phase, solute, picks, own):
@@ -331,29 +340,31 @@
 
 
 def pack(own, table, send):
-    records = send.shape[0] * (send.shape[1] // REC)
-    cap = records // send.shape[0]
-    for record in range(records):
-        out, edge = merge_record(own, lambda face: table[face, SLOTS + record])
-        owner, row = record // cap, record % cap * REC
-        send[owner, row : row + TE, :] = out
-        send[owner, row + TE : row + REC, :] = edge
-
-
-def first_pack_kernel(table, phase, solute, picks, own, send):
+    cap = send[0].shape[0] // REC
+    for number, out in enumerate(send):
+        for rank in range(cap):
+            record = number * cap + rank
+            planes, edge = merge_record(own, lambda face: table[face, SLOTS + record])
+            out[rank * REC : rank * REC + TE, :] = planes
+            out[rank * REC + TE : rank * REC + REC, :] = edge
+
+
+def first_pack_kernel(table, phase, solute, picks, own, *send):
     write_records(phase[...], solute[...], picks[...], own)
     pack(own, table, send)
 
 
-def take_heat(cap, table, got, spreads, held, heat):
+def take_heat(cap, table, found, got, spreads, blocks, held, heat):
     parts, deep = block_layout(cap)
-    first = got.shape[1] - deep * CB
+    blocks[0] = found[...]
+    for number, value in enumerate(got):
+        blocks[1 + number] = value[value.shape[0] - deep * CB :, :]
     group = iota((CB, 128), 1) // CB
     for slot in range(SLOTS):
-        source, rank = table[6, slot], table[7, slot]
+        back, rank = table[6, slot], table[7, slot]
         for x in range(CB):
-            row = first + (x % deep) * CB
-            patch = got[source, row : row + CB, :]
+            row = (x % deep) * CB
+            patch = blocks[back, row : row + CB, :]
             held[slot * CB + x] = jnp.where(group == rank * parts + x // deep, patch, 0.0)
     rows = held[...].reshape(SLOTS * CB * CB, 128)
     wide = dot(jnp.concatenate(halves(rows), axis=1), spreads)
@@ -367,11 +378,9 @@
 
 def step(table, phase, solute, heat, got, own, stencil, places, all_records, ghosts):
     records = all_records.shape[0] - 2 * SLOTS
-    count = got.shape[0]
-    cap = records // count
-    for owner in range(count):
-        mine = got[owner, 0 : cap * REC, :]
-        all_records[owner * cap : owner * cap + cap] = mine.reshape(cap, REC, 128)
+    cap = records // len(got)
+    for number, value in enumerate(got):
+        all_records[number * cap : number * cap + cap] = value[0 : cap * REC, :].reshape(cap, REC, 128)
     all_records[records : records + 2 * SLOTS] = own[...]
     for slot in range(SLOTS):
         out, edge = merge_record(all_records, lambda face: table[face, slot])
@@ -404,13 +413,14 @@
     return new_phase, new_solute
 
 
-def first_step_kernel(
-    cap, table, phase, solute, got, own, picks, stencil, places, spreads, brick,
-    phase_out, solute_out, heat_out, own_out, send, brick_out, all_records, ghosts, held, sem,
-):
+def first_step_kernel(cap, table, phase, solute, own, picks, stencil, places, spreads, brick, found, *rest):
+    others = lax.axis_size("gx") - 1
+    got, rest = rest[:others], rest[others:]
+    phase_out, solute_out, heat_out, own_out, brick_out, *rest = rest
+    send, (all_records, ghosts, blocks, held, sem) = rest[:others], rest[others:]
     copy = pltpu.make_async_copy(brick, brick_out, sem)
     copy.start()
-    take_heat(cap, table, got, spreads[...], held, heat_out)
+    take_heat(cap, table, found, got, spreads[...], blocks, held, heat_out)
     new_phase, new_solute = step(
         table, phase[...], solute[...], heat_out[...], got, own, stencil[...], places[...],
         all_records, ghosts,
@@ -422,10 +432,10 @@
     copy.wait()
 
 
-def middle_step_kernel(
-    table, phase, solute, heat, got, own, picks, stencil, places,
-    phase_out, solute_out, own_out, send, all_records, ghosts,
-):
+def middle_step_kernel(table, phase, solute, heat, own, picks, stencil, places, *rest):
+    others = lax.axis_size("gx") - 1
+    got, (phase_out, solute_out, own_out, *rest) = rest[:others], rest[others:]
+    send, (all_records, ghosts) = rest[:others], rest[others:]
     new_phase, new_solute = step(
         table, phase[...], solute[...], heat[...], got, own, stencil[...], places[...],
         all_records, ghosts,
@@ -436,9 +446,9 @@
     pack(own_out, table, send)
 
 
-def last_step_kernel(
-    table, phase, solute, heat, got, own, stencil, places, phase_out, solute_out, all_records, ghosts
-):
+def last_step_kernel(table, phase, solute, heat, own, stencil, places, *rest):
+    others = lax.axis_size("gx") - 1
+    got, (phase_out, solute_out, all_records, ghosts) = rest[:others], rest[others:]
     new_phase, new_solute = step(
         table, phase[...], solute[...], heat[...], got, own, stencil[...], places[...],
         all_records, ghosts,
@@ -467,7 +477,8 @@
     sizes = (lax.axis_size("gy"), lax.axis_size("gz"))
     plane_cap = -(-SLOTS // (count - 1))
     block_cap = 2 * SLOTS // count
-    records = count * plane_cap
+    others = count - 1
+    records = others * plane_cap
     bx, by, bz = enthalpy.shape
     picks, stencil, places, spreads = tables()
 
@@ -493,8 +504,8 @@
 
     phase_field = phase.reshape(SLOTS, TE, PLANE)
     solute_field = solute.reshape(SLOTS, TE, PLANE)
-    own_shape, send_shape = shape(2 * SLOTS, REC, 128), shape(count, plane_cap * REC, 128)
-    own, packed = call(first_pack_kernel, [SMEM] + [VMEM] * 3, [own_shape, send_shape])(
+    own_shape, send_shapes = shape(2 * SLOTS, REC, 128), [shape(plane_cap * REC, 128)] * others
+    own, *packed = call(first_pack_kernel, [SMEM] + [VMEM] * 3, [own_shape, *send_shapes])(
         table, phase_field, solute_field, picks
     )
 
@@ -503,7 +514,7 @@
         functools.partial(layers_kernel, sizes),
         [VMEM] * 4 + [ANY],
         [layer, layer] + [shape(8, 128)] * (count - 3),
-    )(enthalpy, conductivity, sides, asked, packed)
+    )(enthalpy, conductivity, sides, asked, packed[0])
 
     def pass_on(value, shift):
         return lax.ppermute(value, "gx", [(i, (i + shift) % count) for i in range(count)])
@@ -516,38 +527,46 @@
     request = jnp.concatenate(request, axis=0)[:, :block_cap].astype(jnp.int32)
     _, deep = block_layout(block_cap)
     brick = shape(bx, by, bz)
-    heated, send = call(
+    heated, found, *send = call(
         functools.partial(heat_kernel, block_cap, sizes),
-        [SMEM] + [VMEM] * 6,
-        [brick, shape(count, plane_cap * REC + deep * CB, 128)],
+        [SMEM] + [VMEM] * (5 + others),
+        [brick, shape(deep * CB, 128)] + [shape(plane_cap * REC + deep * CB, 128)] * others,
         [pltpu.VMEM((bx, by // CB, CB, bz), F32)],
-    )(request, enthalpy, conductivity, sides, from_low, from_high, packed)
-    got = lax.all_to_all(send, "gx", split_axis=0, concat_axis=0, tiled=True)
-
+    )(request, enthalpy, conductivity, sides, from_low, from_high, *packed)
+
+    def exchange(values):
+        return [pass_on(value, 1 + number) for number, value in enumerate(values)]
+
+    got = exchange(send)
     field = shape(SLOTS, TE, PLANE)
     step_scratch = [
         pltpu.VMEM((records + 2 * SLOTS, REC, 128), F32),
         pltpu.VMEM((SLOTS, REC, 128), F32),
     ]
-    phase_field, solute_field, heat, own, send, heat_out = call(
+    phase_field, solute_field, heat, own, heat_out, *send = call(
         functools.partial(first_step_kernel, block_cap),
-        [SMEM] + [VMEM] * 9,
-        [field, field, shape(2, SLOTS * TE, 128), own_shape, send_shape, brick],
-        step_scratch + [pltpu.VMEM((SLOTS * CB, CB, 128), F32), pltpu.SemaphoreType.DMA],
-        [VMEM] * 5 + [ANY],
-    )(
-        table, phase_field, solute_field, got, own, picks, stencil, places, spreads,
-        heated,
-    )
+        [SMEM] + [VMEM] * (9 + others),
+        [field, field, shape(2, SLOTS * TE, 128), own_shape, brick, *send_shapes],
+        step_scratch
+        + [
+            pltpu.VMEM((count, deep * CB, 128), F32),
+            pltpu.VMEM((SLOTS * CB, CB, 128), F32),
+            pltpu.SemaphoreType.DMA,
+        ],
+        [VMEM] * 4 + [ANY] + [VMEM] * others,
+    )(table, phase_field, solute_field, own, picks, stencil, places, spreads, heated, found, *got)
     for _ in range(PHASE_STEPS - 2):
-        got = lax.all_to_all(send, "gx", split_axis=0, concat_axis=0, tiled=True)
-        phase_field, solute_field, own, send = call(
-            middle_step_kernel, [SMEM] + [VMEM] * 8, [field, field, own_shape, send_shape], step_scratch
-        )(table, phase_field, solute_field, heat, got, own, picks, stencil, places)
-    got = lax.all_to_all(send, "gx", split_axis=0, concat_axis=0, tiled=True)
+        got = exchange(send)
+        phase_field, solute_field, own, *send = call(
+            middle_step_kernel,
+            [SMEM] + [VMEM] * (7 + others),
+            [field, field, own_shape, *send_shapes],
+            step_scratch,
+        )(table, phase_field, solute_field, heat, own, picks, stencil, places, *got)
+    got = exchange(send)
     phase_field, solute_field = call(
-        last_step_kernel, [SMEM] + [VMEM] * 7, [field, field], step_scratch
-    )(table, phase_field, solute_field, heat, got, own, stencil, places)
+        last_step_kernel, [SMEM] + [VMEM] * (6 + others), [field, field], step_scratch
+    )(table, phase_field, solute_field, heat, own, stencil, places, *got)
     return heat_out, phase_field.reshape(phase.shape), solute_field.reshape(solute.shape)
 
 

time: 79 us -> 66.6 us (0.84)
  blocking collectives: 46.1 us -> 0 us
  waiting for transfers between devices: 5.31 us -> 23.3 us
  starting transfers between devices: 9.85 us -> 25.7 us
    all_to_all x4 -> x0, blocking collectives: 46.1 us -> none  [local(): got = lax.all_to_all(send, 'gx', split_axis=0, concat_axis=0, tiled=True)]
    ppermute x3 -> x15, waiting for transfers between devices: 3.72 us -> 21.7 us  [pass_on(): lax.ppermute(value, 'gx', [(i, (i + shift) % count) for i in range(count)])]
    ppermute x3 -> x15, starting transfers between devices: 4.67 us -> 20.5 us  [pass_on(): lax.ppermute(value, 'gx', [(i, (i + shift) % count) for i in range(count)])]
  transfers between devices with their start and end apart: 4 -> 16, of which waited for: 2 -> 11; matrix products, arithmetic and copies ran while one was open for 0% -> 0% of each run, Pallas kernels for 1% -> 1%
where the time goes in v5:
time: 66.6 us; the launch traced here: 66 us
  starting transfers between devices  25.7 us (39%)
  waiting for transfers between devices  23.3 us (35%)
  Pallas kernels  13.6 us (20%)
  local copies, waits for them, and re-layouts  2.64 us (4%)
  between operations  0.83 us (1%)
    ppermute x15, waiting for transfers between devices, pass_on(): lax.ppermute(value, 'gx', [(i, (i + shift) % count) for i in range(count)])  21.7 us
    ppermute x15, starting transfers between devices, pass_on(): lax.ppermute(value, 'gx', [(i, (i + shift) % count) for i in range(count)])  20.5 us
    all_to_all x1, starting transfers between devices, local(): lax.all_to_all(sides, ('gy', 'gz'), split_axis=0, concat_axis=0, tiled=True)  5.18 us
    pallas_call x2, Pallas kernels, local(): call(middle_step_kernel, [SMEM] + [VMEM] * (7 + others), [field, field, o...  3.21 us
    pallas_call x1, Pallas kernels, local(): call(functools.partial(sides_kernel, sizes, plane_cap), [VMEM] * 3 + [ANY...  2.91 us
    unnamed x24, local copies, waits for them, and re-layouts  2.63 us
    pallas_call x1, Pallas kernels, local(): call(functools.partial(first_step_kernel, block_cap), [SMEM] + [VMEM] * (...  2.54 us
    pallas_call x1, Pallas kernels, local(): call(last_step_kernel, [SMEM] + [VMEM] * (6 + others), [field, field], st...  2.02 us
  transfers between devices with their start and end apart: 16, of which 11 were waited for; matrix products, arithmetic and copies ran while one was open for 0% of the time, Pallas kernels for 1%

profile of v5, /device:TPU:0, one launch (start us, length us, event | category | flops | bytes accessed | tf_op | source)
XLA Modules:
  0.0 66.0 jit_solution(8345663764209241634)
XLA Ops:
  0.6 0.0 copy-start.1
  0.6 2.9 %shard_map.130 = (f32[8,24,128]{2,1,0:T(8,128)}, f32[4,128]{1,0:T(4,128)}, s32[8,128]{1,0:T(8,128)}) custom-call(s32[1,16]{1,0:T(1,128)} %bitcast.14, s32[1,16]{1,0:T(1,128)} %bitcast.15, s32[6,1,16]{2,1,0:T(1,128)} %bitcast.13, f32[8,32,128]{2,1,0:T(8,128)} %h.3, f32[8,32,128]{2,1,0:T(8,128)} %k.3), custom_call_target="tpu_custom_call" | custom-call | tf_op jit(solution)/shard_map/pallas_call | solution.py:486
  3.6 5.2 %all-to-all-start = ((f32[8,24,128]{2,1,0:T(8,128)}), f32[8,24,128]{2,1,0:T(8,128)S(1)}, u32[]{:S(2)}, u32[]{:S(2)}) async-start(f32[8,24,128]{2,1,0:T(8,128)} %get-tuple-element.43), calls=%async_computation | async-start | bytes 196608 | tf_op jit(solution)/shard_map/all_to_all | solution.py:503
  8.7 0.0 copy-start.10
  8.7 0.0 copy-done.1
  8.8 0.7 %copy-done.10 = s32[8,128]{1,0:T(8,128)S(1)} copy-done((s32[8,128]{1,0:T(8,128)S(1)}, s32[8,128]{1,0:T(8,128)}, u32[]{:S(2)}) %copy-start.10) | copy-done | bytes 4120
  9.4 0.0 copy-start.5
  9.4 0.9 %copy-done.5 = f32[1,1,1,16,16,256]{5,4,3,2,1,0:T(8,128)S(1)} copy-done((f32[1,1,1,16,16,256]{5,4,3,2,1,0:T(8,128)S(1)}, f32[1,1,1,16,16,256]{5,4,3,2,1,0:T(8,128)}, u32[]{:S(2)}) %copy-start.5) | copy-done | bytes 262168
  10.4 0.0 copy-start.7
  10.4 0.9 %copy-done.7 = f32[1,1,1,16,16,256]{5,4,3,2,1,0:T(8,128)S(1)} copy-done((f32[1,1,1,16,16,256]{5,4,3,2,1,0:T(8,128)S(1)}, f32[1,1,1,16,16,256]{5,4,3,2,1,0:T(8,128)}, u32[]{:S(2)}) %copy-start.7) | copy-done | bytes 262168
  11.3 0.0 copy-start.3
  11.3 0.0 copy-start.4
  11.3 1.0 %shard_map.131 = (f32[32,24,128]{2,1,0:T(8,128)S(1)}, f32[144,128]{1,0:T(8,128)S(1)}, f32[144,128]{1,0:T(8,128)S(1)}, f32[144,128]{1,0:T(8,128)S(1)}) custom-call(s32[8,128]{1,0:T(8,128)S(1)} %copy-done.10, f32[16,16,256]{2,1,0:T(8,128)S(1)} %bitcast.9, f32[16,16,256]{2,1,0:T(8,128)S(1)} %bitcast.11, bf16[512,256]{1,0:T(8,128)(2,1)S(1)} %copy-done.1), custom_call_target="tpu_custom_call" | custom-call | tf_op jit(solution)/shard_map/pallas_call | solution.py:508
  12.3 0.0 copy-start.11
  12.3 1.6 %all-to-all-done.got = f32[8,24,128]{2,1,0:T(8,128)S(1)} async-done(((f32[8,24,128]{2,1,0:T(8,128)}), f32[8,24,128]{2,1,0:T(8,128)S(1)}, u32[]{:S(2)}, u32[]{:S(2)}) %all-to-all-start) | async-done | bytes 98336 | tf_op jit(solution)/shard_map/all_to_all | solution.py:503
  13.9 0.0 copy-done.3
  13.9 0.0 copy-done.4
  13.9 0.0 copy-done.11
  13.9 0.0 copy-start.8
  14.0 0.0 copy-start.9
  14.0 1.6 %collective-permute-start = (f32[104,128]{1,0:T(8,128)S(1)}, f32[104,128]{1,0:T(8,128)S(1)}, u32[]{:S(2)}, u32[]{:S(2)}) collective-permute-start(f32[104,128]{1,0:T(8,128)S(1)} %get-tuple-element.45), channel_id=1, source_target_pairs={{0,8},{8,16},{16,24},{24,0},{1,9},{9,17},{17,25},{25,1},{2,10},{10... | collective-permute-start | bytes 159752 | tf_op jit(solution)/shard_map/ppermute | solution.py:520
  15.6 2.2 %collective-permute-start.2 = (f32[104,128]{1,0:T(8,128)S(1)}, f32[104,128]{1,0:T(8,128)S(1)}, u32[]{:S(2)}, u32[]{:S(2)}) collective-permute-start(f32[104,128]{1,0:T(8,128)S(1)} %get-tuple-element.47), channel_id=1, source_target_pairs={{0,24},{8,0},{16,8},{24,16},{1,25},{9,1},{17,9},{25,17},{2,26},{10... | collective-permute-start | bytes 159752 | tf_op jit(solution)/shard_map/ppermute | solution.py:520
  17.9 0.8 %collective-permute-start.1 = (f32[8,128]{1,0:T(8,128)S(1)}, f32[8,128]{1,0:T(8,128)S(1)}, u32[]{:S(2)}, u32[]{:S(2)}) collective-permute-start(f32[8,128]{1,0:T(8,128)S(1)} %get-tuple-element.46), channel_id=1, source_target_pairs={{0,16},{8,24},{16,0},{24,8},{1,17},{9,25},{17,1},{25,9},{2,18},{10... | collective-permute-start | bytes 12296 | tf_op jit(solution)/shard_map/ppermute | solution.py:520
  18.7 3.7 %collective-permute-done.1 = f32[8,128]{1,0:T(8,128)S(1)} collective-permute-done((f32[8,128]{1,0:T(8,128)S(1)}, f32[8,128]{1,0:T(8,128)S(1)}, u32[]{:S(2)}, u32[]{:S(2)}) %collective-permute-start.1) | collective-permute-done | bytes 4128 | tf_op jit(solution)/shard_map/ppermute | solution.py:520
  22.4 0.0 collective-permute-done.low
  22.4 0.0 collective-permute-done.2.high
  22.5 0.0 copy-start
  22.5 0.0 copy-start.2
  22.5 0.0 copy-start.6
  22.5 1.9 %shard_map.133 = (f32[8,32,128]{2,1,0:T(8,128)S(1)}, f32[32,128]{1,0:T(8,128)S(1)}, f32[176,128]{1,0:T(8,128)S(1)}, f32[176,128]{1,0:T(8,128)S(1)}, f32[176,128]{1,0:T(8,128)S(1)}) custom-call(s32[4,8]{1,0:T(4,128)S(1)} %slice_convert_fusion.request, f32[8,32,128]{2,1,0:T(8,128)S(1)} %copy-done.3, f32[8,32,128]{2,1,0:T(8,128)S(1)} %copy-done.4, ...), custom_call_target="tpu_custom_call" | custom-call | tf_op jit(solution)/shard_map/pallas_call | solution.py:530
  24.4 0.1 collective-permute-start.3
  24.5 2.4 %collective-permute-start.4 = (f32[176,128]{1,0:T(8,128)S(1)}, f32[176,128]{1,0:T(8,128)S(1)}, u32[]{:S(2)}, u32[]{:S(2)}) collective-permute-start(f32[176,128]{1,0:T(8,128)S(1)} %get-tuple-element.53), channel_id=1, source_target_pairs={{0,16},{8,24},{16,0},{24,8},{1,17},{9,25},{17,1},{25,9},{2,18},{10... | collective-permute-start | bytes 270344 | tf_op jit(solution)/shard_map/ppermute | solution.py:520
  26.8 1.5 %collective-permute-start.5 = (f32[176,128]{1,0:T(8,128)S(1)}, f32[176,128]{1,0:T(8,128)S(1)}, u32[]{:S(2)}, u32[]{:S(2)}) collective-permute-start(f32[176,128]{1,0:T(8,128)S(1)} %get-tuple-element.54), channel_id=1, source_target_pairs={{0,24},{8,0},{16,8},{24,16},{1,25},{9,1},{17,9},{25,17},{2,26},{10... | collective-permute-start | bytes 270344 | tf_op jit(solution)/shard_map/ppermute | solution.py:520
  28.3 2.8 %collective-permute-done.3.rest_0_ = f32[176,128]{1,0:T(8,128)S(1)} collective-permute-done((f32[176,128]{1,0:T(8,128)S(1)}, f32[176,128]{1,0:T(8,128)S(1)}, u32[]{:S(2)}, u32[]{:S(2)}) %collective-permute-start.3) | collective-permute-done | bytes 90144 | tf_op jit(solution)/shard_map/ppermute | solution.py:520
  31.1 1.9 %collective-permute-done.4.rest_1_ = f32[176,128]{1,0:T(8,128)S(1)} collective-permute-done((f32[176,128]{1,0:T(8,128)S(1)}, f32[176,128]{1,0:T(8,128)S(1)}, u32[]{:S(2)}, u32[]{:S(2)}) %collective-permute-start.4) | collective-permute-done | bytes 90144 | tf_op jit(solution)/shard_map/ppermute | solution.py:520
  33.0 0.0 collective-permute-done.5.rest_2_
  33.0 0.0 copy-done.8
  33.0 0.0 copy-done.9
  33.0 0.0 copy-done
  33.0 0.0 copy-done.2
  33.0 0.0 copy-done.6
  33.0 2.5 %shard_map.134 = (f32[16,16,256]{2,1,0:T(8,128)S(1)}, f32[16,16,256]{2,1,0:T(8,128)S(1)}, f32[2,256,128]{2,1,0:T(8,128)S(1)}, f32[32,24,128]{2,1,0:T(8,128)S(1)}...) custom-call(s32[8,128]{1,0:T(8,128)S(1)} %copy-done.10, ...), custom_call_target="tpu_custom_call" | custom-call | tf_op jit(solution)/shard_map/pallas_call | solution.py:546
  35.5 1.7 %collective-permute-start.6 = (f32[144,128]{1,0:T(8,128)S(1)}, f32[144,128]{1,0:T(8,128)S(1)}, u32[]{:S(2)}, u32[]{:S(2)}) collective-permute-start(f32[144,128]{1,0:T(8,128)S(1)} %get-tuple-element.60), channel_id=1, source_target_pairs={{0,8},{8,16},{16,24},{24,0},{1,9},{9,17},{17,25},{25,1},{2,10},{10... | collective-permute-start | bytes 221192 | tf_op jit(solution)/shard_map/ppermute | solution.py:520
  37.3 1.7 %collective-permute-start.7 = (f32[144,128]{1,0:T(8,128)S(1)}, f32[144,128]{1,0:T(8,128)S(1)}, u32[]{:S(2)}, u32[]{:S(2)}) collective-permute-start(f32[144,128]{1,0:T(8,128)S(1)} %get-tuple-element.61), channel_id=1, source_target_pairs={{0,16},{8,24},{16,0},{24,8},{1,17},{9,25},{17,1},{25,9},{2,18},{10... | collective-permute-start | bytes 221192 | tf_op jit(solution)/shard_map/ppermute | solution.py:520
  38.9 0.8 %collective-permute-start.8 = (f32[144,128]{1,0:T(8,128)S(1)}, f32[144,128]{1,0:T(8,128)S(1)}, u32[]{:S(2)}, u32[]{:S(2)}) collective-permute-start(f32[144,128]{1,0:T(8,128)S(1)} %get-tuple-element.62), channel_id=1, source_target_pairs={{0,24},{8,0},{16,8},{24,16},{1,25},{9,1},{17,9},{25,17},{2,26},{10... | collective-permute-start | bytes 221192 | tf_op jit(solution)/shard_map/ppermute | solution.py:520
  39.7 2.8 %collective-permute-done.6.rest_0_ = f32[144,128]{1,0:T(8,128)S(1)} collective-permute-done((f32[144,128]{1,0:T(8,128)S(1)}, f32[144,128]{1,0:T(8,128)S(1)}, u32[]{:S(2)}, u32[]{:S(2)}) %collective-permute-start.6) | collective-permute-done | bytes 73760 | tf_op jit(solution)/shard_map/ppermute | solution.py:520
  42.5 1.9 %collective-permute-done.7.rest_1_ = f32[144,128]{1,0:T(8,128)S(1)} collective-permute-done((f32[144,128]{1,0:T(8,128)S(1)}, f32[144,128]{1,0:T(8,128)S(1)}, u32[]{:S(2)}, u32[]{:S(2)}) %collective-permute-start.7) | collective-permute-done | bytes 73760 | tf_op jit(solution)/shard_map/ppermute | solution.py:520
  44.4 0.0 collective-permute-done.8.rest_2_
  44.4 1.6 %shard_map.135 = (f32[16,16,256]{2,1,0:T(8,128)S(1)}, f32[16,16,256]{2,1,0:T(8,128)S(1)}, f32[32,24,128]{2,1,0:T(8,128)S(1)}, f32[144,128]{1,0:T(8,128)S(1)}, f3...) custom-call(s32[8,128]{1,0:T(8,128)S(1)} %copy-done.10, f32[16,16,256]{2,1,0:T(8,128)S(1)} %get-tuple-element.56.phase, ...), custom_call_target="tpu_custom_call" | custom-call | tf_op jit(solution)/shard_map/pallas_call | solution.py:560
  46.0 1.4 %collective-permute-start.9 = (f32[144,128]{1,0:T(8,128)S(1)}, f32[144,128]{1,0:T(8,128)S(1)}, u32[]{:S(2)}, u32[]{:S(2)}) collective-permute-start(f32[144,128]{1,0:T(8,128)S(1)} %get-tuple-element.66), channel_id=1, source_target_pairs={{0,8},{8,16},{16,24},{24,0},{1,9},{9,17},{17,25},{25,1},{2,10},{10... | collective-permute-start | bytes 221192 | tf_op jit(solution)/shard_map/ppermute | solution.py:520
  47.4 1.5 %collective-permute-start.10 = (f32[144,128]{1,0:T(8,128)S(1)}, f32[144,128]{1,0:T(8,128)S(1)}, u32[]{:S(2)}, u32[]{:S(2)}) collective-permute-start(f32[144,128]{1,0:T(8,128)S(1)} %get-tuple-element.67), channel_id=1, source_target_pairs={{0,16},{8,24},{16,0},{24,8},{1,17},{9,25},{17,1},{25,9},{2,18},{10... | collective-permute-start | bytes 221192 | tf_op jit(solution)/shard_map/ppermute | solution.py:520
  48.9 1.0 %collective-permute-start.11 = (f32[144,128]{1,0:T(8,128)S(1)}, f32[144,128]{1,0:T(8,128)S(1)}, u32[]{:S(2)}, u32[]{:S(2)}) collective-permute-start(f32[144,128]{1,0:T(8,128)S(1)} %get-tuple-element.68), channel_id=1, source_target_pairs={{0,24},{8,0},{16,8},{24,16},{1,25},{9,1},{17,9},{25,17},{2,26},{10... | collective-permute-start | bytes 221192 | tf_op jit(solution)/shard_map/ppermute | solution.py:520
  49.9 2.4 %collective-permute-done.9.rest_0_ = f32[144,128]{1,0:T(8,128)S(1)} collective-permute-done((f32[144,128]{1,0:T(8,128)S(1)}, f32[144,128]{1,0:T(8,128)S(1)}, u32[]{:S(2)}, u32[]{:S(2)}) %collective-permute-start.9) | collective-permute-done | bytes 73760 | tf_op jit(solution)/shard_map/ppermute | solution.py:520
  52.3 1.8 %collective-permute-done.10.rest_1_ = f32[144,128]{1,0:T(8,128)S(1)} collective-permute-done((f32[144,128]{1,0:T(8,128)S(1)}, f32[144,128]{1,0:T(8,128)S(1)}, u32[]{:S(2)}, u32[]{:S(2)}) %collective-permute-start.10) | collective-permute-done | bytes 73760 | tf_op jit(solution)/shard_map/ppermute | solution.py:520
  54.1 0.0 collective-permute-done.11.rest_2_
  54.1 1.6 %shard_map.136 = (f32[16,16,256]{2,1,0:T(8,128)S(1)}, f32[16,16,256]{2,1,0:T(8,128)S(1)}, f32[32,24,128]{2,1,0:T(8,128)S(1)}, f32[144,128]{1,0:T(8,128)S(1)}, f3...) custom-call(s32[8,128]{1,0:T(8,128)S(1)} %copy-done.10, f32[16,16,256]{2,1,0:T(8,128)S(1)} %get-tuple-element.63.phase, ...), custom_call_target="tpu_custom_call" | custom-call | tf_op jit(solution)/shard_map/pallas_call | solution.py:560
  55.7 1.4 %collective-permute-start.12 = (f32[144,128]{1,0:T(8,128)S(1)}, f32[144,128]{1,0:T(8,128)S(1)}, u32[]{:S(2)}, u32[]{:S(2)}) collective-permute-start(f32[144,128]{1,0:T(8,128)S(1)} %get-tuple-element.72), channel_id=1, source_target_pairs={{0,8},{8,16},{16,24},{24,0},{1,9},{9,17},{17,25},{25,1},{2,10},{10... | collective-permute-start | bytes 221192 | tf_op jit(solution)/shard_map/ppermute | solution.py:520
  57.1 1.9 %collective-permute-start.13 = (f32[144,128]{1,0:T(8,128)S(1)}, f32[144,128]{1,0:T(8,128)S(1)}, u32[]{:S(2)}, u32[]{:S(2)}) collective-permute-start(f32[144,128]{1,0:T(8,128)S(1)} %get-tuple-element.73), channel_id=1, source_target_pairs={{0,16},{8,24},{16,0},{24,8},{1,17},{9,25},{17,1},{25,9},{2,18},{10... | collective-permute-start | bytes 221192 | tf_op jit(solution)/shard_map/ppermute | solution.py:520
  59.0 0.6 collective-permute-start.14
  59.6 2.4 %collective-permute-done.12.rest_0_ = f32[144,128]{1,0:T(8,128)S(1)} collective-permute-done((f32[144,128]{1,0:T(8,128)S(1)}, f32[144,128]{1,0:T(8,128)S(1)}, u32[]{:S(2)}, u32[]{:S(2)}) %collective-permute-start.12) | collective-permute-done | bytes 73760 | tf_op jit(solution)/shard_map/ppermute | solution.py:520
  61.9 1.7 %collective-permute-done.13.rest_1_ = f32[144,128]{1,0:T(8,128)S(1)} collective-permute-done((f32[144,128]{1,0:T(8,128)S(1)}, f32[144,128]{1,0:T(8,128)S(1)}, u32[]{:S(2)}, u32[]{:S(2)}) %collective-permute-start.13) | collective-permute-done | bytes 73760 | tf_op jit(solution)/shard_map/ppermute | solution.py:520
  63.6 0.4 collective-permute-done.14.rest_2_
  64.0 2.0 %shard_map.137 = (f32[16,16,256]{2,1,0:T(8,128)}, f32[16,16,256]{2,1,0:T(8,128)}) custom-call(s32[8,128]{1,0:T(8,128)S(1)} %copy-done.10, f32[16,16,256]{2,1,0:T(8,128)S(1)} %get-tuple-element.69.phase, f32[16,16,256]{2,1,0:T(8,128)S(1)} %get-tuple-element.70.solute, f32[2,256,128]{2,1,0:T(8,128)S(1)} %get-tuple-element.58.heat, ...), custom_call_target="tpu_custom_call" | custom-call | tf_op jit(solution)/shard_map/pallas_call | solution.py:567
  (7 shorter events, 0.1 us)
Async XLA Ops:
  0.6 8.1 %copy-start.1 = (bf16[512,256]{1,0:T(8,128)(2,1)S(1)}, bf16[512,256]{1,0:T(8,128)(2,1)}, u32[]{:S(2)}) copy-start(bf16[512,256]{1,0:T(8,128)(2,1)} %constant.8.clone.picks) | copy-start | bytes 786436
  3.6 10.4 %all-to-all-start = ((f32[8,24,128]{2,1,0:T(8,128)}), f32[8,24,128]{2,1,0:T(8,128)S(1)}, u32[]{:S(2)}, u32[]{:S(2)}) async-start(f32[8,24,128]{2,1,0:T(8,128)} %get-tuple-element.43), calls=%async_computation | async-start | bytes 196608 | tf_op jit(solution)/shard_map/all_to_all | solution.py:503
  8.7 0.7 %copy-start.10 = (s32[8,128]{1,0:T(8,128)S(1)}, s32[8,128]{1,0:T(8,128)}, u32[]{:S(2)}) copy-start(s32[8,128]{1,0:T(8,128)} %get-tuple-element.40.table) | copy-start | bytes 12292
  9.4 0.9 %copy-start.5 = (f32[1,1,1,16,16,256]{5,4,3,2,1,0:T(8,128)S(1)}, f32[1,1,1,16,16,256]{5,4,3,2,1,0:T(8,128)}, u32[]{:S(2)}) copy-start(f32[1,1,1,16,16,256]{5,4,3,2,1,0:T(8,128)} %param.13) | copy-start | bytes 786436
  10.4 0.9 %copy-start.7 = (f32[1,1,1,16,16,256]{5,4,3,2,1,0:T(8,128)S(1)}, f32[1,1,1,16,16,256]{5,4,3,2,1,0:T(8,128)}, u32[]{:S(2)}) copy-start(f32[1,1,1,16,16,256]{5,4,3,2,1,0:T(8,128)} %param.14) | copy-start | bytes 786436
  11.3 2.6 %copy-start.3 = (f32[8,32,128]{2,1,0:T(8,128)S(1)}, f32[8,32,128]{2,1,0:T(8,128)}, u32[]{:S(2)}) copy-start(f32[8,32,128]{2,1,0:T(8,128)} %h.3) | copy-start | bytes 393220
  11.3 2.6 %copy-start.4 = (f32[8,32,128]{2,1,0:T(8,128)S(1)}, f32[8,32,128]{2,1,0:T(8,128)}, u32[]{:S(2)}) copy-start(f32[8,32,128]{2,1,0:T(8,128)} %k.3) | copy-start | bytes 393220
  12.3 1.6 %copy-start.11 = (f32[4,128]{1,0:T(4,128)S(1)}, f32[4,128]{1,0:T(4,128)}, u32[]{:S(2)}) copy-start(f32[4,128]{1,0:T(4,128)} %get-tuple-element.42.asked) | copy-start | bytes 6148
  13.9 19.0 %copy-start.8 = (f32[1,1,1,16,16,256]{5,4,3,2,1,0:T(8,128)S(1)}, f32[1,1,1,16,16,256]{5,4,3,2,1,0:T(8,128)}, u32[]{:S(2)}) copy-start(f32[1,1,1,16,16,256]{5,4,3,2,1,0:T(8,128)} %param.14) | copy-start | bytes 786436
  14.0 19.0 %copy-start.9 = (bf16[256,256]{1,0:T(8,128)(2,1)S(1)}, bf16[256,256]{1,0:T(8,128)(2,1)}, u32[]{:S(2)}) copy-start(bf16[256,256]{1,0:T(8,128)(2,1)} %constant.11.clone.spreads) | copy-start | bytes 393220
  14.0 8.4 %collective-permute-start = (f32[104,128]{1,0:T(8,128)S(1)}, f32[104,128]{1,0:T(8,128)S(1)}, u32[]{:S(2)}, u32[]{:S(2)}) collective-permute-start(f32[104,128]{1,0:T(8,128)S(1)} %get-tuple-element.45), channel_id=1, source_target_pairs={{0,8},{8,16},{16,24},{24,0},{1,9},{9,17},{17,25},{25,1},{2,10},{10... | collective-permute-start | bytes 159752 | tf_op jit(solution)/shard_map/ppermute | solution.py:520
  15.6 6.8 %collective-permute-start.2 = (f32[104,128]{1,0:T(8,128)S(1)}, f32[104,128]{1,0:T(8,128)S(1)}, u32[]{:S(2)}, u32[]{:S(2)}) collective-permute-start(f32[104,128]{1,0:T(8,128)S(1)} %get-tuple-element.47), channel_id=1, source_target_pairs={{0,24},{8,0},{16,8},{24,16},{1,25},{9,1},{17,9},{25,17},{2,26},{10... | collective-permute-start | bytes 159752 | tf_op jit(solution)/shard_map/ppermute | solution.py:520
  17.9 4.5 %collective-permute-start.1 = (f32[8,128]{1,0:T(8,128)S(1)}, f32[8,128]{1,0:T(8,128)S(1)}, u32[]{:S(2)}, u32[]{:S(2)}) collective-permute-start(f32[8,128]{1,0:T(8,128)S(1)} %get-tuple-element.46), channel_id=1, source_target_pairs={{0,16},{8,24},{16,0},{24,8},{1,17},{9,25},{17,1},{25,9},{2,18},{10... | collective-permute-start | bytes 12296 | tf_op jit(solution)/shard_map/ppermute | solution.py:520
  22.5 10.5 %copy-start = (bf16[256,512]{1,0:T(8,128)(2,1)S(1)}, bf16[256,512]{1,0:T(8,128)(2,1)}, u32[]{:S(2)}) copy-start(bf16[256,512]{1,0:T(8,128)(2,1)} %constant.10.clone.places) | copy-start | bytes 786436
  22.5 10.5 %copy-start.2 = (bf16[256,256]{1,0:T(8,128)(2,1)S(1)}, bf16[256,256]{1,0:T(8,128)(2,1)}, u32[]{:S(2)}) copy-start(bf16[256,256]{1,0:T(8,128)(2,1)} %constant.9.clone.stencil) | copy-start | bytes 393220
  22.5 10.5 %copy-start.6 = (f32[1,1,1,16,16,256]{5,4,3,2,1,0:T(8,128)S(1)}, f32[1,1,1,16,16,256]{5,4,3,2,1,0:T(8,128)}, u32[]{:S(2)}) copy-start(f32[1,1,1,16,16,256]{5,4,3,2,1,0:T(8,128)} %param.13) | copy-start | bytes 786436
  24.4 6.7 %collective-permute-start.3 = (f32[176,128]{1,0:T(8,128)S(1)}, f32[176,128]{1,0:T(8,128)S(1)}, u32[]{:S(2)}, u32[]{:S(2)}) collective-permute-start(f32[176,128]{1,0:T(8,128)S(1)} %get-tuple-element.52), channel_id=1, source_target_pairs={{0,8},{8,16},{16,24},{24,0},{1,9},{9,17},{17,25},{25,1},{2,10},{10... | collective-permute-start | bytes 270344 | tf_op jit(solution)/shard_map/ppermute | solution.py:520
  24.5 8.5 %collective-permute-start.4 = (f32[176,128]{1,0:T(8,128)S(1)}, f32[176,128]{1,0:T(8,128)S(1)}, u32[]{:S(2)}, u32[]{:S(2)}) collective-permute-start(f32[176,128]{1,0:T(8,128)S(1)} %get-tuple-element.53), channel_id=1, source_target_pairs={{0,16},{8,24},{16,0},{24,8},{1,17},{9,25},{17,1},{25,9},{2,18},{10... | collective-permute-start | bytes 270344 | tf_op jit(solution)/shard_map/ppermute | solution.py:520
  26.8 6.1 %collective-permute-start.5 = (f32[176,128]{1,0:T(8,128)S(1)}, f32[176,128]{1,0:T(8,128)S(1)}, u32[]{:S(2)}, u32[]{:S(2)}) collective-permute-start(f32[176,128]{1,0:T(8,128)S(1)} %get-tuple-element.54), channel_id=1, source_target_pairs={{0,24},{8,0},{16,8},{24,16},{1,25},{9,1},{17,9},{25,17},{2,26},{10... | collective-permute-start | bytes 270344 | tf_op jit(solution)/shard_map/ppermute | solution.py:520
  35.5 7.0 %collective-permute-start.6 = (f32[144,128]{1,0:T(8,128)S(1)}, f32[144,128]{1,0:T(8,128)S(1)}, u32[]{:S(2)}, u32[]{:S(2)}) collective-permute-start(f32[144,128]{1,0:T(8,128)S(1)} %get-tuple-element.60), channel_id=1, source_target_pairs={{0,8},{8,16},{16,24},{24,0},{1,9},{9,17},{17,25},{25,1},{2,10},{10... | collective-permute-start | bytes 221192 | tf_op jit(solution)/shard_map/ppermute | solution.py:520
  37.3 7.1 %collective-permute-start.7 = (f32[144,128]{1,0:T(8,128)S(1)}, f32[144,128]{1,0:T(8,128)S(1)}, u32[]{:S(2)}, u32[]{:S(2)}) collective-permute-start(f32[144,128]{1,0:T(8,128)S(1)} %get-tuple-element.61), channel_id=1, source_target_pairs={{0,16},{8,24},{16,0},{24,8},{1,17},{9,25},{17,1},{25,9},{2,18},{10... | collective-permute-start | bytes 221192 | tf_op jit(solution)/shard_map/ppermute | solution.py:520
  38.9 5.5 %collective-permute-start.8 = (f32[144,128]{1,0:T(8,128)S(1)}, f32[144,128]{1,0:T(8,128)S(1)}, u32[]{:S(2)}, u32[]{:S(2)}) collective-permute-start(f32[144,128]{1,0:T(8,128)S(1)} %get-tuple-element.62), channel_id=1, source_target_pairs={{0,24},{8,0},{16,8},{24,16},{1,25},{9,1},{17,9},{25,17},{2,26},{10... | collective-permute-start | bytes 221192 | tf_op jit(solution)/shard_map/ppermute | solution.py:520
  46.0 6.3 %collective-permute-start.9 = (f32[144,128]{1,0:T(8,128)S(1)}, f32[144,128]{1,0:T(8,128)S(1)}, u32[]{:S(2)}, u32[]{:S(2)}) collective-permute-start(f32[144,128]{1,0:T(8,128)S(1)} %get-tuple-element.66), channel_id=1, source_target_pairs={{0,8},{8,16},{16,24},{24,0},{1,9},{9,17},{17,25},{25,1},{2,10},{10... | collective-permute-start | bytes 221192 | tf_op jit(solution)/shard_map/ppermute | solution.py:520
  47.4 6.7 %collective-permute-start.10 = (f32[144,128]{1,0:T(8,128)S(1)}, f32[144,128]{1,0:T(8,128)S(1)}, u32[]{:S(2)}, u32[]{:S(2)}) collective-permute-start(f32[144,128]{1,0:T(8,128)S(1)} %get-tuple-element.67), channel_id=1, source_target_pairs={{0,16},{8,24},{16,0},{24,8},{1,17},{9,25},{17,1},{25,9},{2,18},{10... | collective-permute-start | bytes 221192 | tf_op jit(solution)/shard_map/ppermute | solution.py:520
  48.9 5.2 %collective-permute-start.11 = (f32[144,128]{1,0:T(8,128)S(1)}, f32[144,128]{1,0:T(8,128)S(1)}, u32[]{:S(2)}, u32[]{:S(2)}) collective-permute-start(f32[144,128]{1,0:T(8,128)S(1)} %get-tuple-element.68), channel_id=1, source_target_pairs={{0,24},{8,0},{16,8},{24,16},{1,25},{9,1},{17,9},{25,17},{2,26},{10... | collective-permute-start | bytes 221192 | tf_op jit(solution)/shard_map/ppermute | solution.py:520
  55.7 6.2 %collective-permute-start.12 = (f32[144,128]{1,0:T(8,128)S(1)}, f32[144,128]{1,0:T(8,128)S(1)}, u32[]{:S(2)}, u32[]{:S(2)}) collective-permute-start(f32[144,128]{1,0:T(8,128)S(1)} %get-tuple-element.72), channel_id=1, source_target_pairs={{0,8},{8,16},{16,24},{24,0},{1,9},{9,17},{17,25},{25,1},{2,10},{10... | collective-permute-start | bytes 221192 | tf_op jit(solution)/shard_map/ppermute | solution.py:520
  57.1 6.5 %collective-permute-start.13 = (f32[144,128]{1,0:T(8,128)S(1)}, f32[144,128]{1,0:T(8,128)S(1)}, u32[]{:S(2)}, u32[]{:S(2)}) collective-permute-start(f32[144,128]{1,0:T(8,128)S(1)} %get-tuple-element.73), channel_id=1, source_target_pairs={{0,16},{8,24},{16,0},{24,8},{1,17},{9,25},{17,1},{25,9},{2,18},{10... | collective-permute-start | bytes 221192 | tf_op jit(solution)/shard_map/ppermute | solution.py:520
  59.0 5.0 %collective-permute-start.14 = (f32[144,128]{1,0:T(8,128)S(1)}, f32[144,128]{1,0:T(8,128)S(1)}, u32[]{:S(2)}, u32[]{:S(2)}) collective-permute-start(f32[144,128]{1,0:T(8,128)S(1)} %get-tuple-element.74), channel_id=1, source_target_pairs={{0,24},{8,0},{16,8},{24,16},{1,25},{9,1},{17,9},{25,17},{2,26},{10... | collective-permute-start | bytes 221192 | tf_op jit(solution)/shard_map/ppermute | solution.py:520

commit v6 on v5

--- a/solution.py
+++ b/solution.py
@@ -127,7 +127,7 @@
 
 def write_tables(plane_cap, source, block, neighbour, asked, table):
     me = lax.axis_index("gx").astype(F32)
-    count = asked.shape[0]
+    count = len(asked)
     records = (count - 1) * plane_cap
     cap = float(plane_cap)
 
@@ -146,7 +146,8 @@
     lane = iota((SLOTS, 128), 1).astype(F32)
     for shift in range(count):
         hit = (wrapped(source_column - me) == float(shift)) & (rank_column == lane)
-        asked[shift : shift + 1, :] = jnp.sum(jnp.where(hit, block_column, 0.0), axis=0, keepdims=True)
+        row = jnp.sum(jnp.where(hit, block_column, 0.0), axis=0, keepdims=True)
+        asked[shift][...] = jnp.broadcast_to(row, asked[shift].shape)
     table[6:7, 0:SLOTS] = wrapped(me - source_row).astype(jnp.int32)
     table[7:8, 0:SLOTS] = rank.astype(jnp.int32)
     slot_column = iota((SLOTS, records), 0).astype(F32)
@@ -171,60 +172,79 @@
         table[face ^ 1 : (face ^ 1) + 1, SLOTS : SLOTS + records] = tile.astype(jnp.int32)
 
 
-def sides_kernel(
-    sizes, plane_cap, source, block, neighbour, h_far, k_far, send, asked, table, h, k, sems
-):
-    ny, nz = sizes
-    my_y, my_z = lax.axis_index("gy"), lax.axis_index("gz")
+def sides_kernel(sizes, plane_cap, source_far, block_far, neighbour_far, h_far, k_far, *rest):
+    *rest, source, block, neighbour, h, k, sems = rest
+    ny = sizes[0]
+    moves = side_moves(sizes)
+    sends, table, asked = rest[: len(moves)], rest[len(moves)], rest[len(moves) + 1 :]
+    my_y = lax.axis_index("gy")
     bx = h.shape[0]
-    copies = []
+    small = [(source_far, source), (block_far, block), (neighbour_far, neighbour)]
+    copies = [pltpu.make_async_copy(*pair, sems.at[2 * bx + n]) for n, pair in enumerate(small)]
+    large = []
     for x in range(bx):
-        copies.append(pltpu.make_async_copy(h_far.at[x], h.at[x], sems.at[x]))
-        copies.append(pltpu.make_async_copy(k_far.at[x], k.at[x], sems.at[bx + x]))
-    for copy in copies:
+        large.append(pltpu.make_async_copy(h_far.at[x], h.at[x], sems.at[x]))
+        large.append(pltpu.make_async_copy(k_far.at[x], k.at[x], sems.at[bx + x]))
+    for copy in copies + large:
         copy.start()
-    write_tables(plane_cap, source, block, neighbour, asked, table)
     for copy in copies:
         copy.wait()
-    blocks = side_blocks(h[...], k[...])
+    write_tables(plane_cap, source, block, neighbour, asked, table)
+    for copy in large:
+        copy.wait()
+    ylo, yhi, zlo, zhi = side_blocks(h[...], k[...])
+    if ny == 2:
+        yhi = [jnp.where(my_y == 0, up, down) for up, down in zip(yhi, ylo)]
+    for (dy, dz), out in zip(moves, sends):
+        side = (yhi if dy > 0 else ylo) if dy else (zhi if dz > 0 else zlo)
+        for part in range(1 if dy and dz else 3):
+            out[part * bx : part * bx + bx, :] = side[part]
+
+
+def side_moves(sizes):
+    ways = [1] if sizes[0] == 2 else [-1, 1]
+    return [(dy, 0) for dy in ways] + [(0, -1), (0, 1)] + [(dy, dz) for dy in ways for dz in (-1, 1)]
+
+
+def send_side(value, sizes, dy, dz):
+    ny, nz = sizes
+    pairs = []
     for y in range(ny):
         for z in range(nz):
-            for part in range(3):
-                ylo, yhi, zlo, zhi = [block[part] for block in blocks]
-                chosen = jnp.where(
-                    my_y == y, jnp.where(z < my_z, zlo, zhi), jnp.where(y < my_y, ylo, yhi)
-                )
-                send[y * nz + z, part * bx : part * bx + bx, :] = chosen
+            to_y, to_z = y + dy, z + dz
+            if ny == 2:
+                to_y %= 2
+            if 0 <= to_y < ny and 0 <= to_z < nz:
+                pairs.append((y * nz + z, to_y * nz + to_z))
+    return lax.ppermute(value, ("gy", "gz"), pairs)
 
 
 def side_reader(sizes, got, bx):
-    ny, nz = sizes
-    my_y, my_z = lax.axis_index("gy"), lax.axis_index("gz")
+    moves = side_moves(sizes)
+    my_y = lax.axis_index("gy")
 
     def read(dy, dz, part=0):
-        y, z = my_y + dy, my_z + dz
-        inside = (y >= 0) & (y < ny) & (z >= 0) & (z < nz)
-        at = jnp.where(inside, y * nz + z, 0)
-        return jnp.where(inside, got[at, part * bx : part * bx + bx, :], 0.0)
+        if sizes[0] > 2 or dy == 0:
+            value = got[moves.index((-dy, -dz))]
+            return value[part * bx : part * bx + bx, :]
+        value = got[moves.index((1, -dz))]
+        return jnp.where(my_y == max(dy, 0) ^ 1, value[part * bx : part * bx + bx, :], 0.0)
 
     return read
 
 
-def layers_kernel(sizes, h, k, got, asked, _, down, up, *farther):
+def layers_kernel(sizes, h, k, *rest):
+    *got, down, up = rest
     bx, by, bz = h.shape
-    count = asked.shape[0]
     read = side_reader(sizes, got, bx)
     around = [read(-1, 0), read(1, 0), read(0, -1), read(0, 1)]
-    for out, near, far, shift in ((down, 0, 1, count - 1), (up, bx - 1, bx - 2, 1)):
+    for out, near, far in ((down, 0, 1), (up, bx - 1, bx - 2)):
         out[0:by, :] = h[near]
         out[by : 2 * by, :] = h[far]
         out[2 * by : 3 * by, :] = k[near]
         for number, side in enumerate(around):
             out[3 * by + number : 3 * by + number + 1, :] = side[near : near + 1, :]
-        out[3 * by + 4 : 3 * by + 5, :] = asked[shift : shift + 1, :]
-        out[3 * by + 5 : 3 * by + 8, :] = jnp.zeros((3, bz), F32)
-    for number, out in enumerate(farther):
-        out[...] = jnp.broadcast_to(asked[2 + number : 3 + number, :], out.shape)
+        out[3 * by + 4 : 3 * by + 8, :] = jnp.zeros((4, bz), F32)
 
 
 def block_layout(cap):
@@ -244,17 +264,16 @@
     return h + RATE * k * (total - 6.0 * t)
 
 
-def heat_kernel(cap, sizes, request, h, k, got, low, high, *rest):
+def heat_kernel(cap, sizes, request, h, k, low, high, *rest):
     count = lax.axis_size("gx")
-    packed, (out, found, *send, held) = rest[: count - 1], rest[count - 1 :]
+    others, sides = count - 1, len(side_moves(sizes))
+    got, packed, (out, found, *send, held) = rest[:sides], rest[sides : sides + others], rest[sides + others :]
 
     bx, by, bz = h.shape
     h0, k0 = h[...], k[...]
     read = side_reader(sizes, got, bx)
-    me = lax.axis_index("gx")
     layers, lines = [], []
-    for beside, inside in ((low, me > 0), (high, me < count - 1)):
-        beside = jnp.where(inside, beside[...], 0.0)
+    for beside in (low, high):
         layers.append([beside[part * by : part * by + by, :][None] for part in range(3)])
         lines.append([beside[3 * by + n : 3 * by + n + 1, :] for n in range(4)])
     y_sides = [[read(d, 0, part) for part in range(3)] for d in (-1, 1)]
@@ -413,13 +432,11 @@
     return new_phase, new_solute
 
 
-def first_step_kernel(cap, table, phase, solute, own, picks, stencil, places, spreads, brick, found, *rest):
+def first_step_kernel(cap, table, phase, solute, own, picks, stencil, places, spreads, found, *rest):
     others = lax.axis_size("gx") - 1
     got, rest = rest[:others], rest[others:]
-    phase_out, solute_out, heat_out, own_out, brick_out, *rest = rest
-    send, (all_records, ghosts, blocks, held, sem) = rest[:others], rest[others:]
-    copy = pltpu.make_async_copy(brick, brick_out, sem)
-    copy.start()
+    phase_out, solute_out, heat_out, own_out, *rest = rest
+    send, (all_records, ghosts, blocks, held) = rest[:others], rest[others:]
     take_heat(cap, table, found, got, spreads[...], blocks, held, heat_out)
     new_phase, new_solute = step(
         table, phase[...], solute[...], heat_out[...], got, own, stencil[...], places[...],
@@ -429,6 +446,11 @@
     solute_out[...] = new_solute
     write_records(new_phase, new_solute, picks[...], own_out)
     pack(own_out, table, send)
+
+
+def write_out_kernel(value, out, sem):
+    copy = pltpu.make_async_copy(value, out, sem)
+    copy.start()
     copy.wait()
 
 
@@ -483,15 +505,20 @@
     picks, stencil, places, spreads = tables()
 
     integers = functools.partial(jax.ShapeDtypeStruct, dtype=jnp.int32)
-    sides, asked, table = call(
+    moves = side_moves(sizes)
+    side_shapes = [shape(bx if dy and dz else 3 * bx, 128) for dy, dz in moves]
+    first = call(
         functools.partial(sides_kernel, sizes, plane_cap),
-        [VMEM] * 3 + [ANY] * 2,
+        [ANY] * 5,
+        [*side_shapes, integers((8, 128)), *[shape(8, 128)] * count],
         [
-            shape(sizes[0] * sizes[1], 3 * bx, 128),
-            shape(count, 128),
-            integers((8, 128)),
+            pltpu.VMEM((1, SLOTS), jnp.int32),
+            pltpu.VMEM((1, SLOTS), jnp.int32),
+            pltpu.VMEM((FACES, 1, SLOTS), jnp.int32),
+            pltpu.VMEM((bx, by, bz), F32),
+            pltpu.VMEM((bx, by, bz), F32),
+            pltpu.SemaphoreType.DMA((2 * bx + 3,)),
         ],
-        [pltpu.VMEM((bx, by, bz), F32)] * 2 + [pltpu.SemaphoreType.DMA((2 * bx,))],
         mib=56,
     )(
         tile_source.reshape(1, SLOTS),
@@ -500,7 +527,17 @@
         enthalpy,
         conductivity,
     )
-    sides = lax.all_to_all(sides, ("gy", "gz"), split_axis=0, concat_axis=0, tiled=True)
+    sides, table, asked = first[: len(moves)], first[len(moves)], first[len(moves) + 1 :]
+    sides = [send_side(value, sizes, *move) for value, move in zip(sides, moves)]
+
+    def exchange(values):
+        return [
+            lax.ppermute(value, "gx", [(i, (i + shift) % count) for i in range(count)])
+            for shift, value in enumerate(values, 1)
+        ]
+
+    request = [asked[0], *exchange(asked[1:])]
+    request = jnp.stack([value[0, :block_cap] for value in request]).astype(jnp.int32)
 
     phase_field = phase.reshape(SLOTS, TE, PLANE)
     solute_field = solute.reshape(SLOTS, TE, PLANE)
@@ -510,32 +547,22 @@
     )
 
     layer = shape(3 * by + 8, bz)
-    down, up, *farther = call(
-        functools.partial(layers_kernel, sizes),
-        [VMEM] * 4 + [ANY],
-        [layer, layer] + [shape(8, 128)] * (count - 3),
-    )(enthalpy, conductivity, sides, asked, packed[0])
-
-    def pass_on(value, shift):
-        return lax.ppermute(value, "gx", [(i, (i + shift) % count) for i in range(count)])
-
-    from_low, from_high = pass_on(up, 1), pass_on(down, count - 1)
-    farther = [pass_on(value, 2 + number) for number, value in enumerate(farther)]
-    row = 3 * by + 4
-    request = [asked[0:1], from_low[row : row + 1]]
-    request += [value[0:1] for value in farther] + [from_high[row : row + 1]]
-    request = jnp.concatenate(request, axis=0)[:, :block_cap].astype(jnp.int32)
+    down, up = call(
+        functools.partial(layers_kernel, sizes), [VMEM] * (2 + len(sides)), [layer, layer]
+    )(enthalpy, conductivity, *sides)
+    forward = [(i, i + 1) for i in range(others)]
+    from_low = lax.ppermute(up, "gx", forward)
+    from_high = lax.ppermute(down, "gx", [(b, a) for a, b in forward])
     _, deep = block_layout(block_cap)
     brick = shape(bx, by, bz)
     heated, found, *send = call(
         functools.partial(heat_kernel, block_cap, sizes),
-        [SMEM] + [VMEM] * (5 + others),
+        [SMEM] + [VMEM] * (4 + len(sides) + others),
         [brick, shape(deep * CB, 128)] + [shape(plane_cap * REC + deep * CB, 128)] * others,
         [pltpu.VMEM((bx, by // CB, CB, bz), F32)],
-    )(request, enthalpy, conductivity, sides, from_low, from_high, *packed)
-
-    def exchange(values):
-        return [pass_on(value, 1 + number) for number, value in enumerate(values)]
+    )(request, enthalpy, conductivity, from_low, from_high, *sides, *packed)
+
+    (heat_out,) = call(write_out_kernel, [ANY], [brick], [pltpu.SemaphoreType.DMA], [ANY])(heated)
 
     got = exchange(send)
     field = shape(SLOTS, TE, PLANE)
@@ -543,18 +570,16 @@
         pltpu.VMEM((records + 2 * SLOTS, REC, 128), F32),
         pltpu.VMEM((SLOTS, REC, 128), F32),
     ]
-    phase_field, solute_field, heat, own, heat_out, *send = call(
+    phase_field, solute_field, heat, own, *send = call(
         functools.partial(first_step_kernel, block_cap),
-        [SMEM] + [VMEM] * (9 + others),
-        [field, field, shape(2, SLOTS * TE, 128), own_shape, brick, *send_shapes],
+        [SMEM] + [VMEM] * (8 + others),
+        [field, field, shape(2, SLOTS * TE, 128), own_shape, *send_shapes],
         step_scratch
         + [
             pltpu.VMEM((count, deep * CB, 128), F32),
             pltpu.VMEM((SLOTS * CB, CB, 128), F32),
-            pltpu.SemaphoreType.DMA,
         ],
-        [VMEM] * 4 + [ANY] + [VMEM] * others,
-    )(table, phase_field, solute_field, own, picks, stencil, places, spreads, heated, found, *got)
+    )(table, phase_field, solute_field, own, picks, stencil, places, spreads, found, *got)
     for _ in range(PHASE_STEPS - 2):
         got = exchange(send)
         phase_field, solute_field, own, *send = call(

time: 66.6 us -> 83.4 us (1.25)
  starting transfers between devices: 25.7 us -> 41.6 us
  waiting for transfers between devices: 23.3 us -> 25.1 us
    ppermute x15 -> x22, starting transfers between devices: 20.5 us -> 41.6 us  [the longest x15 25.3 us: exchange(): lax.ppermute(value, 'gx', [(i, (i + shift) % count) for i in range(count)])]
    all_to_all x1 -> x0, starting transfers between devices: 5.18 us -> none  [local(): lax.all_to_all(sides, ('gy', 'gz'), split_axis=0, concat_axis=0, tiled=True)]
    ppermute x15 -> x22, waiting for transfers between devices: 21.7 us -> 25.1 us  [the longest x15 20.1 us: exchange(): lax.ppermute(value, 'gx', [(i, (i + shift) % count) for i in range(count)])]
    all_to_all x1 -> x0, waiting for transfers between devices: 1.62 us -> none  [local(): lax.all_to_all(sides, ('gy', 'gz'), split_axis=0, concat_axis=0, tiled=True)]
    unnamed x24 -> x28, local copies, waits for them, and re-layouts: 2.63 us -> 1.95 us
    pallas_call x2 -> x3, Pallas kernels: 2.93 us -> 2.81 us  [the longest x1 2.13 us: local(): call(functools.partial(sides_kernel, sizes, plane_cap), [ANY] * 5, [*side...]
  transfers between devices with their start and end apart: 16 -> 22, of which waited for: 11 -> 12; matrix products, arithmetic and copies ran while one was open for 0% -> 1% of each run, Pallas kernels for 1% -> 2%
where the time goes in v6:
time: 83.4 us; the launch traced here: 83 us
  starting transfers between devices  41.6 us (50%)
  waiting for transfers between devices  25.1 us (30%)
  Pallas kernels  12.8 us (15%)
  local copies, waits for them, and re-layouts  2.64 us (3%)
  between operations  0.91 us (1%)
    ppermute x15, starting transfers between devices, exchange(): lax.ppermute(value, 'gx', [(i, (i + shift) % count) for i in range(count)])  25.3 us
    ppermute x15, waiting for transfers between devices, exchange(): lax.ppermute(value, 'gx', [(i, (i + shift) % count) for i in range(count)])  20.1 us
    ppermute x5, starting transfers between devices, send_side(): return lax.ppermute(value, ('gy', 'gz'), pairs)  11.3 us
    ppermute x1, waiting for transfers between devices, local(): from_high = lax.ppermute(down, 'gx', [(b, a) for a, b in forward])  4.14 us
    ppermute x1, starting transfers between devices, local(): from_low = lax.ppermute(up, 'gx', forward)  3.65 us
    pallas_call x2, Pallas kernels, local(): call(middle_step_kernel, [SMEM] + [VMEM] * (7 + others), [field, field, o...  3.21 us
    pallas_call x1, Pallas kernels, local(): call(functools.partial(sides_kernel, sizes, plane_cap), [ANY] * 5, [*side...  2.13 us
    pallas_call x1, Pallas kernels, local(): call(last_step_kernel, [SMEM] + [VMEM] * (6 + others), [field, field], st...  2.02 us
  transfers between devices with their start and end apart: 22, of which 12 were waited for; matrix products, arithmetic and copies ran while one was open for 1% of the time, Pallas kernels for 2%

profile of v6, /device:TPU:0, one launch (start us, length us, event | category | flops | bytes accessed | tf_op | source)
XLA Modules:
  0.0 83.0 jit_solution(15724848657514785649)
XLA Ops:
  0.6 0.0 copy-start.1
  0.6 2.1 %shard_map.130 = (f32[24,128]{1,0:T(8,128)}, f32[24,128]{1,0:T(8,128)}, f32[24,128]{1,0:T(8,128)}, f32[8,128]{1,0:T(8,128)}, f32[8,128]{1,0:T(8,128)}, /*index=5...) custom-call(s32[1,16]{1,0:T(1,128)} %bitcast.14, ...), custom_call_target="tpu_custom_call" | custom-call | tf_op jit(solution)/shard_map/pallas_call | solution.py:510
  2.8 3.1 %collective-permute-start = (f32[8,128]{1,0:T(8,128)}, f32[8,128]{1,0:T(8,128)S(1)}, u32[]{:S(2)}, u32[]{:S(2)}) collective-permute-start(f32[8,128]{1,0:T(8,128)} %get-tuple-element.46), channel_id=1, source_target_pairs={{0,8},{8,16},{16,24},{24,0},{1,9},{9,17},{17,25},{25,1},{2,10},{10... | collective-permute-start | bytes 12296 | tf_op jit(solution)/shard_map/ppermute | solution.py:535
  5.9 1.5 %collective-permute-start.3 = (f32[24,128]{1,0:T(8,128)}, f32[24,128]{1,0:T(8,128)S(1)}, u32[]{:S(2)}, u32[]{:S(2)}) collective-permute-start(f32[24,128]{1,0:T(8,128)} %get-tuple-element.49), channel_id=1, source_target_pairs={{0,4},{1,5},{2,6},{3,7},{4,0},{5,1},{6,2},{7,3},{8,12},{9,13},{10,... | collective-permute-start | bytes 36872 | tf_op jit(solution)/shard_map/ppermute | solution.py:219
  7.4 1.4 %collective-permute-start.4 = (f32[24,128]{1,0:T(8,128)}, f32[24,128]{1,0:T(8,128)S(1)}, u32[]{:S(2)}, u32[]{:S(2)}) collective-permute-start(f32[24,128]{1,0:T(8,128)} %get-tuple-element.50), channel_id=1, source_target_pairs={{1,0},{2,1},{3,2},{5,4},{6,5},{7,6},{9,8},{10,9},{11,10},{13,12},{... | collective-permute-start | bytes 36872 | tf_op jit(solution)/shard_map/ppermute | solution.py:219
  8.8 0.0 copy-start.11
  8.8 3.0 %collective-permute-start.5 = (f32[24,128]{1,0:T(8,128)}, f32[24,128]{1,0:T(8,128)S(1)}, u32[]{:S(2)}, u32[]{:S(2)}) collective-permute-start(f32[24,128]{1,0:T(8,128)} %get-tuple-element.51), channel_id=1, source_target_pairs={{0,1},{1,2},{2,3},{4,5},{5,6},{6,7},{8,9},{9,10},{10,11},{12,13},{... | collective-permute-start | bytes 36872 | tf_op jit(solution)/shard_map/ppermute | solution.py:219
  11.8 2.7 %collective-permute-start.1 = (f32[8,128]{1,0:T(8,128)}, f32[8,128]{1,0:T(8,128)S(1)}, u32[]{:S(2)}, u32[]{:S(2)}) collective-permute-start(f32[8,128]{1,0:T(8,128)} %get-tuple-element.47), channel_id=1, source_target_pairs={{0,16},{8,24},{16,0},{24,8},{1,17},{9,25},{17,1},{25,9},{2,18},{10... | collective-permute-start | bytes 12296 | tf_op jit(solution)/shard_map/ppermute | solution.py:535
  14.5 0.0 collective-permute-done
  14.5 0.0 copy-done.13
  14.5 1.3 %collective-permute-start.2 = (f32[8,128]{1,0:T(8,128)S(1)}, f32[8,128]{1,0:T(8,128)S(1)}, u32[]{:S(2)}, u32[]{:S(2)}) collective-permute-start(f32[8,128]{1,0:T(8,128)S(1)} %copy-done.13), channel_id=1, source_target_pairs={{0,24},{8,0},{16,8},{24,16},{1,25},{9,1},{17,9},{25,17},{2,26},{10... | collective-permute-start | bytes 12296 | tf_op jit(solution)/shard_map/ppermute | solution.py:535
  15.9 0.8 collective-permute-done.1
  16.6 0.0 copy-done.12
  16.6 1.3 %collective-permute-start.6 = (f32[8,128]{1,0:T(8,128)S(1)}, f32[8,128]{1,0:T(8,128)S(1)}, u32[]{:S(2)}, u32[]{:S(2)}) collective-permute-start(f32[8,128]{1,0:T(8,128)S(1)} %copy-done.12), channel_id=1, source_target_pairs={{1,4},{2,5},{3,6},{5,0},{6,1},{7,2},{9,12},{10,13},{11,14},{13,8},... | collective-permute-start | bytes 12296 | tf_op jit(solution)/shard_map/ppermute | solution.py:219
  17.9 0.2 collective-permute-done.2
  18.1 0.0 copy-done.11
  18.1 4.1 %collective-permute-start.7 = (f32[8,128]{1,0:T(8,128)S(1)}, f32[8,128]{1,0:T(8,128)S(1)}, u32[]{:S(2)}, u32[]{:S(2)}) collective-permute-start(f32[8,128]{1,0:T(8,128)S(1)} %copy-done.11), channel_id=1, source_target_pairs={{0,5},{1,6},{2,7},{4,1},{5,2},{6,3},{8,13},{9,14},{10,15},{12,9},{... | collective-permute-start | bytes 12296 | tf_op jit(solution)/shard_map/ppermute | solution.py:219
  22.2 0.0 copy-start.10
  22.2 0.7 slice.12
  22.9 0.9 %copy-done.5 = f32[1,1,1,16,16,256]{5,4,3,2,1,0:T(8,128)S(1)} copy-done((f32[1,1,1,16,16,256]{5,4,3,2,1,0:T(8,128)S(1)}, f32[1,1,1,16,16,256]{5,4,3,2,1,0:T(8,128)}, u32[]{:S(2)}) %copy-start.5) | copy-done | bytes 262168
  23.9 0.9 %copy-done.7 = f32[1,1,1,16,16,256]{5,4,3,2,1,0:T(8,128)S(1)} copy-done((f32[1,1,1,16,16,256]{5,4,3,2,1,0:T(8,128)S(1)}, f32[1,1,1,16,16,256]{5,4,3,2,1,0:T(8,128)}, u32[]{:S(2)}) %copy-start.7) | copy-done | bytes 262168
  24.8 1.0 %shard_map.132 = (f32[32,24,128]{2,1,0:T(8,128)S(1)}, f32[144,128]{1,0:T(8,128)S(1)}, f32[144,128]{1,0:T(8,128)S(1)}, f32[144,128]{1,0:T(8,128)S(1)}) custom-call(s32[8,128]{1,0:T(8,128)S(1)} %copy-done.10, f32[16,16,256]{2,1,0:T(8,128)S(1)} %bitcast.9, f32[16,16,256]{2,1,0:T(8,128)S(1)} %bitcast.11, bf16[512,256]{1,0:T(8,128)(2,1)S(1)} %copy-done.1), custom_call_target="tpu_custom_call" | custom-call | tf_op jit(solution)/shard_map/pallas_call | solution.py:545
  25.8 0.0 collective-permute-done.6.rest_3_
  25.8 0.0 collective-permute-done.7.rest_4_
  25.8 0.0 collective-permute-done.3.rest_0_
  25.9 0.0 collective-permute-done.4.rest_1_
  25.9 0.0 collective-permute-done.5.rest_2_
  25.9 0.0 copy-start.6
  25.9 0.0 copy-start.8
  25.9 3.7 %collective-permute-start.8 = (f32[104,128]{1,0:T(8,128)S(1)}, f32[104,128]{1,0:T(8,128)S(1)}, u32[]{:S(2)}, u32[]{:S(2)}) collective-permute-start(f32[104,128]{1,0:T(8,128)S(1)} %get-tuple-element.54), channel_id=1, source_target_pairs={{0,8},{8,16},{16,24},{1,9},{9,17},{17,25},{2,10},{10,18},{18,26},{... | collective-permute-start | bytes 159752 | tf_op jit(solution)/shard_map/ppermute | solution.py:554
  29.6 1.3 %collective-permute-start.9 = (f32[104,128]{1,0:T(8,128)S(1)}, f32[104,128]{1,0:T(8,128)S(1)}, u32[]{:S(2)}, u32[]{:S(2)}) collective-permute-start(f32[104,128]{1,0:T(8,128)S(1)} %get-tuple-element.55), channel_id=1, source_target_pairs={{8,0},{16,8},{24,16},{9,1},{17,9},{25,17},{10,2},{18,10},{26,18},{... | collective-permute-start | bytes 159752 | tf_op jit(solution)/shard_map/ppermute | solution.py:555
  30.9 0.9 %collective-permute-done.8.low = f32[104,128]{1,0:T(8,128)S(1)} collective-permute-done((f32[104,128]{1,0:T(8,128)S(1)}, f32[104,128]{1,0:T(8,128)S(1)}, u32[]{:S(2)}, u32[]{:S(2)}) %collective-permute-start.8) | collective-permute-done | bytes 53280 | tf_op jit(solution)/shard_map/ppermute | solution.py:554
  31.8 4.1 %collective-permute-done.9.high = f32[104,128]{1,0:T(8,128)S(1)} collective-permute-done((f32[104,128]{1,0:T(8,128)S(1)}, f32[104,128]{1,0:T(8,128)S(1)}, u32[]{:S(2)}, u32[]{:S(2)}) %collective-permute-start.9) | collective-permute-done | bytes 53280 | tf_op jit(solution)/shard_map/ppermute | solution.py:555
  35.9 1.9 %shard_map.133 = (f32[8,32,128]{2,1,0:T(8,128)S(1)}, f32[32,128]{1,0:T(8,128)S(1)}, f32[176,128]{1,0:T(8,128)S(1)}, f32[176,128]{1,0:T(8,128)S(1)}, f32[176,128]{1,0:T(8,128)S(1)}) custom-call(s32[4,8]{1,0:T(4,128)S(1)} %maximum_convert_fusion.request, f32[8,32,128]{2,1,0:T(8,128)S(1)} %copy-done.3, f32[8,32,128]{2,1,0:T(8,128)S(1)} %copy-done.4, ...), custom_call_target="tpu_custom_call" | custom-call | tf_op jit(solution)/shard_map/pallas_call | solution.py:558
  37.8 1.6 %collective-permute-start.10 = (f32[176,128]{1,0:T(8,128)S(1)}, f32[176,128]{1,0:T(8,128)S(1)}, u32[]{:S(2)}, u32[]{:S(2)}) collective-permute-start(f32[176,128]{1,0:T(8,128)S(1)} %get-tuple-element.63), channel_id=1, source_target_pairs={{0,8},{8,16},{16,24},{24,0},{1,9},{9,17},{17,25},{25,1},{2,10},{10... | collective-permute-start | bytes 270344 | tf_op jit(solution)/shard_map/ppermute | solution.py:535
  39.5 0.0 collective-permute-start.11
  39.5 2.6 %collective-permute-start.12 = (f32[176,128]{1,0:T(8,128)S(1)}, f32[176,128]{1,0:T(8,128)S(1)}, u32[]{:S(2)}, u32[]{:S(2)}) collective-permute-start(f32[176,128]{1,0:T(8,128)S(1)} %get-tuple-element.65), channel_id=1, source_target_pairs={{0,24},{8,0},{16,8},{24,16},{1,25},{9,1},{17,9},{25,17},{2,26},{10... | collective-permute-start | bytes 270344 | tf_op jit(solution)/shard_map/ppermute | solution.py:535
  42.1 3.1 %collective-permute-done.10.rest_0_ = f32[176,128]{1,0:T(8,128)S(1)} collective-permute-done((f32[176,128]{1,0:T(8,128)S(1)}, f32[176,128]{1,0:T(8,128)S(1)}, u32[]{:S(2)}, u32[]{:S(2)}) %collective-permute-start.10) | collective-permute-done | bytes 90144 | tf_op jit(solution)/shard_map/ppermute | solution.py:535
  45.3 2.7 %collective-permute-done.11.rest_1_ = f32[176,128]{1,0:T(8,128)S(1)} collective-permute-done((f32[176,128]{1,0:T(8,128)S(1)}, f32[176,128]{1,0:T(8,128)S(1)}, u32[]{:S(2)}, u32[]{:S(2)}) %collective-permute-start.11) | collective-permute-done | bytes 90144 | tf_op jit(solution)/shard_map/ppermute | solution.py:535
  48.0 0.0 collective-permute-done.12.rest_2_
  48.0 0.0 copy-done.9
  48.0 1.9 %shard_map.135 = (f32[16,16,256]{2,1,0:T(8,128)S(1)}, f32[16,16,256]{2,1,0:T(8,128)S(1)}, f32[2,256,128]{2,1,0:T(8,128)S(1)}, f32[32,24,128]{2,1,0:T(8,128)S(1)}...) custom-call(s32[8,128]{1,0:T(8,128)S(1)} %copy-done.10, f32[16,16,256]{2,1,0:T(8,128)S(1)} %bitcast.10, ...), custom_call_target="tpu_custom_call" | custom-call | tf_op jit(solution)/shard_map/pallas_call | solution.py:573
  49.9 2.4 %collective-permute-start.13 = (f32[144,128]{1,0:T(8,128)S(1)}, f32[144,128]{1,0:T(8,128)S(1)}, u32[]{:S(2)}, u32[]{:S(2)}) collective-permute-start(f32[144,128]{1,0:T(8,128)S(1)} %get-tuple-element.70), channel_id=1, source_target_pairs={{0,8},{8,16},{16,24},{24,0},{1,9},{9,17},{17,25},{25,1},{2,10},{10... | collective-permute-start | bytes 221192 | tf_op jit(solution)/shard_map/ppermute | solution.py:535
  52.4 0.7 collective-permute-start.14
  53.0 1.8 %collective-permute-start.15 = (f32[144,128]{1,0:T(8,128)S(1)}, f32[144,128]{1,0:T(8,128)S(1)}, u32[]{:S(2)}, u32[]{:S(2)}) collective-permute-start(f32[144,128]{1,0:T(8,128)S(1)} %get-tuple-element.72), channel_id=1, source_target_pairs={{0,24},{8,0},{16,8},{24,16},{1,25},{9,1},{17,9},{25,17},{2,26},{10... | collective-permute-start | bytes 221192 | tf_op jit(solution)/shard_map/ppermute | solution.py:535
  54.8 2.1 %collective-permute-done.13.rest_0_ = f32[144,128]{1,0:T(8,128)S(1)} collective-permute-done((f32[144,128]{1,0:T(8,128)S(1)}, f32[144,128]{1,0:T(8,128)S(1)}, u32[]{:S(2)}, u32[]{:S(2)}) %collective-permute-start.13) | collective-permute-done | bytes 73760 | tf_op jit(solution)/shard_map/ppermute | solution.py:535
  57.0 2.4 %collective-permute-done.14.rest_1_ = f32[144,128]{1,0:T(8,128)S(1)} collective-permute-done((f32[144,128]{1,0:T(8,128)S(1)}, f32[144,128]{1,0:T(8,128)S(1)}, u32[]{:S(2)}, u32[]{:S(2)}) %collective-permute-start.14) | collective-permute-done | bytes 73760 | tf_op jit(solution)/shard_map/ppermute | solution.py:535
  59.4 0.0 collective-permute-done.15.rest_2_
  59.4 1.6 %shard_map.136 = (f32[16,16,256]{2,1,0:T(8,128)S(1)}, f32[16,16,256]{2,1,0:T(8,128)S(1)}, f32[32,24,128]{2,1,0:T(8,128)S(1)}, f32[144,128]{1,0:T(8,128)S(1)}, f3...) custom-call(s32[8,128]{1,0:T(8,128)S(1)} %copy-done.10, f32[16,16,256]{2,1,0:T(8,128)S(1)} %get-tuple-element.66.phase, ...), custom_call_target="tpu_custom_call" | custom-call | tf_op jit(solution)/shard_map/pallas_call | solution.py:585
  61.0 2.1 %collective-permute-start.16 = (f32[144,128]{1,0:T(8,128)S(1)}, f32[144,128]{1,0:T(8,128)S(1)}, u32[]{:S(2)}, u32[]{:S(2)}) collective-permute-start(f32[144,128]{1,0:T(8,128)S(1)} %get-tuple-element.76), channel_id=1, source_target_pairs={{0,8},{8,16},{16,24},{24,0},{1,9},{9,17},{17,25},{25,1},{2,10},{10... | collective-permute-start | bytes 221192 | tf_op jit(solution)/shard_map/ppermute | solution.py:535
  63.1 1.1 %collective-permute-start.17 = (f32[144,128]{1,0:T(8,128)S(1)}, f32[144,128]{1,0:T(8,128)S(1)}, u32[]{:S(2)}, u32[]{:S(2)}) collective-permute-start(f32[144,128]{1,0:T(8,128)S(1)} %get-tuple-element.77), channel_id=1, source_target_pairs={{0,16},{8,24},{16,0},{24,8},{1,17},{9,25},{17,1},{25,9},{2,18},{10... | collective-permute-start | bytes 221192 | tf_op jit(solution)/shard_map/ppermute | solution.py:535
  64.2 1.4 %collective-permute-start.18 = (f32[144,128]{1,0:T(8,128)S(1)}, f32[144,128]{1,0:T(8,128)S(1)}, u32[]{:S(2)}, u32[]{:S(2)}) collective-permute-start(f32[144,128]{1,0:T(8,128)S(1)} %get-tuple-element.78), channel_id=1, source_target_pairs={{0,24},{8,0},{16,8},{24,16},{1,25},{9,1},{17,9},{25,17},{2,26},{10... | collective-permute-start | bytes 221192 | tf_op jit(solution)/shard_map/ppermute | solution.py:535
  65.5 2.4 %collective-permute-done.16.rest_0_ = f32[144,128]{1,0:T(8,128)S(1)} collective-permute-done((f32[144,128]{1,0:T(8,128)S(1)}, f32[144,128]{1,0:T(8,128)S(1)}, u32[]{:S(2)}, u32[]{:S(2)}) %collective-permute-start.16) | collective-permute-done | bytes 73760 | tf_op jit(solution)/shard_map/ppermute | solution.py:535
  68.0 2.2 %collective-permute-done.17.rest_1_ = f32[144,128]{1,0:T(8,128)S(1)} collective-permute-done((f32[144,128]{1,0:T(8,128)S(1)}, f32[144,128]{1,0:T(8,128)S(1)}, u32[]{:S(2)}, u32[]{:S(2)}) %collective-permute-start.17) | collective-permute-done | bytes 73760 | tf_op jit(solution)/shard_map/ppermute | solution.py:535
  70.2 0.0 collective-permute-done.18.rest_2_
  70.2 1.6 %shard_map.137 = (f32[16,16,256]{2,1,0:T(8,128)S(1)}, f32[16,16,256]{2,1,0:T(8,128)S(1)}, f32[32,24,128]{2,1,0:T(8,128)S(1)}, f32[144,128]{1,0:T(8,128)S(1)}, f3...) custom-call(s32[8,128]{1,0:T(8,128)S(1)} %copy-done.10, f32[16,16,256]{2,1,0:T(8,128)S(1)} %get-tuple-element.73.phase, ...), custom_call_target="tpu_custom_call" | custom-call | tf_op jit(solution)/shard_map/pallas_call | solution.py:585
  71.8 2.1 %collective-permute-start.19 = (f32[144,128]{1,0:T(8,128)S(1)}, f32[144,128]{1,0:T(8,128)S(1)}, u32[]{:S(2)}, u32[]{:S(2)}) collective-permute-start(f32[144,128]{1,0:T(8,128)S(1)} %get-tuple-element.82), channel_id=1, source_target_pairs={{0,8},{8,16},{16,24},{24,0},{1,9},{9,17},{17,25},{25,1},{2,10},{10... | collective-permute-start | bytes 221192 | tf_op jit(solution)/shard_map/ppermute | solution.py:535
  73.9 1.1 %collective-permute-start.20 = (f32[144,128]{1,0:T(8,128)S(1)}, f32[144,128]{1,0:T(8,128)S(1)}, u32[]{:S(2)}, u32[]{:S(2)}) collective-permute-start(f32[144,128]{1,0:T(8,128)S(1)} %get-tuple-element.83), channel_id=1, source_target_pairs={{0,16},{8,24},{16,0},{24,8},{1,17},{9,25},{17,1},{25,9},{2,18},{10... | collective-permute-start | bytes 221192 | tf_op jit(solution)/shard_map/ppermute | solution.py:535
  75.0 1.4 %collective-permute-start.21 = (f32[144,128]{1,0:T(8,128)S(1)}, f32[144,128]{1,0:T(8,128)S(1)}, u32[]{:S(2)}, u32[]{:S(2)}) collective-permute-start(f32[144,128]{1,0:T(8,128)S(1)} %get-tuple-element.84), channel_id=1, source_target_pairs={{0,24},{8,0},{16,8},{24,16},{1,25},{9,1},{17,9},{25,17},{2,26},{10... | collective-permute-start | bytes 221192 | tf_op jit(solution)/shard_map/ppermute | solution.py:535
  76.4 0.7 shard_map.134
  77.0 1.8 %collective-permute-done.19.rest_0_ = f32[144,128]{1,0:T(8,128)S(1)} collective-permute-done((f32[144,128]{1,0:T(8,128)S(1)}, f32[144,128]{1,0:T(8,128)S(1)}, u32[]{:S(2)}, u32[]{:S(2)}) %collective-permute-start.19) | collective-permute-done | bytes 73760 | tf_op jit(solution)/shard_map/ppermute | solution.py:535
  78.8 2.2 %collective-permute-done.20.rest_1_ = f32[144,128]{1,0:T(8,128)S(1)} collective-permute-done((f32[144,128]{1,0:T(8,128)S(1)}, f32[144,128]{1,0:T(8,128)S(1)}, u32[]{:S(2)}, u32[]{:S(2)}) %collective-permute-start.20) | collective-permute-done | bytes 73760 | tf_op jit(solution)/shard_map/ppermute | solution.py:535
  81.0 0.0 collective-permute-done.21.rest_2_
  81.0 2.0 %shard_map.138 = (f32[16,16,256]{2,1,0:T(8,128)}, f32[16,16,256]{2,1,0:T(8,128)}) custom-call(s32[8,128]{1,0:T(8,128)S(1)} %copy-done.10, f32[16,16,256]{2,1,0:T(8,128)S(1)} %get-tuple-element.79.phase, f32[16,16,256]{2,1,0:T(8,128)S(1)} %get-tuple-element.80.solute, f32[2,256,128]{2,1,0:T(8,128)S(1)} %get-tuple-element.68.heat, ...), custom_call_target="tpu_custom_call" | custom-call | tf_op jit(solution)/shard_map/pallas_call | solution.py:592
  (22 shorter events, 0.1 us)
Async XLA Ops:
  0.6 22.3 %copy-start.1 = (bf16[512,256]{1,0:T(8,128)(2,1)S(1)}, bf16[512,256]{1,0:T(8,128)(2,1)}, u32[]{:S(2)}) copy-start(bf16[512,256]{1,0:T(8,128)(2,1)} %constant.8.clone.picks) | copy-start | bytes 786436
  2.8 11.7 %collective-permute-start = (f32[8,128]{1,0:T(8,128)}, f32[8,128]{1,0:T(8,128)S(1)}, u32[]{:S(2)}, u32[]{:S(2)}) collective-permute-start(f32[8,128]{1,0:T(8,128)} %get-tuple-element.46), channel_id=1, source_target_pairs={{0,8},{8,16},{16,24},{24,0},{1,9},{9,17},{17,25},{25,1},{2,10},{10... | collective-permute-start | bytes 12296 | tf_op jit(solution)/shard_map/ppermute | solution.py:535
  5.9 8.7 %copy-start.13 = (f32[8,128]{1,0:T(8,128)S(1)}, f32[8,128]{1,0:T(8,128)}, u32[]{:S(2)}) copy-start(f32[8,128]{1,0:T(8,128)} %get-tuple-element.48) | copy-start | bytes 12292
  5.9 20.0 %collective-permute-start.3 = (f32[24,128]{1,0:T(8,128)}, f32[24,128]{1,0:T(8,128)S(1)}, u32[]{:S(2)}, u32[]{:S(2)}) collective-permute-start(f32[24,128]{1,0:T(8,128)} %get-tuple-element.49), channel_id=1, source_target_pairs={{0,4},{1,5},{2,6},{3,7},{4,0},{5,1},{6,2},{7,3},{8,12},{9,13},{10,... | collective-permute-start | bytes 36872 | tf_op jit(solution)/shard_map/ppermute | solution.py:219
  7.4 9.3 %copy-start.12 = (f32[8,128]{1,0:T(8,128)S(1)}, f32[8,128]{1,0:T(8,128)}, u32[]{:S(2)}) copy-start(f32[8,128]{1,0:T(8,128)} %get-tuple-element.52) | copy-start | bytes 12292
  7.4 18.5 %collective-permute-start.4 = (f32[24,128]{1,0:T(8,128)}, f32[24,128]{1,0:T(8,128)S(1)}, u32[]{:S(2)}, u32[]{:S(2)}) collective-permute-start(f32[24,128]{1,0:T(8,128)} %get-tuple-element.50), channel_id=1, source_target_pairs={{1,0},{2,1},{3,2},{5,4},{6,5},{7,6},{9,8},{10,9},{11,10},{13,12},{... | collective-permute-start | bytes 36872 | tf_op jit(solution)/shard_map/ppermute | solution.py:219
  8.8 9.3 %copy-start.11 = (f32[8,128]{1,0:T(8,128)S(1)}, f32[8,128]{1,0:T(8,128)}, u32[]{:S(2)}) copy-start(f32[8,128]{1,0:T(8,128)} %get-tuple-element.53) | copy-start | bytes 12292
  8.8 17.1 %collective-permute-start.5 = (f32[24,128]{1,0:T(8,128)}, f32[24,128]{1,0:T(8,128)S(1)}, u32[]{:S(2)}, u32[]{:S(2)}) collective-permute-start(f32[24,128]{1,0:T(8,128)} %get-tuple-element.51), channel_id=1, source_target_pairs={{0,1},{1,2},{2,3},{4,5},{5,6},{6,7},{8,9},{9,10},{10,11},{12,13},{... | collective-permute-start | bytes 36872 | tf_op jit(solution)/shard_map/ppermute | solution.py:219
  11.8 4.8 %collective-permute-start.1 = (f32[8,128]{1,0:T(8,128)}, f32[8,128]{1,0:T(8,128)S(1)}, u32[]{:S(2)}, u32[]{:S(2)}) collective-permute-start(f32[8,128]{1,0:T(8,128)} %get-tuple-element.47), channel_id=1, source_target_pairs={{0,16},{8,24},{16,0},{24,8},{1,17},{9,25},{17,1},{25,9},{2,18},{10... | collective-permute-start | bytes 12296 | tf_op jit(solution)/shard_map/ppermute | solution.py:535
  14.5 3.6 %collective-permute-start.2 = (f32[8,128]{1,0:T(8,128)S(1)}, f32[8,128]{1,0:T(8,128)S(1)}, u32[]{:S(2)}, u32[]{:S(2)}) collective-permute-start(f32[8,128]{1,0:T(8,128)S(1)} %copy-done.13), channel_id=1, source_target_pairs={{0,24},{8,0},{16,8},{24,16},{1,25},{9,1},{17,9},{25,17},{2,26},{10... | collective-permute-start | bytes 12296 | tf_op jit(solution)/shard_map/ppermute | solution.py:535
  16.6 9.2 %collective-permute-start.6 = (f32[8,128]{1,0:T(8,128)S(1)}, f32[8,128]{1,0:T(8,128)S(1)}, u32[]{:S(2)}, u32[]{:S(2)}) collective-permute-start(f32[8,128]{1,0:T(8,128)S(1)} %copy-done.12), channel_id=1, source_target_pairs={{1,4},{2,5},{3,6},{5,0},{6,1},{7,2},{9,12},{10,13},{11,14},{13,8},... | collective-permute-start | bytes 12296 | tf_op jit(solution)/shard_map/ppermute | solution.py:219
  18.1 7.7 %collective-permute-start.7 = (f32[8,128]{1,0:T(8,128)S(1)}, f32[8,128]{1,0:T(8,128)S(1)}, u32[]{:S(2)}, u32[]{:S(2)}) collective-permute-start(f32[8,128]{1,0:T(8,128)S(1)} %copy-done.11), channel_id=1, source_target_pairs={{0,5},{1,6},{2,7},{4,1},{5,2},{6,3},{8,13},{9,14},{10,15},{12,9},{... | collective-permute-start | bytes 12296 | tf_op jit(solution)/shard_map/ppermute | solution.py:219
  22.2 0.7 copy-start.10
  22.9 1.0 %copy-start.5 = (f32[1,1,1,16,16,256]{5,4,3,2,1,0:T(8,128)S(1)}, f32[1,1,1,16,16,256]{5,4,3,2,1,0:T(8,128)}, u32[]{:S(2)}) copy-start(f32[1,1,1,16,16,256]{5,4,3,2,1,0:T(8,128)} %param.13) | copy-start | bytes 786436
  23.9 0.9 %copy-start.7 = (f32[1,1,1,16,16,256]{5,4,3,2,1,0:T(8,128)S(1)}, f32[1,1,1,16,16,256]{5,4,3,2,1,0:T(8,128)}, u32[]{:S(2)}) copy-start(f32[1,1,1,16,16,256]{5,4,3,2,1,0:T(8,128)} %param.14) | copy-start | bytes 786436
  24.8 1.1 %copy-start.3 = (f32[8,32,128]{2,1,0:T(8,128)S(1)}, f32[8,32,128]{2,1,0:T(8,128)}, u32[]{:S(2)}) copy-start(f32[8,32,128]{2,1,0:T(8,128)} %h.3) | copy-start | bytes 393220
  24.8 1.1 %copy-start.4 = (f32[8,32,128]{2,1,0:T(8,128)S(1)}, f32[8,32,128]{2,1,0:T(8,128)}, u32[]{:S(2)}) copy-start(f32[8,32,128]{2,1,0:T(8,128)} %k.3) | copy-start | bytes 393220
  24.8 23.2 %copy-start.9 = (bf16[256,256]{1,0:T(8,128)(2,1)S(1)}, bf16[256,256]{1,0:T(8,128)(2,1)}, u32[]{:S(2)}) copy-start(bf16[256,256]{1,0:T(8,128)(2,1)} %constant.11.clone.spreads) | copy-start | bytes 393220
  25.9 22.1 %copy-start.6 = (f32[1,1,1,16,16,256]{5,4,3,2,1,0:T(8,128)S(1)}, f32[1,1,1,16,16,256]{5,4,3,2,1,0:T(8,128)}, u32[]{:S(2)}) copy-start(f32[1,1,1,16,16,256]{5,4,3,2,1,0:T(8,128)} %param.13) | copy-start | bytes 786436
  25.9 22.1 %copy-start.8 = (f32[1,1,1,16,16,256]{5,4,3,2,1,0:T(8,128)S(1)}, f32[1,1,1,16,16,256]{5,4,3,2,1,0:T(8,128)}, u32[]{:S(2)}) copy-start(f32[1,1,1,16,16,256]{5,4,3,2,1,0:T(8,128)} %param.14) | copy-start | bytes 786436
  25.9 5.9 %collective-permute-start.8 = (f32[104,128]{1,0:T(8,128)S(1)}, f32[104,128]{1,0:T(8,128)S(1)}, u32[]{:S(2)}, u32[]{:S(2)}) collective-permute-start(f32[104,128]{1,0:T(8,128)S(1)} %get-tuple-element.54), channel_id=1, source_target_pairs={{0,8},{8,16},{16,24},{1,9},{9,17},{17,25},{2,10},{10,18},{18,26},{... | collective-permute-start | bytes 159752 | tf_op jit(solution)/shard_map/ppermute | solution.py:554
  29.6 6.3 %collective-permute-start.9 = (f32[104,128]{1,0:T(8,128)S(1)}, f32[104,128]{1,0:T(8,128)S(1)}, u32[]{:S(2)}, u32[]{:S(2)}) collective-permute-start(f32[104,128]{1,0:T(8,128)S(1)} %get-tuple-element.55), channel_id=1, source_target_pairs={{8,0},{16,8},{24,16},{9,1},{17,9},{25,17},{10,2},{18,10},{26,18},{... | collective-permute-start | bytes 159752 | tf_op jit(solution)/shard_map/ppermute | solution.py:555
  35.9 12.1 %copy-start = (bf16[256,512]{1,0:T(8,128)(2,1)S(1)}, bf16[256,512]{1,0:T(8,128)(2,1)}, u32[]{:S(2)}) copy-start(bf16[256,512]{1,0:T(8,128)(2,1)} %constant.10.clone.places) | copy-start | bytes 786436
  35.9 12.1 %copy-start.2 = (bf16[256,256]{1,0:T(8,128)(2,1)S(1)}, bf16[256,256]{1,0:T(8,128)(2,1)}, u32[]{:S(2)}) copy-start(bf16[256,256]{1,0:T(8,128)(2,1)} %constant.9.clone.stencil) | copy-start | bytes 393220
  37.8 7.4 %collective-permute-start.10 = (f32[176,128]{1,0:T(8,128)S(1)}, f32[176,128]{1,0:T(8,128)S(1)}, u32[]{:S(2)}, u32[]{:S(2)}) collective-permute-start(f32[176,128]{1,0:T(8,128)S(1)} %get-tuple-element.63), channel_id=1, source_target_pairs={{0,8},{8,16},{16,24},{24,0},{1,9},{9,17},{17,25},{25,1},{2,10},{10... | collective-permute-start | bytes 270344 | tf_op jit(solution)/shard_map/ppermute | solution.py:535
  39.5 8.5 %collective-permute-start.11 = (f32[176,128]{1,0:T(8,128)S(1)}, f32[176,128]{1,0:T(8,128)S(1)}, u32[]{:S(2)}, u32[]{:S(2)}) collective-permute-start(f32[176,128]{1,0:T(8,128)S(1)} %get-tuple-element.64), channel_id=1, source_target_pairs={{0,16},{8,24},{16,0},{24,8},{1,17},{9,25},{17,1},{25,9},{2,18},{10... | collective-permute-start | bytes 270344 | tf_op jit(solution)/shard_map/ppermute | solution.py:535
  39.5 8.5 %collective-permute-start.12 = (f32[176,128]{1,0:T(8,128)S(1)}, f32[176,128]{1,0:T(8,128)S(1)}, u32[]{:S(2)}, u32[]{:S(2)}) collective-permute-start(f32[176,128]{1,0:T(8,128)S(1)} %get-tuple-element.65), channel_id=1, source_target_pairs={{0,24},{8,0},{16,8},{24,16},{1,25},{9,1},{17,9},{25,17},{2,26},{10... | collective-permute-start | bytes 270344 | tf_op jit(solution)/shard_map/ppermute | solution.py:535
  49.9 7.0 %collective-permute-start.13 = (f32[144,128]{1,0:T(8,128)S(1)}, f32[144,128]{1,0:T(8,128)S(1)}, u32[]{:S(2)}, u32[]{:S(2)}) collective-permute-start(f32[144,128]{1,0:T(8,128)S(1)} %get-tuple-element.70), channel_id=1, source_target_pairs={{0,8},{8,16},{16,24},{24,0},{1,9},{9,17},{17,25},{25,1},{2,10},{10... | collective-permute-start | bytes 221192 | tf_op jit(solution)/shard_map/ppermute | solution.py:535
  52.4 7.0 %collective-permute-start.14 = (f32[144,128]{1,0:T(8,128)S(1)}, f32[144,128]{1,0:T(8,128)S(1)}, u32[]{:S(2)}, u32[]{:S(2)}) collective-permute-start(f32[144,128]{1,0:T(8,128)S(1)} %get-tuple-element.71), channel_id=1, source_target_pairs={{0,16},{8,24},{16,0},{24,8},{1,17},{9,25},{17,1},{25,9},{2,18},{10... | collective-permute-start | bytes 221192 | tf_op jit(solution)/shard_map/ppermute | solution.py:535
  53.0 6.3 %collective-permute-start.15 = (f32[144,128]{1,0:T(8,128)S(1)}, f32[144,128]{1,0:T(8,128)S(1)}, u32[]{:S(2)}, u32[]{:S(2)}) collective-permute-start(f32[144,128]{1,0:T(8,128)S(1)} %get-tuple-element.72), channel_id=1, source_target_pairs={{0,24},{8,0},{16,8},{24,16},{1,25},{9,1},{17,9},{25,17},{2,26},{10... | collective-permute-start | bytes 221192 | tf_op jit(solution)/shard_map/ppermute | solution.py:535
  61.0 7.0 %collective-permute-start.16 = (f32[144,128]{1,0:T(8,128)S(1)}, f32[144,128]{1,0:T(8,128)S(1)}, u32[]{:S(2)}, u32[]{:S(2)}) collective-permute-start(f32[144,128]{1,0:T(8,128)S(1)} %get-tuple-element.76), channel_id=1, source_target_pairs={{0,8},{8,16},{16,24},{24,0},{1,9},{9,17},{17,25},{25,1},{2,10},{10... | collective-permute-start | bytes 221192 | tf_op jit(solution)/shard_map/ppermute | solution.py:535
  63.1 7.1 %collective-permute-start.17 = (f32[144,128]{1,0:T(8,128)S(1)}, f32[144,128]{1,0:T(8,128)S(1)}, u32[]{:S(2)}, u32[]{:S(2)}) collective-permute-start(f32[144,128]{1,0:T(8,128)S(1)} %get-tuple-element.77), channel_id=1, source_target_pairs={{0,16},{8,24},{16,0},{24,8},{1,17},{9,25},{17,1},{25,9},{2,18},{10... | collective-permute-start | bytes 221192 | tf_op jit(solution)/shard_map/ppermute | solution.py:535
  64.2 6.0 %collective-permute-start.18 = (f32[144,128]{1,0:T(8,128)S(1)}, f32[144,128]{1,0:T(8,128)S(1)}, u32[]{:S(2)}, u32[]{:S(2)}) collective-permute-start(f32[144,128]{1,0:T(8,128)S(1)} %get-tuple-element.78), channel_id=1, source_target_pairs={{0,24},{8,0},{16,8},{24,16},{1,25},{9,1},{17,9},{25,17},{2,26},{10... | collective-permute-start | bytes 221192 | tf_op jit(solution)/shard_map/ppermute | solution.py:535
  71.8 7.0 %collective-permute-start.19 = (f32[144,128]{1,0:T(8,128)S(1)}, f32[144,128]{1,0:T(8,128)S(1)}, u32[]{:S(2)}, u32[]{:S(2)}) collective-permute-start(f32[144,128]{1,0:T(8,128)S(1)} %get-tuple-element.82), channel_id=1, source_target_pairs={{0,8},{8,16},{16,24},{24,0},{1,9},{9,17},{17,25},{25,1},{2,10},{10... | collective-permute-start | bytes 221192 | tf_op jit(solution)/shard_map/ppermute | solution.py:535
  73.9 7.1 %collective-permute-start.20 = (f32[144,128]{1,0:T(8,128)S(1)}, f32[144,128]{1,0:T(8,128)S(1)}, u32[]{:S(2)}, u32[]{:S(2)}) collective-permute-start(f32[144,128]{1,0:T(8,128)S(1)} %get-tuple-element.83), channel_id=1, source_target_pairs={{0,16},{8,24},{16,0},{24,8},{1,17},{9,25},{17,1},{25,9},{2,18},{10... | collective-permute-start | bytes 221192 | tf_op jit(solution)/shard_map/ppermute | solution.py:535
  75.0 6.0 %collective-permute-start.21 = (f32[144,128]{1,0:T(8,128)S(1)}, f32[144,128]{1,0:T(8,128)S(1)}, u32[]{:S(2)}, u32[]{:S(2)}) collective-permute-start(f32[144,128]{1,0:T(8,128)S(1)} %get-tuple-element.84), channel_id=1, source_target_pairs={{0,24},{8,0},{16,8},{24,16},{1,25},{9,1},{17,9},{25,17},{2,26},{10... | collective-permute-start | bytes 221192 | tf_op jit(solution)/shard_map/ppermute | solution.py:535

commit v7 on v5

--- a/solution.py
+++ b/solution.py
@@ -127,7 +127,7 @@
 
 def write_tables(plane_cap, source, block, neighbour, asked, table):
     me = lax.axis_index("gx").astype(F32)
-    count = asked.shape[0]
+    count = len(asked)
     records = (count - 1) * plane_cap
     cap = float(plane_cap)
 
@@ -146,7 +146,8 @@
     lane = iota((SLOTS, 128), 1).astype(F32)
     for shift in range(count):
         hit = (wrapped(source_column - me) == float(shift)) & (rank_column == lane)
-        asked[shift : shift + 1, :] = jnp.sum(jnp.where(hit, block_column, 0.0), axis=0, keepdims=True)
+        row = jnp.sum(jnp.where(hit, block_column, 0.0), axis=0, keepdims=True)
+        asked[shift][...] = jnp.broadcast_to(row, asked[shift].shape)
     table[6:7, 0:SLOTS] = wrapped(me - source_row).astype(jnp.int32)
     table[7:8, 0:SLOTS] = rank.astype(jnp.int32)
     slot_column = iota((SLOTS, records), 0).astype(F32)
@@ -172,19 +173,24 @@
 
 
 def sides_kernel(
-    sizes, plane_cap, source, block, neighbour, h_far, k_far, send, asked, table, h, k, sems
+    sizes, plane_cap, source_far, block_far, neighbour_far, h_far, k_far, send, table, *rest
 ):
+    *asked, source, block, neighbour, h, k, sems = rest
     ny, nz = sizes
     my_y, my_z = lax.axis_index("gy"), lax.axis_index("gz")
     bx = h.shape[0]
-    copies = []
+    small = [(source_far, source), (block_far, block), (neighbour_far, neighbour)]
+    copies = [pltpu.make_async_copy(*pair, sems.at[2 * bx + n]) for n, pair in enumerate(small)]
+    large = []
     for x in range(bx):
-        copies.append(pltpu.make_async_copy(h_far.at[x], h.at[x], sems.at[x]))
-        copies.append(pltpu.make_async_copy(k_far.at[x], k.at[x], sems.at[bx + x]))
+        large.append(pltpu.make_async_copy(h_far.at[x], h.at[x], sems.at[x]))
+        large.append(pltpu.make_async_copy(k_far.at[x], k.at[x], sems.at[bx + x]))
+    for copy in copies + large:
+        copy.start()
     for copy in copies:
-        copy.start()
+        copy.wait()
     write_tables(plane_cap, source, block, neighbour, asked, table)
-    for copy in copies:
+    for copy in large:
         copy.wait()
     blocks = side_blocks(h[...], k[...])
     for y in range(ny):
@@ -210,21 +216,18 @@
     return read
 
 
-def layers_kernel(sizes, h, k, got, asked, _, down, up, *farther):
+def layers_kernel(sizes, h, k, got, ask_up, ask_down, *rest):
+    down, up = rest[-2:]
     bx, by, bz = h.shape
-    count = asked.shape[0]
     read = side_reader(sizes, got, bx)
     around = [read(-1, 0), read(1, 0), read(0, -1), read(0, 1)]
-    for out, near, far, shift in ((down, 0, 1, count - 1), (up, bx - 1, bx - 2, 1)):
+    for out, near, far, ask in ((down, 0, 1, ask_down), (up, bx - 1, bx - 2, ask_up)):
         out[0:by, :] = h[near]
         out[by : 2 * by, :] = h[far]
         out[2 * by : 3 * by, :] = k[near]
         for number, side in enumerate(around):
             out[3 * by + number : 3 * by + number + 1, :] = side[near : near + 1, :]
-        out[3 * by + 4 : 3 * by + 5, :] = asked[shift : shift + 1, :]
-        out[3 * by + 5 : 3 * by + 8, :] = jnp.zeros((3, bz), F32)
-    for number, out in enumerate(farther):
-        out[...] = jnp.broadcast_to(asked[2 + number : 3 + number, :], out.shape)
+        out[3 * by + 4 : 3 * by + 8, :] = ask[0:4, :]
 
 
 def block_layout(cap):
@@ -413,13 +416,11 @@
     return new_phase, new_solute
 
 
-def first_step_kernel(cap, table, phase, solute, own, picks, stencil, places, spreads, brick, found, *rest):
+def first_step_kernel(cap, table, phase, solute, own, picks, stencil, places, spreads, found, *rest):
     others = lax.axis_size("gx") - 1
     got, rest = rest[:others], rest[others:]
-    phase_out, solute_out, heat_out, own_out, brick_out, *rest = rest
-    send, (all_records, ghosts, blocks, held, sem) = rest[:others], rest[others:]
-    copy = pltpu.make_async_copy(brick, brick_out, sem)
-    copy.start()
+    phase_out, solute_out, heat_out, own_out, *rest = rest
+    send, (all_records, ghosts, blocks, held) = rest[:others], rest[others:]
     take_heat(cap, table, found, got, spreads[...], blocks, held, heat_out)
     new_phase, new_solute = step(
         table, phase[...], solute[...], heat_out[...], got, own, stencil[...], places[...],
@@ -429,6 +430,11 @@
     solute_out[...] = new_solute
     write_records(new_phase, new_solute, picks[...], own_out)
     pack(own_out, table, send)
+
+
+def write_out_kernel(value, out, sem):
+    copy = pltpu.make_async_copy(value, out, sem)
+    copy.start()
     copy.wait()
 
 
@@ -483,15 +489,18 @@
     picks, stencil, places, spreads = tables()
 
     integers = functools.partial(jax.ShapeDtypeStruct, dtype=jnp.int32)
-    sides, asked, table = call(
+    sides, table, *asked = call(
         functools.partial(sides_kernel, sizes, plane_cap),
-        [VMEM] * 3 + [ANY] * 2,
+        [ANY] * 5,
+        [shape(sizes[0] * sizes[1], 3 * bx, 128), integers((8, 128)), *[shape(8, 128)] * count],
         [
-            shape(sizes[0] * sizes[1], 3 * bx, 128),
-            shape(count, 128),
-            integers((8, 128)),
+            pltpu.VMEM((1, SLOTS), jnp.int32),
+            pltpu.VMEM((1, SLOTS), jnp.int32),
+            pltpu.VMEM((FACES, 1, SLOTS), jnp.int32),
+            pltpu.VMEM((bx, by, bz), F32),
+            pltpu.VMEM((bx, by, bz), F32),
+            pltpu.SemaphoreType.DMA((2 * bx + 3,)),
         ],
-        [pltpu.VMEM((bx, by, bz), F32)] * 2 + [pltpu.SemaphoreType.DMA((2 * bx,))],
         mib=56,
     )(
         tile_source.reshape(1, SLOTS),
@@ -502,6 +511,14 @@
     )
     sides = lax.all_to_all(sides, ("gy", "gz"), split_axis=0, concat_axis=0, tiled=True)
 
+    def pass_on(value, shift):
+        return lax.ppermute(value, "gx", [(i, (i + shift) % count) for i in range(count)])
+
+    def exchange(values):
+        return [pass_on(value, shift) for shift, value in enumerate(values, 1)]
+
+    farther = [pass_on(asked[shift], shift) for shift in range(2, others)]
+
     phase_field = phase.reshape(SLOTS, TE, PLANE)
     solute_field = solute.reshape(SLOTS, TE, PLANE)
     own_shape, send_shapes = shape(2 * SLOTS, REC, 128), [shape(plane_cap * REC, 128)] * others
@@ -510,21 +527,13 @@
     )
 
     layer = shape(3 * by + 8, bz)
-    down, up, *farther = call(
-        functools.partial(layers_kernel, sizes),
-        [VMEM] * 4 + [ANY],
-        [layer, layer] + [shape(8, 128)] * (count - 3),
-    )(enthalpy, conductivity, sides, asked, packed[0])
-
-    def pass_on(value, shift):
-        return lax.ppermute(value, "gx", [(i, (i + shift) % count) for i in range(count)])
-
-    from_low, from_high = pass_on(up, 1), pass_on(down, count - 1)
-    farther = [pass_on(value, 2 + number) for number, value in enumerate(farther)]
+    down, up = call(
+        functools.partial(layers_kernel, sizes), [VMEM] * 5 + [ANY] * (1 + len(farther)), [layer, layer]
+    )(enthalpy, conductivity, sides, asked[1], asked[others], packed[0], *farther)
+    from_low, from_high = pass_on(up, 1), pass_on(down, others)
     row = 3 * by + 4
-    request = [asked[0:1], from_low[row : row + 1]]
-    request += [value[0:1] for value in farther] + [from_high[row : row + 1]]
-    request = jnp.concatenate(request, axis=0)[:, :block_cap].astype(jnp.int32)
+    request = [asked[0][0], from_low[row], *[value[0] for value in farther], from_high[row]]
+    request = jnp.stack([value[:block_cap] for value in request]).astype(jnp.int32)
     _, deep = block_layout(block_cap)
     brick = shape(bx, by, bz)
     heated, found, *send = call(
@@ -534,8 +543,7 @@
         [pltpu.VMEM((bx, by // CB, CB, bz), F32)],
     )(request, enthalpy, conductivity, sides, from_low, from_high, *packed)
 
-    def exchange(values):
-        return [pass_on(value, 1 + number) for number, value in enumerate(values)]
+    (heat_out,) = call(write_out_kernel, [ANY], [brick], [pltpu.SemaphoreType.DMA], [ANY])(heated)
 
     got = exchange(send)
     field = shape(SLOTS, TE, PLANE)
@@ -543,18 +551,16 @@
         pltpu.VMEM((records + 2 * SLOTS, REC, 128), F32),
         pltpu.VMEM((SLOTS, REC, 128), F32),
     ]
-    phase_field, solute_field, heat, own, heat_out, *send = call(
+    phase_field, solute_field, heat, own, *send = call(
         functools.partial(first_step_kernel, block_cap),
-        [SMEM] + [VMEM] * (9 + others),
-        [field, field, shape(2, SLOTS * TE, 128), own_shape, brick, *send_shapes],
+        [SMEM] + [VMEM] * (8 + others),
+        [field, field, shape(2, SLOTS * TE, 128), own_shape, *send_shapes],
         step_scratch
         + [
             pltpu.VMEM((count, deep * CB, 128), F32),
             pltpu.VMEM((SLOTS * CB, CB, 128), F32),
-            pltpu.SemaphoreType.DMA,
         ],
-        [VMEM] * 4 + [ANY] + [VMEM] * others,
-    )(table, phase_field, solute_field, own, picks, stencil, places, spreads, heated, found, *got)
+    )(table, phase_field, solute_field, own, picks, stencil, places, spreads, found, *got)
     for _ in range(PHASE_STEPS - 2):
         got = exchange(send)
         phase_field, solute_field, own, *send = call(

time: 66.6 us -> 66.7 us (level)
  starting transfers between devices: 25.7 us -> 29.1 us
  waiting for transfers between devices: 23.3 us -> 20.3 us
  Pallas kernels: 13.6 us -> 12.8 us
    ppermute x15, starting transfers between devices: 20.5 us -> 23.9 us  [pass_on(): lax.ppermute(value, 'gx', [(i, (i + shift) % count) for i in range(count)])]
    all_to_all x1, waiting for transfers between devices: 1.62 us -> 0.01 us  [local(): lax.all_to_all(sides, ('gy', 'gz'), split_axis=0, concat_axis=0, tiled=True)]
    ppermute x15, waiting for transfers between devices: 21.7 us -> 20.3 us  [pass_on(): lax.ppermute(value, 'gx', [(i, (i + shift) % count) for i in range(count)])]
    slice x4, local copies, waits for them, and re-layouts: 0.01 us -> 0.7 us  [local(): value[:block_cap]]
    pallas_call x2 -> x3, Pallas kernels: 2.93 us -> 2.85 us  [the longest x1 2.17 us: local(): call(functools.partial(sides_kernel, sizes, plane_cap), [ANY] * 5, [shape...]
    unnamed x24 -> x28, local copies, waits for them, and re-layouts: 2.63 us -> 2.57 us
  transfers between devices with their start and end apart: 16 -> 16, of which waited for: 11 -> 10; matrix products, arithmetic and copies ran while one was open for 0% -> 1% of each run, Pallas kernels for 1% -> 2%
where the time goes in v7:
time: 66.7 us; the launch traced here: 66.3 us
  starting transfers between devices  29.1 us (44%)
  waiting for transfers between devices  20.3 us (30%)
  Pallas kernels  12.8 us (19%)
  local copies, waits for them, and re-layouts  3.26 us (5%)
  between operations  0.82 us (1%)
    ppermute x15, starting transfers between devices, pass_on(): lax.ppermute(value, 'gx', [(i, (i + shift) % count) for i in range(count)])  23.9 us
    ppermute x15, waiting for transfers between devices, pass_on(): lax.ppermute(value, 'gx', [(i, (i + shift) % count) for i in range(count)])  20.3 us
    all_to_all x1, starting transfers between devices, local(): lax.all_to_all(sides, ('gy', 'gz'), split_axis=0, concat_axis=0, tiled=True)  5.18 us
    pallas_call x2, Pallas kernels, local(): call(middle_step_kernel, [SMEM] + [VMEM] * (7 + others), [field, field, o...  3.21 us
    unnamed x28, local copies, waits for them, and re-layouts  2.57 us
    pallas_call x1, Pallas kernels, local(): call(functools.partial(sides_kernel, sizes, plane_cap), [ANY] * 5, [shape...  2.17 us
    pallas_call x1, Pallas kernels, local(): call(last_step_kernel, [SMEM] + [VMEM] * (6 + others), [field, field], st...  2.02 us
    pallas_call x1, Pallas kernels, local(): call(functools.partial(heat_kernel, block_cap, sizes), [SMEM] + [VMEM] *...  1.92 us
  transfers between devices with their start and end apart: 16, of which 10 were waited for; matrix products, arithmetic and copies ran while one was open for 1% of the time, Pallas kernels for 2%

profile of v7, /device:TPU:0, one launch (start us, length us, event | category | flops | bytes accessed | tf_op | source)
XLA Modules:
  0.0 66.3 jit_solution(11199177180067600896)
XLA Ops:
  0.6 0.0 copy-start.1
  0.6 2.2 %shard_map.130 = (f32[8,24,128]{2,1,0:T(8,128)}, s32[8,128]{1,0:T(8,128)}, f32[8,128]{1,0:T(8,128)}, f32[8,128]{1,0:T(8,128)}, f32[8,128]{1,0:T(8,128)}, /*index=5*/f32[8,128]{1,0:T(8,128)}) custom-call(s32[1,16]{1,0:T(1,128)} %bitcast.14, s32[1,16]{1,0:T(1,128)} %bitcast.15, s32[6,1,16]{2,1,0:T(1,128)} %bitcast.13, f32[8,32,128]{2,1,0:T(8,128)} %h.3, ...), custom_call_target="tpu_custom_call" | custom-call | tf_op jit(solution)/shard_map/pallas_call | solution.py:492
  2.8 0.0 copy-start.13
  2.8 5.2 %all-to-all-start = ((f32[8,24,128]{2,1,0:T(8,128)}), f32[8,24,128]{2,1,0:T(8,128)S(1)}, u32[]{:S(2)}, u32[]{:S(2)}) async-start(f32[8,24,128]{2,1,0:T(8,128)} %get-tuple-element.42), calls=%async_computation | async-start | bytes 196608 | tf_op jit(solution)/shard_map/all_to_all | solution.py:512
  8.0 0.0 copy-start.10
  8.0 0.0 copy-done.13
  8.0 2.7 %collective-permute-start = (f32[8,128]{1,0:T(8,128)S(1)}, f32[8,128]{1,0:T(8,128)S(1)}, u32[]{:S(2)}, u32[]{:S(2)}) collective-permute-start(f32[8,128]{1,0:T(8,128)S(1)} %copy-done.13), channel_id=1, source_target_pairs={{0,16},{8,24},{16,0},{24,8},{1,17},{9,25},{17,1},{25,9},{2,18},{10... | collective-permute-start | bytes 12296 | tf_op jit(solution)/shard_map/ppermute | solution.py:515
  10.7 0.0 copy-done.1
  10.7 0.0 copy-done.10
  10.7 0.0 copy-start.5
  10.7 0.9 %copy-done.5 = f32[1,1,1,16,16,256]{5,4,3,2,1,0:T(8,128)S(1)} copy-done((f32[1,1,1,16,16,256]{5,4,3,2,1,0:T(8,128)S(1)}, f32[1,1,1,16,16,256]{5,4,3,2,1,0:T(8,128)}, u32[]{:S(2)}) %copy-start.5) | copy-done | bytes 262168
  11.6 0.0 copy-start.7
  11.6 0.9 %copy-done.7 = f32[1,1,1,16,16,256]{5,4,3,2,1,0:T(8,128)S(1)} copy-done((f32[1,1,1,16,16,256]{5,4,3,2,1,0:T(8,128)S(1)}, f32[1,1,1,16,16,256]{5,4,3,2,1,0:T(8,128)}, u32[]{:S(2)}) %copy-start.7) | copy-done | bytes 262168
  12.6 1.0 %shard_map.131 = (f32[32,24,128]{2,1,0:T(8,128)S(1)}, f32[144,128]{1,0:T(8,128)S(1)}, f32[144,128]{1,0:T(8,128)S(1)}, f32[144,128]{1,0:T(8,128)S(1)}) custom-call(s32[8,128]{1,0:T(8,128)S(1)} %copy-done.10, f32[16,16,256]{2,1,0:T(8,128)S(1)} %bitcast.9, f32[16,16,256]{2,1,0:T(8,128)S(1)} %bitcast.11, bf16[512,256]{1,0:T(8,128)(2,1)S(1)} %copy-done.1), custom_call_target="tpu_custom_call" | custom-call | tf_op jit(solution)/shard_map/pallas_call | solution.py:525
  13.6 0.0 copy-start.11
  13.6 0.0 collective-permute-done.rest_1_
  13.6 0.0 all-to-all-done.got
  13.6 0.0 copy-done.3
  13.6 0.0 copy-done.4
  13.6 0.0 copy-done.12
  13.6 0.6 copy-done.11
  14.3 1.6 %collective-permute-start.1 = (f32[104,128]{1,0:T(8,128)S(1)}, f32[104,128]{1,0:T(8,128)S(1)}, u32[]{:S(2)}, u32[]{:S(2)}) collective-permute-start(f32[104,128]{1,0:T(8,128)S(1)} %get-tuple-element.48), channel_id=1, source_target_pairs={{0,8},{8,16},{16,24},{24,0},{1,9},{9,17},{17,25},{25,1},{2,10},{10... | collective-permute-start | bytes 159752 | tf_op jit(solution)/shard_map/ppermute | solution.py:515
  15.9 2.2 %collective-permute-start.2 = (f32[104,128]{1,0:T(8,128)S(1)}, f32[104,128]{1,0:T(8,128)S(1)}, u32[]{:S(2)}, u32[]{:S(2)}) collective-permute-start(f32[104,128]{1,0:T(8,128)S(1)} %get-tuple-element.49), channel_id=1, source_target_pairs={{0,24},{8,0},{16,8},{24,16},{1,25},{9,1},{17,9},{25,17},{2,26},{10... | collective-permute-start | bytes 159752 | tf_op jit(solution)/shard_map/ppermute | solution.py:515
  18.2 0.7 %slice.24 = f32[1,8]{1,0:T(1,128)S(1)} slice(f32[8,128]{1,0:T(8,128)} %get-tuple-element.41), slice={[0:1], [0:8]} | slice | bytes 64 | tf_op jit(solution)/shard_map/slice | solution.py:536
  18.8 1.8 %collective-permute-done.1.low = f32[104,128]{1,0:T(8,128)S(1)} collective-permute-done((f32[104,128]{1,0:T(8,128)S(1)}, f32[104,128]{1,0:T(8,128)S(1)}, u32[]{:S(2)}, u32[]{:S(2)}) %collective-permute-start.1) | collective-permute-done | bytes 53280 | tf_op jit(solution)/shard_map/ppermute | solution.py:515
  20.7 0.0 collective-permute-done.2.high
  20.7 0.0 copy-start
  20.7 0.0 copy-start.2
  20.8 0.0 copy-start.6
  20.8 1.9 %shard_map.133 = (f32[8,32,128]{2,1,0:T(8,128)S(1)}, f32[32,128]{1,0:T(8,128)S(1)}, f32[176,128]{1,0:T(8,128)S(1)}, f32[176,128]{1,0:T(8,128)S(1)}, f32[176,128]{1,0:T(8,128)S(1)}) custom-call(s32[4,8]{1,0:T(4,128)S(1)} %maximum_convert_fusion.request, f32[8,32,128]{2,1,0:T(8,128)S(1)} %copy-done.3, f32[8,32,128]{2,1,0:T(8,128)S(1)} %copy-done.4, ...), custom_call_target="tpu_custom_call" | custom-call | tf_op jit(solution)/shard_map/pallas_call | solution.py:539
  22.7 0.4 collective-permute-start.3
  23.1 3.6 %collective-permute-start.4 = (f32[176,128]{1,0:T(8,128)S(1)}, f32[176,128]{1,0:T(8,128)S(1)}, u32[]{:S(2)}, u32[]{:S(2)}) collective-permute-start(f32[176,128]{1,0:T(8,128)S(1)} %get-tuple-element.56), channel_id=1, source_target_pairs={{0,16},{8,24},{16,0},{24,8},{1,17},{9,25},{17,1},{25,9},{2,18},{10... | collective-permute-start | bytes 270344 | tf_op jit(solution)/shard_map/ppermute | solution.py:515
  26.7 0.1 collective-permute-start.5
  26.7 3.1 %collective-permute-done.3.rest_0_ = f32[176,128]{1,0:T(8,128)S(1)} collective-permute-done((f32[176,128]{1,0:T(8,128)S(1)}, f32[176,128]{1,0:T(8,128)S(1)}, u32[]{:S(2)}, u32[]{:S(2)}) %collective-permute-start.3) | collective-permute-done | bytes 90144 | tf_op jit(solution)/shard_map/ppermute | solution.py:515
  29.8 2.4 %collective-permute-done.4.rest_1_ = f32[176,128]{1,0:T(8,128)S(1)} collective-permute-done((f32[176,128]{1,0:T(8,128)S(1)}, f32[176,128]{1,0:T(8,128)S(1)}, u32[]{:S(2)}, u32[]{:S(2)}) %collective-permute-start.4) | collective-permute-done | bytes 90144 | tf_op jit(solution)/shard_map/ppermute | solution.py:515
  32.2 0.1 collective-permute-done.5.rest_2_
  32.2 0.0 copy-done.8
  32.2 0.0 copy-done.9
  32.2 0.0 copy-done
  32.2 0.0 copy-done.2
  32.2 0.0 copy-done.6
  32.2 1.9 %shard_map.135 = (f32[16,16,256]{2,1,0:T(8,128)S(1)}, f32[16,16,256]{2,1,0:T(8,128)S(1)}, f32[2,256,128]{2,1,0:T(8,128)S(1)}, f32[32,24,128]{2,1,0:T(8,128)S(1)}...) custom-call(s32[8,128]{1,0:T(8,128)S(1)} %copy-done.10, f32[16,16,256]{2,1,0:T(8,128)S(1)} %bitcast.10, ...), custom_call_target="tpu_custom_call" | custom-call | tf_op jit(solution)/shard_map/pallas_call | solution.py:554
  34.1 2.0 %collective-permute-start.6 = (f32[144,128]{1,0:T(8,128)S(1)}, f32[144,128]{1,0:T(8,128)S(1)}, u32[]{:S(2)}, u32[]{:S(2)}) collective-permute-start(f32[144,128]{1,0:T(8,128)S(1)} %get-tuple-element.62), channel_id=1, source_target_pairs={{0,8},{8,16},{16,24},{24,0},{1,9},{9,17},{17,25},{25,1},{2,10},{10... | collective-permute-start | bytes 221192 | tf_op jit(solution)/shard_map/ppermute | solution.py:515
  36.1 1.4 %collective-permute-start.7 = (f32[144,128]{1,0:T(8,128)S(1)}, f32[144,128]{1,0:T(8,128)S(1)}, u32[]{:S(2)}, u32[]{:S(2)}) collective-permute-start(f32[144,128]{1,0:T(8,128)S(1)} %get-tuple-element.63), channel_id=1, source_target_pairs={{0,16},{8,24},{16,0},{24,8},{1,17},{9,25},{17,1},{25,9},{2,18},{10... | collective-permute-start | bytes 221192 | tf_op jit(solution)/shard_map/ppermute | solution.py:515
  37.6 1.0 %collective-permute-start.8 = (f32[144,128]{1,0:T(8,128)S(1)}, f32[144,128]{1,0:T(8,128)S(1)}, u32[]{:S(2)}, u32[]{:S(2)}) collective-permute-start(f32[144,128]{1,0:T(8,128)S(1)} %get-tuple-element.64), channel_id=1, source_target_pairs={{0,24},{8,0},{16,8},{24,16},{1,25},{9,1},{17,9},{25,17},{2,26},{10... | collective-permute-start | bytes 221192 | tf_op jit(solution)/shard_map/ppermute | solution.py:515
  38.6 2.1 %collective-permute-done.6.rest_0_ = f32[144,128]{1,0:T(8,128)S(1)} collective-permute-done((f32[144,128]{1,0:T(8,128)S(1)}, f32[144,128]{1,0:T(8,128)S(1)}, u32[]{:S(2)}, u32[]{:S(2)}) %collective-permute-start.6) | collective-permute-done | bytes 73760 | tf_op jit(solution)/shard_map/ppermute | solution.py:515
  40.7 2.3 %collective-permute-done.7.rest_1_ = f32[144,128]{1,0:T(8,128)S(1)} collective-permute-done((f32[144,128]{1,0:T(8,128)S(1)}, f32[144,128]{1,0:T(8,128)S(1)}, u32[]{:S(2)}, u32[]{:S(2)}) %collective-permute-start.7) | collective-permute-done | bytes 73760 | tf_op jit(solution)/shard_map/ppermute | solution.py:515
  43.0 0.0 collective-permute-done.8.rest_2_
  43.0 1.6 %shard_map.136 = (f32[16,16,256]{2,1,0:T(8,128)S(1)}, f32[16,16,256]{2,1,0:T(8,128)S(1)}, f32[32,24,128]{2,1,0:T(8,128)S(1)}, f32[144,128]{1,0:T(8,128)S(1)}, f3...) custom-call(s32[8,128]{1,0:T(8,128)S(1)} %copy-done.10, f32[16,16,256]{2,1,0:T(8,128)S(1)} %get-tuple-element.58.phase, ...), custom_call_target="tpu_custom_call" | custom-call | tf_op jit(solution)/shard_map/pallas_call | solution.py:566
  44.6 1.9 %collective-permute-start.9 = (f32[144,128]{1,0:T(8,128)S(1)}, f32[144,128]{1,0:T(8,128)S(1)}, u32[]{:S(2)}, u32[]{:S(2)}) collective-permute-start(f32[144,128]{1,0:T(8,128)S(1)} %get-tuple-element.68), channel_id=1, source_target_pairs={{0,8},{8,16},{16,24},{24,0},{1,9},{9,17},{17,25},{25,1},{2,10},{10... | collective-permute-start | bytes 221192 | tf_op jit(solution)/shard_map/ppermute | solution.py:515
  46.6 1.2 %collective-permute-start.10 = (f32[144,128]{1,0:T(8,128)S(1)}, f32[144,128]{1,0:T(8,128)S(1)}, u32[]{:S(2)}, u32[]{:S(2)}) collective-permute-start(f32[144,128]{1,0:T(8,128)S(1)} %get-tuple-element.69), channel_id=1, source_target_pairs={{0,16},{8,24},{16,0},{24,8},{1,17},{9,25},{17,1},{25,9},{2,18},{10... | collective-permute-start | bytes 221192 | tf_op jit(solution)/shard_map/ppermute | solution.py:515
  47.8 1.2 %collective-permute-start.11 = (f32[144,128]{1,0:T(8,128)S(1)}, f32[144,128]{1,0:T(8,128)S(1)}, u32[]{:S(2)}, u32[]{:S(2)}) collective-permute-start(f32[144,128]{1,0:T(8,128)S(1)} %get-tuple-element.70), channel_id=1, source_target_pairs={{0,24},{8,0},{16,8},{24,16},{1,25},{9,1},{17,9},{25,17},{2,26},{10... | collective-permute-start | bytes 221192 | tf_op jit(solution)/shard_map/ppermute | solution.py:515
  49.0 2.3 %collective-permute-done.9.rest_0_ = f32[144,128]{1,0:T(8,128)S(1)} collective-permute-done((f32[144,128]{1,0:T(8,128)S(1)}, f32[144,128]{1,0:T(8,128)S(1)}, u32[]{:S(2)}, u32[]{:S(2)}) %collective-permute-start.9) | collective-permute-done | bytes 73760 | tf_op jit(solution)/shard_map/ppermute | solution.py:515
  51.3 2.2 %collective-permute-done.10.rest_1_ = f32[144,128]{1,0:T(8,128)S(1)} collective-permute-done((f32[144,128]{1,0:T(8,128)S(1)}, f32[144,128]{1,0:T(8,128)S(1)}, u32[]{:S(2)}, u32[]{:S(2)}) %collective-permute-start.10) | collective-permute-done | bytes 73760 | tf_op jit(solution)/shard_map/ppermute | solution.py:515
  53.5 0.0 collective-permute-done.11.rest_2_
  53.5 1.6 %shard_map.137 = (f32[16,16,256]{2,1,0:T(8,128)S(1)}, f32[16,16,256]{2,1,0:T(8,128)S(1)}, f32[32,24,128]{2,1,0:T(8,128)S(1)}, f32[144,128]{1,0:T(8,128)S(1)}, f3...) custom-call(s32[8,128]{1,0:T(8,128)S(1)} %copy-done.10, f32[16,16,256]{2,1,0:T(8,128)S(1)} %get-tuple-element.65.phase, ...), custom_call_target="tpu_custom_call" | custom-call | tf_op jit(solution)/shard_map/pallas_call | solution.py:566
  55.1 2.1 %collective-permute-start.12 = (f32[144,128]{1,0:T(8,128)S(1)}, f32[144,128]{1,0:T(8,128)S(1)}, u32[]{:S(2)}, u32[]{:S(2)}) collective-permute-start(f32[144,128]{1,0:T(8,128)S(1)} %get-tuple-element.74), channel_id=1, source_target_pairs={{0,8},{8,16},{16,24},{24,0},{1,9},{9,17},{17,25},{25,1},{2,10},{10... | collective-permute-start | bytes 221192 | tf_op jit(solution)/shard_map/ppermute | solution.py:515
  57.2 1.1 %collective-permute-start.13 = (f32[144,128]{1,0:T(8,128)S(1)}, f32[144,128]{1,0:T(8,128)S(1)}, u32[]{:S(2)}, u32[]{:S(2)}) collective-permute-start(f32[144,128]{1,0:T(8,128)S(1)} %get-tuple-element.75), channel_id=1, source_target_pairs={{0,16},{8,24},{16,0},{24,8},{1,17},{9,25},{17,1},{25,9},{2,18},{10... | collective-permute-start | bytes 221192 | tf_op jit(solution)/shard_map/ppermute | solution.py:515
  58.4 1.3 %collective-permute-start.14 = (f32[144,128]{1,0:T(8,128)S(1)}, f32[144,128]{1,0:T(8,128)S(1)}, u32[]{:S(2)}, u32[]{:S(2)}) collective-permute-start(f32[144,128]{1,0:T(8,128)S(1)} %get-tuple-element.76), channel_id=1, source_target_pairs={{0,24},{8,0},{16,8},{24,16},{1,25},{9,1},{17,9},{25,17},{2,26},{10... | collective-permute-start | bytes 221192 | tf_op jit(solution)/shard_map/ppermute | solution.py:515
  59.7 0.7 shard_map.134
  60.3 1.7 %collective-permute-done.12.rest_0_ = f32[144,128]{1,0:T(8,128)S(1)} collective-permute-done((f32[144,128]{1,0:T(8,128)S(1)}, f32[144,128]{1,0:T(8,128)S(1)}, u32[]{:S(2)}, u32[]{:S(2)}) %collective-permute-start.12) | collective-permute-done | bytes 73760 | tf_op jit(solution)/shard_map/ppermute | solution.py:515
  62.1 2.2 %collective-permute-done.13.rest_1_ = f32[144,128]{1,0:T(8,128)S(1)} collective-permute-done((f32[144,128]{1,0:T(8,128)S(1)}, f32[144,128]{1,0:T(8,128)S(1)}, u32[]{:S(2)}, u32[]{:S(2)}) %collective-permute-start.13) | collective-permute-done | bytes 73760 | tf_op jit(solution)/shard_map/ppermute | solution.py:515
  64.3 0.0 collective-permute-done.14.rest_2_
  64.3 2.0 %shard_map.138 = (f32[16,16,256]{2,1,0:T(8,128)}, f32[16,16,256]{2,1,0:T(8,128)}) custom-call(s32[8,128]{1,0:T(8,128)S(1)} %copy-done.10, f32[16,16,256]{2,1,0:T(8,128)S(1)} %get-tuple-element.71.phase, f32[16,16,256]{2,1,0:T(8,128)S(1)} %get-tuple-element.72.solute, f32[2,256,128]{2,1,0:T(8,128)S(1)} %get-tuple-element.60.heat, ...), custom_call_target="tpu_custom_call" | custom-call | tf_op jit(solution)/shard_map/pallas_call | solution.py:573
  (10 shorter events, 0.0 us)
Async XLA Ops:
  0.6 10.1 %copy-start.1 = (bf16[512,256]{1,0:T(8,128)(2,1)S(1)}, bf16[512,256]{1,0:T(8,128)(2,1)}, u32[]{:S(2)}) copy-start(bf16[512,256]{1,0:T(8,128)(2,1)} %constant.8.clone.picks) | copy-start | bytes 786436
  2.8 5.2 %copy-start.13 = (f32[8,128]{1,0:T(8,128)S(1)}, f32[8,128]{1,0:T(8,128)}, u32[]{:S(2)}) copy-start(f32[8,128]{1,0:T(8,128)} %get-tuple-element.47) | copy-start | bytes 12292
  2.8 10.8 %all-to-all-start = ((f32[8,24,128]{2,1,0:T(8,128)}), f32[8,24,128]{2,1,0:T(8,128)S(1)}, u32[]{:S(2)}, u32[]{:S(2)}) async-start(f32[8,24,128]{2,1,0:T(8,128)} %get-tuple-element.42), calls=%async_computation | async-start | bytes 196608 | tf_op jit(solution)/shard_map/all_to_all | solution.py:512
  8.0 2.7 %copy-start.10 = (s32[8,128]{1,0:T(8,128)S(1)}, s32[8,128]{1,0:T(8,128)}, u32[]{:S(2)}) copy-start(s32[8,128]{1,0:T(8,128)} %get-tuple-element.45.table) | copy-start | bytes 12292
  8.0 5.6 %collective-permute-start = (f32[8,128]{1,0:T(8,128)S(1)}, f32[8,128]{1,0:T(8,128)S(1)}, u32[]{:S(2)}, u32[]{:S(2)}) collective-permute-start(f32[8,128]{1,0:T(8,128)S(1)} %copy-done.13), channel_id=1, source_target_pairs={{0,16},{8,24},{16,0},{24,8},{1,17},{9,25},{17,1},{25,9},{2,18},{10... | collective-permute-start | bytes 12296 | tf_op jit(solution)/shard_map/ppermute | solution.py:515
  10.7 1.0 %copy-start.5 = (f32[1,1,1,16,16,256]{5,4,3,2,1,0:T(8,128)S(1)}, f32[1,1,1,16,16,256]{5,4,3,2,1,0:T(8,128)}, u32[]{:S(2)}) copy-start(f32[1,1,1,16,16,256]{5,4,3,2,1,0:T(8,128)} %param.13) | copy-start | bytes 786436
  11.6 0.9 %copy-start.7 = (f32[1,1,1,16,16,256]{5,4,3,2,1,0:T(8,128)S(1)}, f32[1,1,1,16,16,256]{5,4,3,2,1,0:T(8,128)}, u32[]{:S(2)}) copy-start(f32[1,1,1,16,16,256]{5,4,3,2,1,0:T(8,128)} %param.14) | copy-start | bytes 786436
  12.6 1.0 %copy-start.3 = (f32[8,32,128]{2,1,0:T(8,128)S(1)}, f32[8,32,128]{2,1,0:T(8,128)}, u32[]{:S(2)}) copy-start(f32[8,32,128]{2,1,0:T(8,128)} %h.3) | copy-start | bytes 393220
  12.6 1.0 %copy-start.4 = (f32[8,32,128]{2,1,0:T(8,128)S(1)}, f32[8,32,128]{2,1,0:T(8,128)}, u32[]{:S(2)}) copy-start(f32[8,32,128]{2,1,0:T(8,128)} %k.3) | copy-start | bytes 393220
  12.6 1.0 %copy-start.12 = (f32[8,128]{1,0:T(8,128)S(1)}, f32[8,128]{1,0:T(8,128)}, u32[]{:S(2)}) copy-start(f32[8,128]{1,0:T(8,128)} %get-tuple-element.44.ask_down) | copy-start | bytes 12292
  13.6 0.7 %copy-start.11 = (f32[8,128]{1,0:T(8,128)S(1)}, f32[8,128]{1,0:T(8,128)}, u32[]{:S(2)}) copy-start(f32[8,128]{1,0:T(8,128)} %get-tuple-element.43.ask_up) | copy-start | bytes 12292
  14.2 18.0 %copy-start.8 = (f32[1,1,1,16,16,256]{5,4,3,2,1,0:T(8,128)S(1)}, f32[1,1,1,16,16,256]{5,4,3,2,1,0:T(8,128)}, u32[]{:S(2)}) copy-start(f32[1,1,1,16,16,256]{5,4,3,2,1,0:T(8,128)} %param.14) | copy-start | bytes 786436
  14.2 18.0 %copy-start.9 = (bf16[256,256]{1,0:T(8,128)(2,1)S(1)}, bf16[256,256]{1,0:T(8,128)(2,1)}, u32[]{:S(2)}) copy-start(bf16[256,256]{1,0:T(8,128)(2,1)} %constant.11.clone.spreads) | copy-start | bytes 393220
  14.3 6.4 %collective-permute-start.1 = (f32[104,128]{1,0:T(8,128)S(1)}, f32[104,128]{1,0:T(8,128)S(1)}, u32[]{:S(2)}, u32[]{:S(2)}) collective-permute-start(f32[104,128]{1,0:T(8,128)S(1)} %get-tuple-element.48), channel_id=1, source_target_pairs={{0,8},{8,16},{16,24},{24,0},{1,9},{9,17},{17,25},{25,1},{2,10},{10... | collective-permute-start | bytes 159752 | tf_op jit(solution)/shard_map/ppermute | solution.py:515
  15.9 4.8 %collective-permute-start.2 = (f32[104,128]{1,0:T(8,128)S(1)}, f32[104,128]{1,0:T(8,128)S(1)}, u32[]{:S(2)}, u32[]{:S(2)}) collective-permute-start(f32[104,128]{1,0:T(8,128)S(1)} %get-tuple-element.49), channel_id=1, source_target_pairs={{0,24},{8,0},{16,8},{24,16},{1,25},{9,1},{17,9},{25,17},{2,26},{10... | collective-permute-start | bytes 159752 | tf_op jit(solution)/shard_map/ppermute | solution.py:515
  20.7 11.5 %copy-start = (bf16[256,512]{1,0:T(8,128)(2,1)S(1)}, bf16[256,512]{1,0:T(8,128)(2,1)}, u32[]{:S(2)}) copy-start(bf16[256,512]{1,0:T(8,128)(2,1)} %constant.10.clone.places) | copy-start | bytes 786436
  20.7 11.5 %copy-start.2 = (bf16[256,256]{1,0:T(8,128)(2,1)S(1)}, bf16[256,256]{1,0:T(8,128)(2,1)}, u32[]{:S(2)}) copy-start(bf16[256,256]{1,0:T(8,128)(2,1)} %constant.9.clone.stencil) | copy-start | bytes 393220
  20.8 11.5 %copy-start.6 = (f32[1,1,1,16,16,256]{5,4,3,2,1,0:T(8,128)S(1)}, f32[1,1,1,16,16,256]{5,4,3,2,1,0:T(8,128)}, u32[]{:S(2)}) copy-start(f32[1,1,1,16,16,256]{5,4,3,2,1,0:T(8,128)} %param.13) | copy-start | bytes 786436
  22.7 7.1 %collective-permute-start.3 = (f32[176,128]{1,0:T(8,128)S(1)}, f32[176,128]{1,0:T(8,128)S(1)}, u32[]{:S(2)}, u32[]{:S(2)}) collective-permute-start(f32[176,128]{1,0:T(8,128)S(1)} %get-tuple-element.55), channel_id=1, source_target_pairs={{0,8},{8,16},{16,24},{24,0},{1,9},{9,17},{17,25},{25,1},{2,10},{10... | collective-permute-start | bytes 270344 | tf_op jit(solution)/shard_map/ppermute | solution.py:515
  23.1 9.1 %collective-permute-start.4 = (f32[176,128]{1,0:T(8,128)S(1)}, f32[176,128]{1,0:T(8,128)S(1)}, u32[]{:S(2)}, u32[]{:S(2)}) collective-permute-start(f32[176,128]{1,0:T(8,128)S(1)} %get-tuple-element.56), channel_id=1, source_target_pairs={{0,16},{8,24},{16,0},{24,8},{1,17},{9,25},{17,1},{25,9},{2,18},{10... | collective-permute-start | bytes 270344 | tf_op jit(solution)/shard_map/ppermute | solution.py:515
  26.7 5.5 %collective-permute-start.5 = (f32[176,128]{1,0:T(8,128)S(1)}, f32[176,128]{1,0:T(8,128)S(1)}, u32[]{:S(2)}, u32[]{:S(2)}) collective-permute-start(f32[176,128]{1,0:T(8,128)S(1)} %get-tuple-element.57), channel_id=1, source_target_pairs={{0,24},{8,0},{16,8},{24,16},{1,25},{9,1},{17,9},{25,17},{2,26},{10... | collective-permute-start | bytes 270344 | tf_op jit(solution)/shard_map/ppermute | solution.py:515
  34.1 6.6 %collective-permute-start.6 = (f32[144,128]{1,0:T(8,128)S(1)}, f32[144,128]{1,0:T(8,128)S(1)}, u32[]{:S(2)}, u32[]{:S(2)}) collective-permute-start(f32[144,128]{1,0:T(8,128)S(1)} %get-tuple-element.62), channel_id=1, source_target_pairs={{0,8},{8,16},{16,24},{24,0},{1,9},{9,17},{17,25},{25,1},{2,10},{10... | collective-permute-start | bytes 221192 | tf_op jit(solution)/shard_map/ppermute | solution.py:515
  36.1 6.8 %collective-permute-start.7 = (f32[144,128]{1,0:T(8,128)S(1)}, f32[144,128]{1,0:T(8,128)S(1)}, u32[]{:S(2)}, u32[]{:S(2)}) collective-permute-start(f32[144,128]{1,0:T(8,128)S(1)} %get-tuple-element.63), channel_id=1, source_target_pairs={{0,16},{8,24},{16,0},{24,8},{1,17},{9,25},{17,1},{25,9},{2,18},{10... | collective-permute-start | bytes 221192 | tf_op jit(solution)/shard_map/ppermute | solution.py:515
  37.6 5.4 %collective-permute-start.8 = (f32[144,128]{1,0:T(8,128)S(1)}, f32[144,128]{1,0:T(8,128)S(1)}, u32[]{:S(2)}, u32[]{:S(2)}) collective-permute-start(f32[144,128]{1,0:T(8,128)S(1)} %get-tuple-element.64), channel_id=1, source_target_pairs={{0,24},{8,0},{16,8},{24,16},{1,25},{9,1},{17,9},{25,17},{2,26},{10... | collective-permute-start | bytes 221192 | tf_op jit(solution)/shard_map/ppermute | solution.py:515
  44.6 6.7 %collective-permute-start.9 = (f32[144,128]{1,0:T(8,128)S(1)}, f32[144,128]{1,0:T(8,128)S(1)}, u32[]{:S(2)}, u32[]{:S(2)}) collective-permute-start(f32[144,128]{1,0:T(8,128)S(1)} %get-tuple-element.68), channel_id=1, source_target_pairs={{0,8},{8,16},{16,24},{24,0},{1,9},{9,17},{17,25},{25,1},{2,10},{10... | collective-permute-start | bytes 221192 | tf_op jit(solution)/shard_map/ppermute | solution.py:515
  46.6 7.0 %collective-permute-start.10 = (f32[144,128]{1,0:T(8,128)S(1)}, f32[144,128]{1,0:T(8,128)S(1)}, u32[]{:S(2)}, u32[]{:S(2)}) collective-permute-start(f32[144,128]{1,0:T(8,128)S(1)} %get-tuple-element.69), channel_id=1, source_target_pairs={{0,16},{8,24},{16,0},{24,8},{1,17},{9,25},{17,1},{25,9},{2,18},{10... | collective-permute-start | bytes 221192 | tf_op jit(solution)/shard_map/ppermute | solution.py:515
  47.8 5.7 %collective-permute-start.11 = (f32[144,128]{1,0:T(8,128)S(1)}, f32[144,128]{1,0:T(8,128)S(1)}, u32[]{:S(2)}, u32[]{:S(2)}) collective-permute-start(f32[144,128]{1,0:T(8,128)S(1)} %get-tuple-element.70), channel_id=1, source_target_pairs={{0,24},{8,0},{16,8},{24,16},{1,25},{9,1},{17,9},{25,17},{2,26},{10... | collective-permute-start | bytes 221192 | tf_op jit(solution)/shard_map/ppermute | solution.py:515
  55.1 6.9 %collective-permute-start.12 = (f32[144,128]{1,0:T(8,128)S(1)}, f32[144,128]{1,0:T(8,128)S(1)}, u32[]{:S(2)}, u32[]{:S(2)}) collective-permute-start(f32[144,128]{1,0:T(8,128)S(1)} %get-tuple-element.74), channel_id=1, source_target_pairs={{0,8},{8,16},{16,24},{24,0},{1,9},{9,17},{17,25},{25,1},{2,10},{10... | collective-permute-start | bytes 221192 | tf_op jit(solution)/shard_map/ppermute | solution.py:515
  57.2 7.1 %collective-permute-start.13 = (f32[144,128]{1,0:T(8,128)S(1)}, f32[144,128]{1,0:T(8,128)S(1)}, u32[]{:S(2)}, u32[]{:S(2)}) collective-permute-start(f32[144,128]{1,0:T(8,128)S(1)} %get-tuple-element.75), channel_id=1, source_target_pairs={{0,16},{8,24},{16,0},{24,8},{1,17},{9,25},{17,1},{25,9},{2,18},{10... | collective-permute-start | bytes 221192 | tf_op jit(solution)/shard_map/ppermute | solution.py:515
  58.4 6.0 %collective-permute-start.14 = (f32[144,128]{1,0:T(8,128)S(1)}, f32[144,128]{1,0:T(8,128)S(1)}, u32[]{:S(2)}, u32[]{:S(2)}) collective-permute-start(f32[144,128]{1,0:T(8,128)S(1)} %get-tuple-element.76), channel_id=1, source_target_pairs={{0,24},{8,0},{16,8},{24,16},{1,25},{9,1},{17,9},{25,17},{2,26},{10... | collective-permute-start | bytes 221192 | tf_op jit(solution)/shard_map/ppermute | solution.py:515

commit v8 on v7

--- a/solution.py
+++ b/solution.py
@@ -379,7 +379,28 @@
             heat[half, pl.ds(odd, SLOTS * CB, 2), :] = coarse[:, half * 128 : half * 128 + 128]
 
 
-def step(table, phase, solute, heat, got, own, stencil, places, all_records, ghosts):
+def inner_step(phase, solute, heat, stencil):
+    row = iota((SLOTS, TE, PLANE), 1)
+    lap = []
+    for field in (phase, solute):
+        high, low = halves(field.reshape(SLOTS * TE, PLANE))
+        total = (dot(high, stencil) + dot(low, stencil)).reshape(SLOTS, TE, PLANE) - 6.0 * field
+        total += jnp.where(row == 0, 0.0, pltpu.roll(field, 1, 1))
+        total += jnp.where(row == TE - 1, 0.0, pltpu.roll(field, TE - 1, 1))
+        lap.append(total)
+    squared = 1.0 - phase * phase
+    drive = solute if heat is None else heat + solute
+    change = ORDER_SPEED * (
+        lap[0] + phase - phase * phase * phase - COUPLING * drive * squared * squared
+    )
+    return phase + change, solute + SOLUTE_RATE * lap[1] + REJECTION * change
+
+
+def wide_heat(heat):
+    return jnp.concatenate([heat[0], heat[1]], axis=1).reshape(SLOTS, TE, PLANE)
+
+
+def gather_ghosts(table, got, own, all_records, ghosts):
     records = all_records.shape[0] - 2 * SLOTS
     cap = records // len(got)
     for number, value in enumerate(got):
@@ -389,42 +410,47 @@
         out, edge = merge_record(all_records, lambda face: table[face, slot])
         ghosts[slot, 0:TE, :] = out
         ghosts[slot, TE:REC, :] = edge
+
+
+def ghost_shares(ghosts, places):
     beside = jnp.concatenate(halves(ghosts[:, 0:TE, :].reshape(SLOTS * TE, 128)), axis=1)
     beside = dot(beside, places)
     row = iota((SLOTS, TE, PLANE), 1)
-    lap = []
-    for number, field in enumerate((phase, solute)):
-        high, low = halves(field.reshape(SLOTS * TE, PLANE))
-        total = dot(high, stencil) + dot(low, stencil)
-        total += beside[:, number * PLANE : number * PLANE + PLANE]
-        total = total.reshape(SLOTS, TE, PLANE) - 6.0 * field
-        sides = []
-        for face in range(2):
+    shares = []
+    for number in range(2):
+        share = beside[:, number * PLANE : number * PLANE + PLANE].reshape(SLOTS, TE, PLANE)
+        for face, at_row in ((0, 0), (1, TE - 1)):
             at = TE + face * 4 + number * 2
-            sides.append(
-                jnp.concatenate([ghosts[:, at : at + 1, :], ghosts[:, at + 1 : at + 2, :]], axis=2)
-            )
-        total += jnp.where(row == 0, sides[0], pltpu.roll(field, 1, 1))
-        total += jnp.where(row == TE - 1, sides[1], pltpu.roll(field, TE - 1, 1))
-        lap.append(total)
-    warm = jnp.concatenate([heat[0], heat[1]], axis=1).reshape(SLOTS, TE, PLANE)
-    squared = 1.0 - phase * phase
-    new_phase = phase + ORDER_SPEED * (
-        lap[0] + phase - phase * phase * phase - COUPLING * (warm + solute) * squared * squared
-    )
-    new_solute = solute + SOLUTE_RATE * lap[1] + REJECTION * (new_phase - phase)
-    return new_phase, new_solute
-
-
-def first_step_kernel(cap, table, phase, solute, own, picks, stencil, places, spreads, found, *rest):
+            side = jnp.concatenate([ghosts[:, at : at + 1, :], ghosts[:, at + 1 : at + 2, :]], axis=2)
+            share += jnp.where(row == at_row, side, 0.0)
+        shares.append(share)
+    return shares
+
+
+def add_shares(phase, solute, shares, heat_share=None):
+    change = ORDER_SPEED * shares[0]
+    if heat_share is not None:
+        change += heat_share
+    return phase + change, solute + SOLUTE_RATE * shares[1] + REJECTION * change
+
+
+def inner_kernel(has_heat, phase, solute, stencil, *rest):
+    phase_out, solute_out = rest[-2:]
+    heat = wide_heat(rest[0]) if has_heat else None
+    phase_out[...], solute_out[...] = inner_step(phase[...], solute[...], heat, stencil[...])
+
+
+def first_step_kernel(cap, table, old_phase, phase, solute, own, picks, places, spreads, found, *rest):
     others = lax.axis_size("gx") - 1
     got, rest = rest[:others], rest[others:]
     phase_out, solute_out, heat_out, own_out, *rest = rest
     send, (all_records, ghosts, blocks, held) = rest[:others], rest[others:]
     take_heat(cap, table, found, got, spreads[...], blocks, held, heat_out)
-    new_phase, new_solute = step(
-        table, phase[...], solute[...], heat_out[...], got, own, stencil[...], places[...],
-        all_records, ghosts,
+    gather_ghosts(table, got, own, all_records, ghosts)
+    squared = 1.0 - old_phase[...] * old_phase[...]
+    heat_share = (-ORDER_SPEED * COUPLING) * wide_heat(heat_out) * squared * squared
+    new_phase, new_solute = add_shares(
+        phase[...], solute[...], ghost_shares(ghosts, places[...]), heat_share
     )
     phase_out[...] = new_phase
     solute_out[...] = new_solute
@@ -438,29 +464,25 @@
     copy.wait()
 
 
-def middle_step_kernel(table, phase, solute, heat, own, picks, stencil, places, *rest):
+def middle_step_kernel(table, phase, solute, own, picks, places, *rest):
     others = lax.axis_size("gx") - 1
     got, (phase_out, solute_out, own_out, *rest) = rest[:others], rest[others:]
     send, (all_records, ghosts) = rest[:others], rest[others:]
-    new_phase, new_solute = step(
-        table, phase[...], solute[...], heat[...], got, own, stencil[...], places[...],
-        all_records, ghosts,
-    )
+    gather_ghosts(table, got, own, all_records, ghosts)
+    new_phase, new_solute = add_shares(phase[...], solute[...], ghost_shares(ghosts, places[...]))
     phase_out[...] = new_phase
     solute_out[...] = new_solute
     write_records(new_phase, new_solute, picks[...], own_out)
     pack(own_out, table, send)
 
 
-def last_step_kernel(table, phase, solute, heat, own, stencil, places, *rest):
+def last_step_kernel(table, phase, solute, own, places, *rest):
     others = lax.axis_size("gx") - 1
     got, (phase_out, solute_out, all_records, ghosts) = rest[:others], rest[others:]
-    new_phase, new_solute = step(
-        table, phase[...], solute[...], heat[...], got, own, stencil[...], places[...],
-        all_records, ghosts,
-    )
-    phase_out[...] = new_phase
-    solute_out[...] = new_solute
+    gather_ghosts(table, got, own, all_records, ghosts)
+    phase_out[...], solute_out[...] = add_shares(
+        phase[...], solute[...], ghost_shares(ghosts, places[...])
+    )
 
 
 def call(kernel, in_specs, out_shapes, scratch=(), out_specs=None, mib=16):
@@ -551,6 +573,12 @@
         pltpu.VMEM((records + 2 * SLOTS, REC, 128), F32),
         pltpu.VMEM((SLOTS, REC, 128), F32),
     ]
+    def inner(phase_field, solute_field, *heat):
+        return call(
+            functools.partial(inner_kernel, bool(heat)), [VMEM] * (3 + len(heat)), [field, field]
+        )(phase_field, solute_field, stencil, *heat)
+
+    inner_fields = inner(phase_field, solute_field)
     phase_field, solute_field, heat, own, *send = call(
         functools.partial(first_step_kernel, block_cap),
         [SMEM] + [VMEM] * (8 + others),
@@ -560,19 +588,21 @@
             pltpu.VMEM((count, deep * CB, 128), F32),
             pltpu.VMEM((SLOTS * CB, CB, 128), F32),
         ],
-    )(table, phase_field, solute_field, own, picks, stencil, places, spreads, found, *got)
+    )(table, phase_field, *inner_fields, own, picks, places, spreads, found, *got)
     for _ in range(PHASE_STEPS - 2):
         got = exchange(send)
+        inner_fields = inner(phase_field, solute_field, heat)
         phase_field, solute_field, own, *send = call(
             middle_step_kernel,
-            [SMEM] + [VMEM] * (7 + others),
+            [SMEM] + [VMEM] * (5 + others),
             [field, field, own_shape, *send_shapes],
             step_scratch,
-        )(table, phase_field, solute_field, heat, own, picks, stencil, places, *got)
+        )(table, *inner_fields, own, picks, places, *got)
     got = exchange(send)
+    inner_fields = inner(phase_field, solute_field, heat)
     phase_field, solute_field = call(
-        last_step_kernel, [SMEM] + [VMEM] * (6 + others), [field, field], step_scratch
-    )(table, phase_field, solute_field, heat, own, stencil, places, *got)
+        last_step_kernel, [SMEM] + [VMEM] * (4 + others), [field, field], step_scratch
+    )(table, *inner_fields, own, places, *got)
     return heat_out, phase_field.reshape(phase.shape), solute_field.reshape(solute.shape)
 
 

time: 66.7 us -> 65.5 us (0.982)
  waiting for transfers between devices: 20.3 us -> 18.3 us
  Pallas kernels: 12.8 us -> 13.6 us
    ppermute x15, waiting for transfers between devices: 20.3 us -> 18.3 us  [pass_on(): lax.ppermute(value, 'gx', [(i, (i + shift) % count) for i in range(count)])]
    pallas_call x3 -> x7, Pallas kernels: 5.24 us -> 6.21 us  [the longest x2 2.56 us: local(): call(middle_step_kernel, [SMEM] + [VMEM] * (5 + others), [field, field, o...]
  transfers between devices with their start and end apart: 16 -> 16, of which waited for: 10 -> 10; matrix products, arithmetic and copies ran while one was open for 1% -> 1% of each run, Pallas kernels for 2% -> 6%
where the time goes in v8:
time: 65.5 us; the launch traced here: 65.1 us
  starting transfers between devices  29.1 us (44%)
  waiting for transfers between devices  18.3 us (28%)
  Pallas kernels  13.6 us (21%)
  local copies, waits for them, and re-layouts  3.27 us (5%)
  between operations  0.83 us (1%)
    ppermute x15, starting transfers between devices, pass_on(): lax.ppermute(value, 'gx', [(i, (i + shift) % count) for i in range(count)])  23.9 us
    ppermute x15, waiting for transfers between devices, pass_on(): lax.ppermute(value, 'gx', [(i, (i + shift) % count) for i in range(count)])  18.3 us
    all_to_all x1, starting transfers between devices, local(): lax.all_to_all(sides, ('gy', 'gz'), split_axis=0, concat_axis=0, tiled=True)  5.18 us
    unnamed x28, local copies, waits for them, and re-layouts  2.58 us
    pallas_call x2, Pallas kernels, local(): call(middle_step_kernel, [SMEM] + [VMEM] * (5 + others), [field, field, o...  2.56 us
    pallas_call x1, Pallas kernels, local(): call(functools.partial(sides_kernel, sizes, plane_cap), [ANY] * 5, [shape...  2.17 us
    pallas_call x4, Pallas kernels, inner(): call(functools.partial(inner_kernel, bool(heat)), [VMEM] * (3 + len(heat)...  1.97 us
    pallas_call x1, Pallas kernels, local(): call(functools.partial(heat_kernel, block_cap, sizes), [SMEM] + [VMEM] *...  1.91 us
  transfers between devices with their start and end apart: 16, of which 10 were waited for; matrix products, arithmetic and copies ran while one was open for 1% of the time, Pallas kernels for 6%

profile of v8, /device:TPU:0, one launch (start us, length us, event | category | flops | bytes accessed | tf_op | source)
XLA Modules:
  0.0 65.1 jit_solution(14518243667720289084)
XLA Ops:
  0.6 0.0 copy-start
  0.6 2.2 %shard_map.130 = (f32[8,24,128]{2,1,0:T(8,128)}, s32[8,128]{1,0:T(8,128)}, f32[8,128]{1,0:T(8,128)}, f32[8,128]{1,0:T(8,128)}, f32[8,128]{1,0:T(8,128)}, /*index=5*/f32[8,128]{1,0:T(8,128)}) custom-call(s32[1,16]{1,0:T(1,128)} %bitcast.15, s32[1,16]{1,0:T(1,128)} %bitcast.16, s32[6,1,16]{2,1,0:T(1,128)} %bitcast.14, f32[8,32,128]{2,1,0:T(8,128)} %h.3, ...), custom_call_target="tpu_custom_call" | custom-call | tf_op jit(solution)/shard_map/pallas_call | solution.py:514
  2.8 0.0 copy-start.13
  2.8 5.2 %all-to-all-start = ((f32[8,24,128]{2,1,0:T(8,128)}), f32[8,24,128]{2,1,0:T(8,128)S(1)}, u32[]{:S(2)}, u32[]{:S(2)}) async-start(f32[8,24,128]{2,1,0:T(8,128)} %get-tuple-element.50), calls=%async_computation | async-start | bytes 196608 | tf_op jit(solution)/shard_map/all_to_all | solution.py:534
  8.0 0.0 copy-done.13
  8.0 2.7 %collective-permute-start = (f32[8,128]{1,0:T(8,128)S(1)}, f32[8,128]{1,0:T(8,128)S(1)}, u32[]{:S(2)}, u32[]{:S(2)}) collective-permute-start(f32[8,128]{1,0:T(8,128)S(1)} %copy-done.13), channel_id=1, source_target_pairs={{0,16},{8,24},{16,0},{24,8},{1,17},{9,25},{17,1},{25,9},{2,18},{10... | collective-permute-start | bytes 12296 | tf_op jit(solution)/shard_map/ppermute | solution.py:537
  10.7 0.0 copy-done
  10.7 0.0 copy-done.10
  10.7 0.9 %copy-done.2 = f32[1,1,1,16,16,256]{5,4,3,2,1,0:T(8,128)S(1)} copy-done((f32[1,1,1,16,16,256]{5,4,3,2,1,0:T(8,128)S(1)}, f32[1,1,1,16,16,256]{5,4,3,2,1,0:T(8,128)}, u32[]{:S(2)}) %copy-start.2) | copy-done | bytes 262168
  11.6 0.9 %copy-done.7 = f32[1,1,1,16,16,256]{5,4,3,2,1,0:T(8,128)S(1)} copy-done((f32[1,1,1,16,16,256]{5,4,3,2,1,0:T(8,128)S(1)}, f32[1,1,1,16,16,256]{5,4,3,2,1,0:T(8,128)}, u32[]{:S(2)}) %copy-start.7) | copy-done | bytes 262168
  12.6 1.0 %shard_map.131 = (f32[32,24,128]{2,1,0:T(8,128)S(1)}, f32[144,128]{1,0:T(8,128)S(1)}, f32[144,128]{1,0:T(8,128)S(1)}, f32[144,128]{1,0:T(8,128)S(1)}) custom-call(s32[8,128]{1,0:T(8,128)S(1)} %copy-done.10, f32[16,16,256]{2,1,0:T(8,128)S(1)} %bitcast.9, f32[16,16,256]{2,1,0:T(8,128)S(1)} %bitcast.12, bf16[512,256]{1,0:T(8,128)(2,1)S(1)} %copy-done), custom_call_target="tpu_custom_call" | custom-call | tf_op jit(solution)/shard_map/pallas_call | solution.py:547
  13.6 0.0 copy-start.11
  13.6 0.0 collective-permute-done.rest_1_
  13.6 0.0 all-to-all-done.got
  13.6 0.0 copy-done.5
  13.6 0.0 copy-done.6
  13.6 0.0 copy-done.12
  13.6 0.6 copy-done.11
  14.3 1.6 %collective-permute-start.1 = (f32[104,128]{1,0:T(8,128)S(1)}, f32[104,128]{1,0:T(8,128)S(1)}, u32[]{:S(2)}, u32[]{:S(2)}) collective-permute-start(f32[104,128]{1,0:T(8,128)S(1)} %get-tuple-element.56), channel_id=1, source_target_pairs={{0,8},{8,16},{16,24},{24,0},{1,9},{9,17},{17,25},{25,1},{2,10},{10... | collective-permute-start | bytes 159752 | tf_op jit(solution)/shard_map/ppermute | solution.py:537
  15.9 2.2 %collective-permute-start.2 = (f32[104,128]{1,0:T(8,128)S(1)}, f32[104,128]{1,0:T(8,128)S(1)}, u32[]{:S(2)}, u32[]{:S(2)}) collective-permute-start(f32[104,128]{1,0:T(8,128)S(1)} %get-tuple-element.57), channel_id=1, source_target_pairs={{0,24},{8,0},{16,8},{24,16},{1,25},{9,1},{17,9},{25,17},{2,26},{10... | collective-permute-start | bytes 159752 | tf_op jit(solution)/shard_map/ppermute | solution.py:537
  18.1 0.7 %slice.24 = f32[1,8]{1,0:T(1,128)S(1)} slice(f32[8,128]{1,0:T(8,128)} %get-tuple-element.49), slice={[0:1], [0:8]} | slice | bytes 64 | tf_op jit(solution)/shard_map/slice | solution.py:558
  18.8 1.8 %collective-permute-done.1.low = f32[104,128]{1,0:T(8,128)S(1)} collective-permute-done((f32[104,128]{1,0:T(8,128)S(1)}, f32[104,128]{1,0:T(8,128)S(1)}, u32[]{:S(2)}, u32[]{:S(2)}) %collective-permute-start.1) | collective-permute-done | bytes 53280 | tf_op jit(solution)/shard_map/ppermute | solution.py:537
  20.7 0.0 collective-permute-done.2.high
  20.7 0.0 copy-start.3
  20.7 0.0 copy-start.4
  20.8 0.0 copy-start.8
  20.8 1.9 %shard_map.133 = (f32[8,32,128]{2,1,0:T(8,128)S(1)}, f32[32,128]{1,0:T(8,128)S(1)}, f32[176,128]{1,0:T(8,128)S(1)}, f32[176,128]{1,0:T(8,128)S(1)}, f32[176,128]{1,0:T(8,128)S(1)}) custom-call(s32[4,8]{1,0:T(4,128)S(1)} %maximum_convert_fusion.request, f32[8,32,128]{2,1,0:T(8,128)S(1)} %copy-done.5, f32[8,32,128]{2,1,0:T(8,128)S(1)} %copy-done.6, ...), custom_call_target="tpu_custom_call" | custom-call | tf_op jit(solution)/shard_map/pallas_call | solution.py:561
  22.7 0.4 collective-permute-start.3
  23.1 3.6 %collective-permute-start.4 = (f32[176,128]{1,0:T(8,128)S(1)}, f32[176,128]{1,0:T(8,128)S(1)}, u32[]{:S(2)}, u32[]{:S(2)}) collective-permute-start(f32[176,128]{1,0:T(8,128)S(1)} %get-tuple-element.66), channel_id=1, source_target_pairs={{0,16},{8,24},{16,0},{24,8},{1,17},{9,25},{17,1},{25,9},{2,18},{10... | collective-permute-start | bytes 270344 | tf_op jit(solution)/shard_map/ppermute | solution.py:537
  26.7 0.1 collective-permute-start.5
  26.7 0.0 copy-done.3
  26.7 0.0 copy-done.4
  26.7 0.0 copy-done.8
  26.7 0.5 shard_map.135
  27.2 2.6 %collective-permute-done.3.rest_0_ = f32[176,128]{1,0:T(8,128)S(1)} collective-permute-done((f32[176,128]{1,0:T(8,128)S(1)}, f32[176,128]{1,0:T(8,128)S(1)}, u32[]{:S(2)}, u32[]{:S(2)}) %collective-permute-start.3) | collective-permute-done | bytes 90144 | tf_op jit(solution)/shard_map/ppermute | solution.py:537
  29.8 2.4 %collective-permute-done.4.rest_1_ = f32[176,128]{1,0:T(8,128)S(1)} collective-permute-done((f32[176,128]{1,0:T(8,128)S(1)}, f32[176,128]{1,0:T(8,128)S(1)}, u32[]{:S(2)}, u32[]{:S(2)}) %collective-permute-start.4) | collective-permute-done | bytes 90144 | tf_op jit(solution)/shard_map/ppermute | solution.py:537
  32.1 0.1 collective-permute-done.5.rest_2_
  32.2 0.0 copy-done.1
  32.2 1.7 %shard_map.136 = (f32[16,16,256]{2,1,0:T(8,128)S(1)}, f32[16,16,256]{2,1,0:T(8,128)S(1)}, f32[2,256,128]{2,1,0:T(8,128)S(1)}, f32[32,24,128]{2,1,0:T(8,128)S(1)}...) custom-call(s32[8,128]{1,0:T(8,128)S(1)} %copy-done.10, f32[16,16,256]{2,1,0:T(8,128)S(1)} %bitcast.11, ...), custom_call_target="tpu_custom_call" | custom-call | tf_op jit(solution)/shard_map/pallas_call | solution.py:582
  33.9 2.0 %collective-permute-start.6 = (f32[144,128]{1,0:T(8,128)S(1)}, f32[144,128]{1,0:T(8,128)S(1)}, u32[]{:S(2)}, u32[]{:S(2)}) collective-permute-start(f32[144,128]{1,0:T(8,128)S(1)} %get-tuple-element.74), channel_id=1, source_target_pairs={{0,8},{8,16},{16,24},{24,0},{1,9},{9,17},{17,25},{25,1},{2,10},{10... | collective-permute-start | bytes 221192 | tf_op jit(solution)/shard_map/ppermute | solution.py:537
  35.9 1.4 %collective-permute-start.7 = (f32[144,128]{1,0:T(8,128)S(1)}, f32[144,128]{1,0:T(8,128)S(1)}, u32[]{:S(2)}, u32[]{:S(2)}) collective-permute-start(f32[144,128]{1,0:T(8,128)S(1)} %get-tuple-element.75), channel_id=1, source_target_pairs={{0,16},{8,24},{16,0},{24,8},{1,17},{9,25},{17,1},{25,9},{2,18},{10... | collective-permute-start | bytes 221192 | tf_op jit(solution)/shard_map/ppermute | solution.py:537
  37.4 1.0 %collective-permute-start.8 = (f32[144,128]{1,0:T(8,128)S(1)}, f32[144,128]{1,0:T(8,128)S(1)}, u32[]{:S(2)}, u32[]{:S(2)}) collective-permute-start(f32[144,128]{1,0:T(8,128)S(1)} %get-tuple-element.76), channel_id=1, source_target_pairs={{0,24},{8,0},{16,8},{24,16},{1,25},{9,1},{17,9},{25,17},{2,26},{10... | collective-permute-start | bytes 221192 | tf_op jit(solution)/shard_map/ppermute | solution.py:537
  38.4 0.5 shard_map.137
  38.9 1.6 %collective-permute-done.6.rest_0_ = f32[144,128]{1,0:T(8,128)S(1)} collective-permute-done((f32[144,128]{1,0:T(8,128)S(1)}, f32[144,128]{1,0:T(8,128)S(1)}, u32[]{:S(2)}, u32[]{:S(2)}) %collective-permute-start.6) | collective-permute-done | bytes 73760 | tf_op jit(solution)/shard_map/ppermute | solution.py:537
  40.5 2.3 %collective-permute-done.7.rest_1_ = f32[144,128]{1,0:T(8,128)S(1)} collective-permute-done((f32[144,128]{1,0:T(8,128)S(1)}, f32[144,128]{1,0:T(8,128)S(1)}, u32[]{:S(2)}, u32[]{:S(2)}) %collective-permute-start.7) | collective-permute-done | bytes 73760 | tf_op jit(solution)/shard_map/ppermute | solution.py:537
  42.8 0.0 collective-permute-done.8.rest_2_
  42.8 1.3 %shard_map.138 = (f32[16,16,256]{2,1,0:T(8,128)S(1)}, f32[16,16,256]{2,1,0:T(8,128)S(1)}, f32[32,24,128]{2,1,0:T(8,128)S(1)}, f32[144,128]{1,0:T(8,128)S(1)}, f3...) custom-call(s32[8,128]{1,0:T(8,128)S(1)} %copy-done.10, f32[16,16,256]{2,1,0:T(8,128)S(1)} %get-tuple-element.71.phase, ...), custom_call_target="tpu_custom_call" | custom-call | tf_op jit(solution)/shard_map/pallas_call | solution.py:595
  44.1 1.9 %collective-permute-start.9 = (f32[144,128]{1,0:T(8,128)S(1)}, f32[144,128]{1,0:T(8,128)S(1)}, u32[]{:S(2)}, u32[]{:S(2)}) collective-permute-start(f32[144,128]{1,0:T(8,128)S(1)} %get-tuple-element.82), channel_id=1, source_target_pairs={{0,8},{8,16},{16,24},{24,0},{1,9},{9,17},{17,25},{25,1},{2,10},{10... | collective-permute-start | bytes 221192 | tf_op jit(solution)/shard_map/ppermute | solution.py:537
  46.0 1.2 %collective-permute-start.10 = (f32[144,128]{1,0:T(8,128)S(1)}, f32[144,128]{1,0:T(8,128)S(1)}, u32[]{:S(2)}, u32[]{:S(2)}) collective-permute-start(f32[144,128]{1,0:T(8,128)S(1)} %get-tuple-element.83), channel_id=1, source_target_pairs={{0,16},{8,24},{16,0},{24,8},{1,17},{9,25},{17,1},{25,9},{2,18},{10... | collective-permute-start | bytes 221192 | tf_op jit(solution)/shard_map/ppermute | solution.py:537
  47.3 1.2 %collective-permute-start.11 = (f32[144,128]{1,0:T(8,128)S(1)}, f32[144,128]{1,0:T(8,128)S(1)}, u32[]{:S(2)}, u32[]{:S(2)}) collective-permute-start(f32[144,128]{1,0:T(8,128)S(1)} %get-tuple-element.84), channel_id=1, source_target_pairs={{0,24},{8,0},{16,8},{24,16},{1,25},{9,1},{17,9},{25,17},{2,26},{10... | collective-permute-start | bytes 221192 | tf_op jit(solution)/shard_map/ppermute | solution.py:537
  48.5 0.5 shard_map.139
  49.0 1.8 %collective-permute-done.9.rest_0_ = f32[144,128]{1,0:T(8,128)S(1)} collective-permute-done((f32[144,128]{1,0:T(8,128)S(1)}, f32[144,128]{1,0:T(8,128)S(1)}, u32[]{:S(2)}, u32[]{:S(2)}) %collective-permute-start.9) | collective-permute-done | bytes 73760 | tf_op jit(solution)/shard_map/ppermute | solution.py:537
  50.8 2.2 %collective-permute-done.10.rest_1_ = f32[144,128]{1,0:T(8,128)S(1)} collective-permute-done((f32[144,128]{1,0:T(8,128)S(1)}, f32[144,128]{1,0:T(8,128)S(1)}, u32[]{:S(2)}, u32[]{:S(2)}) %collective-permute-start.10) | collective-permute-done | bytes 73760 | tf_op jit(solution)/shard_map/ppermute | solution.py:537
  53.0 0.0 collective-permute-done.11.rest_2_
  53.0 1.3 %shard_map.140 = (f32[16,16,256]{2,1,0:T(8,128)S(1)}, f32[16,16,256]{2,1,0:T(8,128)S(1)}, f32[32,24,128]{2,1,0:T(8,128)S(1)}, f32[144,128]{1,0:T(8,128)S(1)}, f3...) custom-call(s32[8,128]{1,0:T(8,128)S(1)} %copy-done.10, f32[16,16,256]{2,1,0:T(8,128)S(1)} %get-tuple-element.79.phase, ...), custom_call_target="tpu_custom_call" | custom-call | tf_op jit(solution)/shard_map/pallas_call | solution.py:595
  54.3 2.1 %collective-permute-start.12 = (f32[144,128]{1,0:T(8,128)S(1)}, f32[144,128]{1,0:T(8,128)S(1)}, u32[]{:S(2)}, u32[]{:S(2)}) collective-permute-start(f32[144,128]{1,0:T(8,128)S(1)} %get-tuple-element.90), channel_id=1, source_target_pairs={{0,8},{8,16},{16,24},{24,0},{1,9},{9,17},{17,25},{25,1},{2,10},{10... | collective-permute-start | bytes 221192 | tf_op jit(solution)/shard_map/ppermute | solution.py:537
  56.4 1.1 %collective-permute-start.13 = (f32[144,128]{1,0:T(8,128)S(1)}, f32[144,128]{1,0:T(8,128)S(1)}, u32[]{:S(2)}, u32[]{:S(2)}) collective-permute-start(f32[144,128]{1,0:T(8,128)S(1)} %get-tuple-element.91), channel_id=1, source_target_pairs={{0,16},{8,24},{16,0},{24,8},{1,17},{9,25},{17,1},{25,9},{2,18},{10... | collective-permute-start | bytes 221192 | tf_op jit(solution)/shard_map/ppermute | solution.py:537
  57.5 1.3 %collective-permute-start.14 = (f32[144,128]{1,0:T(8,128)S(1)}, f32[144,128]{1,0:T(8,128)S(1)}, u32[]{:S(2)}, u32[]{:S(2)}) collective-permute-start(f32[144,128]{1,0:T(8,128)S(1)} %get-tuple-element.92), channel_id=1, source_target_pairs={{0,24},{8,0},{16,8},{24,16},{1,25},{9,1},{17,9},{25,17},{2,26},{10... | collective-permute-start | bytes 221192 | tf_op jit(solution)/shard_map/ppermute | solution.py:537
  58.8 0.7 %shard_map.134 = f32[8,32,128]{2,1,0:T(8,128)} custom-call(f32[8,32,128]{2,1,0:T(8,128)S(1)} %get-tuple-element.60.value), custom_call_target="tpu_custom_call" | custom-call | tf_op jit(solution)/shard_map/pallas_call | solution.py:568
  59.5 0.5 shard_map.141
  60.0 1.2 %collective-permute-done.12.rest_0_ = f32[144,128]{1,0:T(8,128)S(1)} collective-permute-done((f32[144,128]{1,0:T(8,128)S(1)}, f32[144,128]{1,0:T(8,128)S(1)}, u32[]{:S(2)}, u32[]{:S(2)}) %collective-permute-start.12) | collective-permute-done | bytes 73760 | tf_op jit(solution)/shard_map/ppermute | solution.py:537
  61.2 2.2 %collective-permute-done.13.rest_1_ = f32[144,128]{1,0:T(8,128)S(1)} collective-permute-done((f32[144,128]{1,0:T(8,128)S(1)}, f32[144,128]{1,0:T(8,128)S(1)}, u32[]{:S(2)}, u32[]{:S(2)}) %collective-permute-start.13) | collective-permute-done | bytes 73760 | tf_op jit(solution)/shard_map/ppermute | solution.py:537
  63.5 0.0 collective-permute-done.14.rest_2_
  63.5 1.7 %shard_map.142 = (f32[16,16,256]{2,1,0:T(8,128)}, f32[16,16,256]{2,1,0:T(8,128)}) custom-call(s32[8,128]{1,0:T(8,128)S(1)} %copy-done.10, f32[16,16,256]{2,1,0:T(8,128)S(1)} %get-tuple-element.87.phase, f32[16,16,256]{2,1,0:T(8,128)S(1)} %get-tuple-element.88.solute, f32[32,24,128]{2,1,0:T(8,128)S(1)} %get-tuple-element.89.own, ...), custom_call_target="tpu_custom_call" | custom-call | tf_op jit(solution)/shard_map/pallas_call | solution.py:603
  (14 shorter events, 0.1 us)
Async XLA Ops:
  0.6 10.1 %copy-start = (bf16[512,256]{1,0:T(8,128)(2,1)S(1)}, bf16[512,256]{1,0:T(8,128)(2,1)}, u32[]{:S(2)}) copy-start(bf16[512,256]{1,0:T(8,128)(2,1)} %constant.8.clone.picks) | copy-start | bytes 786436
  2.8 5.2 %copy-start.13 = (f32[8,128]{1,0:T(8,128)S(1)}, f32[8,128]{1,0:T(8,128)}, u32[]{:S(2)}) copy-start(f32[8,128]{1,0:T(8,128)} %get-tuple-element.55) | copy-start | bytes 12292
  2.8 10.8 %all-to-all-start = ((f32[8,24,128]{2,1,0:T(8,128)}), f32[8,24,128]{2,1,0:T(8,128)S(1)}, u32[]{:S(2)}, u32[]{:S(2)}) async-start(f32[8,24,128]{2,1,0:T(8,128)} %get-tuple-element.50), calls=%async_computation | async-start | bytes 196608 | tf_op jit(solution)/shard_map/all_to_all | solution.py:534
  8.0 2.7 %copy-start.10 = (s32[8,128]{1,0:T(8,128)S(1)}, s32[8,128]{1,0:T(8,128)}, u32[]{:S(2)}) copy-start(s32[8,128]{1,0:T(8,128)} %get-tuple-element.53.table) | copy-start | bytes 12292
  8.0 5.6 %collective-permute-start = (f32[8,128]{1,0:T(8,128)S(1)}, f32[8,128]{1,0:T(8,128)S(1)}, u32[]{:S(2)}, u32[]{:S(2)}) collective-permute-start(f32[8,128]{1,0:T(8,128)S(1)} %copy-done.13), channel_id=1, source_target_pairs={{0,16},{8,24},{16,0},{24,8},{1,17},{9,25},{17,1},{25,9},{2,18},{10... | collective-permute-start | bytes 12296 | tf_op jit(solution)/shard_map/ppermute | solution.py:537
  10.7 1.0 %copy-start.2 = (f32[1,1,1,16,16,256]{5,4,3,2,1,0:T(8,128)S(1)}, f32[1,1,1,16,16,256]{5,4,3,2,1,0:T(8,128)}, u32[]{:S(2)}) copy-start(f32[1,1,1,16,16,256]{5,4,3,2,1,0:T(8,128)} %param.13) | copy-start | bytes 786436
  11.6 0.9 %copy-start.7 = (f32[1,1,1,16,16,256]{5,4,3,2,1,0:T(8,128)S(1)}, f32[1,1,1,16,16,256]{5,4,3,2,1,0:T(8,128)}, u32[]{:S(2)}) copy-start(f32[1,1,1,16,16,256]{5,4,3,2,1,0:T(8,128)} %param.14) | copy-start | bytes 786436
  12.6 1.0 %copy-start.5 = (f32[8,32,128]{2,1,0:T(8,128)S(1)}, f32[8,32,128]{2,1,0:T(8,128)}, u32[]{:S(2)}) copy-start(f32[8,32,128]{2,1,0:T(8,128)} %h.3) | copy-start | bytes 393220
  12.6 1.0 %copy-start.6 = (f32[8,32,128]{2,1,0:T(8,128)S(1)}, f32[8,32,128]{2,1,0:T(8,128)}, u32[]{:S(2)}) copy-start(f32[8,32,128]{2,1,0:T(8,128)} %k.3) | copy-start | bytes 393220
  12.6 1.0 %copy-start.12 = (f32[8,128]{1,0:T(8,128)S(1)}, f32[8,128]{1,0:T(8,128)}, u32[]{:S(2)}) copy-start(f32[8,128]{1,0:T(8,128)} %get-tuple-element.52.ask_down) | copy-start | bytes 12292
  13.6 0.7 %copy-start.11 = (f32[8,128]{1,0:T(8,128)S(1)}, f32[8,128]{1,0:T(8,128)}, u32[]{:S(2)}) copy-start(f32[8,128]{1,0:T(8,128)} %get-tuple-element.51.ask_up) | copy-start | bytes 12292
  14.3 6.4 %collective-permute-start.1 = (f32[104,128]{1,0:T(8,128)S(1)}, f32[104,128]{1,0:T(8,128)S(1)}, u32[]{:S(2)}, u32[]{:S(2)}) collective-permute-start(f32[104,128]{1,0:T(8,128)S(1)} %get-tuple-element.56), channel_id=1, source_target_pairs={{0,8},{8,16},{16,24},{24,0},{1,9},{9,17},{17,25},{25,1},{2,10},{10... | collective-permute-start | bytes 159752 | tf_op jit(solution)/shard_map/ppermute | solution.py:537
  15.9 4.8 %collective-permute-start.2 = (f32[104,128]{1,0:T(8,128)S(1)}, f32[104,128]{1,0:T(8,128)S(1)}, u32[]{:S(2)}, u32[]{:S(2)}) collective-permute-start(f32[104,128]{1,0:T(8,128)S(1)} %get-tuple-element.57), channel_id=1, source_target_pairs={{0,24},{8,0},{16,8},{24,16},{1,25},{9,1},{17,9},{25,17},{2,26},{10... | collective-permute-start | bytes 159752 | tf_op jit(solution)/shard_map/ppermute | solution.py:537
  20.7 6.0 %copy-start.3 = (f32[1,1,1,16,16,256]{5,4,3,2,1,0:T(8,128)S(1)}, f32[1,1,1,16,16,256]{5,4,3,2,1,0:T(8,128)}, u32[]{:S(2)}) copy-start(f32[1,1,1,16,16,256]{5,4,3,2,1,0:T(8,128)} %param.13) | copy-start | bytes 786436
  20.7 6.0 %copy-start.4 = (bf16[256,256]{1,0:T(8,128)(2,1)S(1)}, bf16[256,256]{1,0:T(8,128)(2,1)}, u32[]{:S(2)}) copy-start(bf16[256,256]{1,0:T(8,128)(2,1)} %constant.9.clone.stencil) | copy-start | bytes 393220
  20.8 6.0 %copy-start.8 = (f32[1,1,1,16,16,256]{5,4,3,2,1,0:T(8,128)S(1)}, f32[1,1,1,16,16,256]{5,4,3,2,1,0:T(8,128)}, u32[]{:S(2)}) copy-start(f32[1,1,1,16,16,256]{5,4,3,2,1,0:T(8,128)} %param.14) | copy-start | bytes 786436
  22.7 7.1 %collective-permute-start.3 = (f32[176,128]{1,0:T(8,128)S(1)}, f32[176,128]{1,0:T(8,128)S(1)}, u32[]{:S(2)}, u32[]{:S(2)}) collective-permute-start(f32[176,128]{1,0:T(8,128)S(1)} %get-tuple-element.65), channel_id=1, source_target_pairs={{0,8},{8,16},{16,24},{24,0},{1,9},{9,17},{17,25},{25,1},{2,10},{10... | collective-permute-start | bytes 270344 | tf_op jit(solution)/shard_map/ppermute | solution.py:537
  23.1 9.1 %collective-permute-start.4 = (f32[176,128]{1,0:T(8,128)S(1)}, f32[176,128]{1,0:T(8,128)S(1)}, u32[]{:S(2)}, u32[]{:S(2)}) collective-permute-start(f32[176,128]{1,0:T(8,128)S(1)} %get-tuple-element.66), channel_id=1, source_target_pairs={{0,16},{8,24},{16,0},{24,8},{1,17},{9,25},{17,1},{25,9},{2,18},{10... | collective-permute-start | bytes 270344 | tf_op jit(solution)/shard_map/ppermute | solution.py:537
  26.7 5.6 %copy-start.1 = (bf16[256,512]{1,0:T(8,128)(2,1)S(1)}, bf16[256,512]{1,0:T(8,128)(2,1)}, u32[]{:S(2)}) copy-start(bf16[256,512]{1,0:T(8,128)(2,1)} %constant.10.clone.places) | copy-start | bytes 786436
  26.7 5.6 %copy-start.9 = (bf16[256,256]{1,0:T(8,128)(2,1)S(1)}, bf16[256,256]{1,0:T(8,128)(2,1)}, u32[]{:S(2)}) copy-start(bf16[256,256]{1,0:T(8,128)(2,1)} %constant.11.clone.spreads) | copy-start | bytes 393220
  26.7 5.5 %collective-permute-start.5 = (f32[176,128]{1,0:T(8,128)S(1)}, f32[176,128]{1,0:T(8,128)S(1)}, u32[]{:S(2)}, u32[]{:S(2)}) collective-permute-start(f32[176,128]{1,0:T(8,128)S(1)} %get-tuple-element.67), channel_id=1, source_target_pairs={{0,24},{8,0},{16,8},{24,16},{1,25},{9,1},{17,9},{25,17},{2,26},{10... | collective-permute-start | bytes 270344 | tf_op jit(solution)/shard_map/ppermute | solution.py:537
  33.9 6.6 %collective-permute-start.6 = (f32[144,128]{1,0:T(8,128)S(1)}, f32[144,128]{1,0:T(8,128)S(1)}, u32[]{:S(2)}, u32[]{:S(2)}) collective-permute-start(f32[144,128]{1,0:T(8,128)S(1)} %get-tuple-element.74), channel_id=1, source_target_pairs={{0,8},{8,16},{16,24},{24,0},{1,9},{9,17},{17,25},{25,1},{2,10},{10... | collective-permute-start | bytes 221192 | tf_op jit(solution)/shard_map/ppermute | solution.py:537
  35.9 6.9 %collective-permute-start.7 = (f32[144,128]{1,0:T(8,128)S(1)}, f32[144,128]{1,0:T(8,128)S(1)}, u32[]{:S(2)}, u32[]{:S(2)}) collective-permute-start(f32[144,128]{1,0:T(8,128)S(1)} %get-tuple-element.75), channel_id=1, source_target_pairs={{0,16},{8,24},{16,0},{24,8},{1,17},{9,25},{17,1},{25,9},{2,18},{10... | collective-permute-start | bytes 221192 | tf_op jit(solution)/shard_map/ppermute | solution.py:537
  37.4 5.5 %collective-permute-start.8 = (f32[144,128]{1,0:T(8,128)S(1)}, f32[144,128]{1,0:T(8,128)S(1)}, u32[]{:S(2)}, u32[]{:S(2)}) collective-permute-start(f32[144,128]{1,0:T(8,128)S(1)} %get-tuple-element.76), channel_id=1, source_target_pairs={{0,24},{8,0},{16,8},{24,16},{1,25},{9,1},{17,9},{25,17},{2,26},{10... | collective-permute-start | bytes 221192 | tf_op jit(solution)/shard_map/ppermute | solution.py:537
  44.1 6.7 %collective-permute-start.9 = (f32[144,128]{1,0:T(8,128)S(1)}, f32[144,128]{1,0:T(8,128)S(1)}, u32[]{:S(2)}, u32[]{:S(2)}) collective-permute-start(f32[144,128]{1,0:T(8,128)S(1)} %get-tuple-element.82), channel_id=1, source_target_pairs={{0,8},{8,16},{16,24},{24,0},{1,9},{9,17},{17,25},{25,1},{2,10},{10... | collective-permute-start | bytes 221192 | tf_op jit(solution)/shard_map/ppermute | solution.py:537
  46.0 7.0 %collective-permute-start.10 = (f32[144,128]{1,0:T(8,128)S(1)}, f32[144,128]{1,0:T(8,128)S(1)}, u32[]{:S(2)}, u32[]{:S(2)}) collective-permute-start(f32[144,128]{1,0:T(8,128)S(1)} %get-tuple-element.83), channel_id=1, source_target_pairs={{0,16},{8,24},{16,0},{24,8},{1,17},{9,25},{17,1},{25,9},{2,18},{10... | collective-permute-start | bytes 221192 | tf_op jit(solution)/shard_map/ppermute | solution.py:537
  47.3 5.7 %collective-permute-start.11 = (f32[144,128]{1,0:T(8,128)S(1)}, f32[144,128]{1,0:T(8,128)S(1)}, u32[]{:S(2)}, u32[]{:S(2)}) collective-permute-start(f32[144,128]{1,0:T(8,128)S(1)} %get-tuple-element.84), channel_id=1, source_target_pairs={{0,24},{8,0},{16,8},{24,16},{1,25},{9,1},{17,9},{25,17},{2,26},{10... | collective-permute-start | bytes 221192 | tf_op jit(solution)/shard_map/ppermute | solution.py:537
  54.3 6.9 %collective-permute-start.12 = (f32[144,128]{1,0:T(8,128)S(1)}, f32[144,128]{1,0:T(8,128)S(1)}, u32[]{:S(2)}, u32[]{:S(2)}) collective-permute-start(f32[144,128]{1,0:T(8,128)S(1)} %get-tuple-element.90), channel_id=1, source_target_pairs={{0,8},{8,16},{16,24},{24,0},{1,9},{9,17},{17,25},{25,1},{2,10},{10... | collective-permute-start | bytes 221192 | tf_op jit(solution)/shard_map/ppermute | solution.py:537
  56.4 7.1 %collective-permute-start.13 = (f32[144,128]{1,0:T(8,128)S(1)}, f32[144,128]{1,0:T(8,128)S(1)}, u32[]{:S(2)}, u32[]{:S(2)}) collective-permute-start(f32[144,128]{1,0:T(8,128)S(1)} %get-tuple-element.91), channel_id=1, source_target_pairs={{0,16},{8,24},{16,0},{24,8},{1,17},{9,25},{17,1},{25,9},{2,18},{10... | collective-permute-start | bytes 221192 | tf_op jit(solution)/shard_map/ppermute | solution.py:537
  57.5 6.0 %collective-permute-start.14 = (f32[144,128]{1,0:T(8,128)S(1)}, f32[144,128]{1,0:T(8,128)S(1)}, u32[]{:S(2)}, u32[]{:S(2)}) collective-permute-start(f32[144,128]{1,0:T(8,128)S(1)} %get-tuple-element.92), channel_id=1, source_target_pairs={{0,24},{8,0},{16,8},{24,16},{1,25},{9,1},{17,9},{25,17},{2,26},{10... | collective-permute-start | bytes 221192 | tf_op jit(solution)/shard_map/ppermute | solution.py:537

commit v9 on v8

--- a/solution.py
+++ b/solution.py
@@ -126,18 +126,14 @@
 
 
 def write_tables(plane_cap, source, block, neighbour, asked, table):
-    me = lax.axis_index("gx").astype(F32)
-    count = len(asked)
+    me = lax.axis_index("gx")
+    count = asked.shape[0]
     records = (count - 1) * plane_cap
     cap = float(plane_cap)
-
-    def wrapped(shift):
-        return jnp.where(shift < 0.0, shift + float(count), shift)
-
     square = (SLOTS, SLOTS)
     before = iota(square, 0) < iota(square, 1)
     slot = iota((1, SLOTS), 1).astype(F32)
-    source_row, block_column = source[...].astype(F32), column_of(block[...].astype(F32))
+    source_row, block_column = (source[...] ^ me).astype(F32), column_of(block[...].astype(F32))
     source_column = column_of(source_row)
     rank = jnp.sum(
         jnp.where((source_column == source_row) & before, 1.0, 0.0), axis=0, keepdims=True
@@ -145,37 +141,37 @@
     rank_column = column_of(rank)
     lane = iota((SLOTS, 128), 1).astype(F32)
     for shift in range(count):
-        hit = (wrapped(source_column - me) == float(shift)) & (rank_column == lane)
+        hit = (source_column == float(shift)) & (rank_column == lane)
         row = jnp.sum(jnp.where(hit, block_column, 0.0), axis=0, keepdims=True)
-        asked[shift][...] = jnp.broadcast_to(row, asked[shift].shape)
-    table[6:7, 0:SLOTS] = wrapped(me - source_row).astype(jnp.int32)
+        asked[shift : shift + 1, :] = row
+    table[6:7, 0:SLOTS] = source[...] ^ me
     table[7:8, 0:SLOTS] = rank.astype(jnp.int32)
     slot_column = iota((SLOTS, records), 0).astype(F32)
     for face in range(FACES):
         number = neighbour[face]
-        owner_row, number_row = (number >> 4).astype(F32), number.astype(F32)
-        owner_column, number_column = column_of(owner_row), column_of(number_row)
-        other_row = (number_row >= 0.0) & (owner_row != me)
-        alike = (owner_column == owner_row) & (owner_column >= 0.0) & (owner_column != me)
+        shift = jnp.where(number < 0, 0, (number >> 4) ^ me)
+        shift_row, number_row = shift.astype(F32), number.astype(F32)
+        shift_column, number_column = column_of(shift_row), column_of(number_row)
+        alike = (shift_column == shift_row) & (shift_column > 0.0)
         receive_rank = jnp.sum(
             jnp.where(alike & (number_column < number_row), 1.0, 0.0), axis=0, keepdims=True
         )
         send_rank = jnp.sum(jnp.where(alike & before, 1.0, 0.0), axis=0, keepdims=True)
-        here = records + (number_row - owner_row * SLOTS)
-        there = (wrapped(me - owner_row) - 1.0) * cap + receive_rank
-        receive = jnp.where(owner_row == me, here, there)
+        here = records + (number & (SLOTS - 1)).astype(F32)
+        there = (shift_row - 1.0) * cap + receive_rank
+        receive = jnp.where(shift_row == 0.0, here, there)
         receive = jnp.where(number_row < 0.0, records + SLOTS + slot, receive)
         table[face : face + 1, 0:SLOTS] = receive.astype(jnp.int32)
-        key = jnp.where(other_row, (wrapped(owner_row - me) - 1.0) * cap + send_rank, -1.0)
+        key = jnp.where(shift_row > 0.0, (shift_row - 1.0) * cap + send_rank, -1.0)
         hit = iota((SLOTS, records), 1).astype(F32) == column_of(key)
         tile = jnp.sum(jnp.where(hit, slot_column, 0.0), axis=0, keepdims=True)
         table[face ^ 1 : (face ^ 1) + 1, SLOTS : SLOTS + records] = tile.astype(jnp.int32)
 
 
 def sides_kernel(
-    sizes, plane_cap, source_far, block_far, neighbour_far, h_far, k_far, send, table, *rest
+    sizes, plane_cap, source_far, block_far, neighbour_far, h_far, k_far, send, table, asked,
+    source, block, neighbour, h, k, sems,
 ):
-    *asked, source, block, neighbour, h, k, sems = rest
     ny, nz = sizes
     my_y, my_z = lax.axis_index("gy"), lax.axis_index("gz")
     bx = h.shape[0]
@@ -216,18 +212,20 @@
     return read
 
 
-def layers_kernel(sizes, h, k, got, ask_up, ask_down, *rest):
-    down, up = rest[-2:]
+def layers_kernel(sizes, h, k, got, _, first, second):
     bx, by, bz = h.shape
     read = side_reader(sizes, got, bx)
+    even = lax.rem(lax.axis_index("gx"), 2) == 0
     around = [read(-1, 0), read(1, 0), read(0, -1), read(0, 1)]
-    for out, near, far, ask in ((down, 0, 1, ask_down), (up, bx - 1, bx - 2, ask_up)):
-        out[0:by, :] = h[near]
-        out[by : 2 * by, :] = h[far]
-        out[2 * by : 3 * by, :] = k[near]
-        for number, side in enumerate(around):
-            out[3 * by + number : 3 * by + number + 1, :] = side[near : near + 1, :]
-        out[3 * by + 4 : 3 * by + 8, :] = ask[0:4, :]
+    layers = [(h[bx - 1], h[0]), (h[bx - 2], h[1]), (k[bx - 1], k[0])]
+    layers += [(side[bx - 1 : bx, :], side[0:1, :]) for side in around]
+    row = 0
+    for upper, lower in layers:
+        first[row : row + upper.shape[0], :] = jnp.where(even, upper, lower)
+        second[row : row + upper.shape[0], :] = jnp.where(even, lower, upper)
+        row += upper.shape[0]
+    for out in (first, second):
+        out[row:, :] = jnp.zeros((out.shape[0] - row, bz), F32)
 
 
 def block_layout(cap):
@@ -247,17 +245,18 @@
     return h + RATE * k * (total - 6.0 * t)
 
 
-def heat_kernel(cap, sizes, request, h, k, got, low, high, *rest):
-    count = lax.axis_size("gx")
-    packed, (out, found, *send, held) = rest[: count - 1], rest[count - 1 :]
-
+def heat_kernel(cap, sizes, request, h, k, got, first, second, out, found, *rest):
+    *send, held = rest
     bx, by, bz = h.shape
     h0, k0 = h[...], k[...]
     read = side_reader(sizes, got, bx)
-    me = lax.axis_index("gx")
+    me, count = lax.axis_index("gx"), lax.axis_size("gx")
+    even = lax.rem(me, 2) == 0
     layers, lines = [], []
+    pairs = (first[...], second[...])
+    low, high = jnp.where(even, *pairs[::-1]), jnp.where(even, *pairs)
     for beside, inside in ((low, me > 0), (high, me < count - 1)):
-        beside = jnp.where(inside, beside[...], 0.0)
+        beside = jnp.where(inside, beside, 0.0)
         layers.append([beside[part * by : part * by + by, :][None] for part in range(3)])
         lines.append([beside[3 * by + n : 3 * by + n + 1, :] for n in range(4)])
     y_sides = [[read(d, 0, part) for part in range(3)] for d in (-1, 1)]
@@ -299,7 +298,7 @@
     for shift in range(count):
         total = jnp.zeros((deep, CB, bz), F32)
         for rank in range(cap):
-            block = request[(count - shift) % count, rank]
+            block = request[shift, rank]
             a, b, c = block // (nby * nbz), (block // nbz) % nby, block % nbz
             for part in range(parts):
                 at = rank * parts + part
@@ -307,12 +306,7 @@
                 moved = pltpu.roll(patch, (CB * at - CB * c + bz) % bz, 2)
                 total = jnp.where(group == at, moved, total)
         total = total.reshape(deep * CB, bz)
-        if shift == 0:
-            found[...] = total
-        else:
-            behind = packed[shift - 1].shape[0]
-            send[shift - 1][0:behind, :] = packed[shift - 1][...]
-            send[shift - 1][behind:, :] = total
+        (send[shift - 1] if shift else found)[...] = total
 
 
 def write_records(phase, solute, picks, own):
@@ -352,16 +346,18 @@
             out[rank * REC + TE : rank * REC + REC, :] = edge
 
 
-def first_pack_kernel(table, phase, solute, picks, own, *send):
+def first_pack_kernel(table, asked, phase, solute, picks, own, *send):
     write_records(phase[...], solute[...], picks[...], own)
     pack(own, table, send)
-
-
-def take_heat(cap, table, found, got, spreads, blocks, held, heat):
+    for number, out in enumerate(send):
+        row = asked[number + 1 : number + 2, :]
+        out[out.shape[0] - 8 :, :] = jnp.broadcast_to(row, (8, 128))
+
+
+def take_heat(cap, table, found, spreads, blocks, held, heat):
     parts, deep = block_layout(cap)
-    blocks[0] = found[...]
-    for number, value in enumerate(got):
-        blocks[1 + number] = value[value.shape[0] - deep * CB :, :]
+    for number, value in enumerate(found):
+        blocks[number] = value[...]
     group = iota((CB, 128), 1) // CB
     for slot in range(SLOTS):
         back, rank = table[6, slot], table[7, slot]
@@ -440,12 +436,12 @@
     phase_out[...], solute_out[...] = inner_step(phase[...], solute[...], heat, stencil[...])
 
 
-def first_step_kernel(cap, table, old_phase, phase, solute, own, picks, places, spreads, found, *rest):
+def first_step_kernel(cap, table, old_phase, phase, solute, own, picks, places, spreads, *rest):
     others = lax.axis_size("gx") - 1
-    got, rest = rest[:others], rest[others:]
+    found, got, rest = rest[: others + 1], rest[others + 1 : 2 * others + 1], rest[2 * others + 1 :]
     phase_out, solute_out, heat_out, own_out, *rest = rest
     send, (all_records, ghosts, blocks, held) = rest[:others], rest[others:]
-    take_heat(cap, table, found, got, spreads[...], blocks, held, heat_out)
+    take_heat(cap, table, found, spreads[...], blocks, held, heat_out)
     gather_ghosts(table, got, own, all_records, ghosts)
     squared = 1.0 - old_phase[...] * old_phase[...]
     heat_share = (-ORDER_SPEED * COUPLING) * wide_heat(heat_out) * squared * squared
@@ -511,10 +507,10 @@
     picks, stencil, places, spreads = tables()
 
     integers = functools.partial(jax.ShapeDtypeStruct, dtype=jnp.int32)
-    sides, table, *asked = call(
+    sides, table, asked = call(
         functools.partial(sides_kernel, sizes, plane_cap),
         [ANY] * 5,
-        [shape(sizes[0] * sizes[1], 3 * bx, 128), integers((8, 128)), *[shape(8, 128)] * count],
+        [shape(sizes[0] * sizes[1], 3 * bx, 128), integers((8, 128)), shape(count, 128)],
         [
             pltpu.VMEM((1, SLOTS), jnp.int32),
             pltpu.VMEM((1, SLOTS), jnp.int32),
@@ -533,41 +529,42 @@
     )
     sides = lax.all_to_all(sides, ("gy", "gz"), split_axis=0, concat_axis=0, tiled=True)
 
-    def pass_on(value, shift):
-        return lax.ppermute(value, "gx", [(i, (i + shift) % count) for i in range(count)])
+    def swap(value, partner):
+        return lax.ppermute(value, "gx", [(i, partner(i)) for i in range(count)])
 
     def exchange(values):
-        return [pass_on(value, shift) for shift, value in enumerate(values, 1)]
-
-    farther = [pass_on(asked[shift], shift) for shift in range(2, others)]
+        got = {s: swap(values[s - 1], lambda i, s=s: i ^ s) for s in range(others, 0, -1)}
+        return [got[s] for s in range(1, count)]
 
     phase_field = phase.reshape(SLOTS, TE, PLANE)
     solute_field = solute.reshape(SLOTS, TE, PLANE)
     own_shape, send_shapes = shape(2 * SLOTS, REC, 128), [shape(plane_cap * REC, 128)] * others
-    own, *packed = call(first_pack_kernel, [SMEM] + [VMEM] * 3, [own_shape, *send_shapes])(
-        table, phase_field, solute_field, picks
-    )
+    own, *packed = call(
+        first_pack_kernel,
+        [SMEM] + [VMEM] * 4,
+        [own_shape] + [shape(plane_cap * REC + 8, 128)] * others,
+    )(table, asked, phase_field, solute_field, picks)
+    got = exchange(packed)
+    request = jnp.stack([asked[0], *[value[plane_cap * REC] for value in got]])
+    request = request[:, :block_cap].astype(jnp.int32)
 
     layer = shape(3 * by + 8, bz)
-    down, up = call(
-        functools.partial(layers_kernel, sizes), [VMEM] * 5 + [ANY] * (1 + len(farther)), [layer, layer]
-    )(enthalpy, conductivity, sides, asked[1], asked[others], packed[0], *farther)
-    from_low, from_high = pass_on(up, 1), pass_on(down, others)
-    row = 3 * by + 4
-    request = [asked[0][0], from_low[row], *[value[0] for value in farther], from_high[row]]
-    request = jnp.stack([value[:block_cap] for value in request]).astype(jnp.int32)
+    first, second = call(
+        functools.partial(layers_kernel, sizes), [VMEM] * 3 + [ANY], [layer, layer]
+    )(enthalpy, conductivity, sides, packed[0])
+    first = swap(first, lambda i: i ^ 1)
+    second = swap(second, lambda i: i if i in (0, others) else ((i + 1) ^ 1) - 1)
     _, deep = block_layout(block_cap)
     brick = shape(bx, by, bz)
-    heated, found, *send = call(
+    heated, *found = call(
         functools.partial(heat_kernel, block_cap, sizes),
-        [SMEM] + [VMEM] * (5 + others),
-        [brick, shape(deep * CB, 128)] + [shape(plane_cap * REC + deep * CB, 128)] * others,
+        [SMEM] + [VMEM] * 5,
+        [brick] + [shape(deep * CB, 128)] * count,
         [pltpu.VMEM((bx, by // CB, CB, bz), F32)],
-    )(request, enthalpy, conductivity, sides, from_low, from_high, *packed)
-
+    )(request, enthalpy, conductivity, sides, first, second)
+    found[1:] = exchange(found[1:])
     (heat_out,) = call(write_out_kernel, [ANY], [brick], [pltpu.SemaphoreType.DMA], [ANY])(heated)
 
-    got = exchange(send)
     field = shape(SLOTS, TE, PLANE)
     step_scratch = [
         pltpu.VMEM((records + 2 * SLOTS, REC, 128), F32),
@@ -581,14 +578,14 @@
     inner_fields = inner(phase_field, solute_field)
     phase_field, solute_field, heat, own, *send = call(
         functools.partial(first_step_kernel, block_cap),
-        [SMEM] + [VMEM] * (8 + others),
+        [SMEM] + [VMEM] * (7 + count + others),
         [field, field, shape(2, SLOTS * TE, 128), own_shape, *send_shapes],
         step_scratch
         + [
             pltpu.VMEM((count, deep * CB, 128), F32),
             pltpu.VMEM((SLOTS * CB, CB, 128), F32),
         ],
-    )(table, phase_field, *inner_fields, own, picks, places, spreads, found, *got)
+    )(table, phase_field, *inner_fields, own, picks, places, spreads, *found, *got)
     for _ in range(PHASE_STEPS - 2):
         got = exchange(send)
         inner_fields = inner(phase_field, solute_field, heat)

time: 65.5 us -> 71.4 us (1.090)
  waiting for transfers between devices: 18.3 us -> 21.8 us
  starting transfers between devices: 29.1 us -> 32.1 us
    ppermute x15 -> x17, starting transfers between devices: 23.9 us -> 28.4 us  [swap(): return lax.ppermute(value, 'gx', [(i, partner(i)) for i in range(count)])]
    all_to_all x1, waiting for transfers between devices: 0.01 us -> 3.58 us  [local(): lax.all_to_all(sides, ('gy', 'gz'), split_axis=0, concat_axis=0, tiled=True)]
    all_to_all x1, starting transfers between devices: 5.18 us -> 3.72 us  [local(): lax.all_to_all(sides, ('gy', 'gz'), split_axis=0, concat_axis=0, tiled=True)]
    ppermute x15 -> x17, waiting for transfers between devices: 18.3 us -> 18.2 us  [swap(): return lax.ppermute(value, 'gx', [(i, partner(i)) for i in range(count)])]
    unnamed x28 -> x24, local copies, waits for them, and re-layouts: 2.58 us -> 2.61 us
  transfers between devices with their start and end apart: 16 -> 18, of which waited for: 10 -> 11; matrix products, arithmetic and copies ran while one was open for 1% -> 0% of each run, Pallas kernels for 6% -> 4%
where the time goes in v9:
time: 71.4 us; the launch traced here: 71.1 us
  starting transfers between devices  32.1 us (45%)
  waiting for transfers between devices  21.8 us (31%)
  Pallas kernels  13.6 us (19%)
  local copies, waits for them, and re-layouts  2.62 us (4%)
  between operations  0.88 us (1%)
    ppermute x17, starting transfers between devices, swap(): return lax.ppermute(value, 'gx', [(i, partner(i)) for i in range(count)])  28.4 us
    ppermute x17, waiting for transfers between devices, swap(): return lax.ppermute(value, 'gx', [(i, partner(i)) for i in range(count)])  18.2 us
    all_to_all x1, starting transfers between devices, local(): lax.all_to_all(sides, ('gy', 'gz'), split_axis=0, concat_axis=0, tiled=True)  3.72 us
    all_to_all x1, waiting for transfers between devices, local(): lax.all_to_all(sides, ('gy', 'gz'), split_axis=0, concat_axis=0, tiled=True)  3.58 us
    unnamed x24, local copies, waits for them, and re-layouts  2.61 us
    pallas_call x2, Pallas kernels, local(): call(middle_step_kernel, [SMEM] + [VMEM] * (5 + others), [field, field, o...  2.55 us
    pallas_call x1, Pallas kernels, local(): call(functools.partial(sides_kernel, sizes, plane_cap), [ANY] * 5, [shape...  2.17 us
    pallas_call x4, Pallas kernels, inner(): call(functools.partial(inner_kernel, bool(heat)), [VMEM] * (3 + len(heat)...  1.96 us
  transfers between devices with their start and end apart: 18, of which 11 were waited for; matrix products, arithmetic and copies ran while one was open for 0% of the time, Pallas kernels for 4%

profile of v9, /device:TPU:0, one launch (start us, length us, event | category | flops | bytes accessed | tf_op | source)
XLA Modules:
  0.0 71.1 jit_solution(9375783398020414590)
XLA Ops:
  0.6 0.0 copy-start
  0.6 2.2 %shard_map.130 = (f32[8,24,128]{2,1,0:T(8,128)}, s32[8,128]{1,0:T(8,128)}, f32[4,128]{1,0:T(4,128)}) custom-call(s32[1,16]{1,0:T(1,128)} %bitcast.15, s32[1,16]{1,0:T(1,128)} %bitcast.16, s32[6,1,16]{2,1,0:T(1,128)} %bitcast.14, f32[8,32,128]{2,1,0:T(8,128)} %h.3, f32[8,32,128]{2,1,0:T(8,128)} %k.3), custom_call_target="tpu_custom_call" | custom-call | tf_op jit(solution)/shard_map/pallas_call | solution.py:510
  2.8 0.0 copy-start.10
  2.8 0.0 copy-start.11
  2.8 0.0 copy-done
  2.9 0.7 copy-done.10
  3.5 0.0 copy-done.11
  3.5 0.9 %copy-done.2 = f32[1,1,1,16,16,256]{5,4,3,2,1,0:T(8,128)S(1)} copy-done((f32[1,1,1,16,16,256]{5,4,3,2,1,0:T(8,128)S(1)}, f32[1,1,1,16,16,256]{5,4,3,2,1,0:T(8,128)}, u32[]{:S(2)}) %copy-start.2) | copy-done | bytes 262168
  4.5 0.9 %copy-done.7 = f32[1,1,1,16,16,256]{5,4,3,2,1,0:T(8,128)S(1)} copy-done((f32[1,1,1,16,16,256]{5,4,3,2,1,0:T(8,128)S(1)}, f32[1,1,1,16,16,256]{5,4,3,2,1,0:T(8,128)}, u32[]{:S(2)}) %copy-start.7) | copy-done | bytes 262168
  5.4 1.0 %shard_map.131 = (f32[32,24,128]{2,1,0:T(8,128)S(1)}, f32[152,128]{1,0:T(8,128)S(1)}, f32[152,128]{1,0:T(8,128)S(1)}, f32[152,128]{1,0:T(8,128)S(1)}) custom-call(s32[8,128]{1,0:T(8,128)S(1)} %copy-done.10, f32[4,128]{1,0:T(4,128)S(1)} %copy-done.11, f32[16,16,256]{2,1,0:T(8,128)S(1)} %bitcast.9, f32[16,16,256]{2,1,0:T(8,128)S(1)} %bitcast.12, ...), custom_call_target="tpu_custom_call" | custom-call | tf_op jit(solution)/shard_map/pallas_call | solution.py:542
  6.4 0.0 copy-start.5
  6.4 4.1 %collective-permute-start.1 = (f32[152,128]{1,0:T(8,128)S(1)}, f32[152,128]{1,0:T(8,128)S(1)}, u32[]{:S(2)}, u32[]{:S(2)}) collective-permute-start(f32[152,128]{1,0:T(8,128)S(1)} %get-tuple-element.49), channel_id=1, source_target_pairs={{0,16},{8,24},{16,0},{24,8},{1,17},{9,25},{17,1},{25,9},{2,18},{10... | collective-permute-start | bytes 233480 | tf_op jit(solution)/shard_map/ppermute | solution.py:533
  10.5 1.3 %collective-permute-start.2 = (f32[152,128]{1,0:T(8,128)S(1)}, f32[152,128]{1,0:T(8,128)S(1)}, u32[]{:S(2)}, u32[]{:S(2)}) collective-permute-start(f32[152,128]{1,0:T(8,128)S(1)} %get-tuple-element.50), channel_id=1, source_target_pairs={{0,24},{8,16},{16,8},{24,0},{1,25},{9,17},{17,9},{25,1},{2,26},{10... | collective-permute-start | bytes 233480 | tf_op jit(solution)/shard_map/ppermute | solution.py:533
  11.9 0.2 collective-permute-start
  12.1 3.7 %all-to-all-start = ((f32[8,24,128]{2,1,0:T(8,128)}), f32[8,24,128]{2,1,0:T(8,128)S(1)}, u32[]{:S(2)}, u32[]{:S(2)}) async-start(f32[8,24,128]{2,1,0:T(8,128)} %get-tuple-element.51), calls=%async_computation | async-start | bytes 196608 | tf_op jit(solution)/shard_map/all_to_all | solution.py:530
  15.8 0.0 collective-permute-done.1.rest_5_
  15.8 1.3 %collective-permute-done.2.rest_6_ = f32[152,128]{1,0:T(8,128)S(1)} collective-permute-done((f32[152,128]{1,0:T(8,128)S(1)}, f32[152,128]{1,0:T(8,128)S(1)}, u32[]{:S(2)}, u32[]{:S(2)}) %collective-permute-start.2) | collective-permute-done | bytes 77856 | tf_op jit(solution)/shard_map/ppermute | solution.py:533
  17.1 0.3 collective-permute-done.rest_4_
  17.4 3.6 %all-to-all-done.got = f32[8,24,128]{2,1,0:T(8,128)S(1)} async-done(((f32[8,24,128]{2,1,0:T(8,128)}), f32[8,24,128]{2,1,0:T(8,128)S(1)}, u32[]{:S(2)}, u32[]{:S(2)}) %all-to-all-start) | async-done | bytes 98336 | tf_op jit(solution)/shard_map/all_to_all | solution.py:530
  21.0 0.0 copy-done.6
  21.0 0.0 copy-done.5
  21.1 0.0 copy-start.3
  21.1 1.9 %collective-permute-start.3 = (f32[104,128]{1,0:T(8,128)S(1)}, f32[104,128]{1,0:T(8,128)S(1)}, u32[]{:S(2)}, u32[]{:S(2)}) collective-permute-start(f32[104,128]{1,0:T(8,128)S(1)} %get-tuple-element.52), channel_id=1, source_target_pairs={{0,8},{8,0},{16,24},{24,16},{1,9},{9,1},{17,25},{25,17},{2,10},{10... | collective-permute-start | bytes 159752 | tf_op jit(solution)/shard_map/ppermute | solution.py:533
  22.9 0.7 collective-permute-start.4
  23.6 0.0 copy-start.4
  23.6 1.7 %collective-permute-done.3.first = f32[104,128]{1,0:T(8,128)S(1)} collective-permute-done((f32[104,128]{1,0:T(8,128)S(1)}, f32[104,128]{1,0:T(8,128)S(1)}, u32[]{:S(2)}, u32[]{:S(2)}) %collective-permute-start.3) | collective-permute-done | bytes 53280 | tf_op jit(solution)/shard_map/ppermute | solution.py:533
  25.3 0.0 collective-permute-done.4.second
  25.3 1.9 %shard_map.133 = (f32[8,32,128]{2,1,0:T(8,128)S(1)}, f32[32,128]{1,0:T(8,128)S(1)}, f32[32,128]{1,0:T(8,128)S(1)}, f32[32,128]{1,0:T(8,128)S(1)}, f32[32,128]{1,0:T(8,128)S(1)}) custom-call(s32[4,8]{1,0:T(4,128)S(1)} %slice_convert_fusion.request, f32[8,32,128]{2,1,0:T(8,128)S(1)} %copy-done.5, f32[8,32,128]{2,1,0:T(8,128)S(1)} %copy-done.6, ...), custom_call_target="tpu_custom_call" | custom-call | tf_op jit(solution)/shard_map/pallas_call | solution.py:559
  27.2 4.0 %collective-permute-start.5 = (f32[32,128]{1,0:T(8,128)S(1)}, f32[32,128]{1,0:T(8,128)S(1)}, u32[]{:S(2)}, u32[]{:S(2)}) collective-permute-start(f32[32,128]{1,0:T(8,128)S(1)} %get-tuple-element.59), channel_id=1, source_target_pairs={{0,8},{8,0},{16,24},{24,16},{1,9},{9,1},{17,25},{25,17},{2,10},{10... | collective-permute-start | bytes 49160 | tf_op jit(solution)/shard_map/ppermute | solution.py:533
  31.1 1.5 %collective-permute-start.6 = (f32[32,128]{1,0:T(8,128)S(1)}, f32[32,128]{1,0:T(8,128)S(1)}, u32[]{:S(2)}, u32[]{:S(2)}) collective-permute-start(f32[32,128]{1,0:T(8,128)S(1)} %get-tuple-element.60), channel_id=1, source_target_pairs={{0,16},{8,24},{16,0},{24,8},{1,17},{9,25},{17,1},{25,9},{2,18},{10... | collective-permute-start | bytes 49160 | tf_op jit(solution)/shard_map/ppermute | solution.py:533
  32.7 1.4 %collective-permute-start.7 = (f32[32,128]{1,0:T(8,128)S(1)}, f32[32,128]{1,0:T(8,128)S(1)}, u32[]{:S(2)}, u32[]{:S(2)}) collective-permute-start(f32[32,128]{1,0:T(8,128)S(1)} %get-tuple-element.61), channel_id=1, source_target_pairs={{0,24},{8,16},{16,8},{24,0},{1,25},{9,17},{17,9},{25,1},{2,26},{10... | collective-permute-start | bytes 49160 | tf_op jit(solution)/shard_map/ppermute | solution.py:533
  34.1 0.0 copy-done.8
  34.1 0.0 copy-done.3
  34.1 0.5 shard_map.135
  34.6 0.0 collective-permute-done.5.rest_1_
  34.6 1.2 %collective-permute-done.6.rest_2_ = f32[32,128]{1,0:T(8,128)S(1)} collective-permute-done((f32[32,128]{1,0:T(8,128)S(1)}, f32[32,128]{1,0:T(8,128)S(1)}, u32[]{:S(2)}, u32[]{:S(2)}) %collective-permute-start.6) | collective-permute-done | bytes 16416 | tf_op jit(solution)/shard_map/ppermute | solution.py:533
  35.8 2.4 %collective-permute-done.7.rest_3_ = f32[32,128]{1,0:T(8,128)S(1)} collective-permute-done((f32[32,128]{1,0:T(8,128)S(1)}, f32[32,128]{1,0:T(8,128)S(1)}, u32[]{:S(2)}, u32[]{:S(2)}) %collective-permute-start.7) | collective-permute-done | bytes 16416 | tf_op jit(solution)/shard_map/ppermute | solution.py:533
  38.2 0.0 copy-done.9
  38.2 1.7 %shard_map.136 = (f32[16,16,256]{2,1,0:T(8,128)S(1)}, f32[16,16,256]{2,1,0:T(8,128)S(1)}, f32[2,256,128]{2,1,0:T(8,128)S(1)}, f32[32,24,128]{2,1,0:T(8,128)S(1)}...) custom-call(s32[8,128]{1,0:T(8,128)S(1)} %copy-done.10, f32[16,16,256]{2,1,0:T(8,128)S(1)} %bitcast.11, ...), custom_call_target="tpu_custom_call" | custom-call | tf_op jit(solution)/shard_map/pallas_call | solution.py:579
  39.9 0.2 collective-permute-start.8
  40.1 1.8 %collective-permute-start.9 = (f32[144,128]{1,0:T(8,128)S(1)}, f32[144,128]{1,0:T(8,128)S(1)}, u32[]{:S(2)}, u32[]{:S(2)}) collective-permute-start(f32[144,128]{1,0:T(8,128)S(1)} %get-tuple-element.69), channel_id=1, source_target_pairs={{0,16},{8,24},{16,0},{24,8},{1,17},{9,25},{17,1},{25,9},{2,18},{10... | collective-permute-start | bytes 221192 | tf_op jit(solution)/shard_map/ppermute | solution.py:533
  41.9 2.4 %collective-permute-start.10 = (f32[144,128]{1,0:T(8,128)S(1)}, f32[144,128]{1,0:T(8,128)S(1)}, u32[]{:S(2)}, u32[]{:S(2)}) collective-permute-start(f32[144,128]{1,0:T(8,128)S(1)} %get-tuple-element.70), channel_id=1, source_target_pairs={{0,24},{8,16},{16,8},{24,0},{1,25},{9,17},{17,9},{25,1},{2,26},{10... | collective-permute-start | bytes 221192 | tf_op jit(solution)/shard_map/ppermute | solution.py:533
  44.4 0.5 shard_map.137
  44.9 0.0 collective-permute-done.8.rest_0_
  44.9 0.5 collective-permute-done.9.rest_1_
  45.4 2.8 %collective-permute-done.10.rest_2_ = f32[144,128]{1,0:T(8,128)S(1)} collective-permute-done((f32[144,128]{1,0:T(8,128)S(1)}, f32[144,128]{1,0:T(8,128)S(1)}, u32[]{:S(2)}, u32[]{:S(2)}) %collective-permute-start.10) | collective-permute-done | bytes 73760 | tf_op jit(solution)/shard_map/ppermute | solution.py:533
  48.2 1.3 %shard_map.138 = (f32[16,16,256]{2,1,0:T(8,128)S(1)}, f32[16,16,256]{2,1,0:T(8,128)S(1)}, f32[32,24,128]{2,1,0:T(8,128)S(1)}, f32[144,128]{1,0:T(8,128)S(1)}, f3...) custom-call(s32[8,128]{1,0:T(8,128)S(1)} %copy-done.10, f32[16,16,256]{2,1,0:T(8,128)S(1)} %get-tuple-element.65.phase, ...), custom_call_target="tpu_custom_call" | custom-call | tf_op jit(solution)/shard_map/pallas_call | solution.py:592
  49.5 0.1 collective-permute-start.11
  49.5 3.7 %collective-permute-start.12 = (f32[144,128]{1,0:T(8,128)S(1)}, f32[144,128]{1,0:T(8,128)S(1)}, u32[]{:S(2)}, u32[]{:S(2)}) collective-permute-start(f32[144,128]{1,0:T(8,128)S(1)} %get-tuple-element.77), channel_id=1, source_target_pairs={{0,16},{8,24},{16,0},{24,8},{1,17},{9,25},{17,1},{25,9},{2,18},{10... | collective-permute-start | bytes 221192 | tf_op jit(solution)/shard_map/ppermute | solution.py:533
  53.3 0.7 collective-permute-start.13
  53.9 0.5 shard_map.139
  54.4 0.0 collective-permute-done.11.rest_0_
  54.4 2.1 %collective-permute-done.12.rest_1_ = f32[144,128]{1,0:T(8,128)S(1)} collective-permute-done((f32[144,128]{1,0:T(8,128)S(1)}, f32[144,128]{1,0:T(8,128)S(1)}, u32[]{:S(2)}, u32[]{:S(2)}) %collective-permute-start.12) | collective-permute-done | bytes 73760 | tf_op jit(solution)/shard_map/ppermute | solution.py:533
  56.5 3.7 %collective-permute-done.13.rest_2_ = f32[144,128]{1,0:T(8,128)S(1)} collective-permute-done((f32[144,128]{1,0:T(8,128)S(1)}, f32[144,128]{1,0:T(8,128)S(1)}, u32[]{:S(2)}, u32[]{:S(2)}) %collective-permute-start.13) | collective-permute-done | bytes 73760 | tf_op jit(solution)/shard_map/ppermute | solution.py:533
  60.2 1.3 %shard_map.140 = (f32[16,16,256]{2,1,0:T(8,128)S(1)}, f32[16,16,256]{2,1,0:T(8,128)S(1)}, f32[32,24,128]{2,1,0:T(8,128)S(1)}, f32[144,128]{1,0:T(8,128)S(1)}, f3...) custom-call(s32[8,128]{1,0:T(8,128)S(1)} %copy-done.10, f32[16,16,256]{2,1,0:T(8,128)S(1)} %get-tuple-element.73.phase, ...), custom_call_target="tpu_custom_call" | custom-call | tf_op jit(solution)/shard_map/pallas_call | solution.py:592
  61.5 0.1 collective-permute-start.14
  61.6 1.7 %collective-permute-start.15 = (f32[144,128]{1,0:T(8,128)S(1)}, f32[144,128]{1,0:T(8,128)S(1)}, u32[]{:S(2)}, u32[]{:S(2)}) collective-permute-start(f32[144,128]{1,0:T(8,128)S(1)} %get-tuple-element.85), channel_id=1, source_target_pairs={{0,16},{8,24},{16,0},{24,8},{1,17},{9,25},{17,1},{25,9},{2,18},{10... | collective-permute-start | bytes 221192 | tf_op jit(solution)/shard_map/ppermute | solution.py:533
  63.2 2.7 %collective-permute-start.16 = (f32[144,128]{1,0:T(8,128)S(1)}, f32[144,128]{1,0:T(8,128)S(1)}, u32[]{:S(2)}, u32[]{:S(2)}) collective-permute-start(f32[144,128]{1,0:T(8,128)S(1)} %get-tuple-element.86), channel_id=1, source_target_pairs={{0,24},{8,16},{16,8},{24,0},{1,25},{9,17},{17,9},{25,1},{2,26},{10... | collective-permute-start | bytes 221192 | tf_op jit(solution)/shard_map/ppermute | solution.py:533
  65.9 0.7 shard_map.134
  66.6 0.5 shard_map.141
  67.1 0.0 collective-permute-done.14.rest_0_
  67.1 0.0 collective-permute-done.15.rest_1_
  67.1 2.3 %collective-permute-done.16.rest_2_ = f32[144,128]{1,0:T(8,128)S(1)} collective-permute-done((f32[144,128]{1,0:T(8,128)S(1)}, f32[144,128]{1,0:T(8,128)S(1)}, u32[]{:S(2)}, u32[]{:S(2)}) %collective-permute-start.16) | collective-permute-done | bytes 73760 | tf_op jit(solution)/shard_map/ppermute | solution.py:533
  69.4 1.7 %shard_map.142 = (f32[16,16,256]{2,1,0:T(8,128)}, f32[16,16,256]{2,1,0:T(8,128)}) custom-call(s32[8,128]{1,0:T(8,128)S(1)} %copy-done.10, f32[16,16,256]{2,1,0:T(8,128)S(1)} %get-tuple-element.81.phase, f32[16,16,256]{2,1,0:T(8,128)S(1)} %get-tuple-element.82.solute, f32[32,24,128]{2,1,0:T(8,128)S(1)} %get-tuple-element.83.own, ...), custom_call_target="tpu_custom_call" | custom-call | tf_op jit(solution)/shard_map/pallas_call | solution.py:600
  (15 shorter events, 0.1 us)
Async XLA Ops:
  0.6 2.2 %copy-start = (bf16[512,256]{1,0:T(8,128)(2,1)S(1)}, bf16[512,256]{1,0:T(8,128)(2,1)}, u32[]{:S(2)}) copy-start(bf16[512,256]{1,0:T(8,128)(2,1)} %constant.8.clone.picks) | copy-start | bytes 786436
  2.8 0.7 copy-start.10
  2.8 0.7 copy-start.11
  3.5 0.9 %copy-start.2 = (f32[1,1,1,16,16,256]{5,4,3,2,1,0:T(8,128)S(1)}, f32[1,1,1,16,16,256]{5,4,3,2,1,0:T(8,128)}, u32[]{:S(2)}) copy-start(f32[1,1,1,16,16,256]{5,4,3,2,1,0:T(8,128)} %param.13) | copy-start | bytes 786436
  4.5 0.9 %copy-start.7 = (f32[1,1,1,16,16,256]{5,4,3,2,1,0:T(8,128)S(1)}, f32[1,1,1,16,16,256]{5,4,3,2,1,0:T(8,128)}, u32[]{:S(2)}) copy-start(f32[1,1,1,16,16,256]{5,4,3,2,1,0:T(8,128)} %param.14) | copy-start | bytes 786436
  5.4 15.6 %copy-start.6 = (f32[8,32,128]{2,1,0:T(8,128)S(1)}, f32[8,32,128]{2,1,0:T(8,128)}, u32[]{:S(2)}) copy-start(f32[8,32,128]{2,1,0:T(8,128)} %k.3) | copy-start | bytes 393220
  6.4 14.6 %copy-start.5 = (f32[8,32,128]{2,1,0:T(8,128)S(1)}, f32[8,32,128]{2,1,0:T(8,128)}, u32[]{:S(2)}) copy-start(f32[8,32,128]{2,1,0:T(8,128)} %h.3) | copy-start | bytes 393220
  6.4 9.4 %collective-permute-start.1 = (f32[152,128]{1,0:T(8,128)S(1)}, f32[152,128]{1,0:T(8,128)S(1)}, u32[]{:S(2)}, u32[]{:S(2)}) collective-permute-start(f32[152,128]{1,0:T(8,128)S(1)} %get-tuple-element.49), channel_id=1, source_target_pairs={{0,16},{8,24},{16,0},{24,8},{1,17},{9,25},{17,1},{25,9},{2,18},{10... | collective-permute-start | bytes 233480 | tf_op jit(solution)/shard_map/ppermute | solution.py:533
  10.5 6.6 %collective-permute-start.2 = (f32[152,128]{1,0:T(8,128)S(1)}, f32[152,128]{1,0:T(8,128)S(1)}, u32[]{:S(2)}, u32[]{:S(2)}) collective-permute-start(f32[152,128]{1,0:T(8,128)S(1)} %get-tuple-element.50), channel_id=1, source_target_pairs={{0,24},{8,16},{16,8},{24,0},{1,25},{9,17},{17,9},{25,1},{2,26},{10... | collective-permute-start | bytes 233480 | tf_op jit(solution)/shard_map/ppermute | solution.py:533
  11.9 5.6 %collective-permute-start = (f32[152,128]{1,0:T(8,128)S(1)}, f32[152,128]{1,0:T(8,128)S(1)}, u32[]{:S(2)}, u32[]{:S(2)}) collective-permute-start(f32[152,128]{1,0:T(8,128)S(1)} %get-tuple-element.48._), channel_id=1, source_target_pairs={{0,8},{8,0},{16,24},{24,16},{1,9},{9,1},{17,25},{25,17},{2,10},{10... | collective-permute-start | bytes 233480 | tf_op jit(solution)/shard_map/ppermute | solution.py:533
  12.1 8.9 %all-to-all-start = ((f32[8,24,128]{2,1,0:T(8,128)}), f32[8,24,128]{2,1,0:T(8,128)S(1)}, u32[]{:S(2)}, u32[]{:S(2)}) async-start(f32[8,24,128]{2,1,0:T(8,128)} %get-tuple-element.51), calls=%async_computation | async-start | bytes 196608 | tf_op jit(solution)/shard_map/all_to_all | solution.py:530
  21.0 13.0 %copy-start.8 = (f32[1,1,1,16,16,256]{5,4,3,2,1,0:T(8,128)S(1)}, f32[1,1,1,16,16,256]{5,4,3,2,1,0:T(8,128)}, u32[]{:S(2)}) copy-start(f32[1,1,1,16,16,256]{5,4,3,2,1,0:T(8,128)} %param.14) | copy-start | bytes 786436
  21.1 13.0 %copy-start.3 = (f32[1,1,1,16,16,256]{5,4,3,2,1,0:T(8,128)S(1)}, f32[1,1,1,16,16,256]{5,4,3,2,1,0:T(8,128)}, u32[]{:S(2)}) copy-start(f32[1,1,1,16,16,256]{5,4,3,2,1,0:T(8,128)} %param.13) | copy-start | bytes 786436
  21.1 4.2 %collective-permute-start.3 = (f32[104,128]{1,0:T(8,128)S(1)}, f32[104,128]{1,0:T(8,128)S(1)}, u32[]{:S(2)}, u32[]{:S(2)}) collective-permute-start(f32[104,128]{1,0:T(8,128)S(1)} %get-tuple-element.52), channel_id=1, source_target_pairs={{0,8},{8,0},{16,24},{24,16},{1,9},{9,1},{17,25},{25,17},{2,10},{10... | collective-permute-start | bytes 159752 | tf_op jit(solution)/shard_map/ppermute | solution.py:533
  22.9 2.3 %collective-permute-start.4 = (f32[104,128]{1,0:T(8,128)S(1)}, f32[104,128]{1,0:T(8,128)S(1)}, u32[]{:S(2)}, u32[]{:S(2)}) collective-permute-start(f32[104,128]{1,0:T(8,128)S(1)} %get-tuple-element.53), channel_id=1, source_target_pairs={{0,0},{8,16},{16,8},{24,24},{1,1},{9,17},{17,9},{25,25},{2,2},{10,... | collective-permute-start | bytes 159752 | tf_op jit(solution)/shard_map/ppermute | solution.py:533
  23.6 10.5 %copy-start.4 = (bf16[256,256]{1,0:T(8,128)(2,1)S(1)}, bf16[256,256]{1,0:T(8,128)(2,1)}, u32[]{:S(2)}) copy-start(bf16[256,256]{1,0:T(8,128)(2,1)} %constant.9.clone.stencil) | copy-start | bytes 393220
  27.2 7.4 %collective-permute-start.5 = (f32[32,128]{1,0:T(8,128)S(1)}, f32[32,128]{1,0:T(8,128)S(1)}, u32[]{:S(2)}, u32[]{:S(2)}) collective-permute-start(f32[32,128]{1,0:T(8,128)S(1)} %get-tuple-element.59), channel_id=1, source_target_pairs={{0,8},{8,0},{16,24},{24,16},{1,9},{9,1},{17,25},{25,17},{2,10},{10... | collective-permute-start | bytes 49160 | tf_op jit(solution)/shard_map/ppermute | solution.py:533
  31.1 4.6 %collective-permute-start.6 = (f32[32,128]{1,0:T(8,128)S(1)}, f32[32,128]{1,0:T(8,128)S(1)}, u32[]{:S(2)}, u32[]{:S(2)}) collective-permute-start(f32[32,128]{1,0:T(8,128)S(1)} %get-tuple-element.60), channel_id=1, source_target_pairs={{0,16},{8,24},{16,0},{24,8},{1,17},{9,25},{17,1},{25,9},{2,18},{10... | collective-permute-start | bytes 49160 | tf_op jit(solution)/shard_map/ppermute | solution.py:533
  32.7 5.5 %copy-start.1 = (bf16[256,512]{1,0:T(8,128)(2,1)S(1)}, bf16[256,512]{1,0:T(8,128)(2,1)}, u32[]{:S(2)}) copy-start(bf16[256,512]{1,0:T(8,128)(2,1)} %constant.10.clone.places) | copy-start | bytes 786436
  32.7 5.5 %copy-start.9 = (bf16[256,256]{1,0:T(8,128)(2,1)S(1)}, bf16[256,256]{1,0:T(8,128)(2,1)}, u32[]{:S(2)}) copy-start(bf16[256,256]{1,0:T(8,128)(2,1)} %constant.11.clone.spreads) | copy-start | bytes 393220
  32.7 5.5 %collective-permute-start.7 = (f32[32,128]{1,0:T(8,128)S(1)}, f32[32,128]{1,0:T(8,128)S(1)}, u32[]{:S(2)}, u32[]{:S(2)}) collective-permute-start(f32[32,128]{1,0:T(8,128)S(1)} %get-tuple-element.61), channel_id=1, source_target_pairs={{0,24},{8,16},{16,8},{24,0},{1,25},{9,17},{17,9},{25,1},{2,26},{10... | collective-permute-start | bytes 49160 | tf_op jit(solution)/shard_map/ppermute | solution.py:533
  39.9 4.9 %collective-permute-start.8 = (f32[144,128]{1,0:T(8,128)S(1)}, f32[144,128]{1,0:T(8,128)S(1)}, u32[]{:S(2)}, u32[]{:S(2)}) collective-permute-start(f32[144,128]{1,0:T(8,128)S(1)} %get-tuple-element.68), channel_id=1, source_target_pairs={{0,8},{8,0},{16,24},{24,16},{1,9},{9,1},{17,25},{25,17},{2,10},{10... | collective-permute-start | bytes 221192 | tf_op jit(solution)/shard_map/ppermute | solution.py:533
  40.1 5.3 %collective-permute-start.9 = (f32[144,128]{1,0:T(8,128)S(1)}, f32[144,128]{1,0:T(8,128)S(1)}, u32[]{:S(2)}, u32[]{:S(2)}) collective-permute-start(f32[144,128]{1,0:T(8,128)S(1)} %get-tuple-element.69), channel_id=1, source_target_pairs={{0,16},{8,24},{16,0},{24,8},{1,17},{9,25},{17,1},{25,9},{2,18},{10... | collective-permute-start | bytes 221192 | tf_op jit(solution)/shard_map/ppermute | solution.py:533
  41.9 6.2 %collective-permute-start.10 = (f32[144,128]{1,0:T(8,128)S(1)}, f32[144,128]{1,0:T(8,128)S(1)}, u32[]{:S(2)}, u32[]{:S(2)}) collective-permute-start(f32[144,128]{1,0:T(8,128)S(1)} %get-tuple-element.70), channel_id=1, source_target_pairs={{0,24},{8,16},{16,8},{24,0},{1,25},{9,17},{17,9},{25,1},{2,26},{10... | collective-permute-start | bytes 221192 | tf_op jit(solution)/shard_map/ppermute | solution.py:533
  49.5 5.0 %collective-permute-start.11 = (f32[144,128]{1,0:T(8,128)S(1)}, f32[144,128]{1,0:T(8,128)S(1)}, u32[]{:S(2)}, u32[]{:S(2)}) collective-permute-start(f32[144,128]{1,0:T(8,128)S(1)} %get-tuple-element.76), channel_id=1, source_target_pairs={{0,8},{8,0},{16,24},{24,16},{1,9},{9,1},{17,25},{25,17},{2,10},{10... | collective-permute-start | bytes 221192 | tf_op jit(solution)/shard_map/ppermute | solution.py:533
  49.5 6.9 %collective-permute-start.12 = (f32[144,128]{1,0:T(8,128)S(1)}, f32[144,128]{1,0:T(8,128)S(1)}, u32[]{:S(2)}, u32[]{:S(2)}) collective-permute-start(f32[144,128]{1,0:T(8,128)S(1)} %get-tuple-element.77), channel_id=1, source_target_pairs={{0,16},{8,24},{16,0},{24,8},{1,17},{9,25},{17,1},{25,9},{2,18},{10... | collective-permute-start | bytes 221192 | tf_op jit(solution)/shard_map/ppermute | solution.py:533
  53.3 6.9 %collective-permute-start.13 = (f32[144,128]{1,0:T(8,128)S(1)}, f32[144,128]{1,0:T(8,128)S(1)}, u32[]{:S(2)}, u32[]{:S(2)}) collective-permute-start(f32[144,128]{1,0:T(8,128)S(1)} %get-tuple-element.78), channel_id=1, source_target_pairs={{0,24},{8,16},{16,8},{24,0},{1,25},{9,17},{17,9},{25,1},{2,26},{10... | collective-permute-start | bytes 221192 | tf_op jit(solution)/shard_map/ppermute | solution.py:533
  61.5 5.6 %collective-permute-start.14 = (f32[144,128]{1,0:T(8,128)S(1)}, f32[144,128]{1,0:T(8,128)S(1)}, u32[]{:S(2)}, u32[]{:S(2)}) collective-permute-start(f32[144,128]{1,0:T(8,128)S(1)} %get-tuple-element.84), channel_id=1, source_target_pairs={{0,8},{8,0},{16,24},{24,16},{1,9},{9,1},{17,25},{25,17},{2,10},{10... | collective-permute-start | bytes 221192 | tf_op jit(solution)/shard_map/ppermute | solution.py:533
  61.6 5.6 %collective-permute-start.15 = (f32[144,128]{1,0:T(8,128)S(1)}, f32[144,128]{1,0:T(8,128)S(1)}, u32[]{:S(2)}, u32[]{:S(2)}) collective-permute-start(f32[144,128]{1,0:T(8,128)S(1)} %get-tuple-element.85), channel_id=1, source_target_pairs={{0,16},{8,24},{16,0},{24,8},{1,17},{9,25},{17,1},{25,9},{2,18},{10... | collective-permute-start | bytes 221192 | tf_op jit(solution)/shard_map/ppermute | solution.py:533
  63.2 6.2 %collective-permute-start.16 = (f32[144,128]{1,0:T(8,128)S(1)}, f32[144,128]{1,0:T(8,128)S(1)}, u32[]{:S(2)}, u32[]{:S(2)}) collective-permute-start(f32[144,128]{1,0:T(8,128)S(1)} %get-tuple-element.86), channel_id=1, source_target_pairs={{0,24},{8,16},{16,8},{24,0},{1,25},{9,17},{17,9},{25,1},{2,26},{10... | collective-permute-start | bytes 221192 | tf_op jit(solution)/shard_map/ppermute | solution.py:533

commit v10 on v8

--- a/solution.py
+++ b/solution.py
@@ -247,10 +247,9 @@
     return h + RATE * k * (total - 6.0 * t)
 
 
-def heat_kernel(cap, sizes, request, h, k, got, low, high, *rest):
+def heat_kernel(cap, sizes, request, h, k, got, low, high, out, found, *rest):
+    *send, held = rest
     count = lax.axis_size("gx")
-    packed, (out, found, *send, held) = rest[: count - 1], rest[count - 1 :]
-
     bx, by, bz = h.shape
     h0, k0 = h[...], k[...]
     read = side_reader(sizes, got, bx)
@@ -307,12 +306,7 @@
                 moved = pltpu.roll(patch, (CB * at - CB * c + bz) % bz, 2)
                 total = jnp.where(group == at, moved, total)
         total = total.reshape(deep * CB, bz)
-        if shift == 0:
-            found[...] = total
-        else:
-            behind = packed[shift - 1].shape[0]
-            send[shift - 1][0:behind, :] = packed[shift - 1][...]
-            send[shift - 1][behind:, :] = total
+        (send[shift - 1] if shift else found)[...] = total
 
 
 def write_records(phase, solute, picks, own):
@@ -357,11 +351,10 @@
     pack(own, table, send)
 
 
-def take_heat(cap, table, found, got, spreads, blocks, held, heat):
+def take_heat(cap, table, found, spreads, blocks, held, heat):
     parts, deep = block_layout(cap)
-    blocks[0] = found[...]
-    for number, value in enumerate(got):
-        blocks[1 + number] = value[value.shape[0] - deep * CB :, :]
+    for number, value in enumerate(found):
+        blocks[number] = value[...]
     group = iota((CB, 128), 1) // CB
     for slot in range(SLOTS):
         back, rank = table[6, slot], table[7, slot]
@@ -440,12 +433,12 @@
     phase_out[...], solute_out[...] = inner_step(phase[...], solute[...], heat, stencil[...])
 
 
-def first_step_kernel(cap, table, old_phase, phase, solute, own, picks, places, spreads, found, *rest):
+def first_step_kernel(cap, table, old_phase, phase, solute, own, picks, places, spreads, *rest):
     others = lax.axis_size("gx") - 1
-    got, rest = rest[:others], rest[others:]
+    found, got, rest = rest[: others + 1], rest[others + 1 : 2 * others + 1], rest[2 * others + 1 :]
     phase_out, solute_out, heat_out, own_out, *rest = rest
     send, (all_records, ghosts, blocks, held) = rest[:others], rest[others:]
-    take_heat(cap, table, found, got, spreads[...], blocks, held, heat_out)
+    take_heat(cap, table, found, spreads[...], blocks, held, heat_out)
     gather_ghosts(table, got, own, all_records, ghosts)
     squared = 1.0 - old_phase[...] * old_phase[...]
     heat_share = (-ORDER_SPEED * COUPLING) * wide_heat(heat_out) * squared * squared
@@ -558,16 +551,16 @@
     request = jnp.stack([value[:block_cap] for value in request]).astype(jnp.int32)
     _, deep = block_layout(block_cap)
     brick = shape(bx, by, bz)
-    heated, found, *send = call(
+    got = exchange(packed)
+    heated, *found = call(
         functools.partial(heat_kernel, block_cap, sizes),
-        [SMEM] + [VMEM] * (5 + others),
-        [brick, shape(deep * CB, 128)] + [shape(plane_cap * REC + deep * CB, 128)] * others,
+        [SMEM] + [VMEM] * 5,
+        [brick] + [shape(deep * CB, 128)] * count,
         [pltpu.VMEM((bx, by // CB, CB, bz), F32)],
-    )(request, enthalpy, conductivity, sides, from_low, from_high, *packed)
-
+    )(request, enthalpy, conductivity, sides, from_low, from_high)
+    found[1:] = exchange(found[1:])
     (heat_out,) = call(write_out_kernel, [ANY], [brick], [pltpu.SemaphoreType.DMA], [ANY])(heated)
 
-    got = exchange(send)
     field = shape(SLOTS, TE, PLANE)
     step_scratch = [
         pltpu.VMEM((records + 2 * SLOTS, REC, 128), F32),
@@ -581,14 +574,14 @@
     inner_fields = inner(phase_field, solute_field)
     phase_field, solute_field, heat, own, *send = call(
         functools.partial(first_step_kernel, block_cap),
-        [SMEM] + [VMEM] * (8 + others),
+        [SMEM] + [VMEM] * (7 + count + others),
         [field, field, shape(2, SLOTS * TE, 128), own_shape, *send_shapes],
         step_scratch
         + [
             pltpu.VMEM((count, deep * CB, 128), F32),
             pltpu.VMEM((SLOTS * CB, CB, 128), F32),
         ],
-    )(table, phase_field, *inner_fields, own, picks, places, spreads, found, *got)
+    )(table, phase_field, *inner_fields, own, picks, places, spreads, *found, *got)
     for _ in range(PHASE_STEPS - 2):
         got = exchange(send)
         inner_fields = inner(phase_field, solute_field, heat)

time: 65.5 us -> 63.2 us (0.965)
  waiting for transfers between devices: 18.3 us -> 11.6 us
  starting transfers between devices: 29.1 us -> 33.3 us
    ppermute x15 -> x18, waiting for transfers between devices: 18.3 us -> 11.6 us  [pass_on(): lax.ppermute(value, 'gx', [(i, (i + shift) % count) for i in range(count)])]
    ppermute x15 -> x18, starting transfers between devices: 23.9 us -> 28.1 us  [pass_on(): lax.ppermute(value, 'gx', [(i, (i + shift) % count) for i in range(count)])]
  transfers between devices with their start and end apart: 16 -> 19, of which waited for: 10 -> 11; matrix products, arithmetic and copies ran while one was open for 1% -> 1% of each run, Pallas kernels for 6% -> 9%
where the time goes in v10:
time: 63.2 us; the launch traced here: 62.6 us
  starting transfers between devices  33.3 us (53%)
  Pallas kernels  13.6 us (22%)
  waiting for transfers between devices  11.6 us (18%)
  local copies, waits for them, and re-layouts  3.25 us (5%)
  between operations  0.86 us (1%)
    ppermute x18, starting transfers between devices, pass_on(): lax.ppermute(value, 'gx', [(i, (i + shift) % count) for i in range(count)])  28.1 us
    ppermute x18, waiting for transfers between devices, pass_on(): lax.ppermute(value, 'gx', [(i, (i + shift) % count) for i in range(count)])  11.6 us
    all_to_all x1, starting transfers between devices, local(): lax.all_to_all(sides, ('gy', 'gz'), split_axis=0, concat_axis=0, tiled=True)  5.18 us
    unnamed x28, local copies, waits for them, and re-layouts  2.56 us
    pallas_call x2, Pallas kernels, local(): call(middle_step_kernel, [SMEM] + [VMEM] * (5 + others), [field, field, o...  2.56 us
    pallas_call x1, Pallas kernels, local(): call(functools.partial(sides_kernel, sizes, plane_cap), [ANY] * 5, [shape...  2.17 us
    pallas_call x4, Pallas kernels, inner(): call(functools.partial(inner_kernel, bool(heat)), [VMEM] * (3 + len(heat)...  1.96 us
    pallas_call x1, Pallas kernels, local(): call(functools.partial(heat_kernel, block_cap, sizes), [SMEM] + [VMEM] *...  1.91 us
  transfers between devices with their start and end apart: 19, of which 11 were waited for; matrix products, arithmetic and copies ran while one was open for 1% of the time, Pallas kernels for 9%

profile of v10, /device:TPU:0, one launch (start us, length us, event | category | flops | bytes accessed | tf_op | source)
XLA Modules:
  0.0 62.6 jit_solution(12714828295631100960)
XLA Ops:
  0.6 0.0 copy-start
  0.6 2.2 %shard_map.130 = (f32[8,24,128]{2,1,0:T(8,128)}, s32[8,128]{1,0:T(8,128)}, f32[8,128]{1,0:T(8,128)}, f32[8,128]{1,0:T(8,128)}, f32[8,128]{1,0:T(8,128)}, /*index=5*/f32[8,128]{1,0:T(8,128)}) custom-call(s32[1,16]{1,0:T(1,128)} %bitcast.15, s32[1,16]{1,0:T(1,128)} %bitcast.16, s32[6,1,16]{2,1,0:T(1,128)} %bitcast.14, f32[8,32,128]{2,1,0:T(8,128)} %h.3, ...), custom_call_target="tpu_custom_call" | custom-call | tf_op jit(solution)/shard_map/pallas_call | solution.py:507
  2.8 0.0 copy-start.13
  2.8 5.2 %all-to-all-start = ((f32[8,24,128]{2,1,0:T(8,128)}), f32[8,24,128]{2,1,0:T(8,128)S(1)}, u32[]{:S(2)}, u32[]{:S(2)}) async-start(f32[8,24,128]{2,1,0:T(8,128)} %get-tuple-element.50), calls=%async_computation | async-start | bytes 196608 | tf_op jit(solution)/shard_map/all_to_all | solution.py:527
  8.0 0.0 copy-done.13
  8.0 2.7 %collective-permute-start = (f32[8,128]{1,0:T(8,128)S(1)}, f32[8,128]{1,0:T(8,128)S(1)}, u32[]{:S(2)}, u32[]{:S(2)}) collective-permute-start(f32[8,128]{1,0:T(8,128)S(1)} %copy-done.13), channel_id=1, source_target_pairs={{0,16},{8,24},{16,0},{24,8},{1,17},{9,25},{17,1},{25,9},{2,18},{10... | collective-permute-start | bytes 12296 | tf_op jit(solution)/shard_map/ppermute | solution.py:530
  10.7 0.0 copy-done
  10.7 0.0 copy-done.10
  10.7 0.9 %copy-done.2 = f32[1,1,1,16,16,256]{5,4,3,2,1,0:T(8,128)S(1)} copy-done((f32[1,1,1,16,16,256]{5,4,3,2,1,0:T(8,128)S(1)}, f32[1,1,1,16,16,256]{5,4,3,2,1,0:T(8,128)}, u32[]{:S(2)}) %copy-start.2) | copy-done | bytes 262168
  11.6 0.9 %copy-done.7 = f32[1,1,1,16,16,256]{5,4,3,2,1,0:T(8,128)S(1)} copy-done((f32[1,1,1,16,16,256]{5,4,3,2,1,0:T(8,128)S(1)}, f32[1,1,1,16,16,256]{5,4,3,2,1,0:T(8,128)}, u32[]{:S(2)}) %copy-start.7) | copy-done | bytes 262168
  12.6 1.0 %shard_map.131 = (f32[32,24,128]{2,1,0:T(8,128)S(1)}, f32[144,128]{1,0:T(8,128)S(1)}, f32[144,128]{1,0:T(8,128)S(1)}, f32[144,128]{1,0:T(8,128)S(1)}) custom-call(s32[8,128]{1,0:T(8,128)S(1)} %copy-done.10, f32[16,16,256]{2,1,0:T(8,128)S(1)} %bitcast.9, f32[16,16,256]{2,1,0:T(8,128)S(1)} %bitcast.12, bf16[512,256]{1,0:T(8,128)(2,1)S(1)} %copy-done), custom_call_target="tpu_custom_call" | custom-call | tf_op jit(solution)/shard_map/pallas_call | solution.py:540
  13.6 0.0 copy-start.11
  13.6 0.0 collective-permute-done.rest_1_
  13.6 0.0 all-to-all-done.got
  13.6 0.0 copy-done.5
  13.6 0.6 copy-done.11
  14.3 0.0 copy-start.3
  14.3 1.6 %collective-permute-start.1 = (f32[104,128]{1,0:T(8,128)S(1)}, f32[104,128]{1,0:T(8,128)S(1)}, u32[]{:S(2)}, u32[]{:S(2)}) collective-permute-start(f32[104,128]{1,0:T(8,128)S(1)} %get-tuple-element.56), channel_id=1, source_target_pairs={{0,8},{8,16},{16,24},{24,0},{1,9},{9,17},{17,25},{25,1},{2,10},{10... | collective-permute-start | bytes 159752 | tf_op jit(solution)/shard_map/ppermute | solution.py:530
  15.9 2.2 %collective-permute-start.2 = (f32[104,128]{1,0:T(8,128)S(1)}, f32[104,128]{1,0:T(8,128)S(1)}, u32[]{:S(2)}, u32[]{:S(2)}) collective-permute-start(f32[104,128]{1,0:T(8,128)S(1)} %get-tuple-element.57), channel_id=1, source_target_pairs={{0,24},{8,0},{16,8},{24,16},{1,25},{9,1},{17,9},{25,17},{2,26},{10... | collective-permute-start | bytes 159752 | tf_op jit(solution)/shard_map/ppermute | solution.py:530
  18.1 0.0 collective-permute-start.6
  18.2 1.4 %collective-permute-start.7 = (f32[144,128]{1,0:T(8,128)S(1)}, f32[144,128]{1,0:T(8,128)S(1)}, u32[]{:S(2)}, u32[]{:S(2)}) collective-permute-start(f32[144,128]{1,0:T(8,128)S(1)} %get-tuple-element.66), channel_id=1, source_target_pairs={{0,16},{8,24},{16,0},{24,8},{1,17},{9,25},{17,1},{25,9},{2,18},{10... | collective-permute-start | bytes 221192 | tf_op jit(solution)/shard_map/ppermute | solution.py:530
  19.5 2.4 %collective-permute-start.8 = (f32[144,128]{1,0:T(8,128)S(1)}, f32[144,128]{1,0:T(8,128)S(1)}, u32[]{:S(2)}, u32[]{:S(2)}) collective-permute-start(f32[144,128]{1,0:T(8,128)S(1)} %get-tuple-element.67), channel_id=1, source_target_pairs={{0,24},{8,0},{16,8},{24,16},{1,25},{9,1},{17,9},{25,17},{2,26},{10... | collective-permute-start | bytes 221192 | tf_op jit(solution)/shard_map/ppermute | solution.py:530
  22.0 0.7 %slice.24 = f32[1,8]{1,0:T(1,128)S(1)} slice(f32[8,128]{1,0:T(8,128)} %get-tuple-element.49), slice={[0:1], [0:8]} | slice | bytes 64 | tf_op jit(solution)/shard_map/slice | solution.py:551
  22.7 0.0 collective-permute-done.1.low
  22.7 0.0 collective-permute-done.2.high
  22.7 0.0 copy-start.4
  22.7 1.9 %shard_map.133 = (f32[8,32,128]{2,1,0:T(8,128)S(1)}, f32[32,128]{1,0:T(8,128)S(1)}, f32[32,128]{1,0:T(8,128)S(1)}, f32[32,128]{1,0:T(8,128)S(1)}, f32[32,128]{1,0:T(8,128)S(1)}) custom-call(s32[4,8]{1,0:T(4,128)S(1)} %maximum_convert_fusion.request, f32[8,32,128]{2,1,0:T(8,128)S(1)} %copy-done.5, f32[8,32,128]{2,1,0:T(8,128)S(1)} %copy-done.6, ...), custom_call_target="tpu_custom_call" | custom-call | tf_op jit(solution)/shard_map/pallas_call | solution.py:555
  24.6 0.6 collective-permute-start.3
  25.3 2.0 %collective-permute-start.4 = (f32[32,128]{1,0:T(8,128)S(1)}, f32[32,128]{1,0:T(8,128)S(1)}, u32[]{:S(2)}, u32[]{:S(2)}) collective-permute-start(f32[32,128]{1,0:T(8,128)S(1)} %get-tuple-element.64), channel_id=1, source_target_pairs={{0,16},{8,24},{16,0},{24,8},{1,17},{9,25},{17,1},{25,9},{2,18},{10... | collective-permute-start | bytes 49160 | tf_op jit(solution)/shard_map/ppermute | solution.py:530
  27.2 0.0 collective-permute-done.7.rest_5_
  27.2 2.4 %collective-permute-start.5 = (f32[32,128]{1,0:T(8,128)S(1)}, f32[32,128]{1,0:T(8,128)S(1)}, u32[]{:S(2)}, u32[]{:S(2)}) collective-permute-start(f32[32,128]{1,0:T(8,128)S(1)} %get-tuple-element.65), channel_id=1, source_target_pairs={{0,24},{8,0},{16,8},{24,16},{1,25},{9,1},{17,9},{25,17},{2,26},{10... | collective-permute-start | bytes 49160 | tf_op jit(solution)/shard_map/ppermute | solution.py:530
  29.6 0.0 copy-done.8
  29.7 0.5 shard_map.135
  30.1 0.0 collective-permute-done.8.rest_6_
  30.2 0.0 collective-permute-done.6.rest_4_
  30.2 0.1 collective-permute-done.3.rest_1_
  30.2 0.0 collective-permute-done.4.rest_2_
  30.2 0.9 %collective-permute-done.5.rest_3_ = f32[32,128]{1,0:T(8,128)S(1)} collective-permute-done((f32[32,128]{1,0:T(8,128)S(1)}, f32[32,128]{1,0:T(8,128)S(1)}, u32[]{:S(2)}, u32[]{:S(2)}) %collective-permute-start.5) | collective-permute-done | bytes 16416 | tf_op jit(solution)/shard_map/ppermute | solution.py:530
  31.1 1.7 %shard_map.136 = (f32[16,16,256]{2,1,0:T(8,128)S(1)}, f32[16,16,256]{2,1,0:T(8,128)S(1)}, f32[2,256,128]{2,1,0:T(8,128)S(1)}, f32[32,24,128]{2,1,0:T(8,128)S(1)}...) custom-call(s32[8,128]{1,0:T(8,128)S(1)} %copy-done.10, f32[16,16,256]{2,1,0:T(8,128)S(1)} %bitcast.11, ...), custom_call_target="tpu_custom_call" | custom-call | tf_op jit(solution)/shard_map/pallas_call | solution.py:575
  32.8 1.8 %collective-permute-start.9 = (f32[144,128]{1,0:T(8,128)S(1)}, f32[144,128]{1,0:T(8,128)S(1)}, u32[]{:S(2)}, u32[]{:S(2)}) collective-permute-start(f32[144,128]{1,0:T(8,128)S(1)} %get-tuple-element.74), channel_id=1, source_target_pairs={{0,8},{8,16},{16,24},{24,0},{1,9},{9,17},{17,25},{25,1},{2,10},{10... | collective-permute-start | bytes 221192 | tf_op jit(solution)/shard_map/ppermute | solution.py:530
  34.6 2.9 %collective-permute-start.10 = (f32[144,128]{1,0:T(8,128)S(1)}, f32[144,128]{1,0:T(8,128)S(1)}, u32[]{:S(2)}, u32[]{:S(2)}) collective-permute-start(f32[144,128]{1,0:T(8,128)S(1)} %get-tuple-element.75), channel_id=1, source_target_pairs={{0,16},{8,24},{16,0},{24,8},{1,17},{9,25},{17,1},{25,9},{2,18},{10... | collective-permute-start | bytes 221192 | tf_op jit(solution)/shard_map/ppermute | solution.py:530
  37.5 0.0 collective-permute-start.11
  37.5 0.5 shard_map.137
  38.0 1.4 %collective-permute-done.9.rest_0_ = f32[144,128]{1,0:T(8,128)S(1)} collective-permute-done((f32[144,128]{1,0:T(8,128)S(1)}, f32[144,128]{1,0:T(8,128)S(1)}, u32[]{:S(2)}, u32[]{:S(2)}) %collective-permute-start.9) | collective-permute-done | bytes 73760 | tf_op jit(solution)/shard_map/ppermute | solution.py:530
  39.4 1.8 %collective-permute-done.10.rest_1_ = f32[144,128]{1,0:T(8,128)S(1)} collective-permute-done((f32[144,128]{1,0:T(8,128)S(1)}, f32[144,128]{1,0:T(8,128)S(1)}, u32[]{:S(2)}, u32[]{:S(2)}) %collective-permute-start.10) | collective-permute-done | bytes 73760 | tf_op jit(solution)/shard_map/ppermute | solution.py:530
  41.2 0.8 %collective-permute-done.11.rest_2_ = f32[144,128]{1,0:T(8,128)S(1)} collective-permute-done((f32[144,128]{1,0:T(8,128)S(1)}, f32[144,128]{1,0:T(8,128)S(1)}, u32[]{:S(2)}, u32[]{:S(2)}) %collective-permute-start.11) | collective-permute-done | bytes 73760 | tf_op jit(solution)/shard_map/ppermute | solution.py:530
  42.0 1.3 %shard_map.138 = (f32[16,16,256]{2,1,0:T(8,128)S(1)}, f32[16,16,256]{2,1,0:T(8,128)S(1)}, f32[32,24,128]{2,1,0:T(8,128)S(1)}, f32[144,128]{1,0:T(8,128)S(1)}, f3...) custom-call(s32[8,128]{1,0:T(8,128)S(1)} %copy-done.10, f32[16,16,256]{2,1,0:T(8,128)S(1)} %get-tuple-element.71.phase, ...), custom_call_target="tpu_custom_call" | custom-call | tf_op jit(solution)/shard_map/pallas_call | solution.py:588
  43.3 0.6 collective-permute-start.12
  43.9 2.4 %collective-permute-start.13 = (f32[144,128]{1,0:T(8,128)S(1)}, f32[144,128]{1,0:T(8,128)S(1)}, u32[]{:S(2)}, u32[]{:S(2)}) collective-permute-start(f32[144,128]{1,0:T(8,128)S(1)} %get-tuple-element.83), channel_id=1, source_target_pairs={{0,16},{8,24},{16,0},{24,8},{1,17},{9,25},{17,1},{25,9},{2,18},{10... | collective-permute-start | bytes 221192 | tf_op jit(solution)/shard_map/ppermute | solution.py:530
  46.4 0.8 %collective-permute-start.14 = (f32[144,128]{1,0:T(8,128)S(1)}, f32[144,128]{1,0:T(8,128)S(1)}, u32[]{:S(2)}, u32[]{:S(2)}) collective-permute-start(f32[144,128]{1,0:T(8,128)S(1)} %get-tuple-element.84), channel_id=1, source_target_pairs={{0,24},{8,0},{16,8},{24,16},{1,25},{9,1},{17,9},{25,17},{2,26},{10... | collective-permute-start | bytes 221192 | tf_op jit(solution)/shard_map/ppermute | solution.py:530
  47.2 0.5 shard_map.139
  47.7 1.9 %collective-permute-done.12.rest_0_ = f32[144,128]{1,0:T(8,128)S(1)} collective-permute-done((f32[144,128]{1,0:T(8,128)S(1)}, f32[144,128]{1,0:T(8,128)S(1)}, u32[]{:S(2)}, u32[]{:S(2)}) %collective-permute-start.12) | collective-permute-done | bytes 73760 | tf_op jit(solution)/shard_map/ppermute | solution.py:530
  49.6 1.3 %collective-permute-done.13.rest_1_ = f32[144,128]{1,0:T(8,128)S(1)} collective-permute-done((f32[144,128]{1,0:T(8,128)S(1)}, f32[144,128]{1,0:T(8,128)S(1)}, u32[]{:S(2)}, u32[]{:S(2)}) %collective-permute-start.13) | collective-permute-done | bytes 73760 | tf_op jit(solution)/shard_map/ppermute | solution.py:530
  50.9 0.2 collective-permute-done.14.rest_2_
  51.1 1.3 %shard_map.140 = (f32[16,16,256]{2,1,0:T(8,128)S(1)}, f32[16,16,256]{2,1,0:T(8,128)S(1)}, f32[32,24,128]{2,1,0:T(8,128)S(1)}, f32[144,128]{1,0:T(8,128)S(1)}, f3...) custom-call(s32[8,128]{1,0:T(8,128)S(1)} %copy-done.10, f32[16,16,256]{2,1,0:T(8,128)S(1)} %get-tuple-element.79.phase, ...), custom_call_target="tpu_custom_call" | custom-call | tf_op jit(solution)/shard_map/pallas_call | solution.py:588
  52.4 1.1 %collective-permute-start.15 = (f32[144,128]{1,0:T(8,128)S(1)}, f32[144,128]{1,0:T(8,128)S(1)}, u32[]{:S(2)}, u32[]{:S(2)}) collective-permute-start(f32[144,128]{1,0:T(8,128)S(1)} %get-tuple-element.90), channel_id=1, source_target_pairs={{0,8},{8,16},{16,24},{24,0},{1,9},{9,17},{17,25},{25,1},{2,10},{10... | collective-permute-start | bytes 221192 | tf_op jit(solution)/shard_map/ppermute | solution.py:530
  53.4 3.1 %collective-permute-start.16 = (f32[144,128]{1,0:T(8,128)S(1)}, f32[144,128]{1,0:T(8,128)S(1)}, u32[]{:S(2)}, u32[]{:S(2)}) collective-permute-start(f32[144,128]{1,0:T(8,128)S(1)} %get-tuple-element.91), channel_id=1, source_target_pairs={{0,16},{8,24},{16,0},{24,8},{1,17},{9,25},{17,1},{25,9},{2,18},{10... | collective-permute-start | bytes 221192 | tf_op jit(solution)/shard_map/ppermute | solution.py:530
  56.5 0.0 collective-permute-start.17
  56.5 0.7 %shard_map.134 = f32[8,32,128]{2,1,0:T(8,128)} custom-call(f32[8,32,128]{2,1,0:T(8,128)S(1)} %get-tuple-element.58.value), custom_call_target="tpu_custom_call" | custom-call | tf_op jit(solution)/shard_map/pallas_call | solution.py:562
  57.2 0.5 shard_map.141
  57.7 0.9 %collective-permute-done.15.rest_0_ = f32[144,128]{1,0:T(8,128)S(1)} collective-permute-done((f32[144,128]{1,0:T(8,128)S(1)}, f32[144,128]{1,0:T(8,128)S(1)}, u32[]{:S(2)}, u32[]{:S(2)}) %collective-permute-start.15) | collective-permute-done | bytes 73760 | tf_op jit(solution)/shard_map/ppermute | solution.py:530
  58.6 1.5 %collective-permute-done.16.rest_1_ = f32[144,128]{1,0:T(8,128)S(1)} collective-permute-done((f32[144,128]{1,0:T(8,128)S(1)}, f32[144,128]{1,0:T(8,128)S(1)}, u32[]{:S(2)}, u32[]{:S(2)}) %collective-permute-start.16) | collective-permute-done | bytes 73760 | tf_op jit(solution)/shard_map/ppermute | solution.py:530
  60.1 0.8 %collective-permute-done.17.rest_2_ = f32[144,128]{1,0:T(8,128)S(1)} collective-permute-done((f32[144,128]{1,0:T(8,128)S(1)}, f32[144,128]{1,0:T(8,128)S(1)}, u32[]{:S(2)}, u32[]{:S(2)}) %collective-permute-start.17) | collective-permute-done | bytes 73760 | tf_op jit(solution)/shard_map/ppermute | solution.py:530
  60.9 1.7 %shard_map.142 = (f32[16,16,256]{2,1,0:T(8,128)}, f32[16,16,256]{2,1,0:T(8,128)}) custom-call(s32[8,128]{1,0:T(8,128)S(1)} %copy-done.10, f32[16,16,256]{2,1,0:T(8,128)S(1)} %get-tuple-element.87.phase, f32[16,16,256]{2,1,0:T(8,128)S(1)} %get-tuple-element.88.solute, f32[32,24,128]{2,1,0:T(8,128)S(1)} %get-tuple-element.89.own, ...), custom_call_target="tpu_custom_call" | custom-call | tf_op jit(solution)/shard_map/pallas_call | solution.py:596
  (20 shorter events, 0.1 us)
Async XLA Ops:
  0.6 10.1 %copy-start = (bf16[512,256]{1,0:T(8,128)(2,1)S(1)}, bf16[512,256]{1,0:T(8,128)(2,1)}, u32[]{:S(2)}) copy-start(bf16[512,256]{1,0:T(8,128)(2,1)} %constant.8.clone.picks) | copy-start | bytes 786436
  2.8 5.2 %copy-start.13 = (f32[8,128]{1,0:T(8,128)S(1)}, f32[8,128]{1,0:T(8,128)}, u32[]{:S(2)}) copy-start(f32[8,128]{1,0:T(8,128)} %get-tuple-element.55) | copy-start | bytes 12292
  2.8 10.8 %all-to-all-start = ((f32[8,24,128]{2,1,0:T(8,128)}), f32[8,24,128]{2,1,0:T(8,128)S(1)}, u32[]{:S(2)}, u32[]{:S(2)}) async-start(f32[8,24,128]{2,1,0:T(8,128)} %get-tuple-element.50), calls=%async_computation | async-start | bytes 196608 | tf_op jit(solution)/shard_map/all_to_all | solution.py:527
  8.0 2.7 %copy-start.10 = (s32[8,128]{1,0:T(8,128)S(1)}, s32[8,128]{1,0:T(8,128)}, u32[]{:S(2)}) copy-start(s32[8,128]{1,0:T(8,128)} %get-tuple-element.53.table) | copy-start | bytes 12292
  8.0 5.6 %collective-permute-start = (f32[8,128]{1,0:T(8,128)S(1)}, f32[8,128]{1,0:T(8,128)S(1)}, u32[]{:S(2)}, u32[]{:S(2)}) collective-permute-start(f32[8,128]{1,0:T(8,128)S(1)} %copy-done.13), channel_id=1, source_target_pairs={{0,16},{8,24},{16,0},{24,8},{1,17},{9,25},{17,1},{25,9},{2,18},{10... | collective-permute-start | bytes 12296 | tf_op jit(solution)/shard_map/ppermute | solution.py:530
  10.7 1.0 %copy-start.2 = (f32[1,1,1,16,16,256]{5,4,3,2,1,0:T(8,128)S(1)}, f32[1,1,1,16,16,256]{5,4,3,2,1,0:T(8,128)}, u32[]{:S(2)}) copy-start(f32[1,1,1,16,16,256]{5,4,3,2,1,0:T(8,128)} %param.13) | copy-start | bytes 786436
  11.6 0.9 %copy-start.7 = (f32[1,1,1,16,16,256]{5,4,3,2,1,0:T(8,128)S(1)}, f32[1,1,1,16,16,256]{5,4,3,2,1,0:T(8,128)}, u32[]{:S(2)}) copy-start(f32[1,1,1,16,16,256]{5,4,3,2,1,0:T(8,128)} %param.14) | copy-start | bytes 786436
  12.6 1.0 %copy-start.5 = (f32[8,32,128]{2,1,0:T(8,128)S(1)}, f32[8,32,128]{2,1,0:T(8,128)}, u32[]{:S(2)}) copy-start(f32[8,32,128]{2,1,0:T(8,128)} %h.3) | copy-start | bytes 393220
  12.6 1.0 %copy-start.6 = (f32[8,32,128]{2,1,0:T(8,128)S(1)}, f32[8,32,128]{2,1,0:T(8,128)}, u32[]{:S(2)}) copy-start(f32[8,32,128]{2,1,0:T(8,128)} %k.3) | copy-start | bytes 393220
  12.6 1.0 %copy-start.12 = (f32[8,128]{1,0:T(8,128)S(1)}, f32[8,128]{1,0:T(8,128)}, u32[]{:S(2)}) copy-start(f32[8,128]{1,0:T(8,128)} %get-tuple-element.52.ask_down) | copy-start | bytes 12292
  13.6 0.7 %copy-start.11 = (f32[8,128]{1,0:T(8,128)S(1)}, f32[8,128]{1,0:T(8,128)}, u32[]{:S(2)}) copy-start(f32[8,128]{1,0:T(8,128)} %get-tuple-element.51.ask_up) | copy-start | bytes 12292
  14.2 15.4 %copy-start.8 = (f32[1,1,1,16,16,256]{5,4,3,2,1,0:T(8,128)S(1)}, f32[1,1,1,16,16,256]{5,4,3,2,1,0:T(8,128)}, u32[]{:S(2)}) copy-start(f32[1,1,1,16,16,256]{5,4,3,2,1,0:T(8,128)} %param.14) | copy-start | bytes 786436
  14.3 15.4 %copy-start.3 = (f32[1,1,1,16,16,256]{5,4,3,2,1,0:T(8,128)S(1)}, f32[1,1,1,16,16,256]{5,4,3,2,1,0:T(8,128)}, u32[]{:S(2)}) copy-start(f32[1,1,1,16,16,256]{5,4,3,2,1,0:T(8,128)} %param.13) | copy-start | bytes 786436
  14.3 8.4 %collective-permute-start.1 = (f32[104,128]{1,0:T(8,128)S(1)}, f32[104,128]{1,0:T(8,128)S(1)}, u32[]{:S(2)}, u32[]{:S(2)}) collective-permute-start(f32[104,128]{1,0:T(8,128)S(1)} %get-tuple-element.56), channel_id=1, source_target_pairs={{0,8},{8,16},{16,24},{24,0},{1,9},{9,17},{17,25},{25,1},{2,10},{10... | collective-permute-start | bytes 159752 | tf_op jit(solution)/shard_map/ppermute | solution.py:530
  15.9 6.8 %collective-permute-start.2 = (f32[104,128]{1,0:T(8,128)S(1)}, f32[104,128]{1,0:T(8,128)S(1)}, u32[]{:S(2)}, u32[]{:S(2)}) collective-permute-start(f32[104,128]{1,0:T(8,128)S(1)} %get-tuple-element.57), channel_id=1, source_target_pairs={{0,24},{8,0},{16,8},{24,16},{1,25},{9,1},{17,9},{25,17},{2,26},{10... | collective-permute-start | bytes 159752 | tf_op jit(solution)/shard_map/ppermute | solution.py:530
  18.1 12.0 %collective-permute-start.6 = (f32[144,128]{1,0:T(8,128)S(1)}, f32[144,128]{1,0:T(8,128)S(1)}, u32[]{:S(2)}, u32[]{:S(2)}) collective-permute-start(f32[144,128]{1,0:T(8,128)S(1)} %get-tuple-element.54.rest_0_), channel_id=1, source_target_pairs={{0,8},{8,16},{16,24},{24,0},{1,9},{9,17},{17,25},{25,1},{2,10},{10... | collective-permute-start | bytes 221192 | tf_op jit(solution)/shard_map/ppermute | solution.py:530
  18.2 9.1 %collective-permute-start.7 = (f32[144,128]{1,0:T(8,128)S(1)}, f32[144,128]{1,0:T(8,128)S(1)}, u32[]{:S(2)}, u32[]{:S(2)}) collective-permute-start(f32[144,128]{1,0:T(8,128)S(1)} %get-tuple-element.66), channel_id=1, source_target_pairs={{0,16},{8,24},{16,0},{24,8},{1,17},{9,25},{17,1},{25,9},{2,18},{10... | collective-permute-start | bytes 221192 | tf_op jit(solution)/shard_map/ppermute | solution.py:530
  19.5 10.6 %collective-permute-start.8 = (f32[144,128]{1,0:T(8,128)S(1)}, f32[144,128]{1,0:T(8,128)S(1)}, u32[]{:S(2)}, u32[]{:S(2)}) collective-permute-start(f32[144,128]{1,0:T(8,128)S(1)} %get-tuple-element.67), channel_id=1, source_target_pairs={{0,24},{8,0},{16,8},{24,16},{1,25},{9,1},{17,9},{25,17},{2,26},{10... | collective-permute-start | bytes 221192 | tf_op jit(solution)/shard_map/ppermute | solution.py:530
  22.7 6.9 %copy-start.4 = (bf16[256,256]{1,0:T(8,128)(2,1)S(1)}, bf16[256,256]{1,0:T(8,128)(2,1)}, u32[]{:S(2)}) copy-start(bf16[256,256]{1,0:T(8,128)(2,1)} %constant.9.clone.stencil) | copy-start | bytes 393220
  24.6 5.6 %collective-permute-start.3 = (f32[32,128]{1,0:T(8,128)S(1)}, f32[32,128]{1,0:T(8,128)S(1)}, u32[]{:S(2)}, u32[]{:S(2)}) collective-permute-start(f32[32,128]{1,0:T(8,128)S(1)} %get-tuple-element.63), channel_id=1, source_target_pairs={{0,8},{8,16},{16,24},{24,0},{1,9},{9,17},{17,25},{25,1},{2,10},{10... | collective-permute-start | bytes 49160 | tf_op jit(solution)/shard_map/ppermute | solution.py:530
  25.3 5.0 %collective-permute-start.4 = (f32[32,128]{1,0:T(8,128)S(1)}, f32[32,128]{1,0:T(8,128)S(1)}, u32[]{:S(2)}, u32[]{:S(2)}) collective-permute-start(f32[32,128]{1,0:T(8,128)S(1)} %get-tuple-element.64), channel_id=1, source_target_pairs={{0,16},{8,24},{16,0},{24,8},{1,17},{9,25},{17,1},{25,9},{2,18},{10... | collective-permute-start | bytes 49160 | tf_op jit(solution)/shard_map/ppermute | solution.py:530
  27.2 3.9 %copy-start.1 = (bf16[256,512]{1,0:T(8,128)(2,1)S(1)}, bf16[256,512]{1,0:T(8,128)(2,1)}, u32[]{:S(2)}) copy-start(bf16[256,512]{1,0:T(8,128)(2,1)} %constant.10.clone.places) | copy-start | bytes 786436
  27.2 3.9 %copy-start.9 = (bf16[256,256]{1,0:T(8,128)(2,1)S(1)}, bf16[256,256]{1,0:T(8,128)(2,1)}, u32[]{:S(2)}) copy-start(bf16[256,256]{1,0:T(8,128)(2,1)} %constant.11.clone.spreads) | copy-start | bytes 393220
  27.2 3.9 %collective-permute-start.5 = (f32[32,128]{1,0:T(8,128)S(1)}, f32[32,128]{1,0:T(8,128)S(1)}, u32[]{:S(2)}, u32[]{:S(2)}) collective-permute-start(f32[32,128]{1,0:T(8,128)S(1)} %get-tuple-element.65), channel_id=1, source_target_pairs={{0,24},{8,0},{16,8},{24,16},{1,25},{9,1},{17,9},{25,17},{2,26},{10... | collective-permute-start | bytes 49160 | tf_op jit(solution)/shard_map/ppermute | solution.py:530
  32.8 6.6 %collective-permute-start.9 = (f32[144,128]{1,0:T(8,128)S(1)}, f32[144,128]{1,0:T(8,128)S(1)}, u32[]{:S(2)}, u32[]{:S(2)}) collective-permute-start(f32[144,128]{1,0:T(8,128)S(1)} %get-tuple-element.74), channel_id=1, source_target_pairs={{0,8},{8,16},{16,24},{24,0},{1,9},{9,17},{17,25},{25,1},{2,10},{10... | collective-permute-start | bytes 221192 | tf_op jit(solution)/shard_map/ppermute | solution.py:530
  34.6 6.7 %collective-permute-start.10 = (f32[144,128]{1,0:T(8,128)S(1)}, f32[144,128]{1,0:T(8,128)S(1)}, u32[]{:S(2)}, u32[]{:S(2)}) collective-permute-start(f32[144,128]{1,0:T(8,128)S(1)} %get-tuple-element.75), channel_id=1, source_target_pairs={{0,16},{8,24},{16,0},{24,8},{1,17},{9,25},{17,1},{25,9},{2,18},{10... | collective-permute-start | bytes 221192 | tf_op jit(solution)/shard_map/ppermute | solution.py:530
  37.5 4.5 %collective-permute-start.11 = (f32[144,128]{1,0:T(8,128)S(1)}, f32[144,128]{1,0:T(8,128)S(1)}, u32[]{:S(2)}, u32[]{:S(2)}) collective-permute-start(f32[144,128]{1,0:T(8,128)S(1)} %get-tuple-element.76), channel_id=1, source_target_pairs={{0,24},{8,0},{16,8},{24,16},{1,25},{9,1},{17,9},{25,17},{2,26},{10... | collective-permute-start | bytes 221192 | tf_op jit(solution)/shard_map/ppermute | solution.py:530
  43.3 6.3 %collective-permute-start.12 = (f32[144,128]{1,0:T(8,128)S(1)}, f32[144,128]{1,0:T(8,128)S(1)}, u32[]{:S(2)}, u32[]{:S(2)}) collective-permute-start(f32[144,128]{1,0:T(8,128)S(1)} %get-tuple-element.82), channel_id=1, source_target_pairs={{0,8},{8,16},{16,24},{24,0},{1,9},{9,17},{17,25},{25,1},{2,10},{10... | collective-permute-start | bytes 221192 | tf_op jit(solution)/shard_map/ppermute | solution.py:530
  43.9 6.9 %collective-permute-start.13 = (f32[144,128]{1,0:T(8,128)S(1)}, f32[144,128]{1,0:T(8,128)S(1)}, u32[]{:S(2)}, u32[]{:S(2)}) collective-permute-start(f32[144,128]{1,0:T(8,128)S(1)} %get-tuple-element.83), channel_id=1, source_target_pairs={{0,16},{8,24},{16,0},{24,8},{1,17},{9,25},{17,1},{25,9},{2,18},{10... | collective-permute-start | bytes 221192 | tf_op jit(solution)/shard_map/ppermute | solution.py:530
  46.4 4.7 %collective-permute-start.14 = (f32[144,128]{1,0:T(8,128)S(1)}, f32[144,128]{1,0:T(8,128)S(1)}, u32[]{:S(2)}, u32[]{:S(2)}) collective-permute-start(f32[144,128]{1,0:T(8,128)S(1)} %get-tuple-element.84), channel_id=1, source_target_pairs={{0,24},{8,0},{16,8},{24,16},{1,25},{9,1},{17,9},{25,17},{2,26},{10... | collective-permute-start | bytes 221192 | tf_op jit(solution)/shard_map/ppermute | solution.py:530
  52.4 6.3 %collective-permute-start.15 = (f32[144,128]{1,0:T(8,128)S(1)}, f32[144,128]{1,0:T(8,128)S(1)}, u32[]{:S(2)}, u32[]{:S(2)}) collective-permute-start(f32[144,128]{1,0:T(8,128)S(1)} %get-tuple-element.90), channel_id=1, source_target_pairs={{0,8},{8,16},{16,24},{24,0},{1,9},{9,17},{17,25},{25,1},{2,10},{10... | collective-permute-start | bytes 221192 | tf_op jit(solution)/shard_map/ppermute | solution.py:530
  53.4 6.7 %collective-permute-start.16 = (f32[144,128]{1,0:T(8,128)S(1)}, f32[144,128]{1,0:T(8,128)S(1)}, u32[]{:S(2)}, u32[]{:S(2)}) collective-permute-start(f32[144,128]{1,0:T(8,128)S(1)} %get-tuple-element.91), channel_id=1, source_target_pairs={{0,16},{8,24},{16,0},{24,8},{1,17},{9,25},{17,1},{25,9},{2,18},{10... | collective-permute-start | bytes 221192 | tf_op jit(solution)/shard_map/ppermute | solution.py:530
  56.5 4.4 %collective-permute-start.17 = (f32[144,128]{1,0:T(8,128)S(1)}, f32[144,128]{1,0:T(8,128)S(1)}, u32[]{:S(2)}, u32[]{:S(2)}) collective-permute-start(f32[144,128]{1,0:T(8,128)S(1)} %get-tuple-element.92), channel_id=1, source_target_pairs={{0,24},{8,0},{16,8},{24,16},{1,25},{9,1},{17,9},{25,17},{2,26},{10... | collective-permute-start | bytes 221192 | tf_op jit(solution)/shard_map/ppermute | solution.py:530

commit v11 on v10

--- a/solution.py
+++ b/solution.py
@@ -125,9 +125,9 @@
     return jnp.sum(jnp.where(iota(square, 0) == iota(square, 1), row, 0.0), axis=1, keepdims=True)
 
 
-def write_tables(plane_cap, source, block, neighbour, asked, table):
+def write_tables(plane_cap, source, block, neighbour, table, farther):
     me = lax.axis_index("gx").astype(F32)
-    count = len(asked)
+    count = lax.axis_size("gx")
     records = (count - 1) * plane_cap
     cap = float(plane_cap)
 
@@ -147,7 +147,9 @@
     for shift in range(count):
         hit = (wrapped(source_column - me) == float(shift)) & (rank_column == lane)
         row = jnp.sum(jnp.where(hit, block_column, 0.0), axis=0, keepdims=True)
-        asked[shift][...] = jnp.broadcast_to(row, asked[shift].shape)
+        table[8 + shift : 9 + shift, :] = row.astype(jnp.int32)
+        if 2 <= shift < count - 1:
+            farther[shift - 2][...] = jnp.broadcast_to(row, (8, 128))
     table[6:7, 0:SLOTS] = wrapped(me - source_row).astype(jnp.int32)
     table[7:8, 0:SLOTS] = rank.astype(jnp.int32)
     slot_column = iota((SLOTS, records), 0).astype(F32)
@@ -173,23 +175,21 @@
 
 
 def sides_kernel(
-    sizes, plane_cap, source_far, block_far, neighbour_far, h_far, k_far, send, table, *rest
+    sizes, plane_cap, source_far, block_far, neighbour_far, h_far, k_far, send_far, table, *rest
 ):
-    *asked, source, block, neighbour, h, k, sems = rest
+    *farther, source, block, neighbour, h, k, send, sems = rest
     ny, nz = sizes
     my_y, my_z = lax.axis_index("gy"), lax.axis_index("gz")
     bx = h.shape[0]
     small = [(source_far, source), (block_far, block), (neighbour_far, neighbour)]
     copies = [pltpu.make_async_copy(*pair, sems.at[2 * bx + n]) for n, pair in enumerate(small)]
+    out = pltpu.make_async_copy(send, send_far, sems.at[2 * bx + 3])
     large = []
     for x in range(bx):
         large.append(pltpu.make_async_copy(h_far.at[x], h.at[x], sems.at[x]))
         large.append(pltpu.make_async_copy(k_far.at[x], k.at[x], sems.at[bx + x]))
     for copy in copies + large:
         copy.start()
-    for copy in copies:
-        copy.wait()
-    write_tables(plane_cap, source, block, neighbour, asked, table)
     for copy in large:
         copy.wait()
     blocks = side_blocks(h[...], k[...])
@@ -201,6 +201,11 @@
                     my_y == y, jnp.where(z < my_z, zlo, zhi), jnp.where(y < my_y, ylo, yhi)
                 )
                 send[y * nz + z, part * bx : part * bx + bx, :] = chosen
+    out.start()
+    for copy in copies:
+        copy.wait()
+    write_tables(plane_cap, source, block, neighbour, table, farther)
+    out.wait()
 
 
 def side_reader(sizes, got, bx):
@@ -216,18 +221,20 @@
     return read
 
 
-def layers_kernel(sizes, h, k, got, ask_up, ask_down, *rest):
+def layers_kernel(sizes, h, k, got, table, *rest):
     down, up = rest[-2:]
     bx, by, bz = h.shape
     read = side_reader(sizes, got, bx)
     around = [read(-1, 0), read(1, 0), read(0, -1), read(0, 1)]
-    for out, near, far, ask in ((down, 0, 1, ask_down), (up, bx - 1, bx - 2, ask_up)):
+    down_ask = 7 + lax.axis_size("gx")
+    for out, near, far, ask in ((down, 0, 1, down_ask), (up, bx - 1, bx - 2, 9)):
         out[0:by, :] = h[near]
         out[by : 2 * by, :] = h[far]
         out[2 * by : 3 * by, :] = k[near]
         for number, side in enumerate(around):
             out[3 * by + number : 3 * by + number + 1, :] = side[near : near + 1, :]
-        out[3 * by + 4 : 3 * by + 8, :] = ask[0:4, :]
+        row = table[ask : ask + 1, :].astype(F32)
+        out[3 * by + 4 : 3 * by + 8, :] = jnp.broadcast_to(row, (4, bz))
 
 
 def block_layout(cap):
@@ -247,7 +254,7 @@
     return h + RATE * k * (total - 6.0 * t)
 
 
-def heat_kernel(cap, sizes, request, h, k, got, low, high, out, found, *rest):
+def heat_kernel(cap, sizes, table, request, h, k, got, low, high, out, found, *rest):
     *send, held = rest
     count = lax.axis_size("gx")
     bx, by, bz = h.shape
@@ -298,7 +305,7 @@
     for shift in range(count):
         total = jnp.zeros((deep, CB, bz), F32)
         for rank in range(cap):
-            block = request[(count - shift) % count, rank]
+            block = request[count - shift - 1, rank] if shift else table[8, rank]
             a, b, c = block // (nby * nbz), (block // nbz) % nby, block % nbz
             for part in range(parts):
                 at = rank * parts + part
@@ -471,11 +478,24 @@
 
 def last_step_kernel(table, phase, solute, own, places, *rest):
     others = lax.axis_size("gx") - 1
-    got, (phase_out, solute_out, all_records, ghosts) = rest[:others], rest[others:]
+    got, (phase_far, solute_far, all_records, ghosts, phase_out, solute_out, sems) = (
+        rest[:others], rest[others:]
+    )
     gather_ghosts(table, got, own, all_records, ghosts)
-    phase_out[...], solute_out[...] = add_shares(
-        phase[...], solute[...], ghost_shares(ghosts, places[...])
-    )
+    shares = ghost_shares(ghosts, places[...])
+    copies = []
+    for piece in range(4):
+        at = pl.ds(piece * SLOTS // 4, SLOTS // 4)
+        part = slice(piece * SLOTS // 4, (piece + 1) * SLOTS // 4)
+        phase_out[at], solute_out[at] = add_shares(
+            phase[at], solute[at], [share[part] for share in shares]
+        )
+        for number, (out, far) in enumerate(((phase_out, phase_far), (solute_out, solute_far))):
+            copy = pltpu.make_async_copy(out.at[at], far.at[at], sems.at[2 * piece + number])
+            copy.start()
+            copies.append(copy)
+    for copy in copies:
+        copy.wait()
 
 
 def call(kernel, in_specs, out_shapes, scratch=(), out_specs=None, mib=16):
@@ -504,18 +524,20 @@
     picks, stencil, places, spreads = tables()
 
     integers = functools.partial(jax.ShapeDtypeStruct, dtype=jnp.int32)
-    sides, table, *asked = call(
+    sides, table, *farther = call(
         functools.partial(sides_kernel, sizes, plane_cap),
         [ANY] * 5,
-        [shape(sizes[0] * sizes[1], 3 * bx, 128), integers((8, 128)), *[shape(8, 128)] * count],
+        [shape(sizes[0] * sizes[1], 3 * bx, 128), integers((8 + -(-count // 8) * 8, 128)), *[shape(8, 128)] * (count - 3)],
         [
             pltpu.VMEM((1, SLOTS), jnp.int32),
             pltpu.VMEM((1, SLOTS), jnp.int32),
             pltpu.VMEM((FACES, 1, SLOTS), jnp.int32),
             pltpu.VMEM((bx, by, bz), F32),
             pltpu.VMEM((bx, by, bz), F32),
-            pltpu.SemaphoreType.DMA((2 * bx + 3,)),
+            pltpu.VMEM((sizes[0] * sizes[1], 3 * bx, 128), F32),
+            pltpu.SemaphoreType.DMA((2 * bx + 4,)),
         ],
+        [ANY] + [VMEM] * (count - 2),
         mib=56,
     )(
         tile_source.reshape(1, SLOTS),
@@ -532,7 +554,7 @@
     def exchange(values):
         return [pass_on(value, shift) for shift, value in enumerate(values, 1)]
 
-    farther = [pass_on(asked[shift], shift) for shift in range(2, others)]
+    farther = [pass_on(value, shift) for shift, value in enumerate(farther, 2)]
 
     phase_field = phase.reshape(SLOTS, TE, PLANE)
     solute_field = solute.reshape(SLOTS, TE, PLANE)
@@ -543,21 +565,21 @@
 
     layer = shape(3 * by + 8, bz)
     down, up = call(
-        functools.partial(layers_kernel, sizes), [VMEM] * 5 + [ANY] * (1 + len(farther)), [layer, layer]
-    )(enthalpy, conductivity, sides, asked[1], asked[others], packed[0], *farther)
+        functools.partial(layers_kernel, sizes), [VMEM] * 4 + [ANY] * (1 + len(farther)), [layer, layer]
+    )(enthalpy, conductivity, sides, table, packed[0], *farther)
     from_low, from_high = pass_on(up, 1), pass_on(down, others)
     row = 3 * by + 4
-    request = [asked[0][0], from_low[row], *[value[0] for value in farther], from_high[row]]
+    request = [from_low[row], *[value[0] for value in farther], from_high[row]]
     request = jnp.stack([value[:block_cap] for value in request]).astype(jnp.int32)
     _, deep = block_layout(block_cap)
     brick = shape(bx, by, bz)
     got = exchange(packed)
     heated, *found = call(
         functools.partial(heat_kernel, block_cap, sizes),
-        [SMEM] + [VMEM] * 5,
+        [SMEM] * 2 + [VMEM] * 5,
         [brick] + [shape(deep * CB, 128)] * count,
         [pltpu.VMEM((bx, by // CB, CB, bz), F32)],
-    )(request, enthalpy, conductivity, sides, from_low, from_high)
+    )(table, request, enthalpy, conductivity, sides, from_low, from_high)
     found[1:] = exchange(found[1:])
     (heat_out,) = call(write_out_kernel, [ANY], [brick], [pltpu.SemaphoreType.DMA], [ANY])(heated)
 
@@ -594,7 +616,11 @@
     got = exchange(send)
     inner_fields = inner(phase_field, solute_field, heat)
     phase_field, solute_field = call(
-        last_step_kernel, [SMEM] + [VMEM] * (4 + others), [field, field], step_scratch
+        last_step_kernel,
+        [SMEM] + [VMEM] * (4 + others),
+        [field, field],
+        step_scratch + [pltpu.VMEM(field.shape, F32)] * 2 + [pltpu.SemaphoreType.DMA((8,))],
+        [ANY] * 2,
     )(table, *inner_fields, own, places, *got)
     return heat_out, phase_field.reshape(phase.shape), solute_field.reshape(solute.shape)
 

time: 63.2 us -> 63.6 us (level)
  local copies, waits for them, and re-layouts: 3.25 us -> 1.96 us
  Pallas kernels: 13.6 us -> 14.5 us
  waiting for transfers between devices: 11.6 us -> 12.3 us
    ppermute x18, waiting for transfers between devices: 11.6 us -> 12.3 us  [pass_on(): lax.ppermute(value, 'gx', [(i, (i + shift) % count) for i in range(count)])]
    slice x4 -> x3, local copies, waits for them, and re-layouts: 0.7 us -> 0.01 us  [local(): value[:block_cap]]
    unnamed x28 -> x24, local copies, waits for them, and re-layouts: 2.56 us -> 1.95 us
  transfers between devices with their start and end apart: 19 -> 19, of which waited for: 11 -> 10; matrix products, arithmetic and copies ran while one was open for 1% -> 0% of each run, Pallas kernels for 9% -> 9%
where the time goes in v11:
time: 63.6 us; the launch traced here: 63.2 us
  starting transfers between devices  33.5 us (53%)
  Pallas kernels  14.5 us (23%)
  waiting for transfers between devices  12.3 us (19%)
  local copies, waits for them, and re-layouts  1.96 us (3%)
  between operations  0.87 us (1%)
    ppermute x18, starting transfers between devices, pass_on(): lax.ppermute(value, 'gx', [(i, (i + shift) % count) for i in range(count)])  28.3 us
    ppermute x18, waiting for transfers between devices, pass_on(): lax.ppermute(value, 'gx', [(i, (i + shift) % count) for i in range(count)])  12.3 us
    all_to_all x1, starting transfers between devices, local(): lax.all_to_all(sides, ('gy', 'gz'), split_axis=0, concat_axis=0, tiled=True)  5.18 us
    pallas_call x2, Pallas kernels, local(): call(middle_step_kernel, [SMEM] + [VMEM] * (5 + others), [field, field, o...  2.7 us
    pallas_call x1, Pallas kernels, local(): call(functools.partial(sides_kernel, sizes, plane_cap), [ANY] * 5, [shape...  2.64 us
    pallas_call x1, Pallas kernels, local(): call(functools.partial(heat_kernel, block_cap, sizes), [SMEM] * 2 + [VMEM...  2.03 us
    pallas_call x4, Pallas kernels, inner(): call(functools.partial(inner_kernel, bool(heat)), [VMEM] * (3 + len(heat)...  1.96 us
    unnamed x24, local copies, waits for them, and re-layouts  1.95 us
  transfers between devices with their start and end apart: 19, of which 10 were waited for; matrix products, arithmetic and copies ran while one was open for 0% of the time, Pallas kernels for 9%

profile of v11, /device:TPU:0, one launch (start us, length us, event | category | flops | bytes accessed | tf_op | source)
XLA Modules:
  0.0 63.2 jit_solution(11742086222361085333)
XLA Ops:
  0.6 0.0 copy-start
  0.6 2.6 %shard_map.130 = (f32[8,24,128]{2,1,0:T(8,128)}, s32[16,128]{1,0:T(8,128)}, f32[8,128]{1,0:T(8,128)}) custom-call(s32[1,16]{1,0:T(1,128)} %bitcast.15, s32[1,16]{1,0:T(1,128)} %bitcast.16, s32[6,1,16]{2,1,0:T(1,128)} %bitcast.14, f32[8,32,128]{2,1,0:T(8,128)} %h.3, f32[8,32,128]{2,1,0:T(8,128)} %k.3), custom_call_target="tpu_custom_call" | custom-call | tf_op jit(solution)/shard_map/pallas_call | solution.py:527
  3.3 0.0 copy-start.11
  3.3 0.0 copy-start.9
  3.3 5.2 %all-to-all-start = ((f32[8,24,128]{2,1,0:T(8,128)}), f32[8,24,128]{2,1,0:T(8,128)S(1)}, u32[]{:S(2)}, u32[]{:S(2)}) async-start(f32[8,24,128]{2,1,0:T(8,128)} %get-tuple-element.47), calls=%async_computation | async-start | bytes 196608 | tf_op jit(solution)/shard_map/all_to_all | solution.py:549
  8.5 0.0 copy-done.11
  8.5 2.7 %collective-permute-start = (f32[8,128]{1,0:T(8,128)S(1)}, f32[8,128]{1,0:T(8,128)S(1)}, u32[]{:S(2)}, u32[]{:S(2)}) collective-permute-start(f32[8,128]{1,0:T(8,128)S(1)} %copy-done.11), channel_id=1, source_target_pairs={{0,16},{8,24},{16,0},{24,8},{1,17},{9,25},{17,1},{25,9},{2,18},{10... | collective-permute-start | bytes 12296 | tf_op jit(solution)/shard_map/ppermute | solution.py:552
  11.2 0.0 copy-done
  11.2 0.0 copy-done.9
  11.2 0.9 %copy-done.2 = f32[1,1,1,16,16,256]{5,4,3,2,1,0:T(8,128)S(1)} copy-done((f32[1,1,1,16,16,256]{5,4,3,2,1,0:T(8,128)S(1)}, f32[1,1,1,16,16,256]{5,4,3,2,1,0:T(8,128)}, u32[]{:S(2)}) %copy-start.2) | copy-done | bytes 262168
  12.1 0.9 %copy-done.7 = f32[1,1,1,16,16,256]{5,4,3,2,1,0:T(8,128)S(1)} copy-done((f32[1,1,1,16,16,256]{5,4,3,2,1,0:T(8,128)S(1)}, f32[1,1,1,16,16,256]{5,4,3,2,1,0:T(8,128)}, u32[]{:S(2)}) %copy-start.7) | copy-done | bytes 262168
  13.1 1.0 %shard_map.131 = (f32[32,24,128]{2,1,0:T(8,128)S(1)}, f32[144,128]{1,0:T(8,128)S(1)}, f32[144,128]{1,0:T(8,128)S(1)}, f32[144,128]{1,0:T(8,128)S(1)}) custom-call(s32[16,128]{1,0:T(8,128)S(1)} %copy-done.9, f32[16,16,256]{2,1,0:T(8,128)S(1)} %bitcast.9, f32[16,16,256]{2,1,0:T(8,128)S(1)} %bitcast.12, bf16[512,256]{1,0:T(8,128)(2,1)S(1)} %copy-done), custom_call_target="tpu_custom_call" | custom-call | tf_op jit(solution)/shard_map/pallas_call | solution.py:562
  14.1 0.0 collective-permute-done.rest_1_
  14.1 0.0 all-to-all-done.got
  14.2 0.0 copy-start.8
  14.2 0.0 copy-start.3
  14.2 1.6 %collective-permute-start.1 = (f32[104,128]{1,0:T(8,128)S(1)}, f32[104,128]{1,0:T(8,128)S(1)}, u32[]{:S(2)}, u32[]{:S(2)}) collective-permute-start(f32[104,128]{1,0:T(8,128)S(1)} %get-tuple-element.50), channel_id=1, source_target_pairs={{0,8},{8,16},{16,24},{24,0},{1,9},{9,17},{17,25},{25,1},{2,10},{10... | collective-permute-start | bytes 159752 | tf_op jit(solution)/shard_map/ppermute | solution.py:552
  15.8 2.2 %collective-permute-start.2 = (f32[104,128]{1,0:T(8,128)S(1)}, f32[104,128]{1,0:T(8,128)S(1)}, u32[]{:S(2)}, u32[]{:S(2)}) collective-permute-start(f32[104,128]{1,0:T(8,128)S(1)} %get-tuple-element.51), channel_id=1, source_target_pairs={{0,24},{8,0},{16,8},{24,16},{1,25},{9,1},{17,9},{25,17},{2,26},{10... | collective-permute-start | bytes 159752 | tf_op jit(solution)/shard_map/ppermute | solution.py:552
  18.1 0.0 collective-permute-start.6
  18.1 1.9 %collective-permute-start.7 = (f32[144,128]{1,0:T(8,128)S(1)}, f32[144,128]{1,0:T(8,128)S(1)}, u32[]{:S(2)}, u32[]{:S(2)}) collective-permute-start(f32[144,128]{1,0:T(8,128)S(1)} %get-tuple-element.60), channel_id=1, source_target_pairs={{0,16},{8,24},{16,0},{24,8},{1,17},{9,25},{17,1},{25,9},{2,18},{10... | collective-permute-start | bytes 221192 | tf_op jit(solution)/shard_map/ppermute | solution.py:552
  20.0 1.9 %collective-permute-start.8 = (f32[144,128]{1,0:T(8,128)S(1)}, f32[144,128]{1,0:T(8,128)S(1)}, u32[]{:S(2)}, u32[]{:S(2)}) collective-permute-start(f32[144,128]{1,0:T(8,128)S(1)} %get-tuple-element.61), channel_id=1, source_target_pairs={{0,24},{8,0},{16,8},{24,16},{1,25},{9,1},{17,9},{25,17},{2,26},{10... | collective-permute-start | bytes 221192 | tf_op jit(solution)/shard_map/ppermute | solution.py:552
  21.9 0.0 collective-permute-done.1.low
  21.9 0.0 collective-permute-done.2.high
  22.0 0.0 copy-start.4
  22.0 2.0 %shard_map.133 = (f32[8,32,128]{2,1,0:T(8,128)S(1)}, f32[32,128]{1,0:T(8,128)S(1)}, f32[32,128]{1,0:T(8,128)S(1)}, f32[32,128]{1,0:T(8,128)S(1)}, f32[32,128]{1,0:T(8,128)S(1)}) custom-call(s32[16,128]{1,0:T(8,128)S(1)} %copy-done.9, s32[3,8]{1,0:T(4,128)S(1)} %maximum_convert_fusion.request, f32[8,32,128]{2,1,0:T(8,128)S(1)} %copy-done.5, ...), custom_call_target="tpu_custom_call" | custom-call | tf_op jit(solution)/shard_map/pallas_call | solution.py:577
  24.0 0.6 collective-permute-start.3
  24.6 2.6 %collective-permute-start.4 = (f32[32,128]{1,0:T(8,128)S(1)}, f32[32,128]{1,0:T(8,128)S(1)}, u32[]{:S(2)}, u32[]{:S(2)}) collective-permute-start(f32[32,128]{1,0:T(8,128)S(1)} %get-tuple-element.58), channel_id=1, source_target_pairs={{0,16},{8,24},{16,0},{24,8},{1,17},{9,25},{17,1},{25,9},{2,18},{10... | collective-permute-start | bytes 49160 | tf_op jit(solution)/shard_map/ppermute | solution.py:552
  27.3 0.0 collective-permute-done.7.rest_5_
  27.3 2.0 %collective-permute-start.5 = (f32[32,128]{1,0:T(8,128)S(1)}, f32[32,128]{1,0:T(8,128)S(1)}, u32[]{:S(2)}, u32[]{:S(2)}) collective-permute-start(f32[32,128]{1,0:T(8,128)S(1)} %get-tuple-element.59), channel_id=1, source_target_pairs={{0,24},{8,0},{16,8},{24,16},{1,25},{9,1},{17,9},{25,17},{2,26},{10... | collective-permute-start | bytes 49160 | tf_op jit(solution)/shard_map/ppermute | solution.py:552
  29.3 0.0 copy-done.8
  29.3 0.0 copy-done.4
  29.3 0.5 shard_map.135
  29.8 0.0 collective-permute-done.8.rest_6_
  29.8 0.0 collective-permute-done.6.rest_4_
  29.8 0.0 collective-permute-done.3.rest_1_
  29.8 0.0 collective-permute-done.4.rest_2_
  29.8 1.2 %collective-permute-done.5.rest_3_ = f32[32,128]{1,0:T(8,128)S(1)} collective-permute-done((f32[32,128]{1,0:T(8,128)S(1)}, f32[32,128]{1,0:T(8,128)S(1)}, u32[]{:S(2)}, u32[]{:S(2)}) %collective-permute-start.5) | collective-permute-done | bytes 16416 | tf_op jit(solution)/shard_map/ppermute | solution.py:552
  31.0 0.0 copy-done.10
  31.0 1.8 %shard_map.136 = (f32[16,16,256]{2,1,0:T(8,128)S(1)}, f32[16,16,256]{2,1,0:T(8,128)S(1)}, f32[2,256,128]{2,1,0:T(8,128)S(1)}, f32[32,24,128]{2,1,0:T(8,128)S(1)}...) custom-call(s32[16,128]{1,0:T(8,128)S(1)} %copy-done.9, f32[16,16,256]{2,1,0:T(8,128)S(1)} %bitcast.11, ...), custom_call_target="tpu_custom_call" | custom-call | tf_op jit(solution)/shard_map/pallas_call | solution.py:597
  32.8 1.2 %collective-permute-start.9 = (f32[144,128]{1,0:T(8,128)S(1)}, f32[144,128]{1,0:T(8,128)S(1)}, u32[]{:S(2)}, u32[]{:S(2)}) collective-permute-start(f32[144,128]{1,0:T(8,128)S(1)} %get-tuple-element.68), channel_id=1, source_target_pairs={{0,8},{8,16},{16,24},{24,0},{1,9},{9,17},{17,25},{25,1},{2,10},{10... | collective-permute-start | bytes 221192 | tf_op jit(solution)/shard_map/ppermute | solution.py:552
  34.0 3.3 %collective-permute-start.10 = (f32[144,128]{1,0:T(8,128)S(1)}, f32[144,128]{1,0:T(8,128)S(1)}, u32[]{:S(2)}, u32[]{:S(2)}) collective-permute-start(f32[144,128]{1,0:T(8,128)S(1)} %get-tuple-element.69), channel_id=1, source_target_pairs={{0,16},{8,24},{16,0},{24,8},{1,17},{9,25},{17,1},{25,9},{2,18},{10... | collective-permute-start | bytes 221192 | tf_op jit(solution)/shard_map/ppermute | solution.py:552
  37.3 0.0 collective-permute-start.11
  37.3 0.5 shard_map.137
  37.8 1.3 %collective-permute-done.9.rest_0_ = f32[144,128]{1,0:T(8,128)S(1)} collective-permute-done((f32[144,128]{1,0:T(8,128)S(1)}, f32[144,128]{1,0:T(8,128)S(1)}, u32[]{:S(2)}, u32[]{:S(2)}) %collective-permute-start.9) | collective-permute-done | bytes 73760 | tf_op jit(solution)/shard_map/ppermute | solution.py:552
  39.1 1.6 %collective-permute-done.10.rest_1_ = f32[144,128]{1,0:T(8,128)S(1)} collective-permute-done((f32[144,128]{1,0:T(8,128)S(1)}, f32[144,128]{1,0:T(8,128)S(1)}, u32[]{:S(2)}, u32[]{:S(2)}) %collective-permute-start.10) | collective-permute-done | bytes 73760 | tf_op jit(solution)/shard_map/ppermute | solution.py:552
  40.6 1.0 %collective-permute-done.11.rest_2_ = f32[144,128]{1,0:T(8,128)S(1)} collective-permute-done((f32[144,128]{1,0:T(8,128)S(1)}, f32[144,128]{1,0:T(8,128)S(1)}, u32[]{:S(2)}, u32[]{:S(2)}) %collective-permute-start.11) | collective-permute-done | bytes 73760 | tf_op jit(solution)/shard_map/ppermute | solution.py:552
  41.7 1.4 %shard_map.138 = (f32[16,16,256]{2,1,0:T(8,128)S(1)}, f32[16,16,256]{2,1,0:T(8,128)S(1)}, f32[32,24,128]{2,1,0:T(8,128)S(1)}, f32[144,128]{1,0:T(8,128)S(1)}, f3...) custom-call(s32[16,128]{1,0:T(8,128)S(1)} %copy-done.9, f32[16,16,256]{2,1,0:T(8,128)S(1)} %get-tuple-element.65.phase, ...), custom_call_target="tpu_custom_call" | custom-call | tf_op jit(solution)/shard_map/pallas_call | solution.py:610
  43.0 0.4 collective-permute-start.12
  43.4 3.1 %collective-permute-start.13 = (f32[144,128]{1,0:T(8,128)S(1)}, f32[144,128]{1,0:T(8,128)S(1)}, u32[]{:S(2)}, u32[]{:S(2)}) collective-permute-start(f32[144,128]{1,0:T(8,128)S(1)} %get-tuple-element.77), channel_id=1, source_target_pairs={{0,16},{8,24},{16,0},{24,8},{1,17},{9,25},{17,1},{25,9},{2,18},{10... | collective-permute-start | bytes 221192 | tf_op jit(solution)/shard_map/ppermute | solution.py:552
  46.5 0.5 collective-permute-start.14
  47.0 0.5 shard_map.139
  47.5 1.9 %collective-permute-done.12.rest_0_ = f32[144,128]{1,0:T(8,128)S(1)} collective-permute-done((f32[144,128]{1,0:T(8,128)S(1)}, f32[144,128]{1,0:T(8,128)S(1)}, u32[]{:S(2)}, u32[]{:S(2)}) %collective-permute-start.12) | collective-permute-done | bytes 73760 | tf_op jit(solution)/shard_map/ppermute | solution.py:552
  49.3 1.2 %collective-permute-done.13.rest_1_ = f32[144,128]{1,0:T(8,128)S(1)} collective-permute-done((f32[144,128]{1,0:T(8,128)S(1)}, f32[144,128]{1,0:T(8,128)S(1)}, u32[]{:S(2)}, u32[]{:S(2)}) %collective-permute-start.13) | collective-permute-done | bytes 73760 | tf_op jit(solution)/shard_map/ppermute | solution.py:552
  50.5 1.5 %collective-permute-done.14.rest_2_ = f32[144,128]{1,0:T(8,128)S(1)} collective-permute-done((f32[144,128]{1,0:T(8,128)S(1)}, f32[144,128]{1,0:T(8,128)S(1)}, u32[]{:S(2)}, u32[]{:S(2)}) %collective-permute-start.14) | collective-permute-done | bytes 73760 | tf_op jit(solution)/shard_map/ppermute | solution.py:552
  52.1 1.3 %shard_map.140 = (f32[16,16,256]{2,1,0:T(8,128)S(1)}, f32[16,16,256]{2,1,0:T(8,128)S(1)}, f32[32,24,128]{2,1,0:T(8,128)S(1)}, f32[144,128]{1,0:T(8,128)S(1)}, f3...) custom-call(s32[16,128]{1,0:T(8,128)S(1)} %copy-done.9, f32[16,16,256]{2,1,0:T(8,128)S(1)} %get-tuple-element.73.phase, ...), custom_call_target="tpu_custom_call" | custom-call | tf_op jit(solution)/shard_map/pallas_call | solution.py:610
  53.4 1.8 %collective-permute-start.15 = (f32[144,128]{1,0:T(8,128)S(1)}, f32[144,128]{1,0:T(8,128)S(1)}, u32[]{:S(2)}, u32[]{:S(2)}) collective-permute-start(f32[144,128]{1,0:T(8,128)S(1)} %get-tuple-element.84), channel_id=1, source_target_pairs={{0,8},{8,16},{16,24},{24,0},{1,9},{9,17},{17,25},{25,1},{2,10},{10... | collective-permute-start | bytes 221192 | tf_op jit(solution)/shard_map/ppermute | solution.py:552
  55.2 1.1 %collective-permute-start.16 = (f32[144,128]{1,0:T(8,128)S(1)}, f32[144,128]{1,0:T(8,128)S(1)}, u32[]{:S(2)}, u32[]{:S(2)}) collective-permute-start(f32[144,128]{1,0:T(8,128)S(1)} %get-tuple-element.85), channel_id=1, source_target_pairs={{0,16},{8,24},{16,0},{24,8},{1,17},{9,25},{17,1},{25,9},{2,18},{10... | collective-permute-start | bytes 221192 | tf_op jit(solution)/shard_map/ppermute | solution.py:552
  56.4 1.3 %collective-permute-start.17 = (f32[144,128]{1,0:T(8,128)S(1)}, f32[144,128]{1,0:T(8,128)S(1)}, u32[]{:S(2)}, u32[]{:S(2)}) collective-permute-start(f32[144,128]{1,0:T(8,128)S(1)} %get-tuple-element.86), channel_id=1, source_target_pairs={{0,24},{8,0},{16,8},{24,16},{1,25},{9,1},{17,9},{25,17},{2,26},{10... | collective-permute-start | bytes 221192 | tf_op jit(solution)/shard_map/ppermute | solution.py:552
  57.7 0.7 %shard_map.134 = f32[8,32,128]{2,1,0:T(8,128)} custom-call(f32[8,32,128]{2,1,0:T(8,128)S(1)} %get-tuple-element.52.value), custom_call_target="tpu_custom_call" | custom-call | tf_op jit(solution)/shard_map/pallas_call | solution.py:584
  58.4 0.5 shard_map.141
  58.8 0.8 %collective-permute-done.15.rest_0_ = f32[144,128]{1,0:T(8,128)S(1)} collective-permute-done((f32[144,128]{1,0:T(8,128)S(1)}, f32[144,128]{1,0:T(8,128)S(1)}, u32[]{:S(2)}, u32[]{:S(2)}) %collective-permute-start.15) | collective-permute-done | bytes 73760 | tf_op jit(solution)/shard_map/ppermute | solution.py:552
  59.6 1.7 %collective-permute-done.16.rest_1_ = f32[144,128]{1,0:T(8,128)S(1)} collective-permute-done((f32[144,128]{1,0:T(8,128)S(1)}, f32[144,128]{1,0:T(8,128)S(1)}, u32[]{:S(2)}, u32[]{:S(2)}) %collective-permute-start.16) | collective-permute-done | bytes 73760 | tf_op jit(solution)/shard_map/ppermute | solution.py:552
  61.3 0.2 collective-permute-done.17.rest_2_
  61.5 1.7 %shard_map.142 = (f32[16,16,256]{2,1,0:T(8,128)}, f32[16,16,256]{2,1,0:T(8,128)}) custom-call(s32[16,128]{1,0:T(8,128)S(1)} %copy-done.9, f32[16,16,256]{2,1,0:T(8,128)S(1)} %get-tuple-element.81.phase, f32[16,16,256]{2,1,0:T(8,128)S(1)} %get-tuple-element.82.solute, f32[32,24,128]{2,1,0:T(8,128)S(1)} %get-tuple-element.83.own, ...), custom_call_target="tpu_custom_call" | custom-call | tf_op jit(solution)/shard_map/pallas_call | solution.py:618
  (15 shorter events, 0.1 us)
Async XLA Ops:
  0.6 10.5 %copy-start = (bf16[512,256]{1,0:T(8,128)(2,1)S(1)}, bf16[512,256]{1,0:T(8,128)(2,1)}, u32[]{:S(2)}) copy-start(bf16[512,256]{1,0:T(8,128)(2,1)} %constant.8.clone.picks) | copy-start | bytes 786436
  3.3 5.2 %copy-start.11 = (f32[8,128]{1,0:T(8,128)S(1)}, f32[8,128]{1,0:T(8,128)}, u32[]{:S(2)}) copy-start(f32[8,128]{1,0:T(8,128)} %get-tuple-element.49) | copy-start | bytes 12292
  3.3 7.9 %copy-start.9 = (s32[16,128]{1,0:T(8,128)S(1)}, s32[16,128]{1,0:T(8,128)}, u32[]{:S(2)}) copy-start(s32[16,128]{1,0:T(8,128)} %get-tuple-element.46.table) | copy-start | bytes 24580
  3.3 10.8 %all-to-all-start = ((f32[8,24,128]{2,1,0:T(8,128)}), f32[8,24,128]{2,1,0:T(8,128)S(1)}, u32[]{:S(2)}, u32[]{:S(2)}) async-start(f32[8,24,128]{2,1,0:T(8,128)} %get-tuple-element.47), calls=%async_computation | async-start | bytes 196608 | tf_op jit(solution)/shard_map/all_to_all | solution.py:549
  8.5 5.6 %collective-permute-start = (f32[8,128]{1,0:T(8,128)S(1)}, f32[8,128]{1,0:T(8,128)S(1)}, u32[]{:S(2)}, u32[]{:S(2)}) collective-permute-start(f32[8,128]{1,0:T(8,128)S(1)} %copy-done.11), channel_id=1, source_target_pairs={{0,16},{8,24},{16,0},{24,8},{1,17},{9,25},{17,1},{25,9},{2,18},{10... | collective-permute-start | bytes 12296 | tf_op jit(solution)/shard_map/ppermute | solution.py:552
  11.2 1.0 %copy-start.2 = (f32[1,1,1,16,16,256]{5,4,3,2,1,0:T(8,128)S(1)}, f32[1,1,1,16,16,256]{5,4,3,2,1,0:T(8,128)}, u32[]{:S(2)}) copy-start(f32[1,1,1,16,16,256]{5,4,3,2,1,0:T(8,128)} %param.13) | copy-start | bytes 786436
  12.1 0.9 %copy-start.7 = (f32[1,1,1,16,16,256]{5,4,3,2,1,0:T(8,128)S(1)}, f32[1,1,1,16,16,256]{5,4,3,2,1,0:T(8,128)}, u32[]{:S(2)}) copy-start(f32[1,1,1,16,16,256]{5,4,3,2,1,0:T(8,128)} %param.14) | copy-start | bytes 786436
  13.1 1.1 %copy-start.5 = (f32[8,32,128]{2,1,0:T(8,128)S(1)}, f32[8,32,128]{2,1,0:T(8,128)}, u32[]{:S(2)}) copy-start(f32[8,32,128]{2,1,0:T(8,128)} %h.3) | copy-start | bytes 393220
  13.1 1.1 %copy-start.6 = (f32[8,32,128]{2,1,0:T(8,128)S(1)}, f32[8,32,128]{2,1,0:T(8,128)}, u32[]{:S(2)}) copy-start(f32[8,32,128]{2,1,0:T(8,128)} %k.3) | copy-start | bytes 393220
  14.2 15.1 %copy-start.8 = (f32[1,1,1,16,16,256]{5,4,3,2,1,0:T(8,128)S(1)}, f32[1,1,1,16,16,256]{5,4,3,2,1,0:T(8,128)}, u32[]{:S(2)}) copy-start(f32[1,1,1,16,16,256]{5,4,3,2,1,0:T(8,128)} %param.14) | copy-start | bytes 786436
  14.2 15.1 %copy-start.3 = (f32[1,1,1,16,16,256]{5,4,3,2,1,0:T(8,128)S(1)}, f32[1,1,1,16,16,256]{5,4,3,2,1,0:T(8,128)}, u32[]{:S(2)}) copy-start(f32[1,1,1,16,16,256]{5,4,3,2,1,0:T(8,128)} %param.13) | copy-start | bytes 786436
  14.2 7.7 %collective-permute-start.1 = (f32[104,128]{1,0:T(8,128)S(1)}, f32[104,128]{1,0:T(8,128)S(1)}, u32[]{:S(2)}, u32[]{:S(2)}) collective-permute-start(f32[104,128]{1,0:T(8,128)S(1)} %get-tuple-element.50), channel_id=1, source_target_pairs={{0,8},{8,16},{16,24},{24,0},{1,9},{9,17},{17,25},{25,1},{2,10},{10... | collective-permute-start | bytes 159752 | tf_op jit(solution)/shard_map/ppermute | solution.py:552
  15.8 6.1 %collective-permute-start.2 = (f32[104,128]{1,0:T(8,128)S(1)}, f32[104,128]{1,0:T(8,128)S(1)}, u32[]{:S(2)}, u32[]{:S(2)}) collective-permute-start(f32[104,128]{1,0:T(8,128)S(1)} %get-tuple-element.51), channel_id=1, source_target_pairs={{0,24},{8,0},{16,8},{24,16},{1,25},{9,1},{17,9},{25,17},{2,26},{10... | collective-permute-start | bytes 159752 | tf_op jit(solution)/shard_map/ppermute | solution.py:552
  18.1 11.7 %collective-permute-start.6 = (f32[144,128]{1,0:T(8,128)S(1)}, f32[144,128]{1,0:T(8,128)S(1)}, u32[]{:S(2)}, u32[]{:S(2)}) collective-permute-start(f32[144,128]{1,0:T(8,128)S(1)} %get-tuple-element.48.rest_0_), channel_id=1, source_target_pairs={{0,8},{8,16},{16,24},{24,0},{1,9},{9,17},{17,25},{25,1},{2,10},{10... | collective-permute-start | bytes 221192 | tf_op jit(solution)/shard_map/ppermute | solution.py:552
  18.1 9.2 %collective-permute-start.7 = (f32[144,128]{1,0:T(8,128)S(1)}, f32[144,128]{1,0:T(8,128)S(1)}, u32[]{:S(2)}, u32[]{:S(2)}) collective-permute-start(f32[144,128]{1,0:T(8,128)S(1)} %get-tuple-element.60), channel_id=1, source_target_pairs={{0,16},{8,24},{16,0},{24,8},{1,17},{9,25},{17,1},{25,9},{2,18},{10... | collective-permute-start | bytes 221192 | tf_op jit(solution)/shard_map/ppermute | solution.py:552
  20.0 9.8 %collective-permute-start.8 = (f32[144,128]{1,0:T(8,128)S(1)}, f32[144,128]{1,0:T(8,128)S(1)}, u32[]{:S(2)}, u32[]{:S(2)}) collective-permute-start(f32[144,128]{1,0:T(8,128)S(1)} %get-tuple-element.61), channel_id=1, source_target_pairs={{0,24},{8,0},{16,8},{24,16},{1,25},{9,1},{17,9},{25,17},{2,26},{10... | collective-permute-start | bytes 221192 | tf_op jit(solution)/shard_map/ppermute | solution.py:552
  22.0 7.3 %copy-start.4 = (bf16[256,256]{1,0:T(8,128)(2,1)S(1)}, bf16[256,256]{1,0:T(8,128)(2,1)}, u32[]{:S(2)}) copy-start(bf16[256,256]{1,0:T(8,128)(2,1)} %constant.9.clone.stencil) | copy-start | bytes 393220
  24.0 5.8 %collective-permute-start.3 = (f32[32,128]{1,0:T(8,128)S(1)}, f32[32,128]{1,0:T(8,128)S(1)}, u32[]{:S(2)}, u32[]{:S(2)}) collective-permute-start(f32[32,128]{1,0:T(8,128)S(1)} %get-tuple-element.57), channel_id=1, source_target_pairs={{0,8},{8,16},{16,24},{24,0},{1,9},{9,17},{17,25},{25,1},{2,10},{10... | collective-permute-start | bytes 49160 | tf_op jit(solution)/shard_map/ppermute | solution.py:552
  24.6 5.2 %collective-permute-start.4 = (f32[32,128]{1,0:T(8,128)S(1)}, f32[32,128]{1,0:T(8,128)S(1)}, u32[]{:S(2)}, u32[]{:S(2)}) collective-permute-start(f32[32,128]{1,0:T(8,128)S(1)} %get-tuple-element.58), channel_id=1, source_target_pairs={{0,16},{8,24},{16,0},{24,8},{1,17},{9,25},{17,1},{25,9},{2,18},{10... | collective-permute-start | bytes 49160 | tf_op jit(solution)/shard_map/ppermute | solution.py:552
  27.3 3.7 %copy-start.1 = (bf16[256,512]{1,0:T(8,128)(2,1)S(1)}, bf16[256,512]{1,0:T(8,128)(2,1)}, u32[]{:S(2)}) copy-start(bf16[256,512]{1,0:T(8,128)(2,1)} %constant.10.clone.places) | copy-start | bytes 786436
  27.3 3.7 %copy-start.10 = (bf16[256,256]{1,0:T(8,128)(2,1)S(1)}, bf16[256,256]{1,0:T(8,128)(2,1)}, u32[]{:S(2)}) copy-start(bf16[256,256]{1,0:T(8,128)(2,1)} %constant.11.clone.spreads) | copy-start | bytes 393220
  27.3 3.7 %collective-permute-start.5 = (f32[32,128]{1,0:T(8,128)S(1)}, f32[32,128]{1,0:T(8,128)S(1)}, u32[]{:S(2)}, u32[]{:S(2)}) collective-permute-start(f32[32,128]{1,0:T(8,128)S(1)} %get-tuple-element.59), channel_id=1, source_target_pairs={{0,24},{8,0},{16,8},{24,16},{1,25},{9,1},{17,9},{25,17},{2,26},{10... | collective-permute-start | bytes 49160 | tf_op jit(solution)/shard_map/ppermute | solution.py:552
  32.8 6.3 %collective-permute-start.9 = (f32[144,128]{1,0:T(8,128)S(1)}, f32[144,128]{1,0:T(8,128)S(1)}, u32[]{:S(2)}, u32[]{:S(2)}) collective-permute-start(f32[144,128]{1,0:T(8,128)S(1)} %get-tuple-element.68), channel_id=1, source_target_pairs={{0,8},{8,16},{16,24},{24,0},{1,9},{9,17},{17,25},{25,1},{2,10},{10... | collective-permute-start | bytes 221192 | tf_op jit(solution)/shard_map/ppermute | solution.py:552
  34.0 6.6 %collective-permute-start.10 = (f32[144,128]{1,0:T(8,128)S(1)}, f32[144,128]{1,0:T(8,128)S(1)}, u32[]{:S(2)}, u32[]{:S(2)}) collective-permute-start(f32[144,128]{1,0:T(8,128)S(1)} %get-tuple-element.69), channel_id=1, source_target_pairs={{0,16},{8,24},{16,0},{24,8},{1,17},{9,25},{17,1},{25,9},{2,18},{10... | collective-permute-start | bytes 221192 | tf_op jit(solution)/shard_map/ppermute | solution.py:552
  37.3 4.4 %collective-permute-start.11 = (f32[144,128]{1,0:T(8,128)S(1)}, f32[144,128]{1,0:T(8,128)S(1)}, u32[]{:S(2)}, u32[]{:S(2)}) collective-permute-start(f32[144,128]{1,0:T(8,128)S(1)} %get-tuple-element.70), channel_id=1, source_target_pairs={{0,24},{8,0},{16,8},{24,16},{1,25},{9,1},{17,9},{25,17},{2,26},{10... | collective-permute-start | bytes 221192 | tf_op jit(solution)/shard_map/ppermute | solution.py:552
  43.0 6.3 %collective-permute-start.12 = (f32[144,128]{1,0:T(8,128)S(1)}, f32[144,128]{1,0:T(8,128)S(1)}, u32[]{:S(2)}, u32[]{:S(2)}) collective-permute-start(f32[144,128]{1,0:T(8,128)S(1)} %get-tuple-element.76), channel_id=1, source_target_pairs={{0,8},{8,16},{16,24},{24,0},{1,9},{9,17},{17,25},{25,1},{2,10},{10... | collective-permute-start | bytes 221192 | tf_op jit(solution)/shard_map/ppermute | solution.py:552
  43.4 7.1 %collective-permute-start.13 = (f32[144,128]{1,0:T(8,128)S(1)}, f32[144,128]{1,0:T(8,128)S(1)}, u32[]{:S(2)}, u32[]{:S(2)}) collective-permute-start(f32[144,128]{1,0:T(8,128)S(1)} %get-tuple-element.77), channel_id=1, source_target_pairs={{0,16},{8,24},{16,0},{24,8},{1,17},{9,25},{17,1},{25,9},{2,18},{10... | collective-permute-start | bytes 221192 | tf_op jit(solution)/shard_map/ppermute | solution.py:552
  46.5 5.6 %collective-permute-start.14 = (f32[144,128]{1,0:T(8,128)S(1)}, f32[144,128]{1,0:T(8,128)S(1)}, u32[]{:S(2)}, u32[]{:S(2)}) collective-permute-start(f32[144,128]{1,0:T(8,128)S(1)} %get-tuple-element.78), channel_id=1, source_target_pairs={{0,24},{8,0},{16,8},{24,16},{1,25},{9,1},{17,9},{25,17},{2,26},{10... | collective-permute-start | bytes 221192 | tf_op jit(solution)/shard_map/ppermute | solution.py:552
  53.4 6.2 %collective-permute-start.15 = (f32[144,128]{1,0:T(8,128)S(1)}, f32[144,128]{1,0:T(8,128)S(1)}, u32[]{:S(2)}, u32[]{:S(2)}) collective-permute-start(f32[144,128]{1,0:T(8,128)S(1)} %get-tuple-element.84), channel_id=1, source_target_pairs={{0,8},{8,16},{16,24},{24,0},{1,9},{9,17},{17,25},{25,1},{2,10},{10... | collective-permute-start | bytes 221192 | tf_op jit(solution)/shard_map/ppermute | solution.py:552
  55.2 6.1 %collective-permute-start.16 = (f32[144,128]{1,0:T(8,128)S(1)}, f32[144,128]{1,0:T(8,128)S(1)}, u32[]{:S(2)}, u32[]{:S(2)}) collective-permute-start(f32[144,128]{1,0:T(8,128)S(1)} %get-tuple-element.85), channel_id=1, source_target_pairs={{0,16},{8,24},{16,0},{24,8},{1,17},{9,25},{17,1},{25,9},{2,18},{10... | collective-permute-start | bytes 221192 | tf_op jit(solution)/shard_map/ppermute | solution.py:552
  56.4 5.1 %collective-permute-start.17 = (f32[144,128]{1,0:T(8,128)S(1)}, f32[144,128]{1,0:T(8,128)S(1)}, u32[]{:S(2)}, u32[]{:S(2)}) collective-permute-start(f32[144,128]{1,0:T(8,128)S(1)} %get-tuple-element.86), channel_id=1, source_target_pairs={{0,24},{8,0},{16,8},{24,16},{1,25},{9,1},{17,9},{25,17},{2,26},{10... | collective-permute-start | bytes 221192 | tf_op jit(solution)/shard_map/ppermute | solution.py:552

commit v12 on v10

--- a/solution.py
+++ b/solution.py
@@ -125,10 +125,20 @@
     return jnp.sum(jnp.where(iota(square, 0) == iota(square, 1), row, 0.0), axis=1, keepdims=True)
 
 
-def write_tables(plane_cap, source, block, neighbour, asked, table):
+def table_sizes(count, plane_cap):
+    records = (count - 1) * plane_cap
+    faces = min(FACES, 128 // records)
+    return records, faces, 1 + -(-FACES // faces)
+
+
+def place_of(table, slot):
+    return table[0, FACES * SLOTS + slot], table[0, FACES * SLOTS + SLOTS + slot]
+
+
+def write_tables(plane_cap, source, block, neighbour, asked, farther, table):
     me = lax.axis_index("gx").astype(F32)
-    count = len(asked)
-    records = (count - 1) * plane_cap
+    count = lax.axis_size("gx")
+    records, faces, _ = table_sizes(count, plane_cap)
     cap = float(plane_cap)
 
     def wrapped(shift):
@@ -147,9 +157,12 @@
     for shift in range(count):
         hit = (wrapped(source_column - me) == float(shift)) & (rank_column == lane)
         row = jnp.sum(jnp.where(hit, block_column, 0.0), axis=0, keepdims=True)
-        asked[shift][...] = jnp.broadcast_to(row, asked[shift].shape)
-    table[6:7, 0:SLOTS] = wrapped(me - source_row).astype(jnp.int32)
-    table[7:8, 0:SLOTS] = rank.astype(jnp.int32)
+        asked[shift : shift + 1, :] = row
+        if 2 <= shift < count - 1:
+            farther[shift - 2][...] = jnp.broadcast_to(row, (8, 128))
+    at = FACES * SLOTS
+    table[0:1, at : at + SLOTS] = wrapped(me - source_row).astype(jnp.int32)
+    table[0:1, at + SLOTS : at + 2 * SLOTS] = rank.astype(jnp.int32)
     slot_column = iota((SLOTS, records), 0).astype(F32)
     for face in range(FACES):
         number = neighbour[face]
@@ -165,17 +178,18 @@
         there = (wrapped(me - owner_row) - 1.0) * cap + receive_rank
         receive = jnp.where(owner_row == me, here, there)
         receive = jnp.where(number_row < 0.0, records + SLOTS + slot, receive)
-        table[face : face + 1, 0:SLOTS] = receive.astype(jnp.int32)
+        table[0:1, face * SLOTS : face * SLOTS + SLOTS] = receive.astype(jnp.int32)
         key = jnp.where(other_row, (wrapped(owner_row - me) - 1.0) * cap + send_rank, -1.0)
         hit = iota((SLOTS, records), 1).astype(F32) == column_of(key)
         tile = jnp.sum(jnp.where(hit, slot_column, 0.0), axis=0, keepdims=True)
-        table[face ^ 1 : (face ^ 1) + 1, SLOTS : SLOTS + records] = tile.astype(jnp.int32)
+        row, at = 1 + (face ^ 1) // faces, (face ^ 1) % faces * records
+        table[row : row + 1, at : at + records] = tile.astype(jnp.int32)
 
 
 def sides_kernel(
     sizes, plane_cap, source_far, block_far, neighbour_far, h_far, k_far, send, table, *rest
 ):
-    *asked, source, block, neighbour, h, k, sems = rest
+    asked, *farther, source, block, neighbour, h, k, sems = rest
     ny, nz = sizes
     my_y, my_z = lax.axis_index("gy"), lax.axis_index("gz")
     bx = h.shape[0]
@@ -189,7 +203,7 @@
         copy.start()
     for copy in copies:
         copy.wait()
-    write_tables(plane_cap, source, block, neighbour, asked, table)
+    write_tables(plane_cap, source, block, neighbour, asked, farther, table)
     for copy in large:
         copy.wait()
     blocks = side_blocks(h[...], k[...])
@@ -216,18 +230,19 @@
     return read
 
 
-def layers_kernel(sizes, h, k, got, ask_up, ask_down, *rest):
+def layers_kernel(sizes, h, k, got, asked, *rest):
     down, up = rest[-2:]
     bx, by, bz = h.shape
     read = side_reader(sizes, got, bx)
     around = [read(-1, 0), read(1, 0), read(0, -1), read(0, 1)]
-    for out, near, far, ask in ((down, 0, 1, ask_down), (up, bx - 1, bx - 2, ask_up)):
+    last = asked.shape[0] - 1
+    for out, near, far, ask in ((down, 0, 1, last), (up, bx - 1, bx - 2, 1)):
         out[0:by, :] = h[near]
         out[by : 2 * by, :] = h[far]
         out[2 * by : 3 * by, :] = k[near]
         for number, side in enumerate(around):
             out[3 * by + number : 3 * by + number + 1, :] = side[near : near + 1, :]
-        out[3 * by + 4 : 3 * by + 8, :] = ask[0:4, :]
+        out[3 * by + 4 : 3 * by + 8, :] = jnp.broadcast_to(asked[ask : ask + 1, :], (4, bz))
 
 
 def block_layout(cap):
@@ -309,46 +324,48 @@
         (send[shift - 1] if shift else found)[...] = total
 
 
-def write_records(phase, solute, picks, own):
+def write_records(phase, solute, picks, own, own_edges, rows):
     flat = [f.reshape(SLOTS * TE, PLANE) for f in (phase, solute)]
     high, low = halves(jnp.concatenate(flat, axis=1))
     planes = dot(high, picks) + dot(low, picks)
-    own[0:SLOTS, 0:TE, :] = planes[:, 0:128].reshape(SLOTS, TE, 128)
-    own[SLOTS : 2 * SLOTS, 0:TE, :] = planes[:, 128:256].reshape(SLOTS, TE, 128)
-    for face in range(2):
-        for number, field in enumerate((phase, solute)):
-            for half in range(2):
-                row = TE + face * 4 + number * 2 + half
-                lanes = slice(half * 128, half * 128 + 128)
-                near, far = (0, TE - 1) if face == 0 else (TE - 1, 0)
-                own[0:SLOTS, row : row + 1, :] = field[:, far : far + 1, lanes]
-                own[SLOTS : 2 * SLOTS, row : row + 1, :] = field[:, near : near + 1, lanes]
-
-
-def merge_record(source, number):
+    own[0:SLOTS] = planes[:, 0:128].reshape(SLOTS, TE, 128)
+    own[SLOTS : 2 * SLOTS] = planes[:, 128:256].reshape(SLOTS, TE, 128)
+    for part in range(4):
+        rows[part] = flat[part // 2][:, part % 2 * 128 : part % 2 * 128 + 128]
+    for part in range(4):
+        low_face = rows[part, pl.ds(0, SLOTS, TE), :]
+        high_face = rows[part, pl.ds(TE - 1, SLOTS, TE), :]
+        for at, value in ((0, high_face), (4, low_face)):
+            own_edges[pl.ds(at + part, SLOTS, 8), :] = value
+            own_edges[pl.ds(8 * SLOTS + 4 - at + part, SLOTS, 8), :] = value
+
+
+def merge_record(planes, edges, number):
     side = (iota((TE, 128), 1) % 64) // TE
-    out = source[number(2), 0:TE, :]
+    out = planes[number(2)]
     for face in range(3, 6):
-        out = jnp.where(side == face - 2, source[number(face), 0:TE, :], out)
-    edge = jnp.where(
-        iota((8, 128), 0) < 4, source[number(0), TE:REC, :], source[number(1), TE:REC, :]
-    )
-    return out, edge
-
-
-def pack(own, table, send):
+        out = jnp.where(side == face - 2, planes[number(face)], out)
+    first, second = [edges[pl.ds(pl.multiple_of(number(face) * 8, 8), 8), :] for face in range(2)]
+    return out, jnp.where(iota((8, 128), 0) < 4, first, second)
+
+
+def pack(own, own_edges, table, send):
     cap = send[0].shape[0] // REC
-    for number, out in enumerate(send):
-        for rank in range(cap):
-            record = number * cap + rank
-            planes, edge = merge_record(own, lambda face: table[face, SLOTS + record])
-            out[rank * REC : rank * REC + TE, :] = planes
-            out[rank * REC + TE : rank * REC + REC, :] = edge
-
-
-def first_pack_kernel(table, phase, solute, picks, own, *send):
-    write_records(phase[...], solute[...], picks[...], own)
-    pack(own, table, send)
+    records, faces, _ = table_sizes(len(send) + 1, cap)
+    for record in range(records):
+        out, row = send[record // cap], record % cap * REC
+        planes, edge = merge_record(
+            own, own_edges, lambda face: table[1 + face // faces, face % faces * records + record]
+        )
+        out[row : row + TE, :] = planes
+        out[row + TE : row + REC, :] = edge
+
+
+def first_pack_kernel(table, asked, phase, solute, picks, own, own_edges, asked_out, *rest):
+    *send, rows = rest
+    write_records(phase[...], solute[...], picks[...], own, own_edges, rows)
+    pack(own, own_edges, table, send)
+    asked_out[...] = asked[...]
 
 
 def take_heat(cap, table, found, spreads, blocks, held, heat):
@@ -357,7 +374,7 @@
         blocks[number] = value[...]
     group = iota((CB, 128), 1) // CB
     for slot in range(SLOTS):
-        back, rank = table[6, slot], table[7, slot]
+        back, rank = place_of(table, slot)
         for x in range(CB):
             row = (x % deep) * CB
             patch = blocks[back, row : row + CB, :]
@@ -393,29 +410,33 @@
     return jnp.concatenate([heat[0], heat[1]], axis=1).reshape(SLOTS, TE, PLANE)
 
 
-def gather_ghosts(table, got, own, all_records, ghosts):
-    records = all_records.shape[0] - 2 * SLOTS
+def gather_ghosts(table, got, own, own_edges, planes, edges, ghosts, ghost_edges):
+    records = planes.shape[0] - 2 * SLOTS
     cap = records // len(got)
-    for number, value in enumerate(got):
-        all_records[number * cap : number * cap + cap] = value[0 : cap * REC, :].reshape(cap, REC, 128)
-    all_records[records : records + 2 * SLOTS] = own[...]
+    for record in range(records):
+        value, row = got[record // cap], record % cap * REC
+        planes[record] = value[row : row + TE, :]
+        edges[record * 8 : record * 8 + 8, :] = value[row + TE : row + REC, :]
+    planes[records:] = own[...]
+    edges[records * 8 :, :] = own_edges[...]
     for slot in range(SLOTS):
-        out, edge = merge_record(all_records, lambda face: table[face, slot])
-        ghosts[slot, 0:TE, :] = out
-        ghosts[slot, TE:REC, :] = edge
-
-
-def ghost_shares(ghosts, places):
-    beside = jnp.concatenate(halves(ghosts[:, 0:TE, :].reshape(SLOTS * TE, 128)), axis=1)
+        out, edge = merge_record(planes, edges, lambda face: table[0, face * SLOTS + slot])
+        ghosts[slot] = out
+        ghost_edges[slot] = edge
+
+
+def ghost_shares(ghosts, ghost_edges, places):
+    beside = jnp.concatenate(halves(ghosts[...].reshape(SLOTS * TE, 128)), axis=1)
     beside = dot(beside, places)
-    row = iota((SLOTS, TE, PLANE), 1)
+    rows = iota((SLOTS, TE, PLANE), 1)
     shares = []
     for number in range(2):
         share = beside[:, number * PLANE : number * PLANE + PLANE].reshape(SLOTS, TE, PLANE)
         for face, at_row in ((0, 0), (1, TE - 1)):
-            at = TE + face * 4 + number * 2
-            side = jnp.concatenate([ghosts[:, at : at + 1, :], ghosts[:, at + 1 : at + 2, :]], axis=2)
-            share += jnp.where(row == at_row, side, 0.0)
+            at = face * 4 + number * 2
+            side = [ghost_edges[:, row : row + 1, :] for row in (at, at + 1)]
+            side = jnp.concatenate(side, axis=2)
+            share += jnp.where(rows == at_row, side, 0.0)
         shares.append(share)
     return shares
 
@@ -433,22 +454,22 @@
     phase_out[...], solute_out[...] = inner_step(phase[...], solute[...], heat, stencil[...])
 
 
-def first_step_kernel(cap, table, old_phase, phase, solute, own, picks, places, spreads, *rest):
+def first_step_kernel(cap, table, old_phase, phase, solute, own, own_edges, picks, places, spreads, *rest):
     others = lax.axis_size("gx") - 1
     found, got, rest = rest[: others + 1], rest[others + 1 : 2 * others + 1], rest[2 * others + 1 :]
-    phase_out, solute_out, heat_out, own_out, *rest = rest
-    send, (all_records, ghosts, blocks, held) = rest[:others], rest[others:]
+    phase_out, solute_out, heat_out, own_out, edges_out, *rest = rest
+    send, (*records, ghosts, ghost_edges, rows, blocks, held) = rest[:others], rest[others:]
     take_heat(cap, table, found, spreads[...], blocks, held, heat_out)
-    gather_ghosts(table, got, own, all_records, ghosts)
+    gather_ghosts(table, got, own, own_edges, *records, ghosts, ghost_edges)
     squared = 1.0 - old_phase[...] * old_phase[...]
     heat_share = (-ORDER_SPEED * COUPLING) * wide_heat(heat_out) * squared * squared
     new_phase, new_solute = add_shares(
-        phase[...], solute[...], ghost_shares(ghosts, places[...]), heat_share
+        phase[...], solute[...], ghost_shares(ghosts, ghost_edges, places[...]), heat_share
     )
     phase_out[...] = new_phase
     solute_out[...] = new_solute
-    write_records(new_phase, new_solute, picks[...], own_out)
-    pack(own_out, table, send)
+    write_records(new_phase, new_solute, picks[...], own_out, edges_out, rows)
+    pack(own_out, edges_out, table, send)
 
 
 def write_out_kernel(value, out, sem):
@@ -457,24 +478,24 @@
     copy.wait()
 
 
-def middle_step_kernel(table, phase, solute, own, picks, places, *rest):
+def middle_step_kernel(table, phase, solute, own, own_edges, picks, places, *rest):
     others = lax.axis_size("gx") - 1
-    got, (phase_out, solute_out, own_out, *rest) = rest[:others], rest[others:]
-    send, (all_records, ghosts) = rest[:others], rest[others:]
-    gather_ghosts(table, got, own, all_records, ghosts)
-    new_phase, new_solute = add_shares(phase[...], solute[...], ghost_shares(ghosts, places[...]))
+    got, (phase_out, solute_out, own_out, edges_out, *rest) = rest[:others], rest[others:]
+    send, (*records, ghosts, ghost_edges, rows) = rest[:others], rest[others:]
+    gather_ghosts(table, got, own, own_edges, *records, ghosts, ghost_edges)
+    new_phase, new_solute = add_shares(phase[...], solute[...], ghost_shares(ghosts, ghost_edges, places[...]))
     phase_out[...] = new_phase
     solute_out[...] = new_solute
-    write_records(new_phase, new_solute, picks[...], own_out)
-    pack(own_out, table, send)
-
-
-def last_step_kernel(table, phase, solute, own, places, *rest):
+    write_records(new_phase, new_solute, picks[...], own_out, edges_out, rows)
+    pack(own_out, edges_out, table, send)
+
+
+def last_step_kernel(table, phase, solute, own, own_edges, places, *rest):
     others = lax.axis_size("gx") - 1
-    got, (phase_out, solute_out, all_records, ghosts) = rest[:others], rest[others:]
-    gather_ghosts(table, got, own, all_records, ghosts)
+    got, (phase_out, solute_out, *records, ghosts, ghost_edges, _) = rest[:others], rest[others:]
+    gather_ghosts(table, got, own, own_edges, *records, ghosts, ghost_edges)
     phase_out[...], solute_out[...] = add_shares(
-        phase[...], solute[...], ghost_shares(ghosts, places[...])
+        phase[...], solute[...], ghost_shares(ghosts, ghost_edges, places[...])
     )
 
 
@@ -504,10 +525,15 @@
     picks, stencil, places, spreads = tables()
 
     integers = functools.partial(jax.ShapeDtypeStruct, dtype=jnp.int32)
-    sides, table, *asked = call(
+    sides, table, asked, *farther = call(
         functools.partial(sides_kernel, sizes, plane_cap),
         [ANY] * 5,
-        [shape(sizes[0] * sizes[1], 3 * bx, 128), integers((8, 128)), *[shape(8, 128)] * count],
+        [
+            shape(sizes[0] * sizes[1], 3 * bx, 128),
+            integers((table_sizes(count, plane_cap)[2], 128)),
+            shape(count, 128),
+            *[shape(8, 128)] * (count - 3),
+        ],
         [
             pltpu.VMEM((1, SLOTS), jnp.int32),
             pltpu.VMEM((1, SLOTS), jnp.int32),
@@ -532,22 +558,28 @@
     def exchange(values):
         return [pass_on(value, shift) for shift, value in enumerate(values, 1)]
 
-    farther = [pass_on(asked[shift], shift) for shift in range(2, others)]
+    farther = [pass_on(value, shift) for shift, value in enumerate(farther, 2)]
 
     phase_field = phase.reshape(SLOTS, TE, PLANE)
     solute_field = solute.reshape(SLOTS, TE, PLANE)
-    own_shape, send_shapes = shape(2 * SLOTS, REC, 128), [shape(plane_cap * REC, 128)] * others
-    own, *packed = call(first_pack_kernel, [SMEM] + [VMEM] * 3, [own_shape, *send_shapes])(
-        table, phase_field, solute_field, picks
-    )
+    own_shapes = [shape(2 * SLOTS, TE, 128), shape(2 * SLOTS * 8, 128)]
+    send_shapes = [shape(plane_cap * REC, 128)] * others
+    rows_scratch = pltpu.VMEM((4, SLOTS * TE, 128), F32)
+    packed = call(
+        first_pack_kernel,
+        [SMEM] + [VMEM] * 4,
+        [*own_shapes, shape(count, 128), *send_shapes],
+        [rows_scratch],
+    )(table, asked, phase_field, solute_field, picks)
+    own, asked, packed = packed[:2], packed[2], packed[3:]
 
     layer = shape(3 * by + 8, bz)
     down, up = call(
-        functools.partial(layers_kernel, sizes), [VMEM] * 5 + [ANY] * (1 + len(farther)), [layer, layer]
-    )(enthalpy, conductivity, sides, asked[1], asked[others], packed[0], *farther)
+        functools.partial(layers_kernel, sizes), [VMEM] * 4 + [ANY] * len(farther), [layer, layer]
+    )(enthalpy, conductivity, sides, asked, *farther)
     from_low, from_high = pass_on(up, 1), pass_on(down, others)
     row = 3 * by + 4
-    request = [asked[0][0], from_low[row], *[value[0] for value in farther], from_high[row]]
+    request = [asked[0], from_low[row], *[value[0] for value in farther], from_high[row]]
     request = jnp.stack([value[:block_cap] for value in request]).astype(jnp.int32)
     _, deep = block_layout(block_cap)
     brick = shape(bx, by, bz)
@@ -563,8 +595,11 @@
 
     field = shape(SLOTS, TE, PLANE)
     step_scratch = [
-        pltpu.VMEM((records + 2 * SLOTS, REC, 128), F32),
-        pltpu.VMEM((SLOTS, REC, 128), F32),
+        pltpu.VMEM((records + 2 * SLOTS, TE, 128), F32),
+        pltpu.VMEM(((records + 2 * SLOTS) * 8, 128), F32),
+        pltpu.VMEM((SLOTS, TE, 128), F32),
+        pltpu.VMEM((SLOTS, 8, 128), F32),
+        rows_scratch,
     ]
     def inner(phase_field, solute_field, *heat):
         return call(
@@ -572,30 +607,32 @@
         )(phase_field, solute_field, stencil, *heat)
 
     inner_fields = inner(phase_field, solute_field)
-    phase_field, solute_field, heat, own, *send = call(
+    phase_field, solute_field, heat, *rest = call(
         functools.partial(first_step_kernel, block_cap),
-        [SMEM] + [VMEM] * (7 + count + others),
-        [field, field, shape(2, SLOTS * TE, 128), own_shape, *send_shapes],
+        [SMEM] + [VMEM] * (8 + count + others),
+        [field, field, shape(2, SLOTS * TE, 128), *own_shapes, *send_shapes],
         step_scratch
         + [
             pltpu.VMEM((count, deep * CB, 128), F32),
             pltpu.VMEM((SLOTS * CB, CB, 128), F32),
         ],
-    )(table, phase_field, *inner_fields, own, picks, places, spreads, *found, *got)
+    )(table, phase_field, *inner_fields, *own, picks, places, spreads, *found, *got)
+    own, send = rest[:2], rest[2:]
     for _ in range(PHASE_STEPS - 2):
         got = exchange(send)
         inner_fields = inner(phase_field, solute_field, heat)
-        phase_field, solute_field, own, *send = call(
+        phase_field, solute_field, *rest = call(
             middle_step_kernel,
-            [SMEM] + [VMEM] * (5 + others),
-            [field, field, own_shape, *send_shapes],
+            [SMEM] + [VMEM] * (6 + others),
+            [field, field, *own_shapes, *send_shapes],
             step_scratch,
-        )(table, *inner_fields, own, picks, places, *got)
+        )(table, *inner_fields, *own, picks, places, *got)
+        own, send = rest[:2], rest[2:]
     got = exchange(send)
     inner_fields = inner(phase_field, solute_field, heat)
     phase_field, solute_field = call(
-        last_step_kernel, [SMEM] + [VMEM] * (4 + others), [field, field], step_scratch
-    )(table, *inner_fields, own, places, *got)
+        last_step_kernel, [SMEM] + [VMEM] * (5 + others), [field, field], step_scratch
+    )(table, *inner_fields, *own, places, *got)
     return heat_out, phase_field.reshape(phase.shape), solute_field.reshape(solute.shape)
 
 

time: 63.2 us -> 63.7 us (level)
  starting transfers between devices: 33.3 us -> 34.3 us
    ppermute x18, starting transfers between devices: 28.1 us -> 29.1 us  [pass_on(): lax.ppermute(value, 'gx', [(i, (i + shift) % count) for i in range(count)])]
    slice x4, local copies, waits for them, and re-layouts: 0.7 us -> 0.01 us  [local(): value[:block_cap]]
    ppermute x18, waiting for transfers between devices: 11.6 us -> 12.2 us  [pass_on(): lax.ppermute(value, 'gx', [(i, (i + shift) % count) for i in range(count)])]
    unnamed x28 -> x26, local copies, waits for them, and re-layouts: 2.56 us -> 2.63 us
  transfers between devices with their start and end apart: 19 -> 19, of which waited for: 11 -> 11; matrix products, arithmetic and copies ran while one was open for 1% -> 0% of each run, Pallas kernels for 9% -> 9%
where the time goes in v12:
time: 63.7 us; the launch traced here: 63.4 us
  starting transfers between devices  34.3 us (54%)
  Pallas kernels  13.4 us (21%)
  waiting for transfers between devices  12.2 us (19%)
  local copies, waits for them, and re-layouts  2.64 us (4%)
  between operations  0.85 us (1%)
    ppermute x18, starting transfers between devices, pass_on(): lax.ppermute(value, 'gx', [(i, (i + shift) % count) for i in range(count)])  29.1 us
    ppermute x18, waiting for transfers between devices, pass_on(): lax.ppermute(value, 'gx', [(i, (i + shift) % count) for i in range(count)])  12.2 us
    all_to_all x1, starting transfers between devices, local(): lax.all_to_all(sides, ('gy', 'gz'), split_axis=0, concat_axis=0, tiled=True)  5.18 us
    unnamed x26, local copies, waits for them, and re-layouts  2.63 us
    pallas_call x2, Pallas kernels, local(): call(middle_step_kernel, [SMEM] + [VMEM] * (6 + others), [field, field, *...  2.44 us
    pallas_call x1, Pallas kernels, local(): call(functools.partial(sides_kernel, sizes, plane_cap), [ANY] * 5, [shape...  2.21 us
    pallas_call x4, Pallas kernels, inner(): call(functools.partial(inner_kernel, bool(heat)), [VMEM] * (3 + len(heat)...  1.96 us
    pallas_call x1, Pallas kernels, local(): call(functools.partial(heat_kernel, block_cap, sizes), [SMEM] + [VMEM] *...  1.91 us
  transfers between devices with their start and end apart: 19, of which 11 were waited for; matrix products, arithmetic and copies ran while one was open for 0% of the time, Pallas kernels for 9%

profile of v12, /device:TPU:0, one launch (start us, length us, event | category | flops | bytes accessed | tf_op | source)
XLA Modules:
  0.0 63.4 jit_solution(11271791123970972882)
XLA Ops:
  0.6 0.0 copy-start.1
  0.6 2.2 %shard_map.130 = (f32[8,24,128]{2,1,0:T(8,128)}, s32[2,128]{1,0:T(2,128)}, f32[4,128]{1,0:T(4,128)}, f32[8,128]{1,0:T(8,128)}) custom-call(s32[1,16]{1,0:T(1,128)} %bitcast.15, s32[1,16]{1,0:T(1,128)} %bitcast.16, s32[6,1,16]{2,1,0:T(1,128)} %bitcast.14, f32[8,32,128]{2,1,0:T(8,128)} %h.3, f32[8,32,128]{2,1,0:T(8,128)} %k.3), custom_call_target="tpu_custom_call" | custom-call | tf_op jit(solution)/shard_map/pallas_call | solution.py:528
  2.9 0.0 copy-start.12
  2.9 5.2 %all-to-all-start = ((f32[8,24,128]{2,1,0:T(8,128)}), f32[8,24,128]{2,1,0:T(8,128)S(1)}, u32[]{:S(2)}, u32[]{:S(2)}) async-start(f32[8,24,128]{2,1,0:T(8,128)} %get-tuple-element.55), calls=%async_computation | async-start | bytes 196608 | tf_op jit(solution)/shard_map/all_to_all | solution.py:553
  8.1 0.0 copy-done.12
  8.1 2.7 %collective-permute-start = (f32[8,128]{1,0:T(8,128)S(1)}, f32[8,128]{1,0:T(8,128)S(1)}, u32[]{:S(2)}, u32[]{:S(2)}) collective-permute-start(f32[8,128]{1,0:T(8,128)S(1)} %copy-done.12), channel_id=1, source_target_pairs={{0,16},{8,24},{16,0},{24,8},{1,17},{9,25},{17,1},{25,9},{2,18},{10... | collective-permute-start | bytes 12296 | tf_op jit(solution)/shard_map/ppermute | solution.py:556
  10.7 0.0 copy-done.1
  10.7 0.7 %copy-done.11 = f32[4,128]{1,0:T(4,128)S(1)} copy-done((f32[4,128]{1,0:T(4,128)S(1)}, f32[4,128]{1,0:T(4,128)}, u32[]{:S(2)}) %copy-start.11) | copy-done | bytes 2072
  11.4 0.0 copy-done.10
  11.4 0.9 %copy-done.2 = f32[1,1,1,16,16,256]{5,4,3,2,1,0:T(8,128)S(1)} copy-done((f32[1,1,1,16,16,256]{5,4,3,2,1,0:T(8,128)S(1)}, f32[1,1,1,16,16,256]{5,4,3,2,1,0:T(8,128)}, u32[]{:S(2)}) %copy-start.2) | copy-done | bytes 262168
  12.4 0.9 %copy-done.7 = f32[1,1,1,16,16,256]{5,4,3,2,1,0:T(8,128)S(1)} copy-done((f32[1,1,1,16,16,256]{5,4,3,2,1,0:T(8,128)S(1)}, f32[1,1,1,16,16,256]{5,4,3,2,1,0:T(8,128)}, u32[]{:S(2)}) %copy-start.7) | copy-done | bytes 262168
  13.3 0.9 %shard_map.131 = (f32[32,16,128]{2,1,0:T(8,128)S(1)}, f32[256,128]{1,0:T(8,128)S(1)}, f32[4,128]{1,0:T(4,128)S(1)}, f32[144,128]{1,0:T(8,128)S(1)}, f32[144,128]{1,0:T(8,128)S(1)}, /*index=5*/f32[144,128]{1,0:T(8,128)S(1)}) custom-call(s32[2,128]{1,0:T(2,128)S(1)} %copy-done.10, f32[4,128]{1,0:T(4,128)S(1)} %copy-done.11, f32[16,16,256]{2,1,0:T(8,128)S(1)} %bitcast.9, ...), custom_call_target="tpu_custom_call" | custom-call | tf_op jit(solution)/shard_map/pallas_call | solution.py:568
  14.2 0.0 collective-permute-done.rest_0_
  14.2 0.0 all-to-all-done.got
  14.3 0.0 copy-done.5
  14.3 0.0 copy-done.6
  14.3 0.0 copy-start.8
  14.3 0.0 copy-start.3
  14.3 1.6 %collective-permute-start.1 = (f32[104,128]{1,0:T(8,128)S(1)}, f32[104,128]{1,0:T(8,128)S(1)}, u32[]{:S(2)}, u32[]{:S(2)}) collective-permute-start(f32[104,128]{1,0:T(8,128)S(1)} %get-tuple-element.57), channel_id=1, source_target_pairs={{0,8},{8,16},{16,24},{24,0},{1,9},{9,17},{17,25},{25,1},{2,10},{10... | collective-permute-start | bytes 159752 | tf_op jit(solution)/shard_map/ppermute | solution.py:556
  16.0 2.2 %collective-permute-start.2 = (f32[104,128]{1,0:T(8,128)S(1)}, f32[104,128]{1,0:T(8,128)S(1)}, u32[]{:S(2)}, u32[]{:S(2)}) collective-permute-start(f32[104,128]{1,0:T(8,128)S(1)} %get-tuple-element.58), channel_id=1, source_target_pairs={{0,24},{8,0},{16,8},{24,16},{1,25},{9,1},{17,9},{25,17},{2,26},{10... | collective-permute-start | bytes 159752 | tf_op jit(solution)/shard_map/ppermute | solution.py:556
  18.2 0.0 collective-permute-start.6
  18.2 1.3 %collective-permute-start.7 = (f32[144,128]{1,0:T(8,128)S(1)}, f32[144,128]{1,0:T(8,128)S(1)}, u32[]{:S(2)}, u32[]{:S(2)}) collective-permute-start(f32[144,128]{1,0:T(8,128)S(1)} %get-tuple-element.69), channel_id=1, source_target_pairs={{0,16},{8,24},{16,0},{24,8},{1,17},{9,25},{17,1},{25,9},{2,18},{10... | collective-permute-start | bytes 221192 | tf_op jit(solution)/shard_map/ppermute | solution.py:556
  19.5 2.5 %collective-permute-start.8 = (f32[144,128]{1,0:T(8,128)S(1)}, f32[144,128]{1,0:T(8,128)S(1)}, u32[]{:S(2)}, u32[]{:S(2)}) collective-permute-start(f32[144,128]{1,0:T(8,128)S(1)} %get-tuple-element.70), channel_id=1, source_target_pairs={{0,24},{8,0},{16,8},{24,16},{1,25},{9,1},{17,9},{25,17},{2,26},{10... | collective-permute-start | bytes 221192 | tf_op jit(solution)/shard_map/ppermute | solution.py:556
  22.0 0.0 collective-permute-done.1.low
  22.0 0.0 collective-permute-done.2.high
  22.1 0.0 copy-start.4
  22.1 1.9 %shard_map.133 = (f32[8,32,128]{2,1,0:T(8,128)S(1)}, f32[32,128]{1,0:T(8,128)S(1)}, f32[32,128]{1,0:T(8,128)S(1)}, f32[32,128]{1,0:T(8,128)S(1)}, f32[32,128]{1,0:T(8,128)S(1)}) custom-call(s32[4,8]{1,0:T(4,128)S(1)} %maximum_convert_fusion.request, f32[8,32,128]{2,1,0:T(8,128)S(1)} %copy-done.5, f32[8,32,128]{2,1,0:T(8,128)S(1)} %copy-done.6, ...), custom_call_target="tpu_custom_call" | custom-call | tf_op jit(solution)/shard_map/pallas_call | solution.py:587
  24.0 0.6 collective-permute-start.3
  24.6 2.6 %collective-permute-start.4 = (f32[32,128]{1,0:T(8,128)S(1)}, f32[32,128]{1,0:T(8,128)S(1)}, u32[]{:S(2)}, u32[]{:S(2)}) collective-permute-start(f32[32,128]{1,0:T(8,128)S(1)} %get-tuple-element.66), channel_id=1, source_target_pairs={{0,16},{8,24},{16,0},{24,8},{1,17},{9,25},{17,1},{25,9},{2,18},{10... | collective-permute-start | bytes 49160 | tf_op jit(solution)/shard_map/ppermute | solution.py:556
  27.3 0.0 collective-permute-done.6.rest_4_
  27.3 1.7 %collective-permute-start.5 = (f32[32,128]{1,0:T(8,128)S(1)}, f32[32,128]{1,0:T(8,128)S(1)}, u32[]{:S(2)}, u32[]{:S(2)}) collective-permute-start(f32[32,128]{1,0:T(8,128)S(1)} %get-tuple-element.67), channel_id=1, source_target_pairs={{0,24},{8,0},{16,8},{24,16},{1,25},{9,1},{17,9},{25,17},{2,26},{10... | collective-permute-start | bytes 49160 | tf_op jit(solution)/shard_map/ppermute | solution.py:556
  29.0 0.0 copy-done.8
  29.0 0.5 shard_map.135
  29.5 0.0 collective-permute-done.7.rest_5_
  29.5 0.0 collective-permute-done.8.rest_6_
  29.5 0.1 collective-permute-done.3.rest_1_
  29.6 0.0 collective-permute-done.4.rest_2_
  29.6 1.4 %collective-permute-done.5.rest_3_ = f32[32,128]{1,0:T(8,128)S(1)} collective-permute-done((f32[32,128]{1,0:T(8,128)S(1)}, f32[32,128]{1,0:T(8,128)S(1)}, u32[]{:S(2)}, u32[]{:S(2)}) %collective-permute-start.5) | collective-permute-done | bytes 16416 | tf_op jit(solution)/shard_map/ppermute | solution.py:556
  31.0 1.7 %shard_map.136 = (f32[16,16,256]{2,1,0:T(8,128)S(1)}, f32[16,16,256]{2,1,0:T(8,128)S(1)}, f32[2,256,128]{2,1,0:T(8,128)S(1)}, f32[32,16,128]{2,1,0:T(8,128)S(1)}...) custom-call(s32[2,128]{1,0:T(2,128)S(1)} %copy-done.10, ...), custom_call_target="tpu_custom_call" | custom-call | tf_op jit(solution)/shard_map/pallas_call | solution.py:610
  32.7 1.2 %collective-permute-start.9 = (f32[144,128]{1,0:T(8,128)S(1)}, f32[144,128]{1,0:T(8,128)S(1)}, u32[]{:S(2)}, u32[]{:S(2)}) collective-permute-start(f32[144,128]{1,0:T(8,128)S(1)} %get-tuple-element.78), channel_id=1, source_target_pairs={{0,8},{8,16},{16,24},{24,0},{1,9},{9,17},{17,25},{25,1},{2,10},{10... | collective-permute-start | bytes 221192 | tf_op jit(solution)/shard_map/ppermute | solution.py:556
  33.9 2.9 %collective-permute-start.10 = (f32[144,128]{1,0:T(8,128)S(1)}, f32[144,128]{1,0:T(8,128)S(1)}, u32[]{:S(2)}, u32[]{:S(2)}) collective-permute-start(f32[144,128]{1,0:T(8,128)S(1)} %get-tuple-element.79), channel_id=1, source_target_pairs={{0,16},{8,24},{16,0},{24,8},{1,17},{9,25},{17,1},{25,9},{2,18},{10... | collective-permute-start | bytes 221192 | tf_op jit(solution)/shard_map/ppermute | solution.py:556
  36.8 0.0 collective-permute-start.11
  36.8 0.5 shard_map.137
  37.3 1.6 %collective-permute-done.9.rest_0_ = f32[144,128]{1,0:T(8,128)S(1)} collective-permute-done((f32[144,128]{1,0:T(8,128)S(1)}, f32[144,128]{1,0:T(8,128)S(1)}, u32[]{:S(2)}, u32[]{:S(2)}) %collective-permute-start.9) | collective-permute-done | bytes 73760 | tf_op jit(solution)/shard_map/ppermute | solution.py:556
  38.9 1.5 %collective-permute-done.10.rest_1_ = f32[144,128]{1,0:T(8,128)S(1)} collective-permute-done((f32[144,128]{1,0:T(8,128)S(1)}, f32[144,128]{1,0:T(8,128)S(1)}, u32[]{:S(2)}, u32[]{:S(2)}) %collective-permute-start.10) | collective-permute-done | bytes 73760 | tf_op jit(solution)/shard_map/ppermute | solution.py:556
  40.5 0.8 %collective-permute-done.11.rest_2_ = f32[144,128]{1,0:T(8,128)S(1)} collective-permute-done((f32[144,128]{1,0:T(8,128)S(1)}, f32[144,128]{1,0:T(8,128)S(1)}, u32[]{:S(2)}, u32[]{:S(2)}) %collective-permute-start.11) | collective-permute-done | bytes 73760 | tf_op jit(solution)/shard_map/ppermute | solution.py:556
  41.3 1.2 %shard_map.138 = (f32[16,16,256]{2,1,0:T(8,128)S(1)}, f32[16,16,256]{2,1,0:T(8,128)S(1)}, f32[32,16,128]{2,1,0:T(8,128)S(1)}, f32[256,128]{1,0:T(8,128)S(1)}, f3...) custom-call(s32[2,128]{1,0:T(2,128)S(1)} %copy-done.10, ...), custom_call_target="tpu_custom_call" | custom-call | tf_op jit(solution)/shard_map/pallas_call | solution.py:624
  42.5 0.6 collective-permute-start.12
  43.1 2.7 %collective-permute-start.13 = (f32[144,128]{1,0:T(8,128)S(1)}, f32[144,128]{1,0:T(8,128)S(1)}, u32[]{:S(2)}, u32[]{:S(2)}) collective-permute-start(f32[144,128]{1,0:T(8,128)S(1)} %get-tuple-element.88), channel_id=1, source_target_pairs={{0,16},{8,24},{16,0},{24,8},{1,17},{9,25},{17,1},{25,9},{2,18},{10... | collective-permute-start | bytes 221192 | tf_op jit(solution)/shard_map/ppermute | solution.py:556
  45.8 0.6 collective-permute-start.14
  46.4 0.5 shard_map.139
  46.9 1.9 %collective-permute-done.12.rest_0_ = f32[144,128]{1,0:T(8,128)S(1)} collective-permute-done((f32[144,128]{1,0:T(8,128)S(1)}, f32[144,128]{1,0:T(8,128)S(1)}, u32[]{:S(2)}, u32[]{:S(2)}) %collective-permute-start.12) | collective-permute-done | bytes 73760 | tf_op jit(solution)/shard_map/ppermute | solution.py:556
  48.8 1.3 %collective-permute-done.13.rest_1_ = f32[144,128]{1,0:T(8,128)S(1)} collective-permute-done((f32[144,128]{1,0:T(8,128)S(1)}, f32[144,128]{1,0:T(8,128)S(1)}, u32[]{:S(2)}, u32[]{:S(2)}) %collective-permute-start.13) | collective-permute-done | bytes 73760 | tf_op jit(solution)/shard_map/ppermute | solution.py:556
  50.0 0.4 collective-permute-done.14.rest_2_
  50.5 1.2 %shard_map.140 = (f32[16,16,256]{2,1,0:T(8,128)S(1)}, f32[16,16,256]{2,1,0:T(8,128)S(1)}, f32[32,16,128]{2,1,0:T(8,128)S(1)}, f32[256,128]{1,0:T(8,128)S(1)}, f3...) custom-call(s32[2,128]{1,0:T(2,128)S(1)} %copy-done.10, ...), custom_call_target="tpu_custom_call" | custom-call | tf_op jit(solution)/shard_map/pallas_call | solution.py:624
  51.7 2.6 %collective-permute-start.15 = (f32[144,128]{1,0:T(8,128)S(1)}, f32[144,128]{1,0:T(8,128)S(1)}, u32[]{:S(2)}, u32[]{:S(2)}) collective-permute-start(f32[144,128]{1,0:T(8,128)S(1)} %get-tuple-element.96), channel_id=1, source_target_pairs={{0,8},{8,16},{16,24},{24,0},{1,9},{9,17},{17,25},{25,1},{2,10},{10... | collective-permute-start | bytes 221192 | tf_op jit(solution)/shard_map/ppermute | solution.py:556
  54.3 3.1 %collective-permute-start.16 = (f32[144,128]{1,0:T(8,128)S(1)}, f32[144,128]{1,0:T(8,128)S(1)}, u32[]{:S(2)}, u32[]{:S(2)}) collective-permute-start(f32[144,128]{1,0:T(8,128)S(1)} %get-tuple-element.97), channel_id=1, source_target_pairs={{0,16},{8,24},{16,0},{24,8},{1,17},{9,25},{17,1},{25,9},{2,18},{10... | collective-permute-start | bytes 221192 | tf_op jit(solution)/shard_map/ppermute | solution.py:556
  57.4 0.0 collective-permute-start.17
  57.4 0.7 %shard_map.134 = f32[8,32,128]{2,1,0:T(8,128)} custom-call(f32[8,32,128]{2,1,0:T(8,128)S(1)} %get-tuple-element.59.value), custom_call_target="tpu_custom_call" | custom-call | tf_op jit(solution)/shard_map/pallas_call | solution.py:594
  58.1 0.5 shard_map.141
  58.6 0.6 collective-permute-done.15.rest_0_
  59.2 1.6 %collective-permute-done.16.rest_1_ = f32[144,128]{1,0:T(8,128)S(1)} collective-permute-done((f32[144,128]{1,0:T(8,128)S(1)}, f32[144,128]{1,0:T(8,128)S(1)}, u32[]{:S(2)}, u32[]{:S(2)}) %collective-permute-start.16) | collective-permute-done | bytes 73760 | tf_op jit(solution)/shard_map/ppermute | solution.py:556
  60.8 1.0 %collective-permute-done.17.rest_2_ = f32[144,128]{1,0:T(8,128)S(1)} collective-permute-done((f32[144,128]{1,0:T(8,128)S(1)}, f32[144,128]{1,0:T(8,128)S(1)}, u32[]{:S(2)}, u32[]{:S(2)}) %collective-permute-start.17) | collective-permute-done | bytes 73760 | tf_op jit(solution)/shard_map/ppermute | solution.py:556
  61.8 1.6 %shard_map.142 = (f32[16,16,256]{2,1,0:T(8,128)}, f32[16,16,256]{2,1,0:T(8,128)}) custom-call(s32[2,128]{1,0:T(2,128)S(1)} %copy-done.10, f32[16,16,256]{2,1,0:T(8,128)S(1)} %get-tuple-element.92.phase, f32[16,16,256]{2,1,0:T(8,128)S(1)} %get-tuple-element.93.solute, f32[32,16,128]{2,1,0:T(8,128)S(1)} %get-tuple-element.94.own, ...), custom_call_target="tpu_custom_call" | custom-call | tf_op jit(solution)/shard_map/pallas_call | solution.py:633
  (18 shorter events, 0.1 us)
Async XLA Ops:
  0.6 10.1 %copy-start.1 = (bf16[512,256]{1,0:T(8,128)(2,1)S(1)}, bf16[512,256]{1,0:T(8,128)(2,1)}, u32[]{:S(2)}) copy-start(bf16[512,256]{1,0:T(8,128)(2,1)} %constant.8.clone.picks) | copy-start | bytes 786436
  2.9 5.2 %copy-start.12 = (f32[8,128]{1,0:T(8,128)S(1)}, f32[8,128]{1,0:T(8,128)}, u32[]{:S(2)}) copy-start(f32[8,128]{1,0:T(8,128)} %get-tuple-element.56) | copy-start | bytes 12292
  2.9 11.4 %all-to-all-start = ((f32[8,24,128]{2,1,0:T(8,128)}), f32[8,24,128]{2,1,0:T(8,128)S(1)}, u32[]{:S(2)}, u32[]{:S(2)}) async-start(f32[8,24,128]{2,1,0:T(8,128)} %get-tuple-element.55), calls=%async_computation | async-start | bytes 196608 | tf_op jit(solution)/shard_map/all_to_all | solution.py:553
  8.1 6.2 %collective-permute-start = (f32[8,128]{1,0:T(8,128)S(1)}, f32[8,128]{1,0:T(8,128)S(1)}, u32[]{:S(2)}, u32[]{:S(2)}) collective-permute-start(f32[8,128]{1,0:T(8,128)S(1)} %copy-done.12), channel_id=1, source_target_pairs={{0,16},{8,24},{16,0},{24,8},{1,17},{9,25},{17,1},{25,9},{2,18},{10... | collective-permute-start | bytes 12296 | tf_op jit(solution)/shard_map/ppermute | solution.py:556
  10.7 0.7 %copy-start.11 = (f32[4,128]{1,0:T(4,128)S(1)}, f32[4,128]{1,0:T(4,128)}, u32[]{:S(2)}) copy-start(f32[4,128]{1,0:T(4,128)} %get-tuple-element.53.asked) | copy-start | bytes 6148
  10.7 0.7 %copy-start.10 = (s32[2,128]{1,0:T(2,128)S(1)}, s32[2,128]{1,0:T(2,128)}, u32[]{:S(2)}) copy-start(s32[2,128]{1,0:T(2,128)} %get-tuple-element.52.table) | copy-start | bytes 3076
  11.4 0.9 %copy-start.2 = (f32[1,1,1,16,16,256]{5,4,3,2,1,0:T(8,128)S(1)}, f32[1,1,1,16,16,256]{5,4,3,2,1,0:T(8,128)}, u32[]{:S(2)}) copy-start(f32[1,1,1,16,16,256]{5,4,3,2,1,0:T(8,128)} %param.13) | copy-start | bytes 786436
  12.4 0.9 %copy-start.7 = (f32[1,1,1,16,16,256]{5,4,3,2,1,0:T(8,128)S(1)}, f32[1,1,1,16,16,256]{5,4,3,2,1,0:T(8,128)}, u32[]{:S(2)}) copy-start(f32[1,1,1,16,16,256]{5,4,3,2,1,0:T(8,128)} %param.14) | copy-start | bytes 786436
  13.3 1.0 %copy-start.5 = (f32[8,32,128]{2,1,0:T(8,128)S(1)}, f32[8,32,128]{2,1,0:T(8,128)}, u32[]{:S(2)}) copy-start(f32[8,32,128]{2,1,0:T(8,128)} %h.3) | copy-start | bytes 393220
  13.3 1.0 %copy-start.6 = (f32[8,32,128]{2,1,0:T(8,128)S(1)}, f32[8,32,128]{2,1,0:T(8,128)}, u32[]{:S(2)}) copy-start(f32[8,32,128]{2,1,0:T(8,128)} %k.3) | copy-start | bytes 393220
  14.3 14.7 %copy-start.8 = (f32[1,1,1,16,16,256]{5,4,3,2,1,0:T(8,128)S(1)}, f32[1,1,1,16,16,256]{5,4,3,2,1,0:T(8,128)}, u32[]{:S(2)}) copy-start(f32[1,1,1,16,16,256]{5,4,3,2,1,0:T(8,128)} %param.14) | copy-start | bytes 786436
  14.3 14.7 %copy-start.3 = (f32[1,1,1,16,16,256]{5,4,3,2,1,0:T(8,128)S(1)}, f32[1,1,1,16,16,256]{5,4,3,2,1,0:T(8,128)}, u32[]{:S(2)}) copy-start(f32[1,1,1,16,16,256]{5,4,3,2,1,0:T(8,128)} %param.13) | copy-start | bytes 786436
  14.3 7.7 %collective-permute-start.1 = (f32[104,128]{1,0:T(8,128)S(1)}, f32[104,128]{1,0:T(8,128)S(1)}, u32[]{:S(2)}, u32[]{:S(2)}) collective-permute-start(f32[104,128]{1,0:T(8,128)S(1)} %get-tuple-element.57), channel_id=1, source_target_pairs={{0,8},{8,16},{16,24},{24,0},{1,9},{9,17},{17,25},{25,1},{2,10},{10... | collective-permute-start | bytes 159752 | tf_op jit(solution)/shard_map/ppermute | solution.py:556
  16.0 6.1 %collective-permute-start.2 = (f32[104,128]{1,0:T(8,128)S(1)}, f32[104,128]{1,0:T(8,128)S(1)}, u32[]{:S(2)}, u32[]{:S(2)}) collective-permute-start(f32[104,128]{1,0:T(8,128)S(1)} %get-tuple-element.58), channel_id=1, source_target_pairs={{0,24},{8,0},{16,8},{24,16},{1,25},{9,1},{17,9},{25,17},{2,26},{10... | collective-permute-start | bytes 159752 | tf_op jit(solution)/shard_map/ppermute | solution.py:556
  18.2 9.1 %collective-permute-start.6 = (f32[144,128]{1,0:T(8,128)S(1)}, f32[144,128]{1,0:T(8,128)S(1)}, u32[]{:S(2)}, u32[]{:S(2)}) collective-permute-start(f32[144,128]{1,0:T(8,128)S(1)} %get-tuple-element.68), channel_id=1, source_target_pairs={{0,8},{8,16},{16,24},{24,0},{1,9},{9,17},{17,25},{25,1},{2,10},{10... | collective-permute-start | bytes 221192 | tf_op jit(solution)/shard_map/ppermute | solution.py:556
  18.2 11.3 %collective-permute-start.7 = (f32[144,128]{1,0:T(8,128)S(1)}, f32[144,128]{1,0:T(8,128)S(1)}, u32[]{:S(2)}, u32[]{:S(2)}) collective-permute-start(f32[144,128]{1,0:T(8,128)S(1)} %get-tuple-element.69), channel_id=1, source_target_pairs={{0,16},{8,24},{16,0},{24,8},{1,17},{9,25},{17,1},{25,9},{2,18},{10... | collective-permute-start | bytes 221192 | tf_op jit(solution)/shard_map/ppermute | solution.py:556
  19.5 10.0 %collective-permute-start.8 = (f32[144,128]{1,0:T(8,128)S(1)}, f32[144,128]{1,0:T(8,128)S(1)}, u32[]{:S(2)}, u32[]{:S(2)}) collective-permute-start(f32[144,128]{1,0:T(8,128)S(1)} %get-tuple-element.70), channel_id=1, source_target_pairs={{0,24},{8,0},{16,8},{24,16},{1,25},{9,1},{17,9},{25,17},{2,26},{10... | collective-permute-start | bytes 221192 | tf_op jit(solution)/shard_map/ppermute | solution.py:556
  22.1 6.9 %copy-start.4 = (bf16[256,256]{1,0:T(8,128)(2,1)S(1)}, bf16[256,256]{1,0:T(8,128)(2,1)}, u32[]{:S(2)}) copy-start(bf16[256,256]{1,0:T(8,128)(2,1)} %constant.9.clone.stencil) | copy-start | bytes 393220
  24.0 5.6 %collective-permute-start.3 = (f32[32,128]{1,0:T(8,128)S(1)}, f32[32,128]{1,0:T(8,128)S(1)}, u32[]{:S(2)}, u32[]{:S(2)}) collective-permute-start(f32[32,128]{1,0:T(8,128)S(1)} %get-tuple-element.65), channel_id=1, source_target_pairs={{0,8},{8,16},{16,24},{24,0},{1,9},{9,17},{17,25},{25,1},{2,10},{10... | collective-permute-start | bytes 49160 | tf_op jit(solution)/shard_map/ppermute | solution.py:556
  24.6 5.0 %collective-permute-start.4 = (f32[32,128]{1,0:T(8,128)S(1)}, f32[32,128]{1,0:T(8,128)S(1)}, u32[]{:S(2)}, u32[]{:S(2)}) collective-permute-start(f32[32,128]{1,0:T(8,128)S(1)} %get-tuple-element.66), channel_id=1, source_target_pairs={{0,16},{8,24},{16,0},{24,8},{1,17},{9,25},{17,1},{25,9},{2,18},{10... | collective-permute-start | bytes 49160 | tf_op jit(solution)/shard_map/ppermute | solution.py:556
  27.3 3.7 %copy-start = (bf16[256,512]{1,0:T(8,128)(2,1)S(1)}, bf16[256,512]{1,0:T(8,128)(2,1)}, u32[]{:S(2)}) copy-start(bf16[256,512]{1,0:T(8,128)(2,1)} %constant.10.clone.places) | copy-start | bytes 786436
  27.3 3.7 %copy-start.9 = (bf16[256,256]{1,0:T(8,128)(2,1)S(1)}, bf16[256,256]{1,0:T(8,128)(2,1)}, u32[]{:S(2)}) copy-start(bf16[256,256]{1,0:T(8,128)(2,1)} %constant.11.clone.spreads) | copy-start | bytes 393220
  27.3 3.7 %collective-permute-start.5 = (f32[32,128]{1,0:T(8,128)S(1)}, f32[32,128]{1,0:T(8,128)S(1)}, u32[]{:S(2)}, u32[]{:S(2)}) collective-permute-start(f32[32,128]{1,0:T(8,128)S(1)} %get-tuple-element.67), channel_id=1, source_target_pairs={{0,24},{8,0},{16,8},{24,16},{1,25},{9,1},{17,9},{25,17},{2,26},{10... | collective-permute-start | bytes 49160 | tf_op jit(solution)/shard_map/ppermute | solution.py:556
  32.7 6.3 %collective-permute-start.9 = (f32[144,128]{1,0:T(8,128)S(1)}, f32[144,128]{1,0:T(8,128)S(1)}, u32[]{:S(2)}, u32[]{:S(2)}) collective-permute-start(f32[144,128]{1,0:T(8,128)S(1)} %get-tuple-element.78), channel_id=1, source_target_pairs={{0,8},{8,16},{16,24},{24,0},{1,9},{9,17},{17,25},{25,1},{2,10},{10... | collective-permute-start | bytes 221192 | tf_op jit(solution)/shard_map/ppermute | solution.py:556
  33.9 6.6 %collective-permute-start.10 = (f32[144,128]{1,0:T(8,128)S(1)}, f32[144,128]{1,0:T(8,128)S(1)}, u32[]{:S(2)}, u32[]{:S(2)}) collective-permute-start(f32[144,128]{1,0:T(8,128)S(1)} %get-tuple-element.79), channel_id=1, source_target_pairs={{0,16},{8,24},{16,0},{24,8},{1,17},{9,25},{17,1},{25,9},{2,18},{10... | collective-permute-start | bytes 221192 | tf_op jit(solution)/shard_map/ppermute | solution.py:556
  36.8 4.4 %collective-permute-start.11 = (f32[144,128]{1,0:T(8,128)S(1)}, f32[144,128]{1,0:T(8,128)S(1)}, u32[]{:S(2)}, u32[]{:S(2)}) collective-permute-start(f32[144,128]{1,0:T(8,128)S(1)} %get-tuple-element.80), channel_id=1, source_target_pairs={{0,24},{8,0},{16,8},{24,16},{1,25},{9,1},{17,9},{25,17},{2,26},{10... | collective-permute-start | bytes 221192 | tf_op jit(solution)/shard_map/ppermute | solution.py:556
  42.5 6.3 %collective-permute-start.12 = (f32[144,128]{1,0:T(8,128)S(1)}, f32[144,128]{1,0:T(8,128)S(1)}, u32[]{:S(2)}, u32[]{:S(2)}) collective-permute-start(f32[144,128]{1,0:T(8,128)S(1)} %get-tuple-element.87), channel_id=1, source_target_pairs={{0,8},{8,16},{16,24},{24,0},{1,9},{9,17},{17,25},{25,1},{2,10},{10... | collective-permute-start | bytes 221192 | tf_op jit(solution)/shard_map/ppermute | solution.py:556
  43.1 6.9 %collective-permute-start.13 = (f32[144,128]{1,0:T(8,128)S(1)}, f32[144,128]{1,0:T(8,128)S(1)}, u32[]{:S(2)}, u32[]{:S(2)}) collective-permute-start(f32[144,128]{1,0:T(8,128)S(1)} %get-tuple-element.88), channel_id=1, source_target_pairs={{0,16},{8,24},{16,0},{24,8},{1,17},{9,25},{17,1},{25,9},{2,18},{10... | collective-permute-start | bytes 221192 | tf_op jit(solution)/shard_map/ppermute | solution.py:556
  45.8 4.7 %collective-permute-start.14 = (f32[144,128]{1,0:T(8,128)S(1)}, f32[144,128]{1,0:T(8,128)S(1)}, u32[]{:S(2)}, u32[]{:S(2)}) collective-permute-start(f32[144,128]{1,0:T(8,128)S(1)} %get-tuple-element.89), channel_id=1, source_target_pairs={{0,24},{8,0},{16,8},{24,16},{1,25},{9,1},{17,9},{25,17},{2,26},{10... | collective-permute-start | bytes 221192 | tf_op jit(solution)/shard_map/ppermute | solution.py:556
  51.7 7.5 %collective-permute-start.15 = (f32[144,128]{1,0:T(8,128)S(1)}, f32[144,128]{1,0:T(8,128)S(1)}, u32[]{:S(2)}, u32[]{:S(2)}) collective-permute-start(f32[144,128]{1,0:T(8,128)S(1)} %get-tuple-element.96), channel_id=1, source_target_pairs={{0,8},{8,16},{16,24},{24,0},{1,9},{9,17},{17,25},{25,1},{2,10},{10... | collective-permute-start | bytes 221192 | tf_op jit(solution)/shard_map/ppermute | solution.py:556
  54.3 6.4 %collective-permute-start.16 = (f32[144,128]{1,0:T(8,128)S(1)}, f32[144,128]{1,0:T(8,128)S(1)}, u32[]{:S(2)}, u32[]{:S(2)}) collective-permute-start(f32[144,128]{1,0:T(8,128)S(1)} %get-tuple-element.97), channel_id=1, source_target_pairs={{0,16},{8,24},{16,0},{24,8},{1,17},{9,25},{17,1},{25,9},{2,18},{10... | collective-permute-start | bytes 221192 | tf_op jit(solution)/shard_map/ppermute | solution.py:556
  57.4 4.4 %collective-permute-start.17 = (f32[144,128]{1,0:T(8,128)S(1)}, f32[144,128]{1,0:T(8,128)S(1)}, u32[]{:S(2)}, u32[]{:S(2)}) collective-permute-start(f32[144,128]{1,0:T(8,128)S(1)} %get-tuple-element.98), channel_id=1, source_target_pairs={{0,24},{8,0},{16,8},{24,16},{1,25},{9,1},{17,9},{25,17},{2,26},{10... | collective-permute-start | bytes 221192 | tf_op jit(solution)/shard_map/ppermute | solution.py:556

commit v13 on v12

--- a/solution.py
+++ b/solution.py
@@ -410,7 +410,7 @@
     return jnp.concatenate([heat[0], heat[1]], axis=1).reshape(SLOTS, TE, PLANE)
 
 
-def gather_ghosts(table, got, own, own_edges, planes, edges, ghosts, ghost_edges):
+def hold_records(got, own, own_edges, planes, edges):
     records = planes.shape[0] - 2 * SLOTS
     cap = records // len(got)
     for record in range(records):
@@ -419,19 +419,28 @@
         edges[record * 8 : record * 8 + 8, :] = value[row + TE : row + REC, :]
     planes[records:] = own[...]
     edges[records * 8 :, :] = own_edges[...]
-    for slot in range(SLOTS):
+
+
+def place_ghosts(table, planes, edges, ghosts, ghost_edges, tiles):
+    for slot in tiles:
         out, edge = merge_record(planes, edges, lambda face: table[0, face * SLOTS + slot])
         ghosts[slot] = out
         ghost_edges[slot] = edge
 
 
+def gather_ghosts(table, got, own, own_edges, planes, edges, ghosts, ghost_edges):
+    hold_records(got, own, own_edges, planes, edges)
+    place_ghosts(table, planes, edges, ghosts, ghost_edges, range(SLOTS))
+
+
 def ghost_shares(ghosts, ghost_edges, places):
-    beside = jnp.concatenate(halves(ghosts[...].reshape(SLOTS * TE, 128)), axis=1)
+    tiles = ghosts.shape[0]
+    beside = jnp.concatenate(halves(ghosts[...].reshape(tiles * TE, 128)), axis=1)
     beside = dot(beside, places)
-    rows = iota((SLOTS, TE, PLANE), 1)
+    rows = iota((tiles, TE, PLANE), 1)
     shares = []
     for number in range(2):
-        share = beside[:, number * PLANE : number * PLANE + PLANE].reshape(SLOTS, TE, PLANE)
+        share = beside[:, number * PLANE : number * PLANE + PLANE].reshape(tiles, TE, PLANE)
         for face, at_row in ((0, 0), (1, TE - 1)):
             at = face * 4 + number * 2
             side = [ghost_edges[:, row : row + 1, :] for row in (at, at + 1)]
@@ -492,11 +501,23 @@
 
 def last_step_kernel(table, phase, solute, own, own_edges, places, *rest):
     others = lax.axis_size("gx") - 1
-    got, (phase_out, solute_out, *records, ghosts, ghost_edges, _) = rest[:others], rest[others:]
-    gather_ghosts(table, got, own, own_edges, *records, ghosts, ghost_edges)
-    phase_out[...], solute_out[...] = add_shares(
-        phase[...], solute[...], ghost_shares(ghosts, ghost_edges, places[...])
-    )
+    got, (phase_far, solute_far, planes, edges, ghosts, ghost_edges, phase_out, solute_out, sems) = (
+        rest[:others], rest[others:]
+    )
+    hold_records(got, own, own_edges, planes, edges)
+    copies = []
+    step = 4
+    for first in range(0, SLOTS, step):
+        at = pl.ds(first, step)
+        place_ghosts(table, planes, edges, ghosts, ghost_edges, range(first, first + step))
+        shares = ghost_shares(ghosts.at[at], ghost_edges.at[at], places[...])
+        phase_out[at], solute_out[at] = add_shares(phase[at], solute[at], shares)
+        for out, far in ((phase_out, phase_far), (solute_out, solute_far)):
+            copy = pltpu.make_async_copy(out.at[at], far.at[at], sems.at[len(copies)])
+            copy.start()
+            copies.append(copy)
+    for copy in copies:
+        copy.wait()
 
 
 def call(kernel, in_specs, out_shapes, scratch=(), out_specs=None, mib=16):
@@ -556,7 +577,9 @@
         return lax.ppermute(value, "gx", [(i, (i + shift) % count) for i in range(count)])
 
     def exchange(values):
-        return [pass_on(value, shift) for shift, value in enumerate(values, 1)]
+        order = sorted(range(1, count), key=lambda shift: (-min(shift, count - shift), shift))
+        got = {shift: pass_on(values[shift - 1], shift) for shift in order}
+        return [got[shift] for shift in range(1, count)]
 
     farther = [pass_on(value, shift) for shift, value in enumerate(farther, 2)]
 
@@ -631,7 +654,11 @@
     got = exchange(send)
     inner_fields = inner(phase_field, solute_field, heat)
     phase_field, solute_field = call(
-        last_step_kernel, [SMEM] + [VMEM] * (5 + others), [field, field], step_scratch
+        last_step_kernel,
+        [SMEM] + [VMEM] * (5 + others),
+        [field, field],
+        step_scratch[:4] + [pltpu.VMEM(field.shape, F32)] * 2 + [pltpu.SemaphoreType.DMA((8,))],
+        [ANY] * 2,
     )(table, *inner_fields, *own, places, *got)
     return heat_out, phase_field.reshape(phase.shape), solute_field.reshape(solute.shape)
 

time: 63.7 us -> 63.7 us (level)
  no operation moved by 1% of the time
where the time goes in v13:
time: 63.7 us; the launch traced here: 63.3 us
  starting transfers between devices  33.7 us (53%)
  Pallas kernels  13.4 us (21%)
  waiting for transfers between devices  12.7 us (20%)
  local copies, waits for them, and re-layouts  2.65 us (4%)
  between operations  0.85 us (1%)
    ppermute x18, starting transfers between devices, pass_on(): lax.ppermute(value, 'gx', [(i, (i + shift) % count) for i in range(count)])  28.5 us
    ppermute x18, waiting for transfers between devices, pass_on(): lax.ppermute(value, 'gx', [(i, (i + shift) % count) for i in range(count)])  12.7 us
    all_to_all x1, starting transfers between devices, local(): lax.all_to_all(sides, ('gy', 'gz'), split_axis=0, concat_axis=0, tiled=True)  5.18 us
    unnamed x26, local copies, waits for them, and re-layouts  2.64 us
    pallas_call x2, Pallas kernels, local(): call(middle_step_kernel, [SMEM] + [VMEM] * (6 + others), [field, field, *...  2.44 us
    pallas_call x1, Pallas kernels, local(): call(functools.partial(sides_kernel, sizes, plane_cap), [ANY] * 5, [shape...  2.21 us
    pallas_call x4, Pallas kernels, inner(): call(functools.partial(inner_kernel, bool(heat)), [VMEM] * (3 + len(heat)...  1.95 us
    pallas_call x1, Pallas kernels, local(): call(functools.partial(heat_kernel, block_cap, sizes), [SMEM] + [VMEM] *...  1.91 us
  transfers between devices with their start and end apart: 19, of which 11 were waited for; matrix products, arithmetic and copies ran while one was open for 0% of the time, Pallas kernels for 9%

profile of v13, /device:TPU:0, one launch (start us, length us, event | category | flops | bytes accessed | tf_op | source)
XLA Modules:
  0.0 63.3 jit_solution(7268378594255744435)
XLA Ops:
  0.6 0.0 copy-start.1
  0.6 2.2 %shard_map.130 = (f32[8,24,128]{2,1,0:T(8,128)}, s32[2,128]{1,0:T(2,128)}, f32[4,128]{1,0:T(4,128)}, f32[8,128]{1,0:T(8,128)}) custom-call(s32[1,16]{1,0:T(1,128)} %bitcast.15, s32[1,16]{1,0:T(1,128)} %bitcast.16, s32[6,1,16]{2,1,0:T(1,128)} %bitcast.14, f32[8,32,128]{2,1,0:T(8,128)} %h.3, f32[8,32,128]{2,1,0:T(8,128)} %k.3), custom_call_target="tpu_custom_call" | custom-call | tf_op jit(solution)/shard_map/pallas_call | solution.py:549
  2.9 0.0 copy-start.12
  2.9 5.2 %all-to-all-start = ((f32[8,24,128]{2,1,0:T(8,128)}), f32[8,24,128]{2,1,0:T(8,128)S(1)}, u32[]{:S(2)}, u32[]{:S(2)}) async-start(f32[8,24,128]{2,1,0:T(8,128)} %get-tuple-element.55), calls=%async_computation | async-start | bytes 196608 | tf_op jit(solution)/shard_map/all_to_all | solution.py:574
  8.1 0.0 copy-done.12
  8.1 2.7 %collective-permute-start = (f32[8,128]{1,0:T(8,128)S(1)}, f32[8,128]{1,0:T(8,128)S(1)}, u32[]{:S(2)}, u32[]{:S(2)}) collective-permute-start(f32[8,128]{1,0:T(8,128)S(1)} %copy-done.12), channel_id=1, source_target_pairs={{0,16},{8,24},{16,0},{24,8},{1,17},{9,25},{17,1},{25,9},{2,18},{10... | collective-permute-start | bytes 12296 | tf_op jit(solution)/shard_map/ppermute | solution.py:577
  10.7 0.0 copy-done.1
  10.7 0.7 %copy-done.11 = f32[4,128]{1,0:T(4,128)S(1)} copy-done((f32[4,128]{1,0:T(4,128)S(1)}, f32[4,128]{1,0:T(4,128)}, u32[]{:S(2)}) %copy-start.11) | copy-done | bytes 2072
  11.4 0.0 copy-done.10
  11.4 0.9 %copy-done.2 = f32[1,1,1,16,16,256]{5,4,3,2,1,0:T(8,128)S(1)} copy-done((f32[1,1,1,16,16,256]{5,4,3,2,1,0:T(8,128)S(1)}, f32[1,1,1,16,16,256]{5,4,3,2,1,0:T(8,128)}, u32[]{:S(2)}) %copy-start.2) | copy-done | bytes 262168
  12.4 0.9 %copy-done.7 = f32[1,1,1,16,16,256]{5,4,3,2,1,0:T(8,128)S(1)} copy-done((f32[1,1,1,16,16,256]{5,4,3,2,1,0:T(8,128)S(1)}, f32[1,1,1,16,16,256]{5,4,3,2,1,0:T(8,128)}, u32[]{:S(2)}) %copy-start.7) | copy-done | bytes 262168
  13.3 0.9 %shard_map.131 = (f32[32,16,128]{2,1,0:T(8,128)S(1)}, f32[256,128]{1,0:T(8,128)S(1)}, f32[4,128]{1,0:T(4,128)S(1)}, f32[144,128]{1,0:T(8,128)S(1)}, f32[144,128]{1,0:T(8,128)S(1)}, /*index=5*/f32[144,128]{1,0:T(8,128)S(1)}) custom-call(s32[2,128]{1,0:T(2,128)S(1)} %copy-done.10, f32[4,128]{1,0:T(4,128)S(1)} %copy-done.11, f32[16,16,256]{2,1,0:T(8,128)S(1)} %bitcast.9, ...), custom_call_target="tpu_custom_call" | custom-call | tf_op jit(solution)/shard_map/pallas_call | solution.py:591
  14.2 0.0 collective-permute-done.rest_0_
  14.2 0.0 all-to-all-done.got
  14.2 0.0 copy-done.5
  14.3 0.0 copy-done.6
  14.3 0.0 copy-start.8
  14.3 0.0 copy-start.3
  14.3 1.6 %collective-permute-start.1 = (f32[104,128]{1,0:T(8,128)S(1)}, f32[104,128]{1,0:T(8,128)S(1)}, u32[]{:S(2)}, u32[]{:S(2)}) collective-permute-start(f32[104,128]{1,0:T(8,128)S(1)} %get-tuple-element.57), channel_id=1, source_target_pairs={{0,8},{8,16},{16,24},{24,0},{1,9},{9,17},{17,25},{25,1},{2,10},{10... | collective-permute-start | bytes 159752 | tf_op jit(solution)/shard_map/ppermute | solution.py:577
  16.0 2.2 %collective-permute-start.2 = (f32[104,128]{1,0:T(8,128)S(1)}, f32[104,128]{1,0:T(8,128)S(1)}, u32[]{:S(2)}, u32[]{:S(2)}) collective-permute-start(f32[104,128]{1,0:T(8,128)S(1)} %get-tuple-element.58), channel_id=1, source_target_pairs={{0,24},{8,0},{16,8},{24,16},{1,25},{9,1},{17,9},{25,17},{2,26},{10... | collective-permute-start | bytes 159752 | tf_op jit(solution)/shard_map/ppermute | solution.py:577
  18.2 0.0 collective-permute-start.6
  18.2 1.3 %collective-permute-start.7 = (f32[144,128]{1,0:T(8,128)S(1)}, f32[144,128]{1,0:T(8,128)S(1)}, u32[]{:S(2)}, u32[]{:S(2)}) collective-permute-start(f32[144,128]{1,0:T(8,128)S(1)} %get-tuple-element.69), channel_id=1, source_target_pairs={{0,16},{8,24},{16,0},{24,8},{1,17},{9,25},{17,1},{25,9},{2,18},{10... | collective-permute-start | bytes 221192 | tf_op jit(solution)/shard_map/ppermute | solution.py:577
  19.5 2.5 %collective-permute-start.8 = (f32[144,128]{1,0:T(8,128)S(1)}, f32[144,128]{1,0:T(8,128)S(1)}, u32[]{:S(2)}, u32[]{:S(2)}) collective-permute-start(f32[144,128]{1,0:T(8,128)S(1)} %get-tuple-element.70), channel_id=1, source_target_pairs={{0,24},{8,0},{16,8},{24,16},{1,25},{9,1},{17,9},{25,17},{2,26},{10... | collective-permute-start | bytes 221192 | tf_op jit(solution)/shard_map/ppermute | solution.py:577
  22.0 0.0 collective-permute-done.1.low
  22.0 0.0 collective-permute-done.2.high
  22.1 0.0 copy-start.4
  22.1 1.9 %shard_map.133 = (f32[8,32,128]{2,1,0:T(8,128)S(1)}, f32[32,128]{1,0:T(8,128)S(1)}, f32[32,128]{1,0:T(8,128)S(1)}, f32[32,128]{1,0:T(8,128)S(1)}, f32[32,128]{1,0:T(8,128)S(1)}) custom-call(s32[4,8]{1,0:T(4,128)S(1)} %maximum_convert_fusion.request, f32[8,32,128]{2,1,0:T(8,128)S(1)} %copy-done.5, f32[8,32,128]{2,1,0:T(8,128)S(1)} %copy-done.6, ...), custom_call_target="tpu_custom_call" | custom-call | tf_op jit(solution)/shard_map/pallas_call | solution.py:610
  24.0 0.6 collective-permute-start.3
  24.6 2.6 %collective-permute-start.4 = (f32[32,128]{1,0:T(8,128)S(1)}, f32[32,128]{1,0:T(8,128)S(1)}, u32[]{:S(2)}, u32[]{:S(2)}) collective-permute-start(f32[32,128]{1,0:T(8,128)S(1)} %get-tuple-element.66), channel_id=1, source_target_pairs={{0,16},{8,24},{16,0},{24,8},{1,17},{9,25},{17,1},{25,9},{2,18},{10... | collective-permute-start | bytes 49160 | tf_op jit(solution)/shard_map/ppermute | solution.py:577
  27.3 0.0 collective-permute-done.6.rest_4_
  27.3 1.7 %collective-permute-start.5 = (f32[32,128]{1,0:T(8,128)S(1)}, f32[32,128]{1,0:T(8,128)S(1)}, u32[]{:S(2)}, u32[]{:S(2)}) collective-permute-start(f32[32,128]{1,0:T(8,128)S(1)} %get-tuple-element.67), channel_id=1, source_target_pairs={{0,24},{8,0},{16,8},{24,16},{1,25},{9,1},{17,9},{25,17},{2,26},{10... | collective-permute-start | bytes 49160 | tf_op jit(solution)/shard_map/ppermute | solution.py:577
  29.0 0.0 copy-done.8
  29.0 0.5 shard_map.135
  29.5 0.0 collective-permute-done.7.rest_5_
  29.5 0.0 collective-permute-done.8.rest_6_
  29.5 0.1 collective-permute-done.3.rest_1_
  29.6 0.0 collective-permute-done.4.rest_2_
  29.6 1.4 %collective-permute-done.5.rest_3_ = f32[32,128]{1,0:T(8,128)S(1)} collective-permute-done((f32[32,128]{1,0:T(8,128)S(1)}, f32[32,128]{1,0:T(8,128)S(1)}, u32[]{:S(2)}, u32[]{:S(2)}) %collective-permute-start.5) | collective-permute-done | bytes 16416 | tf_op jit(solution)/shard_map/ppermute | solution.py:577
  31.0 1.7 %shard_map.136 = (f32[16,16,256]{2,1,0:T(8,128)S(1)}, f32[16,16,256]{2,1,0:T(8,128)S(1)}, f32[2,256,128]{2,1,0:T(8,128)S(1)}, f32[32,16,128]{2,1,0:T(8,128)S(1)}...) custom-call(s32[2,128]{1,0:T(2,128)S(1)} %copy-done.10, ...), custom_call_target="tpu_custom_call" | custom-call | tf_op jit(solution)/shard_map/pallas_call | solution.py:633
  32.7 1.2 %collective-permute-start.9 = (f32[144,128]{1,0:T(8,128)S(1)}, f32[144,128]{1,0:T(8,128)S(1)}, u32[]{:S(2)}, u32[]{:S(2)}) collective-permute-start(f32[144,128]{1,0:T(8,128)S(1)} %get-tuple-element.78), channel_id=1, source_target_pairs={{0,8},{8,16},{16,24},{24,0},{1,9},{9,17},{17,25},{25,1},{2,10},{10... | collective-permute-start | bytes 221192 | tf_op jit(solution)/shard_map/ppermute | solution.py:577
  33.9 2.9 %collective-permute-start.10 = (f32[144,128]{1,0:T(8,128)S(1)}, f32[144,128]{1,0:T(8,128)S(1)}, u32[]{:S(2)}, u32[]{:S(2)}) collective-permute-start(f32[144,128]{1,0:T(8,128)S(1)} %get-tuple-element.79), channel_id=1, source_target_pairs={{0,16},{8,24},{16,0},{24,8},{1,17},{9,25},{17,1},{25,9},{2,18},{10... | collective-permute-start | bytes 221192 | tf_op jit(solution)/shard_map/ppermute | solution.py:577
  36.8 0.0 collective-permute-start.11
  36.8 0.5 shard_map.137
  37.3 1.6 %collective-permute-done.9.rest_0_ = f32[144,128]{1,0:T(8,128)S(1)} collective-permute-done((f32[144,128]{1,0:T(8,128)S(1)}, f32[144,128]{1,0:T(8,128)S(1)}, u32[]{:S(2)}, u32[]{:S(2)}) %collective-permute-start.9) | collective-permute-done | bytes 73760 | tf_op jit(solution)/shard_map/ppermute | solution.py:577
  39.0 1.5 %collective-permute-done.10.rest_1_ = f32[144,128]{1,0:T(8,128)S(1)} collective-permute-done((f32[144,128]{1,0:T(8,128)S(1)}, f32[144,128]{1,0:T(8,128)S(1)}, u32[]{:S(2)}, u32[]{:S(2)}) %collective-permute-start.10) | collective-permute-done | bytes 73760 | tf_op jit(solution)/shard_map/ppermute | solution.py:577
  40.5 0.8 %collective-permute-done.11.rest_2_ = f32[144,128]{1,0:T(8,128)S(1)} collective-permute-done((f32[144,128]{1,0:T(8,128)S(1)}, f32[144,128]{1,0:T(8,128)S(1)}, u32[]{:S(2)}, u32[]{:S(2)}) %collective-permute-start.11) | collective-permute-done | bytes 73760 | tf_op jit(solution)/shard_map/ppermute | solution.py:577
  41.3 1.2 %shard_map.138 = (f32[16,16,256]{2,1,0:T(8,128)S(1)}, f32[16,16,256]{2,1,0:T(8,128)S(1)}, f32[32,16,128]{2,1,0:T(8,128)S(1)}, f32[256,128]{1,0:T(8,128)S(1)}, f3...) custom-call(s32[2,128]{1,0:T(2,128)S(1)} %copy-done.10, ...), custom_call_target="tpu_custom_call" | custom-call | tf_op jit(solution)/shard_map/pallas_call | solution.py:647
  42.5 0.6 collective-permute-start.12
  43.1 2.7 %collective-permute-start.13 = (f32[144,128]{1,0:T(8,128)S(1)}, f32[144,128]{1,0:T(8,128)S(1)}, u32[]{:S(2)}, u32[]{:S(2)}) collective-permute-start(f32[144,128]{1,0:T(8,128)S(1)} %get-tuple-element.88), channel_id=1, source_target_pairs={{0,16},{8,24},{16,0},{24,8},{1,17},{9,25},{17,1},{25,9},{2,18},{10... | collective-permute-start | bytes 221192 | tf_op jit(solution)/shard_map/ppermute | solution.py:577
  45.8 0.5 collective-permute-start.14
  46.4 0.5 shard_map.139
  46.9 1.9 %collective-permute-done.12.rest_0_ = f32[144,128]{1,0:T(8,128)S(1)} collective-permute-done((f32[144,128]{1,0:T(8,128)S(1)}, f32[144,128]{1,0:T(8,128)S(1)}, u32[]{:S(2)}, u32[]{:S(2)}) %collective-permute-start.12) | collective-permute-done | bytes 73760 | tf_op jit(solution)/shard_map/ppermute | solution.py:577
  48.8 1.3 %collective-permute-done.13.rest_1_ = f32[144,128]{1,0:T(8,128)S(1)} collective-permute-done((f32[144,128]{1,0:T(8,128)S(1)}, f32[144,128]{1,0:T(8,128)S(1)}, u32[]{:S(2)}, u32[]{:S(2)}) %collective-permute-start.13) | collective-permute-done | bytes 73760 | tf_op jit(solution)/shard_map/ppermute | solution.py:577
  50.1 0.9 %collective-permute-done.14.rest_2_ = f32[144,128]{1,0:T(8,128)S(1)} collective-permute-done((f32[144,128]{1,0:T(8,128)S(1)}, f32[144,128]{1,0:T(8,128)S(1)}, u32[]{:S(2)}, u32[]{:S(2)}) %collective-permute-start.14) | collective-permute-done | bytes 73760 | tf_op jit(solution)/shard_map/ppermute | solution.py:577
  51.0 1.2 %shard_map.140 = (f32[16,16,256]{2,1,0:T(8,128)S(1)}, f32[16,16,256]{2,1,0:T(8,128)S(1)}, f32[32,16,128]{2,1,0:T(8,128)S(1)}, f32[256,128]{1,0:T(8,128)S(1)}, f3...) custom-call(s32[2,128]{1,0:T(2,128)S(1)} %copy-done.10, ...), custom_call_target="tpu_custom_call" | custom-call | tf_op jit(solution)/shard_map/pallas_call | solution.py:647
  52.2 2.1 %collective-permute-start.15 = (f32[144,128]{1,0:T(8,128)S(1)}, f32[144,128]{1,0:T(8,128)S(1)}, u32[]{:S(2)}, u32[]{:S(2)}) collective-permute-start(f32[144,128]{1,0:T(8,128)S(1)} %get-tuple-element.96), channel_id=1, source_target_pairs={{0,8},{8,16},{16,24},{24,0},{1,9},{9,17},{17,25},{25,1},{2,10},{10... | collective-permute-start | bytes 221192 | tf_op jit(solution)/shard_map/ppermute | solution.py:577
  54.3 3.0 %collective-permute-start.16 = (f32[144,128]{1,0:T(8,128)S(1)}, f32[144,128]{1,0:T(8,128)S(1)}, u32[]{:S(2)}, u32[]{:S(2)}) collective-permute-start(f32[144,128]{1,0:T(8,128)S(1)} %get-tuple-element.97), channel_id=1, source_target_pairs={{0,16},{8,24},{16,0},{24,8},{1,17},{9,25},{17,1},{25,9},{2,18},{10... | collective-permute-start | bytes 221192 | tf_op jit(solution)/shard_map/ppermute | solution.py:577
  57.4 0.0 collective-permute-start.17
  57.4 0.7 %shard_map.134 = f32[8,32,128]{2,1,0:T(8,128)} custom-call(f32[8,32,128]{2,1,0:T(8,128)S(1)} %get-tuple-element.59.value), custom_call_target="tpu_custom_call" | custom-call | tf_op jit(solution)/shard_map/pallas_call | solution.py:617
  58.0 0.5 shard_map.141
  58.5 0.6 collective-permute-done.15.rest_0_
  59.1 1.6 %collective-permute-done.16.rest_1_ = f32[144,128]{1,0:T(8,128)S(1)} collective-permute-done((f32[144,128]{1,0:T(8,128)S(1)}, f32[144,128]{1,0:T(8,128)S(1)}, u32[]{:S(2)}, u32[]{:S(2)}) %collective-permute-start.16) | collective-permute-done | bytes 73760 | tf_op jit(solution)/shard_map/ppermute | solution.py:577
  60.7 1.0 %collective-permute-done.17.rest_2_ = f32[144,128]{1,0:T(8,128)S(1)} collective-permute-done((f32[144,128]{1,0:T(8,128)S(1)}, f32[144,128]{1,0:T(8,128)S(1)}, u32[]{:S(2)}, u32[]{:S(2)}) %collective-permute-start.17) | collective-permute-done | bytes 73760 | tf_op jit(solution)/shard_map/ppermute | solution.py:577
  61.7 1.6 %shard_map.142 = (f32[16,16,256]{2,1,0:T(8,128)}, f32[16,16,256]{2,1,0:T(8,128)}) custom-call(s32[2,128]{1,0:T(2,128)S(1)} %copy-done.10, f32[16,16,256]{2,1,0:T(8,128)S(1)} %get-tuple-element.92.phase, f32[16,16,256]{2,1,0:T(8,128)S(1)} %get-tuple-element.93.solute, f32[32,16,128]{2,1,0:T(8,128)S(1)} %get-tuple-element.94.own, ...), custom_call_target="tpu_custom_call" | custom-call | tf_op jit(solution)/shard_map/pallas_call | solution.py:656
  (18 shorter events, 0.1 us)
Async XLA Ops:
  0.6 10.1 %copy-start.1 = (bf16[512,256]{1,0:T(8,128)(2,1)S(1)}, bf16[512,256]{1,0:T(8,128)(2,1)}, u32[]{:S(2)}) copy-start(bf16[512,256]{1,0:T(8,128)(2,1)} %constant.8.clone.picks) | copy-start | bytes 786436
  2.9 5.2 %copy-start.12 = (f32[8,128]{1,0:T(8,128)S(1)}, f32[8,128]{1,0:T(8,128)}, u32[]{:S(2)}) copy-start(f32[8,128]{1,0:T(8,128)} %get-tuple-element.56) | copy-start | bytes 12292
  2.9 11.4 %all-to-all-start = ((f32[8,24,128]{2,1,0:T(8,128)}), f32[8,24,128]{2,1,0:T(8,128)S(1)}, u32[]{:S(2)}, u32[]{:S(2)}) async-start(f32[8,24,128]{2,1,0:T(8,128)} %get-tuple-element.55), calls=%async_computation | async-start | bytes 196608 | tf_op jit(solution)/shard_map/all_to_all | solution.py:574
  8.1 6.2 %collective-permute-start = (f32[8,128]{1,0:T(8,128)S(1)}, f32[8,128]{1,0:T(8,128)S(1)}, u32[]{:S(2)}, u32[]{:S(2)}) collective-permute-start(f32[8,128]{1,0:T(8,128)S(1)} %copy-done.12), channel_id=1, source_target_pairs={{0,16},{8,24},{16,0},{24,8},{1,17},{9,25},{17,1},{25,9},{2,18},{10... | collective-permute-start | bytes 12296 | tf_op jit(solution)/shard_map/ppermute | solution.py:577
  10.7 0.7 %copy-start.11 = (f32[4,128]{1,0:T(4,128)S(1)}, f32[4,128]{1,0:T(4,128)}, u32[]{:S(2)}) copy-start(f32[4,128]{1,0:T(4,128)} %get-tuple-element.53.asked) | copy-start | bytes 6148
  10.7 0.7 %copy-start.10 = (s32[2,128]{1,0:T(2,128)S(1)}, s32[2,128]{1,0:T(2,128)}, u32[]{:S(2)}) copy-start(s32[2,128]{1,0:T(2,128)} %get-tuple-element.52.table) | copy-start | bytes 3076
  11.4 0.9 %copy-start.2 = (f32[1,1,1,16,16,256]{5,4,3,2,1,0:T(8,128)S(1)}, f32[1,1,1,16,16,256]{5,4,3,2,1,0:T(8,128)}, u32[]{:S(2)}) copy-start(f32[1,1,1,16,16,256]{5,4,3,2,1,0:T(8,128)} %param.13) | copy-start | bytes 786436
  12.4 0.9 %copy-start.7 = (f32[1,1,1,16,16,256]{5,4,3,2,1,0:T(8,128)S(1)}, f32[1,1,1,16,16,256]{5,4,3,2,1,0:T(8,128)}, u32[]{:S(2)}) copy-start(f32[1,1,1,16,16,256]{5,4,3,2,1,0:T(8,128)} %param.14) | copy-start | bytes 786436
  13.3 0.9 %copy-start.5 = (f32[8,32,128]{2,1,0:T(8,128)S(1)}, f32[8,32,128]{2,1,0:T(8,128)}, u32[]{:S(2)}) copy-start(f32[8,32,128]{2,1,0:T(8,128)} %h.3) | copy-start | bytes 393220
  13.3 1.0 %copy-start.6 = (f32[8,32,128]{2,1,0:T(8,128)S(1)}, f32[8,32,128]{2,1,0:T(8,128)}, u32[]{:S(2)}) copy-start(f32[8,32,128]{2,1,0:T(8,128)} %k.3) | copy-start | bytes 393220
  14.3 14.7 %copy-start.8 = (f32[1,1,1,16,16,256]{5,4,3,2,1,0:T(8,128)S(1)}, f32[1,1,1,16,16,256]{5,4,3,2,1,0:T(8,128)}, u32[]{:S(2)}) copy-start(f32[1,1,1,16,16,256]{5,4,3,2,1,0:T(8,128)} %param.14) | copy-start | bytes 786436
  14.3 14.7 %copy-start.3 = (f32[1,1,1,16,16,256]{5,4,3,2,1,0:T(8,128)S(1)}, f32[1,1,1,16,16,256]{5,4,3,2,1,0:T(8,128)}, u32[]{:S(2)}) copy-start(f32[1,1,1,16,16,256]{5,4,3,2,1,0:T(8,128)} %param.13) | copy-start | bytes 786436
  14.3 7.7 %collective-permute-start.1 = (f32[104,128]{1,0:T(8,128)S(1)}, f32[104,128]{1,0:T(8,128)S(1)}, u32[]{:S(2)}, u32[]{:S(2)}) collective-permute-start(f32[104,128]{1,0:T(8,128)S(1)} %get-tuple-element.57), channel_id=1, source_target_pairs={{0,8},{8,16},{16,24},{24,0},{1,9},{9,17},{17,25},{25,1},{2,10},{10... | collective-permute-start | bytes 159752 | tf_op jit(solution)/shard_map/ppermute | solution.py:577
  16.0 6.1 %collective-permute-start.2 = (f32[104,128]{1,0:T(8,128)S(1)}, f32[104,128]{1,0:T(8,128)S(1)}, u32[]{:S(2)}, u32[]{:S(2)}) collective-permute-start(f32[104,128]{1,0:T(8,128)S(1)} %get-tuple-element.58), channel_id=1, source_target_pairs={{0,24},{8,0},{16,8},{24,16},{1,25},{9,1},{17,9},{25,17},{2,26},{10... | collective-permute-start | bytes 159752 | tf_op jit(solution)/shard_map/ppermute | solution.py:577
  18.2 9.1 %collective-permute-start.6 = (f32[144,128]{1,0:T(8,128)S(1)}, f32[144,128]{1,0:T(8,128)S(1)}, u32[]{:S(2)}, u32[]{:S(2)}) collective-permute-start(f32[144,128]{1,0:T(8,128)S(1)} %get-tuple-element.68), channel_id=1, source_target_pairs={{0,8},{8,16},{16,24},{24,0},{1,9},{9,17},{17,25},{25,1},{2,10},{10... | collective-permute-start | bytes 221192 | tf_op jit(solution)/shard_map/ppermute | solution.py:577
  18.2 11.3 %collective-permute-start.7 = (f32[144,128]{1,0:T(8,128)S(1)}, f32[144,128]{1,0:T(8,128)S(1)}, u32[]{:S(2)}, u32[]{:S(2)}) collective-permute-start(f32[144,128]{1,0:T(8,128)S(1)} %get-tuple-element.69), channel_id=1, source_target_pairs={{0,16},{8,24},{16,0},{24,8},{1,17},{9,25},{17,1},{25,9},{2,18},{10... | collective-permute-start | bytes 221192 | tf_op jit(solution)/shard_map/ppermute | solution.py:577
  19.5 10.0 %collective-permute-start.8 = (f32[144,128]{1,0:T(8,128)S(1)}, f32[144,128]{1,0:T(8,128)S(1)}, u32[]{:S(2)}, u32[]{:S(2)}) collective-permute-start(f32[144,128]{1,0:T(8,128)S(1)} %get-tuple-element.70), channel_id=1, source_target_pairs={{0,24},{8,0},{16,8},{24,16},{1,25},{9,1},{17,9},{25,17},{2,26},{10... | collective-permute-start | bytes 221192 | tf_op jit(solution)/shard_map/ppermute | solution.py:577
  22.1 6.9 %copy-start.4 = (bf16[256,256]{1,0:T(8,128)(2,1)S(1)}, bf16[256,256]{1,0:T(8,128)(2,1)}, u32[]{:S(2)}) copy-start(bf16[256,256]{1,0:T(8,128)(2,1)} %constant.9.clone.stencil) | copy-start | bytes 393220
  24.0 5.6 %collective-permute-start.3 = (f32[32,128]{1,0:T(8,128)S(1)}, f32[32,128]{1,0:T(8,128)S(1)}, u32[]{:S(2)}, u32[]{:S(2)}) collective-permute-start(f32[32,128]{1,0:T(8,128)S(1)} %get-tuple-element.65), channel_id=1, source_target_pairs={{0,8},{8,16},{16,24},{24,0},{1,9},{9,17},{17,25},{25,1},{2,10},{10... | collective-permute-start | bytes 49160 | tf_op jit(solution)/shard_map/ppermute | solution.py:577
  24.6 5.0 %collective-permute-start.4 = (f32[32,128]{1,0:T(8,128)S(1)}, f32[32,128]{1,0:T(8,128)S(1)}, u32[]{:S(2)}, u32[]{:S(2)}) collective-permute-start(f32[32,128]{1,0:T(8,128)S(1)} %get-tuple-element.66), channel_id=1, source_target_pairs={{0,16},{8,24},{16,0},{24,8},{1,17},{9,25},{17,1},{25,9},{2,18},{10... | collective-permute-start | bytes 49160 | tf_op jit(solution)/shard_map/ppermute | solution.py:577
  27.3 3.7 %copy-start = (bf16[256,512]{1,0:T(8,128)(2,1)S(1)}, bf16[256,512]{1,0:T(8,128)(2,1)}, u32[]{:S(2)}) copy-start(bf16[256,512]{1,0:T(8,128)(2,1)} %constant.10.clone.places) | copy-start | bytes 786436
  27.3 3.7 %copy-start.9 = (bf16[256,256]{1,0:T(8,128)(2,1)S(1)}, bf16[256,256]{1,0:T(8,128)(2,1)}, u32[]{:S(2)}) copy-start(bf16[256,256]{1,0:T(8,128)(2,1)} %constant.11.clone.spreads) | copy-start | bytes 393220
  27.3 3.7 %collective-permute-start.5 = (f32[32,128]{1,0:T(8,128)S(1)}, f32[32,128]{1,0:T(8,128)S(1)}, u32[]{:S(2)}, u32[]{:S(2)}) collective-permute-start(f32[32,128]{1,0:T(8,128)S(1)} %get-tuple-element.67), channel_id=1, source_target_pairs={{0,24},{8,0},{16,8},{24,16},{1,25},{9,1},{17,9},{25,17},{2,26},{10... | collective-permute-start | bytes 49160 | tf_op jit(solution)/shard_map/ppermute | solution.py:577
  32.7 6.3 %collective-permute-start.9 = (f32[144,128]{1,0:T(8,128)S(1)}, f32[144,128]{1,0:T(8,128)S(1)}, u32[]{:S(2)}, u32[]{:S(2)}) collective-permute-start(f32[144,128]{1,0:T(8,128)S(1)} %get-tuple-element.78), channel_id=1, source_target_pairs={{0,8},{8,16},{16,24},{24,0},{1,9},{9,17},{17,25},{25,1},{2,10},{10... | collective-permute-start | bytes 221192 | tf_op jit(solution)/shard_map/ppermute | solution.py:577
  33.9 6.6 %collective-permute-start.10 = (f32[144,128]{1,0:T(8,128)S(1)}, f32[144,128]{1,0:T(8,128)S(1)}, u32[]{:S(2)}, u32[]{:S(2)}) collective-permute-start(f32[144,128]{1,0:T(8,128)S(1)} %get-tuple-element.79), channel_id=1, source_target_pairs={{0,16},{8,24},{16,0},{24,8},{1,17},{9,25},{17,1},{25,9},{2,18},{10... | collective-permute-start | bytes 221192 | tf_op jit(solution)/shard_map/ppermute | solution.py:577
  36.8 4.4 %collective-permute-start.11 = (f32[144,128]{1,0:T(8,128)S(1)}, f32[144,128]{1,0:T(8,128)S(1)}, u32[]{:S(2)}, u32[]{:S(2)}) collective-permute-start(f32[144,128]{1,0:T(8,128)S(1)} %get-tuple-element.80), channel_id=1, source_target_pairs={{0,24},{8,0},{16,8},{24,16},{1,25},{9,1},{17,9},{25,17},{2,26},{10... | collective-permute-start | bytes 221192 | tf_op jit(solution)/shard_map/ppermute | solution.py:577
  42.5 6.3 %collective-permute-start.12 = (f32[144,128]{1,0:T(8,128)S(1)}, f32[144,128]{1,0:T(8,128)S(1)}, u32[]{:S(2)}, u32[]{:S(2)}) collective-permute-start(f32[144,128]{1,0:T(8,128)S(1)} %get-tuple-element.87), channel_id=1, source_target_pairs={{0,8},{8,16},{16,24},{24,0},{1,9},{9,17},{17,25},{25,1},{2,10},{10... | collective-permute-start | bytes 221192 | tf_op jit(solution)/shard_map/ppermute | solution.py:577
  43.1 6.9 %collective-permute-start.13 = (f32[144,128]{1,0:T(8,128)S(1)}, f32[144,128]{1,0:T(8,128)S(1)}, u32[]{:S(2)}, u32[]{:S(2)}) collective-permute-start(f32[144,128]{1,0:T(8,128)S(1)} %get-tuple-element.88), channel_id=1, source_target_pairs={{0,16},{8,24},{16,0},{24,8},{1,17},{9,25},{17,1},{25,9},{2,18},{10... | collective-permute-start | bytes 221192 | tf_op jit(solution)/shard_map/ppermute | solution.py:577
  45.8 5.2 %collective-permute-start.14 = (f32[144,128]{1,0:T(8,128)S(1)}, f32[144,128]{1,0:T(8,128)S(1)}, u32[]{:S(2)}, u32[]{:S(2)}) collective-permute-start(f32[144,128]{1,0:T(8,128)S(1)} %get-tuple-element.89), channel_id=1, source_target_pairs={{0,24},{8,0},{16,8},{24,16},{1,25},{9,1},{17,9},{25,17},{2,26},{10... | collective-permute-start | bytes 221192 | tf_op jit(solution)/shard_map/ppermute | solution.py:577
  52.2 6.9 %collective-permute-start.15 = (f32[144,128]{1,0:T(8,128)S(1)}, f32[144,128]{1,0:T(8,128)S(1)}, u32[]{:S(2)}, u32[]{:S(2)}) collective-permute-start(f32[144,128]{1,0:T(8,128)S(1)} %get-tuple-element.96), channel_id=1, source_target_pairs={{0,8},{8,16},{16,24},{24,0},{1,9},{9,17},{17,25},{25,1},{2,10},{10... | collective-permute-start | bytes 221192 | tf_op jit(solution)/shard_map/ppermute | solution.py:577
  54.3 6.4 %collective-permute-start.16 = (f32[144,128]{1,0:T(8,128)S(1)}, f32[144,128]{1,0:T(8,128)S(1)}, u32[]{:S(2)}, u32[]{:S(2)}) collective-permute-start(f32[144,128]{1,0:T(8,128)S(1)} %get-tuple-element.97), channel_id=1, source_target_pairs={{0,16},{8,24},{16,0},{24,8},{1,17},{9,25},{17,1},{25,9},{2,18},{10... | collective-permute-start | bytes 221192 | tf_op jit(solution)/shard_map/ppermute | solution.py:577
  57.4 4.4 %collective-permute-start.17 = (f32[144,128]{1,0:T(8,128)S(1)}, f32[144,128]{1,0:T(8,128)S(1)}, u32[]{:S(2)}, u32[]{:S(2)}) collective-permute-start(f32[144,128]{1,0:T(8,128)S(1)} %get-tuple-element.98), channel_id=1, source_target_pairs={{0,24},{8,0},{16,8},{24,16},{1,25},{9,1},{17,9},{25,17},{2,26},{10... | collective-permute-start | bytes 221192 | tf_op jit(solution)/shard_map/ppermute | solution.py:577

commit v14 on v12

--- a/solution.py
+++ b/solution.py
@@ -131,12 +131,17 @@
     return records, faces, 1 + -(-FACES // faces)
 
 
+def swap_order(count):
+    return sorted(range(1, count), key=lambda s: (-s.bit_length(), s))
+
+
 def place_of(table, slot):
     return table[0, FACES * SLOTS + slot], table[0, FACES * SLOTS + SLOTS + slot]
 
 
 def write_tables(plane_cap, source, block, neighbour, asked, farther, table):
-    me = lax.axis_index("gx").astype(F32)
+    here = lax.axis_index("gx")
+    me = here.astype(F32)
     count = lax.axis_size("gx")
     records, faces, _ = table_sizes(count, plane_cap)
     cap = float(plane_cap)
@@ -174,12 +179,16 @@
             jnp.where(alike & (number_column < number_row), 1.0, 0.0), axis=0, keepdims=True
         )
         send_rank = jnp.sum(jnp.where(alike & before, 1.0, 0.0), axis=0, keepdims=True)
-        here = records + (number_row - owner_row * SLOTS)
-        there = (wrapped(me - owner_row) - 1.0) * cap + receive_rank
-        receive = jnp.where(owner_row == me, here, there)
+        swap = jnp.where(number < 0, 0, (number >> 4) ^ here)
+        position = jnp.zeros(swap.shape, F32)
+        for at, other in enumerate(swap_order(count)):
+            position = jnp.where(swap == other, float(at), position)
+        mine = records + (number_row - owner_row * SLOTS)
+        there = position * cap + receive_rank
+        receive = jnp.where(owner_row == me, mine, there)
         receive = jnp.where(number_row < 0.0, records + SLOTS + slot, receive)
         table[0:1, face * SLOTS : face * SLOTS + SLOTS] = receive.astype(jnp.int32)
-        key = jnp.where(other_row, (wrapped(owner_row - me) - 1.0) * cap + send_rank, -1.0)
+        key = jnp.where(other_row, position * cap + send_rank, -1.0)
         hit = iota((SLOTS, records), 1).astype(F32) == column_of(key)
         tile = jnp.sum(jnp.where(hit, slot_column, 0.0), axis=0, keepdims=True)
         row, at = 1 + (face ^ 1) // faces, (face ^ 1) % faces * records
@@ -558,6 +567,12 @@
     def exchange(values):
         return [pass_on(value, shift) for shift, value in enumerate(values, 1)]
 
+    def swap_all(values):
+        return [
+            lax.ppermute(value, "gx", [(i, i ^ swap) for i in range(count)])
+            for swap, value in zip(swap_order(count), values)
+        ]
+
     farther = [pass_on(value, shift) for shift, value in enumerate(farther, 2)]
 
     phase_field = phase.reshape(SLOTS, TE, PLANE)
@@ -583,7 +598,7 @@
     request = jnp.stack([value[:block_cap] for value in request]).astype(jnp.int32)
     _, deep = block_layout(block_cap)
     brick = shape(bx, by, bz)
-    got = exchange(packed)
+    got = swap_all(packed)
     heated, *found = call(
         functools.partial(heat_kernel, block_cap, sizes),
         [SMEM] + [VMEM] * 5,
@@ -619,7 +634,7 @@
     )(table, phase_field, *inner_fields, *own, picks, places, spreads, *found, *got)
     own, send = rest[:2], rest[2:]
     for _ in range(PHASE_STEPS - 2):
-        got = exchange(send)
+        got = swap_all(send)
         inner_fields = inner(phase_field, solute_field, heat)
         phase_field, solute_field, *rest = call(
             middle_step_kernel,
@@ -628,7 +643,7 @@
             step_scratch,
         )(table, *inner_fields, *own, picks, places, *got)
         own, send = rest[:2], rest[2:]
-    got = exchange(send)
+    got = swap_all(send)
     inner_fields = inner(phase_field, solute_field, heat)
     phase_field, solute_field = call(
         last_step_kernel, [SMEM] + [VMEM] * (5 + others), [field, field], step_scratch

time: 63.7 us -> 62.3 us (0.978)
  starting transfers between devices: 34.3 us -> 30.7 us
  waiting for transfers between devices: 12.2 us -> 14.4 us
    ppermute x18 -> x6, starting transfers between devices: 29.1 us -> 11.2 us  [pass_on(): lax.ppermute(value, 'gx', [(i, (i + shift) % count) for i in range(count)])]
    ppermute x0 -> x12, starting transfers between devices: none -> 14.3 us  [swap_all(): lax.ppermute(value, 'gx', [(i, i ^ swap) for i in range(count)])]
    ppermute x0 -> x12, waiting for transfers between devices: none -> 12 us  [swap_all(): lax.ppermute(value, 'gx', [(i, i ^ swap) for i in range(count)])]
    ppermute x18 -> x6, waiting for transfers between devices: 12.2 us -> 2.34 us  [pass_on(): lax.ppermute(value, 'gx', [(i, (i + shift) % count) for i in range(count)])]
  transfers between devices with their start and end apart: 19 -> 19, of which waited for: 11 -> 9; matrix products, arithmetic and copies ran while one was open for 0% -> 0% of each run, Pallas kernels for 9% -> 9%
where the time goes in v14:
time: 62.3 us; the launch traced here: 62 us
  starting transfers between devices  30.7 us (49%)
  waiting for transfers between devices  14.4 us (23%)
  Pallas kernels  13.4 us (22%)
  local copies, waits for them, and re-layouts  2.65 us (4%)
  between operations  0.85 us (1%)
    ppermute x12, starting transfers between devices, swap_all(): lax.ppermute(value, 'gx', [(i, i ^ swap) for i in range(count)])  14.3 us
    ppermute x12, waiting for transfers between devices, swap_all(): lax.ppermute(value, 'gx', [(i, i ^ swap) for i in range(count)])  12 us
    ppermute x6, starting transfers between devices, pass_on(): lax.ppermute(value, 'gx', [(i, (i + shift) % count) for i in range(count)])  11.2 us
    all_to_all x1, starting transfers between devices, local(): lax.all_to_all(sides, ('gy', 'gz'), split_axis=0, concat_axis=0, tiled=True)  5.18 us
    unnamed x26, local copies, waits for them, and re-layouts  2.64 us
    pallas_call x2, Pallas kernels, local(): call(middle_step_kernel, [SMEM] + [VMEM] * (6 + others), [field, field, *...  2.44 us
    ppermute x6, waiting for transfers between devices, pass_on(): lax.ppermute(value, 'gx', [(i, (i + shift) % count) for i in range(count)])  2.34 us
    pallas_call x1, Pallas kernels, local(): call(functools.partial(sides_kernel, sizes, plane_cap), [ANY] * 5, [shape...  2.21 us
  transfers between devices with their start and end apart: 19, of which 9 were waited for; matrix products, arithmetic and copies ran while one was open for 0% of the time, Pallas kernels for 9%

profile of v14, /device:TPU:0, one launch (start us, length us, event | category | flops | bytes accessed | tf_op | source)
XLA Modules:
  0.0 62.0 jit_solution(1086680760345487043)
XLA Ops:
  0.6 0.0 copy-start.1
  0.6 2.2 %shard_map.130 = (f32[8,24,128]{2,1,0:T(8,128)}, s32[2,128]{1,0:T(2,128)}, f32[4,128]{1,0:T(4,128)}, f32[8,128]{1,0:T(8,128)}) custom-call(s32[1,16]{1,0:T(1,128)} %bitcast.15, s32[1,16]{1,0:T(1,128)} %bitcast.16, s32[6,1,16]{2,1,0:T(1,128)} %bitcast.14, f32[8,32,128]{2,1,0:T(8,128)} %h.3, f32[8,32,128]{2,1,0:T(8,128)} %k.3), custom_call_target="tpu_custom_call" | custom-call | tf_op jit(solution)/shard_map/pallas_call | solution.py:537
  2.9 0.0 copy-start.12
  2.9 5.2 %all-to-all-start = ((f32[8,24,128]{2,1,0:T(8,128)}), f32[8,24,128]{2,1,0:T(8,128)S(1)}, u32[]{:S(2)}, u32[]{:S(2)}) async-start(f32[8,24,128]{2,1,0:T(8,128)} %get-tuple-element.55), calls=%async_computation | async-start | bytes 196608 | tf_op jit(solution)/shard_map/all_to_all | solution.py:562
  8.1 0.0 copy-done.12
  8.1 2.7 %collective-permute-start = (f32[8,128]{1,0:T(8,128)S(1)}, f32[8,128]{1,0:T(8,128)S(1)}, u32[]{:S(2)}, u32[]{:S(2)}) collective-permute-start(f32[8,128]{1,0:T(8,128)S(1)} %copy-done.12), channel_id=1, source_target_pairs={{0,16},{8,24},{16,0},{24,8},{1,17},{9,25},{17,1},{25,9},{2,18},{10... | collective-permute-start | bytes 12296 | tf_op jit(solution)/shard_map/ppermute | solution.py:565
  10.7 0.7 %copy-done.11 = f32[4,128]{1,0:T(4,128)S(1)} copy-done((f32[4,128]{1,0:T(4,128)S(1)}, f32[4,128]{1,0:T(4,128)}, u32[]{:S(2)}) %copy-start.11) | copy-done | bytes 2072
  11.4 0.0 copy-done.10
  11.4 0.9 %copy-done.2 = f32[1,1,1,16,16,256]{5,4,3,2,1,0:T(8,128)S(1)} copy-done((f32[1,1,1,16,16,256]{5,4,3,2,1,0:T(8,128)S(1)}, f32[1,1,1,16,16,256]{5,4,3,2,1,0:T(8,128)}, u32[]{:S(2)}) %copy-start.2) | copy-done | bytes 262168
  12.4 0.9 %copy-done.7 = f32[1,1,1,16,16,256]{5,4,3,2,1,0:T(8,128)S(1)} copy-done((f32[1,1,1,16,16,256]{5,4,3,2,1,0:T(8,128)S(1)}, f32[1,1,1,16,16,256]{5,4,3,2,1,0:T(8,128)}, u32[]{:S(2)}) %copy-start.7) | copy-done | bytes 262168
  13.3 0.9 %shard_map.131 = (f32[32,16,128]{2,1,0:T(8,128)S(1)}, f32[256,128]{1,0:T(8,128)S(1)}, f32[4,128]{1,0:T(4,128)S(1)}, f32[144,128]{1,0:T(8,128)S(1)}, f32[144,128]{1,0:T(8,128)S(1)}, /*index=5*/f32[144,128]{1,0:T(8,128)S(1)}) custom-call(s32[2,128]{1,0:T(2,128)S(1)} %copy-done.10, f32[4,128]{1,0:T(4,128)S(1)} %copy-done.11, f32[16,16,256]{2,1,0:T(8,128)S(1)} %bitcast.9, ...), custom_call_target="tpu_custom_call" | custom-call | tf_op jit(solution)/shard_map/pallas_call | solution.py:583
  14.2 0.0 collective-permute-done.rest_0_
  14.2 0.0 all-to-all-done.got
  14.2 0.0 copy-done.5
  14.3 0.0 copy-done.6
  14.3 0.0 copy-start.8
  14.3 0.0 copy-start.3
  14.3 1.6 %collective-permute-start.1 = (f32[104,128]{1,0:T(8,128)S(1)}, f32[104,128]{1,0:T(8,128)S(1)}, u32[]{:S(2)}, u32[]{:S(2)}) collective-permute-start(f32[104,128]{1,0:T(8,128)S(1)} %get-tuple-element.57), channel_id=1, source_target_pairs={{0,8},{8,16},{16,24},{24,0},{1,9},{9,17},{17,25},{25,1},{2,10},{10... | collective-permute-start | bytes 159752 | tf_op jit(solution)/shard_map/ppermute | solution.py:565
  16.0 2.2 %collective-permute-start.2 = (f32[104,128]{1,0:T(8,128)S(1)}, f32[104,128]{1,0:T(8,128)S(1)}, u32[]{:S(2)}, u32[]{:S(2)}) collective-permute-start(f32[104,128]{1,0:T(8,128)S(1)} %get-tuple-element.58), channel_id=1, source_target_pairs={{0,24},{8,0},{16,8},{24,16},{1,25},{9,1},{17,9},{25,17},{2,26},{10... | collective-permute-start | bytes 159752 | tf_op jit(solution)/shard_map/ppermute | solution.py:565
  18.2 0.0 collective-permute-start.6
  18.2 2.1 %collective-permute-start.7 = (f32[144,128]{1,0:T(8,128)S(1)}, f32[144,128]{1,0:T(8,128)S(1)}, u32[]{:S(2)}, u32[]{:S(2)}) collective-permute-start(f32[144,128]{1,0:T(8,128)S(1)} %get-tuple-element.69), channel_id=1, source_target_pairs={{0,24},{8,16},{16,8},{24,0},{1,25},{9,17},{17,9},{25,1},{2,26},{10... | collective-permute-start | bytes 221192 | tf_op jit(solution)/shard_map/ppermute | solution.py:572
  20.3 1.3 %collective-permute-start.8 = (f32[144,128]{1,0:T(8,128)S(1)}, f32[144,128]{1,0:T(8,128)S(1)}, u32[]{:S(2)}, u32[]{:S(2)}) collective-permute-start(f32[144,128]{1,0:T(8,128)S(1)} %get-tuple-element.70), channel_id=1, source_target_pairs={{0,8},{8,0},{16,24},{24,16},{1,9},{9,1},{17,25},{25,17},{2,10},{10... | collective-permute-start | bytes 221192 | tf_op jit(solution)/shard_map/ppermute | solution.py:572
  21.7 0.0 collective-permute-done.1.low
  21.7 0.0 collective-permute-done.2.high
  21.7 0.0 copy-start.4
  21.8 1.9 %shard_map.133 = (f32[8,32,128]{2,1,0:T(8,128)S(1)}, f32[32,128]{1,0:T(8,128)S(1)}, f32[32,128]{1,0:T(8,128)S(1)}, f32[32,128]{1,0:T(8,128)S(1)}, f32[32,128]{1,0:T(8,128)S(1)}) custom-call(s32[4,8]{1,0:T(4,128)S(1)} %maximum_convert_fusion.request, f32[8,32,128]{2,1,0:T(8,128)S(1)} %copy-done.5, f32[8,32,128]{2,1,0:T(8,128)S(1)} %copy-done.6, ...), custom_call_target="tpu_custom_call" | custom-call | tf_op jit(solution)/shard_map/pallas_call | solution.py:602
  23.7 0.7 %collective-permute-start.3 = (f32[32,128]{1,0:T(8,128)S(1)}, f32[32,128]{1,0:T(8,128)S(1)}, u32[]{:S(2)}, u32[]{:S(2)}) collective-permute-start(f32[32,128]{1,0:T(8,128)S(1)} %get-tuple-element.65), channel_id=1, source_target_pairs={{0,8},{8,16},{16,24},{24,0},{1,9},{9,17},{17,25},{25,1},{2,10},{10... | collective-permute-start | bytes 49160 | tf_op jit(solution)/shard_map/ppermute | solution.py:565
  24.4 3.0 %collective-permute-start.4 = (f32[32,128]{1,0:T(8,128)S(1)}, f32[32,128]{1,0:T(8,128)S(1)}, u32[]{:S(2)}, u32[]{:S(2)}) collective-permute-start(f32[32,128]{1,0:T(8,128)S(1)} %get-tuple-element.66), channel_id=1, source_target_pairs={{0,16},{8,24},{16,0},{24,8},{1,17},{9,25},{17,1},{25,9},{2,18},{10... | collective-permute-start | bytes 49160 | tf_op jit(solution)/shard_map/ppermute | solution.py:565
  27.4 0.0 collective-permute-done.6.rest_4_
  27.4 0.9 %collective-permute-start.5 = (f32[32,128]{1,0:T(8,128)S(1)}, f32[32,128]{1,0:T(8,128)S(1)}, u32[]{:S(2)}, u32[]{:S(2)}) collective-permute-start(f32[32,128]{1,0:T(8,128)S(1)} %get-tuple-element.67), channel_id=1, source_target_pairs={{0,24},{8,0},{16,8},{24,16},{1,25},{9,1},{17,9},{25,17},{2,26},{10... | collective-permute-start | bytes 49160 | tf_op jit(solution)/shard_map/ppermute | solution.py:565
  28.3 0.0 copy-done.3
  28.3 0.5 shard_map.135
  28.8 0.0 collective-permute-done.7.rest_5_
  28.8 0.0 collective-permute-done.8.rest_6_
  28.8 0.5 collective-permute-done.3.rest_1_
  29.3 0.0 collective-permute-done.4.rest_2_
  29.3 1.9 %collective-permute-done.5.rest_3_ = f32[32,128]{1,0:T(8,128)S(1)} collective-permute-done((f32[32,128]{1,0:T(8,128)S(1)}, f32[32,128]{1,0:T(8,128)S(1)}, u32[]{:S(2)}, u32[]{:S(2)}) %collective-permute-start.5) | collective-permute-done | bytes 16416 | tf_op jit(solution)/shard_map/ppermute | solution.py:565
  31.2 0.0 copy-done.9
  31.2 1.7 %shard_map.136 = (f32[16,16,256]{2,1,0:T(8,128)S(1)}, f32[16,16,256]{2,1,0:T(8,128)S(1)}, f32[2,256,128]{2,1,0:T(8,128)S(1)}, f32[32,16,128]{2,1,0:T(8,128)S(1)}...) custom-call(s32[2,128]{1,0:T(2,128)S(1)} %copy-done.10, ...), custom_call_target="tpu_custom_call" | custom-call | tf_op jit(solution)/shard_map/pallas_call | solution.py:625
  32.8 1.0 %collective-permute-start.9 = (f32[144,128]{1,0:T(8,128)S(1)}, f32[144,128]{1,0:T(8,128)S(1)}, u32[]{:S(2)}, u32[]{:S(2)}) collective-permute-start(f32[144,128]{1,0:T(8,128)S(1)} %get-tuple-element.78), channel_id=1, source_target_pairs={{0,16},{8,24},{16,0},{24,8},{1,17},{9,25},{17,1},{25,9},{2,18},{10... | collective-permute-start | bytes 221192 | tf_op jit(solution)/shard_map/ppermute | solution.py:572
  33.8 2.1 %collective-permute-start.10 = (f32[144,128]{1,0:T(8,128)S(1)}, f32[144,128]{1,0:T(8,128)S(1)}, u32[]{:S(2)}, u32[]{:S(2)}) collective-permute-start(f32[144,128]{1,0:T(8,128)S(1)} %get-tuple-element.79), channel_id=1, source_target_pairs={{0,24},{8,16},{16,8},{24,0},{1,25},{9,17},{17,9},{25,1},{2,26},{10... | collective-permute-start | bytes 221192 | tf_op jit(solution)/shard_map/ppermute | solution.py:572
  36.0 0.4 collective-permute-start.11
  36.4 0.5 shard_map.137
  36.9 2.1 %collective-permute-done.9.rest_0_ = f32[144,128]{1,0:T(8,128)S(1)} collective-permute-done((f32[144,128]{1,0:T(8,128)S(1)}, f32[144,128]{1,0:T(8,128)S(1)}, u32[]{:S(2)}, u32[]{:S(2)}) %collective-permute-start.9) | collective-permute-done | bytes 73760 | tf_op jit(solution)/shard_map/ppermute | solution.py:572
  38.9 1.2 %collective-permute-done.10.rest_1_ = f32[144,128]{1,0:T(8,128)S(1)} collective-permute-done((f32[144,128]{1,0:T(8,128)S(1)}, f32[144,128]{1,0:T(8,128)S(1)}, u32[]{:S(2)}, u32[]{:S(2)}) %collective-permute-start.10) | collective-permute-done | bytes 73760 | tf_op jit(solution)/shard_map/ppermute | solution.py:572
  40.1 0.7 %collective-permute-done.11.rest_2_ = f32[144,128]{1,0:T(8,128)S(1)} collective-permute-done((f32[144,128]{1,0:T(8,128)S(1)}, f32[144,128]{1,0:T(8,128)S(1)}, u32[]{:S(2)}, u32[]{:S(2)}) %collective-permute-start.11) | collective-permute-done | bytes 73760 | tf_op jit(solution)/shard_map/ppermute | solution.py:572
  40.9 1.2 %shard_map.138 = (f32[16,16,256]{2,1,0:T(8,128)S(1)}, f32[16,16,256]{2,1,0:T(8,128)S(1)}, f32[32,16,128]{2,1,0:T(8,128)S(1)}, f32[256,128]{1,0:T(8,128)S(1)}, f3...) custom-call(s32[2,128]{1,0:T(2,128)S(1)} %copy-done.10, ...), custom_call_target="tpu_custom_call" | custom-call | tf_op jit(solution)/shard_map/pallas_call | solution.py:639
  42.1 1.7 %collective-permute-start.12 = (f32[144,128]{1,0:T(8,128)S(1)}, f32[144,128]{1,0:T(8,128)S(1)}, u32[]{:S(2)}, u32[]{:S(2)}) collective-permute-start(f32[144,128]{1,0:T(8,128)S(1)} %get-tuple-element.87), channel_id=1, source_target_pairs={{0,16},{8,24},{16,0},{24,8},{1,17},{9,25},{17,1},{25,9},{2,18},{10... | collective-permute-start | bytes 221192 | tf_op jit(solution)/shard_map/ppermute | solution.py:572
  43.8 1.2 %collective-permute-start.13 = (f32[144,128]{1,0:T(8,128)S(1)}, f32[144,128]{1,0:T(8,128)S(1)}, u32[]{:S(2)}, u32[]{:S(2)}) collective-permute-start(f32[144,128]{1,0:T(8,128)S(1)} %get-tuple-element.88), channel_id=1, source_target_pairs={{0,24},{8,16},{16,8},{24,0},{1,25},{9,17},{17,9},{25,1},{2,26},{10... | collective-permute-start | bytes 221192 | tf_op jit(solution)/shard_map/ppermute | solution.py:572
  45.0 0.7 %collective-permute-start.14 = (f32[144,128]{1,0:T(8,128)S(1)}, f32[144,128]{1,0:T(8,128)S(1)}, u32[]{:S(2)}, u32[]{:S(2)}) collective-permute-start(f32[144,128]{1,0:T(8,128)S(1)} %get-tuple-element.89), channel_id=1, source_target_pairs={{0,8},{8,0},{16,24},{24,16},{1,9},{9,1},{17,25},{25,17},{2,10},{10... | collective-permute-start | bytes 221192 | tf_op jit(solution)/shard_map/ppermute | solution.py:572
  45.6 0.5 shard_map.139
  46.1 1.9 %collective-permute-done.12.rest_0_ = f32[144,128]{1,0:T(8,128)S(1)} collective-permute-done((f32[144,128]{1,0:T(8,128)S(1)}, f32[144,128]{1,0:T(8,128)S(1)}, u32[]{:S(2)}, u32[]{:S(2)}) %collective-permute-start.12) | collective-permute-done | bytes 73760 | tf_op jit(solution)/shard_map/ppermute | solution.py:572
  48.1 2.5 %collective-permute-done.13.rest_1_ = f32[144,128]{1,0:T(8,128)S(1)} collective-permute-done((f32[144,128]{1,0:T(8,128)S(1)}, f32[144,128]{1,0:T(8,128)S(1)}, u32[]{:S(2)}, u32[]{:S(2)}) %collective-permute-start.13) | collective-permute-done | bytes 73760 | tf_op jit(solution)/shard_map/ppermute | solution.py:572
  50.6 0.0 collective-permute-done.14.rest_2_
  50.6 1.2 %shard_map.140 = (f32[16,16,256]{2,1,0:T(8,128)S(1)}, f32[16,16,256]{2,1,0:T(8,128)S(1)}, f32[32,16,128]{2,1,0:T(8,128)S(1)}, f32[256,128]{1,0:T(8,128)S(1)}, f3...) custom-call(s32[2,128]{1,0:T(2,128)S(1)} %copy-done.10, ...), custom_call_target="tpu_custom_call" | custom-call | tf_op jit(solution)/shard_map/pallas_call | solution.py:639
  51.8 2.4 %collective-permute-start.15 = (f32[144,128]{1,0:T(8,128)S(1)}, f32[144,128]{1,0:T(8,128)S(1)}, u32[]{:S(2)}, u32[]{:S(2)}) collective-permute-start(f32[144,128]{1,0:T(8,128)S(1)} %get-tuple-element.96), channel_id=1, source_target_pairs={{0,16},{8,24},{16,0},{24,8},{1,17},{9,25},{17,1},{25,9},{2,18},{10... | collective-permute-start | bytes 221192 | tf_op jit(solution)/shard_map/ppermute | solution.py:572
  54.2 0.9 %collective-permute-start.16 = (f32[144,128]{1,0:T(8,128)S(1)}, f32[144,128]{1,0:T(8,128)S(1)}, u32[]{:S(2)}, u32[]{:S(2)}) collective-permute-start(f32[144,128]{1,0:T(8,128)S(1)} %get-tuple-element.97), channel_id=1, source_target_pairs={{0,24},{8,16},{16,8},{24,0},{1,25},{9,17},{17,9},{25,1},{2,26},{10... | collective-permute-start | bytes 221192 | tf_op jit(solution)/shard_map/ppermute | solution.py:572
  55.1 0.5 collective-permute-start.17
  55.5 0.7 %shard_map.134 = f32[8,32,128]{2,1,0:T(8,128)} custom-call(f32[8,32,128]{2,1,0:T(8,128)S(1)} %get-tuple-element.59.value), custom_call_target="tpu_custom_call" | custom-call | tf_op jit(solution)/shard_map/pallas_call | solution.py:609
  56.2 0.5 shard_map.141
  56.7 1.2 %collective-permute-done.15.rest_0_ = f32[144,128]{1,0:T(8,128)S(1)} collective-permute-done((f32[144,128]{1,0:T(8,128)S(1)}, f32[144,128]{1,0:T(8,128)S(1)}, u32[]{:S(2)}, u32[]{:S(2)}) %collective-permute-start.15) | collective-permute-done | bytes 73760 | tf_op jit(solution)/shard_map/ppermute | solution.py:572
  57.9 2.4 %collective-permute-done.16.rest_1_ = f32[144,128]{1,0:T(8,128)S(1)} collective-permute-done((f32[144,128]{1,0:T(8,128)S(1)}, f32[144,128]{1,0:T(8,128)S(1)}, u32[]{:S(2)}, u32[]{:S(2)}) %collective-permute-start.16) | collective-permute-done | bytes 73760 | tf_op jit(solution)/shard_map/ppermute | solution.py:572
  60.3 0.0 collective-permute-done.17.rest_2_
  60.3 1.6 %shard_map.142 = (f32[16,16,256]{2,1,0:T(8,128)}, f32[16,16,256]{2,1,0:T(8,128)}) custom-call(s32[2,128]{1,0:T(2,128)S(1)} %copy-done.10, f32[16,16,256]{2,1,0:T(8,128)S(1)} %get-tuple-element.92.phase, f32[16,16,256]{2,1,0:T(8,128)S(1)} %get-tuple-element.93.solute, f32[32,16,128]{2,1,0:T(8,128)S(1)} %get-tuple-element.94.own, ...), custom_call_target="tpu_custom_call" | custom-call | tf_op jit(solution)/shard_map/pallas_call | solution.py:648
  (18 shorter events, 0.1 us)
Async XLA Ops:
  0.6 10.1 %copy-start.1 = (bf16[512,256]{1,0:T(8,128)(2,1)S(1)}, bf16[512,256]{1,0:T(8,128)(2,1)}, u32[]{:S(2)}) copy-start(bf16[512,256]{1,0:T(8,128)(2,1)} %constant.8.clone.picks) | copy-start | bytes 786436
  2.9 5.2 %copy-start.12 = (f32[8,128]{1,0:T(8,128)S(1)}, f32[8,128]{1,0:T(8,128)}, u32[]{:S(2)}) copy-start(f32[8,128]{1,0:T(8,128)} %get-tuple-element.56) | copy-start | bytes 12292
  2.9 11.4 %all-to-all-start = ((f32[8,24,128]{2,1,0:T(8,128)}), f32[8,24,128]{2,1,0:T(8,128)S(1)}, u32[]{:S(2)}, u32[]{:S(2)}) async-start(f32[8,24,128]{2,1,0:T(8,128)} %get-tuple-element.55), calls=%async_computation | async-start | bytes 196608 | tf_op jit(solution)/shard_map/all_to_all | solution.py:562
  8.1 6.2 %collective-permute-start = (f32[8,128]{1,0:T(8,128)S(1)}, f32[8,128]{1,0:T(8,128)S(1)}, u32[]{:S(2)}, u32[]{:S(2)}) collective-permute-start(f32[8,128]{1,0:T(8,128)S(1)} %copy-done.12), channel_id=1, source_target_pairs={{0,16},{8,24},{16,0},{24,8},{1,17},{9,25},{17,1},{25,9},{2,18},{10... | collective-permute-start | bytes 12296 | tf_op jit(solution)/shard_map/ppermute | solution.py:565
  10.7 0.7 %copy-start.11 = (f32[4,128]{1,0:T(4,128)S(1)}, f32[4,128]{1,0:T(4,128)}, u32[]{:S(2)}) copy-start(f32[4,128]{1,0:T(4,128)} %get-tuple-element.53.asked) | copy-start | bytes 6148
  10.7 0.7 %copy-start.10 = (s32[2,128]{1,0:T(2,128)S(1)}, s32[2,128]{1,0:T(2,128)}, u32[]{:S(2)}) copy-start(s32[2,128]{1,0:T(2,128)} %get-tuple-element.52.table) | copy-start | bytes 3076
  11.4 0.9 %copy-start.2 = (f32[1,1,1,16,16,256]{5,4,3,2,1,0:T(8,128)S(1)}, f32[1,1,1,16,16,256]{5,4,3,2,1,0:T(8,128)}, u32[]{:S(2)}) copy-start(f32[1,1,1,16,16,256]{5,4,3,2,1,0:T(8,128)} %param.13) | copy-start | bytes 786436
  12.4 0.9 %copy-start.7 = (f32[1,1,1,16,16,256]{5,4,3,2,1,0:T(8,128)S(1)}, f32[1,1,1,16,16,256]{5,4,3,2,1,0:T(8,128)}, u32[]{:S(2)}) copy-start(f32[1,1,1,16,16,256]{5,4,3,2,1,0:T(8,128)} %param.14) | copy-start | bytes 786436
  13.3 0.9 %copy-start.5 = (f32[8,32,128]{2,1,0:T(8,128)S(1)}, f32[8,32,128]{2,1,0:T(8,128)}, u32[]{:S(2)}) copy-start(f32[8,32,128]{2,1,0:T(8,128)} %h.3) | copy-start | bytes 393220
  13.3 1.0 %copy-start.6 = (f32[8,32,128]{2,1,0:T(8,128)S(1)}, f32[8,32,128]{2,1,0:T(8,128)}, u32[]{:S(2)}) copy-start(f32[8,32,128]{2,1,0:T(8,128)} %k.3) | copy-start | bytes 393220
  14.3 14.1 %copy-start.8 = (f32[1,1,1,16,16,256]{5,4,3,2,1,0:T(8,128)S(1)}, f32[1,1,1,16,16,256]{5,4,3,2,1,0:T(8,128)}, u32[]{:S(2)}) copy-start(f32[1,1,1,16,16,256]{5,4,3,2,1,0:T(8,128)} %param.14) | copy-start | bytes 786436
  14.3 14.0 %copy-start.3 = (f32[1,1,1,16,16,256]{5,4,3,2,1,0:T(8,128)S(1)}, f32[1,1,1,16,16,256]{5,4,3,2,1,0:T(8,128)}, u32[]{:S(2)}) copy-start(f32[1,1,1,16,16,256]{5,4,3,2,1,0:T(8,128)} %param.13) | copy-start | bytes 786436
  14.3 7.4 %collective-permute-start.1 = (f32[104,128]{1,0:T(8,128)S(1)}, f32[104,128]{1,0:T(8,128)S(1)}, u32[]{:S(2)}, u32[]{:S(2)}) collective-permute-start(f32[104,128]{1,0:T(8,128)S(1)} %get-tuple-element.57), channel_id=1, source_target_pairs={{0,8},{8,16},{16,24},{24,0},{1,9},{9,17},{17,25},{25,1},{2,10},{10... | collective-permute-start | bytes 159752 | tf_op jit(solution)/shard_map/ppermute | solution.py:565
  16.0 5.8 %collective-permute-start.2 = (f32[104,128]{1,0:T(8,128)S(1)}, f32[104,128]{1,0:T(8,128)S(1)}, u32[]{:S(2)}, u32[]{:S(2)}) collective-permute-start(f32[104,128]{1,0:T(8,128)S(1)} %get-tuple-element.58), channel_id=1, source_target_pairs={{0,24},{8,0},{16,8},{24,16},{1,25},{9,1},{17,9},{25,17},{2,26},{10... | collective-permute-start | bytes 159752 | tf_op jit(solution)/shard_map/ppermute | solution.py:565
  18.2 9.2 %collective-permute-start.6 = (f32[144,128]{1,0:T(8,128)S(1)}, f32[144,128]{1,0:T(8,128)S(1)}, u32[]{:S(2)}, u32[]{:S(2)}) collective-permute-start(f32[144,128]{1,0:T(8,128)S(1)} %get-tuple-element.68), channel_id=1, source_target_pairs={{0,16},{8,24},{16,0},{24,8},{1,17},{9,25},{17,1},{25,9},{2,18},{10... | collective-permute-start | bytes 221192 | tf_op jit(solution)/shard_map/ppermute | solution.py:572
  18.2 10.6 %collective-permute-start.7 = (f32[144,128]{1,0:T(8,128)S(1)}, f32[144,128]{1,0:T(8,128)S(1)}, u32[]{:S(2)}, u32[]{:S(2)}) collective-permute-start(f32[144,128]{1,0:T(8,128)S(1)} %get-tuple-element.69), channel_id=1, source_target_pairs={{0,24},{8,16},{16,8},{24,0},{1,25},{9,17},{17,9},{25,1},{2,26},{10... | collective-permute-start | bytes 221192 | tf_op jit(solution)/shard_map/ppermute | solution.py:572
  20.3 8.5 %collective-permute-start.8 = (f32[144,128]{1,0:T(8,128)S(1)}, f32[144,128]{1,0:T(8,128)S(1)}, u32[]{:S(2)}, u32[]{:S(2)}) collective-permute-start(f32[144,128]{1,0:T(8,128)S(1)} %get-tuple-element.70), channel_id=1, source_target_pairs={{0,8},{8,0},{16,24},{24,16},{1,9},{9,1},{17,25},{25,17},{2,10},{10... | collective-permute-start | bytes 221192 | tf_op jit(solution)/shard_map/ppermute | solution.py:572
  21.7 6.6 %copy-start.4 = (bf16[256,256]{1,0:T(8,128)(2,1)S(1)}, bf16[256,256]{1,0:T(8,128)(2,1)}, u32[]{:S(2)}) copy-start(bf16[256,256]{1,0:T(8,128)(2,1)} %constant.9.clone.stencil) | copy-start | bytes 393220
  23.7 5.6 %collective-permute-start.3 = (f32[32,128]{1,0:T(8,128)S(1)}, f32[32,128]{1,0:T(8,128)S(1)}, u32[]{:S(2)}, u32[]{:S(2)}) collective-permute-start(f32[32,128]{1,0:T(8,128)S(1)} %get-tuple-element.65), channel_id=1, source_target_pairs={{0,8},{8,16},{16,24},{24,0},{1,9},{9,17},{17,25},{25,1},{2,10},{10... | collective-permute-start | bytes 49160 | tf_op jit(solution)/shard_map/ppermute | solution.py:565
  24.4 4.9 %collective-permute-start.4 = (f32[32,128]{1,0:T(8,128)S(1)}, f32[32,128]{1,0:T(8,128)S(1)}, u32[]{:S(2)}, u32[]{:S(2)}) collective-permute-start(f32[32,128]{1,0:T(8,128)S(1)} %get-tuple-element.66), channel_id=1, source_target_pairs={{0,16},{8,24},{16,0},{24,8},{1,17},{9,25},{17,1},{25,9},{2,18},{10... | collective-permute-start | bytes 49160 | tf_op jit(solution)/shard_map/ppermute | solution.py:565
  27.4 3.7 %copy-start = (bf16[256,512]{1,0:T(8,128)(2,1)S(1)}, bf16[256,512]{1,0:T(8,128)(2,1)}, u32[]{:S(2)}) copy-start(bf16[256,512]{1,0:T(8,128)(2,1)} %constant.10.clone.places) | copy-start | bytes 786436
  27.4 3.7 %copy-start.9 = (bf16[256,256]{1,0:T(8,128)(2,1)S(1)}, bf16[256,256]{1,0:T(8,128)(2,1)}, u32[]{:S(2)}) copy-start(bf16[256,256]{1,0:T(8,128)(2,1)} %constant.11.clone.spreads) | copy-start | bytes 393220
  27.4 3.7 %collective-permute-start.5 = (f32[32,128]{1,0:T(8,128)S(1)}, f32[32,128]{1,0:T(8,128)S(1)}, u32[]{:S(2)}, u32[]{:S(2)}) collective-permute-start(f32[32,128]{1,0:T(8,128)S(1)} %get-tuple-element.67), channel_id=1, source_target_pairs={{0,24},{8,0},{16,8},{24,16},{1,25},{9,1},{17,9},{25,17},{2,26},{10... | collective-permute-start | bytes 49160 | tf_op jit(solution)/shard_map/ppermute | solution.py:565
  32.8 6.1 %collective-permute-start.9 = (f32[144,128]{1,0:T(8,128)S(1)}, f32[144,128]{1,0:T(8,128)S(1)}, u32[]{:S(2)}, u32[]{:S(2)}) collective-permute-start(f32[144,128]{1,0:T(8,128)S(1)} %get-tuple-element.78), channel_id=1, source_target_pairs={{0,16},{8,24},{16,0},{24,8},{1,17},{9,25},{17,1},{25,9},{2,18},{10... | collective-permute-start | bytes 221192 | tf_op jit(solution)/shard_map/ppermute | solution.py:572
  33.8 6.3 %collective-permute-start.10 = (f32[144,128]{1,0:T(8,128)S(1)}, f32[144,128]{1,0:T(8,128)S(1)}, u32[]{:S(2)}, u32[]{:S(2)}) collective-permute-start(f32[144,128]{1,0:T(8,128)S(1)} %get-tuple-element.79), channel_id=1, source_target_pairs={{0,24},{8,16},{16,8},{24,0},{1,25},{9,17},{17,9},{25,1},{2,26},{10... | collective-permute-start | bytes 221192 | tf_op jit(solution)/shard_map/ppermute | solution.py:572
  36.0 4.9 %collective-permute-start.11 = (f32[144,128]{1,0:T(8,128)S(1)}, f32[144,128]{1,0:T(8,128)S(1)}, u32[]{:S(2)}, u32[]{:S(2)}) collective-permute-start(f32[144,128]{1,0:T(8,128)S(1)} %get-tuple-element.80), channel_id=1, source_target_pairs={{0,8},{8,0},{16,24},{24,16},{1,9},{9,1},{17,25},{25,17},{2,10},{10... | collective-permute-start | bytes 221192 | tf_op jit(solution)/shard_map/ppermute | solution.py:572
  42.1 6.0 %collective-permute-start.12 = (f32[144,128]{1,0:T(8,128)S(1)}, f32[144,128]{1,0:T(8,128)S(1)}, u32[]{:S(2)}, u32[]{:S(2)}) collective-permute-start(f32[144,128]{1,0:T(8,128)S(1)} %get-tuple-element.87), channel_id=1, source_target_pairs={{0,16},{8,24},{16,0},{24,8},{1,17},{9,25},{17,1},{25,9},{2,18},{10... | collective-permute-start | bytes 221192 | tf_op jit(solution)/shard_map/ppermute | solution.py:572
  43.8 6.8 %collective-permute-start.13 = (f32[144,128]{1,0:T(8,128)S(1)}, f32[144,128]{1,0:T(8,128)S(1)}, u32[]{:S(2)}, u32[]{:S(2)}) collective-permute-start(f32[144,128]{1,0:T(8,128)S(1)} %get-tuple-element.88), channel_id=1, source_target_pairs={{0,24},{8,16},{16,8},{24,0},{1,25},{9,17},{17,9},{25,1},{2,26},{10... | collective-permute-start | bytes 221192 | tf_op jit(solution)/shard_map/ppermute | solution.py:572
  45.0 5.6 %collective-permute-start.14 = (f32[144,128]{1,0:T(8,128)S(1)}, f32[144,128]{1,0:T(8,128)S(1)}, u32[]{:S(2)}, u32[]{:S(2)}) collective-permute-start(f32[144,128]{1,0:T(8,128)S(1)} %get-tuple-element.89), channel_id=1, source_target_pairs={{0,8},{8,0},{16,24},{24,16},{1,9},{9,1},{17,25},{25,17},{2,10},{10... | collective-permute-start | bytes 221192 | tf_op jit(solution)/shard_map/ppermute | solution.py:572
  51.8 6.1 %collective-permute-start.15 = (f32[144,128]{1,0:T(8,128)S(1)}, f32[144,128]{1,0:T(8,128)S(1)}, u32[]{:S(2)}, u32[]{:S(2)}) collective-permute-start(f32[144,128]{1,0:T(8,128)S(1)} %get-tuple-element.96), channel_id=1, source_target_pairs={{0,16},{8,24},{16,0},{24,8},{1,17},{9,25},{17,1},{25,9},{2,18},{10... | collective-permute-start | bytes 221192 | tf_op jit(solution)/shard_map/ppermute | solution.py:572
  54.2 6.2 %collective-permute-start.16 = (f32[144,128]{1,0:T(8,128)S(1)}, f32[144,128]{1,0:T(8,128)S(1)}, u32[]{:S(2)}, u32[]{:S(2)}) collective-permute-start(f32[144,128]{1,0:T(8,128)S(1)} %get-tuple-element.97), channel_id=1, source_target_pairs={{0,24},{8,16},{16,8},{24,0},{1,25},{9,17},{17,9},{25,1},{2,26},{10... | collective-permute-start | bytes 221192 | tf_op jit(solution)/shard_map/ppermute | solution.py:572
  55.1 5.3 %collective-permute-start.17 = (f32[144,128]{1,0:T(8,128)S(1)}, f32[144,128]{1,0:T(8,128)S(1)}, u32[]{:S(2)}, u32[]{:S(2)}) collective-permute-start(f32[144,128]{1,0:T(8,128)S(1)} %get-tuple-element.98), channel_id=1, source_target_pairs={{0,8},{8,0},{16,24},{24,16},{1,9},{9,1},{17,25},{25,17},{2,10},{10... | collective-permute-start | bytes 221192 | tf_op jit(solution)/shard_map/ppermute | solution.py:572

commit v15 on v14

--- a/solution.py
+++ b/solution.py
@@ -146,6 +146,12 @@
     records, faces, _ = table_sizes(count, plane_cap)
     cap = float(plane_cap)
 
+    def position_of(swap):
+        position = jnp.zeros(swap.shape, F32)
+        for at, other in enumerate(swap_order(count)):
+            position = jnp.where(swap == other, float(at), position)
+        return position
+
     def wrapped(shift):
         return jnp.where(shift < 0.0, shift + float(count), shift)
 
@@ -166,7 +172,9 @@
         if 2 <= shift < count - 1:
             farther[shift - 2][...] = jnp.broadcast_to(row, (8, 128))
     at = FACES * SLOTS
-    table[0:1, at : at + SLOTS] = wrapped(me - source_row).astype(jnp.int32)
+    swap = source[...] ^ here
+    found = jnp.where(swap == 0, 0.0, 1.0 + position_of(swap))
+    table[0:1, at : at + SLOTS] = found.astype(jnp.int32)
     table[0:1, at + SLOTS : at + 2 * SLOTS] = rank.astype(jnp.int32)
     slot_column = iota((SLOTS, records), 0).astype(F32)
     for face in range(FACES):
@@ -179,10 +187,7 @@
             jnp.where(alike & (number_column < number_row), 1.0, 0.0), axis=0, keepdims=True
         )
         send_rank = jnp.sum(jnp.where(alike & before, 1.0, 0.0), axis=0, keepdims=True)
-        swap = jnp.where(number < 0, 0, (number >> 4) ^ here)
-        position = jnp.zeros(swap.shape, F32)
-        for at, other in enumerate(swap_order(count)):
-            position = jnp.where(swap == other, float(at), position)
+        position = position_of(jnp.where(number < 0, 0, (number >> 4) ^ here))
         mine = records + (number_row - owner_row * SLOTS)
         there = position * cap + receive_rank
         receive = jnp.where(owner_row == me, mine, there)
@@ -319,18 +324,18 @@
     parts, deep = block_layout(cap)
     nby, nbz = by // CB, bz // CB
     group = iota((deep, CB, bz), 2) // CB
-    for shift in range(count):
+    for out, swap in zip((found, *send), (0, *swap_order(count))):
+        back = lax.rem(me - (me ^ swap) + count, count)
         total = jnp.zeros((deep, CB, bz), F32)
         for rank in range(cap):
-            block = request[(count - shift) % count, rank]
+            block = request[back, rank]
             a, b, c = block // (nby * nbz), (block // nbz) % nby, block % nbz
             for part in range(parts):
                 at = rank * parts + part
                 patch = held[pl.ds(a * CB + part * deep, deep), b]
                 moved = pltpu.roll(patch, (CB * at - CB * c + bz) % bz, 2)
                 total = jnp.where(group == at, moved, total)
-        total = total.reshape(deep * CB, bz)
-        (send[shift - 1] if shift else found)[...] = total
+        out[...] = total.reshape(deep * CB, bz)
 
 
 def write_records(phase, solute, picks, own, own_edges, rows):
@@ -564,9 +569,6 @@
     def pass_on(value, shift):
         return lax.ppermute(value, "gx", [(i, (i + shift) % count) for i in range(count)])
 
-    def exchange(values):
-        return [pass_on(value, shift) for shift, value in enumerate(values, 1)]
-
     def swap_all(values):
         return [
             lax.ppermute(value, "gx", [(i, i ^ swap) for i in range(count)])
@@ -605,7 +607,7 @@
         [brick] + [shape(deep * CB, 128)] * count,
         [pltpu.VMEM((bx, by // CB, CB, bz), F32)],
     )(request, enthalpy, conductivity, sides, from_low, from_high)
-    found[1:] = exchange(found[1:])
+    found[1:] = swap_all(found[1:])
     (heat_out,) = call(write_out_kernel, [ANY], [brick], [pltpu.SemaphoreType.DMA], [ANY])(heated)
 
     field = shape(SLOTS, TE, PLANE)

time: 62.3 us -> 62.4 us (level)
  starting transfers between devices: 30.7 us -> 29.7 us
  waiting for transfers between devices: 14.4 us -> 15.4 us
    ppermute x6 -> x3, starting transfers between devices: 11.2 us -> 6.53 us  [pass_on(): lax.ppermute(value, 'gx', [(i, (i + shift) % count) for i in range(count)])]
    ppermute x12 -> x15, starting transfers between devices: 14.3 us -> 18 us  [swap_all(): lax.ppermute(value, 'gx', [(i, i ^ swap) for i in range(count)])]
    ppermute x12 -> x15, waiting for transfers between devices: 12 us -> 15.4 us  [swap_all(): lax.ppermute(value, 'gx', [(i, i ^ swap) for i in range(count)])]
    ppermute x6 -> x3, waiting for transfers between devices: 2.34 us -> 0.01 us  [pass_on(): lax.ppermute(value, 'gx', [(i, (i + shift) % count) for i in range(count)])]
where the time goes in v15:
time: 62.4 us; the launch traced here: 62 us
  starting transfers between devices  29.7 us (48%)
  waiting for transfers between devices  15.4 us (25%)
  Pallas kernels  13.4 us (21%)
  local copies, waits for them, and re-layouts  2.64 us (4%)
  between operations  0.85 us (1%)
    ppermute x15, starting transfers between devices, swap_all(): lax.ppermute(value, 'gx', [(i, i ^ swap) for i in range(count)])  18 us
    ppermute x15, waiting for transfers between devices, swap_all(): lax.ppermute(value, 'gx', [(i, i ^ swap) for i in range(count)])  15.4 us
    ppermute x3, starting transfers between devices, pass_on(): lax.ppermute(value, 'gx', [(i, (i + shift) % count) for i in range(count)])  6.53 us
    all_to_all x1, starting transfers between devices, local(): lax.all_to_all(sides, ('gy', 'gz'), split_axis=0, concat_axis=0, tiled=True)  5.18 us
    unnamed x26, local copies, waits for them, and re-layouts  2.63 us
    pallas_call x2, Pallas kernels, local(): call(middle_step_kernel, [SMEM] + [VMEM] * (6 + others), [field, field, *...  2.44 us
    pallas_call x1, Pallas kernels, local(): call(functools.partial(sides_kernel, sizes, plane_cap), [ANY] * 5, [shape...  2.21 us
    pallas_call x4, Pallas kernels, inner(): call(functools.partial(inner_kernel, bool(heat)), [VMEM] * (3 + len(heat)...  1.96 us
  transfers between devices with their start and end apart: 19, of which 9 were waited for; matrix products, arithmetic and copies ran while one was open for 0% of the time, Pallas kernels for 9%

profile of v15, /device:TPU:0, one launch (start us, length us, event | category | flops | bytes accessed | tf_op | source)
XLA Modules:
  0.0 62.0 jit_solution(10212306417102400088)
XLA Ops:
  0.6 0.0 copy-start.1
  0.6 2.2 %shard_map.130 = (f32[8,24,128]{2,1,0:T(8,128)}, s32[2,128]{1,0:T(2,128)}, f32[4,128]{1,0:T(4,128)}, f32[8,128]{1,0:T(8,128)}) custom-call(s32[1,16]{1,0:T(1,128)} %bitcast.15, s32[1,16]{1,0:T(1,128)} %bitcast.16, s32[6,1,16]{2,1,0:T(1,128)} %bitcast.14, f32[8,32,128]{2,1,0:T(8,128)} %h.3, f32[8,32,128]{2,1,0:T(8,128)} %k.3), custom_call_target="tpu_custom_call" | custom-call | tf_op jit(solution)/shard_map/pallas_call | solution.py:542
  2.9 0.0 copy-start.12
  2.9 5.2 %all-to-all-start = ((f32[8,24,128]{2,1,0:T(8,128)}), f32[8,24,128]{2,1,0:T(8,128)S(1)}, u32[]{:S(2)}, u32[]{:S(2)}) async-start(f32[8,24,128]{2,1,0:T(8,128)} %get-tuple-element.55), calls=%async_computation | async-start | bytes 196608 | tf_op jit(solution)/shard_map/all_to_all | solution.py:567
  8.1 0.0 copy-done.12
  8.1 2.7 %collective-permute-start = (f32[8,128]{1,0:T(8,128)S(1)}, f32[8,128]{1,0:T(8,128)S(1)}, u32[]{:S(2)}, u32[]{:S(2)}) collective-permute-start(f32[8,128]{1,0:T(8,128)S(1)} %copy-done.12), channel_id=1, source_target_pairs={{0,16},{8,24},{16,0},{24,8},{1,17},{9,25},{17,1},{25,9},{2,18},{10... | collective-permute-start | bytes 12296 | tf_op jit(solution)/shard_map/ppermute | solution.py:570
  10.7 0.0 copy-done.1
  10.7 0.7 %copy-done.11 = f32[4,128]{1,0:T(4,128)S(1)} copy-done((f32[4,128]{1,0:T(4,128)S(1)}, f32[4,128]{1,0:T(4,128)}, u32[]{:S(2)}) %copy-start.11) | copy-done | bytes 2072
  11.4 0.0 copy-done.10
  11.4 0.9 %copy-done.2 = f32[1,1,1,16,16,256]{5,4,3,2,1,0:T(8,128)S(1)} copy-done((f32[1,1,1,16,16,256]{5,4,3,2,1,0:T(8,128)S(1)}, f32[1,1,1,16,16,256]{5,4,3,2,1,0:T(8,128)}, u32[]{:S(2)}) %copy-start.2) | copy-done | bytes 262168
  12.4 0.9 %copy-done.7 = f32[1,1,1,16,16,256]{5,4,3,2,1,0:T(8,128)S(1)} copy-done((f32[1,1,1,16,16,256]{5,4,3,2,1,0:T(8,128)S(1)}, f32[1,1,1,16,16,256]{5,4,3,2,1,0:T(8,128)}, u32[]{:S(2)}) %copy-start.7) | copy-done | bytes 262168
  13.3 0.9 %shard_map.131 = (f32[32,16,128]{2,1,0:T(8,128)S(1)}, f32[256,128]{1,0:T(8,128)S(1)}, f32[4,128]{1,0:T(4,128)S(1)}, f32[144,128]{1,0:T(8,128)S(1)}, f32[144,128]{1,0:T(8,128)S(1)}, /*index=5*/f32[144,128]{1,0:T(8,128)S(1)}) custom-call(s32[2,128]{1,0:T(2,128)S(1)} %copy-done.10, f32[4,128]{1,0:T(4,128)S(1)} %copy-done.11, f32[16,16,256]{2,1,0:T(8,128)S(1)} %bitcast.9, ...), custom_call_target="tpu_custom_call" | custom-call | tf_op jit(solution)/shard_map/pallas_call | solution.py:585
  14.2 0.0 collective-permute-done.rest_0_
  14.2 0.0 all-to-all-done.got
  14.3 0.0 copy-done.5
  14.3 0.0 copy-done.6
  14.3 0.0 copy-start.8
  14.3 0.0 copy-start.3
  14.3 1.6 %collective-permute-start.1 = (f32[104,128]{1,0:T(8,128)S(1)}, f32[104,128]{1,0:T(8,128)S(1)}, u32[]{:S(2)}, u32[]{:S(2)}) collective-permute-start(f32[104,128]{1,0:T(8,128)S(1)} %get-tuple-element.57), channel_id=1, source_target_pairs={{0,8},{8,16},{16,24},{24,0},{1,9},{9,17},{17,25},{25,1},{2,10},{10... | collective-permute-start | bytes 159752 | tf_op jit(solution)/shard_map/ppermute | solution.py:570
  16.0 2.2 %collective-permute-start.2 = (f32[104,128]{1,0:T(8,128)S(1)}, f32[104,128]{1,0:T(8,128)S(1)}, u32[]{:S(2)}, u32[]{:S(2)}) collective-permute-start(f32[104,128]{1,0:T(8,128)S(1)} %get-tuple-element.58), channel_id=1, source_target_pairs={{0,24},{8,0},{16,8},{24,16},{1,25},{9,1},{17,9},{25,17},{2,26},{10... | collective-permute-start | bytes 159752 | tf_op jit(solution)/shard_map/ppermute | solution.py:570
  18.2 0.0 collective-permute-start.6
  18.2 2.1 %collective-permute-start.7 = (f32[144,128]{1,0:T(8,128)S(1)}, f32[144,128]{1,0:T(8,128)S(1)}, u32[]{:S(2)}, u32[]{:S(2)}) collective-permute-start(f32[144,128]{1,0:T(8,128)S(1)} %get-tuple-element.69), channel_id=1, source_target_pairs={{0,24},{8,16},{16,8},{24,0},{1,25},{9,17},{17,9},{25,1},{2,26},{10... | collective-permute-start | bytes 221192 | tf_op jit(solution)/shard_map/ppermute | solution.py:574
  20.3 1.4 %collective-permute-start.8 = (f32[144,128]{1,0:T(8,128)S(1)}, f32[144,128]{1,0:T(8,128)S(1)}, u32[]{:S(2)}, u32[]{:S(2)}) collective-permute-start(f32[144,128]{1,0:T(8,128)S(1)} %get-tuple-element.70), channel_id=1, source_target_pairs={{0,8},{8,0},{16,24},{24,16},{1,9},{9,1},{17,25},{25,17},{2,10},{10... | collective-permute-start | bytes 221192 | tf_op jit(solution)/shard_map/ppermute | solution.py:574
  21.7 0.0 collective-permute-done.1.low
  21.7 0.0 collective-permute-done.2.high
  21.8 0.0 copy-start.4
  21.8 1.9 %shard_map.133 = (f32[8,32,128]{2,1,0:T(8,128)S(1)}, f32[32,128]{1,0:T(8,128)S(1)}, f32[32,128]{1,0:T(8,128)S(1)}, f32[32,128]{1,0:T(8,128)S(1)}, f32[32,128]{1,0:T(8,128)S(1)}) custom-call(s32[4,8]{1,0:T(4,128)S(1)} %maximum_convert_fusion.request, f32[8,32,128]{2,1,0:T(8,128)S(1)} %copy-done.5, f32[8,32,128]{2,1,0:T(8,128)S(1)} %copy-done.6, ...), custom_call_target="tpu_custom_call" | custom-call | tf_op jit(solution)/shard_map/pallas_call | solution.py:604
  23.7 1.0 %collective-permute-start.3 = (f32[32,128]{1,0:T(8,128)S(1)}, f32[32,128]{1,0:T(8,128)S(1)}, u32[]{:S(2)}, u32[]{:S(2)}) collective-permute-start(f32[32,128]{1,0:T(8,128)S(1)} %get-tuple-element.65), channel_id=1, source_target_pairs={{0,16},{8,24},{16,0},{24,8},{1,17},{9,25},{17,1},{25,9},{2,18},{10... | collective-permute-start | bytes 49160 | tf_op jit(solution)/shard_map/ppermute | solution.py:574
  24.6 2.3 %collective-permute-start.4 = (f32[32,128]{1,0:T(8,128)S(1)}, f32[32,128]{1,0:T(8,128)S(1)}, u32[]{:S(2)}, u32[]{:S(2)}) collective-permute-start(f32[32,128]{1,0:T(8,128)S(1)} %get-tuple-element.66), channel_id=1, source_target_pairs={{0,24},{8,16},{16,8},{24,0},{1,25},{9,17},{17,9},{25,1},{2,26},{10... | collective-permute-start | bytes 49160 | tf_op jit(solution)/shard_map/ppermute | solution.py:574
  27.0 0.0 collective-permute-done.6.rest_4_
  27.0 0.6 collective-permute-start.5
  27.5 0.0 copy-done.8
  27.5 0.5 shard_map.135
  28.0 0.0 collective-permute-done.7.rest_5_
  28.0 0.0 collective-permute-done.8.rest_6_
  28.1 0.3 collective-permute-done.3.rest_1_
  28.4 1.8 %collective-permute-done.4.rest_2_ = f32[32,128]{1,0:T(8,128)S(1)} collective-permute-done((f32[32,128]{1,0:T(8,128)S(1)}, f32[32,128]{1,0:T(8,128)S(1)}, u32[]{:S(2)}, u32[]{:S(2)}) %collective-permute-start.4) | collective-permute-done | bytes 16416 | tf_op jit(solution)/shard_map/ppermute | solution.py:574
  30.2 0.5 collective-permute-done.5.rest_3_
  30.7 1.7 %shard_map.136 = (f32[16,16,256]{2,1,0:T(8,128)S(1)}, f32[16,16,256]{2,1,0:T(8,128)S(1)}, f32[2,256,128]{2,1,0:T(8,128)S(1)}, f32[32,16,128]{2,1,0:T(8,128)S(1)}...) custom-call(s32[2,128]{1,0:T(2,128)S(1)} %copy-done.10, ...), custom_call_target="tpu_custom_call" | custom-call | tf_op jit(solution)/shard_map/pallas_call | solution.py:627
  32.4 2.0 %collective-permute-start.9 = (f32[144,128]{1,0:T(8,128)S(1)}, f32[144,128]{1,0:T(8,128)S(1)}, u32[]{:S(2)}, u32[]{:S(2)}) collective-permute-start(f32[144,128]{1,0:T(8,128)S(1)} %get-tuple-element.78), channel_id=1, source_target_pairs={{0,16},{8,24},{16,0},{24,8},{1,17},{9,25},{17,1},{25,9},{2,18},{10... | collective-permute-start | bytes 221192 | tf_op jit(solution)/shard_map/ppermute | solution.py:574
  34.4 1.0 %collective-permute-start.10 = (f32[144,128]{1,0:T(8,128)S(1)}, f32[144,128]{1,0:T(8,128)S(1)}, u32[]{:S(2)}, u32[]{:S(2)}) collective-permute-start(f32[144,128]{1,0:T(8,128)S(1)} %get-tuple-element.79), channel_id=1, source_target_pairs={{0,24},{8,16},{16,8},{24,0},{1,25},{9,17},{17,9},{25,1},{2,26},{10... | collective-permute-start | bytes 221192 | tf_op jit(solution)/shard_map/ppermute | solution.py:574
  35.4 0.6 collective-permute-start.11
  35.9 0.5 shard_map.137
  36.4 2.1 %collective-permute-done.9.rest_0_ = f32[144,128]{1,0:T(8,128)S(1)} collective-permute-done((f32[144,128]{1,0:T(8,128)S(1)}, f32[144,128]{1,0:T(8,128)S(1)}, u32[]{:S(2)}, u32[]{:S(2)}) %collective-permute-start.9) | collective-permute-done | bytes 73760 | tf_op jit(solution)/shard_map/ppermute | solution.py:574
  38.5 2.0 %collective-permute-done.10.rest_1_ = f32[144,128]{1,0:T(8,128)S(1)} collective-permute-done((f32[144,128]{1,0:T(8,128)S(1)}, f32[144,128]{1,0:T(8,128)S(1)}, u32[]{:S(2)}, u32[]{:S(2)}) %collective-permute-start.10) | collective-permute-done | bytes 73760 | tf_op jit(solution)/shard_map/ppermute | solution.py:574
  40.5 0.0 collective-permute-done.11.rest_2_
  40.5 1.2 %shard_map.138 = (f32[16,16,256]{2,1,0:T(8,128)S(1)}, f32[16,16,256]{2,1,0:T(8,128)S(1)}, f32[32,16,128]{2,1,0:T(8,128)S(1)}, f32[256,128]{1,0:T(8,128)S(1)}, f3...) custom-call(s32[2,128]{1,0:T(2,128)S(1)} %copy-done.10, ...), custom_call_target="tpu_custom_call" | custom-call | tf_op jit(solution)/shard_map/pallas_call | solution.py:641
  41.8 1.9 %collective-permute-start.12 = (f32[144,128]{1,0:T(8,128)S(1)}, f32[144,128]{1,0:T(8,128)S(1)}, u32[]{:S(2)}, u32[]{:S(2)}) collective-permute-start(f32[144,128]{1,0:T(8,128)S(1)} %get-tuple-element.87), channel_id=1, source_target_pairs={{0,16},{8,24},{16,0},{24,8},{1,17},{9,25},{17,1},{25,9},{2,18},{10... | collective-permute-start | bytes 221192 | tf_op jit(solution)/shard_map/ppermute | solution.py:574
  43.7 0.5 collective-permute-start.13
  44.2 1.2 %collective-permute-start.14 = (f32[144,128]{1,0:T(8,128)S(1)}, f32[144,128]{1,0:T(8,128)S(1)}, u32[]{:S(2)}, u32[]{:S(2)}) collective-permute-start(f32[144,128]{1,0:T(8,128)S(1)} %get-tuple-element.89), channel_id=1, source_target_pairs={{0,8},{8,0},{16,24},{24,16},{1,9},{9,1},{17,25},{25,17},{2,10},{10... | collective-permute-start | bytes 221192 | tf_op jit(solution)/shard_map/ppermute | solution.py:574
  45.3 0.5 shard_map.139
  45.8 1.5 %collective-permute-done.12.rest_0_ = f32[144,128]{1,0:T(8,128)S(1)} collective-permute-done((f32[144,128]{1,0:T(8,128)S(1)}, f32[144,128]{1,0:T(8,128)S(1)}, u32[]{:S(2)}, u32[]{:S(2)}) %collective-permute-start.12) | collective-permute-done | bytes 73760 | tf_op jit(solution)/shard_map/ppermute | solution.py:574
  47.3 3.0 %collective-permute-done.13.rest_1_ = f32[144,128]{1,0:T(8,128)S(1)} collective-permute-done((f32[144,128]{1,0:T(8,128)S(1)}, f32[144,128]{1,0:T(8,128)S(1)}, u32[]{:S(2)}, u32[]{:S(2)}) %collective-permute-start.13) | collective-permute-done | bytes 73760 | tf_op jit(solution)/shard_map/ppermute | solution.py:574
  50.3 0.0 collective-permute-done.14.rest_2_
  50.3 1.2 %shard_map.140 = (f32[16,16,256]{2,1,0:T(8,128)S(1)}, f32[16,16,256]{2,1,0:T(8,128)S(1)}, f32[32,16,128]{2,1,0:T(8,128)S(1)}, f32[256,128]{1,0:T(8,128)S(1)}, f3...) custom-call(s32[2,128]{1,0:T(2,128)S(1)} %copy-done.10, ...), custom_call_target="tpu_custom_call" | custom-call | tf_op jit(solution)/shard_map/pallas_call | solution.py:641
  51.6 2.7 %collective-permute-start.15 = (f32[144,128]{1,0:T(8,128)S(1)}, f32[144,128]{1,0:T(8,128)S(1)}, u32[]{:S(2)}, u32[]{:S(2)}) collective-permute-start(f32[144,128]{1,0:T(8,128)S(1)} %get-tuple-element.96), channel_id=1, source_target_pairs={{0,16},{8,24},{16,0},{24,8},{1,17},{9,25},{17,1},{25,9},{2,18},{10... | collective-permute-start | bytes 221192 | tf_op jit(solution)/shard_map/ppermute | solution.py:574
  54.3 0.4 collective-permute-start.16
  54.7 0.4 collective-permute-start.17
  55.1 0.7 %shard_map.134 = f32[8,32,128]{2,1,0:T(8,128)} custom-call(f32[8,32,128]{2,1,0:T(8,128)S(1)} %get-tuple-element.59.value), custom_call_target="tpu_custom_call" | custom-call | tf_op jit(solution)/shard_map/pallas_call | solution.py:611
  55.8 0.5 shard_map.141
  56.3 1.4 %collective-permute-done.15.rest_0_ = f32[144,128]{1,0:T(8,128)S(1)} collective-permute-done((f32[144,128]{1,0:T(8,128)S(1)}, f32[144,128]{1,0:T(8,128)S(1)}, u32[]{:S(2)}, u32[]{:S(2)}) %collective-permute-start.15) | collective-permute-done | bytes 73760 | tf_op jit(solution)/shard_map/ppermute | solution.py:574
  57.7 2.7 %collective-permute-done.16.rest_1_ = f32[144,128]{1,0:T(8,128)S(1)} collective-permute-done((f32[144,128]{1,0:T(8,128)S(1)}, f32[144,128]{1,0:T(8,128)S(1)}, u32[]{:S(2)}, u32[]{:S(2)}) %collective-permute-start.16) | collective-permute-done | bytes 73760 | tf_op jit(solution)/shard_map/ppermute | solution.py:574
  60.4 0.0 collective-permute-done.17.rest_2_
  60.4 1.6 %shard_map.142 = (f32[16,16,256]{2,1,0:T(8,128)}, f32[16,16,256]{2,1,0:T(8,128)}) custom-call(s32[2,128]{1,0:T(2,128)S(1)} %copy-done.10, f32[16,16,256]{2,1,0:T(8,128)S(1)} %get-tuple-element.92.phase, f32[16,16,256]{2,1,0:T(8,128)S(1)} %get-tuple-element.93.solute, f32[32,16,128]{2,1,0:T(8,128)S(1)} %get-tuple-element.94.own, ...), custom_call_target="tpu_custom_call" | custom-call | tf_op jit(solution)/shard_map/pallas_call | solution.py:650
  (18 shorter events, 0.1 us)
Async XLA Ops:
  0.6 10.1 %copy-start.1 = (bf16[512,256]{1,0:T(8,128)(2,1)S(1)}, bf16[512,256]{1,0:T(8,128)(2,1)}, u32[]{:S(2)}) copy-start(bf16[512,256]{1,0:T(8,128)(2,1)} %constant.8.clone.picks) | copy-start | bytes 786436
  2.9 5.2 %copy-start.12 = (f32[8,128]{1,0:T(8,128)S(1)}, f32[8,128]{1,0:T(8,128)}, u32[]{:S(2)}) copy-start(f32[8,128]{1,0:T(8,128)} %get-tuple-element.56) | copy-start | bytes 12292
  2.9 11.4 %all-to-all-start = ((f32[8,24,128]{2,1,0:T(8,128)}), f32[8,24,128]{2,1,0:T(8,128)S(1)}, u32[]{:S(2)}, u32[]{:S(2)}) async-start(f32[8,24,128]{2,1,0:T(8,128)} %get-tuple-element.55), calls=%async_computation | async-start | bytes 196608 | tf_op jit(solution)/shard_map/all_to_all | solution.py:567
  8.1 6.2 %collective-permute-start = (f32[8,128]{1,0:T(8,128)S(1)}, f32[8,128]{1,0:T(8,128)S(1)}, u32[]{:S(2)}, u32[]{:S(2)}) collective-permute-start(f32[8,128]{1,0:T(8,128)S(1)} %copy-done.12), channel_id=1, source_target_pairs={{0,16},{8,24},{16,0},{24,8},{1,17},{9,25},{17,1},{25,9},{2,18},{10... | collective-permute-start | bytes 12296 | tf_op jit(solution)/shard_map/ppermute | solution.py:570
  10.7 0.7 %copy-start.11 = (f32[4,128]{1,0:T(4,128)S(1)}, f32[4,128]{1,0:T(4,128)}, u32[]{:S(2)}) copy-start(f32[4,128]{1,0:T(4,128)} %get-tuple-element.53.asked) | copy-start | bytes 6148
  10.7 0.7 %copy-start.10 = (s32[2,128]{1,0:T(2,128)S(1)}, s32[2,128]{1,0:T(2,128)}, u32[]{:S(2)}) copy-start(s32[2,128]{1,0:T(2,128)} %get-tuple-element.52.table) | copy-start | bytes 3076
  11.4 0.9 %copy-start.2 = (f32[1,1,1,16,16,256]{5,4,3,2,1,0:T(8,128)S(1)}, f32[1,1,1,16,16,256]{5,4,3,2,1,0:T(8,128)}, u32[]{:S(2)}) copy-start(f32[1,1,1,16,16,256]{5,4,3,2,1,0:T(8,128)} %param.13) | copy-start | bytes 786436
  12.4 0.9 %copy-start.7 = (f32[1,1,1,16,16,256]{5,4,3,2,1,0:T(8,128)S(1)}, f32[1,1,1,16,16,256]{5,4,3,2,1,0:T(8,128)}, u32[]{:S(2)}) copy-start(f32[1,1,1,16,16,256]{5,4,3,2,1,0:T(8,128)} %param.14) | copy-start | bytes 786436
  13.3 1.0 %copy-start.5 = (f32[8,32,128]{2,1,0:T(8,128)S(1)}, f32[8,32,128]{2,1,0:T(8,128)}, u32[]{:S(2)}) copy-start(f32[8,32,128]{2,1,0:T(8,128)} %h.3) | copy-start | bytes 393220
  13.3 1.0 %copy-start.6 = (f32[8,32,128]{2,1,0:T(8,128)S(1)}, f32[8,32,128]{2,1,0:T(8,128)}, u32[]{:S(2)}) copy-start(f32[8,32,128]{2,1,0:T(8,128)} %k.3) | copy-start | bytes 393220
  14.3 13.3 %copy-start.8 = (f32[1,1,1,16,16,256]{5,4,3,2,1,0:T(8,128)S(1)}, f32[1,1,1,16,16,256]{5,4,3,2,1,0:T(8,128)}, u32[]{:S(2)}) copy-start(f32[1,1,1,16,16,256]{5,4,3,2,1,0:T(8,128)} %param.14) | copy-start | bytes 786436
  14.3 13.2 %copy-start.3 = (f32[1,1,1,16,16,256]{5,4,3,2,1,0:T(8,128)S(1)}, f32[1,1,1,16,16,256]{5,4,3,2,1,0:T(8,128)}, u32[]{:S(2)}) copy-start(f32[1,1,1,16,16,256]{5,4,3,2,1,0:T(8,128)} %param.13) | copy-start | bytes 786436
  14.3 7.4 %collective-permute-start.1 = (f32[104,128]{1,0:T(8,128)S(1)}, f32[104,128]{1,0:T(8,128)S(1)}, u32[]{:S(2)}, u32[]{:S(2)}) collective-permute-start(f32[104,128]{1,0:T(8,128)S(1)} %get-tuple-element.57), channel_id=1, source_target_pairs={{0,8},{8,16},{16,24},{24,0},{1,9},{9,17},{17,25},{25,1},{2,10},{10... | collective-permute-start | bytes 159752 | tf_op jit(solution)/shard_map/ppermute | solution.py:570
  16.0 5.8 %collective-permute-start.2 = (f32[104,128]{1,0:T(8,128)S(1)}, f32[104,128]{1,0:T(8,128)S(1)}, u32[]{:S(2)}, u32[]{:S(2)}) collective-permute-start(f32[104,128]{1,0:T(8,128)S(1)} %get-tuple-element.58), channel_id=1, source_target_pairs={{0,24},{8,0},{16,8},{24,16},{1,25},{9,1},{17,9},{25,17},{2,26},{10... | collective-permute-start | bytes 159752 | tf_op jit(solution)/shard_map/ppermute | solution.py:570
  18.2 8.8 %collective-permute-start.6 = (f32[144,128]{1,0:T(8,128)S(1)}, f32[144,128]{1,0:T(8,128)S(1)}, u32[]{:S(2)}, u32[]{:S(2)}) collective-permute-start(f32[144,128]{1,0:T(8,128)S(1)} %get-tuple-element.68), channel_id=1, source_target_pairs={{0,16},{8,24},{16,0},{24,8},{1,17},{9,25},{17,1},{25,9},{2,18},{10... | collective-permute-start | bytes 221192 | tf_op jit(solution)/shard_map/ppermute | solution.py:574
  18.2 9.8 %collective-permute-start.7 = (f32[144,128]{1,0:T(8,128)S(1)}, f32[144,128]{1,0:T(8,128)S(1)}, u32[]{:S(2)}, u32[]{:S(2)}) collective-permute-start(f32[144,128]{1,0:T(8,128)S(1)} %get-tuple-element.69), channel_id=1, source_target_pairs={{0,24},{8,16},{16,8},{24,0},{1,25},{9,17},{17,9},{25,1},{2,26},{10... | collective-permute-start | bytes 221192 | tf_op jit(solution)/shard_map/ppermute | solution.py:574
  20.3 7.7 %collective-permute-start.8 = (f32[144,128]{1,0:T(8,128)S(1)}, f32[144,128]{1,0:T(8,128)S(1)}, u32[]{:S(2)}, u32[]{:S(2)}) collective-permute-start(f32[144,128]{1,0:T(8,128)S(1)} %get-tuple-element.70), channel_id=1, source_target_pairs={{0,8},{8,0},{16,24},{24,16},{1,9},{9,1},{17,25},{25,17},{2,10},{10... | collective-permute-start | bytes 221192 | tf_op jit(solution)/shard_map/ppermute | solution.py:574
  21.8 5.8 %copy-start.4 = (bf16[256,256]{1,0:T(8,128)(2,1)S(1)}, bf16[256,256]{1,0:T(8,128)(2,1)}, u32[]{:S(2)}) copy-start(bf16[256,256]{1,0:T(8,128)(2,1)} %constant.9.clone.stencil) | copy-start | bytes 393220
  23.7 4.7 %collective-permute-start.3 = (f32[32,128]{1,0:T(8,128)S(1)}, f32[32,128]{1,0:T(8,128)S(1)}, u32[]{:S(2)}, u32[]{:S(2)}) collective-permute-start(f32[32,128]{1,0:T(8,128)S(1)} %get-tuple-element.65), channel_id=1, source_target_pairs={{0,16},{8,24},{16,0},{24,8},{1,17},{9,25},{17,1},{25,9},{2,18},{10... | collective-permute-start | bytes 49160 | tf_op jit(solution)/shard_map/ppermute | solution.py:574
  24.6 5.5 %collective-permute-start.4 = (f32[32,128]{1,0:T(8,128)S(1)}, f32[32,128]{1,0:T(8,128)S(1)}, u32[]{:S(2)}, u32[]{:S(2)}) collective-permute-start(f32[32,128]{1,0:T(8,128)S(1)} %get-tuple-element.66), channel_id=1, source_target_pairs={{0,24},{8,16},{16,8},{24,0},{1,25},{9,17},{17,9},{25,1},{2,26},{10... | collective-permute-start | bytes 49160 | tf_op jit(solution)/shard_map/ppermute | solution.py:574
  27.0 3.7 %copy-start = (bf16[256,512]{1,0:T(8,128)(2,1)S(1)}, bf16[256,512]{1,0:T(8,128)(2,1)}, u32[]{:S(2)}) copy-start(bf16[256,512]{1,0:T(8,128)(2,1)} %constant.10.clone.places) | copy-start | bytes 786436
  27.0 3.7 %copy-start.9 = (bf16[256,256]{1,0:T(8,128)(2,1)S(1)}, bf16[256,256]{1,0:T(8,128)(2,1)}, u32[]{:S(2)}) copy-start(bf16[256,256]{1,0:T(8,128)(2,1)} %constant.11.clone.spreads) | copy-start | bytes 393220
  27.0 3.7 %collective-permute-start.5 = (f32[32,128]{1,0:T(8,128)S(1)}, f32[32,128]{1,0:T(8,128)S(1)}, u32[]{:S(2)}, u32[]{:S(2)}) collective-permute-start(f32[32,128]{1,0:T(8,128)S(1)} %get-tuple-element.67), channel_id=1, source_target_pairs={{0,8},{8,0},{16,24},{24,16},{1,9},{9,1},{17,25},{25,17},{2,10},{10... | collective-permute-start | bytes 49160 | tf_op jit(solution)/shard_map/ppermute | solution.py:574
  32.4 6.1 %collective-permute-start.9 = (f32[144,128]{1,0:T(8,128)S(1)}, f32[144,128]{1,0:T(8,128)S(1)}, u32[]{:S(2)}, u32[]{:S(2)}) collective-permute-start(f32[144,128]{1,0:T(8,128)S(1)} %get-tuple-element.78), channel_id=1, source_target_pairs={{0,16},{8,24},{16,0},{24,8},{1,17},{9,25},{17,1},{25,9},{2,18},{10... | collective-permute-start | bytes 221192 | tf_op jit(solution)/shard_map/ppermute | solution.py:574
  34.4 6.2 %collective-permute-start.10 = (f32[144,128]{1,0:T(8,128)S(1)}, f32[144,128]{1,0:T(8,128)S(1)}, u32[]{:S(2)}, u32[]{:S(2)}) collective-permute-start(f32[144,128]{1,0:T(8,128)S(1)} %get-tuple-element.79), channel_id=1, source_target_pairs={{0,24},{8,16},{16,8},{24,0},{1,25},{9,17},{17,9},{25,1},{2,26},{10... | collective-permute-start | bytes 221192 | tf_op jit(solution)/shard_map/ppermute | solution.py:574
  35.4 5.2 %collective-permute-start.11 = (f32[144,128]{1,0:T(8,128)S(1)}, f32[144,128]{1,0:T(8,128)S(1)}, u32[]{:S(2)}, u32[]{:S(2)}) collective-permute-start(f32[144,128]{1,0:T(8,128)S(1)} %get-tuple-element.80), channel_id=1, source_target_pairs={{0,8},{8,0},{16,24},{24,16},{1,9},{9,1},{17,25},{25,17},{2,10},{10... | collective-permute-start | bytes 221192 | tf_op jit(solution)/shard_map/ppermute | solution.py:574
  41.8 5.5 %collective-permute-start.12 = (f32[144,128]{1,0:T(8,128)S(1)}, f32[144,128]{1,0:T(8,128)S(1)}, u32[]{:S(2)}, u32[]{:S(2)}) collective-permute-start(f32[144,128]{1,0:T(8,128)S(1)} %get-tuple-element.87), channel_id=1, source_target_pairs={{0,16},{8,24},{16,0},{24,8},{1,17},{9,25},{17,1},{25,9},{2,18},{10... | collective-permute-start | bytes 221192 | tf_op jit(solution)/shard_map/ppermute | solution.py:574
  43.7 6.7 %collective-permute-start.13 = (f32[144,128]{1,0:T(8,128)S(1)}, f32[144,128]{1,0:T(8,128)S(1)}, u32[]{:S(2)}, u32[]{:S(2)}) collective-permute-start(f32[144,128]{1,0:T(8,128)S(1)} %get-tuple-element.88), channel_id=1, source_target_pairs={{0,24},{8,16},{16,8},{24,0},{1,25},{9,17},{17,9},{25,1},{2,26},{10... | collective-permute-start | bytes 221192 | tf_op jit(solution)/shard_map/ppermute | solution.py:574
  44.2 6.1 %collective-permute-start.14 = (f32[144,128]{1,0:T(8,128)S(1)}, f32[144,128]{1,0:T(8,128)S(1)}, u32[]{:S(2)}, u32[]{:S(2)}) collective-permute-start(f32[144,128]{1,0:T(8,128)S(1)} %get-tuple-element.89), channel_id=1, source_target_pairs={{0,8},{8,0},{16,24},{24,16},{1,9},{9,1},{17,25},{25,17},{2,10},{10... | collective-permute-start | bytes 221192 | tf_op jit(solution)/shard_map/ppermute | solution.py:574
  51.6 6.1 %collective-permute-start.15 = (f32[144,128]{1,0:T(8,128)S(1)}, f32[144,128]{1,0:T(8,128)S(1)}, u32[]{:S(2)}, u32[]{:S(2)}) collective-permute-start(f32[144,128]{1,0:T(8,128)S(1)} %get-tuple-element.96), channel_id=1, source_target_pairs={{0,16},{8,24},{16,0},{24,8},{1,17},{9,25},{17,1},{25,9},{2,18},{10... | collective-permute-start | bytes 221192 | tf_op jit(solution)/shard_map/ppermute | solution.py:574
  54.3 6.2 %collective-permute-start.16 = (f32[144,128]{1,0:T(8,128)S(1)}, f32[144,128]{1,0:T(8,128)S(1)}, u32[]{:S(2)}, u32[]{:S(2)}) collective-permute-start(f32[144,128]{1,0:T(8,128)S(1)} %get-tuple-element.97), channel_id=1, source_target_pairs={{0,24},{8,16},{16,8},{24,0},{1,25},{9,17},{17,9},{25,1},{2,26},{10... | collective-permute-start | bytes 221192 | tf_op jit(solution)/shard_map/ppermute | solution.py:574
  54.7 5.7 %collective-permute-start.17 = (f32[144,128]{1,0:T(8,128)S(1)}, f32[144,128]{1,0:T(8,128)S(1)}, u32[]{:S(2)}, u32[]{:S(2)}) collective-permute-start(f32[144,128]{1,0:T(8,128)S(1)} %get-tuple-element.98), channel_id=1, source_target_pairs={{0,8},{8,0},{16,24},{24,16},{1,9},{9,1},{17,25},{25,17},{2,10},{10... | collective-permute-start | bytes 221192 | tf_op jit(solution)/shard_map/ppermute | solution.py:574

commit v16 on v15

--- a/solution.py
+++ b/solution.py
@@ -152,9 +152,6 @@
             position = jnp.where(swap == other, float(at), position)
         return position
 
-    def wrapped(shift):
-        return jnp.where(shift < 0.0, shift + float(count), shift)
-
     square = (SLOTS, SLOTS)
     before = iota(square, 0) < iota(square, 1)
     slot = iota((1, SLOTS), 1).astype(F32)
@@ -165,14 +162,15 @@
     )
     rank_column = column_of(rank)
     lane = iota((SLOTS, 128), 1).astype(F32)
+    swap = source[...] ^ here
+    swap_column = column_of(swap.astype(F32))
     for shift in range(count):
-        hit = (wrapped(source_column - me) == float(shift)) & (rank_column == lane)
+        hit = (swap_column == float(shift)) & (rank_column == lane)
         row = jnp.sum(jnp.where(hit, block_column, 0.0), axis=0, keepdims=True)
         asked[shift : shift + 1, :] = row
-        if 2 <= shift < count - 1:
+        if shift > 1:
             farther[shift - 2][...] = jnp.broadcast_to(row, (8, 128))
     at = FACES * SLOTS
-    swap = source[...] ^ here
     found = jnp.where(swap == 0, 0.0, 1.0 + position_of(swap))
     table[0:1, at : at + SLOTS] = found.astype(jnp.int32)
     table[0:1, at + SLOTS : at + 2 * SLOTS] = rank.astype(jnp.int32)
@@ -245,18 +243,20 @@
 
 
 def layers_kernel(sizes, h, k, got, asked, *rest):
-    down, up = rest[-2:]
+    first, second = rest[-2:]
     bx, by, bz = h.shape
     read = side_reader(sizes, got, bx)
+    even = lax.rem(lax.axis_index("gx"), 2) == 0
     around = [read(-1, 0), read(1, 0), read(0, -1), read(0, 1)]
-    last = asked.shape[0] - 1
-    for out, near, far, ask in ((down, 0, 1, last), (up, bx - 1, bx - 2, 1)):
-        out[0:by, :] = h[near]
-        out[by : 2 * by, :] = h[far]
-        out[2 * by : 3 * by, :] = k[near]
-        for number, side in enumerate(around):
-            out[3 * by + number : 3 * by + number + 1, :] = side[near : near + 1, :]
-        out[3 * by + 4 : 3 * by + 8, :] = jnp.broadcast_to(asked[ask : ask + 1, :], (4, bz))
+    layers = [(h[bx - 1], h[0]), (h[bx - 2], h[1]), (k[bx - 1], k[0])]
+    layers += [(side[bx - 1 : bx, :], side[0:1, :]) for side in around]
+    row = 0
+    for upper, lower in layers:
+        first[row : row + upper.shape[0], :] = jnp.where(even, upper, lower)
+        second[row : row + upper.shape[0], :] = jnp.where(even, lower, upper)
+        row += upper.shape[0]
+    for out in (first, second):
+        out[row:, :] = jnp.broadcast_to(asked[1:2, :], (out.shape[0] - row, bz))
 
 
 def block_layout(cap):
@@ -276,7 +276,7 @@
     return h + RATE * k * (total - 6.0 * t)
 
 
-def heat_kernel(cap, sizes, request, h, k, got, low, high, out, found, *rest):
+def heat_kernel(cap, sizes, request, h, k, got, first, second, out, found, *rest):
     *send, held = rest
     count = lax.axis_size("gx")
     bx, by, bz = h.shape
@@ -284,8 +284,11 @@
     read = side_reader(sizes, got, bx)
     me = lax.axis_index("gx")
     layers, lines = [], []
+    even = lax.rem(me, 2) == 0
+    pairs = (first[...], second[...])
+    low, high = jnp.where(even, *pairs[::-1]), jnp.where(even, *pairs)
     for beside, inside in ((low, me > 0), (high, me < count - 1)):
-        beside = jnp.where(inside, beside[...], 0.0)
+        beside = jnp.where(inside, beside, 0.0)
         layers.append([beside[part * by : part * by + by, :][None] for part in range(3)])
         lines.append([beside[3 * by + n : 3 * by + n + 1, :] for n in range(4)])
     y_sides = [[read(d, 0, part) for part in range(3)] for d in (-1, 1)]
@@ -325,10 +328,9 @@
     nby, nbz = by // CB, bz // CB
     group = iota((deep, CB, bz), 2) // CB
     for out, swap in zip((found, *send), (0, *swap_order(count))):
-        back = lax.rem(me - (me ^ swap) + count, count)
         total = jnp.zeros((deep, CB, bz), F32)
         for rank in range(cap):
-            block = request[back, rank]
+            block = request[swap, rank]
             a, b, c = block // (nby * nbz), (block // nbz) % nby, block % nbz
             for part in range(parts):
                 at = rank * parts + part
@@ -546,7 +548,7 @@
             shape(sizes[0] * sizes[1], 3 * bx, 128),
             integers((table_sizes(count, plane_cap)[2], 128)),
             shape(count, 128),
-            *[shape(8, 128)] * (count - 3),
+            *[shape(8, 128)] * (count - 2),
         ],
         [
             pltpu.VMEM((1, SLOTS), jnp.int32),
@@ -566,16 +568,16 @@
     )
     sides = lax.all_to_all(sides, ("gy", "gz"), split_axis=0, concat_axis=0, tiled=True)
 
-    def pass_on(value, shift):
-        return lax.ppermute(value, "gx", [(i, (i + shift) % count) for i in range(count)])
+    def swap_with(value, partner):
+        return lax.ppermute(value, "gx", [(i, partner(i)) for i in range(count)])
 
     def swap_all(values):
         return [
-            lax.ppermute(value, "gx", [(i, i ^ swap) for i in range(count)])
+            swap_with(value, lambda i, swap=swap: i ^ swap)
             for swap, value in zip(swap_order(count), values)
         ]
 
-    farther = [pass_on(value, shift) for shift, value in enumerate(farther, 2)]
+    farther = [swap_with(value, lambda i, s=s: i ^ s) for s, value in enumerate(farther, 2)]
 
     phase_field = phase.reshape(SLOTS, TE, PLANE)
     solute_field = solute.reshape(SLOTS, TE, PLANE)
@@ -591,12 +593,13 @@
     own, asked, packed = packed[:2], packed[2], packed[3:]
 
     layer = shape(3 * by + 8, bz)
-    down, up = call(
+    first, second = call(
         functools.partial(layers_kernel, sizes), [VMEM] * 4 + [ANY] * len(farther), [layer, layer]
     )(enthalpy, conductivity, sides, asked, *farther)
-    from_low, from_high = pass_on(up, 1), pass_on(down, others)
+    first = swap_with(first, lambda i: i ^ 1)
+    second = swap_with(second, lambda i: i if i in (0, others) else ((i + 1) ^ 1) - 1)
     row = 3 * by + 4
-    request = [asked[0], from_low[row], *[value[0] for value in farther], from_high[row]]
+    request = [asked[0], first[row], *[value[0] for value in farther]]
     request = jnp.stack([value[:block_cap] for value in request]).astype(jnp.int32)
     _, deep = block_layout(block_cap)
     brick = shape(bx, by, bz)
@@ -606,7 +609,7 @@
         [SMEM] + [VMEM] * 5,
         [brick] + [shape(deep * CB, 128)] * count,
         [pltpu.VMEM((bx, by // CB, CB, bz), F32)],
-    )(request, enthalpy, conductivity, sides, from_low, from_high)
+    )(request, enthalpy, conductivity, sides, first, second)
     found[1:] = swap_all(found[1:])
     (heat_out,) = call(write_out_kernel, [ANY], [brick], [pltpu.SemaphoreType.DMA], [ANY])(heated)
 

time: 62.4 us -> 67.2 us (1.077)
  starting transfers between devices: 29.7 us -> 34.7 us
    ppermute x18 -> x19, starting transfers between devices: 24.5 us -> 29.5 us  [swap_with(): return lax.ppermute(value, 'gx', [(i, partner(i)) for i in range(count)])]
    ppermute x18 -> x19, waiting for transfers between devices: 15.4 us -> 15 us  [swap_with(): return lax.ppermute(value, 'gx', [(i, partner(i)) for i in range(count)])]
    unnamed x26 -> x28, local copies, waits for them, and re-layouts: 2.63 us -> 2.63 us
  transfers between devices with their start and end apart: 19 -> 20, of which waited for: 9 -> 12; matrix products, arithmetic and copies ran while one was open for 0% -> 0% of each run, Pallas kernels for 9% -> 8%
where the time goes in v16:
time: 67.2 us; the launch traced here: 66.7 us
  starting transfers between devices  34.7 us (52%)
  waiting for transfers between devices  15 us (22%)
  Pallas kernels  13.4 us (20%)
  local copies, waits for them, and re-layouts  2.64 us (4%)
  between operations  0.9 us (1%)
    ppermute x19, starting transfers between devices, swap_with(): return lax.ppermute(value, 'gx', [(i, partner(i)) for i in range(count)])  29.5 us
    ppermute x19, waiting for transfers between devices, swap_with(): return lax.ppermute(value, 'gx', [(i, partner(i)) for i in range(count)])  15 us
    all_to_all x1, starting transfers between devices, local(): lax.all_to_all(sides, ('gy', 'gz'), split_axis=0, concat_axis=0, tiled=True)  5.18 us
    unnamed x28, local copies, waits for them, and re-layouts  2.63 us
    pallas_call x2, Pallas kernels, local(): call(middle_step_kernel, [SMEM] + [VMEM] * (6 + others), [field, field, *...  2.45 us
    pallas_call x1, Pallas kernels, local(): call(functools.partial(sides_kernel, sizes, plane_cap), [ANY] * 5, [shape...  2.21 us
    pallas_call x4, Pallas kernels, inner(): call(functools.partial(inner_kernel, bool(heat)), [VMEM] * (3 + len(heat)...  1.97 us
    pallas_call x1, Pallas kernels, local(): call(functools.partial(heat_kernel, block_cap, sizes), [SMEM] + [VMEM] *...  1.91 us
  transfers between devices with their start and end apart: 20, of which 12 were waited for; matrix products, arithmetic and copies ran while one was open for 0% of the time, Pallas kernels for 8%

profile of v16, /device:TPU:0, one launch (start us, length us, event | category | flops | bytes accessed | tf_op | source)
XLA Modules:
  0.0 66.7 jit_solution(9909095228187353017)
XLA Ops:
  0.6 0.0 copy-start.1
  0.6 2.2 %shard_map.130 = (f32[8,24,128]{2,1,0:T(8,128)}, s32[2,128]{1,0:T(2,128)}, f32[4,128]{1,0:T(4,128)}, f32[8,128]{1,0:T(8,128)}, f32[8,128]{1,0:T(8,128)}) custom-call(s32[1,16]{1,0:T(1,128)} %bitcast.15, s32[1,16]{1,0:T(1,128)} %bitcast.16, s32[6,1,16]{2,1,0:T(1,128)} %bitcast.14, f32[8,32,128]{2,1,0:T(8,128)} %h.3, f32[8,32,128]{2,1,0:T(8,128)} %k.3), custom_call_target="tpu_custom_call" | custom-call | tf_op jit(solution)/shard_map/pallas_call | solution.py:544
  2.9 0.0 copy-start.13
  2.9 0.0 copy-start.12
  2.9 5.2 %all-to-all-start = ((f32[8,24,128]{2,1,0:T(8,128)}), f32[8,24,128]{2,1,0:T(8,128)S(1)}, u32[]{:S(2)}, u32[]{:S(2)}) async-start(f32[8,24,128]{2,1,0:T(8,128)} %get-tuple-element.56), calls=%async_computation | async-start | bytes 196608 | tf_op jit(solution)/shard_map/all_to_all | solution.py:569
  8.1 2.7 %collective-permute-start = (f32[8,128]{1,0:T(8,128)S(1)}, f32[8,128]{1,0:T(8,128)S(1)}, u32[]{:S(2)}, u32[]{:S(2)}) collective-permute-start(f32[8,128]{1,0:T(8,128)S(1)} %copy-done.13), channel_id=1, source_target_pairs={{0,16},{8,24},{16,0},{24,8},{1,17},{9,25},{17,1},{25,9},{2,18},{10... | collective-permute-start | bytes 12296 | tf_op jit(solution)/shard_map/ppermute | solution.py:572
  10.7 1.3 %collective-permute-start.1 = (f32[8,128]{1,0:T(8,128)S(1)}, f32[8,128]{1,0:T(8,128)S(1)}, u32[]{:S(2)}, u32[]{:S(2)}) collective-permute-start(f32[8,128]{1,0:T(8,128)S(1)} %copy-done.12), channel_id=1, source_target_pairs={{0,24},{8,16},{16,8},{24,0},{1,25},{9,17},{17,9},{25,1},{2,26},{10... | collective-permute-start | bytes 12296 | tf_op jit(solution)/shard_map/ppermute | solution.py:572
  12.1 0.7 %copy-done.11 = f32[4,128]{1,0:T(4,128)S(1)} copy-done((f32[4,128]{1,0:T(4,128)S(1)}, f32[4,128]{1,0:T(4,128)}, u32[]{:S(2)}) %copy-start.11) | copy-done | bytes 2072
  12.8 0.9 %copy-done.2 = f32[1,1,1,16,16,256]{5,4,3,2,1,0:T(8,128)S(1)} copy-done((f32[1,1,1,16,16,256]{5,4,3,2,1,0:T(8,128)S(1)}, f32[1,1,1,16,16,256]{5,4,3,2,1,0:T(8,128)}, u32[]{:S(2)}) %copy-start.2) | copy-done | bytes 262168
  13.7 0.9 %copy-done.7 = f32[1,1,1,16,16,256]{5,4,3,2,1,0:T(8,128)S(1)} copy-done((f32[1,1,1,16,16,256]{5,4,3,2,1,0:T(8,128)S(1)}, f32[1,1,1,16,16,256]{5,4,3,2,1,0:T(8,128)}, u32[]{:S(2)}) %copy-start.7) | copy-done | bytes 262168
  14.7 0.9 %shard_map.131 = (f32[32,16,128]{2,1,0:T(8,128)S(1)}, f32[256,128]{1,0:T(8,128)S(1)}, f32[4,128]{1,0:T(4,128)S(1)}, f32[144,128]{1,0:T(8,128)S(1)}, f32[144,128]{1,0:T(8,128)S(1)}, /*index=5*/f32[144,128]{1,0:T(8,128)S(1)}) custom-call(s32[2,128]{1,0:T(2,128)S(1)} %copy-done.10, f32[4,128]{1,0:T(4,128)S(1)} %copy-done.11, f32[16,16,256]{2,1,0:T(8,128)S(1)} %bitcast.9, ...), custom_call_target="tpu_custom_call" | custom-call | tf_op jit(solution)/shard_map/pallas_call | solution.py:587
  15.6 0.0 collective-permute-done.rest_0_
  15.6 0.5 collective-permute-done.1.rest_1_
  16.1 0.0 all-to-all-done.got
  16.2 0.0 copy-start.8
  16.2 0.0 copy-start.3
  16.2 0.1 collective-permute-start.2
  16.3 2.5 %collective-permute-start.7 = (f32[144,128]{1,0:T(8,128)S(1)}, f32[144,128]{1,0:T(8,128)S(1)}, u32[]{:S(2)}, u32[]{:S(2)}) collective-permute-start(f32[144,128]{1,0:T(8,128)S(1)} %get-tuple-element.70), channel_id=1, source_target_pairs={{0,16},{8,24},{16,0},{24,8},{1,17},{9,25},{17,1},{25,9},{2,18},{10... | collective-permute-start | bytes 221192 | tf_op jit(solution)/shard_map/ppermute | solution.py:572
  18.8 1.9 %collective-permute-start.8 = (f32[144,128]{1,0:T(8,128)S(1)}, f32[144,128]{1,0:T(8,128)S(1)}, u32[]{:S(2)}, u32[]{:S(2)}) collective-permute-start(f32[144,128]{1,0:T(8,128)S(1)} %get-tuple-element.71), channel_id=1, source_target_pairs={{0,24},{8,16},{16,8},{24,0},{1,25},{9,17},{17,9},{25,1},{2,26},{10... | collective-permute-start | bytes 221192 | tf_op jit(solution)/shard_map/ppermute | solution.py:572
  20.7 0.0 collective-permute-start.9
  20.7 0.7 collective-permute-start.3
  21.4 0.0 collective-permute-done.2.first
  21.4 0.0 copy-start.4
  21.4 0.0 collective-permute-done.3.second
  21.4 1.9 %shard_map.133 = (f32[8,32,128]{2,1,0:T(8,128)S(1)}, f32[32,128]{1,0:T(8,128)S(1)}, f32[32,128]{1,0:T(8,128)S(1)}, f32[32,128]{1,0:T(8,128)S(1)}, f32[32,128]{1,0:T(8,128)S(1)}) custom-call(s32[4,8]{1,0:T(4,128)S(1)} %maximum_convert_fusion.request, f32[8,32,128]{2,1,0:T(8,128)S(1)} %copy-done.5, f32[8,32,128]{2,1,0:T(8,128)S(1)} %copy-done.6, ...), custom_call_target="tpu_custom_call" | custom-call | tf_op jit(solution)/shard_map/pallas_call | solution.py:607
  23.3 7.9 %collective-permute-start.4 = (f32[32,128]{1,0:T(8,128)S(1)}, f32[32,128]{1,0:T(8,128)S(1)}, u32[]{:S(2)}, u32[]{:S(2)}) collective-permute-start(f32[32,128]{1,0:T(8,128)S(1)} %get-tuple-element.67), channel_id=1, source_target_pairs={{0,16},{8,24},{16,0},{24,8},{1,17},{9,25},{17,1},{25,9},{2,18},{10... | collective-permute-start | bytes 49160 | tf_op jit(solution)/shard_map/ppermute | solution.py:572
  31.2 1.9 %collective-permute-start.5 = (f32[32,128]{1,0:T(8,128)S(1)}, f32[32,128]{1,0:T(8,128)S(1)}, u32[]{:S(2)}, u32[]{:S(2)}) collective-permute-start(f32[32,128]{1,0:T(8,128)S(1)} %get-tuple-element.68), channel_id=1, source_target_pairs={{0,24},{8,16},{16,8},{24,0},{1,25},{9,17},{17,9},{25,1},{2,26},{10... | collective-permute-start | bytes 49160 | tf_op jit(solution)/shard_map/ppermute | solution.py:572
  33.0 0.0 collective-permute-done.7.rest_4_
  33.1 0.0 collective-permute-start.6
  33.1 0.0 copy-done.8
  33.1 0.0 copy-done.3
  33.1 0.0 copy-done.4
  33.1 0.5 shard_map.135
  33.6 0.0 collective-permute-done.8.rest_5_
  33.6 0.0 collective-permute-done.9.rest_6_
  33.6 0.0 collective-permute-done.4.rest_1_
  33.6 3.1 %collective-permute-done.5.rest_2_ = f32[32,128]{1,0:T(8,128)S(1)} collective-permute-done((f32[32,128]{1,0:T(8,128)S(1)}, f32[32,128]{1,0:T(8,128)S(1)}, u32[]{:S(2)}, u32[]{:S(2)}) %collective-permute-start.5) | collective-permute-done | bytes 16416 | tf_op jit(solution)/shard_map/ppermute | solution.py:572
  36.7 0.2 collective-permute-done.6.rest_3_
  36.9 1.7 %shard_map.136 = (f32[16,16,256]{2,1,0:T(8,128)S(1)}, f32[16,16,256]{2,1,0:T(8,128)S(1)}, f32[2,256,128]{2,1,0:T(8,128)S(1)}, f32[32,16,128]{2,1,0:T(8,128)S(1)}...) custom-call(s32[2,128]{1,0:T(2,128)S(1)} %copy-done.10, ...), custom_call_target="tpu_custom_call" | custom-call | tf_op jit(solution)/shard_map/pallas_call | solution.py:630
  38.6 0.6 collective-permute-start.10
  39.2 1.9 %collective-permute-start.11 = (f32[144,128]{1,0:T(8,128)S(1)}, f32[144,128]{1,0:T(8,128)S(1)}, u32[]{:S(2)}, u32[]{:S(2)}) collective-permute-start(f32[144,128]{1,0:T(8,128)S(1)} %get-tuple-element.81), channel_id=1, source_target_pairs={{0,24},{8,16},{16,8},{24,0},{1,25},{9,17},{17,9},{25,1},{2,26},{10... | collective-permute-start | bytes 221192 | tf_op jit(solution)/shard_map/ppermute | solution.py:572
  41.1 1.1 %collective-permute-start.12 = (f32[144,128]{1,0:T(8,128)S(1)}, f32[144,128]{1,0:T(8,128)S(1)}, u32[]{:S(2)}, u32[]{:S(2)}) collective-permute-start(f32[144,128]{1,0:T(8,128)S(1)} %get-tuple-element.82), channel_id=1, source_target_pairs={{0,8},{8,0},{16,24},{24,16},{1,9},{9,1},{17,25},{25,17},{2,10},{10... | collective-permute-start | bytes 221192 | tf_op jit(solution)/shard_map/ppermute | solution.py:572
  42.1 0.5 shard_map.137
  42.6 1.5 %collective-permute-done.10.rest_0_ = f32[144,128]{1,0:T(8,128)S(1)} collective-permute-done((f32[144,128]{1,0:T(8,128)S(1)}, f32[144,128]{1,0:T(8,128)S(1)}, u32[]{:S(2)}, u32[]{:S(2)}) %collective-permute-start.10) | collective-permute-done | bytes 73760 | tf_op jit(solution)/shard_map/ppermute | solution.py:572
  44.2 1.4 %collective-permute-done.11.rest_1_ = f32[144,128]{1,0:T(8,128)S(1)} collective-permute-done((f32[144,128]{1,0:T(8,128)S(1)}, f32[144,128]{1,0:T(8,128)S(1)}, u32[]{:S(2)}, u32[]{:S(2)}) %collective-permute-start.11) | collective-permute-done | bytes 73760 | tf_op jit(solution)/shard_map/ppermute | solution.py:572
  45.6 0.6 collective-permute-done.12.rest_2_
  46.2 1.2 %shard_map.138 = (f32[16,16,256]{2,1,0:T(8,128)S(1)}, f32[16,16,256]{2,1,0:T(8,128)S(1)}, f32[32,16,128]{2,1,0:T(8,128)S(1)}, f32[256,128]{1,0:T(8,128)S(1)}, f3...) custom-call(s32[2,128]{1,0:T(2,128)S(1)} %copy-done.10, ...), custom_call_target="tpu_custom_call" | custom-call | tf_op jit(solution)/shard_map/pallas_call | solution.py:644
  47.4 0.8 %collective-permute-start.13 = (f32[144,128]{1,0:T(8,128)S(1)}, f32[144,128]{1,0:T(8,128)S(1)}, u32[]{:S(2)}, u32[]{:S(2)}) collective-permute-start(f32[144,128]{1,0:T(8,128)S(1)} %get-tuple-element.89), channel_id=1, source_target_pairs={{0,16},{8,24},{16,0},{24,8},{1,17},{9,25},{17,1},{25,9},{2,18},{10... | collective-permute-start | bytes 221192 | tf_op jit(solution)/shard_map/ppermute | solution.py:572
  48.2 2.0 %collective-permute-start.14 = (f32[144,128]{1,0:T(8,128)S(1)}, f32[144,128]{1,0:T(8,128)S(1)}, u32[]{:S(2)}, u32[]{:S(2)}) collective-permute-start(f32[144,128]{1,0:T(8,128)S(1)} %get-tuple-element.90), channel_id=1, source_target_pairs={{0,24},{8,16},{16,8},{24,0},{1,25},{9,17},{17,9},{25,1},{2,26},{10... | collective-permute-start | bytes 221192 | tf_op jit(solution)/shard_map/ppermute | solution.py:572
  50.1 0.8 %collective-permute-start.15 = (f32[144,128]{1,0:T(8,128)S(1)}, f32[144,128]{1,0:T(8,128)S(1)}, u32[]{:S(2)}, u32[]{:S(2)}) collective-permute-start(f32[144,128]{1,0:T(8,128)S(1)} %get-tuple-element.91), channel_id=1, source_target_pairs={{0,8},{8,0},{16,24},{24,16},{1,9},{9,1},{17,25},{25,17},{2,10},{10... | collective-permute-start | bytes 221192 | tf_op jit(solution)/shard_map/ppermute | solution.py:572
  51.0 0.5 shard_map.139
  51.5 1.8 %collective-permute-done.13.rest_0_ = f32[144,128]{1,0:T(8,128)S(1)} collective-permute-done((f32[144,128]{1,0:T(8,128)S(1)}, f32[144,128]{1,0:T(8,128)S(1)}, u32[]{:S(2)}, u32[]{:S(2)}) %collective-permute-start.13) | collective-permute-done | bytes 73760 | tf_op jit(solution)/shard_map/ppermute | solution.py:572
  53.3 1.3 %collective-permute-done.14.rest_1_ = f32[144,128]{1,0:T(8,128)S(1)} collective-permute-done((f32[144,128]{1,0:T(8,128)S(1)}, f32[144,128]{1,0:T(8,128)S(1)}, u32[]{:S(2)}, u32[]{:S(2)}) %collective-permute-start.14) | collective-permute-done | bytes 73760 | tf_op jit(solution)/shard_map/ppermute | solution.py:572
  54.6 0.8 %collective-permute-done.15.rest_2_ = f32[144,128]{1,0:T(8,128)S(1)} collective-permute-done((f32[144,128]{1,0:T(8,128)S(1)}, f32[144,128]{1,0:T(8,128)S(1)}, u32[]{:S(2)}, u32[]{:S(2)}) %collective-permute-start.15) | collective-permute-done | bytes 73760 | tf_op jit(solution)/shard_map/ppermute | solution.py:572
  55.4 1.2 %shard_map.140 = (f32[16,16,256]{2,1,0:T(8,128)S(1)}, f32[16,16,256]{2,1,0:T(8,128)S(1)}, f32[32,16,128]{2,1,0:T(8,128)S(1)}, f32[256,128]{1,0:T(8,128)S(1)}, f3...) custom-call(s32[2,128]{1,0:T(2,128)S(1)} %copy-done.10, ...), custom_call_target="tpu_custom_call" | custom-call | tf_op jit(solution)/shard_map/pallas_call | solution.py:644
  56.6 1.5 %collective-permute-start.16 = (f32[144,128]{1,0:T(8,128)S(1)}, f32[144,128]{1,0:T(8,128)S(1)}, u32[]{:S(2)}, u32[]{:S(2)}) collective-permute-start(f32[144,128]{1,0:T(8,128)S(1)} %get-tuple-element.98), channel_id=1, source_target_pairs={{0,16},{8,24},{16,0},{24,8},{1,17},{9,25},{17,1},{25,9},{2,18},{10... | collective-permute-start | bytes 221192 | tf_op jit(solution)/shard_map/ppermute | solution.py:572
  58.1 2.1 %collective-permute-start.17 = (f32[144,128]{1,0:T(8,128)S(1)}, f32[144,128]{1,0:T(8,128)S(1)}, u32[]{:S(2)}, u32[]{:S(2)}) collective-permute-start(f32[144,128]{1,0:T(8,128)S(1)} %get-tuple-element.99), channel_id=1, source_target_pairs={{0,24},{8,16},{16,8},{24,0},{1,25},{9,17},{17,9},{25,1},{2,26},{10... | collective-permute-start | bytes 221192 | tf_op jit(solution)/shard_map/ppermute | solution.py:572
  60.2 0.0 collective-permute-start.18
  60.2 0.7 shard_map.134
  60.9 0.5 shard_map.141
  61.4 1.3 %collective-permute-done.16.rest_0_ = f32[144,128]{1,0:T(8,128)S(1)} collective-permute-done((f32[144,128]{1,0:T(8,128)S(1)}, f32[144,128]{1,0:T(8,128)S(1)}, u32[]{:S(2)}, u32[]{:S(2)}) %collective-permute-start.16) | collective-permute-done | bytes 73760 | tf_op jit(solution)/shard_map/ppermute | solution.py:572
  62.7 1.6 %collective-permute-done.17.rest_1_ = f32[144,128]{1,0:T(8,128)S(1)} collective-permute-done((f32[144,128]{1,0:T(8,128)S(1)}, f32[144,128]{1,0:T(8,128)S(1)}, u32[]{:S(2)}, u32[]{:S(2)}) %collective-permute-start.17) | collective-permute-done | bytes 73760 | tf_op jit(solution)/shard_map/ppermute | solution.py:572
  64.3 0.7 %collective-permute-done.18.rest_2_ = f32[144,128]{1,0:T(8,128)S(1)} collective-permute-done((f32[144,128]{1,0:T(8,128)S(1)}, f32[144,128]{1,0:T(8,128)S(1)}, u32[]{:S(2)}, u32[]{:S(2)}) %collective-permute-start.18) | collective-permute-done | bytes 73760 | tf_op jit(solution)/shard_map/ppermute | solution.py:572
  65.1 1.6 %shard_map.142 = (f32[16,16,256]{2,1,0:T(8,128)}, f32[16,16,256]{2,1,0:T(8,128)}) custom-call(s32[2,128]{1,0:T(2,128)S(1)} %copy-done.10, f32[16,16,256]{2,1,0:T(8,128)S(1)} %get-tuple-element.94.phase, f32[16,16,256]{2,1,0:T(8,128)S(1)} %get-tuple-element.95.solute, f32[32,16,128]{2,1,0:T(8,128)S(1)} %get-tuple-element.96.own, ...), custom_call_target="tpu_custom_call" | custom-call | tf_op jit(solution)/shard_map/pallas_call | solution.py:653
  (22 shorter events, 0.1 us)
Async XLA Ops:
  0.6 11.5 %copy-start.1 = (bf16[512,256]{1,0:T(8,128)(2,1)S(1)}, bf16[512,256]{1,0:T(8,128)(2,1)}, u32[]{:S(2)}) copy-start(bf16[512,256]{1,0:T(8,128)(2,1)} %constant.8.clone.picks) | copy-start | bytes 786436
  2.9 5.2 %copy-start.13 = (f32[8,128]{1,0:T(8,128)S(1)}, f32[8,128]{1,0:T(8,128)}, u32[]{:S(2)}) copy-start(f32[8,128]{1,0:T(8,128)} %get-tuple-element.57) | copy-start | bytes 12292
  2.9 7.9 %copy-start.12 = (f32[8,128]{1,0:T(8,128)S(1)}, f32[8,128]{1,0:T(8,128)}, u32[]{:S(2)}) copy-start(f32[8,128]{1,0:T(8,128)} %get-tuple-element.58) | copy-start | bytes 12292
  2.9 13.3 %all-to-all-start = ((f32[8,24,128]{2,1,0:T(8,128)}), f32[8,24,128]{2,1,0:T(8,128)S(1)}, u32[]{:S(2)}, u32[]{:S(2)}) async-start(f32[8,24,128]{2,1,0:T(8,128)} %get-tuple-element.56), calls=%async_computation | async-start | bytes 196608 | tf_op jit(solution)/shard_map/all_to_all | solution.py:569
  8.1 7.5 %collective-permute-start = (f32[8,128]{1,0:T(8,128)S(1)}, f32[8,128]{1,0:T(8,128)S(1)}, u32[]{:S(2)}, u32[]{:S(2)}) collective-permute-start(f32[8,128]{1,0:T(8,128)S(1)} %copy-done.13), channel_id=1, source_target_pairs={{0,16},{8,24},{16,0},{24,8},{1,17},{9,25},{17,1},{25,9},{2,18},{10... | collective-permute-start | bytes 12296 | tf_op jit(solution)/shard_map/ppermute | solution.py:572
  10.7 5.4 %collective-permute-start.1 = (f32[8,128]{1,0:T(8,128)S(1)}, f32[8,128]{1,0:T(8,128)S(1)}, u32[]{:S(2)}, u32[]{:S(2)}) collective-permute-start(f32[8,128]{1,0:T(8,128)S(1)} %copy-done.12), channel_id=1, source_target_pairs={{0,24},{8,16},{16,8},{24,0},{1,25},{9,17},{17,9},{25,1},{2,26},{10... | collective-permute-start | bytes 12296 | tf_op jit(solution)/shard_map/ppermute | solution.py:572
  12.1 0.7 %copy-start.11 = (f32[4,128]{1,0:T(4,128)S(1)}, f32[4,128]{1,0:T(4,128)}, u32[]{:S(2)}) copy-start(f32[4,128]{1,0:T(4,128)} %get-tuple-element.54.asked) | copy-start | bytes 6148
  12.1 0.7 %copy-start.10 = (s32[2,128]{1,0:T(2,128)S(1)}, s32[2,128]{1,0:T(2,128)}, u32[]{:S(2)}) copy-start(s32[2,128]{1,0:T(2,128)} %get-tuple-element.53.table) | copy-start | bytes 3076
  12.8 1.0 %copy-start.2 = (f32[1,1,1,16,16,256]{5,4,3,2,1,0:T(8,128)S(1)}, f32[1,1,1,16,16,256]{5,4,3,2,1,0:T(8,128)}, u32[]{:S(2)}) copy-start(f32[1,1,1,16,16,256]{5,4,3,2,1,0:T(8,128)} %param.13) | copy-start | bytes 786436
  13.7 0.9 %copy-start.7 = (f32[1,1,1,16,16,256]{5,4,3,2,1,0:T(8,128)S(1)}, f32[1,1,1,16,16,256]{5,4,3,2,1,0:T(8,128)}, u32[]{:S(2)}) copy-start(f32[1,1,1,16,16,256]{5,4,3,2,1,0:T(8,128)} %param.14) | copy-start | bytes 786436
  14.7 1.5 %copy-start.5 = (f32[8,32,128]{2,1,0:T(8,128)S(1)}, f32[8,32,128]{2,1,0:T(8,128)}, u32[]{:S(2)}) copy-start(f32[8,32,128]{2,1,0:T(8,128)} %h.3) | copy-start | bytes 393220
  14.7 1.5 %copy-start.6 = (f32[8,32,128]{2,1,0:T(8,128)S(1)}, f32[8,32,128]{2,1,0:T(8,128)}, u32[]{:S(2)}) copy-start(f32[8,32,128]{2,1,0:T(8,128)} %k.3) | copy-start | bytes 393220
  16.2 16.9 %copy-start.8 = (f32[1,1,1,16,16,256]{5,4,3,2,1,0:T(8,128)S(1)}, f32[1,1,1,16,16,256]{5,4,3,2,1,0:T(8,128)}, u32[]{:S(2)}) copy-start(f32[1,1,1,16,16,256]{5,4,3,2,1,0:T(8,128)} %param.14) | copy-start | bytes 786436
  16.2 16.9 %copy-start.3 = (f32[1,1,1,16,16,256]{5,4,3,2,1,0:T(8,128)S(1)}, f32[1,1,1,16,16,256]{5,4,3,2,1,0:T(8,128)}, u32[]{:S(2)}) copy-start(f32[1,1,1,16,16,256]{5,4,3,2,1,0:T(8,128)} %param.13) | copy-start | bytes 786436
  16.2 5.1 %collective-permute-start.2 = (f32[104,128]{1,0:T(8,128)S(1)}, f32[104,128]{1,0:T(8,128)S(1)}, u32[]{:S(2)}, u32[]{:S(2)}) collective-permute-start(f32[104,128]{1,0:T(8,128)S(1)} %get-tuple-element.59), channel_id=1, source_target_pairs={{0,8},{8,0},{16,24},{24,16},{1,9},{9,1},{17,25},{25,17},{2,10},{10... | collective-permute-start | bytes 159752 | tf_op jit(solution)/shard_map/ppermute | solution.py:572
  16.3 16.8 %collective-permute-start.7 = (f32[144,128]{1,0:T(8,128)S(1)}, f32[144,128]{1,0:T(8,128)S(1)}, u32[]{:S(2)}, u32[]{:S(2)}) collective-permute-start(f32[144,128]{1,0:T(8,128)S(1)} %get-tuple-element.70), channel_id=1, source_target_pairs={{0,16},{8,24},{16,0},{24,8},{1,17},{9,25},{17,1},{25,9},{2,18},{10... | collective-permute-start | bytes 221192 | tf_op jit(solution)/shard_map/ppermute | solution.py:572
  18.8 14.8 %collective-permute-start.8 = (f32[144,128]{1,0:T(8,128)S(1)}, f32[144,128]{1,0:T(8,128)S(1)}, u32[]{:S(2)}, u32[]{:S(2)}) collective-permute-start(f32[144,128]{1,0:T(8,128)S(1)} %get-tuple-element.71), channel_id=1, source_target_pairs={{0,24},{8,16},{16,8},{24,0},{1,25},{9,17},{17,9},{25,1},{2,26},{10... | collective-permute-start | bytes 221192 | tf_op jit(solution)/shard_map/ppermute | solution.py:572
  20.7 12.9 %collective-permute-start.9 = (f32[144,128]{1,0:T(8,128)S(1)}, f32[144,128]{1,0:T(8,128)S(1)}, u32[]{:S(2)}, u32[]{:S(2)}) collective-permute-start(f32[144,128]{1,0:T(8,128)S(1)} %get-tuple-element.72), channel_id=1, source_target_pairs={{0,8},{8,0},{16,24},{24,16},{1,9},{9,1},{17,25},{25,17},{2,10},{10... | collective-permute-start | bytes 221192 | tf_op jit(solution)/shard_map/ppermute | solution.py:572
  20.7 0.7 %collective-permute-start.3 = (f32[104,128]{1,0:T(8,128)S(1)}, f32[104,128]{1,0:T(8,128)S(1)}, u32[]{:S(2)}, u32[]{:S(2)}) collective-permute-start(f32[104,128]{1,0:T(8,128)S(1)} %get-tuple-element.60), channel_id=1, source_target_pairs={{0,0},{8,16},{16,8},{24,24},{1,1},{9,17},{17,9},{25,25},{2,2},{10,... | collective-permute-start | bytes 159752 | tf_op jit(solution)/shard_map/ppermute | solution.py:572
  21.4 11.7 %copy-start.4 = (bf16[256,256]{1,0:T(8,128)(2,1)S(1)}, bf16[256,256]{1,0:T(8,128)(2,1)}, u32[]{:S(2)}) copy-start(bf16[256,256]{1,0:T(8,128)(2,1)} %constant.9.clone.stencil) | copy-start | bytes 393220
  23.3 10.3 %collective-permute-start.4 = (f32[32,128]{1,0:T(8,128)S(1)}, f32[32,128]{1,0:T(8,128)S(1)}, u32[]{:S(2)}, u32[]{:S(2)}) collective-permute-start(f32[32,128]{1,0:T(8,128)S(1)} %get-tuple-element.67), channel_id=1, source_target_pairs={{0,16},{8,24},{16,0},{24,8},{1,17},{9,25},{17,1},{25,9},{2,18},{10... | collective-permute-start | bytes 49160 | tf_op jit(solution)/shard_map/ppermute | solution.py:572
  31.2 5.5 %collective-permute-start.5 = (f32[32,128]{1,0:T(8,128)S(1)}, f32[32,128]{1,0:T(8,128)S(1)}, u32[]{:S(2)}, u32[]{:S(2)}) collective-permute-start(f32[32,128]{1,0:T(8,128)S(1)} %get-tuple-element.68), channel_id=1, source_target_pairs={{0,24},{8,16},{16,8},{24,0},{1,25},{9,17},{17,9},{25,1},{2,26},{10... | collective-permute-start | bytes 49160 | tf_op jit(solution)/shard_map/ppermute | solution.py:572
  33.1 3.9 %copy-start = (bf16[256,512]{1,0:T(8,128)(2,1)S(1)}, bf16[256,512]{1,0:T(8,128)(2,1)}, u32[]{:S(2)}) copy-start(bf16[256,512]{1,0:T(8,128)(2,1)} %constant.10.clone.places) | copy-start | bytes 786436
  33.1 3.9 %copy-start.9 = (bf16[256,256]{1,0:T(8,128)(2,1)S(1)}, bf16[256,256]{1,0:T(8,128)(2,1)}, u32[]{:S(2)}) copy-start(bf16[256,256]{1,0:T(8,128)(2,1)} %constant.11.clone.spreads) | copy-start | bytes 393220
  33.1 3.8 %collective-permute-start.6 = (f32[32,128]{1,0:T(8,128)S(1)}, f32[32,128]{1,0:T(8,128)S(1)}, u32[]{:S(2)}, u32[]{:S(2)}) collective-permute-start(f32[32,128]{1,0:T(8,128)S(1)} %get-tuple-element.69), channel_id=1, source_target_pairs={{0,8},{8,0},{16,24},{24,16},{1,9},{9,1},{17,25},{25,17},{2,10},{10... | collective-permute-start | bytes 49160 | tf_op jit(solution)/shard_map/ppermute | solution.py:572
  38.6 5.6 %collective-permute-start.10 = (f32[144,128]{1,0:T(8,128)S(1)}, f32[144,128]{1,0:T(8,128)S(1)}, u32[]{:S(2)}, u32[]{:S(2)}) collective-permute-start(f32[144,128]{1,0:T(8,128)S(1)} %get-tuple-element.80), channel_id=1, source_target_pairs={{0,16},{8,24},{16,0},{24,8},{1,17},{9,25},{17,1},{25,9},{2,18},{10... | collective-permute-start | bytes 221192 | tf_op jit(solution)/shard_map/ppermute | solution.py:572
  39.2 6.4 %collective-permute-start.11 = (f32[144,128]{1,0:T(8,128)S(1)}, f32[144,128]{1,0:T(8,128)S(1)}, u32[]{:S(2)}, u32[]{:S(2)}) collective-permute-start(f32[144,128]{1,0:T(8,128)S(1)} %get-tuple-element.81), channel_id=1, source_target_pairs={{0,24},{8,16},{16,8},{24,0},{1,25},{9,17},{17,9},{25,1},{2,26},{10... | collective-permute-start | bytes 221192 | tf_op jit(solution)/shard_map/ppermute | solution.py:572
  41.1 5.1 %collective-permute-start.12 = (f32[144,128]{1,0:T(8,128)S(1)}, f32[144,128]{1,0:T(8,128)S(1)}, u32[]{:S(2)}, u32[]{:S(2)}) collective-permute-start(f32[144,128]{1,0:T(8,128)S(1)} %get-tuple-element.82), channel_id=1, source_target_pairs={{0,8},{8,0},{16,24},{24,16},{1,9},{9,1},{17,25},{25,17},{2,10},{10... | collective-permute-start | bytes 221192 | tf_op jit(solution)/shard_map/ppermute | solution.py:572
  47.4 5.8 %collective-permute-start.13 = (f32[144,128]{1,0:T(8,128)S(1)}, f32[144,128]{1,0:T(8,128)S(1)}, u32[]{:S(2)}, u32[]{:S(2)}) collective-permute-start(f32[144,128]{1,0:T(8,128)S(1)} %get-tuple-element.89), channel_id=1, source_target_pairs={{0,16},{8,24},{16,0},{24,8},{1,17},{9,25},{17,1},{25,9},{2,18},{10... | collective-permute-start | bytes 221192 | tf_op jit(solution)/shard_map/ppermute | solution.py:572
  48.2 6.4 %collective-permute-start.14 = (f32[144,128]{1,0:T(8,128)S(1)}, f32[144,128]{1,0:T(8,128)S(1)}, u32[]{:S(2)}, u32[]{:S(2)}) collective-permute-start(f32[144,128]{1,0:T(8,128)S(1)} %get-tuple-element.90), channel_id=1, source_target_pairs={{0,24},{8,16},{16,8},{24,0},{1,25},{9,17},{17,9},{25,1},{2,26},{10... | collective-permute-start | bytes 221192 | tf_op jit(solution)/shard_map/ppermute | solution.py:572
  50.1 5.2 %collective-permute-start.15 = (f32[144,128]{1,0:T(8,128)S(1)}, f32[144,128]{1,0:T(8,128)S(1)}, u32[]{:S(2)}, u32[]{:S(2)}) collective-permute-start(f32[144,128]{1,0:T(8,128)S(1)} %get-tuple-element.91), channel_id=1, source_target_pairs={{0,8},{8,0},{16,24},{24,16},{1,9},{9,1},{17,25},{25,17},{2,10},{10... | collective-permute-start | bytes 221192 | tf_op jit(solution)/shard_map/ppermute | solution.py:572
  56.6 6.1 %collective-permute-start.16 = (f32[144,128]{1,0:T(8,128)S(1)}, f32[144,128]{1,0:T(8,128)S(1)}, u32[]{:S(2)}, u32[]{:S(2)}) collective-permute-start(f32[144,128]{1,0:T(8,128)S(1)} %get-tuple-element.98), channel_id=1, source_target_pairs={{0,16},{8,24},{16,0},{24,8},{1,17},{9,25},{17,1},{25,9},{2,18},{10... | collective-permute-start | bytes 221192 | tf_op jit(solution)/shard_map/ppermute | solution.py:572
  58.1 6.2 %collective-permute-start.17 = (f32[144,128]{1,0:T(8,128)S(1)}, f32[144,128]{1,0:T(8,128)S(1)}, u32[]{:S(2)}, u32[]{:S(2)}) collective-permute-start(f32[144,128]{1,0:T(8,128)S(1)} %get-tuple-element.99), channel_id=1, source_target_pairs={{0,24},{8,16},{16,8},{24,0},{1,25},{9,17},{17,9},{25,1},{2,26},{10... | collective-permute-start | bytes 221192 | tf_op jit(solution)/shard_map/ppermute | solution.py:572
  60.2 4.9 %collective-permute-start.18 = (f32[144,128]{1,0:T(8,128)S(1)}, f32[144,128]{1,0:T(8,128)S(1)}, u32[]{:S(2)}, u32[]{:S(2)}) collective-permute-start(f32[144,128]{1,0:T(8,128)S(1)} %get-tuple-element.100), channel_id=1, source_target_pairs={{0,8},{8,0},{16,24},{24,16},{1,9},{9,1},{17,25},{25,17},{2,10},{10... | collective-permute-start | bytes 221192 | tf_op jit(solution)/shard_map/ppermute | solution.py:572

commit v17 on v14

--- a/solution.py
+++ b/solution.py
@@ -437,16 +437,18 @@
 def ghost_shares(ghosts, ghost_edges, places):
     beside = jnp.concatenate(halves(ghosts[...].reshape(SLOTS * TE, 128)), axis=1)
     beside = dot(beside, places)
-    rows = iota((SLOTS, TE, PLANE), 1)
+    half = TE // 2
+    rows = iota((SLOTS, half, PLANE), 1)
     shares = []
     for number in range(2):
         share = beside[:, number * PLANE : number * PLANE + PLANE].reshape(SLOTS, TE, PLANE)
-        for face, at_row in ((0, 0), (1, TE - 1)):
+        parts = []
+        for face, at_row in ((0, 0), (1, half - 1)):
             at = face * 4 + number * 2
             side = [ghost_edges[:, row : row + 1, :] for row in (at, at + 1)]
-            side = jnp.concatenate(side, axis=2)
-            share += jnp.where(rows == at_row, side, 0.0)
-        shares.append(share)
+            side = jnp.where(rows == at_row, jnp.concatenate(side, axis=2), 0.0)
+            parts.append(share[:, face * half : face * half + half] + side)
+        shares.append(jnp.concatenate(parts, axis=1))
     return shares
 
 

time: 62.3 us -> 62.3 us (level)
  no operation moved by 1% of the time
where the time goes in v17:
time: 62.3 us; the launch traced here: 62 us
  starting transfers between devices  30.7 us (49%)
  waiting for transfers between devices  14.3 us (23%)
  Pallas kernels  13.4 us (22%)
  local copies, waits for them, and re-layouts  2.65 us (4%)
  between operations  0.85 us (1%)
    ppermute x12, starting transfers between devices, swap_all(): lax.ppermute(value, 'gx', [(i, i ^ swap) for i in range(count)])  14.4 us
    ppermute x12, waiting for transfers between devices, swap_all(): lax.ppermute(value, 'gx', [(i, i ^ swap) for i in range(count)])  12 us
    ppermute x6, starting transfers between devices, pass_on(): lax.ppermute(value, 'gx', [(i, (i + shift) % count) for i in range(count)])  11.2 us
    all_to_all x1, starting transfers between devices, local(): lax.all_to_all(sides, ('gy', 'gz'), split_axis=0, concat_axis=0, tiled=True)  5.18 us
    unnamed x26, local copies, waits for them, and re-layouts  2.64 us
    pallas_call x2, Pallas kernels, local(): call(middle_step_kernel, [SMEM] + [VMEM] * (6 + others), [field, field, *...  2.44 us
    ppermute x6, waiting for transfers between devices, pass_on(): lax.ppermute(value, 'gx', [(i, (i + shift) % count) for i in range(count)])  2.33 us
    pallas_call x1, Pallas kernels, local(): call(functools.partial(sides_kernel, sizes, plane_cap), [ANY] * 5, [shape...  2.21 us
  transfers between devices with their start and end apart: 19, of which 9 were waited for; matrix products, arithmetic and copies ran while one was open for 0% of the time, Pallas kernels for 9%

profile of v17, /device:TPU:0, one launch (start us, length us, event | category | flops | bytes accessed | tf_op | source)
XLA Modules:
  0.0 62.0 jit_solution(145796831555363454)
XLA Ops:
  0.6 0.0 copy-start.1
  0.6 2.2 %shard_map.130 = (f32[8,24,128]{2,1,0:T(8,128)}, s32[2,128]{1,0:T(2,128)}, f32[4,128]{1,0:T(4,128)}, f32[8,128]{1,0:T(8,128)}) custom-call(s32[1,16]{1,0:T(1,128)} %bitcast.15, s32[1,16]{1,0:T(1,128)} %bitcast.16, s32[6,1,16]{2,1,0:T(1,128)} %bitcast.14, f32[8,32,128]{2,1,0:T(8,128)} %h.3, f32[8,32,128]{2,1,0:T(8,128)} %k.3), custom_call_target="tpu_custom_call" | custom-call | tf_op jit(solution)/shard_map/pallas_call | solution.py:539
  2.9 0.0 copy-start.12
  2.9 5.2 %all-to-all-start = ((f32[8,24,128]{2,1,0:T(8,128)}), f32[8,24,128]{2,1,0:T(8,128)S(1)}, u32[]{:S(2)}, u32[]{:S(2)}) async-start(f32[8,24,128]{2,1,0:T(8,128)} %get-tuple-element.55), calls=%async_computation | async-start | bytes 196608 | tf_op jit(solution)/shard_map/all_to_all | solution.py:564
  8.1 0.0 copy-done.12
  8.1 2.7 %collective-permute-start = (f32[8,128]{1,0:T(8,128)S(1)}, f32[8,128]{1,0:T(8,128)S(1)}, u32[]{:S(2)}, u32[]{:S(2)}) collective-permute-start(f32[8,128]{1,0:T(8,128)S(1)} %copy-done.12), channel_id=1, source_target_pairs={{0,16},{8,24},{16,0},{24,8},{1,17},{9,25},{17,1},{25,9},{2,18},{10... | collective-permute-start | bytes 12296 | tf_op jit(solution)/shard_map/ppermute | solution.py:567
  10.7 0.0 copy-done.1
  10.7 0.7 %copy-done.11 = f32[4,128]{1,0:T(4,128)S(1)} copy-done((f32[4,128]{1,0:T(4,128)S(1)}, f32[4,128]{1,0:T(4,128)}, u32[]{:S(2)}) %copy-start.11) | copy-done | bytes 2072
  11.4 0.0 copy-done.10
  11.4 0.9 %copy-done.2 = f32[1,1,1,16,16,256]{5,4,3,2,1,0:T(8,128)S(1)} copy-done((f32[1,1,1,16,16,256]{5,4,3,2,1,0:T(8,128)S(1)}, f32[1,1,1,16,16,256]{5,4,3,2,1,0:T(8,128)}, u32[]{:S(2)}) %copy-start.2) | copy-done | bytes 262168
  12.4 0.9 %copy-done.7 = f32[1,1,1,16,16,256]{5,4,3,2,1,0:T(8,128)S(1)} copy-done((f32[1,1,1,16,16,256]{5,4,3,2,1,0:T(8,128)S(1)}, f32[1,1,1,16,16,256]{5,4,3,2,1,0:T(8,128)}, u32[]{:S(2)}) %copy-start.7) | copy-done | bytes 262168
  13.3 0.9 %shard_map.131 = (f32[32,16,128]{2,1,0:T(8,128)S(1)}, f32[256,128]{1,0:T(8,128)S(1)}, f32[4,128]{1,0:T(4,128)S(1)}, f32[144,128]{1,0:T(8,128)S(1)}, f32[144,128]{1,0:T(8,128)S(1)}, /*index=5*/f32[144,128]{1,0:T(8,128)S(1)}) custom-call(s32[2,128]{1,0:T(2,128)S(1)} %copy-done.10, f32[4,128]{1,0:T(4,128)S(1)} %copy-done.11, f32[16,16,256]{2,1,0:T(8,128)S(1)} %bitcast.9, ...), custom_call_target="tpu_custom_call" | custom-call | tf_op jit(solution)/shard_map/pallas_call | solution.py:585
  14.2 0.0 collective-permute-done.rest_0_
  14.2 0.0 all-to-all-done.got
  14.3 0.0 copy-done.5
  14.3 0.0 copy-done.6
  14.3 0.0 copy-start.8
  14.3 0.0 copy-start.3
  14.3 1.6 %collective-permute-start.1 = (f32[104,128]{1,0:T(8,128)S(1)}, f32[104,128]{1,0:T(8,128)S(1)}, u32[]{:S(2)}, u32[]{:S(2)}) collective-permute-start(f32[104,128]{1,0:T(8,128)S(1)} %get-tuple-element.57), channel_id=1, source_target_pairs={{0,8},{8,16},{16,24},{24,0},{1,9},{9,17},{17,25},{25,1},{2,10},{10... | collective-permute-start | bytes 159752 | tf_op jit(solution)/shard_map/ppermute | solution.py:567
  16.0 2.2 %collective-permute-start.2 = (f32[104,128]{1,0:T(8,128)S(1)}, f32[104,128]{1,0:T(8,128)S(1)}, u32[]{:S(2)}, u32[]{:S(2)}) collective-permute-start(f32[104,128]{1,0:T(8,128)S(1)} %get-tuple-element.58), channel_id=1, source_target_pairs={{0,24},{8,0},{16,8},{24,16},{1,25},{9,1},{17,9},{25,17},{2,26},{10... | collective-permute-start | bytes 159752 | tf_op jit(solution)/shard_map/ppermute | solution.py:567
  18.2 0.0 collective-permute-start.6
  18.2 2.1 %collective-permute-start.7 = (f32[144,128]{1,0:T(8,128)S(1)}, f32[144,128]{1,0:T(8,128)S(1)}, u32[]{:S(2)}, u32[]{:S(2)}) collective-permute-start(f32[144,128]{1,0:T(8,128)S(1)} %get-tuple-element.69), channel_id=1, source_target_pairs={{0,24},{8,16},{16,8},{24,0},{1,25},{9,17},{17,9},{25,1},{2,26},{10... | collective-permute-start | bytes 221192 | tf_op jit(solution)/shard_map/ppermute | solution.py:574
  20.3 1.3 %collective-permute-start.8 = (f32[144,128]{1,0:T(8,128)S(1)}, f32[144,128]{1,0:T(8,128)S(1)}, u32[]{:S(2)}, u32[]{:S(2)}) collective-permute-start(f32[144,128]{1,0:T(8,128)S(1)} %get-tuple-element.70), channel_id=1, source_target_pairs={{0,8},{8,0},{16,24},{24,16},{1,9},{9,1},{17,25},{25,17},{2,10},{10... | collective-permute-start | bytes 221192 | tf_op jit(solution)/shard_map/ppermute | solution.py:574
  21.7 0.0 collective-permute-done.1.low
  21.7 0.0 collective-permute-done.2.high
  21.8 0.0 copy-start.4
  21.8 1.9 %shard_map.133 = (f32[8,32,128]{2,1,0:T(8,128)S(1)}, f32[32,128]{1,0:T(8,128)S(1)}, f32[32,128]{1,0:T(8,128)S(1)}, f32[32,128]{1,0:T(8,128)S(1)}, f32[32,128]{1,0:T(8,128)S(1)}) custom-call(s32[4,8]{1,0:T(4,128)S(1)} %maximum_convert_fusion.request, f32[8,32,128]{2,1,0:T(8,128)S(1)} %copy-done.5, f32[8,32,128]{2,1,0:T(8,128)S(1)} %copy-done.6, ...), custom_call_target="tpu_custom_call" | custom-call | tf_op jit(solution)/shard_map/pallas_call | solution.py:604
  23.7 0.7 %collective-permute-start.3 = (f32[32,128]{1,0:T(8,128)S(1)}, f32[32,128]{1,0:T(8,128)S(1)}, u32[]{:S(2)}, u32[]{:S(2)}) collective-permute-start(f32[32,128]{1,0:T(8,128)S(1)} %get-tuple-element.65), channel_id=1, source_target_pairs={{0,8},{8,16},{16,24},{24,0},{1,9},{9,17},{17,25},{25,1},{2,10},{10... | collective-permute-start | bytes 49160 | tf_op jit(solution)/shard_map/ppermute | solution.py:567
  24.4 3.0 %collective-permute-start.4 = (f32[32,128]{1,0:T(8,128)S(1)}, f32[32,128]{1,0:T(8,128)S(1)}, u32[]{:S(2)}, u32[]{:S(2)}) collective-permute-start(f32[32,128]{1,0:T(8,128)S(1)} %get-tuple-element.66), channel_id=1, source_target_pairs={{0,16},{8,24},{16,0},{24,8},{1,17},{9,25},{17,1},{25,9},{2,18},{10... | collective-permute-start | bytes 49160 | tf_op jit(solution)/shard_map/ppermute | solution.py:567
  27.4 0.0 collective-permute-done.6.rest_4_
  27.4 0.9 %collective-permute-start.5 = (f32[32,128]{1,0:T(8,128)S(1)}, f32[32,128]{1,0:T(8,128)S(1)}, u32[]{:S(2)}, u32[]{:S(2)}) collective-permute-start(f32[32,128]{1,0:T(8,128)S(1)} %get-tuple-element.67), channel_id=1, source_target_pairs={{0,24},{8,0},{16,8},{24,16},{1,25},{9,1},{17,9},{25,17},{2,26},{10... | collective-permute-start | bytes 49160 | tf_op jit(solution)/shard_map/ppermute | solution.py:567
  28.3 0.0 copy-done.4
  28.3 0.5 shard_map.135
  28.8 0.0 collective-permute-done.7.rest_5_
  28.8 0.0 collective-permute-done.8.rest_6_
  28.8 0.5 collective-permute-done.3.rest_1_
  29.3 0.0 collective-permute-done.4.rest_2_
  29.3 1.9 %collective-permute-done.5.rest_3_ = f32[32,128]{1,0:T(8,128)S(1)} collective-permute-done((f32[32,128]{1,0:T(8,128)S(1)}, f32[32,128]{1,0:T(8,128)S(1)}, u32[]{:S(2)}, u32[]{:S(2)}) %collective-permute-start.5) | collective-permute-done | bytes 16416 | tf_op jit(solution)/shard_map/ppermute | solution.py:567
  31.2 1.7 %shard_map.136 = (f32[16,16,256]{2,1,0:T(8,128)S(1)}, f32[16,16,256]{2,1,0:T(8,128)S(1)}, f32[2,256,128]{2,1,0:T(8,128)S(1)}, f32[32,16,128]{2,1,0:T(8,128)S(1)}...) custom-call(s32[2,128]{1,0:T(2,128)S(1)} %copy-done.10, ...), custom_call_target="tpu_custom_call" | custom-call | tf_op jit(solution)/shard_map/pallas_call | solution.py:627
  32.8 1.0 %collective-permute-start.9 = (f32[144,128]{1,0:T(8,128)S(1)}, f32[144,128]{1,0:T(8,128)S(1)}, u32[]{:S(2)}, u32[]{:S(2)}) collective-permute-start(f32[144,128]{1,0:T(8,128)S(1)} %get-tuple-element.78), channel_id=1, source_target_pairs={{0,16},{8,24},{16,0},{24,8},{1,17},{9,25},{17,1},{25,9},{2,18},{10... | collective-permute-start | bytes 221192 | tf_op jit(solution)/shard_map/ppermute | solution.py:574
  33.8 2.1 %collective-permute-start.10 = (f32[144,128]{1,0:T(8,128)S(1)}, f32[144,128]{1,0:T(8,128)S(1)}, u32[]{:S(2)}, u32[]{:S(2)}) collective-permute-start(f32[144,128]{1,0:T(8,128)S(1)} %get-tuple-element.79), channel_id=1, source_target_pairs={{0,24},{8,16},{16,8},{24,0},{1,25},{9,17},{17,9},{25,1},{2,26},{10... | collective-permute-start | bytes 221192 | tf_op jit(solution)/shard_map/ppermute | solution.py:574
  36.0 0.4 collective-permute-start.11
  36.4 0.5 shard_map.137
  36.9 2.1 %collective-permute-done.9.rest_0_ = f32[144,128]{1,0:T(8,128)S(1)} collective-permute-done((f32[144,128]{1,0:T(8,128)S(1)}, f32[144,128]{1,0:T(8,128)S(1)}, u32[]{:S(2)}, u32[]{:S(2)}) %collective-permute-start.9) | collective-permute-done | bytes 73760 | tf_op jit(solution)/shard_map/ppermute | solution.py:574
  39.0 1.2 %collective-permute-done.10.rest_1_ = f32[144,128]{1,0:T(8,128)S(1)} collective-permute-done((f32[144,128]{1,0:T(8,128)S(1)}, f32[144,128]{1,0:T(8,128)S(1)}, u32[]{:S(2)}, u32[]{:S(2)}) %collective-permute-start.10) | collective-permute-done | bytes 73760 | tf_op jit(solution)/shard_map/ppermute | solution.py:574
  40.1 0.7 %collective-permute-done.11.rest_2_ = f32[144,128]{1,0:T(8,128)S(1)} collective-permute-done((f32[144,128]{1,0:T(8,128)S(1)}, f32[144,128]{1,0:T(8,128)S(1)}, u32[]{:S(2)}, u32[]{:S(2)}) %collective-permute-start.11) | collective-permute-done | bytes 73760 | tf_op jit(solution)/shard_map/ppermute | solution.py:574
  40.9 1.2 %shard_map.138 = (f32[16,16,256]{2,1,0:T(8,128)S(1)}, f32[16,16,256]{2,1,0:T(8,128)S(1)}, f32[32,16,128]{2,1,0:T(8,128)S(1)}, f32[256,128]{1,0:T(8,128)S(1)}, f3...) custom-call(s32[2,128]{1,0:T(2,128)S(1)} %copy-done.10, ...), custom_call_target="tpu_custom_call" | custom-call | tf_op jit(solution)/shard_map/pallas_call | solution.py:641
  42.1 1.7 %collective-permute-start.12 = (f32[144,128]{1,0:T(8,128)S(1)}, f32[144,128]{1,0:T(8,128)S(1)}, u32[]{:S(2)}, u32[]{:S(2)}) collective-permute-start(f32[144,128]{1,0:T(8,128)S(1)} %get-tuple-element.87), channel_id=1, source_target_pairs={{0,16},{8,24},{16,0},{24,8},{1,17},{9,25},{17,1},{25,9},{2,18},{10... | collective-permute-start | bytes 221192 | tf_op jit(solution)/shard_map/ppermute | solution.py:574
  43.8 1.2 %collective-permute-start.13 = (f32[144,128]{1,0:T(8,128)S(1)}, f32[144,128]{1,0:T(8,128)S(1)}, u32[]{:S(2)}, u32[]{:S(2)}) collective-permute-start(f32[144,128]{1,0:T(8,128)S(1)} %get-tuple-element.88), channel_id=1, source_target_pairs={{0,24},{8,16},{16,8},{24,0},{1,25},{9,17},{17,9},{25,1},{2,26},{10... | collective-permute-start | bytes 221192 | tf_op jit(solution)/shard_map/ppermute | solution.py:574
  45.0 0.7 %collective-permute-start.14 = (f32[144,128]{1,0:T(8,128)S(1)}, f32[144,128]{1,0:T(8,128)S(1)}, u32[]{:S(2)}, u32[]{:S(2)}) collective-permute-start(f32[144,128]{1,0:T(8,128)S(1)} %get-tuple-element.89), channel_id=1, source_target_pairs={{0,8},{8,0},{16,24},{24,16},{1,9},{9,1},{17,25},{25,17},{2,10},{10... | collective-permute-start | bytes 221192 | tf_op jit(solution)/shard_map/ppermute | solution.py:574
  45.6 0.5 shard_map.139
  46.1 1.9 %collective-permute-done.12.rest_0_ = f32[144,128]{1,0:T(8,128)S(1)} collective-permute-done((f32[144,128]{1,0:T(8,128)S(1)}, f32[144,128]{1,0:T(8,128)S(1)}, u32[]{:S(2)}, u32[]{:S(2)}) %collective-permute-start.12) | collective-permute-done | bytes 73760 | tf_op jit(solution)/shard_map/ppermute | solution.py:574
  48.1 2.5 %collective-permute-done.13.rest_1_ = f32[144,128]{1,0:T(8,128)S(1)} collective-permute-done((f32[144,128]{1,0:T(8,128)S(1)}, f32[144,128]{1,0:T(8,128)S(1)}, u32[]{:S(2)}, u32[]{:S(2)}) %collective-permute-start.13) | collective-permute-done | bytes 73760 | tf_op jit(solution)/shard_map/ppermute | solution.py:574
  50.6 0.0 collective-permute-done.14.rest_2_
  50.6 1.2 %shard_map.140 = (f32[16,16,256]{2,1,0:T(8,128)S(1)}, f32[16,16,256]{2,1,0:T(8,128)S(1)}, f32[32,16,128]{2,1,0:T(8,128)S(1)}, f32[256,128]{1,0:T(8,128)S(1)}, f3...) custom-call(s32[2,128]{1,0:T(2,128)S(1)} %copy-done.10, ...), custom_call_target="tpu_custom_call" | custom-call | tf_op jit(solution)/shard_map/pallas_call | solution.py:641
  51.8 2.4 %collective-permute-start.15 = (f32[144,128]{1,0:T(8,128)S(1)}, f32[144,128]{1,0:T(8,128)S(1)}, u32[]{:S(2)}, u32[]{:S(2)}) collective-permute-start(f32[144,128]{1,0:T(8,128)S(1)} %get-tuple-element.96), channel_id=1, source_target_pairs={{0,16},{8,24},{16,0},{24,8},{1,17},{9,25},{17,1},{25,9},{2,18},{10... | collective-permute-start | bytes 221192 | tf_op jit(solution)/shard_map/ppermute | solution.py:574
  54.2 0.9 %collective-permute-start.16 = (f32[144,128]{1,0:T(8,128)S(1)}, f32[144,128]{1,0:T(8,128)S(1)}, u32[]{:S(2)}, u32[]{:S(2)}) collective-permute-start(f32[144,128]{1,0:T(8,128)S(1)} %get-tuple-element.97), channel_id=1, source_target_pairs={{0,24},{8,16},{16,8},{24,0},{1,25},{9,17},{17,9},{25,1},{2,26},{10... | collective-permute-start | bytes 221192 | tf_op jit(solution)/shard_map/ppermute | solution.py:574
  55.1 0.5 collective-permute-start.17
  55.6 0.7 %shard_map.134 = f32[8,32,128]{2,1,0:T(8,128)} custom-call(f32[8,32,128]{2,1,0:T(8,128)S(1)} %get-tuple-element.59.value), custom_call_target="tpu_custom_call" | custom-call | tf_op jit(solution)/shard_map/pallas_call | solution.py:611
  56.3 0.5 shard_map.141
  56.8 1.1 %collective-permute-done.15.rest_0_ = f32[144,128]{1,0:T(8,128)S(1)} collective-permute-done((f32[144,128]{1,0:T(8,128)S(1)}, f32[144,128]{1,0:T(8,128)S(1)}, u32[]{:S(2)}, u32[]{:S(2)}) %collective-permute-start.15) | collective-permute-done | bytes 73760 | tf_op jit(solution)/shard_map/ppermute | solution.py:574
  57.9 2.4 %collective-permute-done.16.rest_1_ = f32[144,128]{1,0:T(8,128)S(1)} collective-permute-done((f32[144,128]{1,0:T(8,128)S(1)}, f32[144,128]{1,0:T(8,128)S(1)}, u32[]{:S(2)}, u32[]{:S(2)}) %collective-permute-start.16) | collective-permute-done | bytes 73760 | tf_op jit(solution)/shard_map/ppermute | solution.py:574
  60.3 0.0 collective-permute-done.17.rest_2_
  60.3 1.6 %shard_map.142 = (f32[16,16,256]{2,1,0:T(8,128)}, f32[16,16,256]{2,1,0:T(8,128)}) custom-call(s32[2,128]{1,0:T(2,128)S(1)} %copy-done.10, f32[16,16,256]{2,1,0:T(8,128)S(1)} %get-tuple-element.92.phase, f32[16,16,256]{2,1,0:T(8,128)S(1)} %get-tuple-element.93.solute, f32[32,16,128]{2,1,0:T(8,128)S(1)} %get-tuple-element.94.own, ...), custom_call_target="tpu_custom_call" | custom-call | tf_op jit(solution)/shard_map/pallas_call | solution.py:650
  (18 shorter events, 0.1 us)
Async XLA Ops:
  0.6 10.1 %copy-start.1 = (bf16[512,256]{1,0:T(8,128)(2,1)S(1)}, bf16[512,256]{1,0:T(8,128)(2,1)}, u32[]{:S(2)}) copy-start(bf16[512,256]{1,0:T(8,128)(2,1)} %constant.8.clone.picks) | copy-start | bytes 786436
  2.9 5.2 %copy-start.12 = (f32[8,128]{1,0:T(8,128)S(1)}, f32[8,128]{1,0:T(8,128)}, u32[]{:S(2)}) copy-start(f32[8,128]{1,0:T(8,128)} %get-tuple-element.56) | copy-start | bytes 12292
  2.9 11.4 %all-to-all-start = ((f32[8,24,128]{2,1,0:T(8,128)}), f32[8,24,128]{2,1,0:T(8,128)S(1)}, u32[]{:S(2)}, u32[]{:S(2)}) async-start(f32[8,24,128]{2,1,0:T(8,128)} %get-tuple-element.55), calls=%async_computation | async-start | bytes 196608 | tf_op jit(solution)/shard_map/all_to_all | solution.py:564
  8.1 6.2 %collective-permute-start = (f32[8,128]{1,0:T(8,128)S(1)}, f32[8,128]{1,0:T(8,128)S(1)}, u32[]{:S(2)}, u32[]{:S(2)}) collective-permute-start(f32[8,128]{1,0:T(8,128)S(1)} %copy-done.12), channel_id=1, source_target_pairs={{0,16},{8,24},{16,0},{24,8},{1,17},{9,25},{17,1},{25,9},{2,18},{10... | collective-permute-start | bytes 12296 | tf_op jit(solution)/shard_map/ppermute | solution.py:567
  10.7 0.7 %copy-start.11 = (f32[4,128]{1,0:T(4,128)S(1)}, f32[4,128]{1,0:T(4,128)}, u32[]{:S(2)}) copy-start(f32[4,128]{1,0:T(4,128)} %get-tuple-element.53.asked) | copy-start | bytes 6148
  10.7 0.7 %copy-start.10 = (s32[2,128]{1,0:T(2,128)S(1)}, s32[2,128]{1,0:T(2,128)}, u32[]{:S(2)}) copy-start(s32[2,128]{1,0:T(2,128)} %get-tuple-element.52.table) | copy-start | bytes 3076
  11.4 0.9 %copy-start.2 = (f32[1,1,1,16,16,256]{5,4,3,2,1,0:T(8,128)S(1)}, f32[1,1,1,16,16,256]{5,4,3,2,1,0:T(8,128)}, u32[]{:S(2)}) copy-start(f32[1,1,1,16,16,256]{5,4,3,2,1,0:T(8,128)} %param.13) | copy-start | bytes 786436
  12.4 0.9 %copy-start.7 = (f32[1,1,1,16,16,256]{5,4,3,2,1,0:T(8,128)S(1)}, f32[1,1,1,16,16,256]{5,4,3,2,1,0:T(8,128)}, u32[]{:S(2)}) copy-start(f32[1,1,1,16,16,256]{5,4,3,2,1,0:T(8,128)} %param.14) | copy-start | bytes 786436
  13.3 0.9 %copy-start.5 = (f32[8,32,128]{2,1,0:T(8,128)S(1)}, f32[8,32,128]{2,1,0:T(8,128)}, u32[]{:S(2)}) copy-start(f32[8,32,128]{2,1,0:T(8,128)} %h.3) | copy-start | bytes 393220
  13.3 1.0 %copy-start.6 = (f32[8,32,128]{2,1,0:T(8,128)S(1)}, f32[8,32,128]{2,1,0:T(8,128)}, u32[]{:S(2)}) copy-start(f32[8,32,128]{2,1,0:T(8,128)} %k.3) | copy-start | bytes 393220
  14.3 14.1 %copy-start.8 = (f32[1,1,1,16,16,256]{5,4,3,2,1,0:T(8,128)S(1)}, f32[1,1,1,16,16,256]{5,4,3,2,1,0:T(8,128)}, u32[]{:S(2)}) copy-start(f32[1,1,1,16,16,256]{5,4,3,2,1,0:T(8,128)} %param.14) | copy-start | bytes 786436
  14.3 14.0 %copy-start.3 = (f32[1,1,1,16,16,256]{5,4,3,2,1,0:T(8,128)S(1)}, f32[1,1,1,16,16,256]{5,4,3,2,1,0:T(8,128)}, u32[]{:S(2)}) copy-start(f32[1,1,1,16,16,256]{5,4,3,2,1,0:T(8,128)} %param.13) | copy-start | bytes 786436
  14.3 7.4 %collective-permute-start.1 = (f32[104,128]{1,0:T(8,128)S(1)}, f32[104,128]{1,0:T(8,128)S(1)}, u32[]{:S(2)}, u32[]{:S(2)}) collective-permute-start(f32[104,128]{1,0:T(8,128)S(1)} %get-tuple-element.57), channel_id=1, source_target_pairs={{0,8},{8,16},{16,24},{24,0},{1,9},{9,17},{17,25},{25,1},{2,10},{10... | collective-permute-start | bytes 159752 | tf_op jit(solution)/shard_map/ppermute | solution.py:567
  16.0 5.8 %collective-permute-start.2 = (f32[104,128]{1,0:T(8,128)S(1)}, f32[104,128]{1,0:T(8,128)S(1)}, u32[]{:S(2)}, u32[]{:S(2)}) collective-permute-start(f32[104,128]{1,0:T(8,128)S(1)} %get-tuple-element.58), channel_id=1, source_target_pairs={{0,24},{8,0},{16,8},{24,16},{1,25},{9,1},{17,9},{25,17},{2,26},{10... | collective-permute-start | bytes 159752 | tf_op jit(solution)/shard_map/ppermute | solution.py:567
  18.2 9.2 %collective-permute-start.6 = (f32[144,128]{1,0:T(8,128)S(1)}, f32[144,128]{1,0:T(8,128)S(1)}, u32[]{:S(2)}, u32[]{:S(2)}) collective-permute-start(f32[144,128]{1,0:T(8,128)S(1)} %get-tuple-element.68), channel_id=1, source_target_pairs={{0,16},{8,24},{16,0},{24,8},{1,17},{9,25},{17,1},{25,9},{2,18},{10... | collective-permute-start | bytes 221192 | tf_op jit(solution)/shard_map/ppermute | solution.py:574
  18.2 10.6 %collective-permute-start.7 = (f32[144,128]{1,0:T(8,128)S(1)}, f32[144,128]{1,0:T(8,128)S(1)}, u32[]{:S(2)}, u32[]{:S(2)}) collective-permute-start(f32[144,128]{1,0:T(8,128)S(1)} %get-tuple-element.69), channel_id=1, source_target_pairs={{0,24},{8,16},{16,8},{24,0},{1,25},{9,17},{17,9},{25,1},{2,26},{10... | collective-permute-start | bytes 221192 | tf_op jit(solution)/shard_map/ppermute | solution.py:574
  20.3 8.5 %collective-permute-start.8 = (f32[144,128]{1,0:T(8,128)S(1)}, f32[144,128]{1,0:T(8,128)S(1)}, u32[]{:S(2)}, u32[]{:S(2)}) collective-permute-start(f32[144,128]{1,0:T(8,128)S(1)} %get-tuple-element.70), channel_id=1, source_target_pairs={{0,8},{8,0},{16,24},{24,16},{1,9},{9,1},{17,25},{25,17},{2,10},{10... | collective-permute-start | bytes 221192 | tf_op jit(solution)/shard_map/ppermute | solution.py:574
  21.8 6.6 %copy-start.4 = (bf16[256,256]{1,0:T(8,128)(2,1)S(1)}, bf16[256,256]{1,0:T(8,128)(2,1)}, u32[]{:S(2)}) copy-start(bf16[256,256]{1,0:T(8,128)(2,1)} %constant.9.clone.stencil) | copy-start | bytes 393220
  23.7 5.6 %collective-permute-start.3 = (f32[32,128]{1,0:T(8,128)S(1)}, f32[32,128]{1,0:T(8,128)S(1)}, u32[]{:S(2)}, u32[]{:S(2)}) collective-permute-start(f32[32,128]{1,0:T(8,128)S(1)} %get-tuple-element.65), channel_id=1, source_target_pairs={{0,8},{8,16},{16,24},{24,0},{1,9},{9,17},{17,25},{25,1},{2,10},{10... | collective-permute-start | bytes 49160 | tf_op jit(solution)/shard_map/ppermute | solution.py:567
  24.4 4.9 %collective-permute-start.4 = (f32[32,128]{1,0:T(8,128)S(1)}, f32[32,128]{1,0:T(8,128)S(1)}, u32[]{:S(2)}, u32[]{:S(2)}) collective-permute-start(f32[32,128]{1,0:T(8,128)S(1)} %get-tuple-element.66), channel_id=1, source_target_pairs={{0,16},{8,24},{16,0},{24,8},{1,17},{9,25},{17,1},{25,9},{2,18},{10... | collective-permute-start | bytes 49160 | tf_op jit(solution)/shard_map/ppermute | solution.py:567
  27.4 3.7 %copy-start = (bf16[256,512]{1,0:T(8,128)(2,1)S(1)}, bf16[256,512]{1,0:T(8,128)(2,1)}, u32[]{:S(2)}) copy-start(bf16[256,512]{1,0:T(8,128)(2,1)} %constant.10.clone.places) | copy-start | bytes 786436
  27.4 3.7 %copy-start.9 = (bf16[256,256]{1,0:T(8,128)(2,1)S(1)}, bf16[256,256]{1,0:T(8,128)(2,1)}, u32[]{:S(2)}) copy-start(bf16[256,256]{1,0:T(8,128)(2,1)} %constant.11.clone.spreads) | copy-start | bytes 393220
  27.4 3.7 %collective-permute-start.5 = (f32[32,128]{1,0:T(8,128)S(1)}, f32[32,128]{1,0:T(8,128)S(1)}, u32[]{:S(2)}, u32[]{:S(2)}) collective-permute-start(f32[32,128]{1,0:T(8,128)S(1)} %get-tuple-element.67), channel_id=1, source_target_pairs={{0,24},{8,0},{16,8},{24,16},{1,25},{9,1},{17,9},{25,17},{2,26},{10... | collective-permute-start | bytes 49160 | tf_op jit(solution)/shard_map/ppermute | solution.py:567
  32.8 6.1 %collective-permute-start.9 = (f32[144,128]{1,0:T(8,128)S(1)}, f32[144,128]{1,0:T(8,128)S(1)}, u32[]{:S(2)}, u32[]{:S(2)}) collective-permute-start(f32[144,128]{1,0:T(8,128)S(1)} %get-tuple-element.78), channel_id=1, source_target_pairs={{0,16},{8,24},{16,0},{24,8},{1,17},{9,25},{17,1},{25,9},{2,18},{10... | collective-permute-start | bytes 221192 | tf_op jit(solution)/shard_map/ppermute | solution.py:574
  33.8 6.3 %collective-permute-start.10 = (f32[144,128]{1,0:T(8,128)S(1)}, f32[144,128]{1,0:T(8,128)S(1)}, u32[]{:S(2)}, u32[]{:S(2)}) collective-permute-start(f32[144,128]{1,0:T(8,128)S(1)} %get-tuple-element.79), channel_id=1, source_target_pairs={{0,24},{8,16},{16,8},{24,0},{1,25},{9,17},{17,9},{25,1},{2,26},{10... | collective-permute-start | bytes 221192 | tf_op jit(solution)/shard_map/ppermute | solution.py:574
  36.0 4.9 %collective-permute-start.11 = (f32[144,128]{1,0:T(8,128)S(1)}, f32[144,128]{1,0:T(8,128)S(1)}, u32[]{:S(2)}, u32[]{:S(2)}) collective-permute-start(f32[144,128]{1,0:T(8,128)S(1)} %get-tuple-element.80), channel_id=1, source_target_pairs={{0,8},{8,0},{16,24},{24,16},{1,9},{9,1},{17,25},{25,17},{2,10},{10... | collective-permute-start | bytes 221192 | tf_op jit(solution)/shard_map/ppermute | solution.py:574
  42.1 6.0 %collective-permute-start.12 = (f32[144,128]{1,0:T(8,128)S(1)}, f32[144,128]{1,0:T(8,128)S(1)}, u32[]{:S(2)}, u32[]{:S(2)}) collective-permute-start(f32[144,128]{1,0:T(8,128)S(1)} %get-tuple-element.87), channel_id=1, source_target_pairs={{0,16},{8,24},{16,0},{24,8},{1,17},{9,25},{17,1},{25,9},{2,18},{10... | collective-permute-start | bytes 221192 | tf_op jit(solution)/shard_map/ppermute | solution.py:574
  43.8 6.8 %collective-permute-start.13 = (f32[144,128]{1,0:T(8,128)S(1)}, f32[144,128]{1,0:T(8,128)S(1)}, u32[]{:S(2)}, u32[]{:S(2)}) collective-permute-start(f32[144,128]{1,0:T(8,128)S(1)} %get-tuple-element.88), channel_id=1, source_target_pairs={{0,24},{8,16},{16,8},{24,0},{1,25},{9,17},{17,9},{25,1},{2,26},{10... | collective-permute-start | bytes 221192 | tf_op jit(solution)/shard_map/ppermute | solution.py:574
  45.0 5.6 %collective-permute-start.14 = (f32[144,128]{1,0:T(8,128)S(1)}, f32[144,128]{1,0:T(8,128)S(1)}, u32[]{:S(2)}, u32[]{:S(2)}) collective-permute-start(f32[144,128]{1,0:T(8,128)S(1)} %get-tuple-element.89), channel_id=1, source_target_pairs={{0,8},{8,0},{16,24},{24,16},{1,9},{9,1},{17,25},{25,17},{2,10},{10... | collective-permute-start | bytes 221192 | tf_op jit(solution)/shard_map/ppermute | solution.py:574
  51.8 6.1 %collective-permute-start.15 = (f32[144,128]{1,0:T(8,128)S(1)}, f32[144,128]{1,0:T(8,128)S(1)}, u32[]{:S(2)}, u32[]{:S(2)}) collective-permute-start(f32[144,128]{1,0:T(8,128)S(1)} %get-tuple-element.96), channel_id=1, source_target_pairs={{0,16},{8,24},{16,0},{24,8},{1,17},{9,25},{17,1},{25,9},{2,18},{10... | collective-permute-start | bytes 221192 | tf_op jit(solution)/shard_map/ppermute | solution.py:574
  54.2 6.2 %collective-permute-start.16 = (f32[144,128]{1,0:T(8,128)S(1)}, f32[144,128]{1,0:T(8,128)S(1)}, u32[]{:S(2)}, u32[]{:S(2)}) collective-permute-start(f32[144,128]{1,0:T(8,128)S(1)} %get-tuple-element.97), channel_id=1, source_target_pairs={{0,24},{8,16},{16,8},{24,0},{1,25},{9,17},{17,9},{25,1},{2,26},{10... | collective-permute-start | bytes 221192 | tf_op jit(solution)/shard_map/ppermute | solution.py:574
  55.1 5.2 %collective-permute-start.17 = (f32[144,128]{1,0:T(8,128)S(1)}, f32[144,128]{1,0:T(8,128)S(1)}, u32[]{:S(2)}, u32[]{:S(2)}) collective-permute-start(f32[144,128]{1,0:T(8,128)S(1)} %get-tuple-element.98), channel_id=1, source_target_pairs={{0,8},{8,0},{16,24},{24,16},{1,9},{9,1},{17,25},{25,17},{2,10},{10... | collective-permute-start | bytes 221192 | tf_op jit(solution)/shard_map/ppermute | solution.py:574

commit v18 on v14

--- a/solution.py
+++ b/solution.py
@@ -132,7 +132,7 @@
 
 
 def swap_order(count):
-    return sorted(range(1, count), key=lambda s: (-s.bit_length(), s))
+    return list(range(count - 1, 0, -1))
 
 
 def place_of(table, slot):

time: 62.3 us -> 63.4 us (1.018)
  starting transfers between devices: 30.7 us -> 33.4 us
  waiting for transfers between devices: 14.4 us -> 12.7 us
    ppermute x12, starting transfers between devices: 14.3 us -> 17.7 us  [swap_all(): lax.ppermute(value, 'gx', [(i, i ^ swap) for i in range(count)])]
    ppermute x12, waiting for transfers between devices: 12 us -> 10.7 us  [swap_all(): lax.ppermute(value, 'gx', [(i, i ^ swap) for i in range(count)])]
    ppermute x6, starting transfers between devices: 11.2 us -> 10.5 us  [pass_on(): lax.ppermute(value, 'gx', [(i, (i + shift) % count) for i in range(count)])]
  transfers between devices with their start and end apart: 19 -> 19, of which waited for: 9 -> 8; matrix products, arithmetic and copies ran while one was open for 0% -> 0% of each run, Pallas kernels for 9% -> 9%
where the time goes in v18:
time: 63.4 us; the launch traced here: 63.1 us
  starting transfers between devices  33.4 us (53%)
  Pallas kernels  13.4 us (21%)
  waiting for transfers between devices  12.7 us (20%)
  local copies, waits for them, and re-layouts  2.65 us (4%)
  between operations  0.85 us (1%)
    ppermute x12, starting transfers between devices, swap_all(): lax.ppermute(value, 'gx', [(i, i ^ swap) for i in range(count)])  17.7 us
    ppermute x12, waiting for transfers between devices, swap_all(): lax.ppermute(value, 'gx', [(i, i ^ swap) for i in range(count)])  10.7 us
    ppermute x6, starting transfers between devices, pass_on(): lax.ppermute(value, 'gx', [(i, (i + shift) % count) for i in range(count)])  10.5 us
    all_to_all x1, starting transfers between devices, local(): lax.all_to_all(sides, ('gy', 'gz'), split_axis=0, concat_axis=0, tiled=True)  5.18 us
    unnamed x26, local copies, waits for them, and re-layouts  2.64 us
    pallas_call x2, Pallas kernels, local(): call(middle_step_kernel, [SMEM] + [VMEM] * (6 + others), [field, field, *...  2.45 us
    pallas_call x1, Pallas kernels, local(): call(functools.partial(sides_kernel, sizes, plane_cap), [ANY] * 5, [shape...  2.21 us
    ppermute x6, waiting for transfers between devices, pass_on(): lax.ppermute(value, 'gx', [(i, (i + shift) % count) for i in range(count)])  2.04 us
  transfers between devices with their start and end apart: 19, of which 8 were waited for; matrix products, arithmetic and copies ran while one was open for 0% of the time, Pallas kernels for 9%

profile of v18, /device:TPU:0, one launch (start us, length us, event | category | flops | bytes accessed | tf_op | source)
XLA Modules:
  0.0 63.1 jit_solution(14237527172891864135)
XLA Ops:
  0.6 0.0 copy-start.1
  0.6 2.2 %shard_map.130 = (f32[8,24,128]{2,1,0:T(8,128)}, s32[2,128]{1,0:T(2,128)}, f32[4,128]{1,0:T(4,128)}, f32[8,128]{1,0:T(8,128)}) custom-call(s32[1,16]{1,0:T(1,128)} %bitcast.15, s32[1,16]{1,0:T(1,128)} %bitcast.16, s32[6,1,16]{2,1,0:T(1,128)} %bitcast.14, f32[8,32,128]{2,1,0:T(8,128)} %h.3, f32[8,32,128]{2,1,0:T(8,128)} %k.3), custom_call_target="tpu_custom_call" | custom-call | tf_op jit(solution)/shard_map/pallas_call | solution.py:537
  2.9 0.0 copy-start.12
  2.9 5.2 %all-to-all-start = ((f32[8,24,128]{2,1,0:T(8,128)}), f32[8,24,128]{2,1,0:T(8,128)S(1)}, u32[]{:S(2)}, u32[]{:S(2)}) async-start(f32[8,24,128]{2,1,0:T(8,128)} %get-tuple-element.55), calls=%async_computation | async-start | bytes 196608 | tf_op jit(solution)/shard_map/all_to_all | solution.py:562
  8.1 0.0 copy-done.12
  8.1 2.7 %collective-permute-start = (f32[8,128]{1,0:T(8,128)S(1)}, f32[8,128]{1,0:T(8,128)S(1)}, u32[]{:S(2)}, u32[]{:S(2)}) collective-permute-start(f32[8,128]{1,0:T(8,128)S(1)} %copy-done.12), channel_id=1, source_target_pairs={{0,16},{8,24},{16,0},{24,8},{1,17},{9,25},{17,1},{25,9},{2,18},{10... | collective-permute-start | bytes 12296 | tf_op jit(solution)/shard_map/ppermute | solution.py:565
  10.7 0.0 copy-done.1
  10.7 0.7 %copy-done.11 = f32[4,128]{1,0:T(4,128)S(1)} copy-done((f32[4,128]{1,0:T(4,128)S(1)}, f32[4,128]{1,0:T(4,128)}, u32[]{:S(2)}) %copy-start.11) | copy-done | bytes 2072
  11.4 0.0 copy-done.10
  11.4 0.9 %copy-done.2 = f32[1,1,1,16,16,256]{5,4,3,2,1,0:T(8,128)S(1)} copy-done((f32[1,1,1,16,16,256]{5,4,3,2,1,0:T(8,128)S(1)}, f32[1,1,1,16,16,256]{5,4,3,2,1,0:T(8,128)}, u32[]{:S(2)}) %copy-start.2) | copy-done | bytes 262168
  12.4 0.9 %copy-done.7 = f32[1,1,1,16,16,256]{5,4,3,2,1,0:T(8,128)S(1)} copy-done((f32[1,1,1,16,16,256]{5,4,3,2,1,0:T(8,128)S(1)}, f32[1,1,1,16,16,256]{5,4,3,2,1,0:T(8,128)}, u32[]{:S(2)}) %copy-start.7) | copy-done | bytes 262168
  13.3 0.9 %shard_map.131 = (f32[32,16,128]{2,1,0:T(8,128)S(1)}, f32[256,128]{1,0:T(8,128)S(1)}, f32[4,128]{1,0:T(4,128)S(1)}, f32[144,128]{1,0:T(8,128)S(1)}, f32[144,128]{1,0:T(8,128)S(1)}, /*index=5*/f32[144,128]{1,0:T(8,128)S(1)}) custom-call(s32[2,128]{1,0:T(2,128)S(1)} %copy-done.10, f32[4,128]{1,0:T(4,128)S(1)} %copy-done.11, f32[16,16,256]{2,1,0:T(8,128)S(1)} %bitcast.9, ...), custom_call_target="tpu_custom_call" | custom-call | tf_op jit(solution)/shard_map/pallas_call | solution.py:583
  14.2 0.0 collective-permute-done.rest_0_
  14.2 0.0 all-to-all-done.got
  14.3 0.0 copy-done.5
  14.3 0.0 copy-done.6
  14.3 0.0 copy-start.8
  14.3 0.0 copy-start.3
  14.3 1.6 %collective-permute-start.1 = (f32[104,128]{1,0:T(8,128)S(1)}, f32[104,128]{1,0:T(8,128)S(1)}, u32[]{:S(2)}, u32[]{:S(2)}) collective-permute-start(f32[104,128]{1,0:T(8,128)S(1)} %get-tuple-element.57), channel_id=1, source_target_pairs={{0,8},{8,16},{16,24},{24,0},{1,9},{9,17},{17,25},{25,1},{2,10},{10... | collective-permute-start | bytes 159752 | tf_op jit(solution)/shard_map/ppermute | solution.py:565
  16.0 2.2 %collective-permute-start.2 = (f32[104,128]{1,0:T(8,128)S(1)}, f32[104,128]{1,0:T(8,128)S(1)}, u32[]{:S(2)}, u32[]{:S(2)}) collective-permute-start(f32[104,128]{1,0:T(8,128)S(1)} %get-tuple-element.58), channel_id=1, source_target_pairs={{0,24},{8,0},{16,8},{24,16},{1,25},{9,1},{17,9},{25,17},{2,26},{10... | collective-permute-start | bytes 159752 | tf_op jit(solution)/shard_map/ppermute | solution.py:565
  18.2 0.8 %collective-permute-start.6 = (f32[144,128]{1,0:T(8,128)S(1)}, f32[144,128]{1,0:T(8,128)S(1)}, u32[]{:S(2)}, u32[]{:S(2)}) collective-permute-start(f32[144,128]{1,0:T(8,128)S(1)} %get-tuple-element.68), channel_id=1, source_target_pairs={{0,24},{8,16},{16,8},{24,0},{1,25},{9,17},{17,9},{25,1},{2,26},{10... | collective-permute-start | bytes 221192 | tf_op jit(solution)/shard_map/ppermute | solution.py:572
  19.0 0.5 collective-permute-start.7
  19.4 3.1 %collective-permute-start.8 = (f32[144,128]{1,0:T(8,128)S(1)}, f32[144,128]{1,0:T(8,128)S(1)}, u32[]{:S(2)}, u32[]{:S(2)}) collective-permute-start(f32[144,128]{1,0:T(8,128)S(1)} %get-tuple-element.70), channel_id=1, source_target_pairs={{0,8},{8,0},{16,24},{24,16},{1,9},{9,1},{17,25},{25,17},{2,10},{10... | collective-permute-start | bytes 221192 | tf_op jit(solution)/shard_map/ppermute | solution.py:572
  22.6 0.0 collective-permute-done.1.low
  22.6 0.0 collective-permute-done.2.high
  22.6 0.0 copy-start.4
  22.7 1.9 %shard_map.133 = (f32[8,32,128]{2,1,0:T(8,128)S(1)}, f32[32,128]{1,0:T(8,128)S(1)}, f32[32,128]{1,0:T(8,128)S(1)}, f32[32,128]{1,0:T(8,128)S(1)}, f32[32,128]{1,0:T(8,128)S(1)}) custom-call(s32[4,8]{1,0:T(4,128)S(1)} %maximum_convert_fusion.request, f32[8,32,128]{2,1,0:T(8,128)S(1)} %copy-done.5, f32[8,32,128]{2,1,0:T(8,128)S(1)} %copy-done.6, ...), custom_call_target="tpu_custom_call" | custom-call | tf_op jit(solution)/shard_map/pallas_call | solution.py:602
  24.6 0.1 collective-permute-start.3
  24.6 2.7 %collective-permute-start.4 = (f32[32,128]{1,0:T(8,128)S(1)}, f32[32,128]{1,0:T(8,128)S(1)}, u32[]{:S(2)}, u32[]{:S(2)}) collective-permute-start(f32[32,128]{1,0:T(8,128)S(1)} %get-tuple-element.66), channel_id=1, source_target_pairs={{0,16},{8,24},{16,0},{24,8},{1,17},{9,25},{17,1},{25,9},{2,18},{10... | collective-permute-start | bytes 49160 | tf_op jit(solution)/shard_map/ppermute | solution.py:565
  27.3 0.0 collective-permute-done.6.rest_4_
  27.3 1.2 %collective-permute-start.5 = (f32[32,128]{1,0:T(8,128)S(1)}, f32[32,128]{1,0:T(8,128)S(1)}, u32[]{:S(2)}, u32[]{:S(2)}) collective-permute-start(f32[32,128]{1,0:T(8,128)S(1)} %get-tuple-element.67), channel_id=1, source_target_pairs={{0,24},{8,0},{16,8},{24,16},{1,25},{9,1},{17,9},{25,17},{2,26},{10... | collective-permute-start | bytes 49160 | tf_op jit(solution)/shard_map/ppermute | solution.py:565
  28.5 0.0 copy-done.8
  28.5 0.5 shard_map.135
  29.0 0.0 collective-permute-done.7.rest_5_
  29.0 0.0 collective-permute-done.8.rest_6_
  29.0 1.1 %collective-permute-done.3.rest_1_ = f32[32,128]{1,0:T(8,128)S(1)} collective-permute-done((f32[32,128]{1,0:T(8,128)S(1)}, f32[32,128]{1,0:T(8,128)S(1)}, u32[]{:S(2)}, u32[]{:S(2)}) %collective-permute-start.3) | collective-permute-done | bytes 16416 | tf_op jit(solution)/shard_map/ppermute | solution.py:565
  30.2 0.0 collective-permute-done.4.rest_2_
  30.2 0.9 %collective-permute-done.5.rest_3_ = f32[32,128]{1,0:T(8,128)S(1)} collective-permute-done((f32[32,128]{1,0:T(8,128)S(1)}, f32[32,128]{1,0:T(8,128)S(1)}, u32[]{:S(2)}, u32[]{:S(2)}) %collective-permute-start.5) | collective-permute-done | bytes 16416 | tf_op jit(solution)/shard_map/ppermute | solution.py:565
  31.1 1.7 %shard_map.136 = (f32[16,16,256]{2,1,0:T(8,128)S(1)}, f32[16,16,256]{2,1,0:T(8,128)S(1)}, f32[2,256,128]{2,1,0:T(8,128)S(1)}, f32[32,16,128]{2,1,0:T(8,128)S(1)}...) custom-call(s32[2,128]{1,0:T(2,128)S(1)} %copy-done.10, ...), custom_call_target="tpu_custom_call" | custom-call | tf_op jit(solution)/shard_map/pallas_call | solution.py:625
  32.7 3.1 %collective-permute-start.9 = (f32[144,128]{1,0:T(8,128)S(1)}, f32[144,128]{1,0:T(8,128)S(1)}, u32[]{:S(2)}, u32[]{:S(2)}) collective-permute-start(f32[144,128]{1,0:T(8,128)S(1)} %get-tuple-element.78), channel_id=1, source_target_pairs={{0,24},{8,16},{16,8},{24,0},{1,25},{9,17},{17,9},{25,1},{2,26},{10... | collective-permute-start | bytes 221192 | tf_op jit(solution)/shard_map/ppermute | solution.py:572
  35.8 0.2 collective-permute-start.10
  36.0 1.2 %collective-permute-start.11 = (f32[144,128]{1,0:T(8,128)S(1)}, f32[144,128]{1,0:T(8,128)S(1)}, u32[]{:S(2)}, u32[]{:S(2)}) collective-permute-start(f32[144,128]{1,0:T(8,128)S(1)} %get-tuple-element.80), channel_id=1, source_target_pairs={{0,8},{8,0},{16,24},{24,16},{1,9},{9,1},{17,25},{25,17},{2,10},{10... | collective-permute-start | bytes 221192 | tf_op jit(solution)/shard_map/ppermute | solution.py:572
  37.2 0.5 shard_map.137
  37.7 1.4 %collective-permute-done.9.rest_0_ = f32[144,128]{1,0:T(8,128)S(1)} collective-permute-done((f32[144,128]{1,0:T(8,128)S(1)}, f32[144,128]{1,0:T(8,128)S(1)}, u32[]{:S(2)}, u32[]{:S(2)}) %collective-permute-start.9) | collective-permute-done | bytes 73760 | tf_op jit(solution)/shard_map/ppermute | solution.py:572
  39.1 2.0 %collective-permute-done.10.rest_1_ = f32[144,128]{1,0:T(8,128)S(1)} collective-permute-done((f32[144,128]{1,0:T(8,128)S(1)}, f32[144,128]{1,0:T(8,128)S(1)}, u32[]{:S(2)}, u32[]{:S(2)}) %collective-permute-start.10) | collective-permute-done | bytes 73760 | tf_op jit(solution)/shard_map/ppermute | solution.py:572
  41.1 0.0 collective-permute-done.11.rest_2_
  41.1 1.2 %shard_map.138 = (f32[16,16,256]{2,1,0:T(8,128)S(1)}, f32[16,16,256]{2,1,0:T(8,128)S(1)}, f32[32,16,128]{2,1,0:T(8,128)S(1)}, f32[256,128]{1,0:T(8,128)S(1)}, f3...) custom-call(s32[2,128]{1,0:T(2,128)S(1)} %copy-done.10, ...), custom_call_target="tpu_custom_call" | custom-call | tf_op jit(solution)/shard_map/pallas_call | solution.py:639
  42.3 2.4 %collective-permute-start.12 = (f32[144,128]{1,0:T(8,128)S(1)}, f32[144,128]{1,0:T(8,128)S(1)}, u32[]{:S(2)}, u32[]{:S(2)}) collective-permute-start(f32[144,128]{1,0:T(8,128)S(1)} %get-tuple-element.87), channel_id=1, source_target_pairs={{0,24},{8,16},{16,8},{24,0},{1,25},{9,17},{17,9},{25,1},{2,26},{10... | collective-permute-start | bytes 221192 | tf_op jit(solution)/shard_map/ppermute | solution.py:572
  44.8 0.0 collective-permute-start.13
  44.8 2.0 %collective-permute-start.14 = (f32[144,128]{1,0:T(8,128)S(1)}, f32[144,128]{1,0:T(8,128)S(1)}, u32[]{:S(2)}, u32[]{:S(2)}) collective-permute-start(f32[144,128]{1,0:T(8,128)S(1)} %get-tuple-element.89), channel_id=1, source_target_pairs={{0,8},{8,0},{16,24},{24,16},{1,9},{9,1},{17,25},{25,17},{2,10},{10... | collective-permute-start | bytes 221192 | tf_op jit(solution)/shard_map/ppermute | solution.py:572
  46.8 0.5 shard_map.139
  47.3 1.3 %collective-permute-done.12.rest_0_ = f32[144,128]{1,0:T(8,128)S(1)} collective-permute-done((f32[144,128]{1,0:T(8,128)S(1)}, f32[144,128]{1,0:T(8,128)S(1)}, u32[]{:S(2)}, u32[]{:S(2)}) %collective-permute-start.12) | collective-permute-done | bytes 73760 | tf_op jit(solution)/shard_map/ppermute | solution.py:572
  48.6 2.8 %collective-permute-done.13.rest_1_ = f32[144,128]{1,0:T(8,128)S(1)} collective-permute-done((f32[144,128]{1,0:T(8,128)S(1)}, f32[144,128]{1,0:T(8,128)S(1)}, u32[]{:S(2)}, u32[]{:S(2)}) %collective-permute-start.13) | collective-permute-done | bytes 73760 | tf_op jit(solution)/shard_map/ppermute | solution.py:572
  51.4 0.0 collective-permute-done.14.rest_2_
  51.4 1.2 %shard_map.140 = (f32[16,16,256]{2,1,0:T(8,128)S(1)}, f32[16,16,256]{2,1,0:T(8,128)S(1)}, f32[32,16,128]{2,1,0:T(8,128)S(1)}, f32[256,128]{1,0:T(8,128)S(1)}, f3...) custom-call(s32[2,128]{1,0:T(2,128)S(1)} %copy-done.10, ...), custom_call_target="tpu_custom_call" | custom-call | tf_op jit(solution)/shard_map/pallas_call | solution.py:639
  52.6 3.5 %collective-permute-start.15 = (f32[144,128]{1,0:T(8,128)S(1)}, f32[144,128]{1,0:T(8,128)S(1)}, u32[]{:S(2)}, u32[]{:S(2)}) collective-permute-start(f32[144,128]{1,0:T(8,128)S(1)} %get-tuple-element.96), channel_id=1, source_target_pairs={{0,24},{8,16},{16,8},{24,0},{1,25},{9,17},{17,9},{25,1},{2,26},{10... | collective-permute-start | bytes 221192 | tf_op jit(solution)/shard_map/ppermute | solution.py:572
  56.2 0.0 collective-permute-start.16
  56.2 0.9 %collective-permute-start.17 = (f32[144,128]{1,0:T(8,128)S(1)}, f32[144,128]{1,0:T(8,128)S(1)}, u32[]{:S(2)}, u32[]{:S(2)}) collective-permute-start(f32[144,128]{1,0:T(8,128)S(1)} %get-tuple-element.98), channel_id=1, source_target_pairs={{0,8},{8,0},{16,24},{24,16},{1,9},{9,1},{17,25},{25,17},{2,10},{10... | collective-permute-start | bytes 221192 | tf_op jit(solution)/shard_map/ppermute | solution.py:572
  57.1 0.7 %shard_map.134 = f32[8,32,128]{2,1,0:T(8,128)} custom-call(f32[8,32,128]{2,1,0:T(8,128)S(1)} %get-tuple-element.59.value), custom_call_target="tpu_custom_call" | custom-call | tf_op jit(solution)/shard_map/pallas_call | solution.py:609
  57.8 0.5 shard_map.141
  58.3 0.6 collective-permute-done.15.rest_0_
  58.9 2.6 %collective-permute-done.16.rest_1_ = f32[144,128]{1,0:T(8,128)S(1)} collective-permute-done((f32[144,128]{1,0:T(8,128)S(1)}, f32[144,128]{1,0:T(8,128)S(1)}, u32[]{:S(2)}, u32[]{:S(2)}) %collective-permute-start.16) | collective-permute-done | bytes 73760 | tf_op jit(solution)/shard_map/ppermute | solution.py:572
  61.4 0.0 collective-permute-done.17.rest_2_
  61.4 1.6 %shard_map.142 = (f32[16,16,256]{2,1,0:T(8,128)}, f32[16,16,256]{2,1,0:T(8,128)}) custom-call(s32[2,128]{1,0:T(2,128)S(1)} %copy-done.10, f32[16,16,256]{2,1,0:T(8,128)S(1)} %get-tuple-element.92.phase, f32[16,16,256]{2,1,0:T(8,128)S(1)} %get-tuple-element.93.solute, f32[32,16,128]{2,1,0:T(8,128)S(1)} %get-tuple-element.94.own, ...), custom_call_target="tpu_custom_call" | custom-call | tf_op jit(solution)/shard_map/pallas_call | solution.py:648
  (18 shorter events, 0.1 us)
Async XLA Ops:
  0.6 10.1 %copy-start.1 = (bf16[512,256]{1,0:T(8,128)(2,1)S(1)}, bf16[512,256]{1,0:T(8,128)(2,1)}, u32[]{:S(2)}) copy-start(bf16[512,256]{1,0:T(8,128)(2,1)} %constant.8.clone.picks) | copy-start | bytes 786436
  2.9 5.2 %copy-start.12 = (f32[8,128]{1,0:T(8,128)S(1)}, f32[8,128]{1,0:T(8,128)}, u32[]{:S(2)}) copy-start(f32[8,128]{1,0:T(8,128)} %get-tuple-element.56) | copy-start | bytes 12292
  2.9 11.4 %all-to-all-start = ((f32[8,24,128]{2,1,0:T(8,128)}), f32[8,24,128]{2,1,0:T(8,128)S(1)}, u32[]{:S(2)}, u32[]{:S(2)}) async-start(f32[8,24,128]{2,1,0:T(8,128)} %get-tuple-element.55), calls=%async_computation | async-start | bytes 196608 | tf_op jit(solution)/shard_map/all_to_all | solution.py:562
  8.1 6.2 %collective-permute-start = (f32[8,128]{1,0:T(8,128)S(1)}, f32[8,128]{1,0:T(8,128)S(1)}, u32[]{:S(2)}, u32[]{:S(2)}) collective-permute-start(f32[8,128]{1,0:T(8,128)S(1)} %copy-done.12), channel_id=1, source_target_pairs={{0,16},{8,24},{16,0},{24,8},{1,17},{9,25},{17,1},{25,9},{2,18},{10... | collective-permute-start | bytes 12296 | tf_op jit(solution)/shard_map/ppermute | solution.py:565
  10.7 0.7 %copy-start.11 = (f32[4,128]{1,0:T(4,128)S(1)}, f32[4,128]{1,0:T(4,128)}, u32[]{:S(2)}) copy-start(f32[4,128]{1,0:T(4,128)} %get-tuple-element.53.asked) | copy-start | bytes 6148
  10.7 0.7 %copy-start.10 = (s32[2,128]{1,0:T(2,128)S(1)}, s32[2,128]{1,0:T(2,128)}, u32[]{:S(2)}) copy-start(s32[2,128]{1,0:T(2,128)} %get-tuple-element.52.table) | copy-start | bytes 3076
  11.4 0.9 %copy-start.2 = (f32[1,1,1,16,16,256]{5,4,3,2,1,0:T(8,128)S(1)}, f32[1,1,1,16,16,256]{5,4,3,2,1,0:T(8,128)}, u32[]{:S(2)}) copy-start(f32[1,1,1,16,16,256]{5,4,3,2,1,0:T(8,128)} %param.13) | copy-start | bytes 786436
  12.4 0.9 %copy-start.7 = (f32[1,1,1,16,16,256]{5,4,3,2,1,0:T(8,128)S(1)}, f32[1,1,1,16,16,256]{5,4,3,2,1,0:T(8,128)}, u32[]{:S(2)}) copy-start(f32[1,1,1,16,16,256]{5,4,3,2,1,0:T(8,128)} %param.14) | copy-start | bytes 786436
  13.3 1.0 %copy-start.5 = (f32[8,32,128]{2,1,0:T(8,128)S(1)}, f32[8,32,128]{2,1,0:T(8,128)}, u32[]{:S(2)}) copy-start(f32[8,32,128]{2,1,0:T(8,128)} %h.3) | copy-start | bytes 393220
  13.3 1.0 %copy-start.6 = (f32[8,32,128]{2,1,0:T(8,128)S(1)}, f32[8,32,128]{2,1,0:T(8,128)}, u32[]{:S(2)}) copy-start(f32[8,32,128]{2,1,0:T(8,128)} %k.3) | copy-start | bytes 393220
  14.3 14.2 %copy-start.8 = (f32[1,1,1,16,16,256]{5,4,3,2,1,0:T(8,128)S(1)}, f32[1,1,1,16,16,256]{5,4,3,2,1,0:T(8,128)}, u32[]{:S(2)}) copy-start(f32[1,1,1,16,16,256]{5,4,3,2,1,0:T(8,128)} %param.14) | copy-start | bytes 786436
  14.3 14.2 %copy-start.3 = (f32[1,1,1,16,16,256]{5,4,3,2,1,0:T(8,128)S(1)}, f32[1,1,1,16,16,256]{5,4,3,2,1,0:T(8,128)}, u32[]{:S(2)}) copy-start(f32[1,1,1,16,16,256]{5,4,3,2,1,0:T(8,128)} %param.13) | copy-start | bytes 786436
  14.3 8.3 %collective-permute-start.1 = (f32[104,128]{1,0:T(8,128)S(1)}, f32[104,128]{1,0:T(8,128)S(1)}, u32[]{:S(2)}, u32[]{:S(2)}) collective-permute-start(f32[104,128]{1,0:T(8,128)S(1)} %get-tuple-element.57), channel_id=1, source_target_pairs={{0,8},{8,16},{16,24},{24,0},{1,9},{9,17},{17,25},{25,1},{2,10},{10... | collective-permute-start | bytes 159752 | tf_op jit(solution)/shard_map/ppermute | solution.py:565
  16.0 6.7 %collective-permute-start.2 = (f32[104,128]{1,0:T(8,128)S(1)}, f32[104,128]{1,0:T(8,128)S(1)}, u32[]{:S(2)}, u32[]{:S(2)}) collective-permute-start(f32[104,128]{1,0:T(8,128)S(1)} %get-tuple-element.58), channel_id=1, source_target_pairs={{0,24},{8,0},{16,8},{24,16},{1,25},{9,1},{17,9},{25,17},{2,26},{10... | collective-permute-start | bytes 159752 | tf_op jit(solution)/shard_map/ppermute | solution.py:565
  18.2 9.1 %collective-permute-start.6 = (f32[144,128]{1,0:T(8,128)S(1)}, f32[144,128]{1,0:T(8,128)S(1)}, u32[]{:S(2)}, u32[]{:S(2)}) collective-permute-start(f32[144,128]{1,0:T(8,128)S(1)} %get-tuple-element.68), channel_id=1, source_target_pairs={{0,24},{8,16},{16,8},{24,0},{1,25},{9,17},{17,9},{25,1},{2,26},{10... | collective-permute-start | bytes 221192 | tf_op jit(solution)/shard_map/ppermute | solution.py:572
  19.0 10.0 %collective-permute-start.7 = (f32[144,128]{1,0:T(8,128)S(1)}, f32[144,128]{1,0:T(8,128)S(1)}, u32[]{:S(2)}, u32[]{:S(2)}) collective-permute-start(f32[144,128]{1,0:T(8,128)S(1)} %get-tuple-element.69), channel_id=1, source_target_pairs={{0,16},{8,24},{16,0},{24,8},{1,17},{9,25},{17,1},{25,9},{2,18},{10... | collective-permute-start | bytes 221192 | tf_op jit(solution)/shard_map/ppermute | solution.py:572
  19.4 9.6 %collective-permute-start.8 = (f32[144,128]{1,0:T(8,128)S(1)}, f32[144,128]{1,0:T(8,128)S(1)}, u32[]{:S(2)}, u32[]{:S(2)}) collective-permute-start(f32[144,128]{1,0:T(8,128)S(1)} %get-tuple-element.70), channel_id=1, source_target_pairs={{0,8},{8,0},{16,24},{24,16},{1,9},{9,1},{17,25},{25,17},{2,10},{10... | collective-permute-start | bytes 221192 | tf_op jit(solution)/shard_map/ppermute | solution.py:572
  22.6 5.9 %copy-start.4 = (bf16[256,256]{1,0:T(8,128)(2,1)S(1)}, bf16[256,256]{1,0:T(8,128)(2,1)}, u32[]{:S(2)}) copy-start(bf16[256,256]{1,0:T(8,128)(2,1)} %constant.9.clone.stencil) | copy-start | bytes 393220
  24.6 5.6 %collective-permute-start.3 = (f32[32,128]{1,0:T(8,128)S(1)}, f32[32,128]{1,0:T(8,128)S(1)}, u32[]{:S(2)}, u32[]{:S(2)}) collective-permute-start(f32[32,128]{1,0:T(8,128)S(1)} %get-tuple-element.65), channel_id=1, source_target_pairs={{0,8},{8,16},{16,24},{24,0},{1,9},{9,17},{17,25},{25,1},{2,10},{10... | collective-permute-start | bytes 49160 | tf_op jit(solution)/shard_map/ppermute | solution.py:565
  24.6 5.5 %collective-permute-start.4 = (f32[32,128]{1,0:T(8,128)S(1)}, f32[32,128]{1,0:T(8,128)S(1)}, u32[]{:S(2)}, u32[]{:S(2)}) collective-permute-start(f32[32,128]{1,0:T(8,128)S(1)} %get-tuple-element.66), channel_id=1, source_target_pairs={{0,16},{8,24},{16,0},{24,8},{1,17},{9,25},{17,1},{25,9},{2,18},{10... | collective-permute-start | bytes 49160 | tf_op jit(solution)/shard_map/ppermute | solution.py:565
  27.3 3.7 %copy-start = (bf16[256,512]{1,0:T(8,128)(2,1)S(1)}, bf16[256,512]{1,0:T(8,128)(2,1)}, u32[]{:S(2)}) copy-start(bf16[256,512]{1,0:T(8,128)(2,1)} %constant.10.clone.places) | copy-start | bytes 786436
  27.3 3.7 %copy-start.9 = (bf16[256,256]{1,0:T(8,128)(2,1)S(1)}, bf16[256,256]{1,0:T(8,128)(2,1)}, u32[]{:S(2)}) copy-start(bf16[256,256]{1,0:T(8,128)(2,1)} %constant.11.clone.spreads) | copy-start | bytes 393220
  27.3 3.7 %collective-permute-start.5 = (f32[32,128]{1,0:T(8,128)S(1)}, f32[32,128]{1,0:T(8,128)S(1)}, u32[]{:S(2)}, u32[]{:S(2)}) collective-permute-start(f32[32,128]{1,0:T(8,128)S(1)} %get-tuple-element.67), channel_id=1, source_target_pairs={{0,24},{8,0},{16,8},{24,16},{1,25},{9,1},{17,9},{25,17},{2,26},{10... | collective-permute-start | bytes 49160 | tf_op jit(solution)/shard_map/ppermute | solution.py:565
  32.7 6.4 %collective-permute-start.9 = (f32[144,128]{1,0:T(8,128)S(1)}, f32[144,128]{1,0:T(8,128)S(1)}, u32[]{:S(2)}, u32[]{:S(2)}) collective-permute-start(f32[144,128]{1,0:T(8,128)S(1)} %get-tuple-element.78), channel_id=1, source_target_pairs={{0,24},{8,16},{16,8},{24,0},{1,25},{9,17},{17,9},{25,1},{2,26},{10... | collective-permute-start | bytes 221192 | tf_op jit(solution)/shard_map/ppermute | solution.py:572
  35.8 5.3 %collective-permute-start.10 = (f32[144,128]{1,0:T(8,128)S(1)}, f32[144,128]{1,0:T(8,128)S(1)}, u32[]{:S(2)}, u32[]{:S(2)}) collective-permute-start(f32[144,128]{1,0:T(8,128)S(1)} %get-tuple-element.79), channel_id=1, source_target_pairs={{0,16},{8,24},{16,0},{24,8},{1,17},{9,25},{17,1},{25,9},{2,18},{10... | collective-permute-start | bytes 221192 | tf_op jit(solution)/shard_map/ppermute | solution.py:572
  36.0 5.1 %collective-permute-start.11 = (f32[144,128]{1,0:T(8,128)S(1)}, f32[144,128]{1,0:T(8,128)S(1)}, u32[]{:S(2)}, u32[]{:S(2)}) collective-permute-start(f32[144,128]{1,0:T(8,128)S(1)} %get-tuple-element.80), channel_id=1, source_target_pairs={{0,8},{8,0},{16,24},{24,16},{1,9},{9,1},{17,25},{25,17},{2,10},{10... | collective-permute-start | bytes 221192 | tf_op jit(solution)/shard_map/ppermute | solution.py:572
  42.3 6.2 %collective-permute-start.12 = (f32[144,128]{1,0:T(8,128)S(1)}, f32[144,128]{1,0:T(8,128)S(1)}, u32[]{:S(2)}, u32[]{:S(2)}) collective-permute-start(f32[144,128]{1,0:T(8,128)S(1)} %get-tuple-element.87), channel_id=1, source_target_pairs={{0,24},{8,16},{16,8},{24,0},{1,25},{9,17},{17,9},{25,1},{2,26},{10... | collective-permute-start | bytes 221192 | tf_op jit(solution)/shard_map/ppermute | solution.py:572
  44.8 6.6 %collective-permute-start.13 = (f32[144,128]{1,0:T(8,128)S(1)}, f32[144,128]{1,0:T(8,128)S(1)}, u32[]{:S(2)}, u32[]{:S(2)}) collective-permute-start(f32[144,128]{1,0:T(8,128)S(1)} %get-tuple-element.88), channel_id=1, source_target_pairs={{0,16},{8,24},{16,0},{24,8},{1,17},{9,25},{17,1},{25,9},{2,18},{10... | collective-permute-start | bytes 221192 | tf_op jit(solution)/shard_map/ppermute | solution.py:572
  44.8 6.6 %collective-permute-start.14 = (f32[144,128]{1,0:T(8,128)S(1)}, f32[144,128]{1,0:T(8,128)S(1)}, u32[]{:S(2)}, u32[]{:S(2)}) collective-permute-start(f32[144,128]{1,0:T(8,128)S(1)} %get-tuple-element.89), channel_id=1, source_target_pairs={{0,8},{8,0},{16,24},{24,16},{1,9},{9,1},{17,25},{25,17},{2,10},{10... | collective-permute-start | bytes 221192 | tf_op jit(solution)/shard_map/ppermute | solution.py:572
  52.6 6.2 %collective-permute-start.15 = (f32[144,128]{1,0:T(8,128)S(1)}, f32[144,128]{1,0:T(8,128)S(1)}, u32[]{:S(2)}, u32[]{:S(2)}) collective-permute-start(f32[144,128]{1,0:T(8,128)S(1)} %get-tuple-element.96), channel_id=1, source_target_pairs={{0,24},{8,16},{16,8},{24,0},{1,25},{9,17},{17,9},{25,1},{2,26},{10... | collective-permute-start | bytes 221192 | tf_op jit(solution)/shard_map/ppermute | solution.py:572
  56.2 5.3 %collective-permute-start.16 = (f32[144,128]{1,0:T(8,128)S(1)}, f32[144,128]{1,0:T(8,128)S(1)}, u32[]{:S(2)}, u32[]{:S(2)}) collective-permute-start(f32[144,128]{1,0:T(8,128)S(1)} %get-tuple-element.97), channel_id=1, source_target_pairs={{0,16},{8,24},{16,0},{24,8},{1,17},{9,25},{17,1},{25,9},{2,18},{10... | collective-permute-start | bytes 221192 | tf_op jit(solution)/shard_map/ppermute | solution.py:572
  56.2 5.3 %collective-permute-start.17 = (f32[144,128]{1,0:T(8,128)S(1)}, f32[144,128]{1,0:T(8,128)S(1)}, u32[]{:S(2)}, u32[]{:S(2)}) collective-permute-start(f32[144,128]{1,0:T(8,128)S(1)} %get-tuple-element.98), channel_id=1, source_target_pairs={{0,8},{8,0},{16,24},{24,16},{1,9},{9,1},{17,25},{25,17},{2,10},{10... | collective-permute-start | bytes 221192 | tf_op jit(solution)/shard_map/ppermute | solution.py:572

commit v19 on v16

--- a/solution.py
+++ b/solution.py
@@ -135,6 +135,10 @@
     return sorted(range(1, count), key=lambda s: (-s.bit_length(), s))
 
 
+def farther_swaps(count):
+    return [s for s in range(2, count) if count != 4 or s != 3]
+
+
 def place_of(table, slot):
     return table[0, FACES * SLOTS + slot], table[0, FACES * SLOTS + SLOTS + slot]
 
@@ -168,8 +172,8 @@
         hit = (swap_column == float(shift)) & (rank_column == lane)
         row = jnp.sum(jnp.where(hit, block_column, 0.0), axis=0, keepdims=True)
         asked[shift : shift + 1, :] = row
-        if shift > 1:
-            farther[shift - 2][...] = jnp.broadcast_to(row, (8, 128))
+        if shift in farther_swaps(count):
+            farther[farther_swaps(count).index(shift)][...] = jnp.broadcast_to(row, (8, 128))
     at = FACES * SLOTS
     found = jnp.where(swap == 0, 0.0, 1.0 + position_of(swap))
     table[0:1, at : at + SLOTS] = found.astype(jnp.int32)
@@ -255,8 +259,9 @@
         first[row : row + upper.shape[0], :] = jnp.where(even, upper, lower)
         second[row : row + upper.shape[0], :] = jnp.where(even, lower, upper)
         row += upper.shape[0]
-    for out in (first, second):
-        out[row:, :] = jnp.broadcast_to(asked[1:2, :], (out.shape[0] - row, bz))
+    last = asked.shape[0] - 1
+    for out, ask in ((first, 1), (second, last)):
+        out[row:, :] = jnp.broadcast_to(asked[ask : ask + 1, :], (out.shape[0] - row, bz))
 
 
 def block_layout(cap):
@@ -548,7 +553,7 @@
             shape(sizes[0] * sizes[1], 3 * bx, 128),
             integers((table_sizes(count, plane_cap)[2], 128)),
             shape(count, 128),
-            *[shape(8, 128)] * (count - 2),
+            *[shape(8, 128)] * len(farther_swaps(count)),
         ],
         [
             pltpu.VMEM((1, SLOTS), jnp.int32),
@@ -577,7 +582,9 @@
             for swap, value in zip(swap_order(count), values)
         ]
 
-    farther = [swap_with(value, lambda i, s=s: i ^ s) for s, value in enumerate(farther, 2)]
+    farther = [
+        swap_with(value, lambda i, s=s: i ^ s) for s, value in zip(farther_swaps(count), farther)
+    ]
 
     phase_field = phase.reshape(SLOTS, TE, PLANE)
     solute_field = solute.reshape(SLOTS, TE, PLANE)
@@ -597,9 +604,14 @@
         functools.partial(layers_kernel, sizes), [VMEM] * 4 + [ANY] * len(farther), [layer, layer]
     )(enthalpy, conductivity, sides, asked, *farther)
     first = swap_with(first, lambda i: i ^ 1)
-    second = swap_with(second, lambda i: i if i in (0, others) else ((i + 1) ^ 1) - 1)
+    if count == 4:
+        second = swap_with(second, lambda i: i ^ 3)
+    else:
+        second = swap_with(second, lambda i: i if i in (0, others) else ((i + 1) ^ 1) - 1)
     row = 3 * by + 4
     request = [asked[0], first[row], *[value[0] for value in farther]]
+    if count == 4:
+        request.append(second[row])
     request = jnp.stack([value[:block_cap] for value in request]).astype(jnp.int32)
     _, deep = block_layout(block_cap)
     brick = shape(bx, by, bz)

time: 67.2 us -> 64.3 us (0.957)
  starting transfers between devices: 34.7 us -> 28.6 us
  waiting for transfers between devices: 15 us -> 17.8 us
    ppermute x19 -> x18, starting transfers between devices: 29.5 us -> 23.4 us  [swap_with(): return lax.ppermute(value, 'gx', [(i, partner(i)) for i in range(count)])]
    ppermute x19 -> x18, waiting for transfers between devices: 15 us -> 17.7 us  [swap_with(): return lax.ppermute(value, 'gx', [(i, partner(i)) for i in range(count)])]
    unnamed x28 -> x26, local copies, waits for them, and re-layouts: 2.63 us -> 2.63 us
  transfers between devices with their start and end apart: 20 -> 19, of which waited for: 12 -> 12; matrix products, arithmetic and copies ran while one was open for 0% -> 0% of each run, Pallas kernels for 8% -> 9%
where the time goes in v19:
time: 64.3 us; the launch traced here: 63.3 us
  starting transfers between devices  28.6 us (44%)
  waiting for transfers between devices  17.8 us (28%)
  Pallas kernels  13.4 us (21%)
  local copies, waits for them, and re-layouts  2.64 us (4%)
  between operations  0.83 us (1%)
    ppermute x18, starting transfers between devices, swap_with(): return lax.ppermute(value, 'gx', [(i, partner(i)) for i in range(count)])  23.4 us
    ppermute x18, waiting for transfers between devices, swap_with(): return lax.ppermute(value, 'gx', [(i, partner(i)) for i in range(count)])  17.7 us
    all_to_all x1, starting transfers between devices, local(): lax.all_to_all(sides, ('gy', 'gz'), split_axis=0, concat_axis=0, tiled=True)  5.18 us
    unnamed x26, local copies, waits for them, and re-layouts  2.63 us
    pallas_call x2, Pallas kernels, local(): call(middle_step_kernel, [SMEM] + [VMEM] * (6 + others), [field, field, *...  2.44 us
    pallas_call x1, Pallas kernels, local(): call(functools.partial(sides_kernel, sizes, plane_cap), [ANY] * 5, [shape...  2.21 us
    pallas_call x4, Pallas kernels, inner(): call(functools.partial(inner_kernel, bool(heat)), [VMEM] * (3 + len(heat)...  1.96 us
    pallas_call x1, Pallas kernels, local(): call(functools.partial(heat_kernel, block_cap, sizes), [SMEM] + [VMEM] *...  1.91 us
  transfers between devices with their start and end apart: 19, of which 12 were waited for; matrix products, arithmetic and copies ran while one was open for 0% of the time, Pallas kernels for 9%

profile of v19, /device:TPU:0, one launch (start us, length us, event | category | flops | bytes accessed | tf_op | source)
XLA Modules:
  0.0 63.3 jit_solution(2423533620334262194)
XLA Ops:
  0.6 0.0 copy-start.1
  0.6 2.2 %shard_map.130 = (f32[8,24,128]{2,1,0:T(8,128)}, s32[2,128]{1,0:T(2,128)}, f32[4,128]{1,0:T(4,128)}, f32[8,128]{1,0:T(8,128)}) custom-call(s32[1,16]{1,0:T(1,128)} %bitcast.15, s32[1,16]{1,0:T(1,128)} %bitcast.16, s32[6,1,16]{2,1,0:T(1,128)} %bitcast.14, f32[8,32,128]{2,1,0:T(8,128)} %h.3, f32[8,32,128]{2,1,0:T(8,128)} %k.3), custom_call_target="tpu_custom_call" | custom-call | tf_op jit(solution)/shard_map/pallas_call | solution.py:549
  2.9 0.0 copy-start.12
  2.9 5.2 %all-to-all-start = ((f32[8,24,128]{2,1,0:T(8,128)}), f32[8,24,128]{2,1,0:T(8,128)S(1)}, u32[]{:S(2)}, u32[]{:S(2)}) async-start(f32[8,24,128]{2,1,0:T(8,128)} %get-tuple-element.55), calls=%async_computation | async-start | bytes 196608 | tf_op jit(solution)/shard_map/all_to_all | solution.py:574
  8.1 0.0 copy-done.12
  8.1 2.7 %collective-permute-start = (f32[8,128]{1,0:T(8,128)S(1)}, f32[8,128]{1,0:T(8,128)S(1)}, u32[]{:S(2)}, u32[]{:S(2)}) collective-permute-start(f32[8,128]{1,0:T(8,128)S(1)} %copy-done.12), channel_id=1, source_target_pairs={{0,16},{8,24},{16,0},{24,8},{1,17},{9,25},{17,1},{25,9},{2,18},{10... | collective-permute-start | bytes 12296 | tf_op jit(solution)/shard_map/ppermute | solution.py:577
  10.7 0.7 %copy-done.11 = f32[4,128]{1,0:T(4,128)S(1)} copy-done((f32[4,128]{1,0:T(4,128)S(1)}, f32[4,128]{1,0:T(4,128)}, u32[]{:S(2)}) %copy-start.11) | copy-done | bytes 2072
  11.4 0.0 copy-done.10
  11.4 0.9 %copy-done.2 = f32[1,1,1,16,16,256]{5,4,3,2,1,0:T(8,128)S(1)} copy-done((f32[1,1,1,16,16,256]{5,4,3,2,1,0:T(8,128)S(1)}, f32[1,1,1,16,16,256]{5,4,3,2,1,0:T(8,128)}, u32[]{:S(2)}) %copy-start.2) | copy-done | bytes 262168
  12.4 0.9 %copy-done.7 = f32[1,1,1,16,16,256]{5,4,3,2,1,0:T(8,128)S(1)} copy-done((f32[1,1,1,16,16,256]{5,4,3,2,1,0:T(8,128)S(1)}, f32[1,1,1,16,16,256]{5,4,3,2,1,0:T(8,128)}, u32[]{:S(2)}) %copy-start.7) | copy-done | bytes 262168
  13.3 0.9 %shard_map.131 = (f32[32,16,128]{2,1,0:T(8,128)S(1)}, f32[256,128]{1,0:T(8,128)S(1)}, f32[4,128]{1,0:T(4,128)S(1)}, f32[144,128]{1,0:T(8,128)S(1)}, f32[144,128]{1,0:T(8,128)S(1)}, /*index=5*/f32[144,128]{1,0:T(8,128)S(1)}) custom-call(s32[2,128]{1,0:T(2,128)S(1)} %copy-done.10, f32[4,128]{1,0:T(4,128)S(1)} %copy-done.11, f32[16,16,256]{2,1,0:T(8,128)S(1)} %bitcast.9, ...), custom_call_target="tpu_custom_call" | custom-call | tf_op jit(solution)/shard_map/pallas_call | solution.py:594
  14.2 0.0 collective-permute-done.rest_0_
  14.2 0.0 all-to-all-done.got
  14.3 0.0 copy-done.6
  14.3 0.0 copy-start.8
  14.3 0.0 copy-start.3
  14.3 1.6 %collective-permute-start.1 = (f32[104,128]{1,0:T(8,128)S(1)}, f32[104,128]{1,0:T(8,128)S(1)}, u32[]{:S(2)}, u32[]{:S(2)}) collective-permute-start(f32[104,128]{1,0:T(8,128)S(1)} %get-tuple-element.57), channel_id=1, source_target_pairs={{0,8},{8,0},{16,24},{24,16},{1,9},{9,1},{17,25},{25,17},{2,10},{10... | collective-permute-start | bytes 159752 | tf_op jit(solution)/shard_map/ppermute | solution.py:577
  16.0 1.4 %collective-permute-start.2 = (f32[104,128]{1,0:T(8,128)S(1)}, f32[104,128]{1,0:T(8,128)S(1)}, u32[]{:S(2)}, u32[]{:S(2)}) collective-permute-start(f32[104,128]{1,0:T(8,128)S(1)} %get-tuple-element.58), channel_id=1, source_target_pairs={{0,24},{8,16},{16,8},{24,0},{1,25},{9,17},{17,9},{25,1},{2,26},{10... | collective-permute-start | bytes 159752 | tf_op jit(solution)/shard_map/ppermute | solution.py:577
  17.4 0.5 collective-permute-start.6
  17.9 2.6 %collective-permute-start.7 = (f32[144,128]{1,0:T(8,128)S(1)}, f32[144,128]{1,0:T(8,128)S(1)}, u32[]{:S(2)}, u32[]{:S(2)}) collective-permute-start(f32[144,128]{1,0:T(8,128)S(1)} %get-tuple-element.69), channel_id=1, source_target_pairs={{0,24},{8,16},{16,8},{24,0},{1,25},{9,17},{17,9},{25,1},{2,26},{10... | collective-permute-start | bytes 221192 | tf_op jit(solution)/shard_map/ppermute | solution.py:577
  20.5 0.4 collective-permute-start.8
  20.9 0.0 collective-permute-done.1.first
  20.9 1.7 %collective-permute-done.2.second = f32[104,128]{1,0:T(8,128)S(1)} collective-permute-done((f32[104,128]{1,0:T(8,128)S(1)}, f32[104,128]{1,0:T(8,128)S(1)}, u32[]{:S(2)}, u32[]{:S(2)}) %collective-permute-start.2) | collective-permute-done | bytes 53280 | tf_op jit(solution)/shard_map/ppermute | solution.py:577
  22.7 0.0 copy-start.4
  22.7 1.9 %shard_map.133 = (f32[8,32,128]{2,1,0:T(8,128)S(1)}, f32[32,128]{1,0:T(8,128)S(1)}, f32[32,128]{1,0:T(8,128)S(1)}, f32[32,128]{1,0:T(8,128)S(1)}, f32[32,128]{1,0:T(8,128)S(1)}) custom-call(s32[4,8]{1,0:T(4,128)S(1)} %maximum_convert_fusion.request, f32[8,32,128]{2,1,0:T(8,128)S(1)} %copy-done.5, f32[8,32,128]{2,1,0:T(8,128)S(1)} %copy-done.6, ...), custom_call_target="tpu_custom_call" | custom-call | tf_op jit(solution)/shard_map/pallas_call | solution.py:619
  24.6 2.3 %collective-permute-start.3 = (f32[32,128]{1,0:T(8,128)S(1)}, f32[32,128]{1,0:T(8,128)S(1)}, u32[]{:S(2)}, u32[]{:S(2)}) collective-permute-start(f32[32,128]{1,0:T(8,128)S(1)} %get-tuple-element.65), channel_id=1, source_target_pairs={{0,16},{8,24},{16,0},{24,8},{1,17},{9,25},{17,1},{25,9},{2,18},{10... | collective-permute-start | bytes 49160 | tf_op jit(solution)/shard_map/ppermute | solution.py:577
  26.9 0.3 collective-permute-start.4
  27.2 0.0 collective-permute-done.6.rest_4_
  27.2 1.0 %collective-permute-start.5 = (f32[32,128]{1,0:T(8,128)S(1)}, f32[32,128]{1,0:T(8,128)S(1)}, u32[]{:S(2)}, u32[]{:S(2)}) collective-permute-start(f32[32,128]{1,0:T(8,128)S(1)} %get-tuple-element.67), channel_id=1, source_target_pairs={{0,8},{8,0},{16,24},{24,16},{1,9},{9,1},{17,25},{25,17},{2,10},{10... | collective-permute-start | bytes 49160 | tf_op jit(solution)/shard_map/ppermute | solution.py:577
  28.2 0.0 copy-done.8
  28.2 0.0 copy-done.4
  28.2 0.5 shard_map.135
  28.7 0.0 collective-permute-done.7.rest_5_
  28.7 0.0 collective-permute-done.8.rest_6_
  28.7 0.6 collective-permute-done.3.rest_1_
  29.3 3.1 %collective-permute-done.4.rest_2_ = f32[32,128]{1,0:T(8,128)S(1)} collective-permute-done((f32[32,128]{1,0:T(8,128)S(1)}, f32[32,128]{1,0:T(8,128)S(1)}, u32[]{:S(2)}, u32[]{:S(2)}) %collective-permute-start.4) | collective-permute-done | bytes 16416 | tf_op jit(solution)/shard_map/ppermute | solution.py:577
  32.4 0.0 collective-permute-done.5.rest_3_
  32.4 0.0 copy-done.9
  32.4 1.7 %shard_map.136 = (f32[16,16,256]{2,1,0:T(8,128)S(1)}, f32[16,16,256]{2,1,0:T(8,128)S(1)}, f32[2,256,128]{2,1,0:T(8,128)S(1)}, f32[32,16,128]{2,1,0:T(8,128)S(1)}...) custom-call(s32[2,128]{1,0:T(2,128)S(1)} %copy-done.10, ...), custom_call_target="tpu_custom_call" | custom-call | tf_op jit(solution)/shard_map/pallas_call | solution.py:642
  34.1 0.8 %collective-permute-start.9 = (f32[144,128]{1,0:T(8,128)S(1)}, f32[144,128]{1,0:T(8,128)S(1)}, u32[]{:S(2)}, u32[]{:S(2)}) collective-permute-start(f32[144,128]{1,0:T(8,128)S(1)} %get-tuple-element.78), channel_id=1, source_target_pairs={{0,16},{8,24},{16,0},{24,8},{1,17},{9,25},{17,1},{25,9},{2,18},{10... | collective-permute-start | bytes 221192 | tf_op jit(solution)/shard_map/ppermute | solution.py:577
  34.9 1.4 %collective-permute-start.10 = (f32[144,128]{1,0:T(8,128)S(1)}, f32[144,128]{1,0:T(8,128)S(1)}, u32[]{:S(2)}, u32[]{:S(2)}) collective-permute-start(f32[144,128]{1,0:T(8,128)S(1)} %get-tuple-element.79), channel_id=1, source_target_pairs={{0,24},{8,16},{16,8},{24,0},{1,25},{9,17},{17,9},{25,1},{2,26},{10... | collective-permute-start | bytes 221192 | tf_op jit(solution)/shard_map/ppermute | solution.py:577
  36.3 1.4 %collective-permute-start.11 = (f32[144,128]{1,0:T(8,128)S(1)}, f32[144,128]{1,0:T(8,128)S(1)}, u32[]{:S(2)}, u32[]{:S(2)}) collective-permute-start(f32[144,128]{1,0:T(8,128)S(1)} %get-tuple-element.80), channel_id=1, source_target_pairs={{0,8},{8,0},{16,24},{24,16},{1,9},{9,1},{17,25},{25,17},{2,10},{10... | collective-permute-start | bytes 221192 | tf_op jit(solution)/shard_map/ppermute | solution.py:577
  37.6 0.5 shard_map.137
  38.1 1.3 %collective-permute-done.9.rest_0_ = f32[144,128]{1,0:T(8,128)S(1)} collective-permute-done((f32[144,128]{1,0:T(8,128)S(1)}, f32[144,128]{1,0:T(8,128)S(1)}, u32[]{:S(2)}, u32[]{:S(2)}) %collective-permute-start.9) | collective-permute-done | bytes 73760 | tf_op jit(solution)/shard_map/ppermute | solution.py:577
  39.4 1.8 %collective-permute-done.10.rest_1_ = f32[144,128]{1,0:T(8,128)S(1)} collective-permute-done((f32[144,128]{1,0:T(8,128)S(1)}, f32[144,128]{1,0:T(8,128)S(1)}, u32[]{:S(2)}, u32[]{:S(2)}) %collective-permute-start.10) | collective-permute-done | bytes 73760 | tf_op jit(solution)/shard_map/ppermute | solution.py:577
  41.2 0.2 collective-permute-done.11.rest_2_
  41.4 1.2 %shard_map.138 = (f32[16,16,256]{2,1,0:T(8,128)S(1)}, f32[16,16,256]{2,1,0:T(8,128)S(1)}, f32[32,16,128]{2,1,0:T(8,128)S(1)}, f32[256,128]{1,0:T(8,128)S(1)}, f3...) custom-call(s32[2,128]{1,0:T(2,128)S(1)} %copy-done.10, ...), custom_call_target="tpu_custom_call" | custom-call | tf_op jit(solution)/shard_map/pallas_call | solution.py:656
  42.7 2.0 %collective-permute-start.12 = (f32[144,128]{1,0:T(8,128)S(1)}, f32[144,128]{1,0:T(8,128)S(1)}, u32[]{:S(2)}, u32[]{:S(2)}) collective-permute-start(f32[144,128]{1,0:T(8,128)S(1)} %get-tuple-element.87), channel_id=1, source_target_pairs={{0,16},{8,24},{16,0},{24,8},{1,17},{9,25},{17,1},{25,9},{2,18},{10... | collective-permute-start | bytes 221192 | tf_op jit(solution)/shard_map/ppermute | solution.py:577
  44.6 1.5 %collective-permute-start.13 = (f32[144,128]{1,0:T(8,128)S(1)}, f32[144,128]{1,0:T(8,128)S(1)}, u32[]{:S(2)}, u32[]{:S(2)}) collective-permute-start(f32[144,128]{1,0:T(8,128)S(1)} %get-tuple-element.88), channel_id=1, source_target_pairs={{0,24},{8,16},{16,8},{24,0},{1,25},{9,17},{17,9},{25,1},{2,26},{10... | collective-permute-start | bytes 221192 | tf_op jit(solution)/shard_map/ppermute | solution.py:577
  46.1 0.1 collective-permute-start.14
  46.2 0.5 shard_map.139
  46.7 2.1 %collective-permute-done.12.rest_0_ = f32[144,128]{1,0:T(8,128)S(1)} collective-permute-done((f32[144,128]{1,0:T(8,128)S(1)}, f32[144,128]{1,0:T(8,128)S(1)}, u32[]{:S(2)}, u32[]{:S(2)}) %collective-permute-start.12) | collective-permute-done | bytes 73760 | tf_op jit(solution)/shard_map/ppermute | solution.py:577
  48.8 2.1 %collective-permute-done.13.rest_1_ = f32[144,128]{1,0:T(8,128)S(1)} collective-permute-done((f32[144,128]{1,0:T(8,128)S(1)}, f32[144,128]{1,0:T(8,128)S(1)}, u32[]{:S(2)}, u32[]{:S(2)}) %collective-permute-start.13) | collective-permute-done | bytes 73760 | tf_op jit(solution)/shard_map/ppermute | solution.py:577
  50.9 2.3 %collective-permute-done.14.rest_2_ = f32[144,128]{1,0:T(8,128)S(1)} collective-permute-done((f32[144,128]{1,0:T(8,128)S(1)}, f32[144,128]{1,0:T(8,128)S(1)}, u32[]{:S(2)}, u32[]{:S(2)}) %collective-permute-start.14) | collective-permute-done | bytes 73760 | tf_op jit(solution)/shard_map/ppermute | solution.py:577
  53.2 1.2 %shard_map.140 = (f32[16,16,256]{2,1,0:T(8,128)S(1)}, f32[16,16,256]{2,1,0:T(8,128)S(1)}, f32[32,16,128]{2,1,0:T(8,128)S(1)}, f32[256,128]{1,0:T(8,128)S(1)}, f3...) custom-call(s32[2,128]{1,0:T(2,128)S(1)} %copy-done.10, ...), custom_call_target="tpu_custom_call" | custom-call | tf_op jit(solution)/shard_map/pallas_call | solution.py:656
  54.4 0.3 collective-permute-start.15
  54.7 2.0 %collective-permute-start.16 = (f32[144,128]{1,0:T(8,128)S(1)}, f32[144,128]{1,0:T(8,128)S(1)}, u32[]{:S(2)}, u32[]{:S(2)}) collective-permute-start(f32[144,128]{1,0:T(8,128)S(1)} %get-tuple-element.97), channel_id=1, source_target_pairs={{0,24},{8,16},{16,8},{24,0},{1,25},{9,17},{17,9},{25,1},{2,26},{10... | collective-permute-start | bytes 221192 | tf_op jit(solution)/shard_map/ppermute | solution.py:577
  56.8 1.2 %collective-permute-start.17 = (f32[144,128]{1,0:T(8,128)S(1)}, f32[144,128]{1,0:T(8,128)S(1)}, u32[]{:S(2)}, u32[]{:S(2)}) collective-permute-start(f32[144,128]{1,0:T(8,128)S(1)} %get-tuple-element.98), channel_id=1, source_target_pairs={{0,8},{8,0},{16,24},{24,16},{1,9},{9,1},{17,25},{25,17},{2,10},{10... | collective-permute-start | bytes 221192 | tf_op jit(solution)/shard_map/ppermute | solution.py:577
  58.0 0.7 %shard_map.134 = f32[8,32,128]{2,1,0:T(8,128)} custom-call(f32[8,32,128]{2,1,0:T(8,128)S(1)} %get-tuple-element.59.value), custom_call_target="tpu_custom_call" | custom-call | tf_op jit(solution)/shard_map/pallas_call | solution.py:626
  58.6 0.5 shard_map.141
  59.2 0.6 %collective-permute-done.15.rest_0_ = f32[144,128]{1,0:T(8,128)S(1)} collective-permute-done((f32[144,128]{1,0:T(8,128)S(1)}, f32[144,128]{1,0:T(8,128)S(1)}, u32[]{:S(2)}, u32[]{:S(2)}) %collective-permute-start.15) | collective-permute-done | bytes 73760 | tf_op jit(solution)/shard_map/ppermute | solution.py:577
  59.8 1.1 %collective-permute-done.16.rest_1_ = f32[144,128]{1,0:T(8,128)S(1)} collective-permute-done((f32[144,128]{1,0:T(8,128)S(1)}, f32[144,128]{1,0:T(8,128)S(1)}, u32[]{:S(2)}, u32[]{:S(2)}) %collective-permute-start.16) | collective-permute-done | bytes 73760 | tf_op jit(solution)/shard_map/ppermute | solution.py:577
  60.9 0.7 %collective-permute-done.17.rest_2_ = f32[144,128]{1,0:T(8,128)S(1)} collective-permute-done((f32[144,128]{1,0:T(8,128)S(1)}, f32[144,128]{1,0:T(8,128)S(1)}, u32[]{:S(2)}, u32[]{:S(2)}) %collective-permute-start.17) | collective-permute-done | bytes 73760 | tf_op jit(solution)/shard_map/ppermute | solution.py:577
  61.7 1.6 %shard_map.142 = (f32[16,16,256]{2,1,0:T(8,128)}, f32[16,16,256]{2,1,0:T(8,128)}) custom-call(s32[2,128]{1,0:T(2,128)S(1)} %copy-done.10, f32[16,16,256]{2,1,0:T(8,128)S(1)} %get-tuple-element.92.phase, f32[16,16,256]{2,1,0:T(8,128)S(1)} %get-tuple-element.93.solute, f32[32,16,128]{2,1,0:T(8,128)S(1)} %get-tuple-element.94.own, ...), custom_call_target="tpu_custom_call" | custom-call | tf_op jit(solution)/shard_map/pallas_call | solution.py:665
  (18 shorter events, 0.1 us)
Async XLA Ops:
  0.6 10.1 %copy-start.1 = (bf16[512,256]{1,0:T(8,128)(2,1)S(1)}, bf16[512,256]{1,0:T(8,128)(2,1)}, u32[]{:S(2)}) copy-start(bf16[512,256]{1,0:T(8,128)(2,1)} %constant.8.clone.picks) | copy-start | bytes 786436
  2.9 5.2 %copy-start.12 = (f32[8,128]{1,0:T(8,128)S(1)}, f32[8,128]{1,0:T(8,128)}, u32[]{:S(2)}) copy-start(f32[8,128]{1,0:T(8,128)} %get-tuple-element.56) | copy-start | bytes 12292
  2.9 11.4 %all-to-all-start = ((f32[8,24,128]{2,1,0:T(8,128)}), f32[8,24,128]{2,1,0:T(8,128)S(1)}, u32[]{:S(2)}, u32[]{:S(2)}) async-start(f32[8,24,128]{2,1,0:T(8,128)} %get-tuple-element.55), calls=%async_computation | async-start | bytes 196608 | tf_op jit(solution)/shard_map/all_to_all | solution.py:574
  8.1 6.2 %collective-permute-start = (f32[8,128]{1,0:T(8,128)S(1)}, f32[8,128]{1,0:T(8,128)S(1)}, u32[]{:S(2)}, u32[]{:S(2)}) collective-permute-start(f32[8,128]{1,0:T(8,128)S(1)} %copy-done.12), channel_id=1, source_target_pairs={{0,16},{8,24},{16,0},{24,8},{1,17},{9,25},{17,1},{25,9},{2,18},{10... | collective-permute-start | bytes 12296 | tf_op jit(solution)/shard_map/ppermute | solution.py:577
  10.7 0.7 %copy-start.11 = (f32[4,128]{1,0:T(4,128)S(1)}, f32[4,128]{1,0:T(4,128)}, u32[]{:S(2)}) copy-start(f32[4,128]{1,0:T(4,128)} %get-tuple-element.53.asked) | copy-start | bytes 6148
  10.7 0.7 %copy-start.10 = (s32[2,128]{1,0:T(2,128)S(1)}, s32[2,128]{1,0:T(2,128)}, u32[]{:S(2)}) copy-start(s32[2,128]{1,0:T(2,128)} %get-tuple-element.52.table) | copy-start | bytes 3076
  11.4 0.9 %copy-start.2 = (f32[1,1,1,16,16,256]{5,4,3,2,1,0:T(8,128)S(1)}, f32[1,1,1,16,16,256]{5,4,3,2,1,0:T(8,128)}, u32[]{:S(2)}) copy-start(f32[1,1,1,16,16,256]{5,4,3,2,1,0:T(8,128)} %param.13) | copy-start | bytes 786436
  12.4 0.9 %copy-start.7 = (f32[1,1,1,16,16,256]{5,4,3,2,1,0:T(8,128)S(1)}, f32[1,1,1,16,16,256]{5,4,3,2,1,0:T(8,128)}, u32[]{:S(2)}) copy-start(f32[1,1,1,16,16,256]{5,4,3,2,1,0:T(8,128)} %param.14) | copy-start | bytes 786436
  13.3 1.0 %copy-start.5 = (f32[8,32,128]{2,1,0:T(8,128)S(1)}, f32[8,32,128]{2,1,0:T(8,128)}, u32[]{:S(2)}) copy-start(f32[8,32,128]{2,1,0:T(8,128)} %h.3) | copy-start | bytes 393220
  13.3 1.0 %copy-start.6 = (f32[8,32,128]{2,1,0:T(8,128)S(1)}, f32[8,32,128]{2,1,0:T(8,128)}, u32[]{:S(2)}) copy-start(f32[8,32,128]{2,1,0:T(8,128)} %k.3) | copy-start | bytes 393220
  14.3 13.9 %copy-start.8 = (f32[1,1,1,16,16,256]{5,4,3,2,1,0:T(8,128)S(1)}, f32[1,1,1,16,16,256]{5,4,3,2,1,0:T(8,128)}, u32[]{:S(2)}) copy-start(f32[1,1,1,16,16,256]{5,4,3,2,1,0:T(8,128)} %param.14) | copy-start | bytes 786436
  14.3 13.8 %copy-start.3 = (f32[1,1,1,16,16,256]{5,4,3,2,1,0:T(8,128)S(1)}, f32[1,1,1,16,16,256]{5,4,3,2,1,0:T(8,128)}, u32[]{:S(2)}) copy-start(f32[1,1,1,16,16,256]{5,4,3,2,1,0:T(8,128)} %param.13) | copy-start | bytes 786436
  14.3 6.6 %collective-permute-start.1 = (f32[104,128]{1,0:T(8,128)S(1)}, f32[104,128]{1,0:T(8,128)S(1)}, u32[]{:S(2)}, u32[]{:S(2)}) collective-permute-start(f32[104,128]{1,0:T(8,128)S(1)} %get-tuple-element.57), channel_id=1, source_target_pairs={{0,8},{8,0},{16,24},{24,16},{1,9},{9,1},{17,25},{25,17},{2,10},{10... | collective-permute-start | bytes 159752 | tf_op jit(solution)/shard_map/ppermute | solution.py:577
  16.0 6.7 %collective-permute-start.2 = (f32[104,128]{1,0:T(8,128)S(1)}, f32[104,128]{1,0:T(8,128)S(1)}, u32[]{:S(2)}, u32[]{:S(2)}) collective-permute-start(f32[104,128]{1,0:T(8,128)S(1)} %get-tuple-element.58), channel_id=1, source_target_pairs={{0,24},{8,16},{16,8},{24,0},{1,25},{9,17},{17,9},{25,1},{2,26},{10... | collective-permute-start | bytes 159752 | tf_op jit(solution)/shard_map/ppermute | solution.py:577
  17.4 9.7 %collective-permute-start.6 = (f32[144,128]{1,0:T(8,128)S(1)}, f32[144,128]{1,0:T(8,128)S(1)}, u32[]{:S(2)}, u32[]{:S(2)}) collective-permute-start(f32[144,128]{1,0:T(8,128)S(1)} %get-tuple-element.68), channel_id=1, source_target_pairs={{0,16},{8,24},{16,0},{24,8},{1,17},{9,25},{17,1},{25,9},{2,18},{10... | collective-permute-start | bytes 221192 | tf_op jit(solution)/shard_map/ppermute | solution.py:577
  17.9 10.8 %collective-permute-start.7 = (f32[144,128]{1,0:T(8,128)S(1)}, f32[144,128]{1,0:T(8,128)S(1)}, u32[]{:S(2)}, u32[]{:S(2)}) collective-permute-start(f32[144,128]{1,0:T(8,128)S(1)} %get-tuple-element.69), channel_id=1, source_target_pairs={{0,24},{8,16},{16,8},{24,0},{1,25},{9,17},{17,9},{25,1},{2,26},{10... | collective-permute-start | bytes 221192 | tf_op jit(solution)/shard_map/ppermute | solution.py:577
  20.5 8.2 %collective-permute-start.8 = (f32[144,128]{1,0:T(8,128)S(1)}, f32[144,128]{1,0:T(8,128)S(1)}, u32[]{:S(2)}, u32[]{:S(2)}) collective-permute-start(f32[144,128]{1,0:T(8,128)S(1)} %get-tuple-element.70), channel_id=1, source_target_pairs={{0,8},{8,0},{16,24},{24,16},{1,9},{9,1},{17,25},{25,17},{2,10},{10... | collective-permute-start | bytes 221192 | tf_op jit(solution)/shard_map/ppermute | solution.py:577
  22.7 5.5 %copy-start.4 = (bf16[256,256]{1,0:T(8,128)(2,1)S(1)}, bf16[256,256]{1,0:T(8,128)(2,1)}, u32[]{:S(2)}) copy-start(bf16[256,256]{1,0:T(8,128)(2,1)} %constant.9.clone.stencil) | copy-start | bytes 393220
  24.6 4.7 %collective-permute-start.3 = (f32[32,128]{1,0:T(8,128)S(1)}, f32[32,128]{1,0:T(8,128)S(1)}, u32[]{:S(2)}, u32[]{:S(2)}) collective-permute-start(f32[32,128]{1,0:T(8,128)S(1)} %get-tuple-element.65), channel_id=1, source_target_pairs={{0,16},{8,24},{16,0},{24,8},{1,17},{9,25},{17,1},{25,9},{2,18},{10... | collective-permute-start | bytes 49160 | tf_op jit(solution)/shard_map/ppermute | solution.py:577
  26.9 5.5 %collective-permute-start.4 = (f32[32,128]{1,0:T(8,128)S(1)}, f32[32,128]{1,0:T(8,128)S(1)}, u32[]{:S(2)}, u32[]{:S(2)}) collective-permute-start(f32[32,128]{1,0:T(8,128)S(1)} %get-tuple-element.66), channel_id=1, source_target_pairs={{0,24},{8,16},{16,8},{24,0},{1,25},{9,17},{17,9},{25,1},{2,26},{10... | collective-permute-start | bytes 49160 | tf_op jit(solution)/shard_map/ppermute | solution.py:577
  27.2 5.2 %copy-start = (bf16[256,512]{1,0:T(8,128)(2,1)S(1)}, bf16[256,512]{1,0:T(8,128)(2,1)}, u32[]{:S(2)}) copy-start(bf16[256,512]{1,0:T(8,128)(2,1)} %constant.10.clone.places) | copy-start | bytes 786436
  27.2 5.2 %copy-start.9 = (bf16[256,256]{1,0:T(8,128)(2,1)S(1)}, bf16[256,256]{1,0:T(8,128)(2,1)}, u32[]{:S(2)}) copy-start(bf16[256,256]{1,0:T(8,128)(2,1)} %constant.11.clone.spreads) | copy-start | bytes 393220
  27.2 5.2 %collective-permute-start.5 = (f32[32,128]{1,0:T(8,128)S(1)}, f32[32,128]{1,0:T(8,128)S(1)}, u32[]{:S(2)}, u32[]{:S(2)}) collective-permute-start(f32[32,128]{1,0:T(8,128)S(1)} %get-tuple-element.67), channel_id=1, source_target_pairs={{0,8},{8,0},{16,24},{24,16},{1,9},{9,1},{17,25},{25,17},{2,10},{10... | collective-permute-start | bytes 49160 | tf_op jit(solution)/shard_map/ppermute | solution.py:577
  34.1 5.3 %collective-permute-start.9 = (f32[144,128]{1,0:T(8,128)S(1)}, f32[144,128]{1,0:T(8,128)S(1)}, u32[]{:S(2)}, u32[]{:S(2)}) collective-permute-start(f32[144,128]{1,0:T(8,128)S(1)} %get-tuple-element.78), channel_id=1, source_target_pairs={{0,16},{8,24},{16,0},{24,8},{1,17},{9,25},{17,1},{25,9},{2,18},{10... | collective-permute-start | bytes 221192 | tf_op jit(solution)/shard_map/ppermute | solution.py:577
  34.9 6.3 %collective-permute-start.10 = (f32[144,128]{1,0:T(8,128)S(1)}, f32[144,128]{1,0:T(8,128)S(1)}, u32[]{:S(2)}, u32[]{:S(2)}) collective-permute-start(f32[144,128]{1,0:T(8,128)S(1)} %get-tuple-element.79), channel_id=1, source_target_pairs={{0,24},{8,16},{16,8},{24,0},{1,25},{9,17},{17,9},{25,1},{2,26},{10... | collective-permute-start | bytes 221192 | tf_op jit(solution)/shard_map/ppermute | solution.py:577
  36.3 5.2 %collective-permute-start.11 = (f32[144,128]{1,0:T(8,128)S(1)}, f32[144,128]{1,0:T(8,128)S(1)}, u32[]{:S(2)}, u32[]{:S(2)}) collective-permute-start(f32[144,128]{1,0:T(8,128)S(1)} %get-tuple-element.80), channel_id=1, source_target_pairs={{0,8},{8,0},{16,24},{24,16},{1,9},{9,1},{17,25},{25,17},{2,10},{10... | collective-permute-start | bytes 221192 | tf_op jit(solution)/shard_map/ppermute | solution.py:577
  42.7 6.1 %collective-permute-start.12 = (f32[144,128]{1,0:T(8,128)S(1)}, f32[144,128]{1,0:T(8,128)S(1)}, u32[]{:S(2)}, u32[]{:S(2)}) collective-permute-start(f32[144,128]{1,0:T(8,128)S(1)} %get-tuple-element.87), channel_id=1, source_target_pairs={{0,16},{8,24},{16,0},{24,8},{1,17},{9,25},{17,1},{25,9},{2,18},{10... | collective-permute-start | bytes 221192 | tf_op jit(solution)/shard_map/ppermute | solution.py:577
  44.6 6.3 %collective-permute-start.13 = (f32[144,128]{1,0:T(8,128)S(1)}, f32[144,128]{1,0:T(8,128)S(1)}, u32[]{:S(2)}, u32[]{:S(2)}) collective-permute-start(f32[144,128]{1,0:T(8,128)S(1)} %get-tuple-element.88), channel_id=1, source_target_pairs={{0,24},{8,16},{16,8},{24,0},{1,25},{9,17},{17,9},{25,1},{2,26},{10... | collective-permute-start | bytes 221192 | tf_op jit(solution)/shard_map/ppermute | solution.py:577
  46.1 7.1 %collective-permute-start.14 = (f32[144,128]{1,0:T(8,128)S(1)}, f32[144,128]{1,0:T(8,128)S(1)}, u32[]{:S(2)}, u32[]{:S(2)}) collective-permute-start(f32[144,128]{1,0:T(8,128)S(1)} %get-tuple-element.89), channel_id=1, source_target_pairs={{0,8},{8,0},{16,24},{24,16},{1,9},{9,1},{17,25},{25,17},{2,10},{10... | collective-permute-start | bytes 221192 | tf_op jit(solution)/shard_map/ppermute | solution.py:577
  54.4 5.4 %collective-permute-start.15 = (f32[144,128]{1,0:T(8,128)S(1)}, f32[144,128]{1,0:T(8,128)S(1)}, u32[]{:S(2)}, u32[]{:S(2)}) collective-permute-start(f32[144,128]{1,0:T(8,128)S(1)} %get-tuple-element.96), channel_id=1, source_target_pairs={{0,16},{8,24},{16,0},{24,8},{1,17},{9,25},{17,1},{25,9},{2,18},{10... | collective-permute-start | bytes 221192 | tf_op jit(solution)/shard_map/ppermute | solution.py:577
  54.7 6.2 %collective-permute-start.16 = (f32[144,128]{1,0:T(8,128)S(1)}, f32[144,128]{1,0:T(8,128)S(1)}, u32[]{:S(2)}, u32[]{:S(2)}) collective-permute-start(f32[144,128]{1,0:T(8,128)S(1)} %get-tuple-element.97), channel_id=1, source_target_pairs={{0,24},{8,16},{16,8},{24,0},{1,25},{9,17},{17,9},{25,1},{2,26},{10... | collective-permute-start | bytes 221192 | tf_op jit(solution)/shard_map/ppermute | solution.py:577
  56.8 4.9 %collective-permute-start.17 = (f32[144,128]{1,0:T(8,128)S(1)}, f32[144,128]{1,0:T(8,128)S(1)}, u32[]{:S(2)}, u32[]{:S(2)}) collective-permute-start(f32[144,128]{1,0:T(8,128)S(1)} %get-tuple-element.98), channel_id=1, source_target_pairs={{0,8},{8,0},{16,24},{24,16},{1,9},{9,1},{17,25},{25,17},{2,10},{10... | collective-permute-start | bytes 221192 | tf_op jit(solution)/shard_map/ppermute | solution.py:577

commit v20 on v14

--- a/solution.py
+++ b/solution.py
@@ -590,8 +590,8 @@
 
     layer = shape(3 * by + 8, bz)
     down, up = call(
-        functools.partial(layers_kernel, sizes), [VMEM] * 4 + [ANY] * len(farther), [layer, layer]
-    )(enthalpy, conductivity, sides, asked, *farther)
+        functools.partial(layers_kernel, sizes), [VMEM] * 4, [layer, layer]
+    )(enthalpy, conductivity, sides, asked)
     from_low, from_high = pass_on(up, 1), pass_on(down, others)
     row = 3 * by + 4
     request = [asked[0], from_low[row], *[value[0] for value in farther], from_high[row]]

time: 62.3 us -> 65.5 us (1.051)
  waiting for transfers between devices: 14.4 us -> 16.4 us
  starting transfers between devices: 30.7 us -> 32 us
    ppermute x12, starting transfers between devices: 14.3 us -> 16.5 us  [swap_all(): lax.ppermute(value, 'gx', [(i, i ^ swap) for i in range(count)])]
    all_to_all x1, waiting for transfers between devices: 0.01 us -> 1.68 us  [local(): lax.all_to_all(sides, ('gy', 'gz'), split_axis=0, concat_axis=0, tiled=True)]
    ppermute x12, waiting for transfers between devices: 12 us -> 13.5 us  [swap_all(): lax.ppermute(value, 'gx', [(i, i ^ swap) for i in range(count)])]
    ppermute x6, waiting for transfers between devices: 2.34 us -> 1.21 us  [pass_on(): lax.ppermute(value, 'gx', [(i, (i + shift) % count) for i in range(count)])]
    ppermute x6, starting transfers between devices: 11.2 us -> 10.3 us  [pass_on(): lax.ppermute(value, 'gx', [(i, (i + shift) % count) for i in range(count)])]
  transfers between devices with their start and end apart: 19 -> 19, of which waited for: 9 -> 12; matrix products, arithmetic and copies ran while one was open for 0% -> 0% of each run, Pallas kernels for 9% -> 8%
where the time goes in v20:
time: 65.5 us; the launch traced here: 65.2 us
  starting transfers between devices  32 us (49%)
  waiting for transfers between devices  16.4 us (25%)
  Pallas kernels  13.4 us (20%)
  local copies, waits for them, and re-layouts  2.62 us (4%)
  between operations  0.85 us (1%)
    ppermute x12, starting transfers between devices, swap_all(): lax.ppermute(value, 'gx', [(i, i ^ swap) for i in range(count)])  16.5 us
    ppermute x12, waiting for transfers between devices, swap_all(): lax.ppermute(value, 'gx', [(i, i ^ swap) for i in range(count)])  13.5 us
    ppermute x6, starting transfers between devices, pass_on(): lax.ppermute(value, 'gx', [(i, (i + shift) % count) for i in range(count)])  10.3 us
    all_to_all x1, starting transfers between devices, local(): lax.all_to_all(sides, ('gy', 'gz'), split_axis=0, concat_axis=0, tiled=True)  5.18 us
    unnamed x26, local copies, waits for them, and re-layouts  2.61 us
    pallas_call x2, Pallas kernels, local(): call(middle_step_kernel, [SMEM] + [VMEM] * (6 + others), [field, field, *...  2.44 us
    pallas_call x1, Pallas kernels, local(): call(functools.partial(sides_kernel, sizes, plane_cap), [ANY] * 5, [shape...  2.21 us
    pallas_call x4, Pallas kernels, inner(): call(functools.partial(inner_kernel, bool(heat)), [VMEM] * (3 + len(heat)...  1.96 us
  transfers between devices with their start and end apart: 19, of which 12 were waited for; matrix products, arithmetic and copies ran while one was open for 0% of the time, Pallas kernels for 8%

profile of v20, /device:TPU:0, one launch (start us, length us, event | category | flops | bytes accessed | tf_op | source)
XLA Modules:
  0.0 65.2 jit_solution(5346288180015386682)
XLA Ops:
  0.6 0.0 copy-start.1
  0.6 2.2 %shard_map.130 = (f32[8,24,128]{2,1,0:T(8,128)}, s32[2,128]{1,0:T(2,128)}, f32[4,128]{1,0:T(4,128)}, f32[8,128]{1,0:T(8,128)}) custom-call(s32[1,16]{1,0:T(1,128)} %bitcast.15, s32[1,16]{1,0:T(1,128)} %bitcast.16, s32[6,1,16]{2,1,0:T(1,128)} %bitcast.14, f32[8,32,128]{2,1,0:T(8,128)} %h.3, f32[8,32,128]{2,1,0:T(8,128)} %k.3), custom_call_target="tpu_custom_call" | custom-call | tf_op jit(solution)/shard_map/pallas_call | solution.py:537
  2.9 5.2 %all-to-all-start = ((f32[8,24,128]{2,1,0:T(8,128)}), f32[8,24,128]{2,1,0:T(8,128)S(1)}, u32[]{:S(2)}, u32[]{:S(2)}) async-start(f32[8,24,128]{2,1,0:T(8,128)} %get-tuple-element.55), calls=%async_computation | async-start | bytes 196608 | tf_op jit(solution)/shard_map/all_to_all | solution.py:562
  8.0 0.0 copy-start.10
  8.1 0.0 copy-done.1
  8.1 0.7 %copy-done.11 = f32[4,128]{1,0:T(4,128)S(1)} copy-done((f32[4,128]{1,0:T(4,128)S(1)}, f32[4,128]{1,0:T(4,128)}, u32[]{:S(2)}) %copy-start.11) | copy-done | bytes 2072
  8.7 0.0 copy-done.10
  8.7 0.9 %copy-done.2 = f32[1,1,1,16,16,256]{5,4,3,2,1,0:T(8,128)S(1)} copy-done((f32[1,1,1,16,16,256]{5,4,3,2,1,0:T(8,128)S(1)}, f32[1,1,1,16,16,256]{5,4,3,2,1,0:T(8,128)}, u32[]{:S(2)}) %copy-start.2) | copy-done | bytes 262168
  9.7 0.9 %copy-done.7 = f32[1,1,1,16,16,256]{5,4,3,2,1,0:T(8,128)S(1)} copy-done((f32[1,1,1,16,16,256]{5,4,3,2,1,0:T(8,128)S(1)}, f32[1,1,1,16,16,256]{5,4,3,2,1,0:T(8,128)}, u32[]{:S(2)}) %copy-start.7) | copy-done | bytes 262168
  10.6 0.9 %shard_map.131 = (f32[32,16,128]{2,1,0:T(8,128)S(1)}, f32[256,128]{1,0:T(8,128)S(1)}, f32[4,128]{1,0:T(4,128)S(1)}, f32[144,128]{1,0:T(8,128)S(1)}, f32[144,128]{1,0:T(8,128)S(1)}, /*index=5*/f32[144,128]{1,0:T(8,128)S(1)}) custom-call(s32[2,128]{1,0:T(2,128)S(1)} %copy-done.10, f32[4,128]{1,0:T(4,128)S(1)} %copy-done.11, f32[16,16,256]{2,1,0:T(8,128)S(1)} %bitcast.9, ...), custom_call_target="tpu_custom_call" | custom-call | tf_op jit(solution)/shard_map/pallas_call | solution.py:583
  11.6 1.7 %all-to-all-done.got = f32[8,24,128]{2,1,0:T(8,128)S(1)} async-done(((f32[8,24,128]{2,1,0:T(8,128)}), f32[8,24,128]{2,1,0:T(8,128)S(1)}, u32[]{:S(2)}, u32[]{:S(2)}) %all-to-all-start) | async-done | bytes 98336 | tf_op jit(solution)/shard_map/all_to_all | solution.py:562
  13.2 0.0 copy-done.5
  13.2 0.0 copy-done.6
  13.3 0.0 copy-start.3
  13.3 1.6 %collective-permute-start = (f32[104,128]{1,0:T(8,128)S(1)}, f32[104,128]{1,0:T(8,128)S(1)}, u32[]{:S(2)}, u32[]{:S(2)}) collective-permute-start(f32[104,128]{1,0:T(8,128)S(1)} %get-tuple-element.56), channel_id=1, source_target_pairs={{0,8},{8,16},{16,24},{24,0},{1,9},{9,17},{17,25},{25,1},{2,10},{10... | collective-permute-start | bytes 159752 | tf_op jit(solution)/shard_map/ppermute | solution.py:565
  14.9 2.2 %collective-permute-start.2 = (f32[104,128]{1,0:T(8,128)S(1)}, f32[104,128]{1,0:T(8,128)S(1)}, u32[]{:S(2)}, u32[]{:S(2)}) collective-permute-start(f32[104,128]{1,0:T(8,128)S(1)} %get-tuple-element.58), channel_id=1, source_target_pairs={{0,24},{8,0},{16,8},{24,16},{1,25},{9,1},{17,9},{25,17},{2,26},{10... | collective-permute-start | bytes 159752 | tf_op jit(solution)/shard_map/ppermute | solution.py:565
  17.2 0.0 copy-done.12
  17.2 0.8 %collective-permute-start.1 = (f32[8,128]{1,0:T(8,128)S(1)}, f32[8,128]{1,0:T(8,128)S(1)}, u32[]{:S(2)}, u32[]{:S(2)}) collective-permute-start(f32[8,128]{1,0:T(8,128)S(1)} %copy-done.12), channel_id=1, source_target_pairs={{0,16},{8,24},{16,0},{24,8},{1,17},{9,25},{17,1},{25,9},{2,18},{10... | collective-permute-start | bytes 12296 | tf_op jit(solution)/shard_map/ppermute | solution.py:565
  18.0 2.1 %collective-permute-start.6 = (f32[144,128]{1,0:T(8,128)S(1)}, f32[144,128]{1,0:T(8,128)S(1)}, u32[]{:S(2)}, u32[]{:S(2)}) collective-permute-start(f32[144,128]{1,0:T(8,128)S(1)} %get-tuple-element.68), channel_id=1, source_target_pairs={{0,16},{8,24},{16,0},{24,8},{1,17},{9,25},{17,1},{25,9},{2,18},{10... | collective-permute-start | bytes 221192 | tf_op jit(solution)/shard_map/ppermute | solution.py:572
  20.1 1.8 %collective-permute-start.7 = (f32[144,128]{1,0:T(8,128)S(1)}, f32[144,128]{1,0:T(8,128)S(1)}, u32[]{:S(2)}, u32[]{:S(2)}) collective-permute-start(f32[144,128]{1,0:T(8,128)S(1)} %get-tuple-element.69), channel_id=1, source_target_pairs={{0,24},{8,16},{16,8},{24,0},{1,25},{9,17},{17,9},{25,1},{2,26},{10... | collective-permute-start | bytes 221192 | tf_op jit(solution)/shard_map/ppermute | solution.py:572
  21.9 0.3 collective-permute-done.1
  22.2 0.0 collective-permute-start.8
  22.2 0.0 collective-permute-done.low
  22.2 0.0 collective-permute-done.2.high
  22.3 0.0 copy-start.4
  22.3 1.9 %shard_map.133 = (f32[8,32,128]{2,1,0:T(8,128)S(1)}, f32[32,128]{1,0:T(8,128)S(1)}, f32[32,128]{1,0:T(8,128)S(1)}, f32[32,128]{1,0:T(8,128)S(1)}, f32[32,128]{1,0:T(8,128)S(1)}) custom-call(s32[4,8]{1,0:T(4,128)S(1)} %maximum_convert_fusion.request, f32[8,32,128]{2,1,0:T(8,128)S(1)} %copy-done.5, f32[8,32,128]{2,1,0:T(8,128)S(1)} %copy-done.6, ...), custom_call_target="tpu_custom_call" | custom-call | tf_op jit(solution)/shard_map/pallas_call | solution.py:602
  24.2 2.1 %collective-permute-start.3 = (f32[32,128]{1,0:T(8,128)S(1)}, f32[32,128]{1,0:T(8,128)S(1)}, u32[]{:S(2)}, u32[]{:S(2)}) collective-permute-start(f32[32,128]{1,0:T(8,128)S(1)} %get-tuple-element.65), channel_id=1, source_target_pairs={{0,8},{8,16},{16,24},{24,0},{1,9},{9,17},{17,25},{25,1},{2,10},{10... | collective-permute-start | bytes 49160 | tf_op jit(solution)/shard_map/ppermute | solution.py:565
  26.2 0.7 %collective-permute-start.4 = (f32[32,128]{1,0:T(8,128)S(1)}, f32[32,128]{1,0:T(8,128)S(1)}, u32[]{:S(2)}, u32[]{:S(2)}) collective-permute-start(f32[32,128]{1,0:T(8,128)S(1)} %get-tuple-element.66), channel_id=1, source_target_pairs={{0,16},{8,24},{16,0},{24,8},{1,17},{9,25},{17,1},{25,9},{2,18},{10... | collective-permute-start | bytes 49160 | tf_op jit(solution)/shard_map/ppermute | solution.py:565
  26.9 0.0 collective-permute-done.6.rest_4_
  26.9 2.8 %collective-permute-start.5 = (f32[32,128]{1,0:T(8,128)S(1)}, f32[32,128]{1,0:T(8,128)S(1)}, u32[]{:S(2)}, u32[]{:S(2)}) collective-permute-start(f32[32,128]{1,0:T(8,128)S(1)} %get-tuple-element.67), channel_id=1, source_target_pairs={{0,24},{8,0},{16,8},{24,16},{1,25},{9,1},{17,9},{25,17},{2,26},{10... | collective-permute-start | bytes 49160 | tf_op jit(solution)/shard_map/ppermute | solution.py:565
  29.8 0.0 copy-done.8
  29.8 0.0 copy-done.3
  29.8 0.5 shard_map.135
  30.3 0.0 collective-permute-done.7.rest_5_
  30.3 0.0 collective-permute-done.8.rest_6_
  30.3 0.0 collective-permute-done.3.rest_1_
  30.3 0.6 collective-permute-done.4.rest_2_
  30.9 0.3 collective-permute-done.5.rest_3_
  31.2 1.7 %shard_map.136 = (f32[16,16,256]{2,1,0:T(8,128)S(1)}, f32[16,16,256]{2,1,0:T(8,128)S(1)}, f32[2,256,128]{2,1,0:T(8,128)S(1)}, f32[32,16,128]{2,1,0:T(8,128)S(1)}...) custom-call(s32[2,128]{1,0:T(2,128)S(1)} %copy-done.10, ...), custom_call_target="tpu_custom_call" | custom-call | tf_op jit(solution)/shard_map/pallas_call | solution.py:625
  32.9 1.8 %collective-permute-start.9 = (f32[144,128]{1,0:T(8,128)S(1)}, f32[144,128]{1,0:T(8,128)S(1)}, u32[]{:S(2)}, u32[]{:S(2)}) collective-permute-start(f32[144,128]{1,0:T(8,128)S(1)} %get-tuple-element.78), channel_id=1, source_target_pairs={{0,16},{8,24},{16,0},{24,8},{1,17},{9,25},{17,1},{25,9},{2,18},{10... | collective-permute-start | bytes 221192 | tf_op jit(solution)/shard_map/ppermute | solution.py:572
  34.7 2.6 %collective-permute-start.10 = (f32[144,128]{1,0:T(8,128)S(1)}, f32[144,128]{1,0:T(8,128)S(1)}, u32[]{:S(2)}, u32[]{:S(2)}) collective-permute-start(f32[144,128]{1,0:T(8,128)S(1)} %get-tuple-element.79), channel_id=1, source_target_pairs={{0,24},{8,16},{16,8},{24,0},{1,25},{9,17},{17,9},{25,1},{2,26},{10... | collective-permute-start | bytes 221192 | tf_op jit(solution)/shard_map/ppermute | solution.py:572
  37.3 0.5 collective-permute-start.11
  37.8 0.5 shard_map.137
  38.3 0.0 collective-permute-done.9.rest_0_
  38.3 2.5 %collective-permute-done.10.rest_1_ = f32[144,128]{1,0:T(8,128)S(1)} collective-permute-done((f32[144,128]{1,0:T(8,128)S(1)}, f32[144,128]{1,0:T(8,128)S(1)}, u32[]{:S(2)}, u32[]{:S(2)}) %collective-permute-start.10) | collective-permute-done | bytes 73760 | tf_op jit(solution)/shard_map/ppermute | solution.py:572
  40.8 1.1 %collective-permute-done.11.rest_2_ = f32[144,128]{1,0:T(8,128)S(1)} collective-permute-done((f32[144,128]{1,0:T(8,128)S(1)}, f32[144,128]{1,0:T(8,128)S(1)}, u32[]{:S(2)}, u32[]{:S(2)}) %collective-permute-start.11) | collective-permute-done | bytes 73760 | tf_op jit(solution)/shard_map/ppermute | solution.py:572
  41.9 1.2 %shard_map.138 = (f32[16,16,256]{2,1,0:T(8,128)S(1)}, f32[16,16,256]{2,1,0:T(8,128)S(1)}, f32[32,16,128]{2,1,0:T(8,128)S(1)}, f32[256,128]{1,0:T(8,128)S(1)}, f3...) custom-call(s32[2,128]{1,0:T(2,128)S(1)} %copy-done.10, ...), custom_call_target="tpu_custom_call" | custom-call | tf_op jit(solution)/shard_map/pallas_call | solution.py:639
  43.2 3.3 %collective-permute-start.12 = (f32[144,128]{1,0:T(8,128)S(1)}, f32[144,128]{1,0:T(8,128)S(1)}, u32[]{:S(2)}, u32[]{:S(2)}) collective-permute-start(f32[144,128]{1,0:T(8,128)S(1)} %get-tuple-element.87), channel_id=1, source_target_pairs={{0,16},{8,24},{16,0},{24,8},{1,17},{9,25},{17,1},{25,9},{2,18},{10... | collective-permute-start | bytes 221192 | tf_op jit(solution)/shard_map/ppermute | solution.py:572
  46.5 0.9 %collective-permute-start.13 = (f32[144,128]{1,0:T(8,128)S(1)}, f32[144,128]{1,0:T(8,128)S(1)}, u32[]{:S(2)}, u32[]{:S(2)}) collective-permute-start(f32[144,128]{1,0:T(8,128)S(1)} %get-tuple-element.88), channel_id=1, source_target_pairs={{0,24},{8,16},{16,8},{24,0},{1,25},{9,17},{17,9},{25,1},{2,26},{10... | collective-permute-start | bytes 221192 | tf_op jit(solution)/shard_map/ppermute | solution.py:572
  47.3 0.0 collective-permute-start.14
  47.3 0.5 shard_map.139
  47.8 1.3 %collective-permute-done.12.rest_0_ = f32[144,128]{1,0:T(8,128)S(1)} collective-permute-done((f32[144,128]{1,0:T(8,128)S(1)}, f32[144,128]{1,0:T(8,128)S(1)}, u32[]{:S(2)}, u32[]{:S(2)}) %collective-permute-start.12) | collective-permute-done | bytes 73760 | tf_op jit(solution)/shard_map/ppermute | solution.py:572
  49.2 4.3 %collective-permute-done.13.rest_1_ = f32[144,128]{1,0:T(8,128)S(1)} collective-permute-done((f32[144,128]{1,0:T(8,128)S(1)}, f32[144,128]{1,0:T(8,128)S(1)}, u32[]{:S(2)}, u32[]{:S(2)}) %collective-permute-start.13) | collective-permute-done | bytes 73760 | tf_op jit(solution)/shard_map/ppermute | solution.py:572
  53.5 1.1 %collective-permute-done.14.rest_2_ = f32[144,128]{1,0:T(8,128)S(1)} collective-permute-done((f32[144,128]{1,0:T(8,128)S(1)}, f32[144,128]{1,0:T(8,128)S(1)}, u32[]{:S(2)}, u32[]{:S(2)}) %collective-permute-start.14) | collective-permute-done | bytes 73760 | tf_op jit(solution)/shard_map/ppermute | solution.py:572
  54.6 1.2 %shard_map.140 = (f32[16,16,256]{2,1,0:T(8,128)S(1)}, f32[16,16,256]{2,1,0:T(8,128)S(1)}, f32[32,16,128]{2,1,0:T(8,128)S(1)}, f32[256,128]{1,0:T(8,128)S(1)}, f3...) custom-call(s32[2,128]{1,0:T(2,128)S(1)} %copy-done.10, ...), custom_call_target="tpu_custom_call" | custom-call | tf_op jit(solution)/shard_map/pallas_call | solution.py:639
  55.8 0.8 %collective-permute-start.15 = (f32[144,128]{1,0:T(8,128)S(1)}, f32[144,128]{1,0:T(8,128)S(1)}, u32[]{:S(2)}, u32[]{:S(2)}) collective-permute-start(f32[144,128]{1,0:T(8,128)S(1)} %get-tuple-element.96), channel_id=1, source_target_pairs={{0,16},{8,24},{16,0},{24,8},{1,17},{9,25},{17,1},{25,9},{2,18},{10... | collective-permute-start | bytes 221192 | tf_op jit(solution)/shard_map/ppermute | solution.py:572
  56.6 1.9 %collective-permute-start.16 = (f32[144,128]{1,0:T(8,128)S(1)}, f32[144,128]{1,0:T(8,128)S(1)}, u32[]{:S(2)}, u32[]{:S(2)}) collective-permute-start(f32[144,128]{1,0:T(8,128)S(1)} %get-tuple-element.97), channel_id=1, source_target_pairs={{0,24},{8,16},{16,8},{24,0},{1,25},{9,17},{17,9},{25,1},{2,26},{10... | collective-permute-start | bytes 221192 | tf_op jit(solution)/shard_map/ppermute | solution.py:572
  58.5 0.9 %collective-permute-start.17 = (f32[144,128]{1,0:T(8,128)S(1)}, f32[144,128]{1,0:T(8,128)S(1)}, u32[]{:S(2)}, u32[]{:S(2)}) collective-permute-start(f32[144,128]{1,0:T(8,128)S(1)} %get-tuple-element.98), channel_id=1, source_target_pairs={{0,8},{8,0},{16,24},{24,16},{1,9},{9,1},{17,25},{25,17},{2,10},{10... | collective-permute-start | bytes 221192 | tf_op jit(solution)/shard_map/ppermute | solution.py:572
  59.4 0.7 %shard_map.134 = f32[8,32,128]{2,1,0:T(8,128)} custom-call(f32[8,32,128]{2,1,0:T(8,128)S(1)} %get-tuple-element.59.value), custom_call_target="tpu_custom_call" | custom-call | tf_op jit(solution)/shard_map/pallas_call | solution.py:609
  60.0 0.5 shard_map.141
  60.5 1.0 %collective-permute-done.15.rest_0_ = f32[144,128]{1,0:T(8,128)S(1)} collective-permute-done((f32[144,128]{1,0:T(8,128)S(1)}, f32[144,128]{1,0:T(8,128)S(1)}, u32[]{:S(2)}, u32[]{:S(2)}) %collective-permute-start.15) | collective-permute-done | bytes 73760 | tf_op jit(solution)/shard_map/ppermute | solution.py:572
  61.6 1.4 %collective-permute-done.16.rest_1_ = f32[144,128]{1,0:T(8,128)S(1)} collective-permute-done((f32[144,128]{1,0:T(8,128)S(1)}, f32[144,128]{1,0:T(8,128)S(1)}, u32[]{:S(2)}, u32[]{:S(2)}) %collective-permute-start.16) | collective-permute-done | bytes 73760 | tf_op jit(solution)/shard_map/ppermute | solution.py:572
  63.0 0.6 collective-permute-done.17.rest_2_
  63.6 1.6 %shard_map.142 = (f32[16,16,256]{2,1,0:T(8,128)}, f32[16,16,256]{2,1,0:T(8,128)}) custom-call(s32[2,128]{1,0:T(2,128)S(1)} %copy-done.10, f32[16,16,256]{2,1,0:T(8,128)S(1)} %get-tuple-element.92.phase, f32[16,16,256]{2,1,0:T(8,128)S(1)} %get-tuple-element.93.solute, f32[32,16,128]{2,1,0:T(8,128)S(1)} %get-tuple-element.94.own, ...), custom_call_target="tpu_custom_call" | custom-call | tf_op jit(solution)/shard_map/pallas_call | solution.py:648
  (18 shorter events, 0.1 us)
Async XLA Ops:
  0.6 7.4 %copy-start.1 = (bf16[512,256]{1,0:T(8,128)(2,1)S(1)}, bf16[512,256]{1,0:T(8,128)(2,1)}, u32[]{:S(2)}) copy-start(bf16[512,256]{1,0:T(8,128)(2,1)} %constant.8.clone.picks) | copy-start | bytes 786436
  2.9 10.4 %all-to-all-start = ((f32[8,24,128]{2,1,0:T(8,128)}), f32[8,24,128]{2,1,0:T(8,128)S(1)}, u32[]{:S(2)}, u32[]{:S(2)}) async-start(f32[8,24,128]{2,1,0:T(8,128)} %get-tuple-element.55), calls=%async_computation | async-start | bytes 196608 | tf_op jit(solution)/shard_map/all_to_all | solution.py:562
  8.0 0.7 %copy-start.11 = (f32[4,128]{1,0:T(4,128)S(1)}, f32[4,128]{1,0:T(4,128)}, u32[]{:S(2)}) copy-start(f32[4,128]{1,0:T(4,128)} %get-tuple-element.53.asked) | copy-start | bytes 6148
  8.0 0.7 %copy-start.10 = (s32[2,128]{1,0:T(2,128)S(1)}, s32[2,128]{1,0:T(2,128)}, u32[]{:S(2)}) copy-start(s32[2,128]{1,0:T(2,128)} %get-tuple-element.52.table) | copy-start | bytes 3076
  8.7 0.9 %copy-start.2 = (f32[1,1,1,16,16,256]{5,4,3,2,1,0:T(8,128)S(1)}, f32[1,1,1,16,16,256]{5,4,3,2,1,0:T(8,128)}, u32[]{:S(2)}) copy-start(f32[1,1,1,16,16,256]{5,4,3,2,1,0:T(8,128)} %param.13) | copy-start | bytes 786436
  9.7 0.9 %copy-start.7 = (f32[1,1,1,16,16,256]{5,4,3,2,1,0:T(8,128)S(1)}, f32[1,1,1,16,16,256]{5,4,3,2,1,0:T(8,128)}, u32[]{:S(2)}) copy-start(f32[1,1,1,16,16,256]{5,4,3,2,1,0:T(8,128)} %param.14) | copy-start | bytes 786436
  10.6 2.6 %copy-start.5 = (f32[8,32,128]{2,1,0:T(8,128)S(1)}, f32[8,32,128]{2,1,0:T(8,128)}, u32[]{:S(2)}) copy-start(f32[8,32,128]{2,1,0:T(8,128)} %h.3) | copy-start | bytes 393220
  10.6 2.6 %copy-start.6 = (f32[8,32,128]{2,1,0:T(8,128)S(1)}, f32[8,32,128]{2,1,0:T(8,128)}, u32[]{:S(2)}) copy-start(f32[8,32,128]{2,1,0:T(8,128)} %k.3) | copy-start | bytes 393220
  13.2 3.9 %copy-start.12 = (f32[8,128]{1,0:T(8,128)S(1)}, f32[8,128]{1,0:T(8,128)}, u32[]{:S(2)}) copy-start(f32[8,128]{1,0:T(8,128)} %get-tuple-element.57) | copy-start | bytes 12292
  13.2 16.5 %copy-start.8 = (f32[1,1,1,16,16,256]{5,4,3,2,1,0:T(8,128)S(1)}, f32[1,1,1,16,16,256]{5,4,3,2,1,0:T(8,128)}, u32[]{:S(2)}) copy-start(f32[1,1,1,16,16,256]{5,4,3,2,1,0:T(8,128)} %param.14) | copy-start | bytes 786436
  13.3 16.5 %copy-start.3 = (f32[1,1,1,16,16,256]{5,4,3,2,1,0:T(8,128)S(1)}, f32[1,1,1,16,16,256]{5,4,3,2,1,0:T(8,128)}, u32[]{:S(2)}) copy-start(f32[1,1,1,16,16,256]{5,4,3,2,1,0:T(8,128)} %param.13) | copy-start | bytes 786436
  13.3 8.9 %collective-permute-start = (f32[104,128]{1,0:T(8,128)S(1)}, f32[104,128]{1,0:T(8,128)S(1)}, u32[]{:S(2)}, u32[]{:S(2)}) collective-permute-start(f32[104,128]{1,0:T(8,128)S(1)} %get-tuple-element.56), channel_id=1, source_target_pairs={{0,8},{8,16},{16,24},{24,0},{1,9},{9,17},{17,25},{25,1},{2,10},{10... | collective-permute-start | bytes 159752 | tf_op jit(solution)/shard_map/ppermute | solution.py:565
  14.9 7.3 %collective-permute-start.2 = (f32[104,128]{1,0:T(8,128)S(1)}, f32[104,128]{1,0:T(8,128)S(1)}, u32[]{:S(2)}, u32[]{:S(2)}) collective-permute-start(f32[104,128]{1,0:T(8,128)S(1)} %get-tuple-element.58), channel_id=1, source_target_pairs={{0,24},{8,0},{16,8},{24,16},{1,25},{9,1},{17,9},{25,17},{2,26},{10... | collective-permute-start | bytes 159752 | tf_op jit(solution)/shard_map/ppermute | solution.py:565
  17.2 5.0 %collective-permute-start.1 = (f32[8,128]{1,0:T(8,128)S(1)}, f32[8,128]{1,0:T(8,128)S(1)}, u32[]{:S(2)}, u32[]{:S(2)}) collective-permute-start(f32[8,128]{1,0:T(8,128)S(1)} %copy-done.12), channel_id=1, source_target_pairs={{0,16},{8,24},{16,0},{24,8},{1,17},{9,25},{17,1},{25,9},{2,18},{10... | collective-permute-start | bytes 12296 | tf_op jit(solution)/shard_map/ppermute | solution.py:565
  18.0 9.0 %collective-permute-start.6 = (f32[144,128]{1,0:T(8,128)S(1)}, f32[144,128]{1,0:T(8,128)S(1)}, u32[]{:S(2)}, u32[]{:S(2)}) collective-permute-start(f32[144,128]{1,0:T(8,128)S(1)} %get-tuple-element.68), channel_id=1, source_target_pairs={{0,16},{8,24},{16,0},{24,8},{1,17},{9,25},{17,1},{25,9},{2,18},{10... | collective-permute-start | bytes 221192 | tf_op jit(solution)/shard_map/ppermute | solution.py:572
  20.1 10.2 %collective-permute-start.7 = (f32[144,128]{1,0:T(8,128)S(1)}, f32[144,128]{1,0:T(8,128)S(1)}, u32[]{:S(2)}, u32[]{:S(2)}) collective-permute-start(f32[144,128]{1,0:T(8,128)S(1)} %get-tuple-element.69), channel_id=1, source_target_pairs={{0,24},{8,16},{16,8},{24,0},{1,25},{9,17},{17,9},{25,1},{2,26},{10... | collective-permute-start | bytes 221192 | tf_op jit(solution)/shard_map/ppermute | solution.py:572
  22.2 8.1 %collective-permute-start.8 = (f32[144,128]{1,0:T(8,128)S(1)}, f32[144,128]{1,0:T(8,128)S(1)}, u32[]{:S(2)}, u32[]{:S(2)}) collective-permute-start(f32[144,128]{1,0:T(8,128)S(1)} %get-tuple-element.70), channel_id=1, source_target_pairs={{0,8},{8,0},{16,24},{24,16},{1,9},{9,1},{17,25},{25,17},{2,10},{10... | collective-permute-start | bytes 221192 | tf_op jit(solution)/shard_map/ppermute | solution.py:572
  22.3 7.5 %copy-start.4 = (bf16[256,256]{1,0:T(8,128)(2,1)S(1)}, bf16[256,256]{1,0:T(8,128)(2,1)}, u32[]{:S(2)}) copy-start(bf16[256,256]{1,0:T(8,128)(2,1)} %constant.9.clone.stencil) | copy-start | bytes 393220
  24.2 6.1 %collective-permute-start.3 = (f32[32,128]{1,0:T(8,128)S(1)}, f32[32,128]{1,0:T(8,128)S(1)}, u32[]{:S(2)}, u32[]{:S(2)}) collective-permute-start(f32[32,128]{1,0:T(8,128)S(1)} %get-tuple-element.65), channel_id=1, source_target_pairs={{0,8},{8,16},{16,24},{24,0},{1,9},{9,17},{17,25},{25,1},{2,10},{10... | collective-permute-start | bytes 49160 | tf_op jit(solution)/shard_map/ppermute | solution.py:565
  26.2 4.6 %collective-permute-start.4 = (f32[32,128]{1,0:T(8,128)S(1)}, f32[32,128]{1,0:T(8,128)S(1)}, u32[]{:S(2)}, u32[]{:S(2)}) collective-permute-start(f32[32,128]{1,0:T(8,128)S(1)} %get-tuple-element.66), channel_id=1, source_target_pairs={{0,16},{8,24},{16,0},{24,8},{1,17},{9,25},{17,1},{25,9},{2,18},{10... | collective-permute-start | bytes 49160 | tf_op jit(solution)/shard_map/ppermute | solution.py:565
  26.9 4.3 %copy-start = (bf16[256,512]{1,0:T(8,128)(2,1)S(1)}, bf16[256,512]{1,0:T(8,128)(2,1)}, u32[]{:S(2)}) copy-start(bf16[256,512]{1,0:T(8,128)(2,1)} %constant.10.clone.places) | copy-start | bytes 786436
  26.9 4.3 %copy-start.9 = (bf16[256,256]{1,0:T(8,128)(2,1)S(1)}, bf16[256,256]{1,0:T(8,128)(2,1)}, u32[]{:S(2)}) copy-start(bf16[256,256]{1,0:T(8,128)(2,1)} %constant.11.clone.spreads) | copy-start | bytes 393220
  26.9 4.3 %collective-permute-start.5 = (f32[32,128]{1,0:T(8,128)S(1)}, f32[32,128]{1,0:T(8,128)S(1)}, u32[]{:S(2)}, u32[]{:S(2)}) collective-permute-start(f32[32,128]{1,0:T(8,128)S(1)} %get-tuple-element.67), channel_id=1, source_target_pairs={{0,24},{8,0},{16,8},{24,16},{1,25},{9,1},{17,9},{25,17},{2,26},{10... | collective-permute-start | bytes 49160 | tf_op jit(solution)/shard_map/ppermute | solution.py:565
  32.9 5.4 %collective-permute-start.9 = (f32[144,128]{1,0:T(8,128)S(1)}, f32[144,128]{1,0:T(8,128)S(1)}, u32[]{:S(2)}, u32[]{:S(2)}) collective-permute-start(f32[144,128]{1,0:T(8,128)S(1)} %get-tuple-element.78), channel_id=1, source_target_pairs={{0,16},{8,24},{16,0},{24,8},{1,17},{9,25},{17,1},{25,9},{2,18},{10... | collective-permute-start | bytes 221192 | tf_op jit(solution)/shard_map/ppermute | solution.py:572
  34.7 6.2 %collective-permute-start.10 = (f32[144,128]{1,0:T(8,128)S(1)}, f32[144,128]{1,0:T(8,128)S(1)}, u32[]{:S(2)}, u32[]{:S(2)}) collective-permute-start(f32[144,128]{1,0:T(8,128)S(1)} %get-tuple-element.79), channel_id=1, source_target_pairs={{0,24},{8,16},{16,8},{24,0},{1,25},{9,17},{17,9},{25,1},{2,26},{10... | collective-permute-start | bytes 221192 | tf_op jit(solution)/shard_map/ppermute | solution.py:572
  37.3 4.6 %collective-permute-start.11 = (f32[144,128]{1,0:T(8,128)S(1)}, f32[144,128]{1,0:T(8,128)S(1)}, u32[]{:S(2)}, u32[]{:S(2)}) collective-permute-start(f32[144,128]{1,0:T(8,128)S(1)} %get-tuple-element.80), channel_id=1, source_target_pairs={{0,8},{8,0},{16,24},{24,16},{1,9},{9,1},{17,25},{25,17},{2,10},{10... | collective-permute-start | bytes 221192 | tf_op jit(solution)/shard_map/ppermute | solution.py:572
  43.2 6.0 %collective-permute-start.12 = (f32[144,128]{1,0:T(8,128)S(1)}, f32[144,128]{1,0:T(8,128)S(1)}, u32[]{:S(2)}, u32[]{:S(2)}) collective-permute-start(f32[144,128]{1,0:T(8,128)S(1)} %get-tuple-element.87), channel_id=1, source_target_pairs={{0,16},{8,24},{16,0},{24,8},{1,17},{9,25},{17,1},{25,9},{2,18},{10... | collective-permute-start | bytes 221192 | tf_op jit(solution)/shard_map/ppermute | solution.py:572
  46.5 7.0 %collective-permute-start.13 = (f32[144,128]{1,0:T(8,128)S(1)}, f32[144,128]{1,0:T(8,128)S(1)}, u32[]{:S(2)}, u32[]{:S(2)}) collective-permute-start(f32[144,128]{1,0:T(8,128)S(1)} %get-tuple-element.88), channel_id=1, source_target_pairs={{0,24},{8,16},{16,8},{24,0},{1,25},{9,17},{17,9},{25,1},{2,26},{10... | collective-permute-start | bytes 221192 | tf_op jit(solution)/shard_map/ppermute | solution.py:572
  47.3 7.3 %collective-permute-start.14 = (f32[144,128]{1,0:T(8,128)S(1)}, f32[144,128]{1,0:T(8,128)S(1)}, u32[]{:S(2)}, u32[]{:S(2)}) collective-permute-start(f32[144,128]{1,0:T(8,128)S(1)} %get-tuple-element.89), channel_id=1, source_target_pairs={{0,8},{8,0},{16,24},{24,16},{1,9},{9,1},{17,25},{25,17},{2,10},{10... | collective-permute-start | bytes 221192 | tf_op jit(solution)/shard_map/ppermute | solution.py:572
  55.8 5.8 %collective-permute-start.15 = (f32[144,128]{1,0:T(8,128)S(1)}, f32[144,128]{1,0:T(8,128)S(1)}, u32[]{:S(2)}, u32[]{:S(2)}) collective-permute-start(f32[144,128]{1,0:T(8,128)S(1)} %get-tuple-element.96), channel_id=1, source_target_pairs={{0,16},{8,24},{16,0},{24,8},{1,17},{9,25},{17,1},{25,9},{2,18},{10... | collective-permute-start | bytes 221192 | tf_op jit(solution)/shard_map/ppermute | solution.py:572
  56.6 6.4 %collective-permute-start.16 = (f32[144,128]{1,0:T(8,128)S(1)}, f32[144,128]{1,0:T(8,128)S(1)}, u32[]{:S(2)}, u32[]{:S(2)}) collective-permute-start(f32[144,128]{1,0:T(8,128)S(1)} %get-tuple-element.97), channel_id=1, source_target_pairs={{0,24},{8,16},{16,8},{24,0},{1,25},{9,17},{17,9},{25,1},{2,26},{10... | collective-permute-start | bytes 221192 | tf_op jit(solution)/shard_map/ppermute | solution.py:572
  58.5 5.1 %collective-permute-start.17 = (f32[144,128]{1,0:T(8,128)S(1)}, f32[144,128]{1,0:T(8,128)S(1)}, u32[]{:S(2)}, u32[]{:S(2)}) collective-permute-start(f32[144,128]{1,0:T(8,128)S(1)} %get-tuple-element.98), channel_id=1, source_target_pairs={{0,8},{8,0},{16,24},{24,16},{1,9},{9,1},{17,25},{25,17},{2,10},{10... | collective-permute-start | bytes 221192 | tf_op jit(solution)/shard_map/ppermute | solution.py:572

commit v21 on v15

--- a/solution.py
+++ b/solution.py
@@ -442,16 +442,18 @@
 def ghost_shares(ghosts, ghost_edges, places):
     beside = jnp.concatenate(halves(ghosts[...].reshape(SLOTS * TE, 128)), axis=1)
     beside = dot(beside, places)
-    rows = iota((SLOTS, TE, PLANE), 1)
+    half = TE // 2
+    rows = iota((SLOTS, half, PLANE), 1)
     shares = []
     for number in range(2):
         share = beside[:, number * PLANE : number * PLANE + PLANE].reshape(SLOTS, TE, PLANE)
-        for face, at_row in ((0, 0), (1, TE - 1)):
+        parts = []
+        for face, at_row in ((0, 0), (1, half - 1)):
             at = face * 4 + number * 2
             side = [ghost_edges[:, row : row + 1, :] for row in (at, at + 1)]
-            side = jnp.concatenate(side, axis=2)
-            share += jnp.where(rows == at_row, side, 0.0)
-        shares.append(share)
+            side = jnp.where(rows == at_row, jnp.concatenate(side, axis=2), 0.0)
+            parts.append(share[:, face * half : face * half + half] + side)
+        shares.append(jnp.concatenate(parts, axis=1))
     return shares
 
 

time: 62.4 us -> 62.4 us (level)
  no operation moved by 1% of the time
where the time goes in v21:
time: 62.4 us; the launch traced here: 62 us
  starting transfers between devices  29.7 us (48%)
  waiting for transfers between devices  15.4 us (25%)
  Pallas kernels  13.4 us (21%)
  local copies, waits for them, and re-layouts  2.65 us (4%)
  between operations  0.85 us (1%)
    ppermute x15, starting transfers between devices, swap_all(): lax.ppermute(value, 'gx', [(i, i ^ swap) for i in range(count)])  18 us
    ppermute x15, waiting for transfers between devices, swap_all(): lax.ppermute(value, 'gx', [(i, i ^ swap) for i in range(count)])  15.4 us
    ppermute x3, starting transfers between devices, pass_on(): lax.ppermute(value, 'gx', [(i, (i + shift) % count) for i in range(count)])  6.53 us
    all_to_all x1, starting transfers between devices, local(): lax.all_to_all(sides, ('gy', 'gz'), split_axis=0, concat_axis=0, tiled=True)  5.18 us
    unnamed x26, local copies, waits for them, and re-layouts  2.64 us
    pallas_call x2, Pallas kernels, local(): call(middle_step_kernel, [SMEM] + [VMEM] * (6 + others), [field, field, *...  2.44 us
    pallas_call x1, Pallas kernels, local(): call(functools.partial(sides_kernel, sizes, plane_cap), [ANY] * 5, [shape...  2.21 us
    pallas_call x4, Pallas kernels, inner(): call(functools.partial(inner_kernel, bool(heat)), [VMEM] * (3 + len(heat)...  1.95 us
  transfers between devices with their start and end apart: 19, of which 9 were waited for; matrix products, arithmetic and copies ran while one was open for 0% of the time, Pallas kernels for 9%

profile of v21, /device:TPU:0, one launch (start us, length us, event | category | flops | bytes accessed | tf_op | source)
XLA Modules:
  0.0 62.0 jit_solution(10521854563193344420)
XLA Ops:
  0.6 0.0 copy-start.1
  0.6 2.2 %shard_map.130 = (f32[8,24,128]{2,1,0:T(8,128)}, s32[2,128]{1,0:T(2,128)}, f32[4,128]{1,0:T(4,128)}, f32[8,128]{1,0:T(8,128)}) custom-call(s32[1,16]{1,0:T(1,128)} %bitcast.15, s32[1,16]{1,0:T(1,128)} %bitcast.16, s32[6,1,16]{2,1,0:T(1,128)} %bitcast.14, f32[8,32,128]{2,1,0:T(8,128)} %h.3, f32[8,32,128]{2,1,0:T(8,128)} %k.3), custom_call_target="tpu_custom_call" | custom-call | tf_op jit(solution)/shard_map/pallas_call | solution.py:544
  2.9 0.0 copy-start.12
  2.9 5.2 %all-to-all-start = ((f32[8,24,128]{2,1,0:T(8,128)}), f32[8,24,128]{2,1,0:T(8,128)S(1)}, u32[]{:S(2)}, u32[]{:S(2)}) async-start(f32[8,24,128]{2,1,0:T(8,128)} %get-tuple-element.55), calls=%async_computation | async-start | bytes 196608 | tf_op jit(solution)/shard_map/all_to_all | solution.py:569
  8.1 0.0 copy-done.12
  8.1 2.7 %collective-permute-start = (f32[8,128]{1,0:T(8,128)S(1)}, f32[8,128]{1,0:T(8,128)S(1)}, u32[]{:S(2)}, u32[]{:S(2)}) collective-permute-start(f32[8,128]{1,0:T(8,128)S(1)} %copy-done.12), channel_id=1, source_target_pairs={{0,16},{8,24},{16,0},{24,8},{1,17},{9,25},{17,1},{25,9},{2,18},{10... | collective-permute-start | bytes 12296 | tf_op jit(solution)/shard_map/ppermute | solution.py:572
  10.7 0.7 %copy-done.11 = f32[4,128]{1,0:T(4,128)S(1)} copy-done((f32[4,128]{1,0:T(4,128)S(1)}, f32[4,128]{1,0:T(4,128)}, u32[]{:S(2)}) %copy-start.11) | copy-done | bytes 2072
  11.4 0.0 copy-done.10
  11.4 0.9 %copy-done.2 = f32[1,1,1,16,16,256]{5,4,3,2,1,0:T(8,128)S(1)} copy-done((f32[1,1,1,16,16,256]{5,4,3,2,1,0:T(8,128)S(1)}, f32[1,1,1,16,16,256]{5,4,3,2,1,0:T(8,128)}, u32[]{:S(2)}) %copy-start.2) | copy-done | bytes 262168
  12.4 0.9 %copy-done.7 = f32[1,1,1,16,16,256]{5,4,3,2,1,0:T(8,128)S(1)} copy-done((f32[1,1,1,16,16,256]{5,4,3,2,1,0:T(8,128)S(1)}, f32[1,1,1,16,16,256]{5,4,3,2,1,0:T(8,128)}, u32[]{:S(2)}) %copy-start.7) | copy-done | bytes 262168
  13.3 0.9 %shard_map.131 = (f32[32,16,128]{2,1,0:T(8,128)S(1)}, f32[256,128]{1,0:T(8,128)S(1)}, f32[4,128]{1,0:T(4,128)S(1)}, f32[144,128]{1,0:T(8,128)S(1)}, f32[144,128]{1,0:T(8,128)S(1)}, /*index=5*/f32[144,128]{1,0:T(8,128)S(1)}) custom-call(s32[2,128]{1,0:T(2,128)S(1)} %copy-done.10, f32[4,128]{1,0:T(4,128)S(1)} %copy-done.11, f32[16,16,256]{2,1,0:T(8,128)S(1)} %bitcast.9, ...), custom_call_target="tpu_custom_call" | custom-call | tf_op jit(solution)/shard_map/pallas_call | solution.py:587
  14.2 0.0 collective-permute-done.rest_0_
  14.2 0.0 all-to-all-done.got
  14.2 0.0 copy-done.5
  14.3 0.0 copy-done.6
  14.3 0.0 copy-start.8
  14.3 0.0 copy-start.3
  14.3 1.6 %collective-permute-start.1 = (f32[104,128]{1,0:T(8,128)S(1)}, f32[104,128]{1,0:T(8,128)S(1)}, u32[]{:S(2)}, u32[]{:S(2)}) collective-permute-start(f32[104,128]{1,0:T(8,128)S(1)} %get-tuple-element.57), channel_id=1, source_target_pairs={{0,8},{8,16},{16,24},{24,0},{1,9},{9,17},{17,25},{25,1},{2,10},{10... | collective-permute-start | bytes 159752 | tf_op jit(solution)/shard_map/ppermute | solution.py:572
  16.0 2.2 %collective-permute-start.2 = (f32[104,128]{1,0:T(8,128)S(1)}, f32[104,128]{1,0:T(8,128)S(1)}, u32[]{:S(2)}, u32[]{:S(2)}) collective-permute-start(f32[104,128]{1,0:T(8,128)S(1)} %get-tuple-element.58), channel_id=1, source_target_pairs={{0,24},{8,0},{16,8},{24,16},{1,25},{9,1},{17,9},{25,17},{2,26},{10... | collective-permute-start | bytes 159752 | tf_op jit(solution)/shard_map/ppermute | solution.py:572
  18.2 0.0 collective-permute-start.6
  18.2 2.1 %collective-permute-start.7 = (f32[144,128]{1,0:T(8,128)S(1)}, f32[144,128]{1,0:T(8,128)S(1)}, u32[]{:S(2)}, u32[]{:S(2)}) collective-permute-start(f32[144,128]{1,0:T(8,128)S(1)} %get-tuple-element.69), channel_id=1, source_target_pairs={{0,24},{8,16},{16,8},{24,0},{1,25},{9,17},{17,9},{25,1},{2,26},{10... | collective-permute-start | bytes 221192 | tf_op jit(solution)/shard_map/ppermute | solution.py:576
  20.3 1.3 %collective-permute-start.8 = (f32[144,128]{1,0:T(8,128)S(1)}, f32[144,128]{1,0:T(8,128)S(1)}, u32[]{:S(2)}, u32[]{:S(2)}) collective-permute-start(f32[144,128]{1,0:T(8,128)S(1)} %get-tuple-element.70), channel_id=1, source_target_pairs={{0,8},{8,0},{16,24},{24,16},{1,9},{9,1},{17,25},{25,17},{2,10},{10... | collective-permute-start | bytes 221192 | tf_op jit(solution)/shard_map/ppermute | solution.py:576
  21.7 0.0 collective-permute-done.1.low
  21.7 0.0 collective-permute-done.2.high
  21.7 0.0 copy-start.4
  21.8 1.9 %shard_map.133 = (f32[8,32,128]{2,1,0:T(8,128)S(1)}, f32[32,128]{1,0:T(8,128)S(1)}, f32[32,128]{1,0:T(8,128)S(1)}, f32[32,128]{1,0:T(8,128)S(1)}, f32[32,128]{1,0:T(8,128)S(1)}) custom-call(s32[4,8]{1,0:T(4,128)S(1)} %maximum_convert_fusion.request, f32[8,32,128]{2,1,0:T(8,128)S(1)} %copy-done.5, f32[8,32,128]{2,1,0:T(8,128)S(1)} %copy-done.6, ...), custom_call_target="tpu_custom_call" | custom-call | tf_op jit(solution)/shard_map/pallas_call | solution.py:606
  23.7 1.0 %collective-permute-start.3 = (f32[32,128]{1,0:T(8,128)S(1)}, f32[32,128]{1,0:T(8,128)S(1)}, u32[]{:S(2)}, u32[]{:S(2)}) collective-permute-start(f32[32,128]{1,0:T(8,128)S(1)} %get-tuple-element.65), channel_id=1, source_target_pairs={{0,16},{8,24},{16,0},{24,8},{1,17},{9,25},{17,1},{25,9},{2,18},{10... | collective-permute-start | bytes 49160 | tf_op jit(solution)/shard_map/ppermute | solution.py:576
  24.6 2.3 %collective-permute-start.4 = (f32[32,128]{1,0:T(8,128)S(1)}, f32[32,128]{1,0:T(8,128)S(1)}, u32[]{:S(2)}, u32[]{:S(2)}) collective-permute-start(f32[32,128]{1,0:T(8,128)S(1)} %get-tuple-element.66), channel_id=1, source_target_pairs={{0,24},{8,16},{16,8},{24,0},{1,25},{9,17},{17,9},{25,1},{2,26},{10... | collective-permute-start | bytes 49160 | tf_op jit(solution)/shard_map/ppermute | solution.py:576
  27.0 0.0 collective-permute-done.6.rest_4_
  27.0 0.6 collective-permute-start.5
  27.5 0.0 copy-done.8
  27.5 0.5 shard_map.135
  28.0 0.0 collective-permute-done.7.rest_5_
  28.0 0.0 collective-permute-done.8.rest_6_
  28.1 0.3 collective-permute-done.3.rest_1_
  28.4 1.8 %collective-permute-done.4.rest_2_ = f32[32,128]{1,0:T(8,128)S(1)} collective-permute-done((f32[32,128]{1,0:T(8,128)S(1)}, f32[32,128]{1,0:T(8,128)S(1)}, u32[]{:S(2)}, u32[]{:S(2)}) %collective-permute-start.4) | collective-permute-done | bytes 16416 | tf_op jit(solution)/shard_map/ppermute | solution.py:576
  30.2 0.5 collective-permute-done.5.rest_3_
  30.7 0.0 copy-done
  30.7 1.7 %shard_map.136 = (f32[16,16,256]{2,1,0:T(8,128)S(1)}, f32[16,16,256]{2,1,0:T(8,128)S(1)}, f32[2,256,128]{2,1,0:T(8,128)S(1)}, f32[32,16,128]{2,1,0:T(8,128)S(1)}...) custom-call(s32[2,128]{1,0:T(2,128)S(1)} %copy-done.10, ...), custom_call_target="tpu_custom_call" | custom-call | tf_op jit(solution)/shard_map/pallas_call | solution.py:629
  32.4 2.0 %collective-permute-start.9 = (f32[144,128]{1,0:T(8,128)S(1)}, f32[144,128]{1,0:T(8,128)S(1)}, u32[]{:S(2)}, u32[]{:S(2)}) collective-permute-start(f32[144,128]{1,0:T(8,128)S(1)} %get-tuple-element.78), channel_id=1, source_target_pairs={{0,16},{8,24},{16,0},{24,8},{1,17},{9,25},{17,1},{25,9},{2,18},{10... | collective-permute-start | bytes 221192 | tf_op jit(solution)/shard_map/ppermute | solution.py:576
  34.4 1.0 %collective-permute-start.10 = (f32[144,128]{1,0:T(8,128)S(1)}, f32[144,128]{1,0:T(8,128)S(1)}, u32[]{:S(2)}, u32[]{:S(2)}) collective-permute-start(f32[144,128]{1,0:T(8,128)S(1)} %get-tuple-element.79), channel_id=1, source_target_pairs={{0,24},{8,16},{16,8},{24,0},{1,25},{9,17},{17,9},{25,1},{2,26},{10... | collective-permute-start | bytes 221192 | tf_op jit(solution)/shard_map/ppermute | solution.py:576
  35.4 0.6 collective-permute-start.11
  35.9 0.5 shard_map.137
  36.4 2.1 %collective-permute-done.9.rest_0_ = f32[144,128]{1,0:T(8,128)S(1)} collective-permute-done((f32[144,128]{1,0:T(8,128)S(1)}, f32[144,128]{1,0:T(8,128)S(1)}, u32[]{:S(2)}, u32[]{:S(2)}) %collective-permute-start.9) | collective-permute-done | bytes 73760 | tf_op jit(solution)/shard_map/ppermute | solution.py:576
  38.5 2.1 %collective-permute-done.10.rest_1_ = f32[144,128]{1,0:T(8,128)S(1)} collective-permute-done((f32[144,128]{1,0:T(8,128)S(1)}, f32[144,128]{1,0:T(8,128)S(1)}, u32[]{:S(2)}, u32[]{:S(2)}) %collective-permute-start.10) | collective-permute-done | bytes 73760 | tf_op jit(solution)/shard_map/ppermute | solution.py:576
  40.5 0.0 collective-permute-done.11.rest_2_
  40.5 1.2 %shard_map.138 = (f32[16,16,256]{2,1,0:T(8,128)S(1)}, f32[16,16,256]{2,1,0:T(8,128)S(1)}, f32[32,16,128]{2,1,0:T(8,128)S(1)}, f32[256,128]{1,0:T(8,128)S(1)}, f3...) custom-call(s32[2,128]{1,0:T(2,128)S(1)} %copy-done.10, ...), custom_call_target="tpu_custom_call" | custom-call | tf_op jit(solution)/shard_map/pallas_call | solution.py:643
  41.8 1.9 %collective-permute-start.12 = (f32[144,128]{1,0:T(8,128)S(1)}, f32[144,128]{1,0:T(8,128)S(1)}, u32[]{:S(2)}, u32[]{:S(2)}) collective-permute-start(f32[144,128]{1,0:T(8,128)S(1)} %get-tuple-element.87), channel_id=1, source_target_pairs={{0,16},{8,24},{16,0},{24,8},{1,17},{9,25},{17,1},{25,9},{2,18},{10... | collective-permute-start | bytes 221192 | tf_op jit(solution)/shard_map/ppermute | solution.py:576
  43.7 0.5 collective-permute-start.13
  44.2 1.2 %collective-permute-start.14 = (f32[144,128]{1,0:T(8,128)S(1)}, f32[144,128]{1,0:T(8,128)S(1)}, u32[]{:S(2)}, u32[]{:S(2)}) collective-permute-start(f32[144,128]{1,0:T(8,128)S(1)} %get-tuple-element.89), channel_id=1, source_target_pairs={{0,8},{8,0},{16,24},{24,16},{1,9},{9,1},{17,25},{25,17},{2,10},{10... | collective-permute-start | bytes 221192 | tf_op jit(solution)/shard_map/ppermute | solution.py:576
  45.3 0.5 shard_map.139
  45.8 1.5 %collective-permute-done.12.rest_0_ = f32[144,128]{1,0:T(8,128)S(1)} collective-permute-done((f32[144,128]{1,0:T(8,128)S(1)}, f32[144,128]{1,0:T(8,128)S(1)}, u32[]{:S(2)}, u32[]{:S(2)}) %collective-permute-start.12) | collective-permute-done | bytes 73760 | tf_op jit(solution)/shard_map/ppermute | solution.py:576
  47.3 3.0 %collective-permute-done.13.rest_1_ = f32[144,128]{1,0:T(8,128)S(1)} collective-permute-done((f32[144,128]{1,0:T(8,128)S(1)}, f32[144,128]{1,0:T(8,128)S(1)}, u32[]{:S(2)}, u32[]{:S(2)}) %collective-permute-start.13) | collective-permute-done | bytes 73760 | tf_op jit(solution)/shard_map/ppermute | solution.py:576
  50.3 0.0 collective-permute-done.14.rest_2_
  50.3 1.2 %shard_map.140 = (f32[16,16,256]{2,1,0:T(8,128)S(1)}, f32[16,16,256]{2,1,0:T(8,128)S(1)}, f32[32,16,128]{2,1,0:T(8,128)S(1)}, f32[256,128]{1,0:T(8,128)S(1)}, f3...) custom-call(s32[2,128]{1,0:T(2,128)S(1)} %copy-done.10, ...), custom_call_target="tpu_custom_call" | custom-call | tf_op jit(solution)/shard_map/pallas_call | solution.py:643
  51.5 2.7 %collective-permute-start.15 = (f32[144,128]{1,0:T(8,128)S(1)}, f32[144,128]{1,0:T(8,128)S(1)}, u32[]{:S(2)}, u32[]{:S(2)}) collective-permute-start(f32[144,128]{1,0:T(8,128)S(1)} %get-tuple-element.96), channel_id=1, source_target_pairs={{0,16},{8,24},{16,0},{24,8},{1,17},{9,25},{17,1},{25,9},{2,18},{10... | collective-permute-start | bytes 221192 | tf_op jit(solution)/shard_map/ppermute | solution.py:576
  54.2 0.4 collective-permute-start.16
  54.7 0.4 collective-permute-start.17
  55.1 0.7 %shard_map.134 = f32[8,32,128]{2,1,0:T(8,128)} custom-call(f32[8,32,128]{2,1,0:T(8,128)S(1)} %get-tuple-element.59.value), custom_call_target="tpu_custom_call" | custom-call | tf_op jit(solution)/shard_map/pallas_call | solution.py:613
  55.8 0.5 shard_map.141
  56.3 1.4 %collective-permute-done.15.rest_0_ = f32[144,128]{1,0:T(8,128)S(1)} collective-permute-done((f32[144,128]{1,0:T(8,128)S(1)}, f32[144,128]{1,0:T(8,128)S(1)}, u32[]{:S(2)}, u32[]{:S(2)}) %collective-permute-start.15) | collective-permute-done | bytes 73760 | tf_op jit(solution)/shard_map/ppermute | solution.py:576
  57.6 2.8 %collective-permute-done.16.rest_1_ = f32[144,128]{1,0:T(8,128)S(1)} collective-permute-done((f32[144,128]{1,0:T(8,128)S(1)}, f32[144,128]{1,0:T(8,128)S(1)}, u32[]{:S(2)}, u32[]{:S(2)}) %collective-permute-start.16) | collective-permute-done | bytes 73760 | tf_op jit(solution)/shard_map/ppermute | solution.py:576
  60.4 0.0 collective-permute-done.17.rest_2_
  60.4 1.6 %shard_map.142 = (f32[16,16,256]{2,1,0:T(8,128)}, f32[16,16,256]{2,1,0:T(8,128)}) custom-call(s32[2,128]{1,0:T(2,128)S(1)} %copy-done.10, f32[16,16,256]{2,1,0:T(8,128)S(1)} %get-tuple-element.92.phase, f32[16,16,256]{2,1,0:T(8,128)S(1)} %get-tuple-element.93.solute, f32[32,16,128]{2,1,0:T(8,128)S(1)} %get-tuple-element.94.own, ...), custom_call_target="tpu_custom_call" | custom-call | tf_op jit(solution)/shard_map/pallas_call | solution.py:652
  (18 shorter events, 0.1 us)
Async XLA Ops:
  0.6 10.1 %copy-start.1 = (bf16[512,256]{1,0:T(8,128)(2,1)S(1)}, bf16[512,256]{1,0:T(8,128)(2,1)}, u32[]{:S(2)}) copy-start(bf16[512,256]{1,0:T(8,128)(2,1)} %constant.8.clone.picks) | copy-start | bytes 786436
  2.9 5.2 %copy-start.12 = (f32[8,128]{1,0:T(8,128)S(1)}, f32[8,128]{1,0:T(8,128)}, u32[]{:S(2)}) copy-start(f32[8,128]{1,0:T(8,128)} %get-tuple-element.56) | copy-start | bytes 12292
  2.9 11.4 %all-to-all-start = ((f32[8,24,128]{2,1,0:T(8,128)}), f32[8,24,128]{2,1,0:T(8,128)S(1)}, u32[]{:S(2)}, u32[]{:S(2)}) async-start(f32[8,24,128]{2,1,0:T(8,128)} %get-tuple-element.55), calls=%async_computation | async-start | bytes 196608 | tf_op jit(solution)/shard_map/all_to_all | solution.py:569
  8.1 6.2 %collective-permute-start = (f32[8,128]{1,0:T(8,128)S(1)}, f32[8,128]{1,0:T(8,128)S(1)}, u32[]{:S(2)}, u32[]{:S(2)}) collective-permute-start(f32[8,128]{1,0:T(8,128)S(1)} %copy-done.12), channel_id=1, source_target_pairs={{0,16},{8,24},{16,0},{24,8},{1,17},{9,25},{17,1},{25,9},{2,18},{10... | collective-permute-start | bytes 12296 | tf_op jit(solution)/shard_map/ppermute | solution.py:572
  10.7 0.7 %copy-start.11 = (f32[4,128]{1,0:T(4,128)S(1)}, f32[4,128]{1,0:T(4,128)}, u32[]{:S(2)}) copy-start(f32[4,128]{1,0:T(4,128)} %get-tuple-element.53.asked) | copy-start | bytes 6148
  10.7 0.7 %copy-start.10 = (s32[2,128]{1,0:T(2,128)S(1)}, s32[2,128]{1,0:T(2,128)}, u32[]{:S(2)}) copy-start(s32[2,128]{1,0:T(2,128)} %get-tuple-element.52.table) | copy-start | bytes 3076
  11.4 0.9 %copy-start.2 = (f32[1,1,1,16,16,256]{5,4,3,2,1,0:T(8,128)S(1)}, f32[1,1,1,16,16,256]{5,4,3,2,1,0:T(8,128)}, u32[]{:S(2)}) copy-start(f32[1,1,1,16,16,256]{5,4,3,2,1,0:T(8,128)} %param.13) | copy-start | bytes 786436
  12.4 0.9 %copy-start.7 = (f32[1,1,1,16,16,256]{5,4,3,2,1,0:T(8,128)S(1)}, f32[1,1,1,16,16,256]{5,4,3,2,1,0:T(8,128)}, u32[]{:S(2)}) copy-start(f32[1,1,1,16,16,256]{5,4,3,2,1,0:T(8,128)} %param.14) | copy-start | bytes 786436
  13.3 0.9 %copy-start.5 = (f32[8,32,128]{2,1,0:T(8,128)S(1)}, f32[8,32,128]{2,1,0:T(8,128)}, u32[]{:S(2)}) copy-start(f32[8,32,128]{2,1,0:T(8,128)} %h.3) | copy-start | bytes 393220
  13.3 1.0 %copy-start.6 = (f32[8,32,128]{2,1,0:T(8,128)S(1)}, f32[8,32,128]{2,1,0:T(8,128)}, u32[]{:S(2)}) copy-start(f32[8,32,128]{2,1,0:T(8,128)} %k.3) | copy-start | bytes 393220
  14.3 13.3 %copy-start.8 = (f32[1,1,1,16,16,256]{5,4,3,2,1,0:T(8,128)S(1)}, f32[1,1,1,16,16,256]{5,4,3,2,1,0:T(8,128)}, u32[]{:S(2)}) copy-start(f32[1,1,1,16,16,256]{5,4,3,2,1,0:T(8,128)} %param.14) | copy-start | bytes 786436
  14.3 13.2 %copy-start.3 = (f32[1,1,1,16,16,256]{5,4,3,2,1,0:T(8,128)S(1)}, f32[1,1,1,16,16,256]{5,4,3,2,1,0:T(8,128)}, u32[]{:S(2)}) copy-start(f32[1,1,1,16,16,256]{5,4,3,2,1,0:T(8,128)} %param.13) | copy-start | bytes 786436
  14.3 7.4 %collective-permute-start.1 = (f32[104,128]{1,0:T(8,128)S(1)}, f32[104,128]{1,0:T(8,128)S(1)}, u32[]{:S(2)}, u32[]{:S(2)}) collective-permute-start(f32[104,128]{1,0:T(8,128)S(1)} %get-tuple-element.57), channel_id=1, source_target_pairs={{0,8},{8,16},{16,24},{24,0},{1,9},{9,17},{17,25},{25,1},{2,10},{10... | collective-permute-start | bytes 159752 | tf_op jit(solution)/shard_map/ppermute | solution.py:572
  16.0 5.8 %collective-permute-start.2 = (f32[104,128]{1,0:T(8,128)S(1)}, f32[104,128]{1,0:T(8,128)S(1)}, u32[]{:S(2)}, u32[]{:S(2)}) collective-permute-start(f32[104,128]{1,0:T(8,128)S(1)} %get-tuple-element.58), channel_id=1, source_target_pairs={{0,24},{8,0},{16,8},{24,16},{1,25},{9,1},{17,9},{25,17},{2,26},{10... | collective-permute-start | bytes 159752 | tf_op jit(solution)/shard_map/ppermute | solution.py:572
  18.2 8.8 %collective-permute-start.6 = (f32[144,128]{1,0:T(8,128)S(1)}, f32[144,128]{1,0:T(8,128)S(1)}, u32[]{:S(2)}, u32[]{:S(2)}) collective-permute-start(f32[144,128]{1,0:T(8,128)S(1)} %get-tuple-element.68), channel_id=1, source_target_pairs={{0,16},{8,24},{16,0},{24,8},{1,17},{9,25},{17,1},{25,9},{2,18},{10... | collective-permute-start | bytes 221192 | tf_op jit(solution)/shard_map/ppermute | solution.py:576
  18.2 9.8 %collective-permute-start.7 = (f32[144,128]{1,0:T(8,128)S(1)}, f32[144,128]{1,0:T(8,128)S(1)}, u32[]{:S(2)}, u32[]{:S(2)}) collective-permute-start(f32[144,128]{1,0:T(8,128)S(1)} %get-tuple-element.69), channel_id=1, source_target_pairs={{0,24},{8,16},{16,8},{24,0},{1,25},{9,17},{17,9},{25,1},{2,26},{10... | collective-permute-start | bytes 221192 | tf_op jit(solution)/shard_map/ppermute | solution.py:576
  20.3 7.7 %collective-permute-start.8 = (f32[144,128]{1,0:T(8,128)S(1)}, f32[144,128]{1,0:T(8,128)S(1)}, u32[]{:S(2)}, u32[]{:S(2)}) collective-permute-start(f32[144,128]{1,0:T(8,128)S(1)} %get-tuple-element.70), channel_id=1, source_target_pairs={{0,8},{8,0},{16,24},{24,16},{1,9},{9,1},{17,25},{25,17},{2,10},{10... | collective-permute-start | bytes 221192 | tf_op jit(solution)/shard_map/ppermute | solution.py:576
  21.7 5.8 %copy-start.4 = (bf16[256,256]{1,0:T(8,128)(2,1)S(1)}, bf16[256,256]{1,0:T(8,128)(2,1)}, u32[]{:S(2)}) copy-start(bf16[256,256]{1,0:T(8,128)(2,1)} %constant.9.clone.stencil) | copy-start | bytes 393220
  23.7 4.7 %collective-permute-start.3 = (f32[32,128]{1,0:T(8,128)S(1)}, f32[32,128]{1,0:T(8,128)S(1)}, u32[]{:S(2)}, u32[]{:S(2)}) collective-permute-start(f32[32,128]{1,0:T(8,128)S(1)} %get-tuple-element.65), channel_id=1, source_target_pairs={{0,16},{8,24},{16,0},{24,8},{1,17},{9,25},{17,1},{25,9},{2,18},{10... | collective-permute-start | bytes 49160 | tf_op jit(solution)/shard_map/ppermute | solution.py:576
  24.6 5.5 %collective-permute-start.4 = (f32[32,128]{1,0:T(8,128)S(1)}, f32[32,128]{1,0:T(8,128)S(1)}, u32[]{:S(2)}, u32[]{:S(2)}) collective-permute-start(f32[32,128]{1,0:T(8,128)S(1)} %get-tuple-element.66), channel_id=1, source_target_pairs={{0,24},{8,16},{16,8},{24,0},{1,25},{9,17},{17,9},{25,1},{2,26},{10... | collective-permute-start | bytes 49160 | tf_op jit(solution)/shard_map/ppermute | solution.py:576
  27.0 3.7 %copy-start = (bf16[256,512]{1,0:T(8,128)(2,1)S(1)}, bf16[256,512]{1,0:T(8,128)(2,1)}, u32[]{:S(2)}) copy-start(bf16[256,512]{1,0:T(8,128)(2,1)} %constant.10.clone.places) | copy-start | bytes 786436
  27.0 3.7 %copy-start.9 = (bf16[256,256]{1,0:T(8,128)(2,1)S(1)}, bf16[256,256]{1,0:T(8,128)(2,1)}, u32[]{:S(2)}) copy-start(bf16[256,256]{1,0:T(8,128)(2,1)} %constant.11.clone.spreads) | copy-start | bytes 393220
  27.0 3.7 %collective-permute-start.5 = (f32[32,128]{1,0:T(8,128)S(1)}, f32[32,128]{1,0:T(8,128)S(1)}, u32[]{:S(2)}, u32[]{:S(2)}) collective-permute-start(f32[32,128]{1,0:T(8,128)S(1)} %get-tuple-element.67), channel_id=1, source_target_pairs={{0,8},{8,0},{16,24},{24,16},{1,9},{9,1},{17,25},{25,17},{2,10},{10... | collective-permute-start | bytes 49160 | tf_op jit(solution)/shard_map/ppermute | solution.py:576
  32.4 6.1 %collective-permute-start.9 = (f32[144,128]{1,0:T(8,128)S(1)}, f32[144,128]{1,0:T(8,128)S(1)}, u32[]{:S(2)}, u32[]{:S(2)}) collective-permute-start(f32[144,128]{1,0:T(8,128)S(1)} %get-tuple-element.78), channel_id=1, source_target_pairs={{0,16},{8,24},{16,0},{24,8},{1,17},{9,25},{17,1},{25,9},{2,18},{10... | collective-permute-start | bytes 221192 | tf_op jit(solution)/shard_map/ppermute | solution.py:576
  34.4 6.2 %collective-permute-start.10 = (f32[144,128]{1,0:T(8,128)S(1)}, f32[144,128]{1,0:T(8,128)S(1)}, u32[]{:S(2)}, u32[]{:S(2)}) collective-permute-start(f32[144,128]{1,0:T(8,128)S(1)} %get-tuple-element.79), channel_id=1, source_target_pairs={{0,24},{8,16},{16,8},{24,0},{1,25},{9,17},{17,9},{25,1},{2,26},{10... | collective-permute-start | bytes 221192 | tf_op jit(solution)/shard_map/ppermute | solution.py:576
  35.4 5.2 %collective-permute-start.11 = (f32[144,128]{1,0:T(8,128)S(1)}, f32[144,128]{1,0:T(8,128)S(1)}, u32[]{:S(2)}, u32[]{:S(2)}) collective-permute-start(f32[144,128]{1,0:T(8,128)S(1)} %get-tuple-element.80), channel_id=1, source_target_pairs={{0,8},{8,0},{16,24},{24,16},{1,9},{9,1},{17,25},{25,17},{2,10},{10... | collective-permute-start | bytes 221192 | tf_op jit(solution)/shard_map/ppermute | solution.py:576
  41.8 5.5 %collective-permute-start.12 = (f32[144,128]{1,0:T(8,128)S(1)}, f32[144,128]{1,0:T(8,128)S(1)}, u32[]{:S(2)}, u32[]{:S(2)}) collective-permute-start(f32[144,128]{1,0:T(8,128)S(1)} %get-tuple-element.87), channel_id=1, source_target_pairs={{0,16},{8,24},{16,0},{24,8},{1,17},{9,25},{17,1},{25,9},{2,18},{10... | collective-permute-start | bytes 221192 | tf_op jit(solution)/shard_map/ppermute | solution.py:576
  43.7 6.6 %collective-permute-start.13 = (f32[144,128]{1,0:T(8,128)S(1)}, f32[144,128]{1,0:T(8,128)S(1)}, u32[]{:S(2)}, u32[]{:S(2)}) collective-permute-start(f32[144,128]{1,0:T(8,128)S(1)} %get-tuple-element.88), channel_id=1, source_target_pairs={{0,24},{8,16},{16,8},{24,0},{1,25},{9,17},{17,9},{25,1},{2,26},{10... | collective-permute-start | bytes 221192 | tf_op jit(solution)/shard_map/ppermute | solution.py:576
  44.2 6.1 %collective-permute-start.14 = (f32[144,128]{1,0:T(8,128)S(1)}, f32[144,128]{1,0:T(8,128)S(1)}, u32[]{:S(2)}, u32[]{:S(2)}) collective-permute-start(f32[144,128]{1,0:T(8,128)S(1)} %get-tuple-element.89), channel_id=1, source_target_pairs={{0,8},{8,0},{16,24},{24,16},{1,9},{9,1},{17,25},{25,17},{2,10},{10... | collective-permute-start | bytes 221192 | tf_op jit(solution)/shard_map/ppermute | solution.py:576
  51.5 6.1 %collective-permute-start.15 = (f32[144,128]{1,0:T(8,128)S(1)}, f32[144,128]{1,0:T(8,128)S(1)}, u32[]{:S(2)}, u32[]{:S(2)}) collective-permute-start(f32[144,128]{1,0:T(8,128)S(1)} %get-tuple-element.96), channel_id=1, source_target_pairs={{0,16},{8,24},{16,0},{24,8},{1,17},{9,25},{17,1},{25,9},{2,18},{10... | collective-permute-start | bytes 221192 | tf_op jit(solution)/shard_map/ppermute | solution.py:576
  54.2 6.2 %collective-permute-start.16 = (f32[144,128]{1,0:T(8,128)S(1)}, f32[144,128]{1,0:T(8,128)S(1)}, u32[]{:S(2)}, u32[]{:S(2)}) collective-permute-start(f32[144,128]{1,0:T(8,128)S(1)} %get-tuple-element.97), channel_id=1, source_target_pairs={{0,24},{8,16},{16,8},{24,0},{1,25},{9,17},{17,9},{25,1},{2,26},{10... | collective-permute-start | bytes 221192 | tf_op jit(solution)/shard_map/ppermute | solution.py:576
  54.7 5.7 %collective-permute-start.17 = (f32[144,128]{1,0:T(8,128)S(1)}, f32[144,128]{1,0:T(8,128)S(1)}, u32[]{:S(2)}, u32[]{:S(2)}) collective-permute-start(f32[144,128]{1,0:T(8,128)S(1)} %get-tuple-element.98), channel_id=1, source_target_pairs={{0,8},{8,0},{16,24},{24,16},{1,9},{9,1},{17,25},{25,17},{2,10},{10... | collective-permute-start | bytes 221192 | tf_op jit(solution)/shard_map/ppermute | solution.py:576
